TPU v7x, 32 devices: a whole 2x2x4 slice. The times are simulated.
32 devices in a mesh: row: 4 (over y, x), col: 8 (over z, core).
Axes of the slice: x: 2, y: 2, z: 4, core: 2. Of those that a mesh axis runs over, the one named last changes fastest.
Arguments:
- region_inverse: float32 [4096, 4096], P('row', 'col'), may hold values from -6 to 6
- factor_cols: float32 [3, 4096, 512], P(None, 'row'), may hold values from -0.09375 to 0.09375
- parent_factor: float32 [2, 512, 512], P(None, 'col'), may hold values from -0.25 to 0.25
- diag_inverse: float32 [3, 512, 512], P(None, 'col'), may hold values from -6 to 6
- listed: int32 [3, 8], replicated, may hold values from 0 to 1, as said below
Outputs:
- col_blocks: float32 [3, 4096, 512], P(None, ('row', 'col'))
- diag_blocks: float32 [3, 512, 512], P(None, 'col')
- parent_rows: float32 [2, 512, 512], P(None, 'col')
Inputs may be any that keep to these rules, and one draw needn't show every extreme that they name: listed[0] has exactly 6 ones; listed[1] and listed[2] have exactly 4 ones each, all at blocks that listed[0] also lists.
All inputs are finite; a program needn't handle non-finite values.
Results may differ from a plain program's by a relative error of at most 0.0001.
Values sent between devices are 32-bit elements; how exact they have to be, the bound alone decides.
No kernel may reach another device: no remote copies, remote signals or barrier semaphores. Data moves between devices by JAX's collectives and lax.ppermute only.
A program may use at most 128 MiB of HBM per device.

v0:
```python
import jax
import jax.numpy as jnp
from jax import lax
from jax.sharding import PartitionSpec as P


def broadcast(value, axis, source):
    kept = jnp.where(lax.axis_index(axis) == source, value, 0).astype(value.dtype)
    return lax.psum(kept, axis)


def matmul_plain(left, right):
    return jnp.dot(left, right, precision=lax.Precision.HIGHEST, preferred_element_type=jnp.float32)


def matmul_left(left, right):
    return lax.dot_general(
        left,
        right,
        (((0,), (0,)), ((), ())),
        precision=lax.Precision.HIGHEST,
        preferred_element_type=jnp.float32,
    )


def row_weights(listed_row, first_row, count, width):
    global_rows = first_row + lax.iota(jnp.int32, count)
    block_ids = global_rows // width
    table = lax.iota(jnp.int32, listed_row.shape[0])
    hits = (block_ids[:, None] == table[None, :]).astype(jnp.float32) * listed_row.astype(
        jnp.float32
    )[None, :]
    return jnp.sum(hits, axis=1)


def total_sums(values):
    return lax.psum(tuple(values), ("row", "col"))


def shards(region_inverse, factor_cols, parent_factor, diag_inverse, listed):
    row_count = lax.axis_size("row")
    col_count = lax.axis_size("col")
    row_place = lax.axis_index("row")
    col_place = lax.axis_index("col")
    rows_here, cols_here = region_inverse.shape
    width = factor_cols.shape[2]
    group = rows_here // col_count
    ratio = col_count // row_count
    diag_width = width // col_count
    diag_start = col_place * diag_width
    full_diag, full_parent = (
        lax.all_gather(diag_inverse, "col", axis=1, tiled=True),
        lax.all_gather(parent_factor, "col", axis=1, tiled=True),
    )
    masks = [
        row_weights(listed[member], row_place * rows_here, rows_here, width) for member in range(3)
    ]
    factors = [factor_cols[member] * masks[member][:, None] for member in range(3)]
    group_masks = [
        lax.dynamic_slice_in_dim(masks[member], col_place * group, group, 0) for member in range(3)
    ]
    pieces = [
        lax.dynamic_slice_in_dim(factors[member], col_place * group, group, 0)
        for member in range(3)
    ]

    def column_pass(members, extra_rows):
        slices = [
            lax.dynamic_slice_in_dim(factors[member], col_place % ratio * cols_here, cols_here, 0)
            for member in members
        ]
        stacked = jnp.stack(slices, axis=1)
        received = broadcast(stacked, "row", col_place // ratio)
        right_side = received.reshape(cols_here, len(members) * width)
        full_product = matmul_plain(region_inverse, right_side)
        terms = []
        for place, member in enumerate(members):
            diag_term = matmul_left(factors[member], full_product)
            if extra_rows[place] is not None:
                diag_term = diag_term + matmul_left(pieces[member], extra_rows[place])
            terms.append(diag_term)
        summed = lax.psum_scatter(full_product, "col", scatter_dimension=0, tiled=True)
        outputs = []
        for place, member in enumerate(members):
            partial_sum = summed
            if extra_rows[place] is not None:
                partial_sum = partial_sum + extra_rows[place]
            outputs.append(-partial_sum * group_masks[member][:, None])
        return (outputs, terms)

    parent_out, parent_terms = column_pass([0], [None])
    parent_col = parent_out[0]
    parent_totals = total_sums(parent_terms)
    parent_diag = full_diag[0] + parent_totals[0]
    parent_slice = lax.dynamic_slice_in_dim(parent_diag, diag_start, diag_width, 0)
    links = [full_parent[0], full_parent[1]]
    extra_rows = [matmul_plain(parent_col, links[place]) for place in range(2)]
    extra_sums = [matmul_left(parent_col, pieces[place + 1]) for place in range(2)]
    child_cols = []
    diag_list = [parent_slice]
    upper_list = []
    for place in range(2):
        outputs, terms = column_pass([place + 1], [extra_rows[place]])
        child_cols.append(outputs[0])
        link_terms = [extra_sums[place]]
        places = [place]
        count = len(places)
        diags = []
        uppers = []
        totals = total_sums(list(terms) + list(link_terms))
        for k, finish_place in enumerate(places):
            link_cols = lax.dynamic_slice_in_dim(links[finish_place], diag_start, diag_width, 1)
            upper_total = totals[count + k]
            upper_slice = -(
                lax.dynamic_slice_in_dim(upper_total, diag_start, diag_width, 0)
                + matmul_plain(parent_slice, links[finish_place])
            )
            weighted_diag = matmul_left(link_cols, parent_diag)
            link_upper = -(
                matmul_left(link_cols, upper_total)
                + matmul_plain(weighted_diag, links[finish_place])
            )
            diag_rows = lax.dynamic_slice_in_dim(
                full_diag[finish_place + 1], diag_start, diag_width, 0
            )
            total_rows = lax.dynamic_slice_in_dim(totals[k], diag_start, diag_width, 0)
            diags.append(diag_rows + total_rows - link_upper)
            uppers.append(upper_slice)
        diags, uppers = (diags, uppers)
        diag_list = diag_list + diags
        upper_list = upper_list + uppers
    col_blocks = jnp.stack([parent_col] + child_cols)
    diag_blocks = jnp.stack(diag_list)
    parent_rows = jnp.stack(upper_list)
    return (col_blocks, diag_blocks, parent_rows)


def solution(mesh):
    in_specs = (
        P("row", "col"),
        P(None, "row", None),
        P(None, "col", None),
        P(None, "col", None),
        P(),
    )
    out_specs = (P(None, ("row", "col"), None), P(None, "col", None), P(None, "col", None))
    return jax.shard_map(shards, mesh=mesh, in_specs=in_specs, out_specs=out_specs, check_vma=False)
```

profile of v0, /device:TPU:0, one launch (start us, length us, event | category | flops | bytes accessed | tf_op | source)
XLA Modules:
  0.0 360.3 jit_solution(12888149470342964404)
XLA Ops:
  8.0 0.0 copy-start
  8.0 0.0 all-reduce.7.cloned.1.call-start
  8.1 0.9 convert_bitcast_fusion.2
  9.0 0.1 select_reduce_fusion.1
  9.1 3.2 bitcast_multiply_fusion.1
  12.3 1.2 dynamic-slice_select_fusion.2
  13.5 2.2 dynamic-slice_select_fusion
  15.7 0.0 copy-done.7
  15.7 0.2 copy-done.9
  15.9 0.0 all-reduce.7.cloned.1.call-update
  15.9 0.0 all-gather.3.cloned.1.call-start
  15.9 0.5 all-gather.3.cloned.1.call-update
  16.5 0.0 reduce-scatter.4.cloned.1.call-start
  16.5 89.8 %all-reduce.7.cloned.1.call-done = (f32[512,512]{1,0:T(8,128)}, f32[512,512]{1,0:T(8,128)}, f32[512,512]{1,0:T(8,128)}) async-done(((f32[512,512]{1,0:T(8,128)}, f32[512,512]{1,0:T(8,128)}, f32[512,512]{1,0:T(8,128)}), (f32[512,512]{1,0:T(8,128)}, f32[512,512]{1,0:T(8,128)}, f32[512,512]{1,0:T(8,128)})) %all-reduce.7.cloned.1.call-update) | async-done | bytes 3145744 | tf_op jit(solution)/shard_map/psum | solution.py:9
  106.4 9.3 %fusion.67 = f32[512,1024]{1,0:T(8,128)} fusion(f32[512,512]{1,0:T(8,128)} %get-tuple-element.18, f32[1024,512]{1,0:T(8,128)S(1)} %copy-done), kind=kOutput, calls=%fused_computation.102 | convolution fusion | flops 3221225472 | bytes 5242880 | tf_op jit(solution)/shard_map/dot_general | solution.py:13
  115.6 0.0 reduce-scatter.4.cloned.1.call-update
  115.6 0.0 all-gather.5.cloned.1.call-start
  115.7 0.5 all-gather.5.cloned.1.call-update
  116.2 0.3 reduce-scatter.8.cloned.1.call-start
  116.6 0.3 copy-done.16
  116.8 8.0 %fusion.69 = f32[512,1024]{1,0:T(8,128)} fusion(f32[512,512]{1,0:T(8,128)S(1)} %copy-done.16, f32[1024,512]{1,0:T(8,128)S(1)} %copy-done), kind=kOutput, calls=%fused_computation.104 | convolution fusion | flops 3221225472 | bytes 5242880 | tf_op jit(solution)/shard_map/dot_general | solution.py:13
  124.9 0.0 reduce-scatter.8.cloned.1.call-update
  124.9 0.6 reduce-scatter.6.cloned.1.call-start
  125.5 0.6 copy-done.15
  126.1 8.2 %fusion.68 = f32[512,1024]{1,0:T(8,128)} fusion(f32[512,512]{1,0:T(8,128)S(1)} %copy-done.15, f32[1024,512]{1,0:T(8,128)S(1)} %copy-done), kind=kOutput, calls=%fused_computation.103 | convolution fusion | flops 3221225472 | bytes 5242880 | tf_op jit(solution)/shard_map/dot_general | solution.py:13
  134.2 0.0 reduce-scatter.6.cloned.1.call-update
  134.3 0.2 all-reduce.5.cloned.1.call-start
  134.5 0.1 dynamic_slice.60
  134.6 10.0 %fusion.70 = f32[512,512]{1,0:T(8,128)} fusion(f32[1024,512]{1,0:T(8,128)} %copy-done.9, f32[512,1024]{1,0:T(8,128)} %fusion.67), kind=kOutput, calls=%fused_computation.105 | convolution fusion | flops 3221225472 | bytes 5242880 | tf_op jit(solution)/shard_map/dot_general | solution.py:17
  144.5 6.8 %reduce-scatter.4.cloned.1.call-done = f32[128,512]{0,1:T(8,128)} async-done(((f32[1024,512]{0,1:T(8,128)}), f32[128,512]{0,1:T(8,128)}) %reduce-scatter.4.cloned.1.call-update) | async-done | bytes 262160 | tf_op jit(solution)/shard_map/reduce_scatter | solution.py:82
  151.3 2.2 fusion.13
  153.5 2.1 fusion.31
  155.7 1.8 fusion.17
  157.5 1.0 fusion.37
  158.6 2.9 fusion.29
  161.5 2.0 fusion.35
  163.5 8.1 %convolution_add_fusion = f32[512,512]{1,0:T(8,128)} fusion(f32[512,512]{1,0:T(8,128)S(1)} %fusion.31, f32[1024,512]{1,0:T(8,128)S(1)} %copy-done.8, f32[512,1024]{1,0:T(8,128)S(1)} %copy-done.3), kind=kOutput, calls=%fused_computation.3 | convolution fusion | flops 3221487616 | bytes 6291456 | tf_op jit(solution)/shard_map/dot_general | solution.py:17
  171.5 8.1 %convolution_add_fusion.1 = f32[512,512]{1,0:T(8,128)} fusion(f32[512,512]{1,0:T(8,128)S(1)} %fusion.37, f32[1024,512]{1,0:T(8,128)S(1)} %copy-done.6, f32[512,1024]{1,0:T(8,128)S(1)} %copy-done.4), kind=kOutput, calls=%fused_computation.4 | convolution fusion | flops 3221487616 | bytes 6291456 | tf_op jit(solution)/shard_map/dot_general | solution.py:17
  179.7 0.0 all-reduce.5.cloned.1.call-update
  179.7 0.1 dynamic_slice.64
  179.8 0.1 dynamic_slice.62
  179.8 3.0 fusion.66
  182.9 7.2 %all-gather.5.cloned.1.call-done = f32[3,512,512]{2,1,0:T(8,128)} async-done(((f32[3,64,512]{2,1,0:T(8,128)}), f32[3,512,512]{2,1,0:T(8,128)}) %all-gather.5.cloned.1.call-update) | async-done | bytes 3145744 | tf_op jit(solution)/shard_map/all_gather | solution.py:52
  190.0 3.1 fusion.65
  193.2 0.1 copy.12
  193.3 0.1 copy.11
  193.5 42.0 %reduce-scatter.8.cloned.1.call-done = f32[128,512]{0,1:T(8,128)} async-done(((f32[1024,512]{0,1:T(8,128)}), f32[128,512]{0,1:T(8,128)}) %reduce-scatter.8.cloned.1.call-update) | async-done | bytes 262160 | tf_op jit(solution)/shard_map/reduce_scatter | solution.py:82
  235.5 1.7 multiply_bitcast_fusion
  237.1 37.8 %reduce-scatter.6.cloned.1.call-done = f32[128,512]{0,1:T(8,128)} async-done(((f32[1024,512]{0,1:T(8,128)}), f32[128,512]{0,1:T(8,128)}) %reduce-scatter.6.cloned.1.call-update) | async-done | bytes 262160 | tf_op jit(solution)/shard_map/reduce_scatter | solution.py:82
  275.0 1.0 multiply_bitcast_fusion.1
  275.9 1.0 pad_maximum_fusion
  277.0 1.1 copy.13
  278.1 62.7 %all-reduce.5.cloned.1.call-done = (f32[512,512]{1,0:T(8,128)}, f32[512,512]{1,0:T(8,128)}, f32[512,512]{1,0:T(8,128)}, f32[512,512]{1,0:T(8,128)}, f32[512,512]{1,0:T(8,128)}) async-done(((f32[512,512]{1,0:T(8,128)}, f32[512,512]{1,0:T(8,128)}, f32[512,512]{1,0:T(8,128)}, f32[512,512]{1,0:T(8,128)}, f32[512,512]{1,0:T(8,128)}), (f32[512,512]{1,0:T(8,128)}, f32[512,512]{1,0:T(8,128)}, f32[512,512]{1,0:T(8,128)}, ...) | async-done | bytes 5242896 | tf_op jit(solution)/shard_map/psum | solution.py:37
  340.8 1.8 fusion.10
  342.7 0.8 fusion.19
  343.5 0.8 fusion.21
  344.3 0.8 fusion.23
  345.1 0.8 fusion.25
  345.8 0.7 fusion.1
  346.6 0.8 fusion.3
  347.3 0.7 pad_maximum_fusion.2
  348.1 1.7 fusion.9
  349.8 1.7 fusion.7
  351.5 0.8 pad_maximum_fusion.1
  (33 shorter events, 0.1 us)
Async XLA Ops:
  8.0 98.4 %copy-start = (f32[1024,512]{1,0:T(8,128)S(1)}, f32[1024,512]{1,0:T(8,128)}, u32[]{:S(2)}) copy-start(f32[1024,512]{1,0:T(8,128)} %param.5) | copy-start | bytes 6291460
  8.0 98.3 %all-reduce.7.cloned.1.call-start = ((), (), s32[]{:S(2)}) async-start(), calls=%async_computation.9 | async-start | bytes 6291456 | tf_op jit(solution)/shard_map/psum | solution.py:9
  12.3 3.4 copy-start.5
  12.3 3.4 copy-start.7
  12.3 3.6 copy-start.9
  15.9 128.6 %all-gather.3.cloned.1.call-start = ((), (), s32[]{:S(2)}) async-start(), calls=%async_computation.5 | async-start | bytes 2359296 | tf_op jit(solution)/shard_map/all_gather | solution.py:53
  16.5 134.8 %reduce-scatter.4.cloned.1.call-start = ((), (), s32[]{:S(2)}) async-start(), calls=%async_computation.3 | async-start | bytes 2359296 | tf_op jit(solution)/shard_map/reduce_scatter | solution.py:82
  115.6 1.2 copy-start.16
  115.6 74.4 %all-gather.5.cloned.1.call-start = ((), (), s32[]{:S(2)}) async-start(), calls=%async_computation.7 | async-start | bytes 3538944 | tf_op jit(solution)/shard_map/all_gather | solution.py:52
  116.2 119.2 %reduce-scatter.8.cloned.1.call-start = ((), (), s32[]{:S(2)}) async-start(), calls=%async_computation.6 | async-start | bytes 2359296 | tf_op jit(solution)/shard_map/reduce_scatter | solution.py:82
  124.8 1.2 copy-start.15
  124.9 150.1 %reduce-scatter.6.cloned.1.call-start = ((), (), s32[]{:S(2)}) async-start(), calls=%async_computation.4 | async-start | bytes 2359296 | tf_op jit(solution)/shard_map/reduce_scatter | solution.py:82
  134.3 206.6 %all-reduce.5.cloned.1.call-start = ((), (), s32[]{:S(2)}) async-start(), calls=%async_computation.8 | async-start | bytes 10485760 | tf_op jit(solution)/shard_map/psum | solution.py:37
  151.3 4.4 %copy-start.1 = (f32[2,512,512]{2,1,0:T(8,128)S(1)}, f32[2,512,512]{2,1,0:T(8,128)}, u32[]{:S(2)}) copy-start(f32[2,512,512]{2,1,0:T(8,128)} %all-gather.3.cloned.1.call-done) | copy-start | bytes 6291460
  151.3 6.2 %copy-start.6 = (f32[1024,512]{1,0:T(8,128)S(1)}, f32[1024,512]{1,0:T(8,128)}, u32[]{:S(2)}) copy-start(f32[1024,512]{1,0:T(8,128)} %copy-done.5) | copy-start | bytes 6291460
  153.5 5.0 %copy-start.8 = (f32[1024,512]{1,0:T(8,128)S(1)}, f32[1024,512]{1,0:T(8,128)}, u32[]{:S(2)}) copy-start(f32[1024,512]{1,0:T(8,128)} %copy-done.7) | copy-start | bytes 6291460
  155.7 5.8 %copy-start.10 = (f32[128,512]{0,1:T(8,128)S(1)}, f32[128,512]{0,1:T(8,128)}, u32[]{:S(2)}) copy-start(f32[128,512]{0,1:T(8,128)} %reduce-scatter.4.cloned.1.call-done) | copy-start | bytes 786436
  157.5 6.0 %copy-start.3 = (f32[512,1024]{1,0:T(8,128)S(1)}, f32[512,1024]{1,0:T(8,128)}, u32[]{:S(2)}) copy-start(f32[512,1024]{1,0:T(8,128)} %fusion.69) | copy-start | bytes 6291460
  163.5 8.1 %copy-start.4 = (f32[512,1024]{1,0:T(8,128)S(1)}, f32[512,1024]{1,0:T(8,128)}, u32[]{:S(2)}) copy-start(f32[512,1024]{1,0:T(8,128)} %fusion.68) | copy-start | bytes 6291460
  278.1 64.6 %copy-start.12 = (f32[1,512,512]{2,1,0:T(8,128)S(1)}, f32[1,512,512]{2,1,0:T(8,128)}, u32[]{:S(2)}) copy-start(f32[1,512,512]{2,1,0:T(8,128)} %get-tuple-element.26) | copy-start | bytes 3145732
  340.8 2.7 copy-start.14
  342.7 1.6 copy-start.11
  342.7 2.3 copy-start.13
  343.5 2.3 copy-start.2
Sparse Core Ops, SparseCore 0:
  16.0 90.2 all-reduce.6
  179.8 161.0 all-reduce.4
Sparse Core Ops, SparseCore 1:
  18.0 31.7 all-gather.2
  115.7 35.5 reduce-scatter.3
  152.9 37.1 all-gather.4
  192.5 42.9 reduce-scatter.7
  237.9 37.0 reduce-scatter.5
where the time goes:
time: 367 us; the launch traced here: 360 us
  waiting for transfers between devices  247 us (67%)
  matrix products  71.6 us (20%)
  between operations  16.4 us (4%)
  other arithmetic  14.5 us (4%)
  local copies, waits for them, and re-layouts  8.96 us (2%)
    psum x1, waiting for transfers between devices, broadcast(): return lax.psum(kept, axis)  89.8 us
    reduce_scatter x3, waiting for transfers between devices, column_pass(): lax.psum_scatter(full_product, 'col', scatter_dimension=0, tiled=True)  86.6 us
    psum x1, waiting for transfers between devices, total_sums(): return lax.psum(tuple(values), ('row', 'col'))  62.7 us
    dot_general x11, matrix products, matmul_left(): lax.dot_general(left, right, (((0,), (0,)), ((), ())), precision=lax.Prec...  37.3 us
    dot_general x9, matrix products, matmul_plain(): jnp.dot(left, right, precision=lax.Precision.HIGHEST, preferred_element_t...  34.4 us
  transfers between devices with their start and end apart: 7, of which 6 were waited for; matrix products, arithmetic and copies ran while one was open for 21% of the time, Pallas kernels for 0%

commit v1 on v0

v1 whole, which is shorter than its diff:
```python
import jax
import jax.numpy as jnp
from jax import lax
from jax.sharding import PartitionSpec as P

AXES = ("row", "col")
HIGH = lax.Precision.HIGH


def dot(left, right):
    return jnp.dot(left, right, precision=HIGH, preferred_element_type=jnp.float32)


def dot_left(left, right):
    return lax.dot_general(
        left, right, (((0,), (0,)), ((), ())), precision=HIGH, preferred_element_type=jnp.float32
    )


def gray(place):
    return place ^ (place >> 1)


def reversed_bits(count):
    order = [0]
    step = 1
    while step < count:
        order = [value + bit * step for value in order for bit in (0, 1)]
        step *= 2
    return order


def row_weights(listed_row, first_row, count, width):
    block_ids = (first_row + lax.iota(jnp.int32, count)) // width
    table = lax.iota(jnp.int32, listed_row.shape[0])
    hits = (block_ids[:, None] == table[None, :]) & (listed_row[None, :] != 0)
    return jnp.any(hits, axis=1).astype(jnp.float32)


def swap(value, axis, size, bit):
    return lax.ppermute(value, axis, [(place, place ^ (1 << bit)) for place in range(size)])


def shards(region_inverse, factor_cols, parent_factor, diag_inverse, listed):
    row_count = lax.axis_size("row")
    col_count = lax.axis_size("col")
    row_place = lax.axis_index("row")
    col_place = lax.axis_index("col")
    row_bits = row_count.bit_length() - 1
    col_bits = col_count.bit_length() - 1
    rows_here, cols_here = region_inverse.shape
    members, _, width = factor_cols.shape
    group = rows_here // col_count
    ratio = col_count // row_count
    diag_width = width // col_count
    first_row = row_place * rows_here
    source = col_place // ratio

    gathered = lax.all_gather(
        jnp.concatenate([parent_factor, diag_inverse[:1]]), "col", axis=1, tiled=True
    )
    links, full_diag = gathered[:2], gathered[2]

    order = reversed_bits(col_count)
    relative = jnp.array(order, jnp.int32) ^ col_place
    region = jnp.take(region_inverse.reshape(col_count, group, cols_here), relative, axis=0)
    region = region.reshape(rows_here, cols_here)

    own_first = first_row + col_place * group
    own_masks = [row_weights(listed[j], own_first, group, width)[:, None] for j in range(members)]
    own = [
        lax.dynamic_slice_in_dim(factor_cols[j], col_place * group, group, 0) * own_masks[j]
        for j in range(members)
    ]

    def ring(step, forward):
        pairs = []
        for col in range(col_count):
            start = col // ratio
            at = step if forward else -step % row_count
            to = step + 1 if forward else (-step - 1) % row_count
            pairs.append(
                ((start ^ gray(at)) * col_count + col, (start ^ gray(to)) * col_count + col)
            )
        return pairs

    is_source = row_place == source
    col_first = col_place * cols_here

    def received(j):
        block = lax.dynamic_slice_in_dim(
            factor_cols[j], (col_place % ratio) * cols_here, cols_here, 0
        )
        half = cols_here // 2
        parts = []
        for piece, forward in ((block[:half], True), (block[half:], False)):
            total = jnp.where(is_source, piece, 0)
            moving = piece
            for step in range(row_count - 1):
                moving = lax.ppermute(moving, AXES, ring(step, forward))
                total = total + moving
            parts.append(total)
        mask = row_weights(listed[j], col_first, cols_here, width)[:, None]
        return jnp.concatenate(parts) * mask

    def column_sums(j):
        right = received(j)
        keep = None
        size = rows_here // 2
        send = dot(region[size:], right)
        keep = dot(region[:size], right)
        for bit in range(col_bits):
            arrived = swap(send, "col", col_count, bit)
            if bit + 1 < col_bits:
                size //= 2
                send = keep[size:] + arrived[size:]
                keep = keep[:size] + arrived[:size]
            else:
                keep = keep + arrived
        return keep

    def total_rows(matrices):
        count = len(matrices)
        stacked = jnp.stack(matrices).reshape(count, col_count, diag_width, width)
        stacked = jnp.take(stacked, relative, axis=1).transpose(1, 0, 2, 3)
        stacked = stacked.reshape(col_count, count * diag_width, width)
        half = col_count // 2
        value = stacked[:half] + swap(stacked[half:], "col", col_count, 0)
        middle = count * diag_width // 2
        done = []
        for piece, bits in (
            (value[:, :middle], range(row_bits)),
            (value[:, middle:], range(row_bits - 1, -1, -1)),
        ):
            for bit in bits:
                size = piece.shape[1] // 2
                side = (row_place >> bit) & 1
                kept = lax.dynamic_slice_in_dim(piece, side * size, size, 1)
                sent = lax.dynamic_slice_in_dim(piece, (1 - side) * size, size, 1)
                piece = kept + swap(sent, "row", row_count, bit)
            for bit in range(1, col_bits):
                size = piece.shape[0] // 2
                piece = piece[:size] + swap(piece[size:], "col", col_count, bit)
            piece = piece[0]
            for bit in reversed(list(bits)):
                other = swap(piece, "row", row_count, bit)
                side = (row_place >> bit) & 1
                low = jnp.where(side == 0, piece, other)
                high = jnp.where(side == 0, other, piece)
                piece = jnp.concatenate([low, high])
            done.append(piece)
        return jnp.concatenate(done).reshape(count, diag_width, width)

    sums = [column_sums(j) for j in range(members)]
    parent_col = -sums[0] * own_masks[0]
    turned = [dot(parent_col, links[c]) for c in range(2)]
    lifted = [dot(own[0], links[c]) for c in range(2)]
    parent_terms = [-dot_left(own[0], parent_col)]
    for c in range(2):
        parent_terms.append(dot_left(own[0], turned[c]) - dot_left(parent_col, own[c + 1]))
    parent_totals = total_rows(parent_terms)
    child_cols = []
    child_terms = []
    for c in range(2):
        column = -(sums[c + 1] + turned[c]) * own_masks[c + 1]
        child_cols.append(column)
        left = jnp.concatenate([own[c + 1], turned[c], lifted[c]])
        right = jnp.concatenate([-column, own[c + 1], -turned[c]])
        child_terms.append(dot_left(left, right))
    child_totals = total_rows(child_terms)

    start = col_place * diag_width
    uppers = []
    diags = [diag_inverse[0] + parent_totals[0]]
    for c in range(2):
        uppers.append(parent_totals[1 + c] - dot(diag_inverse[0], links[c]))
        link_cols = lax.dynamic_slice_in_dim(links[c], start, diag_width, 1)
        framed = dot(dot_left(link_cols, full_diag), links[c])
        diags.append(diag_inverse[c + 1] + framed + child_totals[c])
    return jnp.stack([parent_col] + child_cols), jnp.stack(diags), jnp.stack(uppers)


def solution(mesh):
    in_specs = (
        P("row", "col"),
        P(None, "row", None),
        P(None, "col", None),
        P(None, "col", None),
        P(),
    )
    out_specs = (P(None, ("row", "col"), None), P(None, "col", None), P(None, "col", None))
    return jax.shard_map(shards, mesh=mesh, in_specs=in_specs, out_specs=out_specs, check_vma=False)
```

time: 367 us -> 286 us (0.78); the launches traced: 360 us -> 285 us
  waiting for transfers between devices: 247 us -> 86.8 us
  starting transfers between devices: 1.28 us -> 95.9 us
  matrix products: 71.6 us -> 24.8 us
  other arithmetic: 14.5 us -> 34.4 us
  local copies, waits for them, and re-layouts: 8.96 us -> 28.1 us
    psum x2 -> x0, waiting for transfers between devices: 153 us -> none  [the longest x1 89.8 us: broadcast(): return lax.psum(kept, axis)]
    ppermute x0 -> x53, starting transfers between devices: none -> 95.9 us  [the longest x35 66.1 us: swap(): lax.ppermute(value, axis, [(place, place ^ 1 << bit) for place in range(s...]
    ppermute x0 -> x53, waiting for transfers between devices: none -> 86.8 us  [the longest x35 75.6 us: swap(): lax.ppermute(value, axis, [(place, place ^ 1 << bit) for place in range(s...]
    reduce_scatter x3 -> x0, waiting for transfers between devices: 86.6 us -> none  [column_pass(): lax.psum_scatter(full_product, 'col', scatter_dimension=0, tiled=True)]
    dot_general x20 -> x23, matrix products: 71.6 us -> 24.8 us  [the longest x14 15.4 us: dot(): jnp.dot(left, right, precision=HIGH, preferred_element_type=jnp.float32)]
    add x1 -> x27, other arithmetic: 1.84 us -> 15.8 us  [the longest x6 9.2 us: received(): total = total + moving]
    gather x0 -> x3, local copies, waits for them, and re-layouts: none -> 10 us  [the longest x2 7.94 us: total_rows(): stacked = jnp.take(stacked, relative, axis=1).transpose(1, 0, 2, 3)]
    slice x2 -> x20, local copies, waits for them, and re-layouts: 6.16 us -> 14.1 us  [the longest x1 5.8 us: received(): factor_cols[j]]
  transfers between devices with their start and end apart: 7 -> 54, of which waited for: 6 -> 25; matrix products, arithmetic and copies ran while one was open for 21% -> 18% of each run, Pallas kernels for 0% -> 0%
where the time goes in v1:
time: 286 us; the launch traced here: 285 us
  starting transfers between devices  95.9 us (34%)
  waiting for transfers between devices  86.8 us (30%)
  other arithmetic  34.4 us (12%)
  local copies, waits for them, and re-layouts  28.1 us (10%)
  matrix products  24.8 us (9%)
  between operations  15.1 us (5%)
    ppermute x35, waiting for transfers between devices, swap(): lax.ppermute(value, axis, [(place, place ^ 1 << bit) for place in range(s...  75.6 us
    ppermute x35, starting transfers between devices, swap(): lax.ppermute(value, axis, [(place, place ^ 1 << bit) for place in range(s...  66.1 us
    ppermute x18, starting transfers between devices, received(): moving = lax.ppermute(moving, AXES, ring(step, forward))  29.8 us
    dot_general x14, matrix products, dot(): jnp.dot(left, right, precision=HIGH, preferred_element_type=jnp.float32)  15.4 us
    ppermute x18, waiting for transfers between devices, received(): moving = lax.ppermute(moving, AXES, ring(step, forward))  11.2 us
    dot_general x9, matrix products, dot_left(): lax.dot_general(left, right, (((0,), (0,)), ((), ())), precision=HIGH, pr...  9.4 us
    add x6, other arithmetic, received(): total = total + moving  9.2 us
    gather x2, local copies, waits for them, and re-layouts, total_rows(): stacked = jnp.take(stacked, relative, axis=1).transpose(1, 0, 2, 3)  7.94 us
  transfers between devices with their start and end apart: 54, of which 25 were waited for; matrix products, arithmetic and copies ran while one was open for 18% of the time, Pallas kernels for 0%

profile of v1, /device:TPU:0, one launch (start us, length us, event | category | flops | bytes accessed | tf_op | source)
XLA Modules:
  0.0 285.1 jit_solution(7280137399525426213)
XLA Ops:
  7.2 5.8 %fusion.149 = (f32[1,1024,512]{2,1,0:T(8,128)}, f32[1,1024,512]{2,1,0:T(8,128)}, f32[1,1024,512]{2,1,0:T(8,128)}) fusion(f32[3,1024,512]{2,1,0:T(8,128)} %param.7), kind=kLoop, calls=%fused_computation.254 | loop fusion | bytes 12582912 | tf_op jit(solution)/shard_map/slice | solution.py:92
  13.1 2.4 dynamic-slice_bitcast_fusion.3
  15.4 5.7 %collective-permute-start.12 = (f32[256,512]{1,0:T(8,128)}, f32[256,512]{1,0:T(8,128)}, u32[]{:S(2)}, u32[]{:S(2)}) collective-permute-start(f32[256,512]{1,0:T(8,128)} %get-tuple-element.27), channel_id=1, source_target_pairs={{0,16},{1,17},{10,26},{11,27},{20,4},{21,5},{30,14},{31,15}} | collective-permute-start | bytes 1572872 | tf_op jit(solution)/shard_map/ppermute | solution.py:100
  21.1 2.1 collective-permute-start.9
  24.1 2.2 collective-permute-start
  26.3 2.1 collective-permute-start.3
  29.2 2.1 dynamic-slice_bitcast_fusion.1
  31.3 2.1 collective-permute-start.18
  33.5 2.1 gather_fusion
  35.6 2.6 collective-permute-start.21
  39.6 6.7 %collective-permute-done = f32[256,512]{1,0:T(8,128)} collective-permute-done((f32[256,512]{1,0:T(8,128)}, f32[256,512]{1,0:T(8,128)}, u32[]{:S(2)}, u32[]{:S(2)}) %collective-permute-start) | collective-permute-done | bytes 524320 | tf_op jit(solution)/shard_map/ppermute | solution.py:100
  46.3 1.5 collective-permute-start.10
  48.5 3.4 %broadcast_select_fusion.2 = f32[8,128,512]{2,1,0:T(8,128)} fusion(f32[8,128,512]{2,1,0:T(8,128)} %gather_fusion, pred[8]{0:T(512)(128)(4,1)S(1)} %get-tuple-element.13), kind=kLoop, calls=%fused_computation.32 | loop fusion | flops 524288 | bytes 4194312 | tf_op jit(solution)/shard_map/jit(_take)/select_n | solution.py:66
  51.9 4.5 %collective-permute-done.18 = f32[256,512]{1,0:T(8,128)} collective-permute-done((f32[256,512]{1,0:T(8,128)}, f32[256,512]{1,0:T(8,128)}, u32[]{:S(2)}, u32[]{:S(2)}) %collective-permute-start.18) | collective-permute-done | bytes 524320 | tf_op jit(solution)/shard_map/ppermute | solution.py:100
  57.8 1.5 collective-permute-start.19
  59.3 1.5 collective-permute-start.22
  60.7 1.5 collective-permute-start.14
  63.8 1.8 fusion.153
  68.7 1.7 add_add_fusion.2
  70.4 1.6 add_add_fusion.3
  77.8 1.6 add_add_fusion.1
  86.4 28.4 %collective-permute-start.7 = (f32[256,512]{1,0:T(8,128)}, f32[256,512]{1,0:T(8,128)}, u32[]{:S(2)}, u32[]{:S(2)}) collective-permute-start(f32[256,512]{1,0:T(8,128)} %get-tuple-element.33), channel_id=1, source_target_pairs={{0,2},{1,3},{2,0},{3,1},{4,6},{5,7},{6,4},{7,5},{8,10},{9,11},{10,... | collective-permute-start | bytes 1572872 | tf_op jit(solution)/shard_map/ppermute | solution.py:41
  116.8 2.0 collective-permute-start.25
  119.0 8.8 %collective-permute-done.7 = f32[256,512]{1,0:T(8,128)} collective-permute-done((f32[256,512]{1,0:T(8,128)}, f32[256,512]{1,0:T(8,128)}, u32[]{:S(2)}, u32[]{:S(2)}) %collective-permute-start.7) | collective-permute-done | bytes 524320 | tf_op jit(solution)/shard_map/ppermute | solution.py:41
  128.8 4.6 %collective-permute-start.8 = (f32[128,512]{1,0:T(8,128)S(1)}, f32[128,512]{1,0:T(8,128)S(1)}, u32[]{:S(2)}, u32[]{:S(2)}) collective-permute-start(f32[128,512]{1,0:T(8,128)S(1)} %slice_add_fusion.10), channel_id=1, source_target_pairs={{0,4},{1,5},{2,6},{3,7},{4,0},{5,1},{6,2},{7,3},{8,12},{9,13},{10,... | collective-permute-start | bytes 786440 | tf_op jit(solution)/shard_map/ppermute | solution.py:41
  133.4 11.1 %collective-permute-done.16 = f32[256,512]{1,0:T(8,128)S(1)} collective-permute-done((f32[256,512]{1,0:T(8,128)}, f32[256,512]{1,0:T(8,128)S(1)}, u32[]{:S(2)}, u32[]{:S(2)}) %collective-permute-start.16) | collective-permute-done | bytes 524320 | tf_op jit(solution)/shard_map/ppermute | solution.py:41
  145.4 2.5 collective-permute-start.17
  147.9 12.8 %collective-permute-done.25 = f32[256,512]{1,0:T(8,128)S(1)} collective-permute-done((f32[256,512]{1,0:T(8,128)}, f32[256,512]{1,0:T(8,128)S(1)}, u32[]{:S(2)}, u32[]{:S(2)}) %collective-permute-start.25) | collective-permute-done | bytes 524320 | tf_op jit(solution)/shard_map/ppermute | solution.py:41
  162.5 1.6 convolution_negate_fusion
  164.3 1.7 fusion.10
  166.0 1.6 fusion.68
  167.6 4.2 %collective-permute-done.17 = f32[128,512]{1,0:T(8,128)S(1)} collective-permute-done((f32[128,512]{1,0:T(8,128)}, f32[128,512]{1,0:T(8,128)S(1)}, u32[]{:S(2)}, u32[]{:S(2)}) %collective-permute-start.17) | collective-permute-done | bytes 262176 | tf_op jit(solution)/shard_map/ppermute | solution.py:41
  171.9 2.1 fusion.145
  174.6 1.7 fusion.4
  176.3 1.6 fusion.67
  178.0 2.2 fusion.147
  180.9 2.1 pad_maximum_fusion
  183.0 4.4 %gather_fusion.1 = f32[8,3,64,512]{3,2,1,0:T(8,128)} fusion(f32[3,8,64,512]{3,2,1,0:T(8,128)} %pad_maximum_fusion, s32[1024]{0:T(1024)S(1)} %pad_clamp_fusion), kind=kCustom, calls=%fused_computation.1 | custom fusion | bytes 6291488 | tf_op jit(solution)/shard_map/jit(_take)/gather | solution.py:125
  187.3 1.7 fusion.7
  190.2 1.8 fusion.2
  193.0 1.6 pad_maximum_fusion.1
  194.6 3.6 %gather_fusion.2 = f32[8,2,64,512]{3,2,1,0:T(8,128)} fusion(f32[2,8,64,512]{3,2,1,0:T(8,128)} %pad_maximum_fusion.1, s32[1024]{0:T(1024)S(1)} %pad_clamp_fusion), kind=kCustom, calls=%fused_computation.2 | custom fusion | bytes 4194336 | tf_op jit(solution)/shard_map/jit(_take)/gather | solution.py:125
  198.2 1.9 broadcast_select_fusion.1
  200.4 1.6 copy-done.3
  205.6 2.8 collective-permute-start.35
  209.9 1.7 collective-permute-start.41
  211.6 2.4 collective-permute-done.35
  214.1 2.4 collective-permute-start.36
  216.5 1.9 collective-permute-done.41
  220.0 3.6 %collective-permute-done.42 = f32[4,16,512]{2,1,0:T(8,128)S(1)} collective-permute-done((f32[4,16,512]{2,1,0:T(8,128)S(1)}, f32[4,16,512]{2,1,0:T(8,128)S(1)}, u32[]{:S(2)}, u32[]{:S(2)}) %collective-permute-start.42) | collective-permute-done | bytes 131104 | tf_op jit(solution)/shard_map/ppermute | solution.py:41
  224.3 1.7 collective-permute-start.38
  226.0 1.9 collective-permute-done.43
  229.2 1.7 collective-permute-start.39
  230.8 2.2 collective-permute-done.44
  235.1 2.2 collective-permute-done.45
  237.3 1.6 collective-permute-start.46
  242.1 8.0 %collective-permute-done.28 = f32[4,48,512]{2,1,0:T(8,128)S(1)} collective-permute-done((f32[4,48,512]{2,1,0:T(8,128)S(1)}, f32[4,48,512]{2,1,0:T(8,128)S(1)}, u32[]{:S(2)}, u32[]{:S(2)}) %collective-permute-start.28) | collective-permute-done | bytes 393248 | tf_op jit(solution)/shard_map/ppermute | solution.py:41
  252.3 3.6 %collective-permute-done.29 = f32[4,24,512]{2,1,0:T(8,128)S(1)} collective-permute-done((f32[4,24,512]{2,1,0:T(8,128)S(1)}, f32[4,24,512]{2,1,0:T(8,128)S(1)}, u32[]{:S(2)}, u32[]{:S(2)}) %collective-permute-start.29) | collective-permute-done | bytes 196640 | tf_op jit(solution)/shard_map/ppermute | solution.py:41
  258.2 2.5 collective-permute-done.30
  261.8 2.0 collective-permute-start.50
  263.8 2.0 collective-permute-done.31
  266.8 1.5 collective-permute-start.51
  268.4 1.7 collective-permute-done.32
  272.6 2.2 collective-permute-done.33
  (215 shorter events, 58.5 us)
Async XLA Ops:
  7.2 26.3 %copy-start = (f32[1024,512]{1,0:T(8,128)S(1)}, f32[1024,512]{1,0:T(8,128)}, u32[]{:S(2)}) copy-start(f32[1024,512]{1,0:T(8,128)} %param.6) | copy-start | bytes 6291460
  7.2 157.0 %all-gather.2.cloned.1.call-start = ((), (), s32[]{:S(2)}) async-start(), calls=%async_computation | async-start | bytes 3538944 | tf_op jit(solution)/shard_map/all_gather | solution.py:59
  13.0 10.2 %copy-start.4 = (f32[1,1024,512]{2,1,0:T(8,128)S(1)}, f32[1,1024,512]{2,1,0:T(8,128)}, u32[]{:S(2)}) copy-start(f32[1,1024,512]{2,1,0:T(8,128)} %get-tuple-element.16) | copy-start | bytes 6291460
  13.0 15.4 %slice-start = ((f32[3,64,512]{2,1,0:T(8,128)}), f32[1,64,512]{2,1,0:T(8,128)S(1)}, s32[]{:S(2)}) async-start(f32[3,64,512]{2,1,0:T(8,128)} %param.9), calls=%async_computation.1 | async-start | bytes 262144 | tf_op jit(solution)/shard_map/slice | solution.py:60
  13.1 15.4 %copy-start.21 = (f32[2,64,512]{2,1,0:T(8,128)S(1)}, f32[2,64,512]{2,1,0:T(8,128)}, u32[]{:S(2)}) copy-start(f32[2,64,512]{2,1,0:T(8,128)} %param.8) | copy-start | bytes 786436
  15.4 20.1 %collective-permute-start.12 = (f32[256,512]{1,0:T(8,128)}, f32[256,512]{1,0:T(8,128)}, u32[]{:S(2)}, u32[]{:S(2)}) collective-permute-start(f32[256,512]{1,0:T(8,128)} %get-tuple-element.27), channel_id=1, source_target_pairs={{0,16},{1,17},{10,26},{11,27},{20,4},{21,5},{30,14},{31,15}} | collective-permute-start | bytes 1572872 | tf_op jit(solution)/shard_map/ppermute | solution.py:100
  21.1 17.0 %collective-permute-start.9 = (f32[256,512]{1,0:T(8,128)}, f32[256,512]{1,0:T(8,128)}, u32[]{:S(2)}, u32[]{:S(2)}) collective-permute-start(f32[256,512]{1,0:T(8,128)} %get-tuple-element.26), channel_id=1, source_target_pairs={{0,8},{1,9},{10,2},{11,3},{20,28},{21,29},{30,22},{31,23}} | collective-permute-start | bytes 1572872 | tf_op jit(solution)/shard_map/ppermute | solution.py:100
  24.1 9.3 %copy-start.23 = (s32[8]{0:T(128)S(1)}, s32[8]{0:T(128)}, u32[]{:S(2)}) copy-start(s32[8]{0:T(128)} %constant.139.clone) | copy-start | bytes 100
  24.1 22.2 %collective-permute-start = (f32[256,512]{1,0:T(8,128)}, f32[256,512]{1,0:T(8,128)}, u32[]{:S(2)}, u32[]{:S(2)}) collective-permute-start(f32[256,512]{1,0:T(8,128)} %get-tuple-element.36), channel_id=1, source_target_pairs={{0,8},{1,9},{10,2},{11,3},{20,28},{21,29},{30,22},{31,23}} | collective-permute-start | bytes 1572872 | tf_op jit(solution)/shard_map/ppermute | solution.py:100
  26.3 21.4 %collective-permute-start.3 = (f32[256,512]{1,0:T(8,128)S(1)}, f32[256,512]{1,0:T(8,128)}, u32[]{:S(2)}, u32[]{:S(2)}) collective-permute-start(f32[256,512]{1,0:T(8,128)S(1)} %get-tuple-element.37), channel_id=1, source_target_pairs={{0,16},{1,17},{10,26},{11,27},{20,4},{21,5},{30,14},{31,15}} | collective-permute-start | bytes 1572872 | tf_op jit(solution)/shard_map/ppermute | solution.py:100
  31.3 25.0 %collective-permute-start.18 = (f32[256,512]{1,0:T(8,128)}, f32[256,512]{1,0:T(8,128)}, u32[]{:S(2)}, u32[]{:S(2)}) collective-permute-start(f32[256,512]{1,0:T(8,128)} %get-tuple-element.30), channel_id=1, source_target_pairs={{0,8},{1,9},{10,2},{11,3},{20,28},{21,29},{30,22},{31,23}} | collective-permute-start | bytes 1572872 | tf_op jit(solution)/shard_map/ppermute | solution.py:100
  33.5 14.3 %copy-start.22 = (s32[3,8]{1,0:T(4,128)S(1)}, s32[3,8]{1,0:T(4,128)}, u32[]{:S(2)}) copy-start(s32[3,8]{1,0:T(4,128)} %param.10) | copy-start | bytes 292
  35.6 22.2 %collective-permute-start.21 = (f32[256,512]{1,0:T(8,128)S(1)}, f32[256,512]{1,0:T(8,128)}, u32[]{:S(2)}, u32[]{:S(2)}) collective-permute-start(f32[256,512]{1,0:T(8,128)S(1)} %get-tuple-element.31), channel_id=1, source_target_pairs={{0,16},{1,17},{10,26},{11,27},{20,4},{21,5},{30,14},{31,15}} | collective-permute-start | bytes 1572872 | tf_op jit(solution)/shard_map/ppermute | solution.py:100
  38.1 21.1 %collective-permute-start.13 = (f32[256,512]{1,0:T(8,128)}, f32[256,512]{1,0:T(8,128)}, u32[]{:S(2)}, u32[]{:S(2)}) collective-permute-start(f32[256,512]{1,0:T(8,128)} %collective-permute-done.12), channel_id=1, source_target_pairs={{16,24},{17,25},{26,18},{27,19},{4,12},{5,13},{14,6},{15,7}} | collective-permute-start | bytes 1572872 | tf_op jit(solution)/shard_map/ppermute | solution.py:100
  46.3 14.5 %collective-permute-start.10 = (f32[256,512]{1,0:T(8,128)}, f32[256,512]{1,0:T(8,128)}, u32[]{:S(2)}, u32[]{:S(2)}) collective-permute-start(f32[256,512]{1,0:T(8,128)} %collective-permute-done.9), channel_id=1, source_target_pairs={{8,24},{9,25},{2,18},{3,19},{28,12},{29,13},{22,6},{23,7}} | collective-permute-start | bytes 1572872 | tf_op jit(solution)/shard_map/ppermute | solution.py:100
  47.7 14.6 %collective-permute-start.1 = (f32[256,512]{1,0:T(8,128)}, f32[256,512]{1,0:T(8,128)S(1)}, u32[]{:S(2)}, u32[]{:S(2)}) collective-permute-start(f32[256,512]{1,0:T(8,128)} %collective-permute-done), channel_id=1, source_target_pairs={{8,24},{9,25},{2,18},{3,19},{28,12},{29,13},{22,6},{23,7}} | collective-permute-start | bytes 1572872 | tf_op jit(solution)/shard_map/ppermute | solution.py:100
  56.4 9.3 %collective-permute-start.4 = (f32[256,512]{1,0:T(8,128)}, f32[256,512]{1,0:T(8,128)}, u32[]{:S(2)}, u32[]{:S(2)}) collective-permute-start(f32[256,512]{1,0:T(8,128)} %collective-permute-done.3), channel_id=1, source_target_pairs={{16,24},{17,25},{26,18},{27,19},{4,12},{5,13},{14,6},{15,7}} | collective-permute-start | bytes 1572872 | tf_op jit(solution)/shard_map/ppermute | solution.py:100
  57.8 8.5 %collective-permute-start.19 = (f32[256,512]{1,0:T(8,128)}, f32[256,512]{1,0:T(8,128)}, u32[]{:S(2)}, u32[]{:S(2)}) collective-permute-start(f32[256,512]{1,0:T(8,128)} %collective-permute-done.18), channel_id=1, source_target_pairs={{8,24},{9,25},{2,18},{3,19},{28,12},{29,13},{22,6},{23,7}} | collective-permute-start | bytes 1572872 | tf_op jit(solution)/shard_map/ppermute | solution.py:100
  59.3 7.8 %collective-permute-start.22 = (f32[256,512]{1,0:T(8,128)}, f32[256,512]{1,0:T(8,128)}, u32[]{:S(2)}, u32[]{:S(2)}) collective-permute-start(f32[256,512]{1,0:T(8,128)} %collective-permute-done.21), channel_id=1, source_target_pairs={{16,24},{17,25},{26,18},{27,19},{4,12},{5,13},{14,6},{15,7}} | collective-permute-start | bytes 1572872 | tf_op jit(solution)/shard_map/ppermute | solution.py:100
  60.7 7.0 %collective-permute-start.14 = (f32[256,512]{1,0:T(8,128)}, f32[256,512]{1,0:T(8,128)}, u32[]{:S(2)}, u32[]{:S(2)}) collective-permute-start(f32[256,512]{1,0:T(8,128)} %collective-permute-done.13), channel_id=1, source_target_pairs={{24,8},{25,9},{18,2},{19,3},{12,28},{13,29},{6,22},{7,23}} | collective-permute-start | bytes 1572872 | tf_op jit(solution)/shard_map/ppermute | solution.py:100
  63.1 7.3 %collective-permute-start.11 = (f32[256,512]{1,0:T(8,128)}, f32[256,512]{1,0:T(8,128)S(1)}, u32[]{:S(2)}, u32[]{:S(2)}) collective-permute-start(f32[256,512]{1,0:T(8,128)} %collective-permute-done.10), channel_id=1, source_target_pairs={{24,16},{25,17},{18,26},{19,27},{12,4},{13,5},{6,14},{7,15}} | collective-permute-start | bytes 1572872 | tf_op jit(solution)/shard_map/ppermute | solution.py:100
  65.6 7.6 %collective-permute-start.2 = (f32[256,512]{1,0:T(8,128)S(1)}, f32[256,512]{1,0:T(8,128)S(1)}, u32[]{:S(2)}, u32[]{:S(2)}) collective-permute-start(f32[256,512]{1,0:T(8,128)S(1)} %copy-done.20), channel_id=1, source_target_pairs={{24,16},{25,17},{18,26},{19,27},{12,4},{13,5},{6,14},{7,15}} | collective-permute-start | bytes 1572872 | tf_op jit(solution)/shard_map/ppermute | solution.py:100
  66.4 8.3 %collective-permute-start.5 = (f32[256,512]{1,0:T(8,128)}, f32[256,512]{1,0:T(8,128)S(1)}, u32[]{:S(2)}, u32[]{:S(2)}) collective-permute-start(f32[256,512]{1,0:T(8,128)} %collective-permute-done.4), channel_id=1, source_target_pairs={{24,8},{25,9},{18,2},{19,3},{12,28},{13,29},{6,22},{7,23}} | collective-permute-start | bytes 1572872 | tf_op jit(solution)/shard_map/ppermute | solution.py:100
  67.1 10.7 %collective-permute-start.20 = (f32[256,512]{1,0:T(8,128)}, f32[256,512]{1,0:T(8,128)S(1)}, u32[]{:S(2)}, u32[]{:S(2)}) collective-permute-start(f32[256,512]{1,0:T(8,128)} %collective-permute-done.19), channel_id=1, source_target_pairs={{24,16},{25,17},{18,26},{19,27},{12,4},{13,5},{6,14},{7,15}} | collective-permute-start | bytes 1572872 | tf_op jit(solution)/shard_map/ppermute | solution.py:100
  67.8 11.6 %collective-permute-start.23 = (f32[256,512]{1,0:T(8,128)}, f32[256,512]{1,0:T(8,128)S(1)}, u32[]{:S(2)}, u32[]{:S(2)}) collective-permute-start(f32[256,512]{1,0:T(8,128)} %collective-permute-done.22), channel_id=1, source_target_pairs={{24,8},{25,9},{18,2},{19,3},{12,28},{13,29},{6,22},{7,23}} | collective-permute-start | bytes 1572872 | tf_op jit(solution)/shard_map/ppermute | solution.py:100
  73.1 41.6 %collective-permute-start.15 = (f32[512,512]{1,0:T(8,128)S(1)}, f32[512,512]{1,0:T(8,128)S(1)}, u32[]{:S(2)}, u32[]{:S(2)}) collective-permute-start(f32[512,512]{1,0:T(8,128)S(1)} %fusion.16), channel_id=1, source_target_pairs={{0,1},{1,0},{2,3},{3,2},{4,5},{5,4},{6,7},{7,6},{8,9},{9,8},{10,11... | collective-permute-start | bytes 3145736 | tf_op jit(solution)/shard_map/ppermute | solution.py:41
  77.2 8.2 %collective-permute-start.6 = (f32[512,512]{1,0:T(8,128)S(1)}, f32[512,512]{1,0:T(8,128)S(1)}, u32[]{:S(2)}, u32[]{:S(2)}) collective-permute-start(f32[512,512]{1,0:T(8,128)S(1)} %fusion.18), channel_id=1, source_target_pairs={{0,1},{1,0},{2,3},{3,2},{4,5},{5,4},{6,7},{7,6},{8,9},{9,8},{10,11... | collective-permute-start | bytes 3145736 | tf_op jit(solution)/shard_map/ppermute | solution.py:41
  81.9 33.9 %collective-permute-start.24 = (f32[512,512]{1,0:T(8,128)S(1)}, f32[512,512]{1,0:T(8,128)S(1)}, u32[]{:S(2)}, u32[]{:S(2)}) collective-permute-start(f32[512,512]{1,0:T(8,128)S(1)} %fusion.14), channel_id=1, source_target_pairs={{0,1},{1,0},{2,3},{3,2},{4,5},{5,4},{6,7},{7,6},{8,9},{9,8},{10,11... | collective-permute-start | bytes 3145736 | tf_op jit(solution)/shard_map/ppermute | solution.py:41
  86.4 41.4 %collective-permute-start.7 = (f32[256,512]{1,0:T(8,128)}, f32[256,512]{1,0:T(8,128)}, u32[]{:S(2)}, u32[]{:S(2)}) collective-permute-start(f32[256,512]{1,0:T(8,128)} %get-tuple-element.33), channel_id=1, source_target_pairs={{0,2},{1,3},{2,0},{3,1},{4,6},{5,7},{6,4},{7,5},{8,10},{9,11},{10,... | collective-permute-start | bytes 1572872 | tf_op jit(solution)/shard_map/ppermute | solution.py:41
  115.8 29.6 %copy-start.7 = (f32[256,512]{1,0:T(8,128)}, f32[256,512]{1,0:T(8,128)S(1)}, u32[]{:S(2)}) copy-start(f32[256,512]{1,0:T(8,128)S(1)} %get-tuple-element.24) | copy-start | bytes 1572868
  115.8 28.8 %collective-permute-start.16 = (f32[256,512]{1,0:T(8,128)}, f32[256,512]{1,0:T(8,128)S(1)}, u32[]{:S(2)}, u32[]{:S(2)}) collective-permute-start(f32[256,512]{1,0:T(8,128)} %get-tuple-element.25), channel_id=1, source_target_pairs={{0,2},{1,3},{2,0},{3,1},{4,6},{5,7},{6,4},{7,5},{8,10},{9,11},{10,... | collective-permute-start | bytes 1572872 | tf_op jit(solution)/shard_map/ppermute | solution.py:41
  116.8 44.6 %copy-start.5 = (f32[256,512]{1,0:T(8,128)}, f32[256,512]{1,0:T(8,128)S(1)}, u32[]{:S(2)}) copy-start(f32[256,512]{1,0:T(8,128)S(1)} %get-tuple-element.28) | copy-start | bytes 1572868
  116.8 43.8 %collective-permute-start.25 = (f32[256,512]{1,0:T(8,128)}, f32[256,512]{1,0:T(8,128)S(1)}, u32[]{:S(2)}, u32[]{:S(2)}) collective-permute-start(f32[256,512]{1,0:T(8,128)} %get-tuple-element.29), channel_id=1, source_target_pairs={{0,2},{1,3},{2,0},{3,1},{4,6},{5,7},{6,4},{7,5},{8,10},{9,11},{10,... | collective-permute-start | bytes 1572872 | tf_op jit(solution)/shard_map/ppermute | solution.py:41
  128.8 32.7 %collective-permute-start.8 = (f32[128,512]{1,0:T(8,128)S(1)}, f32[128,512]{1,0:T(8,128)S(1)}, u32[]{:S(2)}, u32[]{:S(2)}) collective-permute-start(f32[128,512]{1,0:T(8,128)S(1)} %slice_add_fusion.10), channel_id=1, source_target_pairs={{0,4},{1,5},{2,6},{3,7},{4,0},{5,1},{6,2},{7,3},{8,12},{9,13},{10,... | collective-permute-start | bytes 786440 | tf_op jit(solution)/shard_map/ppermute | solution.py:41
  144.6 16.9 %copy-start.17 = (f32[256,512]{1,0:T(8,128)}, f32[256,512]{1,0:T(8,128)S(1)}, u32[]{:S(2)}) copy-start(f32[256,512]{1,0:T(8,128)S(1)} %collective-permute-done.16) | copy-start | bytes 1572868
  145.4 26.5 %collective-permute-start.17 = (f32[128,512]{1,0:T(8,128)}, f32[128,512]{1,0:T(8,128)S(1)}, u32[]{:S(2)}, u32[]{:S(2)}) collective-permute-start(f32[128,512]{1,0:T(8,128)} %slice_add_fusion.8), channel_id=1, source_target_pairs={{0,4},{1,5},{2,6},{3,7},{4,0},{5,1},{6,2},{7,3},{8,12},{9,13},{10,... | collective-permute-start | bytes 786440 | tf_op jit(solution)/shard_map/ppermute | solution.py:41
  161.5 16.5 %collective-permute-start.26 = (f32[128,512]{1,0:T(8,128)}, f32[128,512]{1,0:T(8,128)}, u32[]{:S(2)}, u32[]{:S(2)}) collective-permute-start(f32[128,512]{1,0:T(8,128)} %slice_add_fusion.6), channel_id=1, source_target_pairs={{0,4},{1,5},{2,6},{3,7},{4,0},{5,1},{6,2},{7,3},{8,12},{9,13},{10,... | collective-permute-start | bytes 786440 | tf_op jit(solution)/shard_map/ppermute | solution.py:41
  164.2 7.6 %copy-start.18 = (f32[256,512]{1,0:T(8,128)S(1)}, f32[256,512]{1,0:T(8,128)}, u32[]{:S(2)}) copy-start(f32[256,512]{1,0:T(8,128)} %copy-done.17) | copy-start | bytes 1572868
  200.3 4.9 %collective-permute-start.34 = (f32[4,128,512]{2,1,0:T(8,128)S(1)}, f32[4,128,512]{2,1,0:T(8,128)S(1)}, u32[]{:S(2)}, u32[]{:S(2)}) collective-permute-start(f32[4,128,512]{2,1,0:T(8,128)S(1)} %bitcast.163), channel_id=1, source_target_pairs={{0,1},{1,0},{2,3},{3,2},{4,5},{5,4},{6,7},{7,6},{8,9},{9,8},{10,11... | collective-permute-start | bytes 3145736 | tf_op jit(solution)/shard_map/ppermute | solution.py:41
  203.1 35.9 %collective-permute-start.27 = (f32[4,192,512]{2,1,0:T(8,128)S(1)}, f32[4,192,512]{2,1,0:T(8,128)S(1)}, u32[]{:S(2)}, u32[]{:S(2)}) collective-permute-start(f32[4,192,512]{2,1,0:T(8,128)S(1)} %bitcast.160), channel_id=1, source_target_pairs={{0,1},{1,0},{2,3},{3,2},{4,5},{5,4},{6,7},{7,6},{8,9},{9,8},{10,11... | collective-permute-start | bytes 4718600 | tf_op jit(solution)/shard_map/ppermute | solution.py:41
  205.6 8.4 %collective-permute-start.35 = (f32[4,32,512]{2,1,0:T(8,128)S(1)}, f32[4,32,512]{2,1,0:T(8,128)S(1)}, u32[]{:S(2)}, u32[]{:S(2)}) collective-permute-start(f32[4,32,512]{2,1,0:T(8,128)S(1)} %constant_dynamic-slice_fusion.5), channel_id=1, source_target_pairs={{0,8},{8,0},{16,24},{24,16},{1,9},{9,1},{17,25},{25,17},{2,10},{10... | collective-permute-start | bytes 786440 | tf_op jit(solution)/shard_map/ppermute | solution.py:41
  209.9 8.5 %collective-permute-start.41 = (f32[4,32,512]{2,1,0:T(8,128)S(1)}, f32[4,32,512]{2,1,0:T(8,128)S(1)}, u32[]{:S(2)}, u32[]{:S(2)}) collective-permute-start(f32[4,32,512]{2,1,0:T(8,128)S(1)} %constant_dynamic-slice_fusion.3), channel_id=1, source_target_pairs={{0,16},{8,24},{16,0},{24,8},{1,17},{9,25},{17,1},{25,9},{2,18},{10... | collective-permute-start | bytes 786440 | tf_op jit(solution)/shard_map/ppermute | solution.py:41
  214.1 5.8 %collective-permute-start.36 = (f32[4,16,512]{2,1,0:T(8,128)S(1)}, f32[4,16,512]{2,1,0:T(8,128)S(1)}, u32[]{:S(2)}, u32[]{:S(2)}) collective-permute-start(f32[4,16,512]{2,1,0:T(8,128)S(1)} %constant_dynamic-slice_fusion.4), channel_id=1, source_target_pairs={{0,16},{8,24},{16,0},{24,8},{1,17},{9,25},{17,1},{25,9},{2,18},{10... | collective-permute-start | bytes 393224 | tf_op jit(solution)/shard_map/ppermute | solution.py:41
  218.5 5.0 %collective-permute-start.42 = (f32[4,16,512]{2,1,0:T(8,128)S(1)}, f32[4,16,512]{2,1,0:T(8,128)S(1)}, u32[]{:S(2)}, u32[]{:S(2)}) collective-permute-start(f32[4,16,512]{2,1,0:T(8,128)S(1)} %constant_dynamic-slice_fusion.2), channel_id=1, source_target_pairs={{0,8},{8,0},{16,24},{24,16},{1,9},{9,1},{17,25},{25,17},{2,10},{10... | collective-permute-start | bytes 393224 | tf_op jit(solution)/shard_map/ppermute | solution.py:41
  219.9 4.3 %collective-permute-start.37 = (f32[2,16,512]{2,1,0:T(8,128)S(1)}, f32[2,16,512]{2,1,0:T(8,128)S(1)}, u32[]{:S(2)}, u32[]{:S(2)}) collective-permute-start(f32[2,16,512]{2,1,0:T(8,128)S(1)} %slice.414), channel_id=1, source_target_pairs={{0,2},{1,3},{2,0},{3,1},{4,6},{5,7},{6,4},{7,5},{8,10},{9,11},{10,... | collective-permute-start | bytes 196616 | tf_op jit(solution)/shard_map/ppermute | solution.py:41
  223.6 4.3 %collective-permute-start.43 = (f32[2,16,512]{2,1,0:T(8,128)S(1)}, f32[2,16,512]{2,1,0:T(8,128)S(1)}, u32[]{:S(2)}, u32[]{:S(2)}) collective-permute-start(f32[2,16,512]{2,1,0:T(8,128)S(1)} %slice.419), channel_id=1, source_target_pairs={{0,2},{1,3},{2,0},{3,1},{4,6},{5,7},{6,4},{7,5},{8,10},{9,11},{10,... | collective-permute-start | bytes 196616 | tf_op jit(solution)/shard_map/ppermute | solution.py:41
  224.3 4.9 %collective-permute-start.38 = (f32[1,16,512]{2,1,0:T(8,128)S(1)}, f32[1,16,512]{2,1,0:T(8,128)S(1)}, u32[]{:S(2)}, u32[]{:S(2)}) collective-permute-start(f32[1,16,512]{2,1,0:T(8,128)S(1)} %slice.416), channel_id=1, source_target_pairs={{0,4},{1,5},{2,6},{3,7},{4,0},{5,1},{6,2},{7,3},{8,12},{9,13},{10,... | collective-permute-start | bytes 98312 | tf_op jit(solution)/shard_map/ppermute | solution.py:41
  228.0 5.0 %collective-permute-start.44 = (f32[1,16,512]{2,1,0:T(8,128)S(1)}, f32[1,16,512]{2,1,0:T(8,128)S(1)}, u32[]{:S(2)}, u32[]{:S(2)}) collective-permute-start(f32[1,16,512]{2,1,0:T(8,128)S(1)} %slice.421), channel_id=1, source_target_pairs={{0,4},{1,5},{2,6},{3,7},{4,0},{5,1},{6,2},{7,3},{8,12},{9,13},{10,... | collective-permute-start | bytes 98312 | tf_op jit(solution)/shard_map/ppermute | solution.py:41
  229.2 4.7 %collective-permute-start.39 = (f32[16,512]{1,0:T(8,128)S(1)}, f32[16,512]{1,0:T(8,128)S(1)}, u32[]{:S(2)}, u32[]{:S(2)}) collective-permute-start(f32[16,512]{1,0:T(8,128)S(1)} %fusion.104), channel_id=1, source_target_pairs={{0,16},{8,24},{16,0},{24,8},{1,17},{9,25},{17,1},{25,9},{2,18},{10... | collective-permute-start | bytes 98312 | tf_op jit(solution)/shard_map/ppermute | solution.py:41
  233.0 4.3 %collective-permute-start.45 = (f32[16,512]{1,0:T(8,128)S(1)}, f32[16,512]{1,0:T(8,128)S(1)}, u32[]{:S(2)}, u32[]{:S(2)}) collective-permute-start(f32[16,512]{1,0:T(8,128)S(1)} %fusion.103), channel_id=1, source_target_pairs={{0,8},{8,0},{16,24},{24,16},{1,9},{9,1},{17,25},{25,17},{2,10},{10... | collective-permute-start | bytes 98312 | tf_op jit(solution)/shard_map/ppermute | solution.py:41
  233.9 7.2 %collective-permute-start.40 = (f32[32,512]{1,0:T(8,128)S(1)}, f32[32,512]{1,0:T(8,128)S(1)}, u32[]{:S(2)}, u32[]{:S(2)}) collective-permute-start(f32[32,512]{1,0:T(8,128)S(1)} %pad_maximum_fusion.11), channel_id=1, source_target_pairs={{0,8},{8,0},{16,24},{24,16},{1,9},{9,1},{17,25},{25,17},{2,10},{10... | collective-permute-start | bytes 196616 | tf_op jit(solution)/shard_map/ppermute | solution.py:41
  237.3 4.3 %collective-permute-start.46 = (f32[32,512]{1,0:T(8,128)S(1)}, f32[32,512]{1,0:T(8,128)S(1)}, u32[]{:S(2)}, u32[]{:S(2)}) collective-permute-start(f32[32,512]{1,0:T(8,128)S(1)} %pad_maximum_fusion.12), channel_id=1, source_target_pairs={{0,16},{8,24},{16,0},{24,8},{1,17},{9,25},{17,1},{25,9},{2,18},{10... | collective-permute-start | bytes 196616 | tf_op jit(solution)/shard_map/ppermute | solution.py:41
  239.6 11.3 %collective-permute-start.47 = (f32[4,48,512]{2,1,0:T(8,128)S(1)}, f32[4,48,512]{2,1,0:T(8,128)S(1)}, u32[]{:S(2)}, u32[]{:S(2)}) collective-permute-start(f32[4,48,512]{2,1,0:T(8,128)S(1)} %constant_dynamic-slice_fusion.1), channel_id=1, source_target_pairs={{0,16},{8,24},{16,0},{24,8},{1,17},{9,25},{17,1},{25,9},{2,18},{10... | collective-permute-start | bytes 1179656 | tf_op jit(solution)/shard_map/ppermute | solution.py:41
  240.2 9.9 %collective-permute-start.28 = (f32[4,48,512]{2,1,0:T(8,128)S(1)}, f32[4,48,512]{2,1,0:T(8,128)S(1)}, u32[]{:S(2)}, u32[]{:S(2)}) collective-permute-start(f32[4,48,512]{2,1,0:T(8,128)S(1)} %constant_dynamic-slice_fusion.7), channel_id=1, source_target_pairs={{0,8},{8,0},{16,24},{24,16},{1,9},{9,1},{17,25},{25,17},{2,10},{10... | collective-permute-start | bytes 1179656 | tf_op jit(solution)/shard_map/ppermute | solution.py:41
  250.2 5.7 %collective-permute-start.29 = (f32[4,24,512]{2,1,0:T(8,128)S(1)}, f32[4,24,512]{2,1,0:T(8,128)S(1)}, u32[]{:S(2)}, u32[]{:S(2)}) collective-permute-start(f32[4,24,512]{2,1,0:T(8,128)S(1)} %constant_dynamic-slice_fusion.6), channel_id=1, source_target_pairs={{0,16},{8,24},{16,0},{24,8},{1,17},{9,25},{17,1},{25,9},{2,18},{10... | collective-permute-start | bytes 589832 | tf_op jit(solution)/shard_map/ppermute | solution.py:41
  251.0 5.7 %collective-permute-start.48 = (f32[4,24,512]{2,1,0:T(8,128)S(1)}, f32[4,24,512]{2,1,0:T(8,128)S(1)}, u32[]{:S(2)}, u32[]{:S(2)}) collective-permute-start(f32[4,24,512]{2,1,0:T(8,128)S(1)} %constant_dynamic-slice_fusion), channel_id=1, source_target_pairs={{0,8},{8,0},{16,24},{24,16},{1,9},{9,1},{17,25},{25,17},{2,10},{10... | collective-permute-start | bytes 589832 | tf_op jit(solution)/shard_map/ppermute | solution.py:41
  256.0 4.7 %collective-permute-start.30 = (f32[2,24,512]{2,1,0:T(8,128)S(1)}, f32[2,24,512]{2,1,0:T(8,128)S(1)}, u32[]{:S(2)}, u32[]{:S(2)}) collective-permute-start(f32[2,24,512]{2,1,0:T(8,128)S(1)} %slice.406), channel_id=1, source_target_pairs={{0,2},{1,3},{2,0},{3,1},{4,6},{5,7},{6,4},{7,5},{8,10},{9,11},{10,... | collective-permute-start | bytes 294920 | tf_op jit(solution)/shard_map/ppermute | solution.py:41
  256.8 4.9 %collective-permute-start.49 = (f32[2,24,512]{2,1,0:T(8,128)S(1)}, f32[2,24,512]{2,1,0:T(8,128)S(1)}, u32[]{:S(2)}, u32[]{:S(2)}) collective-permute-start(f32[2,24,512]{2,1,0:T(8,128)S(1)} %slice.424), channel_id=1, source_target_pairs={{0,2},{1,3},{2,0},{3,1},{4,6},{5,7},{6,4},{7,5},{8,10},{9,11},{10,... | collective-permute-start | bytes 294920 | tf_op jit(solution)/shard_map/ppermute | solution.py:41
  260.7 5.1 %collective-permute-start.31 = (f32[1,24,512]{2,1,0:T(8,128)S(1)}, f32[1,24,512]{2,1,0:T(8,128)S(1)}, u32[]{:S(2)}, u32[]{:S(2)}) collective-permute-start(f32[1,24,512]{2,1,0:T(8,128)S(1)} %slice.408), channel_id=1, source_target_pairs={{0,4},{1,5},{2,6},{3,7},{4,0},{5,1},{6,2},{7,3},{8,12},{9,13},{10,... | collective-permute-start | bytes 147464 | tf_op jit(solution)/shard_map/ppermute | solution.py:41
  261.8 5.1 %collective-permute-start.50 = (f32[1,24,512]{2,1,0:T(8,128)S(1)}, f32[1,24,512]{2,1,0:T(8,128)S(1)}, u32[]{:S(2)}, u32[]{:S(2)}) collective-permute-start(f32[1,24,512]{2,1,0:T(8,128)S(1)} %slice.426), channel_id=1, source_target_pairs={{0,4},{1,5},{2,6},{3,7},{4,0},{5,1},{6,2},{7,3},{8,12},{9,13},{10,... | collective-permute-start | bytes 147464 | tf_op jit(solution)/shard_map/ppermute | solution.py:41
  265.9 4.2 %collective-permute-start.32 = (f32[24,512]{1,0:T(8,128)S(1)}, f32[24,512]{1,0:T(8,128)S(1)}, u32[]{:S(2)}, u32[]{:S(2)}) collective-permute-start(f32[24,512]{1,0:T(8,128)S(1)} %fusion.102), channel_id=1, source_target_pairs={{0,16},{8,24},{16,0},{24,8},{1,17},{9,25},{17,1},{25,9},{2,18},{10... | collective-permute-start | bytes 147464 | tf_op jit(solution)/shard_map/ppermute | solution.py:41
  266.8 4.4 %collective-permute-start.51 = (f32[24,512]{1,0:T(8,128)S(1)}, f32[24,512]{1,0:T(8,128)S(1)}, u32[]{:S(2)}, u32[]{:S(2)}) collective-permute-start(f32[24,512]{1,0:T(8,128)S(1)} %fusion.101), channel_id=1, source_target_pairs={{0,8},{8,0},{16,24},{24,16},{1,9},{9,1},{17,25},{25,17},{2,10},{10... | collective-permute-start | bytes 147464 | tf_op jit(solution)/shard_map/ppermute | solution.py:41
  270.0 4.7 %collective-permute-start.33 = (f32[48,512]{1,0:T(8,128)S(1)}, f32[48,512]{1,0:T(8,128)S(1)}, u32[]{:S(2)}, u32[]{:S(2)}) collective-permute-start(f32[48,512]{1,0:T(8,128)S(1)} %pad_maximum_fusion.9), channel_id=1, source_target_pairs={{0,8},{8,0},{16,24},{24,16},{1,9},{9,1},{17,25},{25,17},{2,10},{10... | collective-permute-start | bytes 294920 | tf_op jit(solution)/shard_map/ppermute | solution.py:41
  271.2 4.7 %collective-permute-start.52 = (f32[48,512]{1,0:T(8,128)S(1)}, f32[48,512]{1,0:T(8,128)S(1)}, u32[]{:S(2)}, u32[]{:S(2)}) collective-permute-start(f32[48,512]{1,0:T(8,128)S(1)} %pad_maximum_fusion.10), channel_id=1, source_target_pairs={{0,16},{8,24},{16,0},{24,8},{1,17},{9,25},{17,1},{25,9},{2,18},{10... | collective-permute-start | bytes 294920 | tf_op jit(solution)/shard_map/ppermute | solution.py:41
  (15 other events, 45.8 us)
Sparse Core Ops, SparseCore 0:
  29.4 38.5 all-gather.1

commit v2 on v1

v2 whole, which is shorter than its diff:
```python
import functools

import jax
import jax.numpy as jnp
from jax import lax
from jax.experimental import pallas as pl
from jax.experimental.pallas import tpu as pltpu
from jax.sharding import PartitionSpec as P

AXES = ("row", "col")
F32 = jnp.float32
BF16 = jnp.bfloat16
NN = (((1,), (0,)), ((), ()))
TN = (((0,), (0,)), ((), ()))
VMEM_BYTES = 40 * 1024 * 1024


def split(value):
    high = value.astype(BF16)
    return high, (value - high.astype(F32)).astype(BF16)


def product(left, right, dims=NN):
    def one(a, b):
        return lax.dot_general(a, b, dims, preferred_element_type=F32)

    return one(left[0], right[0]) + (one(left[0], right[1]) + one(left[1], right[0]))


def reordered(chooser, value):
    high, low = split(value)
    return jnp.dot(chooser, high, preferred_element_type=F32) + jnp.dot(
        chooser, low, preferred_element_type=F32
    )


def call(body, out_shapes, flops, *args, smem=0):
    specs = [pl.BlockSpec(memory_space=pltpu.SMEM)] * smem
    specs += [pl.BlockSpec(memory_space=pltpu.VMEM)] * (len(args) - smem)
    moved = sum(a.size * a.dtype.itemsize for a in args)
    moved += sum(s.size * s.dtype.itemsize for s in out_shapes)
    return pl.pallas_call(
        body,
        out_shape=out_shapes,
        in_specs=specs,
        out_specs=[pl.BlockSpec(memory_space=pltpu.VMEM)] * len(out_shapes),
        compiler_params=pltpu.CompilerParams(vmem_limit_bytes=VMEM_BYTES),
        cost_estimate=pl.CostEstimate(flops=flops, bytes_accessed=moved, transcendentals=0),
    )(*args)


def shape(*dims, dtype=F32):
    return jax.ShapeDtypeStruct(dims, dtype)


def gray(place):
    return place ^ (place >> 1)


def reversed_bits(count):
    order = [0]
    step = 1
    while step < count:
        order = [value + bit * step for value in order for bit in (0, 1)]
        step *= 2
    return order


def row_weights(listed_row, first_row, count, width):
    block_ids = (first_row + lax.iota(jnp.int32, count)) // width
    table = lax.iota(jnp.int32, listed_row.shape[0])
    hits = (block_ids[:, None] == table[None, :]) & (listed_row[None, :] != 0)
    return jnp.any(hits, axis=1).astype(F32)


def swap(value, axis, size, change):
    return lax.ppermute(value, axis, [(place, place ^ change) for place in range(size)])


def split_rows_kernel(order_ref, in_ref, mask_ref, high_ref, low_ref):
    high, low = split(in_ref[0] * mask_ref[...])
    high_ref[...] = high
    low_ref[...] = low


def split_rows(array, member, order, group, mask):
    _, rows, columns = array.shape
    block = pl.BlockSpec((group, columns), lambda g, order_ref: (g, 0))
    return pl.pallas_call(
        split_rows_kernel,
        out_shape=[shape(rows, columns, dtype=BF16)] * 2,
        grid_spec=pltpu.PrefetchScalarGridSpec(
            num_scalar_prefetch=1,
            grid=(rows // group,),
            in_specs=[
                pl.BlockSpec((1, group, columns), lambda g, order_ref: (member, order_ref[g], 0)),
                pl.BlockSpec((group, 1), lambda g, order_ref: (order_ref[g], 0)),
            ],
            out_specs=[block, block],
        ),
        cost_estimate=pl.CostEstimate(
            flops=2 * rows * columns, bytes_accessed=8 * rows * columns, transcendentals=0
        ),
    )(order, array, mask)


def unit_kernel(count, place_ref, high_ref, low_ref, *refs):
    ways = (refs[:count], refs[count : 2 * count])
    send_ref, keep_ref = refs[2 * count :]
    half = ways[0][0].shape[0]
    total = None
    for way, candidates in enumerate(ways):
        place = place_ref[way]
        chosen = candidates[0][...]
        for at in range(1, count):
            chosen = jnp.where(place == at, candidates[at][...], chosen)
        columns = slice(way * half, (way + 1) * half)
        part = product((high_ref[:, columns], low_ref[:, columns]), split(chosen))
        total = part if total is None else total + part
    middle = total.shape[0] // 2
    keep_ref[...] = total[:middle]
    send_ref[...] = total[middle:]


def unit_gram_kernel(high_ref, low_ref, keep_ref, send_ref, out_ref):
    middle = keep_ref.shape[0]
    out_ref[...] = product(
        (high_ref[:, :middle], low_ref[:, :middle]), split(keep_ref[...])
    ) + product((high_ref[:, middle:], low_ref[:, middle:]), split(send_ref[...]))


def store_halves(keep_ref, send_ref, index, value):
    middle = value.shape[0] // 2
    keep_ref[index] = value[:middle]
    send_ref[index] = value[middle:]


def parent_kernel(
    children, chooser_ref, mask_ref, left_ref, right_ref, own_ref, links_ref,
    col_ref, turned_ref, keep_ref, send_ref,
):
    sums = jnp.concatenate([left_ref[...], right_ref[...]], axis=1)
    column = -sums * mask_ref[...]
    col_ref[...] = column
    column_pair = split(column)
    parent_pair = split(own_ref[0])
    chooser = chooser_ref[...]
    store_halves(
        keep_ref, send_ref, 0, reordered(chooser, -product(parent_pair, column_pair, TN))
    )
    for c in range(children):
        turned = product(column_pair, split(links_ref[c]))
        turned_ref[c] = turned
        upper = product(parent_pair, split(turned), TN)
        upper -= product(column_pair, split(own_ref[c + 1]), TN)
        store_halves(keep_ref, send_ref, 1 + c, reordered(chooser, upper))


def link_kernel(children, share, own_ref, links_ref, slices_ref, diag_ref, lifted_ref, framed_ref, corner_ref):
    parent_pair = split(own_ref[0])
    diag_pair = split(diag_ref[0])
    for c in range(children):
        link_pair = split(links_ref[c])
        lifted_ref[c] = product(parent_pair, link_pair)
        framed = product(diag_pair, link_pair)
        framed_ref[c] = framed
        corner_ref[c] = share * product(split(slices_ref[c]), split(framed), TN)


def child_kernel(
    children, chooser_ref, own_ref, turned_ref, lifted_ref, corner_ref, *refs
):
    keep_ref, send_ref = refs[-2:]
    for c in range(children):
        left_ref, right_ref = refs[2 * c : 2 * c + 2]
        own = split(own_ref[c + 1])
        turned = split(turned_ref[c])
        total = corner_ref[c] + jnp.concatenate([left_ref[...], right_ref[...]], axis=1)
        total += product(own, turned, TN) + product(turned, own, TN)
        total -= product(split(lifted_ref[c]), turned, TN)
        store_halves(keep_ref, send_ref, c, reordered(chooser_ref[...], total))


def shards(region_inverse, factor_cols, parent_factor, diag_inverse, listed):
    row_count = lax.axis_size("row")
    col_count = lax.axis_size("col")
    row_place = lax.axis_index("row")
    col_place = lax.axis_index("col")
    col_bits = col_count.bit_length() - 1
    rows_here, cols_here = region_inverse.shape
    members, _, width = factor_cols.shape
    children = members - 1
    group = rows_here // col_count
    ratio = col_count // row_count
    diag_width = width // col_count
    part = diag_width // row_count
    first_row = row_place * rows_here
    source = col_place // ratio
    unit = width // 2
    units = [(j, lo) for j in range(members) for lo in range(0, width, unit)]

    links = lax.all_gather(parent_factor, "col", axis=1, tiled=True)

    def ring(forward):
        pairs = []
        for col in range(col_count):
            start = col // ratio
            for place in range(row_count):
                at = (start ^ gray(place)) * col_count + col
                to = (start ^ gray((place + 1) % row_count)) * col_count + col
                pairs.append((at, to) if forward else (to, at))
        return pairs

    distance = row_place ^ source
    forward_place = distance
    shift = 1
    while shift < row_count:
        forward_place = forward_place ^ (forward_place >> shift)
        shift *= 2
    backward_place = (row_count - forward_place) % row_count
    places = jnp.stack([forward_place, backward_place]).astype(jnp.int32)
    is_source = row_place == source
    col_first = col_place * cols_here
    half = cols_here // 2
    col_masks = [row_weights(listed[j], col_first, cols_here, width)[:, None] for j in range(members)]

    def chunk(j, lo, way):
        start = (col_place % ratio) * cols_here + way * half
        block = lax.dynamic_slice(factor_cols, (j, start, lo), (1, half, unit))[0]
        return block * col_masks[j][way * half : (way + 1) * half]

    chunks = [[chunk(j, lo, way) for j, lo in units] for way in range(2)]
    received = [[], []]
    for stage in range(len(units) + row_count - 2):
        for way in range(2):
            if stage == 0:
                moving = chunks[way][0]
            elif stage < len(units):
                moving = jnp.where(is_source, chunks[way][stage], received[way][-1])
            else:
                moving = received[way][-1]
            received[way].append(lax.ppermute(moving, AXES, ring(way == 0)))

    relative = jnp.array(reversed_bits(col_count), jnp.int32) ^ col_place
    ones = jnp.ones((rows_here, 1), F32)
    region = split_rows(region_inverse[None], 0, relative, group, ones)
    row_masks = [row_weights(listed[j], first_row, rows_here, width)[:, None] for j in range(members)]
    turned_factors = []
    for c in range(children):
        pair = split_rows(factor_cols, c + 1, relative, group, row_masks[c + 1])
        turned_factors.append([value.T for value in pair])

    own_first = first_row + col_place * group
    own_masks = [row_weights(listed[j], own_first, group, width)[:, None] for j in range(members)]
    own = lax.dynamic_slice_in_dim(factor_cols, col_place * group, group, 1) * jnp.stack(own_masks)

    halving = jnp.array(reversed_bits(col_count), jnp.int32).reshape(2, 1, col_count // 2, 1)
    by_row = lax.iota(jnp.int32, row_count).reshape(1, row_count, 1, 1) ^ row_place
    inner = lax.iota(jnp.int32, part).reshape(1, 1, 1, part)
    wanted = ((halving ^ col_place) * diag_width + by_row * part + inner).reshape(width, 1)
    chooser = (wanted == lax.iota(jnp.int32, width)[None, :]).astype(BF16)

    def column_unit(index):
        candidates = []
        for way in range(2):
            candidates.append(chunks[way][index])
            candidates += received[way][index : index + row_count - 1]
        size = rows_here // 2
        return call(
            functools.partial(unit_kernel, row_count),
            [shape(size, unit)] * 2,
            6 * rows_here * cols_here * unit,
            places, *region, *candidates,
            smem=1,
        )

    def halved(send, keep):
        size = keep.shape[0]
        for bit in range(col_bits):
            arrived = swap(send, "col", col_count, 1 << bit)
            if bit + 1 < col_bits:
                size //= 2
                send = keep[size:] + arrived[size:]
                keep = keep[:size] + arrived[:size]
            else:
                keep = keep + arrived
        return keep

    def total_rows(keep, send):
        value = keep + swap(send, "col", col_count, 1)
        size = value.shape[1] // row_count
        piece = value[:, :size]
        for change in range(1, row_count):
            sent = value[:, change * size : (change + 1) * size]
            piece = piece + swap(sent, "row", row_count, change)
        for bit in range(1, col_bits):
            size //= 2
            piece = piece[:, :size] + swap(piece[:, size:], "col", col_count, 1 << bit)
        pieces = [piece] + [swap(piece, "row", row_count, d) for d in range(1, row_count)]
        stacked = []
        for row in range(row_count):
            chosen = pieces[0]
            for change in range(1, row_count):
                chosen = jnp.where(row_place ^ change == row, pieces[change], chosen)
            stacked.append(chosen)
        return jnp.concatenate(stacked, axis=1)

    sums = []
    grams = []
    for index, (j, lo) in enumerate(units):
        send, keep = column_unit(index)
        sums.append(halved(send, keep))
        if j > 0:
            grams += call(
                unit_gram_kernel,
                [shape(width, unit)],
                6 * rows_here * width * unit,
                *turned_factors[j - 1], keep, send,
            )

    parent_col, turned, keep, send = call(
        functools.partial(parent_kernel, children),
        [shape(group, width), shape(children, group, width)]
        + [shape(members, width // 2, width)] * 2,
        6 * (1 + 3 * children) * group * width * width,
        chooser, own_masks[0], sums[0], sums[1], own, links,
    )
    parent_totals = total_rows(keep, send)

    lifted, framed, corner = call(
        functools.partial(link_kernel, children, 1.0 / row_count),
        [shape(children, group, width), shape(children, diag_width, width),
         shape(children, width, width)],
        6 * children * (group + 2 * diag_width) * width * width,
        own, links, parent_factor, diag_inverse,
    )
    keep, send = call(
        functools.partial(child_kernel, children),
        [shape(children, width // 2, width)] * 2,
        18 * children * group * width * width,
        chooser, own, turned, lifted, corner, *grams,
    )
    child_totals = total_rows(keep, send)

    child_cols = []
    for c in range(children):
        column = jnp.concatenate(sums[2 * c + 2 : 2 * c + 4], axis=1)
        child_cols.append(-(column + turned[c]) * own_masks[c + 1])
    uppers = parent_totals[1:] - framed
    diags = diag_inverse + jnp.concatenate([parent_totals[:1], child_totals])
    return jnp.stack([parent_col] + child_cols), diags, uppers


def solution(mesh):
    in_specs = (
        P("row", "col"),
        P(None, "row", None),
        P(None, "col", None),
        P(None, "col", None),
        P(),
    )
    out_specs = (P(None, ("row", "col"), None), P(None, "col", None), P(None, "col", None))
    return jax.shard_map(shards, mesh=mesh, in_specs=in_specs, out_specs=out_specs, check_vma=False)
```

time: 286 us -> 301 us (1.052)
  Pallas kernels: 0 us -> 48.3 us
  starting transfers between devices: 95.9 us -> 57 us
  waiting for transfers between devices: 86.8 us -> 117 us
  matrix products: 24.8 us -> 0 us
    pallas_call x0 -> x16, Pallas kernels: none -> 48.3 us  [the longest x13 28.2 us: call(): pl.pallas_call(body, out_shape=out_shapes, in_specs=specs, out_specs=[pl....]
    ppermute x53 -> x52, starting transfers between devices: 95.9 us -> 56.9 us  [the longest x36 34.8 us: swap(): lax.ppermute(value, axis, [(place, place ^ change) for place in range(siz...]
    ppermute x53 -> x52, waiting for transfers between devices: 86.8 us -> 117 us  [the longest x36 72.8 us: swap(): lax.ppermute(value, axis, [(place, place ^ change) for place in range(siz...]
    dot_general x23 -> x0, matrix products: 24.8 us -> none  [the longest x14 15.4 us: dot(): jnp.dot(left, right, precision=HIGH, preferred_element_type=jnp.float32)]
    slice x20 -> x9, local copies, waits for them, and re-layouts: 14.1 us -> 0.21 us  [the longest x2 0.16 us: total_rows(): sent = value[:, change * size:(change + 1) * size]]
    unnamed x48 -> x104, local copies, waits for them, and re-layouts: 3.81 us -> 17.2 us
    select_n x11 -> x12, other arithmetic: 5.99 us -> 16.7 us  [the longest x10 16.6 us: shards(): moving = jnp.where(is_source, chunks[way][stage], received[way][-1])]
    gather x3 -> x0, local copies, waits for them, and re-layouts: 10 us -> none  [the longest x2 7.94 us: total_rows(): stacked = jnp.take(stacked, relative, axis=1).transpose(1, 0, 2, 3)]
  transfers between devices with their start and end apart: 54 -> 53, of which waited for: 25 -> 28; matrix products, arithmetic and copies ran while one was open for 18% -> 13% of each run, Pallas kernels for 0% -> 16%
where the time goes in v2:
time: 301 us; the launch traced here: 299 us
  waiting for transfers between devices  117 us (39%)
  starting transfers between devices  57 us (19%)
  Pallas kernels  48.3 us (16%)
  other arithmetic  34.1 us (11%)
  local copies, waits for them, and re-layouts  28 us (9%)
  between operations  15 us (5%)
    ppermute x36, waiting for transfers between devices, swap(): lax.ppermute(value, axis, [(place, place ^ change) for place in range(siz...  72.8 us
    ppermute x16, waiting for transfers between devices, shards(): received[way].append(lax.ppermute(moving, AXES, ring(way == 0)))  43.9 us
    ppermute x36, starting transfers between devices, swap(): lax.ppermute(value, axis, [(place, place ^ change) for place in range(siz...  34.8 us
    pallas_call x13, Pallas kernels, call(): pl.pallas_call(body, out_shape=out_shapes, in_specs=specs, out_specs=[pl....  28.2 us
    ppermute x16, starting transfers between devices, shards(): received[way].append(lax.ppermute(moving, AXES, ring(way == 0)))  22.1 us
    pallas_call x3, Pallas kernels, split_rows(): pl.pallas_call(split_rows_kernel, out_shape=[shape(rows, columns, dtype=B...  20.1 us
    unnamed x104, local copies, waits for them, and re-layouts  17.2 us
    select_n x10, other arithmetic, shards(): moving = jnp.where(is_source, chunks[way][stage], received[way][-1])  16.6 us
  transfers between devices with their start and end apart: 53, of which 28 were waited for; matrix products, arithmetic and copies ran while one was open for 13% of the time, Pallas kernels for 16%

profile of v2, /device:TPU:0, one launch (start us, length us, event | category | flops | bytes accessed | tf_op | source)
XLA Modules:
  0.0 299.1 jit_solution(4152734031164911976)
XLA Ops:
  9.2 3.0 %collective-permute-start.3 = (f32[256,256]{1,0:T(8,128)S(1)}, f32[256,256]{1,0:T(8,128)S(1)}, u32[]{:S(2)}, u32[]{:S(2)}) collective-permute-start(f32[256,256]{1,0:T(8,128)S(1)} %bitcast_multiply_fusion.8.refs_4_), channel_id=1, source_target_pairs={{8,0},{24,8},{16,24},{0,16},{9,1},{25,9},{17,25},{1,17},{2,10},{18... | collective-permute-start | bytes 786440 | tf_op jit(solution)/shard_map/ppermute | solution.py:242
  12.3 6.3 %collective-permute-done.3.refs_5_ = f32[256,256]{1,0:T(8,128)S(1)} collective-permute-done((f32[256,256]{1,0:T(8,128)S(1)}, f32[256,256]{1,0:T(8,128)S(1)}, u32[]{:S(2)}, u32[]{:S(2)}) %collective-permute-start.3) | collective-permute-done | bytes 262176 | tf_op jit(solution)/shard_map/ppermute | solution.py:242
  18.5 1.8 broadcast_select_fusion.7
  20.4 1.8 collective-permute-start.4
  22.2 5.7 %collective-permute-done.4.refs_6_.refs_5_ = f32[256,256]{1,0:T(8,128)S(1)} collective-permute-done((f32[256,256]{1,0:T(8,128)S(1)}, f32[256,256]{1,0:T(8,128)S(1)}, u32[]{:S(2)}, u32[]{:S(2)}) %collective-permute-start.4) | collective-permute-done | bytes 262176 | tf_op jit(solution)/shard_map/ppermute | solution.py:242
  27.9 1.9 broadcast_select_fusion.6
  31.2 5.1 %collective-permute-done.5.refs_7_.refs_6_.refs_5_ = f32[256,256]{1,0:T(8,128)S(1)} collective-permute-done((f32[256,256]{1,0:T(8,128)S(1)}, f32[256,256]{1,0:T(8,128)S(1)}, u32[]{:S(2)}, u32[]{:S(2)}) %collective-permute-start.5) | collective-permute-done | bytes 262176 | tf_op jit(solution)/shard_map/ppermute | solution.py:242
  36.3 1.9 broadcast_select_fusion.4
  39.5 5.0 %collective-permute-done.10.refs_7_.refs_6_.refs_5_ = f32[256,256]{1,0:T(8,128)S(1)} collective-permute-done((f32[256,256]{1,0:T(8,128)S(1)}, f32[256,256]{1,0:T(8,128)S(1)}, u32[]{:S(2)}, u32[]{:S(2)}) %collective-permute-start.10) | collective-permute-done | bytes 262176 | tf_op jit(solution)/shard_map/ppermute | solution.py:242
  44.5 1.9 broadcast_select_fusion.2
  48.9 3.9 %collective-permute-done.15.refs_7_.refs_6_.refs_5_ = f32[256,256]{1,0:T(8,128)S(1)} collective-permute-done((f32[256,256]{1,0:T(8,128)S(1)}, f32[256,256]{1,0:T(8,128)S(1)}, u32[]{:S(2)}, u32[]{:S(2)}) %collective-permute-start.15) | collective-permute-done | bytes 262176 | tf_op jit(solution)/shard_map/ppermute | solution.py:242
  52.8 2.0 broadcast_select_fusion
  56.2 5.6 %collective-permute-done.refs_1_ = f32[256,256]{1,0:T(8,128)S(1)} collective-permute-done((f32[256,256]{1,0:T(8,128)S(1)}, f32[256,256]{1,0:T(8,128)S(1)}, u32[]{:S(2)}, u32[]{:S(2)}) %collective-permute-start) | collective-permute-done | bytes 262176 | tf_op jit(solution)/shard_map/ppermute | solution.py:242
  61.8 1.9 broadcast_select_fusion.9
  63.7 1.8 collective-permute-start.1
  65.5 6.0 %collective-permute-done.1.refs_2_.refs_1_ = f32[256,256]{1,0:T(8,128)S(1)} collective-permute-done((f32[256,256]{1,0:T(8,128)S(1)}, f32[256,256]{1,0:T(8,128)S(1)}, u32[]{:S(2)}, u32[]{:S(2)}) %collective-permute-start.1) | collective-permute-done | bytes 262176 | tf_op jit(solution)/shard_map/ppermute | solution.py:242
  71.5 1.9 broadcast_select_fusion.8
  73.5 2.4 collective-permute-start.2
  79.0 6.7 %shard_map.106 = (bf16[1024,512]{1,0:T(8,128)(2,1)}, bf16[1024,512]{1,0:T(8,128)(2,1)}) custom-call(s32[8]{0:T(128)} %get-tuple-element.124.order_ref, f32[3,1024,512]{2,1,0:T(8,128)} %in_ref.3, f32[1024,1]{1,0:T(8,128)} %copy.39.mask_ref), custom_call_target="tpu_custom_call" | custom-call | flops 1048576 | bytes 4194304 | tf_op jit(solution)/shard_map/pallas_call | solution.py:89
  88.7 6.7 %shard_map.103 = (bf16[1024,512]{1,0:T(8,128)(2,1)}, bf16[1024,512]{1,0:T(8,128)(2,1)}) custom-call(s32[8]{0:T(128)} %get-tuple-element.124.order_ref, f32[3,1024,512]{2,1,0:T(8,128)} %in_ref.3, f32[1024,1]{1,0:T(8,128)} %copy.36.mask_ref), custom_call_target="tpu_custom_call" | custom-call | flops 1048576 | bytes 4194304 | tf_op jit(solution)/shard_map/pallas_call | solution.py:89
  96.8 2.3 copy.38
  100.0 6.7 %shard_map.94 = (bf16[1024,512]{1,0:T(8,128)(2,1)}, bf16[1024,512]{1,0:T(8,128)(2,1)}) custom-call(s32[8]{0:T(128)} %get-tuple-element.124.order_ref, f32[1,1024,512]{2,1,0:T(8,128)} %bitcast.80, f32[1024,1]{1,0:T(8,128)} %broadcast_in_dim.5.mask_ref), custom_call_target="tpu_custom_call" | custom-call | flops 1048576 | bytes 4194304 | tf_op jit(solution)/shard_map/pallas_call | solution.py:89
  108.1 2.0 collective-permute-start.9
  110.1 2.1 dynamic-slice_multiply_fusion.own_ref
  122.6 2.1 shard_map.95
  125.9 2.0 collective-permute-start.14
  129.0 2.0 shard_map.96
  131.3 3.6 %collective-permute-done.14.refs_3_.refs_2_.refs_1_ = f32[256,256]{1,0:T(8,128)S(1)} collective-permute-done((f32[256,256]{1,0:T(8,128)S(1)}, f32[256,256]{1,0:T(8,128)S(1)}, u32[]{:S(2)}, u32[]{:S(2)}) %collective-permute-start.14) | collective-permute-done | bytes 262176 | tf_op jit(solution)/shard_map/ppermute | solution.py:242
  136.0 1.7 collective-permute-start.19
  137.8 1.7 collective-permute-start.7
  139.6 2.0 shard_map.98
  144.2 1.6 shard_map.99
  148.5 3.4 %collective-permute-start.8 = (f32[128,256]{1,0:T(8,128)S(1)}, f32[128,256]{1,0:T(8,128)S(1)}, u32[]{:S(2)}, u32[]{:S(2)}) collective-permute-start(f32[128,256]{1,0:T(8,128)S(1)} %slice_add_fusion.26), channel_id=1, source_target_pairs={{0,4},{1,5},{2,6},{3,7},{4,0},{5,1},{6,2},{7,3},{8,12},{9,13},{10,... | collective-permute-start | bytes 393224 | tf_op jit(solution)/shard_map/ppermute | solution.py:77
  152.0 6.6 %collective-permute-done.8 = f32[128,256]{1,0:T(8,128)S(1)} collective-permute-done((f32[128,256]{1,0:T(8,128)S(1)}, f32[128,256]{1,0:T(8,128)S(1)}, u32[]{:S(2)}, u32[]{:S(2)}) %collective-permute-start.8) | collective-permute-done | bytes 131104 | tf_op jit(solution)/shard_map/ppermute | solution.py:77
  158.9 1.6 shard_map.100
  161.6 5.0 %collective-permute-done.12 = f32[256,256]{1,0:T(8,128)S(1)} collective-permute-done((f32[256,256]{1,0:T(8,128)S(1)}, f32[256,256]{1,0:T(8,128)S(1)}, u32[]{:S(2)}, u32[]{:S(2)}) %collective-permute-start.12) | collective-permute-done | bytes 262176 | tf_op jit(solution)/shard_map/ppermute | solution.py:77
  167.1 1.6 collective-permute-start.13
  168.8 6.1 %collective-permute-done.13 = f32[128,256]{1,0:T(8,128)S(1)} collective-permute-done((f32[128,256]{1,0:T(8,128)S(1)}, f32[128,256]{1,0:T(8,128)S(1)}, u32[]{:S(2)}, u32[]{:S(2)}) %collective-permute-start.13) | collective-permute-done | bytes 131104 | tf_op jit(solution)/shard_map/ppermute | solution.py:77
  175.6 2.1 collective-permute-start.22
  177.7 6.9 %collective-permute-done.17 = f32[256,256]{1,0:T(8,128)S(1)} collective-permute-done((f32[256,256]{1,0:T(8,128)S(1)}, f32[256,256]{1,0:T(8,128)S(1)}, u32[]{:S(2)}, u32[]{:S(2)}) %collective-permute-start.17) | collective-permute-done | bytes 262176 | tf_op jit(solution)/shard_map/ppermute | solution.py:77
  185.3 2.4 shard_map.101
  187.8 2.2 shard_map.108.refs_3_
  190.0 2.3 collective-permute-done.18
  194.7 1.9 collective-permute-start.27
  196.6 1.6 copy-done.24
  200.2 2.2 shard_map.102
  202.4 1.6 copy-done.25
  206.7 4.9 %shard_map.97 = (f32[128,512]{1,0:T(8,128)S(1)}, f32[2,128,512]{2,1,0:T(8,128)S(1)}, f32[3,256,512]{2,1,0:T(8,128)S(1)}, f32[3,256,512]{2,1,0:T(8,128)S(1)}) custom-call(bf16[512,512]{1,0:T(8,128)(2,1)S(1)} %copy-done.26, f32[128,1]{1,0:T(8,128)S(1)} %copy-done.45, f32[128,256]{1,0:T(8,128)S(1)} %fusion.21.left_ref, f32[128,256]{1,0:T(8,128)S(1)} %copy-done.44, ...), custom_call_target="tpu_custom_call" | custom-call | flops 1409286144 | bytes 7602688 | tf_op jit(solution)/shard_map/pallas_call | solution.py:42
  211.7 4.1 %shard_map.109 = (f32[2,256,512]{2,1,0:T(8,128)S(1)}, f32[2,256,512]{2,1,0:T(8,128)S(1)}) custom-call(bf16[512,512]{1,0:T(8,128)(2,1)S(1)} %copy-done.26, f32[3,128,512]{2,1,0:T(8,128)S(1)} %copy-done.5, f32[2,128,512]{2,1,0:T(8,128)S(1)} %get-tuple-element.41.turned_ref, f32[2,128,512]{2,1,0:T(8,128)S(1)} %get-tuple-element.48.lifted_ref, ...), custom_call_target="tpu_custom_call" | custom-call | flops 1207959552 | bytes 8650752 | tf_op jit(solution)/shard_map/pallas_call | solution.py:42
  219.6 2.9 collective-permute-start.28
  222.6 6.0 %collective-permute-done.32 = f32[256,256]{1,0:T(8,128)S(1)} collective-permute-done((f32[256,256]{1,0:T(8,128)S(1)}, f32[256,256]{1,0:T(8,128)S(1)}, u32[]{:S(2)}, u32[]{:S(2)}) %collective-permute-start.32) | collective-permute-done | bytes 262176 | tf_op jit(solution)/shard_map/ppermute | solution.py:77
  229.7 6.6 %collective-permute-done.33 = f32[128,256]{1,0:T(8,128)S(1)} collective-permute-done((f32[128,256]{1,0:T(8,128)S(1)}, f32[128,256]{1,0:T(8,128)S(1)}, u32[]{:S(2)}, u32[]{:S(2)}) %collective-permute-start.33) | collective-permute-done | bytes 131104 | tf_op jit(solution)/shard_map/ppermute | solution.py:77
  236.6 2.5 collective-permute-start.44
  241.1 2.0 collective-permute-start.35
  244.1 2.1 collective-permute-done.44
  246.2 1.6 collective-permute-start.36
  248.8 4.1 %collective-permute-done.46 = f32[2,64,512]{2,1,0:T(8,128)S(1)} collective-permute-done((f32[2,64,512]{2,1,0:T(8,128)S(1)}, f32[2,64,512]{2,1,0:T(8,128)S(1)}, u32[]{:S(2)}, u32[]{:S(2)}) %collective-permute-start.46) | collective-permute-done | bytes 262176 | tf_op jit(solution)/shard_map/ppermute | solution.py:77
  252.9 1.6 collective-permute-done.45
  254.7 5.6 %collective-permute-done.35 = f32[3,64,512]{2,1,0:T(8,128)S(1)} collective-permute-done((f32[3,64,512]{2,1,0:T(8,128)S(1)}, f32[3,64,512]{2,1,0:T(8,128)S(1)}, u32[]{:S(2)}, u32[]{:S(2)}) %collective-permute-start.35) | collective-permute-done | bytes 393248 | tf_op jit(solution)/shard_map/ppermute | solution.py:77
  260.3 8.5 %collective-permute-done.37 = f32[3,64,512]{2,1,0:T(8,128)S(1)} collective-permute-done((f32[3,64,512]{2,1,0:T(8,128)S(1)}, f32[3,64,512]{2,1,0:T(8,128)S(1)}, u32[]{:S(2)}, u32[]{:S(2)}) %collective-permute-start.37) | collective-permute-done | bytes 393248 | tf_op jit(solution)/shard_map/ppermute | solution.py:77
  270.4 2.8 collective-permute-start.48
  273.2 4.1 %collective-permute-done.38 = f32[3,32,512]{2,1,0:T(8,128)S(1)} collective-permute-done((f32[3,32,512]{2,1,0:T(8,128)S(1)}, f32[3,32,512]{2,1,0:T(8,128)S(1)}, u32[]{:S(2)}, u32[]{:S(2)}) %collective-permute-start.38) | collective-permute-done | bytes 196640 | tf_op jit(solution)/shard_map/ppermute | solution.py:77
  281.1 2.0 collective-permute-done.39
  288.8 1.8 collective-permute-done.40
  (248 shorter events, 70.0 us)
Async XLA Ops:
  7.2 189.4 %all-gather.2.cloned.1.call-start = ((), (), s32[]{:S(2)}) async-start(), calls=%async_computation | async-start | bytes 2359296 | tf_op jit(solution)/shard_map/all_gather | solution.py:202
  9.2 9.3 %collective-permute-start.3 = (f32[256,256]{1,0:T(8,128)S(1)}, f32[256,256]{1,0:T(8,128)S(1)}, u32[]{:S(2)}, u32[]{:S(2)}) collective-permute-start(f32[256,256]{1,0:T(8,128)S(1)} %bitcast_multiply_fusion.8.refs_4_), channel_id=1, source_target_pairs={{8,0},{24,8},{16,24},{0,16},{9,1},{25,9},{17,25},{1,17},{2,10},{18... | collective-permute-start | bytes 786440 | tf_op jit(solution)/shard_map/ppermute | solution.py:242
  18.5 34.3 %copy-start.37 = (f32[256,256]{1,0:T(8,128)}, f32[256,256]{1,0:T(8,128)S(1)}, u32[]{:S(2)}) copy-start(f32[256,256]{1,0:T(8,128)S(1)} %collective-permute-done.3.refs_5_) | copy-start | bytes 786436
  20.4 7.5 %collective-permute-start.4 = (f32[256,256]{1,0:T(8,128)S(1)}, f32[256,256]{1,0:T(8,128)S(1)}, u32[]{:S(2)}, u32[]{:S(2)}) collective-permute-start(f32[256,256]{1,0:T(8,128)S(1)} %get-tuple-element.73), channel_id=1, source_target_pairs={{8,0},{24,8},{16,24},{0,16},{9,1},{25,9},{17,25},{1,17},{2,10},{18... | collective-permute-start | bytes 786440 | tf_op jit(solution)/shard_map/ppermute | solution.py:242
  29.7 6.6 %collective-permute-start.5 = (f32[256,256]{1,0:T(8,128)S(1)}, f32[256,256]{1,0:T(8,128)S(1)}, u32[]{:S(2)}, u32[]{:S(2)}) collective-permute-start(f32[256,256]{1,0:T(8,128)S(1)} %get-tuple-element.71), channel_id=1, source_target_pairs={{8,0},{24,8},{16,24},{0,16},{9,1},{25,9},{17,25},{1,17},{2,10},{18... | collective-permute-start | bytes 786440 | tf_op jit(solution)/shard_map/ppermute | solution.py:242
  36.3 49.3 %copy-start.6 = (f32[256,256]{1,0:T(8,128)}, f32[256,256]{1,0:T(8,128)S(1)}, u32[]{:S(2)}) copy-start(f32[256,256]{1,0:T(8,128)S(1)} %collective-permute-done.5.refs_7_.refs_6_.refs_5_) | copy-start | bytes 786436
  38.2 6.4 %collective-permute-start.10 = (f32[256,256]{1,0:T(8,128)S(1)}, f32[256,256]{1,0:T(8,128)S(1)}, u32[]{:S(2)}, u32[]{:S(2)}) collective-permute-start(f32[256,256]{1,0:T(8,128)S(1)} %get-tuple-element.69), channel_id=1, source_target_pairs={{8,0},{24,8},{16,24},{0,16},{9,1},{25,9},{17,25},{1,17},{2,10},{18... | collective-permute-start | bytes 786440 | tf_op jit(solution)/shard_map/ppermute | solution.py:242
  46.4 6.4 %collective-permute-start.15 = (f32[256,256]{1,0:T(8,128)S(1)}, f32[256,256]{1,0:T(8,128)S(1)}, u32[]{:S(2)}, u32[]{:S(2)}) collective-permute-start(f32[256,256]{1,0:T(8,128)S(1)} %get-tuple-element.67), channel_id=1, source_target_pairs={{8,0},{24,8},{16,24},{0,16},{9,1},{25,9},{17,25},{1,17},{2,10},{18... | collective-permute-start | bytes 786440 | tf_op jit(solution)/shard_map/ppermute | solution.py:242
  54.8 7.0 %collective-permute-start = (f32[256,256]{1,0:T(8,128)S(1)}, f32[256,256]{1,0:T(8,128)S(1)}, u32[]{:S(2)}, u32[]{:S(2)}) collective-permute-start(f32[256,256]{1,0:T(8,128)S(1)} %get-tuple-element.85.refs_0_), channel_id=1, source_target_pairs={{0,8},{8,24},{24,16},{16,0},{1,9},{9,25},{25,17},{17,1},{10,2},{2,... | collective-permute-start | bytes 786440 | tf_op jit(solution)/shard_map/ppermute | solution.py:242
  61.8 23.9 %copy-start.42 = (f32[256,256]{1,0:T(8,128)}, f32[256,256]{1,0:T(8,128)S(1)}, u32[]{:S(2)}) copy-start(f32[256,256]{1,0:T(8,128)S(1)} %collective-permute-done.refs_1_) | copy-start | bytes 786436
  63.7 7.9 %collective-permute-start.1 = (f32[256,256]{1,0:T(8,128)S(1)}, f32[256,256]{1,0:T(8,128)S(1)}, u32[]{:S(2)}, u32[]{:S(2)}) collective-permute-start(f32[256,256]{1,0:T(8,128)S(1)} %get-tuple-element.83), channel_id=1, source_target_pairs={{0,8},{8,24},{24,16},{16,0},{1,9},{9,25},{25,17},{17,1},{10,2},{2,... | collective-permute-start | bytes 786440 | tf_op jit(solution)/shard_map/ppermute | solution.py:242
  73.5 33.4 %collective-permute-start.2 = (f32[256,256]{1,0:T(8,128)}, f32[256,256]{1,0:T(8,128)}, u32[]{:S(2)}, u32[]{:S(2)}) collective-permute-start(f32[256,256]{1,0:T(8,128)} %get-tuple-element.81), channel_id=1, source_target_pairs={{0,8},{8,24},{24,16},{16,0},{1,9},{9,25},{25,17},{17,1},{10,2},{2,... | collective-permute-start | bytes 786440 | tf_op jit(solution)/shard_map/ppermute | solution.py:242
  106.7 22.3 %copy-start.8 = (f32[256,256]{1,0:T(8,128)S(1)}, f32[256,256]{1,0:T(8,128)}, u32[]{:S(2)}) copy-start(f32[256,256]{1,0:T(8,128)} %copy-done.6) | copy-start | bytes 786436
  106.7 22.3 %copy-start.10 = (f32[256,256]{1,0:T(8,128)S(1)}, f32[256,256]{1,0:T(8,128)}, u32[]{:S(2)}) copy-start(f32[256,256]{1,0:T(8,128)} %copy-done.9) | copy-start | bytes 786436
  106.7 22.3 %copy-start.13 = (f32[256,256]{1,0:T(8,128)S(1)}, f32[256,256]{1,0:T(8,128)}, u32[]{:S(2)}) copy-start(f32[256,256]{1,0:T(8,128)} %copy-done.11) | copy-start | bytes 786436
  106.7 22.3 %copy-start.39 = (f32[256,256]{1,0:T(8,128)S(1)}, f32[256,256]{1,0:T(8,128)}, u32[]{:S(2)}) copy-start(f32[256,256]{1,0:T(8,128)} %get-tuple-element.74.refs_4_) | copy-start | bytes 786436
  106.7 22.3 %copy-start.41 = (f32[256,256]{1,0:T(8,128)S(1)}, f32[256,256]{1,0:T(8,128)}, u32[]{:S(2)}) copy-start(f32[256,256]{1,0:T(8,128)} %get-tuple-element.84.refs_0_) | copy-start | bytes 786436
  106.8 6.6 %collective-permute-start.20 = (f32[256,256]{1,0:T(8,128)}, f32[256,256]{1,0:T(8,128)S(1)}, u32[]{:S(2)}, u32[]{:S(2)}) collective-permute-start(f32[256,256]{1,0:T(8,128)} %get-tuple-element.65), channel_id=1, source_target_pairs={{8,0},{24,8},{16,24},{0,16},{9,1},{25,9},{17,25},{1,17},{2,10},{18... | collective-permute-start | bytes 786440 | tf_op jit(solution)/shard_map/ppermute | solution.py:242
  108.1 16.7 %collective-permute-start.9 = (f32[256,256]{1,0:T(8,128)S(1)}, f32[256,256]{1,0:T(8,128)S(1)}, u32[]{:S(2)}, u32[]{:S(2)}) collective-permute-start(f32[256,256]{1,0:T(8,128)S(1)} %get-tuple-element.79), channel_id=1, source_target_pairs={{0,8},{8,24},{24,16},{16,0},{1,9},{9,25},{25,17},{17,1},{10,2},{2,... | collective-permute-start | bytes 786440 | tf_op jit(solution)/shard_map/ppermute | solution.py:242
  113.4 15.5 %collective-permute-start.25 = (f32[256,256]{1,0:T(8,128)S(1)}, f32[256,256]{1,0:T(8,128)S(1)}, u32[]{:S(2)}, u32[]{:S(2)}) collective-permute-start(f32[256,256]{1,0:T(8,128)S(1)} %collective-permute-done.20.refs_7_.refs_6_.refs_5_), channel_id=1, source_target_pairs={{8,0},{24,8},{16,24},{0,16},{9,1},{25,9},{17,25},{1,17},{2,10},{18... | collective-permute-start | bytes 786440 | tf_op jit(solution)/shard_map/ppermute | solution.py:242
  124.7 13.1 %collective-permute-start.6 = (f32[512,256]{1,0:T(8,128)S(1)}, f32[512,256]{1,0:T(8,128)S(1)}, u32[]{:S(2)}, u32[]{:S(2)}) collective-permute-start(f32[512,256]{1,0:T(8,128)S(1)} %get-tuple-element.33), channel_id=1, source_target_pairs={{0,1},{1,0},{2,3},{3,2},{4,5},{5,4},{6,7},{7,6},{8,9},{9,8},{10,11... | collective-permute-start | bytes 1572872 | tf_op jit(solution)/shard_map/ppermute | solution.py:77
  125.9 9.0 %collective-permute-start.14 = (f32[256,256]{1,0:T(8,128)S(1)}, f32[256,256]{1,0:T(8,128)S(1)}, u32[]{:S(2)}, u32[]{:S(2)}) collective-permute-start(f32[256,256]{1,0:T(8,128)S(1)} %get-tuple-element.77), channel_id=1, source_target_pairs={{0,8},{8,24},{24,16},{16,0},{1,9},{9,25},{25,17},{17,1},{10,2},{2,... | collective-permute-start | bytes 786440 | tf_op jit(solution)/shard_map/ppermute | solution.py:242
  128.9 56.4 %collective-permute-start.30 = (f32[256,256]{1,0:T(8,128)S(1)}, f32[256,256]{1,0:T(8,128)S(1)}, u32[]{:S(2)}, u32[]{:S(2)}) collective-permute-start(f32[256,256]{1,0:T(8,128)S(1)} %collective-permute-done.25.refs_7_.refs_6_), channel_id=1, source_target_pairs={{8,0},{24,8},{16,24},{0,16},{9,1},{25,9},{17,25},{1,17},{2,10},{18... | collective-permute-start | bytes 786440 | tf_op jit(solution)/shard_map/ppermute | solution.py:242
  131.1 17.4 %collective-permute-start.11 = (f32[512,256]{1,0:T(8,128)S(1)}, f32[512,256]{1,0:T(8,128)S(1)}, u32[]{:S(2)}, u32[]{:S(2)}) collective-permute-start(f32[512,256]{1,0:T(8,128)S(1)} %get-tuple-element.35), channel_id=1, source_target_pairs={{0,1},{1,0},{2,3},{3,2},{4,5},{5,4},{6,7},{7,6},{8,9},{9,8},{10,11... | collective-permute-start | bytes 1572872 | tf_op jit(solution)/shard_map/ppermute | solution.py:77
  136.0 8.2 %collective-permute-start.19 = (f32[256,256]{1,0:T(8,128)S(1)}, f32[256,256]{1,0:T(8,128)S(1)}, u32[]{:S(2)}, u32[]{:S(2)}) collective-permute-start(f32[256,256]{1,0:T(8,128)S(1)} %get-tuple-element.75), channel_id=1, source_target_pairs={{0,8},{8,24},{24,16},{16,0},{1,9},{9,25},{25,17},{17,1},{10,2},{2,... | collective-permute-start | bytes 786440 | tf_op jit(solution)/shard_map/ppermute | solution.py:242
  137.8 9.1 %collective-permute-start.7 = (f32[256,256]{1,0:T(8,128)S(1)}, f32[256,256]{1,0:T(8,128)S(1)}, u32[]{:S(2)}, u32[]{:S(2)}) collective-permute-start(f32[256,256]{1,0:T(8,128)S(1)} %get-tuple-element.99), channel_id=1, source_target_pairs={{0,2},{1,3},{2,0},{3,1},{4,6},{5,7},{6,4},{7,5},{8,10},{9,11},{10,... | collective-permute-start | bytes 786440 | tf_op jit(solution)/shard_map/ppermute | solution.py:77
  141.6 25.4 %collective-permute-start.16 = (f32[512,256]{1,0:T(8,128)S(1)}, f32[512,256]{1,0:T(8,128)S(1)}, u32[]{:S(2)}, u32[]{:S(2)}) collective-permute-start(f32[512,256]{1,0:T(8,128)S(1)} %get-tuple-element.38.send_ref), channel_id=1, source_target_pairs={{0,1},{1,0},{2,3},{3,2},{4,5},{5,4},{6,7},{7,6},{8,9},{9,8},{10,11... | collective-permute-start | bytes 1572872 | tf_op jit(solution)/shard_map/ppermute | solution.py:77
  145.8 29.7 %collective-permute-start.21 = (f32[512,256]{1,0:T(8,128)S(1)}, f32[512,256]{1,0:T(8,128)S(1)}, u32[]{:S(2)}, u32[]{:S(2)}) collective-permute-start(f32[512,256]{1,0:T(8,128)S(1)} %get-tuple-element.40.send_ref), channel_id=1, source_target_pairs={{0,1},{1,0},{2,3},{3,2},{4,5},{5,4},{6,7},{7,6},{8,9},{9,8},{10,11... | collective-permute-start | bytes 1572872 | tf_op jit(solution)/shard_map/ppermute | solution.py:77
  146.9 28.6 %copy-start.18 = (f32[512,256]{1,0:T(8,128)}, f32[512,256]{1,0:T(8,128)S(1)}, u32[]{:S(2)}) copy-start(f32[512,256]{1,0:T(8,128)S(1)} %shard_map.105.refs_1_) | copy-start | bytes 1572868
  146.9 11.9 %collective-permute-start.24 = (f32[256,256]{1,0:T(8,128)S(1)}, f32[256,256]{1,0:T(8,128)S(1)}, u32[]{:S(2)}, u32[]{:S(2)}) collective-permute-start(f32[256,256]{1,0:T(8,128)S(1)} %collective-permute-done.19.refs_3_.refs_2_.refs_1_), channel_id=1, source_target_pairs={{0,8},{8,24},{24,16},{16,0},{1,9},{9,25},{25,17},{17,1},{10,2},{2,... | collective-permute-start | bytes 786440 | tf_op jit(solution)/shard_map/ppermute | solution.py:242
  148.5 10.1 %collective-permute-start.8 = (f32[128,256]{1,0:T(8,128)S(1)}, f32[128,256]{1,0:T(8,128)S(1)}, u32[]{:S(2)}, u32[]{:S(2)}) collective-permute-start(f32[128,256]{1,0:T(8,128)S(1)} %slice_add_fusion.26), channel_id=1, source_target_pairs={{0,4},{1,5},{2,6},{3,7},{4,0},{5,1},{6,2},{7,3},{8,12},{9,13},{10,... | collective-permute-start | bytes 393224 | tf_op jit(solution)/shard_map/ppermute | solution.py:77
  158.6 7.9 %collective-permute-start.12 = (f32[256,256]{1,0:T(8,128)S(1)}, f32[256,256]{1,0:T(8,128)S(1)}, u32[]{:S(2)}, u32[]{:S(2)}) collective-permute-start(f32[256,256]{1,0:T(8,128)S(1)} %get-tuple-element.97), channel_id=1, source_target_pairs={{0,2},{1,3},{2,0},{3,1},{4,6},{5,7},{6,4},{7,5},{8,10},{9,11},{10,... | collective-permute-start | bytes 786440 | tf_op jit(solution)/shard_map/ppermute | solution.py:77
  158.8 26.5 %copy-start.28 = (f32[256,256]{1,0:T(8,128)S(1)}, f32[256,256]{1,0:T(8,128)}, u32[]{:S(2)}) copy-start(f32[256,256]{1,0:T(8,128)} %get-tuple-element.66.refs_4_) | copy-start | bytes 786436
  160.5 33.3 %collective-permute-start.26 = (f32[512,256]{1,0:T(8,128)S(1)}, f32[512,256]{1,0:T(8,128)S(1)}, u32[]{:S(2)}, u32[]{:S(2)}) collective-permute-start(f32[512,256]{1,0:T(8,128)S(1)} %get-tuple-element.43.send_ref), channel_id=1, source_target_pairs={{0,1},{1,0},{2,3},{3,2},{4,5},{5,4},{6,7},{7,6},{8,9},{9,8},{10,11... | collective-permute-start | bytes 1572872 | tf_op jit(solution)/shard_map/ppermute | solution.py:77
  166.6 18.8 %collective-permute-start.29 = (f32[256,256]{1,0:T(8,128)S(1)}, f32[256,256]{1,0:T(8,128)S(1)}, u32[]{:S(2)}, u32[]{:S(2)}) collective-permute-start(f32[256,256]{1,0:T(8,128)S(1)} %collective-permute-done.24.refs_3_.refs_2_), channel_id=1, source_target_pairs={{0,8},{8,24},{24,16},{16,0},{1,9},{9,25},{25,17},{17,1},{10,2},{2,... | collective-permute-start | bytes 786440 | tf_op jit(solution)/shard_map/ppermute | solution.py:242
  167.1 7.8 %collective-permute-start.13 = (f32[128,256]{1,0:T(8,128)S(1)}, f32[128,256]{1,0:T(8,128)S(1)}, u32[]{:S(2)}, u32[]{:S(2)}) collective-permute-start(f32[128,256]{1,0:T(8,128)S(1)} %slice_add_fusion.24), channel_id=1, source_target_pairs={{0,4},{1,5},{2,6},{3,7},{4,0},{5,1},{6,2},{7,3},{8,12},{9,13},{10,... | collective-permute-start | bytes 393224 | tf_op jit(solution)/shard_map/ppermute | solution.py:77
  174.8 9.8 %collective-permute-start.17 = (f32[256,256]{1,0:T(8,128)S(1)}, f32[256,256]{1,0:T(8,128)S(1)}, u32[]{:S(2)}, u32[]{:S(2)}) collective-permute-start(f32[256,256]{1,0:T(8,128)S(1)} %get-tuple-element.93), channel_id=1, source_target_pairs={{0,2},{1,3},{2,0},{3,1},{4,6},{5,7},{6,4},{7,5},{8,10},{9,11},{10,... | collective-permute-start | bytes 786440 | tf_op jit(solution)/shard_map/ppermute | solution.py:77
  175.6 17.4 %collective-permute-start.22 = (f32[256,256]{1,0:T(8,128)S(1)}, f32[256,256]{1,0:T(8,128)S(1)}, u32[]{:S(2)}, u32[]{:S(2)}) collective-permute-start(f32[256,256]{1,0:T(8,128)S(1)} %get-tuple-element.95), channel_id=1, source_target_pairs={{0,2},{1,3},{2,0},{3,1},{4,6},{5,7},{6,4},{7,5},{8,10},{9,11},{10,... | collective-permute-start | bytes 786440 | tf_op jit(solution)/shard_map/ppermute | solution.py:77
  184.7 7.7 %collective-permute-start.18 = (f32[128,256]{1,0:T(8,128)S(1)}, f32[128,256]{1,0:T(8,128)S(1)}, u32[]{:S(2)}, u32[]{:S(2)}) collective-permute-start(f32[128,256]{1,0:T(8,128)S(1)} %slice_add_fusion.22), channel_id=1, source_target_pairs={{0,4},{1,5},{2,6},{3,7},{4,0},{5,1},{6,2},{7,3},{8,12},{9,13},{10,... | collective-permute-start | bytes 393224 | tf_op jit(solution)/shard_map/ppermute | solution.py:77
  187.8 28.6 %collective-permute-start.31 = (f32[512,256]{1,0:T(8,128)}, f32[512,256]{1,0:T(8,128)}, u32[]{:S(2)}, u32[]{:S(2)}) collective-permute-start(f32[512,256]{1,0:T(8,128)} %get-tuple-element.45.send_ref), channel_id=1, source_target_pairs={{0,1},{1,0},{2,3},{3,2},{4,5},{5,4},{6,7},{7,6},{8,9},{9,8},{10,11... | collective-permute-start | bytes 1572872 | tf_op jit(solution)/shard_map/ppermute | solution.py:77
  190.0 21.6 %copy-start.17 = (f32[512,256]{1,0:T(8,128)S(1)}, f32[512,256]{1,0:T(8,128)}, u32[]{:S(2)}) copy-start(f32[512,256]{1,0:T(8,128)} %copy-done.16) | copy-start | bytes 1572868
  193.7 24.0 %collective-permute-start.23 = (f32[128,256]{1,0:T(8,128)}, f32[128,256]{1,0:T(8,128)}, u32[]{:S(2)}, u32[]{:S(2)}) collective-permute-start(f32[128,256]{1,0:T(8,128)} %slice_add_fusion.20), channel_id=1, source_target_pairs={{0,4},{1,5},{2,6},{3,7},{4,0},{5,1},{6,2},{7,3},{8,12},{9,13},{10,... | collective-permute-start | bytes 393224 | tf_op jit(solution)/shard_map/ppermute | solution.py:77
  194.7 24.0 %collective-permute-start.27 = (f32[256,256]{1,0:T(8,128)}, f32[256,256]{1,0:T(8,128)}, u32[]{:S(2)}, u32[]{:S(2)}) collective-permute-start(f32[256,256]{1,0:T(8,128)} %get-tuple-element.101), channel_id=1, source_target_pairs={{0,2},{1,3},{2,0},{3,1},{4,6},{5,7},{6,4},{7,5},{8,10},{9,11},{10,... | collective-permute-start | bytes 786440 | tf_op jit(solution)/shard_map/ppermute | solution.py:77
  215.8 20.5 %collective-permute-start.43 = (f32[2,256,512]{2,1,0:T(8,128)S(1)}, f32[2,256,512]{2,1,0:T(8,128)S(1)}, u32[]{:S(2)}, u32[]{:S(2)}) collective-permute-start(f32[2,256,512]{2,1,0:T(8,128)S(1)} %get-tuple-element.55), channel_id=1, source_target_pairs={{0,1},{1,0},{2,3},{3,2},{4,5},{5,4},{6,7},{7,6},{8,9},{9,8},{10,11... | collective-permute-start | bytes 3145736 | tf_op jit(solution)/shard_map/ppermute | solution.py:77
  215.9 24.8 %collective-permute-start.34 = (f32[3,256,512]{2,1,0:T(8,128)S(1)}, f32[3,256,512]{2,1,0:T(8,128)S(1)}, u32[]{:S(2)}, u32[]{:S(2)}) collective-permute-start(f32[3,256,512]{2,1,0:T(8,128)S(1)} %get-tuple-element.47), channel_id=1, source_target_pairs={{0,1},{1,0},{2,3},{3,2},{4,5},{5,4},{6,7},{7,6},{8,9},{9,8},{10,11... | collective-permute-start | bytes 4718600 | tf_op jit(solution)/shard_map/ppermute | solution.py:77
  217.5 11.2 %collective-permute-start.32 = (f32[256,256]{1,0:T(8,128)S(1)}, f32[256,256]{1,0:T(8,128)S(1)}, u32[]{:S(2)}, u32[]{:S(2)}) collective-permute-start(f32[256,256]{1,0:T(8,128)S(1)} %get-tuple-element.103), channel_id=1, source_target_pairs={{0,2},{1,3},{2,0},{3,1},{4,6},{5,7},{6,4},{7,5},{8,10},{9,11},{10,... | collective-permute-start | bytes 786440 | tf_op jit(solution)/shard_map/ppermute | solution.py:77
  219.6 9.1 %collective-permute-start.28 = (f32[128,256]{1,0:T(8,128)S(1)}, f32[128,256]{1,0:T(8,128)S(1)}, u32[]{:S(2)}, u32[]{:S(2)}) collective-permute-start(f32[128,256]{1,0:T(8,128)S(1)} %slice_add_fusion.18), channel_id=1, source_target_pairs={{0,4},{1,5},{2,6},{3,7},{4,0},{5,1},{6,2},{7,3},{8,12},{9,13},{10,... | collective-permute-start | bytes 393224 | tf_op jit(solution)/shard_map/ppermute | solution.py:77
  228.6 7.6 %collective-permute-start.33 = (f32[128,256]{1,0:T(8,128)S(1)}, f32[128,256]{1,0:T(8,128)S(1)}, u32[]{:S(2)}, u32[]{:S(2)}) collective-permute-start(f32[128,256]{1,0:T(8,128)S(1)} %slice_add_fusion.16), channel_id=1, source_target_pairs={{0,4},{1,5},{2,6},{3,7},{4,0},{5,1},{6,2},{7,3},{8,12},{9,13},{10,... | collective-permute-start | bytes 393224 | tf_op jit(solution)/shard_map/ppermute | solution.py:77
  236.6 9.6 %collective-permute-start.44 = (f32[2,64,512]{2,1,0:T(8,128)S(1)}, f32[2,64,512]{2,1,0:T(8,128)S(1)}, u32[]{:S(2)}, u32[]{:S(2)}) collective-permute-start(f32[2,64,512]{2,1,0:T(8,128)S(1)} %get-tuple-element.89), channel_id=1, source_target_pairs={{0,8},{8,0},{16,24},{24,16},{1,9},{9,1},{17,25},{25,17},{2,10},{10... | collective-permute-start | bytes 786440 | tf_op jit(solution)/shard_map/ppermute | solution.py:77
  239.1 13.8 %collective-permute-start.46 = (f32[2,64,512]{2,1,0:T(8,128)S(1)}, f32[2,64,512]{2,1,0:T(8,128)S(1)}, u32[]{:S(2)}, u32[]{:S(2)}) collective-permute-start(f32[2,64,512]{2,1,0:T(8,128)S(1)} %get-tuple-element.90), channel_id=1, source_target_pairs={{0,24},{8,16},{16,8},{24,0},{1,25},{9,17},{17,9},{25,1},{2,26},{10... | collective-permute-start | bytes 786440 | tf_op jit(solution)/shard_map/ppermute | solution.py:77
  240.1 14.5 %collective-permute-start.45 = (f32[2,64,512]{2,1,0:T(8,128)S(1)}, f32[2,64,512]{2,1,0:T(8,128)S(1)}, u32[]{:S(2)}, u32[]{:S(2)}) collective-permute-start(f32[2,64,512]{2,1,0:T(8,128)S(1)} %get-tuple-element.91), channel_id=1, source_target_pairs={{0,16},{8,24},{16,0},{24,8},{1,17},{9,25},{17,1},{25,9},{2,18},{10... | collective-permute-start | bytes 786440 | tf_op jit(solution)/shard_map/ppermute | solution.py:77
  241.1 19.2 %collective-permute-start.35 = (f32[3,64,512]{2,1,0:T(8,128)S(1)}, f32[3,64,512]{2,1,0:T(8,128)S(1)}, u32[]{:S(2)}, u32[]{:S(2)}) collective-permute-start(f32[3,64,512]{2,1,0:T(8,128)S(1)} %get-tuple-element.86), channel_id=1, source_target_pairs={{0,8},{8,0},{16,24},{24,16},{1,9},{9,1},{17,25},{25,17},{2,10},{10... | collective-permute-start | bytes 1179656 | tf_op jit(solution)/shard_map/ppermute | solution.py:77
  243.1 25.7 %collective-permute-start.37 = (f32[3,64,512]{2,1,0:T(8,128)S(1)}, f32[3,64,512]{2,1,0:T(8,128)S(1)}, u32[]{:S(2)}, u32[]{:S(2)}) collective-permute-start(f32[3,64,512]{2,1,0:T(8,128)S(1)} %get-tuple-element.87), channel_id=1, source_target_pairs={{0,24},{8,16},{16,8},{24,0},{1,25},{9,17},{17,9},{25,1},{2,26},{10... | collective-permute-start | bytes 1179656 | tf_op jit(solution)/shard_map/ppermute | solution.py:77
  246.2 23.9 %collective-permute-start.36 = (f32[3,64,512]{2,1,0:T(8,128)S(1)}, f32[3,64,512]{2,1,0:T(8,128)S(1)}, u32[]{:S(2)}, u32[]{:S(2)}) collective-permute-start(f32[3,64,512]{2,1,0:T(8,128)S(1)} %get-tuple-element.88), channel_id=1, source_target_pairs={{0,16},{8,24},{16,0},{24,8},{1,17},{9,25},{17,1},{25,9},{2,18},{10... | collective-permute-start | bytes 1179656 | tf_op jit(solution)/shard_map/ppermute | solution.py:77
  254.6 15.7 %collective-permute-start.47 = (f32[2,32,512]{2,1,0:T(8,128)S(1)}, f32[2,32,512]{2,1,0:T(8,128)S(1)}, u32[]{:S(2)}, u32[]{:S(2)}) collective-permute-start(f32[2,32,512]{2,1,0:T(8,128)S(1)} %slice.374), channel_id=1, source_target_pairs={{0,2},{1,3},{2,0},{3,1},{4,6},{5,7},{6,4},{7,5},{8,10},{9,11},{10,... | collective-permute-start | bytes 393224 | tf_op jit(solution)/shard_map/ppermute | solution.py:77
  270.3 7.1 %collective-permute-start.38 = (f32[3,32,512]{2,1,0:T(8,128)S(1)}, f32[3,32,512]{2,1,0:T(8,128)S(1)}, u32[]{:S(2)}, u32[]{:S(2)}) collective-permute-start(f32[3,32,512]{2,1,0:T(8,128)S(1)} %slice.366), channel_id=1, source_target_pairs={{0,2},{1,3},{2,0},{3,1},{4,6},{5,7},{6,4},{7,5},{8,10},{9,11},{10,... | collective-permute-start | bytes 589832 | tf_op jit(solution)/shard_map/ppermute | solution.py:77
  270.4 7.1 %collective-permute-start.48 = (f32[2,16,512]{2,1,0:T(8,128)S(1)}, f32[2,16,512]{2,1,0:T(8,128)S(1)}, u32[]{:S(2)}, u32[]{:S(2)}) collective-permute-start(f32[2,16,512]{2,1,0:T(8,128)S(1)} %slice.376), channel_id=1, source_target_pairs={{0,4},{1,5},{2,6},{3,7},{4,0},{5,1},{6,2},{7,3},{8,12},{9,13},{10,... | collective-permute-start | bytes 196616 | tf_op jit(solution)/shard_map/ppermute | solution.py:77
  277.4 5.7 %collective-permute-start.39 = (f32[3,16,512]{2,1,0:T(8,128)S(1)}, f32[3,16,512]{2,1,0:T(8,128)S(1)}, u32[]{:S(2)}, u32[]{:S(2)}) collective-permute-start(f32[3,16,512]{2,1,0:T(8,128)S(1)} %slice.368), channel_id=1, source_target_pairs={{0,4},{1,5},{2,6},{3,7},{4,0},{5,1},{6,2},{7,3},{8,12},{9,13},{10,... | collective-permute-start | bytes 294920 | tf_op jit(solution)/shard_map/ppermute | solution.py:77
  277.5 7.6 %collective-permute-start.51 = (f32[2,16,512]{2,1,0:T(8,128)S(1)}, f32[2,16,512]{2,1,0:T(8,128)S(1)}, u32[]{:S(2)}, u32[]{:S(2)}) collective-permute-start(f32[2,16,512]{2,1,0:T(8,128)S(1)} %slice_add_fusion.29), channel_id=1, source_target_pairs={{0,8},{8,0},{16,24},{24,16},{1,9},{9,1},{17,25},{25,17},{2,10},{10... | collective-permute-start | bytes 196616 | tf_op jit(solution)/shard_map/ppermute | solution.py:77
  278.6 8.0 %collective-permute-start.50 = (f32[2,16,512]{2,1,0:T(8,128)S(1)}, f32[2,16,512]{2,1,0:T(8,128)S(1)}, u32[]{:S(2)}, u32[]{:S(2)}) collective-permute-start(f32[2,16,512]{2,1,0:T(8,128)S(1)} %slice_add_fusion.29), channel_id=1, source_target_pairs={{0,16},{8,24},{16,0},{24,8},{1,17},{9,25},{17,1},{25,9},{2,18},{10... | collective-permute-start | bytes 196616 | tf_op jit(solution)/shard_map/ppermute | solution.py:77
  279.6 7.1 %collective-permute-start.49 = (f32[2,16,512]{2,1,0:T(8,128)S(1)}, f32[2,16,512]{2,1,0:T(8,128)S(1)}, u32[]{:S(2)}, u32[]{:S(2)}) collective-permute-start(f32[2,16,512]{2,1,0:T(8,128)S(1)} %slice_add_fusion.29), channel_id=1, source_target_pairs={{0,24},{8,16},{16,8},{24,0},{1,25},{9,17},{17,9},{25,1},{2,26},{10... | collective-permute-start | bytes 196616 | tf_op jit(solution)/shard_map/ppermute | solution.py:77
  283.1 4.7 %collective-permute-start.42 = (f32[3,16,512]{2,1,0:T(8,128)S(1)}, f32[3,16,512]{2,1,0:T(8,128)S(1)}, u32[]{:S(2)}, u32[]{:S(2)}) collective-permute-start(f32[3,16,512]{2,1,0:T(8,128)S(1)} %slice_add_fusion.28), channel_id=1, source_target_pairs={{0,8},{8,0},{16,24},{24,16},{1,9},{9,1},{17,25},{25,17},{2,10},{10... | collective-permute-start | bytes 294920 | tf_op jit(solution)/shard_map/ppermute | solution.py:77
  284.2 4.6 %collective-permute-start.41 = (f32[3,16,512]{2,1,0:T(8,128)S(1)}, f32[3,16,512]{2,1,0:T(8,128)S(1)}, u32[]{:S(2)}, u32[]{:S(2)}) collective-permute-start(f32[3,16,512]{2,1,0:T(8,128)S(1)} %slice_add_fusion.28), channel_id=1, source_target_pairs={{0,16},{8,24},{16,0},{24,8},{1,17},{9,25},{17,1},{25,9},{2,18},{10... | collective-permute-start | bytes 294920 | tf_op jit(solution)/shard_map/ppermute | solution.py:77
  285.1 5.5 %collective-permute-start.40 = (f32[3,16,512]{2,1,0:T(8,128)S(1)}, f32[3,16,512]{2,1,0:T(8,128)S(1)}, u32[]{:S(2)}, u32[]{:S(2)}) collective-permute-start(f32[3,16,512]{2,1,0:T(8,128)S(1)} %slice_add_fusion.28), channel_id=1, source_target_pairs={{0,24},{8,16},{16,8},{24,0},{1,25},{9,17},{17,9},{25,1},{2,26},{10... | collective-permute-start | bytes 294920 | tf_op jit(solution)/shard_map/ppermute | solution.py:77
  (41 other events, 341.6 us)
Sparse Core Ops, SparseCore 0:
  31.3 29.3 all-gather.1

commit v3 on v2

--- a/solution.py
+++ b/solution.py
@@ -34,7 +34,7 @@
     )
 
 
-def call(body, out_shapes, flops, *args, smem=0):
+def call(body, out_shapes, flops, *args, smem=0, scratch=()):
     specs = [pl.BlockSpec(memory_space=pltpu.SMEM)] * smem
     specs += [pl.BlockSpec(memory_space=pltpu.VMEM)] * (len(args) - smem)
     moved = sum(a.size * a.dtype.itemsize for a in args)
@@ -44,6 +44,7 @@
         out_shape=out_shapes,
         in_specs=specs,
         out_specs=[pl.BlockSpec(memory_space=pltpu.VMEM)] * len(out_shapes),
+        scratch_shapes=scratch,
         compiler_params=pltpu.CompilerParams(vmem_limit_bytes=VMEM_BYTES),
         cost_estimate=pl.CostEstimate(flops=flops, bytes_accessed=moved, transcendentals=0),
     )(*args)
@@ -66,42 +67,69 @@
     return order
 
 
-def row_weights(listed_row, first_row, count, width):
-    block_ids = (first_row + lax.iota(jnp.int32, count)) // width
-    table = lax.iota(jnp.int32, listed_row.shape[0])
-    hits = (block_ids[:, None] == table[None, :]) & (listed_row[None, :] != 0)
-    return jnp.any(hits, axis=1).astype(F32)
+def relative_links(count, place):
+    return jnp.arange(count, dtype=jnp.int32) ^ place
 
 
 def swap(value, axis, size, change):
     return lax.ppermute(value, axis, [(place, place ^ change) for place in range(size)])
 
 
-def split_rows_kernel(order_ref, in_ref, mask_ref, high_ref, low_ref):
-    high, low = split(in_ref[0] * mask_ref[...])
-    high_ref[...] = high
-    low_ref[...] = low
-
-
-def split_rows(array, member, order, group, mask):
-    _, rows, columns = array.shape
-    block = pl.BlockSpec((group, columns), lambda g, order_ref: (g, 0))
+def region_kernel(groups, info_ref, in_ref, high_ref, low_ref):
+    size = in_ref.shape[0] // groups
+    for g in range(groups):
+        value = in_ref[pl.ds(pl.multiple_of(info_ref[g] * size, size), size), :]
+        high_ref[g * size : (g + 1) * size, :], low_ref[g * size : (g + 1) * size, :] = split(value)
+
+
+def factor_kernel(groups, info_ref, in_ref, high_ref, low_ref, ordered_ref):
+    size = in_ref.shape[1] // groups
+    for g in range(groups):
+        value = in_ref[0, pl.ds(pl.multiple_of(info_ref[g] * size, size), size), :]
+        weight = info_ref[groups + g].astype(F32)
+        ordered_ref[g * size : (g + 1) * size, :] = value * weight
+    high_ref[...], low_ref[...] = split(ordered_ref[...].T)
+
+
+def place_kernel(groups, info_ref, in_ref, out_ref):
+    size = in_ref.shape[2]
+    for g in range(groups):
+        start = pl.ds(pl.multiple_of(info_ref[g] * size, size), size)
+        for c in range(in_ref.shape[1]):
+            out_ref[c, start, :] = in_ref[g, c]
+
+
+def ring_kernel(member, first, waits, info_ref, *refs):
+    outs = refs[-2:]
+    for way in range(2):
+        own = refs[way][0] * info_ref[3 + member].astype(F32)
+        if first:
+            outs[way][...] = own
+        else:
+            outs[way][...] = jnp.where(info_ref[2] != 0, own, refs[2 + way][...])
+
+
+def ring_stage(info, factors, member, column, half, unit, arrived, tokens):
+    block = [
+        pl.BlockSpec((1, half, unit), lambda i, info_ref, way=way: (member, info_ref[way], column))
+        for way in range(2)
+    ]
+    whole = pl.BlockSpec((half, unit), lambda i, info_ref: (0, 0))
     return pl.pallas_call(
-        split_rows_kernel,
-        out_shape=[shape(rows, columns, dtype=BF16)] * 2,
+        functools.partial(ring_kernel, member, not arrived, len(tokens)),
+        out_shape=[shape(half, unit)] * 2,
         grid_spec=pltpu.PrefetchScalarGridSpec(
             num_scalar_prefetch=1,
-            grid=(rows // group,),
-            in_specs=[
-                pl.BlockSpec((1, group, columns), lambda g, order_ref: (member, order_ref[g], 0)),
-                pl.BlockSpec((group, 1), lambda g, order_ref: (order_ref[g], 0)),
-            ],
-            out_specs=[block, block],
+            grid=(1,),
+            in_specs=block
+            + [whole] * len(arrived)
+            + [pl.BlockSpec(memory_space=pl.ANY)] * len(tokens),
+            out_specs=[whole, whole],
         ),
         cost_estimate=pl.CostEstimate(
-            flops=2 * rows * columns, bytes_accessed=8 * rows * columns, transcendentals=0
+            flops=2 * half * unit, bytes_accessed=24 * half * unit, transcendentals=0
         ),
-    )(order, array, mask)
+    )(info, factors, factors, *arrived, *tokens)
 
 
 def unit_kernel(count, place_ref, high_ref, low_ref, *refs):
@@ -136,11 +164,11 @@
 
 
 def parent_kernel(
-    children, chooser_ref, mask_ref, left_ref, right_ref, own_ref, links_ref,
+    children, weight_ref, chooser_ref, left_ref, right_ref, own_ref, links_ref,
     col_ref, turned_ref, keep_ref, send_ref,
 ):
     sums = jnp.concatenate([left_ref[...], right_ref[...]], axis=1)
-    column = -sums * mask_ref[...]
+    column = -sums * weight_ref[0].astype(F32)
     col_ref[...] = column
     column_pair = split(column)
     parent_pair = split(own_ref[0])
@@ -199,8 +227,6 @@
     unit = width // 2
     units = [(j, lo) for j in range(members) for lo in range(0, width, unit)]
 
-    links = lax.all_gather(parent_factor, "col", axis=1, tiled=True)
-
     def ring(forward):
         pairs = []
         for col in range(col_count):
@@ -220,39 +246,81 @@
     backward_place = (row_count - forward_place) % row_count
     places = jnp.stack([forward_place, backward_place]).astype(jnp.int32)
     is_source = row_place == source
-    col_first = col_place * cols_here
     half = cols_here // 2
-    col_masks = [row_weights(listed[j], col_first, cols_here, width)[:, None] for j in range(members)]
-
-    def chunk(j, lo, way):
-        start = (col_place % ratio) * cols_here + way * half
-        block = lax.dynamic_slice(factor_cols, (j, start, lo), (1, half, unit))[0]
-        return block * col_masks[j][way * half : (way + 1) * half]
-
-    chunks = [[chunk(j, lo, way) for j, lo in units] for way in range(2)]
-    received = [[], []]
-    for stage in range(len(units) + row_count - 2):
-        for way in range(2):
-            if stage == 0:
-                moving = chunks[way][0]
-            elif stage < len(units):
-                moving = jnp.where(is_source, chunks[way][stage], received[way][-1])
+
+    relative = jnp.array(reversed_bits(col_count), jnp.int32) ^ col_place
+    col_weights = listed[:, col_place * cols_here // width]
+    own_weights = listed[:, (first_row + col_place * group) // width]
+    group_weights = jnp.take(listed, (first_row + relative * group) // width, axis=1)
+
+    gathered = parent_factor[None]
+    for bit in reversed(range(col_bits)):
+        gathered = jnp.stack([gathered, swap(gathered, "col", col_count, 1 << bit)], axis=1)
+        gathered = gathered.reshape((-1,) + parent_factor.shape)
+
+    first_block = (col_place % ratio) * 2
+    info = jnp.concatenate(
+        [jnp.stack([first_block, first_block + 1, is_source.astype(jnp.int32)]), col_weights]
+    ).astype(jnp.int32)
+    lanes = len(units) // members
+    moved = [[[], []] for _ in range(lanes)]
+    received = [[[], []] for _ in range(lanes)]
+    tokens = []
+    prepared = []
+
+    def prepare(stage):
+        if stage == 0:
+            prepared.append(
+                call(
+                    functools.partial(region_kernel, col_count),
+                    [shape(rows_here, cols_here, dtype=BF16)] * 2,
+                    rows_here * cols_here,
+                    relative, region_inverse,
+                    smem=1,
+                )
+            )
+        elif stage <= children:
+            prepared.append(
+                call(
+                    functools.partial(factor_kernel, col_count),
+                    [shape(width, rows_here, dtype=BF16)] * 2,
+                    rows_here * width,
+                    jnp.concatenate([relative, group_weights[stage]]),
+                    lax.slice_in_dim(factor_cols, stage, stage + 1, axis=0),
+                    smem=1,
+                    scratch=[pltpu.VMEM((rows_here, width), F32)],
+                )
+            )
+        else:
+            return []
+        return [prepared[-1][0]]
+
+    for stage in range(members + row_count - 2):
+        for lane in range(lanes):
+            arrived = [received[lane][way][-1] for way in range(2)] if stage else []
+            if stage < members:
+                moving = ring_stage(
+                    info, factor_cols, stage, lane, half, unit, arrived, tokens
+                )
+                tokens = [moving[0]]
             else:
-                moving = received[way][-1]
-            received[way].append(lax.ppermute(moving, AXES, ring(way == 0)))
-
-    relative = jnp.array(reversed_bits(col_count), jnp.int32) ^ col_place
-    ones = jnp.ones((rows_here, 1), F32)
-    region = split_rows(region_inverse[None], 0, relative, group, ones)
-    row_masks = [row_weights(listed[j], first_row, rows_here, width)[:, None] for j in range(members)]
-    turned_factors = []
-    for c in range(children):
-        pair = split_rows(factor_cols, c + 1, relative, group, row_masks[c + 1])
-        turned_factors.append([value.T for value in pair])
-
-    own_first = first_row + col_place * group
-    own_masks = [row_weights(listed[j], own_first, group, width)[:, None] for j in range(members)]
-    own = lax.dynamic_slice_in_dim(factor_cols, col_place * group, group, 1) * jnp.stack(own_masks)
+                moving = arrived
+            for way in range(2):
+                moved[lane][way].append(moving[way])
+                received[lane][way].append(lax.ppermute(moving[way], AXES, ring(way == 0)))
+        tokens = tokens + prepare(stage)
+
+    region, *turned_factors = prepared
+
+    links = call(
+        functools.partial(place_kernel, col_count),
+        [shape(*parent_factor.shape[:1], width, width)],
+        0,
+        relative_links(col_count, col_place), gathered,
+        smem=1,
+    )[0]
+    own = lax.dynamic_slice_in_dim(factor_cols, col_place * group, group, 1)
+    own = own * own_weights.astype(F32)[:, None, None]
 
     halving = jnp.array(reversed_bits(col_count), jnp.int32).reshape(2, 1, col_count // 2, 1)
     by_row = lax.iota(jnp.int32, row_count).reshape(1, row_count, 1, 1) ^ row_place
@@ -261,10 +329,11 @@
     chooser = (wanted == lax.iota(jnp.int32, width)[None, :]).astype(BF16)
 
     def column_unit(index):
+        member, lane = divmod(index, lanes)
         candidates = []
         for way in range(2):
-            candidates.append(chunks[way][index])
-            candidates += received[way][index : index + row_count - 1]
+            candidates.append(moved[lane][way][member])
+            candidates += received[lane][way][member : member + row_count - 1]
         size = rows_here // 2
         return call(
             functools.partial(unit_kernel, row_count),
@@ -323,7 +392,8 @@
         [shape(group, width), shape(children, group, width)]
         + [shape(members, width // 2, width)] * 2,
         6 * (1 + 3 * children) * group * width * width,
-        chooser, own_masks[0], sums[0], sums[1], own, links,
+        own_weights, chooser, sums[0], sums[1], own, links,
+        smem=1,
     )
     parent_totals = total_rows(keep, send)
 
@@ -345,7 +415,7 @@
     child_cols = []
     for c in range(children):
         column = jnp.concatenate(sums[2 * c + 2 : 2 * c + 4], axis=1)
-        child_cols.append(-(column + turned[c]) * own_masks[c + 1])
+        child_cols.append(-(column + turned[c]) * own_weights[c + 1].astype(F32))
     uppers = parent_totals[1:] - framed
     diags = diag_inverse + jnp.concatenate([parent_totals[:1], child_totals])
     return jnp.stack([parent_col] + child_cols), diags, uppers

time: 301 us -> 229 us (0.76)
  other arithmetic: 34.1 us -> 10 us
  waiting for transfers between devices: 117 us -> 95.3 us
  between operations: 15 us -> 3.01 us
  local copies, waits for them, and re-layouts: 28 us -> 19.3 us
  starting transfers between devices: 57 us -> 52.3 us
    ppermute x16 -> x20, waiting for transfers between devices: 43.9 us -> 5.84 us  [shards(): received[lane][way].append(lax.ppermute(moving[way], AXES, ring(way == 0)))]
    ppermute x36 -> x39, waiting for transfers between devices: 72.8 us -> 89.5 us  [swap(): lax.ppermute(value, axis, [(place, place ^ change) for place in range(siz...]
    select_n x13 -> x1, other arithmetic: 16.6 us -> 0.07 us  [shards(): jnp.take(listed, (first_row + relative * group) // width, axis=1)]
    pallas_call x4 -> x0, local copies, waits for them, and re-layouts: 6.75 us -> none  [split_rows(): pl.pallas_call(split_rows_kernel, out_shape=[shape(rows, columns, dtype=B...]
    unnamed x104 -> x85, local copies, waits for them, and re-layouts: 17.2 us -> 11.7 us
    slice x3, local copies, waits for them, and re-layouts: 0.02 us -> 5.5 us  [the longest x1 4.69 us: prepare(): lax.slice_in_dim(factor_cols, stage, stage + 1, axis=0)]
    pallas_call x3 -> x6, Pallas kernels: 20.1 us -> 16 us  [ring_stage(): pl.pallas_call(functools.partial(ring_kernel, member, not arrived, len(to...]
    pallas_call x13 -> x17, Pallas kernels: 28.2 us -> 32.3 us  [call(): pl.pallas_call(body, out_shape=out_shapes, in_specs=specs, out_specs=[pl....]
  transfers between devices with their start and end apart: 53 -> 59, of which waited for: 28 -> 22; matrix products, arithmetic and copies ran while one was open for 13% -> 6% of each run, Pallas kernels for 16% -> 20%
where the time goes in v3:
time: 229 us; the launch traced here: 228 us
  waiting for transfers between devices  95.3 us (42%)
  starting transfers between devices  52.3 us (23%)
  Pallas kernels  48.3 us (21%)
  local copies, waits for them, and re-layouts  19.3 us (8%)
  other arithmetic  10 us (4%)
  between operations  3.01 us (1%)
    ppermute x39, waiting for transfers between devices, swap(): lax.ppermute(value, axis, [(place, place ^ change) for place in range(siz...  89.5 us
    pallas_call x17, Pallas kernels, call(): pl.pallas_call(body, out_shape=out_shapes, in_specs=specs, out_specs=[pl....  32.3 us
    ppermute x39, starting transfers between devices, swap(): lax.ppermute(value, axis, [(place, place ^ change) for place in range(siz...  30.9 us
    ppermute x20, starting transfers between devices, shards(): received[lane][way].append(lax.ppermute(moving[way], AXES, ring(way == 0)))  21.4 us
    pallas_call x6, Pallas kernels, ring_stage(): pl.pallas_call(functools.partial(ring_kernel, member, not arrived, len(to...  16 us
    unnamed x85, local copies, waits for them, and re-layouts  11.7 us
    ppermute x20, waiting for transfers between devices, shards(): received[lane][way].append(lax.ppermute(moving[way], AXES, ring(way == 0)))  5.84 us
    slice x1, local copies, waits for them, and re-layouts, prepare(): lax.slice_in_dim(factor_cols, stage, stage + 1, axis=0)  4.69 us
  transfers between devices with their start and end apart: 59, of which 22 were waited for; matrix products, arithmetic and copies ran while one was open for 6% of the time, Pallas kernels for 20%

profile of v3, /device:TPU:0, one launch (start us, length us, event | category | flops | bytes accessed | tf_op | source)
XLA Modules:
  0.0 228.3 jit_solution(10294620640267807855)
XLA Ops:
  2.3 2.5 %shard_map.95 = (f32[256,256]{1,0:T(8,128)}, f32[256,256]{1,0:T(8,128)}) custom-call(s32[6]{0:T(128)} %pad_add_fusion.1.info_ref, f32[3,1024,512]{2,1,0:T(8,128)} %refs_1_.11, f32[3,1024,512]{2,1,0:T(8,128)} %refs_1_.11), custom_call_target="tpu_custom_call" | custom-call | flops 131072 | bytes 1572864 | tf_op jit(solution)/shard_map/pallas_call | solution.py:118
  4.8 2.9 %collective-permute-start = (f32[256,256]{1,0:T(8,128)}, f32[256,256]{1,0:T(8,128)S(1)}, u32[]{:S(2)}, u32[]{:S(2)}) collective-permute-start(f32[256,256]{1,0:T(8,128)} %get-tuple-element.44.refs_2_.refs_0_), channel_id=1, source_target_pairs={{0,8},{8,24},{24,16},{16,0},{1,9},{9,25},{25,17},{17,1},{10,2},{2,... | collective-permute-start | bytes 786440 | tf_op jit(solution)/shard_map/ppermute | solution.py:310
  7.9 2.7 %shard_map.96 = (f32[256,256]{1,0:T(8,128)}, f32[256,256]{1,0:T(8,128)}) custom-call(s32[6]{0:T(128)} %pad_add_fusion.1.info_ref, f32[3,1024,512]{2,1,0:T(8,128)} %refs_1_.11, f32[3,1024,512]{2,1,0:T(8,128)} %refs_1_.11, f32[256,256]{1,0:T(8,128)} %get-tuple-element.44.refs_2_.refs_0_), custom_call_target="tpu_custom_call" | custom-call | flops 131072 | bytes 1572864 | tf_op jit(solution)/shard_map/pallas_call | solution.py:118
  10.6 1.8 collective-permute-start.4
  12.6 2.9 %collective-permute-start.18 = (f32[1,2,64,512]{3,2,1,0:T(8,128)S(1)}, f32[1,2,64,512]{3,2,1,0:T(8,128)S(1)}, u32[]{:S(2)}, u32[]{:S(2)}) collective-permute-start(f32[1,2,64,512]{3,2,1,0:T(8,128)S(1)} %bitcast.33), channel_id=1, source_target_pairs={{0,4},{1,5},{2,6},{3,7},{4,0},{5,1},{6,2},{7,3},{8,12},{9,13},{10,... | collective-permute-start | bytes 786440 | tf_op jit(solution)/shard_map/ppermute | solution.py:75
  15.6 4.7 %fusion.25 = (f32[1,1024,512]{2,1,0:T(8,128)}, f32[1,1024,512]{2,1,0:T(8,128)}) fusion(f32[3,1024,512]{2,1,0:T(8,128)} %refs_1_.11), kind=kLoop, calls=%fused_computation.101 | loop fusion | bytes 8388608 | tf_op jit(solution)/shard_map/slice | solution.py:289
  22.8 1.6 copy-done.15
  27.3 2.7 %shard_map.97 = (f32[256,256]{1,0:T(8,128)}, f32[256,256]{1,0:T(8,128)}) custom-call(s32[6]{0:T(128)} %pad_add_fusion.1.info_ref, f32[3,1024,512]{2,1,0:T(8,128)} %refs_1_.11, f32[3,1024,512]{2,1,0:T(8,128)} %refs_1_.11, f32[256,256]{1,0:T(8,128)} %copy-done.17, f32[256,256]{1,0:T(8,128)} %copy-done.19, f32[256,256]{1,0:T(8,128)} %get-tuple-element.46.refs_4_.refs_0_, ...), custom_call_target="tpu_custom_call" | custom-call | flops 131072 | bytes 1572864 | tf_op jit(solution)/shard_map/pallas_call | solution.py:118
  30.0 1.5 collective-permute-start.2
  33.5 2.7 %shard_map.98 = (f32[256,256]{1,0:T(8,128)}, f32[256,256]{1,0:T(8,128)}) custom-call(s32[6]{0:T(128)} %pad_add_fusion.1.info_ref, f32[3,1024,512]{2,1,0:T(8,128)} %refs_1_.11, f32[3,1024,512]{2,1,0:T(8,128)} %refs_1_.11, f32[256,256]{1,0:T(8,128)} %copy-done.26, f32[256,256]{1,0:T(8,128)} %copy-done.28, f32[256,256]{1,0:T(8,128)} %get-tuple-element.47.refs_4_.refs_0_), custom_call_target="tpu_custom_call" | custom-call | flops 131072 | bytes 1572864 | tf_op jit(solution)/shard_map/pallas_call | solution.py:118
  36.2 1.5 collective-permute-start.11
  38.3 1.1 fusion.2
  39.4 1.6 collective-permute-start.19
  41.0 1.6 copy-done.5
  42.5 1.2 shard_map.99
  45.5 2.7 %shard_map.100 = (f32[256,256]{1,0:T(8,128)}, f32[256,256]{1,0:T(8,128)}) custom-call(s32[6]{0:T(128)} %pad_add_fusion.1.info_ref, f32[3,1024,512]{2,1,0:T(8,128)} %refs_1_.11, f32[3,1024,512]{2,1,0:T(8,128)} %refs_1_.11, f32[256,256]{1,0:T(8,128)} %copy-done.6, f32[256,256]{1,0:T(8,128)} %copy-done.8, f32[256,256]{1,0:T(8,128)} %get-tuple-element.50.refs_4_.refs_0_, ...), custom_call_target="tpu_custom_call" | custom-call | flops 131072 | bytes 1572864 | tf_op jit(solution)/shard_map/pallas_call | solution.py:118
  48.2 1.5 collective-permute-start.6
  51.1 2.7 %shard_map.102 = (f32[256,256]{1,0:T(8,128)}, f32[256,256]{1,0:T(8,128)}) custom-call(s32[6]{0:T(128)} %pad_add_fusion.1.info_ref, f32[3,1024,512]{2,1,0:T(8,128)} %refs_1_.11, f32[3,1024,512]{2,1,0:T(8,128)} %refs_1_.11, f32[256,256]{1,0:T(8,128)} %copy-done.10, f32[256,256]{1,0:T(8,128)} %copy-done.12, f32[256,256]{1,0:T(8,128)} %get-tuple-element.52.refs_4_.refs_0_), custom_call_target="tpu_custom_call" | custom-call | flops 131072 | bytes 1572864 | tf_op jit(solution)/shard_map/pallas_call | solution.py:118
  53.8 1.5 collective-permute-start.13
  57.8 1.6 copy-done.4
  59.4 1.2 shard_map.113
  60.7 1.3 dynamic-slice_multiply_fusion.own_ref
  62.0 1.5 collective-permute-start.26
  64.6 1.5 collective-permute-start.21
  66.2 3.6 %collective-permute-done.7.refs_7_.refs_6_.refs_5_ = f32[256,256]{1,0:T(8,128)} collective-permute-done((f32[256,256]{1,0:T(8,128)}, f32[256,256]{1,0:T(8,128)}, u32[]{:S(2)}, u32[]{:S(2)}) %collective-permute-start.7) | collective-permute-done | bytes 262176 | tf_op jit(solution)/shard_map/ppermute | solution.py:310
  70.3 2.1 shard_map.103
  72.6 2.1 shard_map.101
  74.8 1.1 pad_maximum_fusion.1
  76.0 1.6 collective-permute-start.31
  78.1 2.1 shard_map.106
  80.2 1.6 collective-permute-start.36
  83.3 2.0 shard_map.107
  87.0 2.1 shard_map.108
  90.5 1.1 collective-permute-done.37.refs_7_
  91.6 2.0 shard_map.109
  96.0 1.7 collective-permute-start.9
  97.8 6.9 %collective-permute-done.16 = f32[256,256]{1,0:T(8,128)S(1)} collective-permute-done((f32[256,256]{1,0:T(8,128)S(1)}, f32[256,256]{1,0:T(8,128)S(1)}, u32[]{:S(2)}, u32[]{:S(2)}) %collective-permute-start.16) | collective-permute-done | bytes 262176 | tf_op jit(solution)/shard_map/ppermute | solution.py:75
  105.1 5.2 %collective-permute-done.9 = f32[256,256]{1,0:T(8,128)S(1)} collective-permute-done((f32[256,256]{1,0:T(8,128)S(1)}, f32[256,256]{1,0:T(8,128)S(1)}, u32[]{:S(2)}, u32[]{:S(2)}) %collective-permute-start.9) | collective-permute-done | bytes 262176 | tf_op jit(solution)/shard_map/ppermute | solution.py:75
  110.6 8.4 %collective-permute-done.17 = f32[128,256]{1,0:T(8,128)S(1)} collective-permute-done((f32[128,256]{1,0:T(8,128)S(1)}, f32[128,256]{1,0:T(8,128)S(1)}, u32[]{:S(2)}, u32[]{:S(2)}) %collective-permute-start.17) | collective-permute-done | bytes 131104 | tf_op jit(solution)/shard_map/ppermute | solution.py:75
  119.6 6.1 %collective-permute-done.10 = f32[128,256]{1,0:T(8,128)S(1)} collective-permute-done((f32[128,256]{1,0:T(8,128)S(1)}, f32[128,256]{1,0:T(8,128)S(1)}, u32[]{:S(2)}, u32[]{:S(2)}) %collective-permute-start.10) | collective-permute-done | bytes 131104 | tf_op jit(solution)/shard_map/ppermute | solution.py:75
  125.8 2.1 collective-permute-start.25
  127.9 7.7 %collective-permute-done.29 = f32[256,256]{1,0:T(8,128)S(1)} collective-permute-done((f32[256,256]{1,0:T(8,128)S(1)}, f32[256,256]{1,0:T(8,128)S(1)}, u32[]{:S(2)}, u32[]{:S(2)}) %collective-permute-start.29) | collective-permute-done | bytes 262176 | tf_op jit(solution)/shard_map/ppermute | solution.py:75
  137.2 5.4 %shard_map.105 = (f32[128,512]{1,0:T(8,128)S(1)}, f32[2,128,512]{2,1,0:T(8,128)S(1)}, f32[3,256,512]{2,1,0:T(8,128)S(1)}, f32[3,256,512]{2,1,0:T(8,128)S(1)}) custom-call(s32[3]{0:T(128)S(1)} %get-tuple-element.83.weight_ref, bf16[512,512]{1,0:T(8,128)(2,1)S(1)} %copy-done.14, f32[128,256]{1,0:T(8,128)S(1)} %fusion.23.left_ref, ...), custom_call_target="tpu_custom_call" | custom-call | flops 1409286144 | bytes 7602188 | tf_op jit(solution)/shard_map/pallas_call | solution.py:42
  142.7 2.4 %shard_map.110 = (f32[2,128,512]{2,1,0:T(8,128)S(1)}, f32[2,64,512]{2,1,0:T(8,128)S(1)}, f32[2,512,512]{2,1,0:T(8,128)S(1)}) custom-call(f32[3,128,512]{2,1,0:T(8,128)S(1)} %dynamic-slice_multiply_fusion.own_ref, f32[2,512,512]{2,1,0:T(8,128)S(1)} %shard_map.104.links_ref, f32[2,64,512]{2,1,0:T(8,128)S(1)} %copy-done.25, f32[3,64,512]{2,1,0:T(8,128)S(1)} %copy-done.16), custom_call_target="tpu_custom_call" | custom-call | flops 805306368 | bytes 6422528 | tf_op jit(solution)/shard_map/pallas_call | solution.py:42
  145.1 4.1 %shard_map.116 = (f32[2,256,512]{2,1,0:T(8,128)S(1)}, f32[2,256,512]{2,1,0:T(8,128)S(1)}) custom-call(bf16[512,512]{1,0:T(8,128)(2,1)S(1)} %copy-done.14, f32[3,128,512]{2,1,0:T(8,128)S(1)} %dynamic-slice_multiply_fusion.own_ref, f32[2,128,512]{2,1,0:T(8,128)S(1)} %get-tuple-element.66.turned_ref, f32[2,128,512]{2,1,0:T(8,128)S(1)} %get-tuple-element.73.lifted_ref, ...), custom_call_target="tpu_custom_call" | custom-call | flops 1207959552 | bytes 8650752 | tf_op jit(solution)/shard_map/pallas_call | solution.py:42
  150.6 1.6 collective-permute-start.39
  152.3 6.9 %collective-permute-done.34 = f32[256,256]{1,0:T(8,128)S(1)} collective-permute-done((f32[256,256]{1,0:T(8,128)S(1)}, f32[256,256]{1,0:T(8,128)S(1)}, u32[]{:S(2)}, u32[]{:S(2)}) %collective-permute-start.34) | collective-permute-done | bytes 262176 | tf_op jit(solution)/shard_map/ppermute | solution.py:75
  159.2 2.9 %collective-permute-start.35 = (f32[128,256]{1,0:T(8,128)S(1)}, f32[128,256]{1,0:T(8,128)S(1)}, u32[]{:S(2)}, u32[]{:S(2)}) collective-permute-start(f32[128,256]{1,0:T(8,128)S(1)} %slice_add_fusion.18), channel_id=1, source_target_pairs={{0,4},{1,5},{2,6},{3,7},{4,0},{5,1},{6,2},{7,3},{8,12},{9,13},{10,... | collective-permute-start | bytes 393224 | tf_op jit(solution)/shard_map/ppermute | solution.py:75
  162.2 4.5 %collective-permute-done.39 = f32[256,256]{1,0:T(8,128)S(1)} collective-permute-done((f32[256,256]{1,0:T(8,128)S(1)}, f32[256,256]{1,0:T(8,128)S(1)}, u32[]{:S(2)}, u32[]{:S(2)}) %collective-permute-start.39) | collective-permute-done | bytes 262176 | tf_op jit(solution)/shard_map/ppermute | solution.py:75
  166.7 1.1 collective-permute-start.40
  167.8 6.8 %collective-permute-done.40 = f32[128,256]{1,0:T(8,128)S(1)} collective-permute-done((f32[128,256]{1,0:T(8,128)S(1)}, f32[128,256]{1,0:T(8,128)S(1)}, u32[]{:S(2)}, u32[]{:S(2)}) %collective-permute-start.40) | collective-permute-done | bytes 131104 | tf_op jit(solution)/shard_map/ppermute | solution.py:75
  175.6 2.9 %collective-permute-start.53 = (f32[2,64,512]{2,1,0:T(8,128)S(1)}, f32[2,64,512]{2,1,0:T(8,128)S(1)}, u32[]{:S(2)}, u32[]{:S(2)}) collective-permute-start(f32[2,64,512]{2,1,0:T(8,128)S(1)} %get-tuple-element.93), channel_id=1, source_target_pairs={{0,24},{8,16},{16,8},{24,0},{1,25},{9,17},{17,9},{25,1},{2,26},{10... | collective-permute-start | bytes 786440 | tf_op jit(solution)/shard_map/ppermute | solution.py:75
  179.6 4.6 %collective-permute-done.51 = f32[2,64,512]{2,1,0:T(8,128)S(1)} collective-permute-done((f32[2,64,512]{2,1,0:T(8,128)S(1)}, f32[2,64,512]{2,1,0:T(8,128)S(1)}, u32[]{:S(2)}, u32[]{:S(2)}) %collective-permute-start.51) | collective-permute-done | bytes 262176 | tf_op jit(solution)/shard_map/ppermute | solution.py:75
  185.2 5.2 %collective-permute-done.52 = f32[2,64,512]{2,1,0:T(8,128)S(1)} collective-permute-done((f32[2,64,512]{2,1,0:T(8,128)S(1)}, f32[2,64,512]{2,1,0:T(8,128)S(1)}, u32[]{:S(2)}, u32[]{:S(2)}) %collective-permute-start.52) | collective-permute-done | bytes 262176 | tf_op jit(solution)/shard_map/ppermute | solution.py:75
  190.6 7.7 %collective-permute-done.42 = f32[3,64,512]{2,1,0:T(8,128)S(1)} collective-permute-done((f32[3,64,512]{2,1,0:T(8,128)S(1)}, f32[3,64,512]{2,1,0:T(8,128)S(1)}, u32[]{:S(2)}, u32[]{:S(2)}) %collective-permute-start.42) | collective-permute-done | bytes 393248 | tf_op jit(solution)/shard_map/ppermute | solution.py:75
  198.3 7.7 %collective-permute-done.43 = f32[3,64,512]{2,1,0:T(8,128)S(1)} collective-permute-done((f32[3,64,512]{2,1,0:T(8,128)S(1)}, f32[3,64,512]{2,1,0:T(8,128)S(1)}, u32[]{:S(2)}, u32[]{:S(2)}) %collective-permute-start.43) | collective-permute-done | bytes 393248 | tf_op jit(solution)/shard_map/ppermute | solution.py:75
  206.3 1.3 collective-permute-start.55
  207.6 5.7 %collective-permute-done.45 = f32[3,32,512]{2,1,0:T(8,128)S(1)} collective-permute-done((f32[3,32,512]{2,1,0:T(8,128)S(1)}, f32[3,32,512]{2,1,0:T(8,128)S(1)}, u32[]{:S(2)}, u32[]{:S(2)}) %collective-permute-start.45) | collective-permute-done | bytes 196640 | tf_op jit(solution)/shard_map/ppermute | solution.py:75
  213.5 1.6 collective-permute-start.56
  215.1 1.4 collective-permute-start.57
  217.0 2.0 collective-permute-done.46
  219.1 1.6 collective-permute-start.47
  220.7 1.4 collective-permute-start.48
  222.7 2.0 collective-permute-done.47
  (225 shorter events, 36.3 us)
Async XLA Ops:
  4.8 21.6 %collective-permute-start = (f32[256,256]{1,0:T(8,128)}, f32[256,256]{1,0:T(8,128)S(1)}, u32[]{:S(2)}, u32[]{:S(2)}) collective-permute-start(f32[256,256]{1,0:T(8,128)} %get-tuple-element.44.refs_2_.refs_0_), channel_id=1, source_target_pairs={{0,8},{8,24},{24,16},{16,0},{1,9},{9,25},{25,17},{17,1},{10,2},{2,... | collective-permute-start | bytes 786440 | tf_op jit(solution)/shard_map/ppermute | solution.py:310
  7.8 18.7 %collective-permute-start.1 = (f32[256,256]{1,0:T(8,128)}, f32[256,256]{1,0:T(8,128)S(1)}, u32[]{:S(2)}, u32[]{:S(2)}) collective-permute-start(f32[256,256]{1,0:T(8,128)} %get-tuple-element.45.refs_4_), channel_id=1, source_target_pairs={{8,0},{24,8},{16,24},{0,16},{9,1},{25,9},{17,25},{1,17},{2,10},{18... | collective-permute-start | bytes 786440 | tf_op jit(solution)/shard_map/ppermute | solution.py:310
  10.6 21.5 %collective-permute-start.4 = (f32[256,256]{1,0:T(8,128)}, f32[256,256]{1,0:T(8,128)S(1)}, u32[]{:S(2)}, u32[]{:S(2)}) collective-permute-start(f32[256,256]{1,0:T(8,128)} %get-tuple-element.46.refs_4_.refs_0_), channel_id=1, source_target_pairs={{0,8},{8,24},{24,16},{16,0},{1,9},{9,25},{25,17},{17,1},{10,2},{2,... | collective-permute-start | bytes 786440 | tf_op jit(solution)/shard_map/ppermute | solution.py:310
  12.4 19.7 %collective-permute-start.5 = (f32[256,256]{1,0:T(8,128)}, f32[256,256]{1,0:T(8,128)S(1)}, u32[]{:S(2)}, u32[]{:S(2)}) collective-permute-start(f32[256,256]{1,0:T(8,128)} %get-tuple-element.49.refs_4_), channel_id=1, source_target_pairs={{8,0},{24,8},{16,24},{0,16},{9,1},{25,9},{17,25},{1,17},{2,10},{18... | collective-permute-start | bytes 786440 | tf_op jit(solution)/shard_map/ppermute | solution.py:310
  12.6 25.7 %collective-permute-start.18 = (f32[1,2,64,512]{3,2,1,0:T(8,128)S(1)}, f32[1,2,64,512]{3,2,1,0:T(8,128)S(1)}, u32[]{:S(2)}, u32[]{:S(2)}) collective-permute-start(f32[1,2,64,512]{3,2,1,0:T(8,128)S(1)} %bitcast.33), channel_id=1, source_target_pairs={{0,4},{1,5},{2,6},{3,7},{4,0},{5,1},{6,2},{7,3},{8,12},{9,13},{10,... | collective-permute-start | bytes 786440 | tf_op jit(solution)/shard_map/ppermute | solution.py:75
  30.0 14.7 %collective-permute-start.2 = (f32[256,256]{1,0:T(8,128)}, f32[256,256]{1,0:T(8,128)S(1)}, u32[]{:S(2)}, u32[]{:S(2)}) collective-permute-start(f32[256,256]{1,0:T(8,128)} %get-tuple-element.47.refs_4_.refs_0_), channel_id=1, source_target_pairs={{0,8},{8,24},{24,16},{16,0},{1,9},{9,25},{25,17},{17,1},{10,2},{2,... | collective-permute-start | bytes 786440 | tf_op jit(solution)/shard_map/ppermute | solution.py:310
  31.5 13.2 %collective-permute-start.3 = (f32[256,256]{1,0:T(8,128)}, f32[256,256]{1,0:T(8,128)S(1)}, u32[]{:S(2)}, u32[]{:S(2)}) collective-permute-start(f32[256,256]{1,0:T(8,128)} %get-tuple-element.48.refs_4_), channel_id=1, source_target_pairs={{8,0},{24,8},{16,24},{0,16},{9,1},{25,9},{17,25},{1,17},{2,10},{18... | collective-permute-start | bytes 786440 | tf_op jit(solution)/shard_map/ppermute | solution.py:310
  36.2 13.5 %collective-permute-start.11 = (f32[256,256]{1,0:T(8,128)}, f32[256,256]{1,0:T(8,128)S(1)}, u32[]{:S(2)}, u32[]{:S(2)}) collective-permute-start(f32[256,256]{1,0:T(8,128)} %get-tuple-element.50.refs_4_.refs_0_), channel_id=1, source_target_pairs={{0,8},{8,24},{24,16},{16,0},{1,9},{9,25},{25,17},{17,1},{10,2},{2,... | collective-permute-start | bytes 786440 | tf_op jit(solution)/shard_map/ppermute | solution.py:310
  37.7 12.0 %collective-permute-start.12 = (f32[256,256]{1,0:T(8,128)}, f32[256,256]{1,0:T(8,128)S(1)}, u32[]{:S(2)}, u32[]{:S(2)}) collective-permute-start(f32[256,256]{1,0:T(8,128)} %get-tuple-element.56.refs_4_), channel_id=1, source_target_pairs={{8,0},{24,8},{16,24},{0,16},{9,1},{25,9},{17,25},{1,17},{2,10},{18... | collective-permute-start | bytes 786440 | tf_op jit(solution)/shard_map/ppermute | solution.py:310
  39.4 35.4 %collective-permute-start.19 = (f32[2,2,64,512]{3,2,1,0:T(8,128)}, f32[2,2,64,512]{3,2,1,0:T(8,128)}, u32[]{:S(2)}, u32[]{:S(2)}) collective-permute-start(f32[2,2,64,512]{3,2,1,0:T(8,128)} %get-tuple-element.110), channel_id=1, source_target_pairs={{0,2},{1,3},{2,0},{3,1},{4,6},{5,7},{6,4},{7,5},{8,10},{9,11},{10,... | collective-permute-start | bytes 1572872 | tf_op jit(solution)/shard_map/ppermute | solution.py:75
  48.2 16.4 %collective-permute-start.6 = (f32[256,256]{1,0:T(8,128)}, f32[256,256]{1,0:T(8,128)}, u32[]{:S(2)}, u32[]{:S(2)}) collective-permute-start(f32[256,256]{1,0:T(8,128)} %get-tuple-element.52.refs_4_.refs_0_), channel_id=1, source_target_pairs={{0,8},{8,24},{24,16},{16,0},{1,9},{9,25},{25,17},{17,1},{10,2},{2,... | collective-permute-start | bytes 786440 | tf_op jit(solution)/shard_map/ppermute | solution.py:310
  53.8 16.4 %copy-start.1 = (bf16[1024,512]{1,0:T(8,128)(2,1)S(1)}, bf16[1024,512]{1,0:T(8,128)(2,1)}, u32[]{:S(2)}) copy-start(bf16[1024,512]{1,0:T(8,128)(2,1)} %copy-done) | copy-start | bytes 3145732
  53.8 8.2 %collective-permute-start.13 = (f32[256,256]{1,0:T(8,128)}, f32[256,256]{1,0:T(8,128)S(1)}, u32[]{:S(2)}, u32[]{:S(2)}) collective-permute-start(f32[256,256]{1,0:T(8,128)} %get-tuple-element.57.refs_0_), channel_id=1, source_target_pairs={{0,8},{8,24},{24,16},{16,0},{1,9},{9,25},{25,17},{17,1},{10,2},{2,... | collective-permute-start | bytes 786440 | tf_op jit(solution)/shard_map/ppermute | solution.py:310
  55.3 8.8 %collective-permute-start.14 = (f32[256,256]{1,0:T(8,128)}, f32[256,256]{1,0:T(8,128)}, u32[]{:S(2)}, u32[]{:S(2)}) collective-permute-start(f32[256,256]{1,0:T(8,128)} %get-tuple-element.58.refs_4_), channel_id=1, source_target_pairs={{8,0},{24,8},{16,24},{0,16},{9,1},{25,9},{17,25},{1,17},{2,10},{18... | collective-permute-start | bytes 786440 | tf_op jit(solution)/shard_map/ppermute | solution.py:310
  55.8 13.9 %collective-permute-start.7 = (f32[256,256]{1,0:T(8,128)}, f32[256,256]{1,0:T(8,128)}, u32[]{:S(2)}, u32[]{:S(2)}) collective-permute-start(f32[256,256]{1,0:T(8,128)} %get-tuple-element.53.refs_4_), channel_id=1, source_target_pairs={{8,0},{24,8},{16,24},{0,16},{9,1},{25,9},{17,25},{1,17},{2,10},{18... | collective-permute-start | bytes 786440 | tf_op jit(solution)/shard_map/ppermute | solution.py:310
  59.4 10.8 %copy-start.21 = (f32[256,256]{1,0:T(8,128)S(1)}, f32[256,256]{1,0:T(8,128)}, u32[]{:S(2)}) copy-start(f32[256,256]{1,0:T(8,128)} %get-tuple-element.46.refs_4_.refs_0_) | copy-start | bytes 786436
  59.4 10.8 %copy-start.27 = (f32[256,256]{1,0:T(8,128)S(1)}, f32[256,256]{1,0:T(8,128)}, u32[]{:S(2)}) copy-start(f32[256,256]{1,0:T(8,128)} %copy-done.26) | copy-start | bytes 786436
  59.4 10.8 %copy-start.29 = (f32[256,256]{1,0:T(8,128)S(1)}, f32[256,256]{1,0:T(8,128)}, u32[]{:S(2)}) copy-start(f32[256,256]{1,0:T(8,128)} %copy-done.28) | copy-start | bytes 786436
  59.4 10.8 %copy-start.33 = (f32[256,256]{1,0:T(8,128)S(1)}, f32[256,256]{1,0:T(8,128)}, u32[]{:S(2)}) copy-start(f32[256,256]{1,0:T(8,128)} %get-tuple-element.49.refs_4_) | copy-start | bytes 786436
  62.0 18.2 %collective-permute-start.26 = (f32[256,256]{1,0:T(8,128)S(1)}, f32[256,256]{1,0:T(8,128)S(1)}, u32[]{:S(2)}, u32[]{:S(2)}) collective-permute-start(f32[256,256]{1,0:T(8,128)S(1)} %collective-permute-done.13.refs_3_.refs_2_.refs_1_), channel_id=1, source_target_pairs={{0,8},{8,24},{24,16},{16,0},{1,9},{9,25},{25,17},{17,1},{10,2},{2,... | collective-permute-start | bytes 786440 | tf_op jit(solution)/shard_map/ppermute | solution.py:310
  64.1 17.7 %collective-permute-start.27 = (f32[256,256]{1,0:T(8,128)}, f32[256,256]{1,0:T(8,128)S(1)}, u32[]{:S(2)}, u32[]{:S(2)}) collective-permute-start(f32[256,256]{1,0:T(8,128)} %collective-permute-done.14.refs_7_.refs_6_.refs_5_), channel_id=1, source_target_pairs={{8,0},{24,8},{16,24},{0,16},{9,1},{25,9},{17,25},{1,17},{2,10},{18... | collective-permute-start | bytes 786440 | tf_op jit(solution)/shard_map/ppermute | solution.py:310
  64.6 11.4 %collective-permute-start.21 = (f32[256,256]{1,0:T(8,128)}, f32[256,256]{1,0:T(8,128)S(1)}, u32[]{:S(2)}, u32[]{:S(2)}) collective-permute-start(f32[256,256]{1,0:T(8,128)} %collective-permute-done.6.refs_3_.refs_2_.refs_1_), channel_id=1, source_target_pairs={{0,8},{8,24},{24,16},{16,0},{1,9},{9,25},{25,17},{17,1},{10,2},{2,... | collective-permute-start | bytes 786440 | tf_op jit(solution)/shard_map/ppermute | solution.py:310
  69.8 7.9 %collective-permute-start.22 = (f32[256,256]{1,0:T(8,128)}, f32[256,256]{1,0:T(8,128)S(1)}, u32[]{:S(2)}, u32[]{:S(2)}) collective-permute-start(f32[256,256]{1,0:T(8,128)} %collective-permute-done.7.refs_7_.refs_6_.refs_5_), channel_id=1, source_target_pairs={{8,0},{24,8},{16,24},{0,16},{9,1},{25,9},{17,25},{1,17},{2,10},{18... | collective-permute-start | bytes 786440 | tf_op jit(solution)/shard_map/ppermute | solution.py:310
  74.7 18.9 %collective-permute-start.15 = (f32[512,256]{1,0:T(8,128)S(1)}, f32[512,256]{1,0:T(8,128)S(1)}, u32[]{:S(2)}, u32[]{:S(2)}) collective-permute-start(f32[512,256]{1,0:T(8,128)S(1)} %get-tuple-element.60), channel_id=1, source_target_pairs={{0,1},{1,0},{2,3},{3,2},{4,5},{5,4},{6,7},{7,6},{8,9},{9,8},{10,11... | collective-permute-start | bytes 1572872 | tf_op jit(solution)/shard_map/ppermute | solution.py:75
  76.0 10.4 %collective-permute-start.31 = (f32[256,256]{1,0:T(8,128)S(1)}, f32[256,256]{1,0:T(8,128)S(1)}, u32[]{:S(2)}, u32[]{:S(2)}) collective-permute-start(f32[256,256]{1,0:T(8,128)S(1)} %collective-permute-done.21.refs_3_.refs_2_), channel_id=1, source_target_pairs={{0,8},{8,24},{24,16},{16,0},{1,9},{9,25},{25,17},{17,1},{10,2},{2,... | collective-permute-start | bytes 786440 | tf_op jit(solution)/shard_map/ppermute | solution.py:310
  77.6 9.1 %collective-permute-start.32 = (f32[256,256]{1,0:T(8,128)S(1)}, f32[256,256]{1,0:T(8,128)S(1)}, u32[]{:S(2)}, u32[]{:S(2)}) collective-permute-start(f32[256,256]{1,0:T(8,128)S(1)} %collective-permute-done.22.refs_7_.refs_6_), channel_id=1, source_target_pairs={{8,0},{24,8},{16,24},{0,16},{9,1},{25,9},{17,25},{1,17},{2,10},{18... | collective-permute-start | bytes 786440 | tf_op jit(solution)/shard_map/ppermute | solution.py:310
  80.2 10.1 %collective-permute-start.36 = (f32[256,256]{1,0:T(8,128)S(1)}, f32[256,256]{1,0:T(8,128)S(1)}, u32[]{:S(2)}, u32[]{:S(2)}) collective-permute-start(f32[256,256]{1,0:T(8,128)S(1)} %collective-permute-done.26.refs_3_.refs_2_), channel_id=1, source_target_pairs={{0,8},{8,24},{24,16},{16,0},{1,9},{9,25},{25,17},{17,1},{10,2},{2,... | collective-permute-start | bytes 786440 | tf_op jit(solution)/shard_map/ppermute | solution.py:310
  81.8 9.8 %collective-permute-start.37 = (f32[256,256]{1,0:T(8,128)S(1)}, f32[256,256]{1,0:T(8,128)S(1)}, u32[]{:S(2)}, u32[]{:S(2)}) collective-permute-start(f32[256,256]{1,0:T(8,128)S(1)} %collective-permute-done.27.refs_7_.refs_6_), channel_id=1, source_target_pairs={{8,0},{24,8},{16,24},{0,16},{9,1},{25,9},{17,25},{1,17},{2,10},{18... | collective-permute-start | bytes 786440 | tf_op jit(solution)/shard_map/ppermute | solution.py:310
  86.4 8.9 %collective-permute-start.8 = (f32[512,256]{1,0:T(8,128)S(1)}, f32[512,256]{1,0:T(8,128)S(1)}, u32[]{:S(2)}, u32[]{:S(2)}) collective-permute-start(f32[512,256]{1,0:T(8,128)S(1)} %get-tuple-element.55), channel_id=1, source_target_pairs={{0,1},{1,0},{2,3},{3,2},{4,5},{5,4},{6,7},{7,6},{8,9},{9,8},{10,11... | collective-permute-start | bytes 1572872 | tf_op jit(solution)/shard_map/ppermute | solution.py:75
  86.8 49.0 %collective-permute-start.20 = (f32[4,2,64,512]{3,2,1,0:T(8,128)S(1)}, f32[4,2,64,512]{3,2,1,0:T(8,128)S(1)}, u32[]{:S(2)}, u32[]{:S(2)}) collective-permute-start(f32[4,2,64,512]{3,2,1,0:T(8,128)S(1)} %bitcast.36), channel_id=1, source_target_pairs={{0,1},{1,0},{2,3},{3,2},{4,5},{5,4},{6,7},{7,6},{8,9},{9,8},{10,11... | collective-permute-start | bytes 3145736 | tf_op jit(solution)/shard_map/ppermute | solution.py:75
  90.3 5.1 %collective-permute-start.23 = (f32[512,256]{1,0:T(8,128)S(1)}, f32[512,256]{1,0:T(8,128)S(1)}, u32[]{:S(2)}, u32[]{:S(2)}) collective-permute-start(f32[512,256]{1,0:T(8,128)S(1)} %get-tuple-element.63.send_ref), channel_id=1, source_target_pairs={{0,1},{1,0},{2,3},{3,2},{4,5},{5,4},{6,7},{7,6},{8,9},{9,8},{10,11... | collective-permute-start | bytes 1572872 | tf_op jit(solution)/shard_map/ppermute | solution.py:75
  91.6 4.4 %collective-permute-start.28 = (f32[512,256]{1,0:T(8,128)S(1)}, f32[512,256]{1,0:T(8,128)S(1)}, u32[]{:S(2)}, u32[]{:S(2)}) collective-permute-start(f32[512,256]{1,0:T(8,128)S(1)} %get-tuple-element.65.send_ref), channel_id=1, source_target_pairs={{0,1},{1,0},{2,3},{3,2},{4,5},{5,4},{6,7},{7,6},{8,9},{9,8},{10,11... | collective-permute-start | bytes 1572872 | tf_op jit(solution)/shard_map/ppermute | solution.py:75
  93.7 55.6 %collective-permute-start.33 = (f32[512,256]{1,0:T(8,128)S(1)}, f32[512,256]{1,0:T(8,128)S(1)}, u32[]{:S(2)}, u32[]{:S(2)}) collective-permute-start(f32[512,256]{1,0:T(8,128)S(1)} %get-tuple-element.68.send_ref), channel_id=1, source_target_pairs={{0,1},{1,0},{2,3},{3,2},{4,5},{5,4},{6,7},{7,6},{8,9},{9,8},{10,11... | collective-permute-start | bytes 1572872 | tf_op jit(solution)/shard_map/ppermute | solution.py:75
  95.3 54.7 %collective-permute-start.38 = (f32[512,256]{1,0:T(8,128)S(1)}, f32[512,256]{1,0:T(8,128)S(1)}, u32[]{:S(2)}, u32[]{:S(2)}) collective-permute-start(f32[512,256]{1,0:T(8,128)S(1)} %get-tuple-element.70.send_ref), channel_id=1, source_target_pairs={{0,1},{1,0},{2,3},{3,2},{4,5},{5,4},{6,7},{7,6},{8,9},{9,8},{10,11... | collective-permute-start | bytes 1572872 | tf_op jit(solution)/shard_map/ppermute | solution.py:75
  95.5 9.2 %collective-permute-start.16 = (f32[256,256]{1,0:T(8,128)S(1)}, f32[256,256]{1,0:T(8,128)S(1)}, u32[]{:S(2)}, u32[]{:S(2)}) collective-permute-start(f32[256,256]{1,0:T(8,128)S(1)} %get-tuple-element.100), channel_id=1, source_target_pairs={{0,2},{1,3},{2,0},{3,1},{4,6},{5,7},{6,4},{7,5},{8,10},{9,11},{10,... | collective-permute-start | bytes 786440 | tf_op jit(solution)/shard_map/ppermute | solution.py:75
  96.0 14.2 %collective-permute-start.9 = (f32[256,256]{1,0:T(8,128)S(1)}, f32[256,256]{1,0:T(8,128)S(1)}, u32[]{:S(2)}, u32[]{:S(2)}) collective-permute-start(f32[256,256]{1,0:T(8,128)S(1)} %get-tuple-element.102), channel_id=1, source_target_pairs={{0,2},{1,3},{2,0},{3,1},{4,6},{5,7},{6,4},{7,5},{8,10},{9,11},{10,... | collective-permute-start | bytes 786440 | tf_op jit(solution)/shard_map/ppermute | solution.py:75
  104.6 21.2 %collective-permute-start.24 = (f32[256,256]{1,0:T(8,128)S(1)}, f32[256,256]{1,0:T(8,128)S(1)}, u32[]{:S(2)}, u32[]{:S(2)}) collective-permute-start(f32[256,256]{1,0:T(8,128)S(1)} %get-tuple-element.96), channel_id=1, source_target_pairs={{0,2},{1,3},{2,0},{3,1},{4,6},{5,7},{6,4},{7,5},{8,10},{9,11},{10,... | collective-permute-start | bytes 786440 | tf_op jit(solution)/shard_map/ppermute | solution.py:75
  110.2 8.7 %collective-permute-start.17 = (f32[128,256]{1,0:T(8,128)S(1)}, f32[128,256]{1,0:T(8,128)S(1)}, u32[]{:S(2)}, u32[]{:S(2)}) collective-permute-start(f32[128,256]{1,0:T(8,128)S(1)} %slice_add_fusion.24), channel_id=1, source_target_pairs={{0,4},{1,5},{2,6},{3,7},{4,0},{5,1},{6,2},{7,3},{8,12},{9,13},{10,... | collective-permute-start | bytes 393224 | tf_op jit(solution)/shard_map/ppermute | solution.py:75
  118.9 6.8 %collective-permute-start.10 = (f32[128,256]{1,0:T(8,128)S(1)}, f32[128,256]{1,0:T(8,128)S(1)}, u32[]{:S(2)}, u32[]{:S(2)}) collective-permute-start(f32[128,256]{1,0:T(8,128)S(1)} %slice_add_fusion.26), channel_id=1, source_target_pairs={{0,4},{1,5},{2,6},{3,7},{4,0},{5,1},{6,2},{7,3},{8,12},{9,13},{10,... | collective-permute-start | bytes 393224 | tf_op jit(solution)/shard_map/ppermute | solution.py:75
  125.8 9.9 %collective-permute-start.29 = (f32[256,256]{1,0:T(8,128)S(1)}, f32[256,256]{1,0:T(8,128)S(1)}, u32[]{:S(2)}, u32[]{:S(2)}) collective-permute-start(f32[256,256]{1,0:T(8,128)S(1)} %get-tuple-element.98), channel_id=1, source_target_pairs={{0,2},{1,3},{2,0},{3,1},{4,6},{5,7},{6,4},{7,5},{8,10},{9,11},{10,... | collective-permute-start | bytes 786440 | tf_op jit(solution)/shard_map/ppermute | solution.py:75
  125.8 24.7 %collective-permute-start.25 = (f32[128,256]{1,0:T(8,128)S(1)}, f32[128,256]{1,0:T(8,128)S(1)}, u32[]{:S(2)}, u32[]{:S(2)}) collective-permute-start(f32[128,256]{1,0:T(8,128)S(1)} %slice_add_fusion.22), channel_id=1, source_target_pairs={{0,4},{1,5},{2,6},{3,7},{4,0},{5,1},{6,2},{7,3},{8,12},{9,13},{10,... | collective-permute-start | bytes 393224 | tf_op jit(solution)/shard_map/ppermute | solution.py:75
  135.6 16.6 %collective-permute-start.30 = (f32[128,256]{1,0:T(8,128)S(1)}, f32[128,256]{1,0:T(8,128)S(1)}, u32[]{:S(2)}, u32[]{:S(2)}) collective-permute-start(f32[128,256]{1,0:T(8,128)S(1)} %slice_add_fusion.20), channel_id=1, source_target_pairs={{0,4},{1,5},{2,6},{3,7},{4,0},{5,1},{6,2},{7,3},{8,12},{9,13},{10,... | collective-permute-start | bytes 393224 | tf_op jit(solution)/shard_map/ppermute | solution.py:75
  142.6 35.9 %collective-permute-start.41 = (f32[3,256,512]{2,1,0:T(8,128)S(1)}, f32[3,256,512]{2,1,0:T(8,128)S(1)}, u32[]{:S(2)}, u32[]{:S(2)}) collective-permute-start(f32[3,256,512]{2,1,0:T(8,128)S(1)} %get-tuple-element.72), channel_id=1, source_target_pairs={{0,1},{1,0},{2,3},{3,2},{4,5},{5,4},{6,7},{7,6},{8,9},{9,8},{10,11... | collective-permute-start | bytes 4718600 | tf_op jit(solution)/shard_map/ppermute | solution.py:75
  149.3 25.4 %collective-permute-start.50 = (f32[2,256,512]{2,1,0:T(8,128)S(1)}, f32[2,256,512]{2,1,0:T(8,128)S(1)}, u32[]{:S(2)}, u32[]{:S(2)}) collective-permute-start(f32[2,256,512]{2,1,0:T(8,128)S(1)} %get-tuple-element.79), channel_id=1, source_target_pairs={{0,1},{1,0},{2,3},{3,2},{4,5},{5,4},{6,7},{7,6},{8,9},{9,8},{10,11... | collective-permute-start | bytes 3145736 | tf_op jit(solution)/shard_map/ppermute | solution.py:75
  150.0 9.3 %collective-permute-start.34 = (f32[256,256]{1,0:T(8,128)S(1)}, f32[256,256]{1,0:T(8,128)S(1)}, u32[]{:S(2)}, u32[]{:S(2)}) collective-permute-start(f32[256,256]{1,0:T(8,128)S(1)} %get-tuple-element.104), channel_id=1, source_target_pairs={{0,2},{1,3},{2,0},{3,1},{4,6},{5,7},{6,4},{7,5},{8,10},{9,11},{10,... | collective-permute-start | bytes 786440 | tf_op jit(solution)/shard_map/ppermute | solution.py:75
  150.6 16.1 %collective-permute-start.39 = (f32[256,256]{1,0:T(8,128)S(1)}, f32[256,256]{1,0:T(8,128)S(1)}, u32[]{:S(2)}, u32[]{:S(2)}) collective-permute-start(f32[256,256]{1,0:T(8,128)S(1)} %get-tuple-element.106), channel_id=1, source_target_pairs={{0,2},{1,3},{2,0},{3,1},{4,6},{5,7},{6,4},{7,5},{8,10},{9,11},{10,... | collective-permute-start | bytes 786440 | tf_op jit(solution)/shard_map/ppermute | solution.py:75
  159.2 8.6 %collective-permute-start.35 = (f32[128,256]{1,0:T(8,128)S(1)}, f32[128,256]{1,0:T(8,128)S(1)}, u32[]{:S(2)}, u32[]{:S(2)}) collective-permute-start(f32[128,256]{1,0:T(8,128)S(1)} %slice_add_fusion.18), channel_id=1, source_target_pairs={{0,4},{1,5},{2,6},{3,7},{4,0},{5,1},{6,2},{7,3},{8,12},{9,13},{10,... | collective-permute-start | bytes 393224 | tf_op jit(solution)/shard_map/ppermute | solution.py:75
  166.7 7.9 %collective-permute-start.40 = (f32[128,256]{1,0:T(8,128)S(1)}, f32[128,256]{1,0:T(8,128)S(1)}, u32[]{:S(2)}, u32[]{:S(2)}) collective-permute-start(f32[128,256]{1,0:T(8,128)S(1)} %slice_add_fusion.16), channel_id=1, source_target_pairs={{0,4},{1,5},{2,6},{3,7},{4,0},{5,1},{6,2},{7,3},{8,12},{9,13},{10,... | collective-permute-start | bytes 393224 | tf_op jit(solution)/shard_map/ppermute | solution.py:75
  175.0 9.2 %collective-permute-start.51 = (f32[2,64,512]{2,1,0:T(8,128)S(1)}, f32[2,64,512]{2,1,0:T(8,128)S(1)}, u32[]{:S(2)}, u32[]{:S(2)}) collective-permute-start(f32[2,64,512]{2,1,0:T(8,128)S(1)} %get-tuple-element.92), channel_id=1, source_target_pairs={{0,8},{8,0},{16,24},{24,16},{1,9},{9,1},{17,25},{25,17},{2,10},{10... | collective-permute-start | bytes 786440 | tf_op jit(solution)/shard_map/ppermute | solution.py:75
  175.6 14.8 %collective-permute-start.52 = (f32[2,64,512]{2,1,0:T(8,128)S(1)}, f32[2,64,512]{2,1,0:T(8,128)S(1)}, u32[]{:S(2)}, u32[]{:S(2)}) collective-permute-start(f32[2,64,512]{2,1,0:T(8,128)S(1)} %get-tuple-element.94), channel_id=1, source_target_pairs={{0,16},{8,24},{16,0},{24,8},{1,17},{9,25},{17,1},{25,9},{2,18},{10... | collective-permute-start | bytes 786440 | tf_op jit(solution)/shard_map/ppermute | solution.py:75
  175.6 14.8 %collective-permute-start.53 = (f32[2,64,512]{2,1,0:T(8,128)S(1)}, f32[2,64,512]{2,1,0:T(8,128)S(1)}, u32[]{:S(2)}, u32[]{:S(2)}) collective-permute-start(f32[2,64,512]{2,1,0:T(8,128)S(1)} %get-tuple-element.93), channel_id=1, source_target_pairs={{0,24},{8,16},{16,8},{24,0},{1,25},{9,17},{17,9},{25,1},{2,26},{10... | collective-permute-start | bytes 786440 | tf_op jit(solution)/shard_map/ppermute | solution.py:75
  179.0 19.3 %collective-permute-start.42 = (f32[3,64,512]{2,1,0:T(8,128)S(1)}, f32[3,64,512]{2,1,0:T(8,128)S(1)}, u32[]{:S(2)}, u32[]{:S(2)}) collective-permute-start(f32[3,64,512]{2,1,0:T(8,128)S(1)} %get-tuple-element.89), channel_id=1, source_target_pairs={{0,8},{8,0},{16,24},{24,16},{1,9},{9,1},{17,25},{25,17},{2,10},{10... | collective-permute-start | bytes 1179656 | tf_op jit(solution)/shard_map/ppermute | solution.py:75
  179.6 26.4 %collective-permute-start.43 = (f32[3,64,512]{2,1,0:T(8,128)S(1)}, f32[3,64,512]{2,1,0:T(8,128)S(1)}, u32[]{:S(2)}, u32[]{:S(2)}) collective-permute-start(f32[3,64,512]{2,1,0:T(8,128)S(1)} %get-tuple-element.91), channel_id=1, source_target_pairs={{0,16},{8,24},{16,0},{24,8},{1,17},{9,25},{17,1},{25,9},{2,18},{10... | collective-permute-start | bytes 1179656 | tf_op jit(solution)/shard_map/ppermute | solution.py:75
  184.2 21.8 %collective-permute-start.44 = (f32[3,64,512]{2,1,0:T(8,128)S(1)}, f32[3,64,512]{2,1,0:T(8,128)S(1)}, u32[]{:S(2)}, u32[]{:S(2)}) collective-permute-start(f32[3,64,512]{2,1,0:T(8,128)S(1)} %get-tuple-element.90), channel_id=1, source_target_pairs={{0,24},{8,16},{16,8},{24,0},{1,25},{9,17},{17,9},{25,1},{2,26},{10... | collective-permute-start | bytes 1179656 | tf_op jit(solution)/shard_map/ppermute | solution.py:75
  190.6 15.7 %collective-permute-start.54 = (f32[2,32,512]{2,1,0:T(8,128)S(1)}, f32[2,32,512]{2,1,0:T(8,128)S(1)}, u32[]{:S(2)}, u32[]{:S(2)}) collective-permute-start(f32[2,32,512]{2,1,0:T(8,128)S(1)} %slice.349), channel_id=1, source_target_pairs={{0,2},{1,3},{2,0},{3,1},{4,6},{5,7},{6,4},{7,5},{8,10},{9,11},{10,... | collective-permute-start | bytes 393224 | tf_op jit(solution)/shard_map/ppermute | solution.py:75
  206.2 7.1 %collective-permute-start.45 = (f32[3,32,512]{2,1,0:T(8,128)S(1)}, f32[3,32,512]{2,1,0:T(8,128)S(1)}, u32[]{:S(2)}, u32[]{:S(2)}) collective-permute-start(f32[3,32,512]{2,1,0:T(8,128)S(1)} %slice.341), channel_id=1, source_target_pairs={{0,2},{1,3},{2,0},{3,1},{4,6},{5,7},{6,4},{7,5},{8,10},{9,11},{10,... | collective-permute-start | bytes 589832 | tf_op jit(solution)/shard_map/ppermute | solution.py:75
  206.3 7.1 %collective-permute-start.55 = (f32[2,16,512]{2,1,0:T(8,128)S(1)}, f32[2,16,512]{2,1,0:T(8,128)S(1)}, u32[]{:S(2)}, u32[]{:S(2)}) collective-permute-start(f32[2,16,512]{2,1,0:T(8,128)S(1)} %slice.351), channel_id=1, source_target_pairs={{0,4},{1,5},{2,6},{3,7},{4,0},{5,1},{6,2},{7,3},{8,12},{9,13},{10,... | collective-permute-start | bytes 196616 | tf_op jit(solution)/shard_map/ppermute | solution.py:75
  213.4 5.7 %collective-permute-start.46 = (f32[3,16,512]{2,1,0:T(8,128)S(1)}, f32[3,16,512]{2,1,0:T(8,128)S(1)}, u32[]{:S(2)}, u32[]{:S(2)}) collective-permute-start(f32[3,16,512]{2,1,0:T(8,128)S(1)} %slice.343), channel_id=1, source_target_pairs={{0,4},{1,5},{2,6},{3,7},{4,0},{5,1},{6,2},{7,3},{8,12},{9,13},{10,... | collective-permute-start | bytes 294920 | tf_op jit(solution)/shard_map/ppermute | solution.py:75
  213.5 8.5 %collective-permute-start.56 = (f32[2,16,512]{2,1,0:T(8,128)S(1)}, f32[2,16,512]{2,1,0:T(8,128)S(1)}, u32[]{:S(2)}, u32[]{:S(2)}) collective-permute-start(f32[2,16,512]{2,1,0:T(8,128)S(1)} %slice_add_fusion.29), channel_id=1, source_target_pairs={{0,24},{8,16},{16,8},{24,0},{1,25},{9,17},{17,9},{25,1},{2,26},{10... | collective-permute-start | bytes 196616 | tf_op jit(solution)/shard_map/ppermute | solution.py:75
  215.1 7.5 %collective-permute-start.57 = (f32[2,16,512]{2,1,0:T(8,128)S(1)}, f32[2,16,512]{2,1,0:T(8,128)S(1)}, u32[]{:S(2)}, u32[]{:S(2)}) collective-permute-start(f32[2,16,512]{2,1,0:T(8,128)S(1)} %slice_add_fusion.29), channel_id=1, source_target_pairs={{0,16},{8,24},{16,0},{24,8},{1,17},{9,25},{17,1},{25,9},{2,18},{10... | collective-permute-start | bytes 196616 | tf_op jit(solution)/shard_map/ppermute | solution.py:75
  216.5 6.1 %collective-permute-start.58 = (f32[2,16,512]{2,1,0:T(8,128)S(1)}, f32[2,16,512]{2,1,0:T(8,128)S(1)}, u32[]{:S(2)}, u32[]{:S(2)}) collective-permute-start(f32[2,16,512]{2,1,0:T(8,128)S(1)} %slice_add_fusion.29), channel_id=1, source_target_pairs={{0,8},{8,0},{16,24},{24,16},{1,9},{9,1},{17,25},{25,17},{2,10},{10... | collective-permute-start | bytes 196616 | tf_op jit(solution)/shard_map/ppermute | solution.py:75
  219.1 5.6 %collective-permute-start.47 = (f32[3,16,512]{2,1,0:T(8,128)S(1)}, f32[3,16,512]{2,1,0:T(8,128)S(1)}, u32[]{:S(2)}, u32[]{:S(2)}) collective-permute-start(f32[3,16,512]{2,1,0:T(8,128)S(1)} %slice_add_fusion.28), channel_id=1, source_target_pairs={{0,24},{8,16},{16,8},{24,0},{1,25},{9,17},{17,9},{25,1},{2,26},{10... | collective-permute-start | bytes 294920 | tf_op jit(solution)/shard_map/ppermute | solution.py:75
  220.7 5.0 %collective-permute-start.48 = (f32[3,16,512]{2,1,0:T(8,128)S(1)}, f32[3,16,512]{2,1,0:T(8,128)S(1)}, u32[]{:S(2)}, u32[]{:S(2)}) collective-permute-start(f32[3,16,512]{2,1,0:T(8,128)S(1)} %slice_add_fusion.28), channel_id=1, source_target_pairs={{0,16},{8,24},{16,0},{24,8},{1,17},{9,25},{17,1},{25,9},{2,18},{10... | collective-permute-start | bytes 294920 | tf_op jit(solution)/shard_map/ppermute | solution.py:75
  222.0 4.6 %collective-permute-start.49 = (f32[3,16,512]{2,1,0:T(8,128)S(1)}, f32[3,16,512]{2,1,0:T(8,128)S(1)}, u32[]{:S(2)}, u32[]{:S(2)}) collective-permute-start(f32[3,16,512]{2,1,0:T(8,128)S(1)} %slice_add_fusion.28), channel_id=1, source_target_pairs={{0,8},{8,0},{16,24},{24,16},{1,9},{9,1},{17,25},{25,17},{2,10},{10... | collective-permute-start | bytes 294920 | tf_op jit(solution)/shard_map/ppermute | solution.py:75
  (37 other events, 109.6 us)

commit v4 on v3

--- a/solution.py
+++ b/solution.py
@@ -13,6 +13,7 @@
 NN = (((1,), (0,)), ((), ()))
 TN = (((0,), (0,)), ((), ()))
 VMEM_BYTES = 40 * 1024 * 1024
+HINT = 32
 
 
 def split(value):
@@ -34,10 +35,18 @@
     )
 
 
-def call(body, out_shapes, flops, *args, smem=0, scratch=()):
+def call(body, out_shapes, flops, *args, smem=0, scratch=(), after=()):
     specs = [pl.BlockSpec(memory_space=pltpu.SMEM)] * smem
     specs += [pl.BlockSpec(memory_space=pltpu.VMEM)] * (len(args) - smem)
     moved = sum(a.size * a.dtype.itemsize for a in args)
+    if after:
+        inner, count = body, len(args)
+
+        def body(*refs):
+            inner(*refs[:count], *refs[count + len(after) :])
+
+        specs += [pl.BlockSpec(memory_space=pl.ANY)] * len(after)
+        args = args + tuple(after)
     moved += sum(s.size * s.dtype.itemsize for s in out_shapes)
     return pl.pallas_call(
         body,
@@ -46,7 +55,9 @@
         out_specs=[pl.BlockSpec(memory_space=pltpu.VMEM)] * len(out_shapes),
         scratch_shapes=scratch,
         compiler_params=pltpu.CompilerParams(vmem_limit_bytes=VMEM_BYTES),
-        cost_estimate=pl.CostEstimate(flops=flops, bytes_accessed=moved, transcendentals=0),
+        cost_estimate=pl.CostEstimate(
+            flops=flops // HINT, bytes_accessed=moved // HINT, transcendentals=0
+        ),
     )(*args)
 
 
@@ -91,6 +102,26 @@
     high_ref[...], low_ref[...] = split(ordered_ref[...].T)
 
 
+def factor_halves(info, factors, member, groups):
+    _, rows, columns = factors.shape
+    whole = pl.BlockSpec((columns, rows), lambda i, info_ref: (0, 0))
+    return pl.pallas_call(
+        functools.partial(factor_kernel, groups),
+        out_shape=[shape(columns, rows, dtype=BF16)] * 2,
+        grid_spec=pltpu.PrefetchScalarGridSpec(
+            num_scalar_prefetch=1,
+            grid=(1,),
+            in_specs=[pl.BlockSpec((1, rows, columns), lambda i, info_ref: (member, 0, 0))],
+            out_specs=[whole, whole],
+            scratch_shapes=[pltpu.VMEM((rows, columns), F32)],
+        ),
+        compiler_params=pltpu.CompilerParams(vmem_limit_bytes=VMEM_BYTES),
+        cost_estimate=pl.CostEstimate(
+            flops=rows * columns // HINT, bytes_accessed=8 * rows * columns // HINT, transcendentals=0
+        ),
+    )(info, factors)
+
+
 def place_kernel(groups, info_ref, in_ref, out_ref):
     size = in_ref.shape[2]
     for g in range(groups):
@@ -99,55 +130,82 @@
             out_ref[c, start, :] = in_ref[g, c]
 
 
-def ring_kernel(member, first, waits, info_ref, *refs):
-    outs = refs[-2:]
-    for way in range(2):
-        own = refs[way][0] * info_ref[3 + member].astype(F32)
-        if first:
-            outs[way][...] = own
-        else:
-            outs[way][...] = jnp.where(info_ref[2] != 0, own, refs[2 + way][...])
-
-
-def ring_stage(info, factors, member, column, half, unit, arrived, tokens):
-    block = [
-        pl.BlockSpec((1, half, unit), lambda i, info_ref, way=way: (member, info_ref[way], column))
-        for way in range(2)
-    ]
-    whole = pl.BlockSpec((half, unit), lambda i, info_ref: (0, 0))
-    return pl.pallas_call(
-        functools.partial(ring_kernel, member, not arrived, len(tokens)),
-        out_shape=[shape(half, unit)] * 2,
+def chunk_kernel(members, lanes, info_ref, *refs):
+    place = 0
+    for at, member in enumerate(members):
+        weight = info_ref[1 + member].astype(F32)
+        block = refs[at]
+        rows = block.shape[1] // 2
+        columns = block.shape[2] // lanes
+        for lane in range(lanes):
+            for way in range(2):
+                out_ref = refs[len(members) + place]
+                place += 1
+                out_ref[...] = weight * block[
+                    0, way * rows : (way + 1) * rows, lane * columns : (lane + 1) * columns
+                ]
+
+
+def own_chunks(info, factors, members, rows, lanes):
+    width = factors.shape[2]
+    dims = (rows // 2, width // lanes)
+    count = len(members) * lanes * 2
+    flat = pl.pallas_call(
+        functools.partial(chunk_kernel, members, lanes),
+        out_shape=[shape(*dims)] * count,
         grid_spec=pltpu.PrefetchScalarGridSpec(
             num_scalar_prefetch=1,
             grid=(1,),
-            in_specs=block
-            + [whole] * len(arrived)
-            + [pl.BlockSpec(memory_space=pl.ANY)] * len(tokens),
-            out_specs=[whole, whole],
+            in_specs=[
+                pl.BlockSpec((1, rows, width), lambda i, info_ref, j=j: (j, info_ref[0], 0))
+                for j in members
+            ],
+            out_specs=[pl.BlockSpec(dims, lambda i, info_ref: (0, 0))] * count,
         ),
+        compiler_params=pltpu.CompilerParams(vmem_limit_bytes=VMEM_BYTES),
         cost_estimate=pl.CostEstimate(
-            flops=2 * half * unit, bytes_accessed=24 * half * unit, transcendentals=0
+            flops=rows * width // HINT, bytes_accessed=8 * rows * width // HINT, transcendentals=0
         ),
-    )(info, factors, factors, *arrived, *tokens)
-
-
-def unit_kernel(count, place_ref, high_ref, low_ref, *refs):
-    ways = (refs[:count], refs[count : 2 * count])
-    send_ref, keep_ref = refs[2 * count :]
-    half = ways[0][0].shape[0]
-    total = None
-    for way, candidates in enumerate(ways):
-        place = place_ref[way]
-        chosen = candidates[0][...]
-        for at in range(1, count):
-            chosen = jnp.where(place == at, candidates[at][...], chosen)
-        columns = slice(way * half, (way + 1) * half)
-        part = product((high_ref[:, columns], low_ref[:, columns]), split(chosen))
-        total = part if total is None else total + part
-    middle = total.shape[0] // 2
-    keep_ref[...] = total[:middle]
-    send_ref[...] = total[middle:]
+    )(info, *[factors] * len(members))
+    return [[flat[(m * lanes + lane) * 2 :][:2] for lane in range(lanes)] for m in range(len(members))]
+
+
+def ring_kernel(info_ref, *refs):
+    outs = refs[-2:]
+    for way in range(2):
+        outs[way][...] = jnp.where(info_ref[0] != 0, refs[way][...], refs[2 + way][...])
+
+
+def ring_stage(info, own, arrived, tokens):
+    vmem = pl.BlockSpec(memory_space=pltpu.VMEM)
+    return pl.pallas_call(
+        ring_kernel,
+        out_shape=[shape(*own[0].shape)] * 2,
+        in_specs=[pl.BlockSpec(memory_space=pltpu.SMEM)]
+        + [vmem] * 4
+        + [pl.BlockSpec(memory_space=pl.ANY)] * len(tokens),
+        out_specs=[vmem, vmem],
+        cost_estimate=pl.CostEstimate(flops=0, bytes_accessed=own[0].size, transcendentals=0),
+    )(info, *own, *arrived, *tokens)
+
+
+def unit_kernel(count, lanes, place_ref, high_ref, low_ref, *refs):
+    keep_ref, send_ref = refs[-2:]
+    middle = keep_ref.shape[0]
+    for lane in range(lanes):
+        total = None
+        for way in range(2):
+            candidates = refs[(2 * lane + way) * count :][:count]
+            half, unit = candidates[0].shape
+            chosen = candidates[0][...]
+            for at in range(1, count):
+                chosen = jnp.where(place_ref[way] == at, candidates[at][...], chosen)
+            columns = slice(way * half, (way + 1) * half)
+            part = product((high_ref[:, columns], low_ref[:, columns]), split(chosen))
+            total = part if total is None else total + part
+        out = slice(lane * unit, (lane + 1) * unit)
+        keep_ref[:, out] = total[:middle]
+        send_ref[:, out] = total[middle:]
 
 
 def unit_gram_kernel(high_ref, low_ref, keep_ref, send_ref, out_ref):
@@ -200,10 +258,9 @@
 ):
     keep_ref, send_ref = refs[-2:]
     for c in range(children):
-        left_ref, right_ref = refs[2 * c : 2 * c + 2]
         own = split(own_ref[c + 1])
         turned = split(turned_ref[c])
-        total = corner_ref[c] + jnp.concatenate([left_ref[...], right_ref[...]], axis=1)
+        total = corner_ref[c] + refs[c][...]
         total += product(own, turned, TN) + product(turned, own, TN)
         total -= product(split(lifted_ref[c]), turned, TN)
         store_halves(keep_ref, send_ref, c, reordered(chooser_ref[...], total))
@@ -224,8 +281,8 @@
     part = diag_width // row_count
     first_row = row_place * rows_here
     source = col_place // ratio
-    unit = width // 2
-    units = [(j, lo) for j in range(members) for lo in range(0, width, unit)]
+    lanes = 2
+    unit = width // lanes
 
     def ring(forward):
         pairs = []
@@ -258,11 +315,10 @@
         gathered = jnp.stack([gathered, swap(gathered, "col", col_count, 1 << bit)], axis=1)
         gathered = gathered.reshape((-1,) + parent_factor.shape)
 
-    first_block = (col_place % ratio) * 2
-    info = jnp.concatenate(
-        [jnp.stack([first_block, first_block + 1, is_source.astype(jnp.int32)]), col_weights]
-    ).astype(jnp.int32)
-    lanes = len(units) // members
+    first_block = (col_place % ratio)[None]
+    info = jnp.concatenate([first_block, col_weights]).astype(jnp.int32)
+    chunks = own_chunks(info, factor_cols, (0,), cols_here, lanes)
+    source_flag = is_source.astype(jnp.int32)[None]
     moved = [[[], []] for _ in range(lanes)]
     received = [[[], []] for _ in range(lanes)]
     tokens = []
@@ -270,6 +326,7 @@
 
     def prepare(stage):
         if stage == 0:
+            chunks.extend(own_chunks(info, factor_cols, tuple(range(1, members)), cols_here, lanes))
             prepared.append(
                 call(
                     functools.partial(region_kernel, col_count),
@@ -280,31 +337,21 @@
                 )
             )
         elif stage <= children:
-            prepared.append(
-                call(
-                    functools.partial(factor_kernel, col_count),
-                    [shape(width, rows_here, dtype=BF16)] * 2,
-                    rows_here * width,
-                    jnp.concatenate([relative, group_weights[stage]]),
-                    lax.slice_in_dim(factor_cols, stage, stage + 1, axis=0),
-                    smem=1,
-                    scratch=[pltpu.VMEM((rows_here, width), F32)],
-                )
-            )
+            order = jnp.concatenate([relative, group_weights[stage]])
+            prepared.append(factor_halves(order, factor_cols, stage, col_count))
         else:
             return []
         return [prepared[-1][0]]
 
     for stage in range(members + row_count - 2):
         for lane in range(lanes):
-            arrived = [received[lane][way][-1] for way in range(2)] if stage else []
-            if stage < members:
-                moving = ring_stage(
-                    info, factor_cols, stage, lane, half, unit, arrived, tokens
-                )
-                tokens = [moving[0]]
+            if stage == 0:
+                moving = chunks[0][lane]
             else:
-                moving = arrived
+                moving = [received[lane][way][-1] for way in range(2)]
+                if stage < members:
+                    moving = ring_stage(source_flag, chunks[stage][lane], moving, tokens)
+                    tokens = [moving[0]]
             for way in range(2):
                 moved[lane][way].append(moving[way])
                 received[lane][way].append(lax.ppermute(moving[way], AXES, ring(way == 0)))
@@ -328,22 +375,22 @@
     wanted = ((halving ^ col_place) * diag_width + by_row * part + inner).reshape(width, 1)
     chooser = (wanted == lax.iota(jnp.int32, width)[None, :]).astype(BF16)
 
-    def column_unit(index):
-        member, lane = divmod(index, lanes)
+    def column_unit(member, chosen_lanes):
         candidates = []
-        for way in range(2):
-            candidates.append(moved[lane][way][member])
-            candidates += received[lane][way][member : member + row_count - 1]
-        size = rows_here // 2
+        for lane in chosen_lanes:
+            for way in range(2):
+                candidates.append(moved[lane][way][member])
+                candidates += received[lane][way][member : member + row_count - 1]
+        columns = unit * len(chosen_lanes)
         return call(
-            functools.partial(unit_kernel, row_count),
-            [shape(size, unit)] * 2,
-            6 * rows_here * cols_here * unit,
+            functools.partial(unit_kernel, row_count, len(chosen_lanes)),
+            [shape(rows_here // 2, columns)] * 2,
+            6 * rows_here * cols_here * columns,
             places, *region, *candidates,
             smem=1,
         )
 
-    def halved(send, keep):
+    def halved(send, keep, sent=None):
         size = keep.shape[0]
         for bit in range(col_bits):
             arrived = swap(send, "col", col_count, 1 << bit)
@@ -351,6 +398,8 @@
                 size //= 2
                 send = keep[size:] + arrived[size:]
                 keep = keep[:size] + arrived[:size]
+                if sent is not None:
+                    sent.append(send)
             else:
                 keep = keep + arrived
         return keep
@@ -374,26 +423,32 @@
             stacked.append(chosen)
         return jnp.concatenate(stacked, axis=1)
 
-    sums = []
+    parent_sums = []
+    for lane in range(lanes):
+        keep, send = column_unit(0, [lane])
+        parent_sums.append(halved(send, keep))
+    child_sums = []
+    first_sent = []
     grams = []
-    for index, (j, lo) in enumerate(units):
-        send, keep = column_unit(index)
-        sums.append(halved(send, keep))
-        if j > 0:
-            grams += call(
-                unit_gram_kernel,
-                [shape(width, unit)],
-                6 * rows_here * width * unit,
-                *turned_factors[j - 1], keep, send,
-            )
+    for c in range(children):
+        keep, send = column_unit(c + 1, range(lanes))
+        sent = []
+        child_sums.append(halved(send, keep, sent))
+        first_sent.append(sent[0])
+        grams += call(
+            unit_gram_kernel,
+            [shape(width, width)],
+            6 * rows_here * width * width,
+            *turned_factors[c], keep, send,
+        )
 
     parent_col, turned, keep, send = call(
         functools.partial(parent_kernel, children),
         [shape(group, width), shape(children, group, width)]
         + [shape(members, width // 2, width)] * 2,
         6 * (1 + 3 * children) * group * width * width,
-        own_weights, chooser, sums[0], sums[1], own, links,
-        smem=1,
+        own_weights, chooser, *parent_sums, own, links,
+        smem=1, after=first_sent,
     )
     parent_totals = total_rows(keep, send)
 
@@ -414,8 +469,7 @@
 
     child_cols = []
     for c in range(children):
-        column = jnp.concatenate(sums[2 * c + 2 : 2 * c + 4], axis=1)
-        child_cols.append(-(column + turned[c]) * own_weights[c + 1].astype(F32))
+        child_cols.append(-(child_sums[c] + turned[c]) * own_weights[c + 1].astype(F32))
     uppers = parent_totals[1:] - framed
     diags = diag_inverse + jnp.concatenate([parent_totals[:1], child_totals])
     return jnp.stack([parent_col] + child_cols), diags, uppers

time: 229 us -> 228 us (level)
  local copies, waits for them, and re-layouts: 19.3 us -> 30 us
  waiting for transfers between devices: 95.3 us -> 85.2 us
  Pallas kernels: 48.3 us -> 41 us
  other arithmetic: 10 us -> 17.1 us
    ppermute x39 -> x33, waiting for transfers between devices: 89.5 us -> 69.9 us  [swap(): lax.ppermute(value, axis, [(place, place ^ change) for place in range(siz...]
    unnamed x85 -> x137, local copies, waits for them, and re-layouts: 11.7 us -> 27.1 us
    ppermute x20, waiting for transfers between devices: 5.84 us -> 15.4 us  [shards(): received[lane][way].append(lax.ppermute(moving[way], AXES, ring(way == 0)))]
    slice x3 -> x2, local copies, waits for them, and re-layouts: 5.5 us -> 0.75 us  [the longest x1 0.54 us: shards(): own_weights[c + 1].astype(F32)]
    pallas_call x6 -> x8, Pallas kernels: 16 us -> 11.9 us  [the longest x4 8.2 us: ring_stage(): pl.pallas_call(ring_kernel, out_shape=[shape(*own[0].shape)] * 2, in_spec...]
    pallas_call x17 -> x11, Pallas kernels: 32.3 us -> 29.1 us  [call(): pl.pallas_call(body, out_shape=out_shapes, in_specs=specs, out_specs=[pl....]
    ppermute x39 -> x33, starting transfers between devices: 30.9 us -> 28.2 us  [swap(): lax.ppermute(value, axis, [(place, place ^ change) for place in range(siz...]
    add x2, other arithmetic: 0.55 us -> 3.18 us  [total_rows(): value = keep + swap(send, 'col', col_count, 1)]
  transfers between devices with their start and end apart: 59 -> 53, of which waited for: 22 -> 19; matrix products, arithmetic and copies ran while one was open for 6% -> 7% of each run, Pallas kernels for 20% -> 15%
where the time goes in v4:
time: 228 us; the launch traced here: 227 us
  waiting for transfers between devices  85.2 us (37%)
  starting transfers between devices  50.8 us (22%)
  Pallas kernels  41 us (18%)
  local copies, waits for them, and re-layouts  30 us (13%)
  other arithmetic  17.1 us (8%)
  between operations  2.95 us (1%)
    ppermute x33, waiting for transfers between devices, swap(): lax.ppermute(value, axis, [(place, place ^ change) for place in range(siz...  69.9 us
    pallas_call x11, Pallas kernels, call(): pl.pallas_call(body, out_shape=out_shapes, in_specs=specs, out_specs=[pl....  29.1 us
    ppermute x33, starting transfers between devices, swap(): lax.ppermute(value, axis, [(place, place ^ change) for place in range(siz...  28.2 us
    unnamed x137, local copies, waits for them, and re-layouts  27.1 us
    ppermute x20, starting transfers between devices, shards(): received[lane][way].append(lax.ppermute(moving[way], AXES, ring(way == 0)))  22.6 us
    ppermute x20, waiting for transfers between devices, shards(): received[lane][way].append(lax.ppermute(moving[way], AXES, ring(way == 0)))  15.4 us
    pallas_call x4, Pallas kernels, ring_stage(): pl.pallas_call(ring_kernel, out_shape=[shape(*own[0].shape)] * 2, in_spec...  8.2 us
  transfers between devices with their start and end apart: 53, of which 19 were waited for; matrix products, arithmetic and copies ran while one was open for 7% of the time, Pallas kernels for 15%

profile of v4, /device:TPU:0, one launch (start us, length us, event | category | flops | bytes accessed | tf_op | source)
XLA Modules:
  0.0 227.1 jit_solution(9394547170008623209)
XLA Ops:
  1.7 2.8 %copy-done = f32[3,1024,512]{2,1,0:T(8,128)S(1)} copy-done((f32[3,1024,512]{2,1,0:T(8,128)S(1)}, f32[3,1024,512]{2,1,0:T(8,128)}, u32[]{:S(2)}) %copy-start) | copy-done | bytes 6291480
  5.2 3.0 %collective-permute-start = (f32[256,256]{1,0:T(8,128)S(1)}, f32[256,256]{1,0:T(8,128)S(1)}, u32[]{:S(2)}, u32[]{:S(2)}) collective-permute-start(f32[256,256]{1,0:T(8,128)S(1)} %get-tuple-element.48.refs_0_), channel_id=1, source_target_pairs={{0,8},{8,24},{24,16},{16,0},{1,9},{9,25},{25,17},{17,1},{10,2},{2,... | collective-permute-start | bytes 786440 | tf_op jit(solution)/shard_map/ppermute | solution.py:357
  8.3 1.9 collective-permute-start.4
  10.3 3.0 %collective-permute-start.18 = (f32[1,2,64,512]{3,2,1,0:T(8,128)}, f32[1,2,64,512]{3,2,1,0:T(8,128)}, u32[]{:S(2)}, u32[]{:S(2)}) collective-permute-start(f32[1,2,64,512]{3,2,1,0:T(8,128)} %bitcast.6), channel_id=1, source_target_pairs={{0,4},{1,5},{2,6},{3,7},{4,0},{5,1},{6,2},{7,3},{8,12},{9,13},{10,... | collective-permute-start | bytes 786440 | tf_op jit(solution)/shard_map/ppermute | solution.py:86
  14.1 2.8 %copy-done.1 = f32[3,1024,512]{2,1,0:T(8,128)S(1)} copy-done((f32[3,1024,512]{2,1,0:T(8,128)S(1)}, f32[3,1024,512]{2,1,0:T(8,128)}, u32[]{:S(2)}) %copy-start.1) | copy-done | bytes 6291480
  26.2 2.0 shard_map.97
  28.2 1.5 collective-permute-start.2
  31.1 2.1 shard_map.98
  33.1 1.5 collective-permute-start.11
  35.2 2.8 %copy-done.2 = f32[3,1024,512]{2,1,0:T(8,128)S(1)} copy-done((f32[3,1024,512]{2,1,0:T(8,128)S(1)}, f32[3,1024,512]{2,1,0:T(8,128)}, u32[]{:S(2)}) %copy-start.2) | copy-done | bytes 6291480
  37.9 1.2 shard_map.99
  42.1 2.1 shard_map.100
  45.1 2.0 shard_map.102
  47.1 1.5 collective-permute-start.13
  48.6 2.1 fusion.2
  50.7 1.6 collective-permute-start.19
  52.3 1.5 collective-permute-start.14
  54.4 1.5 collective-permute-start.7
  56.9 3.4 %collective-permute-done.14.refs_7_.refs_14_.refs_13_ = f32[256,256]{1,0:T(8,128)S(1)} collective-permute-done((f32[256,256]{1,0:T(8,128)}, f32[256,256]{1,0:T(8,128)S(1)}, u32[]{:S(2)}, u32[]{:S(2)}) %collective-permute-start.14) | collective-permute-done | bytes 262176 | tf_op jit(solution)/shard_map/ppermute | solution.py:357
  65.1 1.6 shard_map.103
  66.8 1.3 dynamic-slice_multiply_fusion.refs_4_.own_ref
  68.2 1.6 shard_map.101
  70.3 1.5 collective-permute-start.24
  72.4 1.5 collective-permute-start.22
  74.0 1.1 pad_maximum_fusion.1
  75.2 4.3 %collective-permute-done.24.refs_15_.refs_14_ = f32[256,256]{1,0:T(8,128)S(1)} collective-permute-done((f32[256,256]{1,0:T(8,128)S(1)}, f32[256,256]{1,0:T(8,128)S(1)}, u32[]{:S(2)}, u32[]{:S(2)}) %collective-permute-start.24) | collective-permute-done | bytes 262176 | tf_op jit(solution)/shard_map/ppermute | solution.py:357
  80.0 1.5 collective-permute-start.29
  81.5 3.6 %collective-permute-done.22.refs_7_.refs_6_ = f32[256,256]{1,0:T(8,128)S(1)} collective-permute-done((f32[256,256]{1,0:T(8,128)S(1)}, f32[256,256]{1,0:T(8,128)S(1)}, u32[]{:S(2)}, u32[]{:S(2)}) %collective-permute-start.22) | collective-permute-done | bytes 262176 | tf_op jit(solution)/shard_map/ppermute | solution.py:357
  85.6 1.5 collective-permute-start.27
  87.9 2.9 %collective-permute-done.29.refs_15_ = f32[256,256]{1,0:T(8,128)S(1)} collective-permute-done((f32[256,256]{1,0:T(8,128)S(1)}, f32[256,256]{1,0:T(8,128)S(1)}, u32[]{:S(2)}, u32[]{:S(2)}) %collective-permute-start.29) | collective-permute-done | bytes 262176 | tf_op jit(solution)/shard_map/ppermute | solution.py:357
  91.2 2.9 %shard_map.105 = (f32[512,512]{1,0:T(8,128)S(1)}, f32[512,512]{1,0:T(8,128)S(1)}) custom-call(s32[2]{0:T(128)S(1)} %pad_add_fusion.place_ref, bf16[1024,512]{1,0:T(8,128)(2,1)S(1)} %copy-done.4, bf16[1024,512]{1,0:T(8,128)(2,1)S(1)} %get-tuple-element.47.low_ref, f32[256,256]{1,0:T(8,128)S(1)} %copy-done.25, f32[256,256]{1,0:T(8,128)S(1)} %copy-done.8, ...), custom_call_target="tpu_custom_call" | custom-call | flops 50331648 | bytes 262144 | tf_op jit(solution)/shard_map/pallas_call | solution.py:51
  94.2 1.2 collective-permute-done.27.refs_7_
  95.5 2.9 %shard_map.106 = (f32[512,512]{1,0:T(8,128)S(1)}, f32[512,512]{1,0:T(8,128)S(1)}) custom-call(s32[2]{0:T(128)S(1)} %pad_add_fusion.place_ref, bf16[1024,512]{1,0:T(8,128)(2,1)S(1)} %copy-done.4, bf16[1024,512]{1,0:T(8,128)(2,1)S(1)} %get-tuple-element.47.low_ref, f32[256,256]{1,0:T(8,128)S(1)} %copy-done.35, ...), custom_call_target="tpu_custom_call" | custom-call | flops 50331648 | bytes 262144 | tf_op jit(solution)/shard_map/pallas_call | solution.py:51
  99.3 2.3 collective-permute-start.10
  101.5 9.3 %collective-permute-done.17 = f32[128,256]{1,0:T(8,128)S(1)} collective-permute-done((f32[128,256]{1,0:T(8,128)S(1)}, f32[128,256]{1,0:T(8,128)S(1)}, u32[]{:S(2)}, u32[]{:S(2)}) %collective-permute-start.17) | collective-permute-done | bytes 131104 | tf_op jit(solution)/shard_map/ppermute | solution.py:86
  110.9 2.7 %collective-permute-done.10 = f32[128,256]{1,0:T(8,128)S(1)} collective-permute-done((f32[128,256]{1,0:T(8,128)S(1)}, f32[128,256]{1,0:T(8,128)S(1)}, u32[]{:S(2)}, u32[]{:S(2)}) %collective-permute-start.10) | collective-permute-done | bytes 131104 | tf_op jit(solution)/shard_map/ppermute | solution.py:86
  116.9 6.5 %shard_map.107 = (f32[128,512]{1,0:T(8,128)S(1)}, f32[2,128,512]{2,1,0:T(8,128)S(1)}, f32[3,256,512]{2,1,0:T(8,128)S(1)}, f32[3,256,512]{2,1,0:T(8,128)}) custom-call(s32[3]{0:T(128)S(1)} %get-tuple-element.91.refs_0_, bf16[512,512]{1,0:T(8,128)(2,1)S(1)} %fusion.refs_1_.chooser_ref, f32[128,256]{1,0:T(8,128)S(1)} %fusion.21.refs_2_, ...), custom_call_target="tpu_custom_call" | custom-call | flops 44040192 | bytes 237568 | tf_op jit(solution)/shard_map/pallas_call | solution.py:51
  124.2 1.2 shard_map.110
  125.7 1.8 shard_map.109.refs_0_
  127.6 1.8 shard_map.111.refs_1_
  129.4 3.4 %shard_map.108 = (f32[2,128,512]{2,1,0:T(8,128)S(1)}, f32[2,64,512]{2,1,0:T(8,128)S(1)}, f32[2,512,512]{2,1,0:T(8,128)S(1)}) custom-call(f32[3,128,512]{2,1,0:T(8,128)S(1)} %dynamic-slice_multiply_fusion.refs_4_.own_ref, f32[2,512,512]{2,1,0:T(8,128)S(1)} %shard_map.104.refs_5_.links_ref, f32[2,64,512]{2,1,0:T(8,128)} %slices_ref.1, f32[3,64,512]{2,1,0:T(8,128)S(1)} %copy-done.18), custom_call_target="tpu_custom_call" | custom-call | flops 25165824 | bytes 200704 | tf_op jit(solution)/shard_map/pallas_call | solution.py:51
  132.7 5.1 %shard_map.112 = (f32[2,256,512]{2,1,0:T(8,128)S(1)}, f32[2,256,512]{2,1,0:T(8,128)}) custom-call(bf16[512,512]{1,0:T(8,128)(2,1)S(1)} %fusion.refs_1_.chooser_ref, f32[3,128,512]{2,1,0:T(8,128)S(1)} %dynamic-slice_multiply_fusion.refs_4_.own_ref, f32[2,128,512]{2,1,0:T(8,128)S(1)} %get-tuple-element.78.turned_ref, ...), custom_call_target="tpu_custom_call" | custom-call | flops 37748736 | bytes 270336 | tf_op jit(solution)/shard_map/pallas_call | solution.py:51
  139.3 2.0 collective-permute-start.33
  143.1 11.1 %collective-permute-done.31 = f32[256,512]{1,0:T(8,128)} collective-permute-done((f32[256,512]{1,0:T(8,128)S(1)}, f32[256,512]{1,0:T(8,128)}, u32[]{:S(2)}, u32[]{:S(2)}) %collective-permute-start.31) | collective-permute-done | bytes 524320 | tf_op jit(solution)/shard_map/ppermute | solution.py:86
  154.2 1.1 slice_add_fusion.8
  155.3 14.8 %collective-permute-done.33 = f32[256,512]{1,0:T(8,128)} collective-permute-done((f32[256,512]{1,0:T(8,128)S(1)}, f32[256,512]{1,0:T(8,128)}, u32[]{:S(2)}, u32[]{:S(2)}) %collective-permute-start.33) | collective-permute-done | bytes 524320 | tf_op jit(solution)/shard_map/ppermute | solution.py:86
  171.3 1.4 add.220
  173.5 1.5 collective-permute-start.46
  175.0 1.4 collective-permute-start.47
  176.4 1.8 add.214
  179.0 5.1 %collective-permute-done.34 = f32[128,512]{1,0:T(8,128)S(1)} collective-permute-done((f32[128,512]{1,0:T(8,128)S(1)}, f32[128,512]{1,0:T(8,128)S(1)}, u32[]{:S(2)}, u32[]{:S(2)}) %collective-permute-start.34) | collective-permute-done | bytes 262176 | tf_op jit(solution)/shard_map/ppermute | solution.py:86
  184.1 1.5 collective-permute-start.37
  186.1 1.3 fusion.19
  189.7 6.5 %collective-permute-done.36 = f32[3,64,512]{2,1,0:T(8,128)S(1)} collective-permute-done((f32[3,64,512]{2,1,0:T(8,128)S(1)}, f32[3,64,512]{2,1,0:T(8,128)S(1)}, u32[]{:S(2)}, u32[]{:S(2)}) %collective-permute-start.36) | collective-permute-done | bytes 393248 | tf_op jit(solution)/shard_map/ppermute | solution.py:86
  196.2 8.3 %collective-permute-done.37 = f32[3,64,512]{2,1,0:T(8,128)S(1)} collective-permute-done((f32[3,64,512]{2,1,0:T(8,128)S(1)}, f32[3,64,512]{2,1,0:T(8,128)S(1)}, u32[]{:S(2)}, u32[]{:S(2)}) %collective-permute-start.37) | collective-permute-done | bytes 393248 | tf_op jit(solution)/shard_map/ppermute | solution.py:86
  204.9 1.9 collective-permute-start.49
  206.7 5.9 %collective-permute-done.39 = f32[3,32,512]{2,1,0:T(8,128)S(1)} collective-permute-done((f32[3,32,512]{2,1,0:T(8,128)S(1)}, f32[3,32,512]{2,1,0:T(8,128)S(1)}, u32[]{:S(2)}, u32[]{:S(2)}) %collective-permute-start.39) | collective-permute-done | bytes 196640 | tf_op jit(solution)/shard_map/ppermute | solution.py:86
  212.8 2.3 collective-permute-start.50
  215.1 1.5 collective-permute-start.51
  216.6 1.8 collective-permute-done.40
  218.4 1.1 collective-permute-start.41
  219.6 1.3 collective-permute-start.42
  220.9 1.1 collective-permute-start.43
  222.1 2.4 %collective-permute-done.41 = f32[3,16,512]{2,1,0:T(8,128)S(1)} collective-permute-done((f32[3,16,512]{2,1,0:T(8,128)S(1)}, f32[3,16,512]{2,1,0:T(8,128)S(1)}, u32[]{:S(2)}, u32[]{:S(2)}) %collective-permute-start.41) | collective-permute-done | bytes 98336 | tf_op jit(solution)/shard_map/ppermute | solution.py:86
  (253 shorter events, 43.4 us)
Async XLA Ops:
  5.2 20.2 %collective-permute-start = (f32[256,256]{1,0:T(8,128)S(1)}, f32[256,256]{1,0:T(8,128)S(1)}, u32[]{:S(2)}, u32[]{:S(2)}) collective-permute-start(f32[256,256]{1,0:T(8,128)S(1)} %get-tuple-element.48.refs_0_), channel_id=1, source_target_pairs={{0,8},{8,24},{24,16},{16,0},{1,9},{9,25},{25,17},{17,1},{10,2},{2,... | collective-permute-start | bytes 786440 | tf_op jit(solution)/shard_map/ppermute | solution.py:357
  8.2 17.2 %collective-permute-start.1 = (f32[256,256]{1,0:T(8,128)S(1)}, f32[256,256]{1,0:T(8,128)S(1)}, u32[]{:S(2)}, u32[]{:S(2)}) collective-permute-start(f32[256,256]{1,0:T(8,128)S(1)} %get-tuple-element.51.refs_4_), channel_id=1, source_target_pairs={{8,0},{24,8},{16,24},{0,16},{9,1},{25,9},{17,25},{1,17},{2,10},{18... | collective-permute-start | bytes 786440 | tf_op jit(solution)/shard_map/ppermute | solution.py:357
  8.3 22.0 %collective-permute-start.4 = (f32[256,256]{1,0:T(8,128)S(1)}, f32[256,256]{1,0:T(8,128)S(1)}, u32[]{:S(2)}, u32[]{:S(2)}) collective-permute-start(f32[256,256]{1,0:T(8,128)S(1)} %get-tuple-element.58.refs_0_), channel_id=1, source_target_pairs={{0,8},{8,24},{24,16},{16,0},{1,9},{9,25},{25,17},{17,1},{10,2},{2,... | collective-permute-start | bytes 786440 | tf_op jit(solution)/shard_map/ppermute | solution.py:357
  10.2 20.1 %collective-permute-start.5 = (f32[256,256]{1,0:T(8,128)S(1)}, f32[256,256]{1,0:T(8,128)S(1)}, u32[]{:S(2)}, u32[]{:S(2)}) collective-permute-start(f32[256,256]{1,0:T(8,128)S(1)} %get-tuple-element.59.refs_4_), channel_id=1, source_target_pairs={{8,0},{24,8},{16,24},{0,16},{9,1},{25,9},{17,25},{1,17},{2,10},{18... | collective-permute-start | bytes 786440 | tf_op jit(solution)/shard_map/ppermute | solution.py:357
  10.3 38.3 %collective-permute-start.18 = (f32[1,2,64,512]{3,2,1,0:T(8,128)}, f32[1,2,64,512]{3,2,1,0:T(8,128)}, u32[]{:S(2)}, u32[]{:S(2)}) collective-permute-start(f32[1,2,64,512]{3,2,1,0:T(8,128)} %bitcast.6), channel_id=1, source_target_pairs={{0,4},{1,5},{2,6},{3,7},{4,0},{5,1},{6,2},{7,3},{8,12},{9,13},{10,... | collective-permute-start | bytes 786440 | tf_op jit(solution)/shard_map/ppermute | solution.py:86
  28.2 13.1 %collective-permute-start.2 = (f32[256,256]{1,0:T(8,128)}, f32[256,256]{1,0:T(8,128)S(1)}, u32[]{:S(2)}, u32[]{:S(2)}) collective-permute-start(f32[256,256]{1,0:T(8,128)} %get-tuple-element.52.refs_4_.refs_0_), channel_id=1, source_target_pairs={{0,8},{8,24},{24,16},{16,0},{1,9},{9,25},{25,17},{17,1},{10,2},{2,... | collective-permute-start | bytes 786440 | tf_op jit(solution)/shard_map/ppermute | solution.py:357
  29.7 11.6 %collective-permute-start.3 = (f32[256,256]{1,0:T(8,128)}, f32[256,256]{1,0:T(8,128)S(1)}, u32[]{:S(2)}, u32[]{:S(2)}) collective-permute-start(f32[256,256]{1,0:T(8,128)} %get-tuple-element.55.refs_4_), channel_id=1, source_target_pairs={{8,0},{24,8},{16,24},{0,16},{9,1},{25,9},{17,25},{1,17},{2,10},{18... | collective-permute-start | bytes 786440 | tf_op jit(solution)/shard_map/ppermute | solution.py:357
  33.1 11.1 %collective-permute-start.11 = (f32[256,256]{1,0:T(8,128)}, f32[256,256]{1,0:T(8,128)S(1)}, u32[]{:S(2)}, u32[]{:S(2)}) collective-permute-start(f32[256,256]{1,0:T(8,128)} %get-tuple-element.60.refs_4_.refs_8_), channel_id=1, source_target_pairs={{0,8},{8,24},{24,16},{16,0},{1,9},{9,25},{25,17},{17,1},{10,2},{2,... | collective-permute-start | bytes 786440 | tf_op jit(solution)/shard_map/ppermute | solution.py:357
  34.6 9.6 %collective-permute-start.12 = (f32[256,256]{1,0:T(8,128)}, f32[256,256]{1,0:T(8,128)S(1)}, u32[]{:S(2)}, u32[]{:S(2)}) collective-permute-start(f32[256,256]{1,0:T(8,128)} %get-tuple-element.68.refs_12_), channel_id=1, source_target_pairs={{8,0},{24,8},{16,24},{0,16},{9,1},{25,9},{17,25},{1,17},{2,10},{18... | collective-permute-start | bytes 786440 | tf_op jit(solution)/shard_map/ppermute | solution.py:357
  42.1 18.2 %copy-start.4 = (bf16[1024,512]{1,0:T(8,128)(2,1)S(1)}, bf16[1024,512]{1,0:T(8,128)(2,1)}, u32[]{:S(2)}) copy-start(bf16[1024,512]{1,0:T(8,128)(2,1)} %copy-done.3) | copy-start | bytes 3145732
  42.1 18.2 %copy-start.32 = (f32[256,256]{1,0:T(8,128)S(1)}, f32[256,256]{1,0:T(8,128)}, u32[]{:S(2)}) copy-start(f32[256,256]{1,0:T(8,128)} %copy-done.31) | copy-start | bytes 786436
  47.1 8.8 %collective-permute-start.13 = (f32[256,256]{1,0:T(8,128)}, f32[256,256]{1,0:T(8,128)S(1)}, u32[]{:S(2)}, u32[]{:S(2)}) collective-permute-start(f32[256,256]{1,0:T(8,128)} %get-tuple-element.69.refs_8_), channel_id=1, source_target_pairs={{0,8},{8,24},{24,16},{16,0},{1,9},{9,25},{25,17},{17,1},{10,2},{2,... | collective-permute-start | bytes 786440 | tf_op jit(solution)/shard_map/ppermute | solution.py:357
  50.7 21.1 %collective-permute-start.19 = (f32[2,2,64,512]{3,2,1,0:T(8,128)}, f32[2,2,64,512]{3,2,1,0:T(8,128)}, u32[]{:S(2)}, u32[]{:S(2)}) collective-permute-start(f32[2,2,64,512]{3,2,1,0:T(8,128)} %get-tuple-element.112), channel_id=1, source_target_pairs={{0,2},{1,3},{2,0},{3,1},{4,6},{5,7},{6,4},{7,5},{8,10},{9,11},{10,... | collective-permute-start | bytes 1572872 | tf_op jit(solution)/shard_map/ppermute | solution.py:86
  52.3 8.0 %collective-permute-start.14 = (f32[256,256]{1,0:T(8,128)}, f32[256,256]{1,0:T(8,128)S(1)}, u32[]{:S(2)}, u32[]{:S(2)}) collective-permute-start(f32[256,256]{1,0:T(8,128)} %get-tuple-element.70.refs_12_), channel_id=1, source_target_pairs={{8,0},{24,8},{16,24},{0,16},{9,1},{25,9},{17,25},{1,17},{2,10},{18... | collective-permute-start | bytes 786440 | tf_op jit(solution)/shard_map/ppermute | solution.py:357
  53.9 14.2 %collective-permute-start.6 = (f32[256,256]{1,0:T(8,128)}, f32[256,256]{1,0:T(8,128)S(1)}, u32[]{:S(2)}, u32[]{:S(2)}) collective-permute-start(f32[256,256]{1,0:T(8,128)} %get-tuple-element.62.refs_4_.refs_0_), channel_id=1, source_target_pairs={{0,8},{8,24},{24,16},{16,0},{1,9},{9,25},{25,17},{17,1},{10,2},{2,... | collective-permute-start | bytes 786440 | tf_op jit(solution)/shard_map/ppermute | solution.py:357
  54.4 13.7 %collective-permute-start.7 = (f32[256,256]{1,0:T(8,128)}, f32[256,256]{1,0:T(8,128)S(1)}, u32[]{:S(2)}, u32[]{:S(2)}) collective-permute-start(f32[256,256]{1,0:T(8,128)} %get-tuple-element.63.refs_4_), channel_id=1, source_target_pairs={{8,0},{24,8},{16,24},{0,16},{9,1},{25,9},{17,25},{1,17},{2,10},{18... | collective-permute-start | bytes 786440 | tf_op jit(solution)/shard_map/ppermute | solution.py:357
  55.9 16.4 %collective-permute-start.23 = (f32[256,256]{1,0:T(8,128)S(1)}, f32[256,256]{1,0:T(8,128)}, u32[]{:S(2)}, u32[]{:S(2)}) collective-permute-start(f32[256,256]{1,0:T(8,128)S(1)} %collective-permute-done.13.refs_3_.refs_10_.refs_9_), channel_id=1, source_target_pairs={{0,8},{8,24},{24,16},{16,0},{1,9},{9,25},{25,17},{17,1},{10,2},{2,... | collective-permute-start | bytes 786440 | tf_op jit(solution)/shard_map/ppermute | solution.py:357
  66.7 18.9 %collective-permute-start.15 = (f32[512,256]{1,0:T(8,128)S(1)}, f32[512,256]{1,0:T(8,128)S(1)}, u32[]{:S(2)}, u32[]{:S(2)}) collective-permute-start(f32[512,256]{1,0:T(8,128)S(1)} %get-tuple-element.72), channel_id=1, source_target_pairs={{0,1},{1,0},{2,3},{3,2},{4,5},{5,4},{6,7},{7,6},{8,9},{9,8},{10,11... | collective-permute-start | bytes 1572872 | tf_op jit(solution)/shard_map/ppermute | solution.py:86
  69.8 17.4 %collective-permute-start.8 = (f32[512,256]{1,0:T(8,128)S(1)}, f32[512,256]{1,0:T(8,128)S(1)}, u32[]{:S(2)}, u32[]{:S(2)}) collective-permute-start(f32[512,256]{1,0:T(8,128)S(1)} %get-tuple-element.65), channel_id=1, source_target_pairs={{0,1},{1,0},{2,3},{3,2},{4,5},{5,4},{6,7},{7,6},{8,9},{9,8},{10,11... | collective-permute-start | bytes 1572872 | tf_op jit(solution)/shard_map/ppermute | solution.py:86
  70.3 9.2 %collective-permute-start.24 = (f32[256,256]{1,0:T(8,128)S(1)}, f32[256,256]{1,0:T(8,128)S(1)}, u32[]{:S(2)}, u32[]{:S(2)}) collective-permute-start(f32[256,256]{1,0:T(8,128)S(1)} %collective-permute-done.14.refs_7_.refs_14_.refs_13_), channel_id=1, source_target_pairs={{8,0},{24,8},{16,24},{0,16},{9,1},{25,9},{17,25},{1,17},{2,10},{18... | collective-permute-start | bytes 786440 | tf_op jit(solution)/shard_map/ppermute | solution.py:357
  71.8 8.2 %collective-permute-start.21 = (f32[256,256]{1,0:T(8,128)S(1)}, f32[256,256]{1,0:T(8,128)S(1)}, u32[]{:S(2)}, u32[]{:S(2)}) collective-permute-start(f32[256,256]{1,0:T(8,128)S(1)} %collective-permute-done.6.refs_3_.refs_2_.refs_1_), channel_id=1, source_target_pairs={{0,8},{8,24},{24,16},{16,0},{1,9},{9,25},{25,17},{17,1},{10,2},{2,... | collective-permute-start | bytes 786440 | tf_op jit(solution)/shard_map/ppermute | solution.py:357
  72.4 12.7 %collective-permute-start.22 = (f32[256,256]{1,0:T(8,128)S(1)}, f32[256,256]{1,0:T(8,128)S(1)}, u32[]{:S(2)}, u32[]{:S(2)}) collective-permute-start(f32[256,256]{1,0:T(8,128)S(1)} %collective-permute-done.7.refs_7_.refs_6_.refs_5_), channel_id=1, source_target_pairs={{8,0},{24,8},{16,24},{0,16},{9,1},{25,9},{17,25},{1,17},{2,10},{18... | collective-permute-start | bytes 786440 | tf_op jit(solution)/shard_map/ppermute | solution.py:357
  75.1 16.0 %copy-start.13 = (f32[256,256]{1,0:T(8,128)S(1)}, f32[256,256]{1,0:T(8,128)}, u32[]{:S(2)}) copy-start(f32[256,256]{1,0:T(8,128)} %copy-done.11) | copy-start | bytes 786436
  75.1 16.0 %copy-start.16 = (f32[256,256]{1,0:T(8,128)S(1)}, f32[256,256]{1,0:T(8,128)}, u32[]{:S(2)}) copy-start(f32[256,256]{1,0:T(8,128)} %copy-done.14) | copy-start | bytes 786436
  75.2 16.0 %copy-start.25 = (f32[256,256]{1,0:T(8,128)S(1)}, f32[256,256]{1,0:T(8,128)}, u32[]{:S(2)}) copy-start(f32[256,256]{1,0:T(8,128)} %get-tuple-element.52.refs_4_.refs_0_) | copy-start | bytes 786436
  75.2 16.0 %copy-start.30 = (f32[256,256]{1,0:T(8,128)S(1)}, f32[256,256]{1,0:T(8,128)}, u32[]{:S(2)}) copy-start(f32[256,256]{1,0:T(8,128)} %get-tuple-element.60.refs_4_.refs_8_) | copy-start | bytes 786436
  75.2 16.0 %copy-start.38 = (f32[256,256]{1,0:T(8,128)S(1)}, f32[256,256]{1,0:T(8,128)}, u32[]{:S(2)}) copy-start(f32[256,256]{1,0:T(8,128)} %get-tuple-element.55.refs_4_) | copy-start | bytes 786436
  75.2 16.0 %copy-start.43 = (f32[256,256]{1,0:T(8,128)S(1)}, f32[256,256]{1,0:T(8,128)}, u32[]{:S(2)}) copy-start(f32[256,256]{1,0:T(8,128)} %get-tuple-element.68.refs_12_) | copy-start | bytes 786436
  79.5 8.3 %collective-permute-start.28 = (f32[256,256]{1,0:T(8,128)}, f32[256,256]{1,0:T(8,128)S(1)}, u32[]{:S(2)}, u32[]{:S(2)}) collective-permute-start(f32[256,256]{1,0:T(8,128)} %collective-permute-done.23.refs_11_.refs_10_), channel_id=1, source_target_pairs={{0,8},{8,24},{24,16},{16,0},{1,9},{9,25},{25,17},{17,1},{10,2},{2,... | collective-permute-start | bytes 786440 | tf_op jit(solution)/shard_map/ppermute | solution.py:357
  80.0 10.7 %collective-permute-start.29 = (f32[256,256]{1,0:T(8,128)S(1)}, f32[256,256]{1,0:T(8,128)S(1)}, u32[]{:S(2)}, u32[]{:S(2)}) collective-permute-start(f32[256,256]{1,0:T(8,128)S(1)} %collective-permute-done.24.refs_15_.refs_14_), channel_id=1, source_target_pairs={{8,0},{24,8},{16,24},{0,16},{9,1},{25,9},{17,25},{1,17},{2,10},{18... | collective-permute-start | bytes 786440 | tf_op jit(solution)/shard_map/ppermute | solution.py:357
  85.1 9.1 %collective-permute-start.26 = (f32[256,256]{1,0:T(8,128)S(1)}, f32[256,256]{1,0:T(8,128)S(1)}, u32[]{:S(2)}, u32[]{:S(2)}) collective-permute-start(f32[256,256]{1,0:T(8,128)S(1)} %collective-permute-done.21.refs_3_.refs_2_), channel_id=1, source_target_pairs={{0,8},{8,24},{24,16},{16,0},{1,9},{9,25},{25,17},{17,1},{10,2},{2,... | collective-permute-start | bytes 786440 | tf_op jit(solution)/shard_map/ppermute | solution.py:357
  85.6 9.8 %collective-permute-start.27 = (f32[256,256]{1,0:T(8,128)S(1)}, f32[256,256]{1,0:T(8,128)S(1)}, u32[]{:S(2)}, u32[]{:S(2)}) collective-permute-start(f32[256,256]{1,0:T(8,128)S(1)} %collective-permute-done.22.refs_7_.refs_6_), channel_id=1, source_target_pairs={{8,0},{24,8},{16,24},{0,16},{9,1},{25,9},{17,25},{1,17},{2,10},{18... | collective-permute-start | bytes 786440 | tf_op jit(solution)/shard_map/ppermute | solution.py:357
  87.2 11.2 %collective-permute-start.16 = (f32[256,256]{1,0:T(8,128)S(1)}, f32[256,256]{1,0:T(8,128)S(1)}, u32[]{:S(2)}, u32[]{:S(2)}) collective-permute-start(f32[256,256]{1,0:T(8,128)S(1)} %get-tuple-element.106), channel_id=1, source_target_pairs={{0,2},{1,3},{2,0},{3,1},{4,6},{5,7},{6,4},{7,5},{8,10},{9,11},{10,... | collective-permute-start | bytes 786440 | tf_op jit(solution)/shard_map/ppermute | solution.py:86
  87.8 25.9 %collective-permute-start.20 = (f32[4,2,64,512]{3,2,1,0:T(8,128)S(1)}, f32[4,2,64,512]{3,2,1,0:T(8,128)S(1)}, u32[]{:S(2)}, u32[]{:S(2)}) collective-permute-start(f32[4,2,64,512]{3,2,1,0:T(8,128)S(1)} %bitcast.35), channel_id=1, source_target_pairs={{0,1},{1,0},{2,3},{3,2},{4,5},{5,4},{6,7},{7,6},{8,9},{9,8},{10,11... | collective-permute-start | bytes 3145736 | tf_op jit(solution)/shard_map/ppermute | solution.py:86
  90.7 8.5 %collective-permute-start.9 = (f32[256,256]{1,0:T(8,128)S(1)}, f32[256,256]{1,0:T(8,128)S(1)}, u32[]{:S(2)}, u32[]{:S(2)}) collective-permute-start(f32[256,256]{1,0:T(8,128)S(1)} %get-tuple-element.108), channel_id=1, source_target_pairs={{0,2},{1,3},{2,0},{3,1},{4,6},{5,7},{6,4},{7,5},{8,10},{9,11},{10,... | collective-permute-start | bytes 786440 | tf_op jit(solution)/shard_map/ppermute | solution.py:86
  94.2 20.6 %collective-permute-start.25 = (f32[512,512]{1,0:T(8,128)S(1)}, f32[512,512]{1,0:T(8,128)S(1)}, u32[]{:S(2)}, u32[]{:S(2)}) collective-permute-start(f32[512,512]{1,0:T(8,128)S(1)} %get-tuple-element.74.send_ref), channel_id=1, source_target_pairs={{0,1},{1,0},{2,3},{3,2},{4,5},{5,4},{6,7},{7,6},{8,9},{9,8},{10,11... | collective-permute-start | bytes 3145736 | tf_op jit(solution)/shard_map/ppermute | solution.py:86
  98.3 15.5 %copy-start.21 = (f32[512,512]{1,0:T(8,128)}, f32[512,512]{1,0:T(8,128)S(1)}, u32[]{:S(2)}) copy-start(f32[512,512]{1,0:T(8,128)S(1)} %get-tuple-element.76.send_ref) | copy-start | bytes 3145732
  98.3 17.5 %collective-permute-start.30 = (f32[512,512]{1,0:T(8,128)S(1)}, f32[512,512]{1,0:T(8,128)S(1)}, u32[]{:S(2)}, u32[]{:S(2)}) collective-permute-start(f32[512,512]{1,0:T(8,128)S(1)} %get-tuple-element.76.send_ref), channel_id=1, source_target_pairs={{0,1},{1,0},{2,3},{3,2},{4,5},{5,4},{6,7},{7,6},{8,9},{9,8},{10,11... | collective-permute-start | bytes 3145736 | tf_op jit(solution)/shard_map/ppermute | solution.py:86
  98.5 12.4 %collective-permute-start.17 = (f32[128,256]{1,0:T(8,128)S(1)}, f32[128,256]{1,0:T(8,128)S(1)}, u32[]{:S(2)}, u32[]{:S(2)}) collective-permute-start(f32[128,256]{1,0:T(8,128)S(1)} %slice_add_fusion.16), channel_id=1, source_target_pairs={{0,4},{1,5},{2,6},{3,7},{4,0},{5,1},{6,2},{7,3},{8,12},{9,13},{10,... | collective-permute-start | bytes 393224 | tf_op jit(solution)/shard_map/ppermute | solution.py:86
  99.3 14.3 %collective-permute-start.10 = (f32[128,256]{1,0:T(8,128)S(1)}, f32[128,256]{1,0:T(8,128)S(1)}, u32[]{:S(2)}, u32[]{:S(2)}) collective-permute-start(f32[128,256]{1,0:T(8,128)S(1)} %slice_add_fusion.18), channel_id=1, source_target_pairs={{0,4},{1,5},{2,6},{3,7},{4,0},{5,1},{6,2},{7,3},{8,12},{9,13},{10,... | collective-permute-start | bytes 393224 | tf_op jit(solution)/shard_map/ppermute | solution.py:86
  124.1 50.8 %collective-permute-start.35 = (f32[3,256,512]{2,1,0:T(8,128)}, f32[3,256,512]{2,1,0:T(8,128)}, u32[]{:S(2)}, u32[]{:S(2)}) collective-permute-start(f32[3,256,512]{2,1,0:T(8,128)} %get-tuple-element.80), channel_id=1, source_target_pairs={{0,1},{1,0},{2,3},{3,2},{4,5},{5,4},{6,7},{7,6},{8,9},{9,8},{10,11... | collective-permute-start | bytes 4718600 | tf_op jit(solution)/shard_map/ppermute | solution.py:86
  138.9 32.4 %collective-permute-start.44 = (f32[2,256,512]{2,1,0:T(8,128)}, f32[2,256,512]{2,1,0:T(8,128)}, u32[]{:S(2)}, u32[]{:S(2)}) collective-permute-start(f32[2,256,512]{2,1,0:T(8,128)} %get-tuple-element.87), channel_id=1, source_target_pairs={{0,1},{1,0},{2,3},{3,2},{4,5},{5,4},{6,7},{7,6},{8,9},{9,8},{10,11... | collective-permute-start | bytes 3145736 | tf_op jit(solution)/shard_map/ppermute | solution.py:86
  139.3 14.9 %collective-permute-start.31 = (f32[256,512]{1,0:T(8,128)S(1)}, f32[256,512]{1,0:T(8,128)}, u32[]{:S(2)}, u32[]{:S(2)}) collective-permute-start(f32[256,512]{1,0:T(8,128)S(1)} %get-tuple-element.96.refs_6_), channel_id=1, source_target_pairs={{0,2},{1,3},{2,0},{3,1},{4,6},{5,7},{6,4},{7,5},{8,10},{9,11},{10,... | collective-permute-start | bytes 1572872 | tf_op jit(solution)/shard_map/ppermute | solution.py:86
  139.3 30.8 %collective-permute-start.33 = (f32[256,512]{1,0:T(8,128)S(1)}, f32[256,512]{1,0:T(8,128)}, u32[]{:S(2)}, u32[]{:S(2)}) collective-permute-start(f32[256,512]{1,0:T(8,128)S(1)} %get-tuple-element.98.refs_7_), channel_id=1, source_target_pairs={{0,2},{1,3},{2,0},{3,1},{4,6},{5,7},{6,4},{7,5},{8,10},{9,11},{10,... | collective-permute-start | bytes 1572872 | tf_op jit(solution)/shard_map/ppermute | solution.py:86
  141.3 30.0 %copy-start.24 = (f32[2,256,512]{2,1,0:T(8,128)S(1)}, f32[2,256,512]{2,1,0:T(8,128)}, u32[]{:S(2)}) copy-start(f32[2,256,512]{2,1,0:T(8,128)} %copy-done.23) | copy-start | bytes 3145732
  155.3 23.1 %collective-permute-start.32 = (f32[128,512]{1,0:T(8,128)S(1)}, f32[128,512]{1,0:T(8,128)S(1)}, u32[]{:S(2)}, u32[]{:S(2)}) collective-permute-start(f32[128,512]{1,0:T(8,128)S(1)} %slice_add_fusion.8), channel_id=1, source_target_pairs={{0,4},{1,5},{2,6},{3,7},{4,0},{5,1},{6,2},{7,3},{8,12},{9,13},{10,... | collective-permute-start | bytes 786440 | tf_op jit(solution)/shard_map/ppermute | solution.py:86
  171.2 12.9 %collective-permute-start.34 = (f32[128,512]{1,0:T(8,128)S(1)}, f32[128,512]{1,0:T(8,128)S(1)}, u32[]{:S(2)}, u32[]{:S(2)}) collective-permute-start(f32[128,512]{1,0:T(8,128)S(1)} %slice_add_fusion.6), channel_id=1, source_target_pairs={{0,4},{1,5},{2,6},{3,7},{4,0},{5,1},{6,2},{7,3},{8,12},{9,13},{10,... | collective-permute-start | bytes 786440 | tf_op jit(solution)/shard_map/ppermute | solution.py:86
  172.8 12.8 %collective-permute-start.45 = (f32[2,64,512]{2,1,0:T(8,128)S(1)}, f32[2,64,512]{2,1,0:T(8,128)S(1)}, u32[]{:S(2)}, u32[]{:S(2)}) collective-permute-start(f32[2,64,512]{2,1,0:T(8,128)S(1)} %get-tuple-element.102), channel_id=1, source_target_pairs={{0,8},{8,0},{16,24},{24,16},{1,9},{9,1},{17,25},{25,17},{2,10},{10... | collective-permute-start | bytes 786440 | tf_op jit(solution)/shard_map/ppermute | solution.py:86
  173.5 14.8 %collective-permute-start.46 = (f32[2,64,512]{2,1,0:T(8,128)S(1)}, f32[2,64,512]{2,1,0:T(8,128)S(1)}, u32[]{:S(2)}, u32[]{:S(2)}) collective-permute-start(f32[2,64,512]{2,1,0:T(8,128)S(1)} %get-tuple-element.104), channel_id=1, source_target_pairs={{0,16},{8,24},{16,0},{24,8},{1,17},{9,25},{17,1},{25,9},{2,18},{10... | collective-permute-start | bytes 786440 | tf_op jit(solution)/shard_map/ppermute | solution.py:86
  175.0 13.7 %collective-permute-start.47 = (f32[2,64,512]{2,1,0:T(8,128)S(1)}, f32[2,64,512]{2,1,0:T(8,128)S(1)}, u32[]{:S(2)}, u32[]{:S(2)}) collective-permute-start(f32[2,64,512]{2,1,0:T(8,128)S(1)} %get-tuple-element.103), channel_id=1, source_target_pairs={{0,24},{8,16},{16,8},{24,0},{1,25},{9,17},{17,9},{25,1},{2,26},{10... | collective-permute-start | bytes 786440 | tf_op jit(solution)/shard_map/ppermute | solution.py:86
  178.3 17.9 %collective-permute-start.36 = (f32[3,64,512]{2,1,0:T(8,128)S(1)}, f32[3,64,512]{2,1,0:T(8,128)S(1)}, u32[]{:S(2)}, u32[]{:S(2)}) collective-permute-start(f32[3,64,512]{2,1,0:T(8,128)S(1)} %get-tuple-element.99), channel_id=1, source_target_pairs={{0,8},{8,0},{16,24},{24,16},{1,9},{9,1},{17,25},{25,17},{2,10},{10... | collective-permute-start | bytes 1179656 | tf_op jit(solution)/shard_map/ppermute | solution.py:86
  184.1 20.5 %collective-permute-start.37 = (f32[3,64,512]{2,1,0:T(8,128)S(1)}, f32[3,64,512]{2,1,0:T(8,128)S(1)}, u32[]{:S(2)}, u32[]{:S(2)}) collective-permute-start(f32[3,64,512]{2,1,0:T(8,128)S(1)} %get-tuple-element.101), channel_id=1, source_target_pairs={{0,16},{8,24},{16,0},{24,8},{1,17},{9,25},{17,1},{25,9},{2,18},{10... | collective-permute-start | bytes 1179656 | tf_op jit(solution)/shard_map/ppermute | solution.py:86
  185.6 19.0 %collective-permute-start.38 = (f32[3,64,512]{2,1,0:T(8,128)S(1)}, f32[3,64,512]{2,1,0:T(8,128)S(1)}, u32[]{:S(2)}, u32[]{:S(2)}) collective-permute-start(f32[3,64,512]{2,1,0:T(8,128)S(1)} %get-tuple-element.100), channel_id=1, source_target_pairs={{0,24},{8,16},{16,8},{24,0},{1,25},{9,17},{17,9},{25,1},{2,26},{10... | collective-permute-start | bytes 1179656 | tf_op jit(solution)/shard_map/ppermute | solution.py:86
  188.8 16.0 %collective-permute-start.48 = (f32[2,32,512]{2,1,0:T(8,128)S(1)}, f32[2,32,512]{2,1,0:T(8,128)S(1)}, u32[]{:S(2)}, u32[]{:S(2)}) collective-permute-start(f32[2,32,512]{2,1,0:T(8,128)S(1)} %slice.265), channel_id=1, source_target_pairs={{0,2},{1,3},{2,0},{3,1},{4,6},{5,7},{6,4},{7,5},{8,10},{9,11},{10,... | collective-permute-start | bytes 393224 | tf_op jit(solution)/shard_map/ppermute | solution.py:86
  204.7 20.8 %copy-start.37 = (f32[2,64,512]{2,1,0:T(8,128)S(1)}, f32[2,64,512]{2,1,0:T(8,128)}, u32[]{:S(2)}) copy-start(f32[2,64,512]{2,1,0:T(8,128)} %copy-done.36) | copy-start | bytes 786436
  204.8 7.9 %collective-permute-start.39 = (f32[3,32,512]{2,1,0:T(8,128)S(1)}, f32[3,32,512]{2,1,0:T(8,128)S(1)}, u32[]{:S(2)}, u32[]{:S(2)}) collective-permute-start(f32[3,32,512]{2,1,0:T(8,128)S(1)} %slice.257), channel_id=1, source_target_pairs={{0,2},{1,3},{2,0},{3,1},{4,6},{5,7},{6,4},{7,5},{8,10},{9,11},{10,... | collective-permute-start | bytes 589832 | tf_op jit(solution)/shard_map/ppermute | solution.py:86
  204.9 7.9 %collective-permute-start.49 = (f32[2,16,512]{2,1,0:T(8,128)S(1)}, f32[2,16,512]{2,1,0:T(8,128)S(1)}, u32[]{:S(2)}, u32[]{:S(2)}) collective-permute-start(f32[2,16,512]{2,1,0:T(8,128)S(1)} %slice.267), channel_id=1, source_target_pairs={{0,4},{1,5},{2,6},{3,7},{4,0},{5,1},{6,2},{7,3},{8,12},{9,13},{10,... | collective-permute-start | bytes 196616 | tf_op jit(solution)/shard_map/ppermute | solution.py:86
  212.7 5.7 %collective-permute-start.40 = (f32[3,16,512]{2,1,0:T(8,128)S(1)}, f32[3,16,512]{2,1,0:T(8,128)S(1)}, u32[]{:S(2)}, u32[]{:S(2)}) collective-permute-start(f32[3,16,512]{2,1,0:T(8,128)S(1)} %slice.259), channel_id=1, source_target_pairs={{0,4},{1,5},{2,6},{3,7},{4,0},{5,1},{6,2},{7,3},{8,12},{9,13},{10,... | collective-permute-start | bytes 294920 | tf_op jit(solution)/shard_map/ppermute | solution.py:86
  212.8 8.0 %collective-permute-start.50 = (f32[2,16,512]{2,1,0:T(8,128)S(1)}, f32[2,16,512]{2,1,0:T(8,128)S(1)}, u32[]{:S(2)}, u32[]{:S(2)}) collective-permute-start(f32[2,16,512]{2,1,0:T(8,128)S(1)} %slice_add_fusion.21), channel_id=1, source_target_pairs={{0,24},{8,16},{16,8},{24,0},{1,25},{9,17},{17,9},{25,1},{2,26},{10... | collective-permute-start | bytes 196616 | tf_op jit(solution)/shard_map/ppermute | solution.py:86
  215.1 6.9 %collective-permute-start.51 = (f32[2,16,512]{2,1,0:T(8,128)S(1)}, f32[2,16,512]{2,1,0:T(8,128)S(1)}, u32[]{:S(2)}, u32[]{:S(2)}) collective-permute-start(f32[2,16,512]{2,1,0:T(8,128)S(1)} %slice_add_fusion.21), channel_id=1, source_target_pairs={{0,16},{8,24},{16,0},{24,8},{1,17},{9,25},{17,1},{25,9},{2,18},{10... | collective-permute-start | bytes 196616 | tf_op jit(solution)/shard_map/ppermute | solution.py:86
  216.6 5.4 %collective-permute-start.52 = (f32[2,16,512]{2,1,0:T(8,128)S(1)}, f32[2,16,512]{2,1,0:T(8,128)S(1)}, u32[]{:S(2)}, u32[]{:S(2)}) collective-permute-start(f32[2,16,512]{2,1,0:T(8,128)S(1)} %slice_add_fusion.21), channel_id=1, source_target_pairs={{0,8},{8,0},{16,24},{24,16},{1,9},{9,1},{17,25},{25,17},{2,10},{10... | collective-permute-start | bytes 196616 | tf_op jit(solution)/shard_map/ppermute | solution.py:86
  218.4 6.0 %collective-permute-start.41 = (f32[3,16,512]{2,1,0:T(8,128)S(1)}, f32[3,16,512]{2,1,0:T(8,128)S(1)}, u32[]{:S(2)}, u32[]{:S(2)}) collective-permute-start(f32[3,16,512]{2,1,0:T(8,128)S(1)} %slice_add_fusion.20), channel_id=1, source_target_pairs={{0,24},{8,16},{16,8},{24,0},{1,25},{9,17},{17,9},{25,1},{2,26},{10... | collective-permute-start | bytes 294920 | tf_op jit(solution)/shard_map/ppermute | solution.py:86
  219.6 5.6 %collective-permute-start.42 = (f32[3,16,512]{2,1,0:T(8,128)S(1)}, f32[3,16,512]{2,1,0:T(8,128)S(1)}, u32[]{:S(2)}, u32[]{:S(2)}) collective-permute-start(f32[3,16,512]{2,1,0:T(8,128)S(1)} %slice_add_fusion.20), channel_id=1, source_target_pairs={{0,16},{8,24},{16,0},{24,8},{1,17},{9,25},{17,1},{25,9},{2,18},{10... | collective-permute-start | bytes 294920 | tf_op jit(solution)/shard_map/ppermute | solution.py:86
  220.9 4.6 %collective-permute-start.43 = (f32[3,16,512]{2,1,0:T(8,128)S(1)}, f32[3,16,512]{2,1,0:T(8,128)S(1)}, u32[]{:S(2)}, u32[]{:S(2)}) collective-permute-start(f32[3,16,512]{2,1,0:T(8,128)S(1)} %slice_add_fusion.20), channel_id=1, source_target_pairs={{0,8},{8,0},{16,24},{24,16},{1,9},{9,1},{17,25},{25,17},{2,10},{10... | collective-permute-start | bytes 294920 | tf_op jit(solution)/shard_map/ppermute | solution.py:86
  (57 other events, 199.7 us)

commit v5 on v0

v5 whole, which is shorter than its diff:
```python
import functools

import jax
import jax.numpy as jnp
from jax import lax
from jax.experimental import pallas as pl
from jax.experimental.pallas import tpu as pltpu
from jax.sharding import PartitionSpec as P

AXES = ("row", "col")
F32 = jnp.float32
BF16 = jnp.bfloat16
NN = (((1,), (0,)), ((), ()))
NT = (((1,), (1,)), ((), ()))
MIB = 1024 * 1024
WAIT = ("wait",)


def split(value):
    high = value.astype(BF16)
    return high, (value - high.astype(F32)).astype(BF16)


def one_pass(left, right, dims=NN):
    return lax.dot_general(left, right, dims, preferred_element_type=F32)


def product(left, right):
    return one_pass(left[0], right[0]) + (
        one_pass(left[0], right[1]) + one_pass(left[1], right[0])
    )


def turn(chooser, pair):
    return [one_pass(chooser, half, NT).astype(BF16) for half in pair]


def pair_of(high_ref, low_ref, *index):
    return (high_ref[index], low_ref[index]) if index else (high_ref[...], low_ref[...])


def store_pair(high_ref, low_ref, pair, *index):
    index = index if index else ...
    high_ref[index], low_ref[index] = pair


def shape(*dims, dtype=F32):
    return jax.ShapeDtypeStruct(dims, dtype)


def gray(place):
    return place ^ (place >> 1)


def reversed_bits(count):
    order = [0]
    step = 1
    while step < count:
        order = [value + bit * step for value in order for bit in (0, 1)]
        step *= 2
    return order


def swap(value, axis, size, change):
    return lax.ppermute(value, axis, [(place, place ^ change) for place in range(size)])


def call(body, outs, args, smem=0, hbm=0, scratch=(), vmem=8, after=None):
    places = [pltpu.SMEM] * smem + [pltpu.HBM] * hbm
    places += [pltpu.VMEM] * (len(args) - len(places))
    count = len(args)
    args = list(args)
    inner = body
    if after is not None:
        args.append(after)
        places.append(pl.ANY)

        def inner(*refs):
            body(*refs[:count], *refs[count + 1 :])

    results = pl.pallas_call(
        inner,
        out_shape=outs,
        in_specs=[pl.BlockSpec(memory_space=place) for place in places],
        out_specs=[pl.BlockSpec(memory_space=pltpu.VMEM)] * len(outs),
        scratch_shapes=scratch,
        compiler_params=pltpu.CompilerParams(vmem_limit_bytes=vmem * MIB),
        cost_estimate=pl.CostEstimate(flops=1024, bytes_accessed=1024, transcendentals=0),
    )(*args)
    return list(results)


def cut_kernel(members, lanes, info_ref, factors_ref, *refs):
    *outs, sems = refs
    half, unit = outs[0].shape
    first = pl.multiple_of(info_ref[0] * (2 * half), 2 * half)
    copies = []
    for at, out_ref in enumerate(outs):
        member, lane, way = at // (2 * lanes), at // 2 % lanes, at % 2
        source = factors_ref.at[
            member, pl.ds(first + way * half, half), lane * unit : (lane + 1) * unit
        ]
        copies.append(pltpu.make_async_copy(source, out_ref, sems.at[at]))
        copies[-1].start()
    for at, out_ref in enumerate(outs):
        copies[at].wait()
        out_ref[...] = out_ref[...] * info_ref[1 + at // (2 * lanes)].astype(F32)


def fetch_groups(order_ref, source_ref, target_ref, sems, groups):
    size = source_ref.shape[0] // groups
    copies = []
    for g in range(groups):
        start = pl.multiple_of(order_ref[g] * size, size)
        copies.append(
            pltpu.make_async_copy(
                source_ref.at[pl.ds(start, size), :],
                target_ref.at[pl.ds(g * size, size), :],
                sems.at[g],
            )
        )
        copies[-1].start()
    return copies


def region_kernel(groups, order_ref, region_ref, high_ref, low_ref, held_ref, sems):
    size = region_ref.shape[0] // groups
    copies = fetch_groups(order_ref, region_ref, held_ref, sems, groups)
    for g in range(groups):
        copies[g].wait()
        rows = slice(g * size, (g + 1) * size)
        store_pair(high_ref, low_ref, split(held_ref[rows, :]), rows)


def factor_kernel(groups, member, order_ref, factors_ref, chooser_ref, high_ref, low_ref, held_ref, sems):
    size = factors_ref.shape[1] // groups
    copies = fetch_groups(order_ref, factors_ref.at[member], held_ref, sems, groups)
    for g in range(groups):
        copies[g].wait()
        rows = slice(g * size, (g + 1) * size)
        held_ref[rows, :] = held_ref[rows, :] * order_ref[groups + g].astype(F32)
    store_pair(high_ref, low_ref, turn(chooser_ref[...], split(held_ref[...])))


def own_kernel(info_ref, factors_ref, chooser_ref, high_ref, low_ref, thigh_ref, tlow_ref, held_ref, sems):
    members, rows, _ = held_ref.shape
    start = pl.multiple_of(info_ref[0] * rows, rows)
    copies = []
    for j in range(members):
        copies.append(
            pltpu.make_async_copy(
                factors_ref.at[j, pl.ds(start, rows), :], held_ref.at[j], sems.at[j]
            )
        )
        copies[-1].start()
    for j in range(members):
        copies[j].wait()
        pair = split(held_ref[j] * info_ref[1 + j].astype(F32))
        store_pair(high_ref, low_ref, pair, j)
        store_pair(thigh_ref, tlow_ref, turn(chooser_ref[...], pair), j)


def link_kernel(
    groups, children, share, order_ref, gathered_ref, slices_ref, diag_ref, chooser_ref,
    own_high_ref, own_low_ref, high_ref, low_ref, lift_high_ref, lift_low_ref, framed_ref,
    corner_ref, held_ref,
):
    size = slices_ref.shape[1]
    chooser = chooser_ref[...]
    for g in range(groups):
        start = pl.ds(pl.multiple_of(order_ref[g] * size, size), size)
        for c in range(children):
            held_ref[c, start, :] = gathered_ref[g, c]
    for c in range(children):
        pair = split(held_ref[c])
        store_pair(high_ref, low_ref, pair, c)
        lifted = product(pair_of(own_high_ref, own_low_ref, 0), pair)
        store_pair(lift_high_ref, lift_low_ref, turn(chooser, split(lifted)), c)
        framed = product(split(diag_ref[0]), pair)
        framed_ref[c] = framed
        corner_ref[c] = share * product(turn(chooser, split(slices_ref[c])), split(framed))


def unit_kernel(count, place_ref, high_ref, low_ref, *refs):
    keep_ref, send_ref = refs[-2:]
    middle = keep_ref.shape[0]
    chosen = []
    for way in range(2):
        candidates = refs[way * count :][:count]
        value = candidates[0][...]
        for at in range(1, count):
            value = jnp.where(place_ref[way] == at, candidates[at][...], value)
        chosen.append(value)
    right = split(jnp.concatenate(chosen))
    send_ref[...] = product((high_ref[middle:], low_ref[middle:]), right)
    keep_ref[...] = product((high_ref[:middle], low_ref[:middle]), right)


def unit_gram_kernel(high_ref, low_ref, keep_ref, send_ref, out_ref):
    middle = keep_ref.shape[0]
    out_ref[...] = product(
        (high_ref[:, :middle], low_ref[:, :middle]), split(keep_ref[...])
    ) + product((high_ref[:, middle:], low_ref[:, middle:]), split(send_ref[...]))


def store_halves(keep_ref, send_ref, index, value):
    middle = value.shape[0] // 2
    keep_ref[index] = value[:middle]
    send_ref[index] = value[middle:]


def parent_kernel(
    children, weight_ref, chooser_ref, own_high_ref, own_low_ref, own_thigh_ref, own_tlow_ref,
    link_high_ref, link_low_ref, left_ref, right_ref,
    col_ref, turned_ref, high_ref, low_ref, thigh_ref, tlow_ref, keep_ref, send_ref,
):
    chooser = chooser_ref[...]
    column = -jnp.concatenate([left_ref[...], right_ref[...]], axis=1)
    column = column * weight_ref[0].astype(F32)
    col_ref[...] = column
    pair = split(column)
    turned_pair = turn(chooser, pair)
    parent = pair_of(own_thigh_ref, own_tlow_ref, 0)
    store_halves(keep_ref, send_ref, 0, -product(parent, pair))
    for c in range(children):
        turned = product(pair, pair_of(link_high_ref, link_low_ref, c))
        turned_ref[c] = turned
        lifted = split(turned)
        store_pair(high_ref, low_ref, lifted, c)
        store_pair(thigh_ref, tlow_ref, turn(chooser, lifted), c)
        upper = product(parent, lifted) - product(
            turned_pair, pair_of(own_high_ref, own_low_ref, c + 1)
        )
        store_halves(keep_ref, send_ref, 1 + c, upper)


def child_kernel(
    children, lanes, own_high_ref, own_low_ref, own_thigh_ref, own_tlow_ref,
    high_ref, low_ref, thigh_ref, tlow_ref, lift_high_ref, lift_low_ref, corner_ref, *refs
):
    keep_ref, send_ref = refs[-2:]
    for c in range(children):
        grams = [ref[...] for ref in refs[c * lanes : (c + 1) * lanes]]
        turned = pair_of(high_ref, low_ref, c)
        total = corner_ref[c] + jnp.concatenate(grams, axis=1)
        total += product(pair_of(own_thigh_ref, own_tlow_ref, c + 1), turned)
        total += product(
            pair_of(thigh_ref, tlow_ref, c), pair_of(own_high_ref, own_low_ref, c + 1)
        )
        total -= product(pair_of(lift_high_ref, lift_low_ref, c), turned)
        store_halves(keep_ref, send_ref, c, total)


def column_kernel(children, lanes, weight_ref, col_ref, turned_ref, *refs):
    out_ref = refs[-1]
    out_ref[0] = col_ref[...]
    for c in range(children):
        total = jnp.concatenate([ref[...] for ref in refs[c * lanes : (c + 1) * lanes]], axis=1)
        out_ref[c + 1] = -(total + turned_ref[c]) * weight_ref[c + 1].astype(F32)


def finish_kernel(rows, place_ref, diag_ref, framed_ref, *refs):
    parents, offspring = refs[:rows], refs[rows : 2 * rows]
    diags_ref, uppers_ref = refs[2 * rows :]
    part = parents[0].shape[1]

    def chosen(pieces, row):
        value = pieces[0][...]
        for change in range(1, rows):
            value = jnp.where(place_ref[0] ^ change == row, pieces[change][...], value)
        return value

    for row in range(rows):
        at = slice(row * part, (row + 1) * part)
        above, below = chosen(parents, row), chosen(offspring, row)
        diags_ref[0, at] = diag_ref[0, at] + above[0]
        diags_ref[1:, at] = diag_ref[1:, at] + below
        uppers_ref[:, at] = above[1:] - framed_ref[:, at]


def select_step(flag_ref, ins, outs):
    for way in range(2):
        outs[way][...] = jnp.where(flag_ref[0] != 0, ins[way][...], ins[2 + way][...])


def stack_step(flag_ref, ins, outs):
    for at in range(ins[0].shape[0]):
        for side in range(2):
            outs[0][2 * at + side] = ins[side][at]


def halve_step(flag_ref, ins, outs):
    size = outs[0].shape[-2]
    for at, out in enumerate(outs):
        rows = pl.ds(at * size, size)
        index = (rows,) if len(out.shape) == 2 else (slice(None), rows)
        total = ins[0][index]
        for other in ins[1:]:
            total = total + other[index]
        out[...] = total


def step_kernel(tasks, flag_ref, *refs):
    start = 0
    end = sum(ins for _, ins, _ in tasks)
    for body, ins, outs in tasks:
        body(flag_ref, refs[start : start + ins], refs[end : end + outs])
        start += ins
        end += outs


def shards(region_inverse, factor_cols, parent_factor, diag_inverse, listed):
    row_count = lax.axis_size("row")
    col_count = lax.axis_size("col")
    row_place = lax.axis_index("row")
    col_place = lax.axis_index("col")
    col_bits = col_count.bit_length() - 1
    rows_here, cols_here = region_inverse.shape
    members, _, width = factor_cols.shape
    children = members - 1
    group = rows_here // col_count
    ratio = col_count // row_count
    diag_width = width // col_count
    part = diag_width // row_count
    first_row = row_place * rows_here
    source = col_place // ratio
    lanes = 2
    unit = width // lanes
    half = cols_here // 2

    def ring(forward):
        pairs = []
        for col in range(col_count):
            start = col // ratio
            for place in range(row_count):
                at = (start ^ gray(place)) * col_count + col
                to = (start ^ gray((place + 1) % row_count)) * col_count + col
                pairs.append((at, to) if forward else (to, at))
        return pairs

    rings = (ring(True), ring(False))

    column_info = jnp.concatenate(
        [(col_place % ratio)[None], listed[:, col_place * cols_here // width]]
    ).astype(jnp.int32)
    flat = call(
        functools.partial(cut_kernel, members, lanes),
        [shape(half, unit)] * (members * lanes * 2),
        [column_info, factor_cols],
        smem=1, hbm=1, vmem=56,
        scratch=[pltpu.SemaphoreType.DMA((members * lanes * 2,))],
    )
    chunks = [
        [flat[(j * lanes + lane) * 2 :][:2] for lane in range(lanes)] for j in range(members)
    ]

    source_flag = (row_place == source).astype(jnp.int32)[None]
    forward_place = row_place ^ source
    shift = 1
    while shift < row_count:
        forward_place = forward_place ^ (forward_place >> shift)
        shift *= 2
    places = jnp.stack([forward_place, (row_count - forward_place) % row_count]).astype(jnp.int32)

    relative = jnp.array(reversed_bits(col_count), jnp.int32) ^ col_place
    own_weights = listed[:, (first_row + col_place * group) // width]
    own_info = jnp.concatenate([col_place[None], own_weights]).astype(jnp.int32)
    group_weights = jnp.take(listed, (first_row + relative * group) // width, axis=1)

    halving = jnp.array(reversed_bits(col_count), jnp.int32).reshape(2, 1, col_count // 2, 1)
    by_row = lax.iota(jnp.int32, row_count).reshape(1, row_count, 1, 1) ^ row_place
    inner = lax.iota(jnp.int32, part).reshape(1, 1, 1, part)
    wanted = ((halving ^ col_place) * diag_width + by_row * part + inner).reshape(width, 1)
    chooser = (wanted == lax.iota(jnp.int32, width)[None, :]).astype(BF16)

    last = [flat[0]]
    held = {}
    moved = [[] for _ in range(lanes)]
    received = [[] for _ in range(lanes)]

    def heavy(body, outs, args, **options):
        results = call(body, outs, args, after=last[0], **options)
        last[0] = results[0]
        return results

    def ring_flow(lane):
        for _ in range(lane):
            yield WAIT
        stages = members + row_count - 2
        for stage in range(stages):
            arrived = received[lane][-1] if stage else None
            if stage == 0:
                moving = chunks[0][lane]
            elif stage < members:
                moving = yield (select_step, chunks[stage][lane] + arrived, [shape(half, unit)] * 2)
            else:
                yield WAIT
                moving = arrived
            moved[lane].append(moving)
            received[lane].append(
                [lax.ppermute(moving[way], AXES, rings[way]) for way in range(2)]
            )
            for _ in range(lanes - 1):
                yield WAIT
            if stage > row_count - 3:
                held["ready", stage - row_count + 2, lane] = True

    def link_flow():
        gathered = parent_factor[None]
        for bit in reversed(range(col_bits)):
            arrived = swap(gathered, "col", col_count, 1 << bit)
            if bit:
                yield WAIT
            dims = (2 * gathered.shape[0],) + parent_factor.shape
            (gathered,) = yield (stack_step, [gathered, arrived], [shape(*dims)])
        order = jnp.arange(col_count, dtype=jnp.int32) ^ col_place
        held["links"] = heavy(
            functools.partial(link_kernel, col_count, children, 1.0 / row_count),
            [shape(children, width, width, dtype=BF16)] * 2
            + [shape(children, width, group, dtype=BF16)] * 2
            + [shape(children, diag_width, width), shape(children, width, width)],
            [order, gathered, parent_factor, diag_inverse, chooser, *held["own"][:2]],
            smem=1, vmem=20,
            scratch=[pltpu.VMEM((children, width, width), F32)],
        )

    def prepare_flow():
        held["region"] = heavy(
            functools.partial(region_kernel, col_count),
            [shape(rows_here, cols_here, dtype=BF16)] * 2,
            [relative, region_inverse],
            smem=1, hbm=1,
            scratch=[
                pltpu.VMEM((rows_here, cols_here), F32), pltpu.SemaphoreType.DMA((col_count,))
            ],
        )
        yield WAIT
        held["own"] = heavy(
            own_kernel,
            [shape(members, group, width, dtype=BF16)] * 2
            + [shape(members, width, group, dtype=BF16)] * 2,
            [own_info, factor_cols, chooser],
            smem=1, hbm=1,
            scratch=[
                pltpu.VMEM((members, group, width), F32), pltpu.SemaphoreType.DMA((members,))
            ],
        )
        for member in range(1, members):
            yield WAIT
            held["turned", member] = heavy(
                functools.partial(factor_kernel, col_count, member),
                [shape(width, rows_here, dtype=BF16)] * 2,
                [jnp.concatenate([relative, group_weights[member]]), factor_cols, chooser],
                smem=1, hbm=1, vmem=20,
                scratch=[
                    pltpu.VMEM((rows_here, width), F32), pltpu.SemaphoreType.DMA((col_count,))
                ],
            )

    def unit_flow(member, lane):
        while ("ready", member, lane) not in held:
            yield WAIT
        candidates = []
        for way in range(2):
            candidates.append(moved[lane][member][way])
            candidates += [received[lane][member + at][way] for at in range(row_count - 1)]
        size = rows_here // 2
        keep, send = heavy(
            functools.partial(unit_kernel, row_count),
            [shape(size, unit)] * 2,
            [places, *held["region"], *candidates],
            smem=1, vmem=12,
        )
        arrived = swap(send, "col", col_count, 1)
        if member:
            held["gram", member, lane] = heavy(
                unit_gram_kernel,
                [shape(width, unit)],
                [*held["turned", member], keep, send],
                vmem=12,
            )[0]
        yield WAIT
        for bit in range(1, col_bits):
            size //= 2
            keep, send = yield (halve_step, [keep, arrived], [shape(size, unit)] * 2)
            arrived = swap(send, "col", col_count, 1 << bit)
        held["sum", member, lane] = (yield (halve_step, [keep, arrived], [shape(size, unit)]))[0]

    def total_flow(keep, send):
        count = keep.shape[0]
        size = keep.shape[1] // row_count
        arrived = swap(send, "col", col_count, 1)
        pieces = yield (halve_step, [keep, arrived], [shape(count, size, width)] * row_count)
        arrived = [swap(pieces[d], "row", row_count, d) for d in range(1, row_count)]
        inputs = [pieces[0]] + arrived
        for bit in range(1, col_bits):
            size //= 2
            keep, send = yield (halve_step, inputs, [shape(count, size, width)] * 2)
            inputs = [keep, swap(send, "col", col_count, 1 << bit)]
        (piece,) = yield (halve_step, inputs, [shape(count, size, width)])
        return [piece] + [swap(piece, "row", row_count, d) for d in range(1, row_count)]

    def parent_flow():
        names = [("sum", 0, lane) for lane in range(lanes)] + ["links"]
        while any(name not in held for name in names):
            yield WAIT
        col, turned, *pairs, keep, send = heavy(
            functools.partial(parent_kernel, children),
            [shape(group, width), shape(children, group, width)]
            + [shape(children, group, width, dtype=BF16)] * 2
            + [shape(children, width, group, dtype=BF16)] * 2
            + [shape(members, width // 2, width)] * 2,
            [own_weights, chooser, *held["own"], *held["links"][:2]]
            + [held["sum", 0, lane] for lane in range(lanes)],
            smem=1, vmem=20,
        )
        held["parent"] = (col, turned, pairs)
        yield WAIT
        held["parent totals"] = yield from total_flow(keep, send)

    def child_flow():
        names = [("gram", 1 + c, lane) for c in range(children) for lane in range(lanes)]
        while any(name not in held for name in names + ["parent"]):
            yield WAIT
        keep, send = heavy(
            functools.partial(child_kernel, children, lanes),
            [shape(children, width // 2, width)] * 2,
            [*held["own"], *held["parent"][2], *held["links"][2:4], held["links"][5]]
            + [held[name] for name in names],
            vmem=20,
        )
        held["child totals"] = yield from total_flow(keep, send)

    def column_flow():
        names = [("sum", 1 + c, lane) for c in range(children) for lane in range(lanes)]
        while any(name not in held for name in names + ["parent"]):
            yield WAIT
        col, turned, _ = held["parent"]
        held["columns"] = heavy(
            functools.partial(column_kernel, children, lanes),
            [shape(members, group, width)],
            [own_weights, col, turned] + [held[name] for name in names],
            smem=1,
        )[0]

    flows = [ring_flow(lane) for lane in range(lanes)] + [link_flow(), prepare_flow()]
    flows += [unit_flow(j, lane) for j in range(members) for lane in range(lanes)]
    flows += [parent_flow(), child_flow(), column_flow()]
    waiting = [(flow, None) for flow in flows]
    while waiting:
        tasks = [wish for _, wish in waiting if wish not in (None, WAIT)]
        results = iter(())
        if tasks:
            outs = [out for _, _, shapes in tasks for out in shapes]
            args = [value for _, values, _ in tasks for value in values]
            sizes = [(body, len(values), len(shapes)) for body, values, shapes in tasks]
            results = iter(
                heavy(
                    functools.partial(step_kernel, sizes), outs, [source_flag, *args], smem=1
                )
            )
        answered = []
        for flow, wish in waiting:
            answer = None
            if wish not in (None, WAIT):
                answer = [next(results) for _ in wish[2]]
            answered.append((flow, answer))
        waiting = []
        for flow, answer in answered:
            try:
                waiting.append((flow, flow.send(answer)))
            except StopIteration:
                pass

    diags, uppers = heavy(
        functools.partial(finish_kernel, row_count),
        [shape(members, diag_width, width), shape(children, diag_width, width)],
        [row_place[None], diag_inverse, held["links"][4]]
        + held["parent totals"] + held["child totals"],
        smem=1,
    )
    return held["columns"], diags, uppers


def solution(mesh):
    in_specs = (
        P("row", "col"),
        P(None, "row", None),
        P(None, "col", None),
        P(None, "col", None),
        P(),
    )
    out_specs = (P(None, ("row", "col"), None), P(None, "col", None), P(None, "col", None))
    return jax.shard_map(shards, mesh=mesh, in_specs=in_specs, out_specs=out_specs, check_vma=False)
```

time: 367 us -> 223 us (0.61); the launches traced: 360 us -> 222 us
  waiting for transfers between devices: 247 us -> 88.3 us
  matrix products: 71.6 us -> 0 us
  starting transfers between devices: 1.28 us -> 56.5 us
  Pallas kernels: 0 us -> 53.3 us
  between operations: 16.4 us -> 1.31 us
  other arithmetic: 14.5 us -> 1.16 us
  local copies, waits for them, and re-layouts: 8.96 us -> 21.1 us
    psum x2 -> x0, waiting for transfers between devices: 153 us -> none  [the longest x1 89.8 us: broadcast(): return lax.psum(kept, axis)]
    ppermute x0 -> x59, waiting for transfers between devices: none -> 88.3 us  [the longest x39 61.4 us: swap(): lax.ppermute(value, axis, [(place, place ^ change) for place in range(siz...]
    reduce_scatter x3 -> x0, waiting for transfers between devices: 86.6 us -> none  [column_pass(): lax.psum_scatter(full_product, 'col', scatter_dimension=0, tiled=True)]
    dot_general x20 -> x0, matrix products: 71.6 us -> none  [the longest x11 37.3 us: matmul_left(): lax.dot_general(left, right, (((0,), (0,)), ((), ())), precision=lax.Prec...]
    ppermute x0 -> x59, starting transfers between devices: none -> 56.5 us  [the longest x39 35.9 us: swap(): lax.ppermute(value, axis, [(place, place ^ change) for place in range(siz...]
    pallas_call x0 -> x33, Pallas kernels: none -> 53.3 us  [call(): pl.pallas_call(inner, out_shape=outs, in_specs=[pl.BlockSpec(memory_space...]
    unnamed x35 -> x83, local copies, waits for them, and re-layouts: 2.31 us -> 19.2 us
    all_gather x2 -> x0, waiting for transfers between devices: 7.17 us -> none  [the longest x1 7.17 us: shards(): lax.all_gather(diag_inverse, 'col', axis=1, tiled=True)]
  transfers between devices with their start and end apart: 7 -> 59, of which waited for: 6 -> 22; matrix products, arithmetic and copies ran while one was open for 21% -> 1% of each run, Pallas kernels for 0% -> 17%
where the time goes in v5:
time: 223 us; the launch traced here: 222 us
  waiting for transfers between devices  88.3 us (40%)
  starting transfers between devices  56.5 us (25%)
  Pallas kernels  53.3 us (24%)
  local copies, waits for them, and re-layouts  21.1 us (9%)
    ppermute x39, waiting for transfers between devices, swap(): lax.ppermute(value, axis, [(place, place ^ change) for place in range(siz...  61.4 us
    pallas_call x33, Pallas kernels, call(): pl.pallas_call(inner, out_shape=outs, in_specs=[pl.BlockSpec(memory_space...  53.3 us
    ppermute x39, starting transfers between devices, swap(): lax.ppermute(value, axis, [(place, place ^ change) for place in range(siz...  35.9 us
    ppermute x20, waiting for transfers between devices, ring_flow(): lax.ppermute(moving[way], AXES, rings[way])  26.9 us
    ppermute x20, starting transfers between devices, ring_flow(): lax.ppermute(moving[way], AXES, rings[way])  20.6 us
    unnamed x83, local copies, waits for them, and re-layouts  19.2 us
  transfers between devices with their start and end apart: 59, of which 22 were waited for; matrix products, arithmetic and copies ran while one was open for 1% of the time, Pallas kernels for 17%

profile of v5, /device:TPU:0, one launch (start us, length us, event | category | flops | bytes accessed | tf_op | source)
XLA Modules:
  0.0 221.7 jit_solution(17561558908676826389)
XLA Ops:
  2.3 4.4 %shard_map.94 = (f32[256,256]{1,0:T(8,128)}, f32[256,256]{1,0:T(8,128)}, f32[256,256]{1,0:T(8,128)}, f32[256,256]{1,0:T(8,128)}, f32[256,256]{1,0:T(8,128)}, /*i...) custom-call(s32[4]{0:T(128)} %get-tuple-element.234.info_ref, ...), custom_call_target="tpu_custom_call" | custom-call | flops 1024 | bytes 1024 | tf_op jit(solution)/shard_map/pallas_call | solution.py:81
  6.6 3.0 %collective-permute-start = (f32[256,256]{1,0:T(8,128)}, f32[256,256]{1,0:T(8,128)}, u32[]{:S(2)}, u32[]{:S(2)}) collective-permute-start(f32[256,256]{1,0:T(8,128)} %get-tuple-element.123.refs_3_), channel_id=1, source_target_pairs={{0,8},{8,24},{24,16},{16,0},{1,9},{9,25},{25,17},{17,1},{10,2},{2,... | collective-permute-start | bytes 786440 | tf_op jit(solution)/shard_map/ppermute | solution.py:401
  9.7 1.9 collective-permute-start.2
  11.7 3.0 %collective-permute-start.4 = (f32[1,2,64,512]{3,2,1,0:T(8,128)}, f32[1,2,64,512]{3,2,1,0:T(8,128)}, u32[]{:S(2)}, u32[]{:S(2)}) collective-permute-start(f32[1,2,64,512]{3,2,1,0:T(8,128)} %bitcast.4.refs_5_), channel_id=1, source_target_pairs={{0,4},{1,5},{2,6},{3,7},{4,0},{5,1},{6,2},{7,3},{8,12},{9,13},{10,... | collective-permute-start | bytes 786440 | tf_op jit(solution)/shard_map/ppermute | solution.py:65
  15.3 1.6 copy-done.15
  17.8 1.1 shard_map.95
  19.0 2.8 %copy-done = f32[3,1024,512]{2,1,0:T(8,128)S(1)} copy-done((f32[3,1024,512]{2,1,0:T(8,128)S(1)}, f32[3,1024,512]{2,1,0:T(8,128)}, u32[]{:S(2)}) %copy-start) | copy-done | bytes 6291480
  21.8 2.0 shard_map.96
  27.8 2.1 shard_map.97
  32.9 1.5 collective-permute-start.7
  35.4 2.8 %copy-done.1 = f32[3,1024,512]{2,1,0:T(8,128)S(1)} copy-done((f32[3,1024,512]{2,1,0:T(8,128)S(1)}, f32[3,1024,512]{2,1,0:T(8,128)}, u32[]{:S(2)}) %copy-start.1) | copy-done | bytes 6291480
  39.1 2.3 %shard_map.98 = (bf16[512,1024]{1,0:T(8,128)(2,1)S(1)}, bf16[512,1024]{1,0:T(8,128)(2,1)S(1)}) custom-call(s32[16]{0:T(128)S(1)} %get-tuple-element.230.refs_0_, f32[3,1024,512]{2,1,0:T(8,128)S(1)} %copy-done.1, bf16[512,512]{1,0:T(8,128)(2,1)S(1)} %fusion.refs_2_.refs_4_.refs_1_, f32[256,256]{1,0:T(8,128)S(1)} %copy-done.22), custom_call_target="tpu_custom_call" | custom-call | flops 1024 | bytes 1024 | tf_op jit(solution)/shard_map/pallas_call | solution.py:81
  41.4 2.2 shard_map.99
  44.6 2.3 %shard_map.100 = (bf16[512,1024]{1,0:T(8,128)(2,1)S(1)}, bf16[512,1024]{1,0:T(8,128)(2,1)S(1)}) custom-call(s32[16]{0:T(128)S(1)} %get-tuple-element.229.refs_0_, f32[3,1024,512]{2,1,0:T(8,128)S(1)} %copy-done.1, bf16[512,512]{1,0:T(8,128)(2,1)S(1)} %fusion.refs_2_.refs_4_.refs_1_, f32[256,256]{1,0:T(8,128)} %get-tuple-element.130.refs_3_), custom_call_target="tpu_custom_call" | custom-call | flops 1024 | bytes 1024 | tf_op jit(solution)/shard_map/pallas_call | solution.py:81
  46.9 2.9 %shard_map.101 = (f32[256,256]{1,0:T(8,128)}, f32[256,256]{1,0:T(8,128)}, f32[4,2,64,512]{3,2,1,0:T(8,128)}) custom-call(s32[1]{0:T(128)} %bitcast.2.refs_0_, f32[256,256]{1,0:T(8,128)S(1)} %copy-done.36, f32[256,256]{1,0:T(8,128)S(1)} %copy-done.37, f32[256,256]{1,0:T(8,128)S(1)} %collective-permute-done.7.refs_3_.refs_5_.refs_4_, ...), custom_call_target="tpu_custom_call" | custom-call | flops 1024 | bytes 1024 | tf_op jit(solution)/shard_map/pallas_call | solution.py:81
  50.9 1.6 collective-permute-start.5
  52.9 1.5 collective-permute-start.11
  55.0 5.3 %collective-permute-done.5.refs_3_.refs_5_.refs_4_ = f32[256,256]{1,0:T(8,128)} collective-permute-done((f32[256,256]{1,0:T(8,128)}, f32[256,256]{1,0:T(8,128)}, u32[]{:S(2)}, u32[]{:S(2)}) %collective-permute-start.5) | collective-permute-done | bytes 262176 | tf_op jit(solution)/shard_map/ppermute | solution.py:401
  60.3 1.5 collective-permute-done.6.refs_4_.refs_9_.refs_8_
  63.8 1.9 shard_map.102
  65.7 1.6 collective-permute-start.14
  67.3 4.5 %shard_map.103 = (bf16[2,512,512]{2,1,0:T(8,128)(2,1)S(1)}, bf16[2,512,512]{2,1,0:T(8,128)(2,1)S(1)}, bf16[2,512,128]{2,1,0:T(8,128)(2,1)S(1)}, bf16[2,512,128]{...) custom-call(s32[8]{0:T(128)S(1)} %iota_xor_fusion.refs_0_, ...), custom_call_target="tpu_custom_call" | custom-call | flops 1024 | bytes 1024 | tf_op jit(solution)/shard_map/pallas_call | solution.py:81
  71.8 2.3 %shard_map.104 = (f32[512,256]{1,0:T(8,128)S(1)}, f32[512,256]{1,0:T(8,128)S(1)}) custom-call(s32[2]{0:T(128)S(1)} %pad_add_fusion.4.refs_0_, bf16[1024,512]{1,0:T(8,128)(2,1)S(1)} %get-tuple-element.114.refs_3_.refs_1_, bf16[1024,512]{1,0:T(8,128)(2,1)S(1)} %get-tuple-element.143.refs_2_, f32[256,256]{1,0:T(8,128)S(1)} %copy-done.25, ...), custom_call_target="tpu_custom_call" | custom-call | flops 1024 | bytes 1024 | tf_op jit(solution)/shard_map/pallas_call | solution.py:81
  74.8 8.1 %collective-permute-done.15.refs_10_.refs_9_.refs_8_ = f32[256,256]{1,0:T(8,128)S(1)} collective-permute-done((f32[256,256]{1,0:T(8,128)S(1)}, f32[256,256]{1,0:T(8,128)S(1)}, u32[]{:S(2)}, u32[]{:S(2)}) %collective-permute-start.15) | collective-permute-done | bytes 262176 | tf_op jit(solution)/shard_map/ppermute | solution.py:401
  82.9 2.3 %shard_map.105 = (f32[512,256]{1,0:T(8,128)S(1)}, f32[512,256]{1,0:T(8,128)S(1)}) custom-call(s32[2]{0:T(128)S(1)} %pad_add_fusion.4.refs_0_, bf16[1024,512]{1,0:T(8,128)(2,1)S(1)} %get-tuple-element.114.refs_3_.refs_1_, bf16[1024,512]{1,0:T(8,128)(2,1)S(1)} %get-tuple-element.143.refs_2_, f32[256,256]{1,0:T(8,128)S(1)} %copy-done.26, ...), custom_call_target="tpu_custom_call" | custom-call | flops 1024 | bytes 1024 | tf_op jit(solution)/shard_map/pallas_call | solution.py:81
  86.1 1.5 collective-permute-start.19
  89.2 5.7 %collective-permute-done.18.refs_6_.refs_5_ = f32[256,256]{1,0:T(8,128)S(1)} collective-permute-done((f32[256,256]{1,0:T(8,128)}, f32[256,256]{1,0:T(8,128)S(1)}, u32[]{:S(2)}, u32[]{:S(2)}) %collective-permute-start.18) | collective-permute-done | bytes 262176 | tf_op jit(solution)/shard_map/ppermute | solution.py:401
  94.9 2.2 shard_map.107
  97.2 1.1 collective-permute-start.24
  99.4 3.1 %collective-permute-start.20 = (f32[128,256]{1,0:T(8,128)S(1)}, f32[128,256]{1,0:T(8,128)S(1)}, u32[]{:S(2)}, u32[]{:S(2)}) collective-permute-start(f32[128,256]{1,0:T(8,128)S(1)} %get-tuple-element.156), channel_id=1, source_target_pairs={{0,4},{1,5},{2,6},{3,7},{4,0},{5,1},{6,2},{7,3},{8,12},{9,13},{10,... | collective-permute-start | bytes 393224 | tf_op jit(solution)/shard_map/ppermute | solution.py:65
  102.5 3.3 %collective-permute-done.24.refs_10_.refs_9_ = f32[256,256]{1,0:T(8,128)S(1)} collective-permute-done((f32[256,256]{1,0:T(8,128)S(1)}, f32[256,256]{1,0:T(8,128)S(1)}, u32[]{:S(2)}, u32[]{:S(2)}) %collective-permute-start.24) | collective-permute-done | bytes 262176 | tf_op jit(solution)/shard_map/ppermute | solution.py:401
  105.9 2.3 %shard_map.110 = (f32[512,256]{1,0:T(8,128)S(1)}, f32[512,256]{1,0:T(8,128)S(1)}) custom-call(s32[2]{0:T(128)S(1)} %pad_add_fusion.4.refs_0_, bf16[1024,512]{1,0:T(8,128)(2,1)S(1)} %get-tuple-element.114.refs_3_.refs_1_, bf16[1024,512]{1,0:T(8,128)(2,1)S(1)} %get-tuple-element.143.refs_2_, f32[256,256]{1,0:T(8,128)} %get-tuple-element.130.refs_3_, ...), custom_call_target="tpu_custom_call" | custom-call | flops 1024 | bytes 1024 | tf_op jit(solution)/shard_map/pallas_call | solution.py:81
  111.3 2.0 collective-permute-done.21.refs_4_
  114.5 2.9 %collective-permute-done.28.refs_6_ = f32[256,256]{1,0:T(8,128)S(1)} collective-permute-done((f32[256,256]{1,0:T(8,128)S(1)}, f32[256,256]{1,0:T(8,128)S(1)}, u32[]{:S(2)}, u32[]{:S(2)}) %collective-permute-start.28) | collective-permute-done | bytes 262176 | tf_op jit(solution)/shard_map/ppermute | solution.py:401
  118.5 3.0 %collective-permute-start.25 = (f32[128,256]{1,0:T(8,128)S(1)}, f32[128,256]{1,0:T(8,128)S(1)}, u32[]{:S(2)}, u32[]{:S(2)}) collective-permute-start(f32[128,256]{1,0:T(8,128)S(1)} %get-tuple-element.163), channel_id=1, source_target_pairs={{0,4},{1,5},{2,6},{3,7},{4,0},{5,1},{6,2},{7,3},{8,12},{9,13},{10,... | collective-permute-start | bytes 393224 | tf_op jit(solution)/shard_map/ppermute | solution.py:65
  121.5 2.4 %shard_map.113 = (f32[512,256]{1,0:T(8,128)S(1)}, f32[512,256]{1,0:T(8,128)S(1)}) custom-call(s32[2]{0:T(128)S(1)} %pad_add_fusion.4.refs_0_, bf16[1024,512]{1,0:T(8,128)(2,1)S(1)} %get-tuple-element.114.refs_3_.refs_1_, bf16[1024,512]{1,0:T(8,128)(2,1)S(1)} %get-tuple-element.143.refs_2_, f32[256,256]{1,0:T(8,128)} %get-tuple-element.138.refs_7_.refs_3_, ...), custom_call_target="tpu_custom_call" | custom-call | flops 1024 | bytes 1024 | tf_op jit(solution)/shard_map/pallas_call | solution.py:81
  124.9 2.0 collective-permute-done.25.refs_2_
  127.0 1.6 shard_map.116
  129.7 4.3 %shard_map.118 = (f32[128,512]{1,0:T(8,128)S(1)}, f32[2,128,512]{2,1,0:T(8,128)S(1)}, bf16[2,128,512]{2,1,0:T(8,128)(2,1)S(1)}, bf16[2,128,512]{2,1,0:T(8,128)(2...) custom-call(s32[3]{0:T(128)S(1)} %get-tuple-element.226.refs_0_, ...), custom_call_target="tpu_custom_call" | custom-call | flops 1024 | bytes 1024 | tf_op jit(solution)/shard_map/pallas_call | solution.py:81
  134.1 2.7 %shard_map.119 = (f32[2,256,512]{2,1,0:T(8,128)S(1)}, f32[2,256,512]{2,1,0:T(8,128)S(1)}) custom-call(bf16[3,128,512]{2,1,0:T(8,128)(2,1)S(1)} %get-tuple-element.115.refs_7_.refs_5_.refs_2_.refs_0_, bf16[3,128,512]{2,1,0:T(8,128)(2,1)S(1)} %get-tuple-element.116.refs_6_.refs_3_.refs_1_, bf16[3,512,128]{2,1,0:T(8,128)(2,1)S(1)} %copy-done.18, ...), custom_call_target="tpu_custom_call" | custom-call | flops 1024 | bytes 1024 | tf_op jit(solution)/shard_map/pallas_call | solution.py:81
  138.5 8.1 %collective-permute-done.32.refs_2_ = f32[128,256]{1,0:T(8,128)S(1)} collective-permute-done((f32[128,256]{1,0:T(8,128)S(1)}, f32[128,256]{1,0:T(8,128)S(1)}, u32[]{:S(2)}, u32[]{:S(2)}) %collective-permute-start.32) | collective-permute-done | bytes 131104 | tf_op jit(solution)/shard_map/ppermute | solution.py:65
  146.6 8.3 %collective-permute-done.33.refs_4_ = f32[256,256]{1,0:T(8,128)S(1)} collective-permute-done((f32[256,256]{1,0:T(8,128)S(1)}, f32[256,256]{1,0:T(8,128)S(1)}, u32[]{:S(2)}, u32[]{:S(2)}) %collective-permute-start.33) | collective-permute-done | bytes 262176 | tf_op jit(solution)/shard_map/ppermute | solution.py:65
  155.1 1.1 collective-permute-start.36
  156.2 1.7 collective-permute-start.37
  159.6 4.1 %collective-permute-done.36.refs_2_ = f32[128,256]{1,0:T(8,128)S(1)} collective-permute-done((f32[128,256]{1,0:T(8,128)S(1)}, f32[128,256]{1,0:T(8,128)S(1)}, u32[]{:S(2)}, u32[]{:S(2)}) %collective-permute-start.36) | collective-permute-done | bytes 131104 | tf_op jit(solution)/shard_map/ppermute | solution.py:65
  163.6 1.1 collective-permute-start.42
  164.8 1.6 collective-permute-done.37.refs_4_
  166.4 6.2 %collective-permute-done.42.refs_12_ = f32[2,64,512]{2,1,0:T(8,128)S(1)} collective-permute-done((f32[2,64,512]{2,1,0:T(8,128)S(1)}, f32[2,64,512]{2,1,0:T(8,128)S(1)}, u32[]{:S(2)}, u32[]{:S(2)}) %collective-permute-start.42) | collective-permute-done | bytes 262176 | tf_op jit(solution)/shard_map/ppermute | solution.py:65
  174.7 1.8 collective-permute-start.47
  176.5 2.8 %collective-permute-start.44 = (f32[256,256]{1,0:T(8,128)S(1)}, f32[256,256]{1,0:T(8,128)S(1)}, u32[]{:S(2)}, u32[]{:S(2)}) collective-permute-start(f32[256,256]{1,0:T(8,128)S(1)} %get-tuple-element.202), channel_id=1, source_target_pairs={{0,2},{1,3},{2,0},{3,1},{4,6},{5,7},{6,4},{7,5},{8,10},{9,11},{10,... | collective-permute-start | bytes 786440 | tf_op jit(solution)/shard_map/ppermute | solution.py:65
  179.2 4.2 %collective-permute-done.43.refs_2_ = f32[128,256]{1,0:T(8,128)S(1)} collective-permute-done((f32[128,256]{1,0:T(8,128)S(1)}, f32[128,256]{1,0:T(8,128)S(1)}, u32[]{:S(2)}, u32[]{:S(2)}) %collective-permute-start.43) | collective-permute-done | bytes 131104 | tf_op jit(solution)/shard_map/ppermute | solution.py:65
  183.6 5.6 %collective-permute-done.48.refs_10_ = f32[2,32,512]{2,1,0:T(8,128)S(1)} collective-permute-done((f32[2,32,512]{2,1,0:T(8,128)S(1)}, f32[2,32,512]{2,1,0:T(8,128)S(1)}, u32[]{:S(2)}, u32[]{:S(2)}) %collective-permute-start.48) | collective-permute-done | bytes 131104 | tf_op jit(solution)/shard_map/ppermute | solution.py:65
  189.2 2.8 %collective-permute-done.46.refs_7_ = f32[3,64,512]{2,1,0:T(8,128)S(1)} collective-permute-done((f32[3,64,512]{2,1,0:T(8,128)S(1)}, f32[3,64,512]{2,1,0:T(8,128)S(1)}, u32[]{:S(2)}, u32[]{:S(2)}) %collective-permute-start.46) | collective-permute-done | bytes 393248 | tf_op jit(solution)/shard_map/ppermute | solution.py:65
  192.3 3.0 %collective-permute-start.49 = (f32[128,256]{1,0:T(8,128)S(1)}, f32[128,256]{1,0:T(8,128)S(1)}, u32[]{:S(2)}, u32[]{:S(2)}) collective-permute-start(f32[128,256]{1,0:T(8,128)S(1)} %get-tuple-element.211), channel_id=1, source_target_pairs={{0,4},{1,5},{2,6},{3,7},{4,0},{5,1},{6,2},{7,3},{8,12},{9,13},{10,... | collective-permute-start | bytes 393224 | tf_op jit(solution)/shard_map/ppermute | solution.py:65
  195.3 8.6 %collective-permute-done.51.refs_6_ = f32[2,16,512]{2,1,0:T(8,128)S(1)} collective-permute-done((f32[2,16,512]{2,1,0:T(8,128)S(1)}, f32[2,16,512]{2,1,0:T(8,128)S(1)}, u32[]{:S(2)}, u32[]{:S(2)}) %collective-permute-start.51) | collective-permute-done | bytes 65568 | tf_op jit(solution)/shard_map/ppermute | solution.py:65
  204.9 1.5 shard_map.124.refs_3_
  206.4 3.1 %collective-permute-done.52.refs_2_ = f32[3,16,512]{2,1,0:T(8,128)S(1)} collective-permute-done((f32[3,16,512]{2,1,0:T(8,128)S(1)}, f32[3,16,512]{2,1,0:T(8,128)S(1)}, u32[]{:S(2)}, u32[]{:S(2)}) %collective-permute-start.52) | collective-permute-done | bytes 98336 | tf_op jit(solution)/shard_map/ppermute | solution.py:65
  209.5 1.1 copy-done.10
  210.7 1.1 collective-permute-start.53
  212.8 1.4 collective-permute-start.55
  214.2 1.3 collective-permute-start.57
  215.5 1.2 collective-permute-start.58
  216.8 2.3 %collective-permute-done.57.refs_9_ = f32[2,16,512]{2,1,0:T(8,128)S(1)} collective-permute-done((f32[2,16,512]{2,1,0:T(8,128)S(1)}, f32[2,16,512]{2,1,0:T(8,128)S(1)}, u32[]{:S(2)}, u32[]{:S(2)}) %collective-permute-start.57) | collective-permute-done | bytes 65568 | tf_op jit(solution)/shard_map/ppermute | solution.py:65
  219.1 1.6 collective-permute-done.58.refs_10_
  (187 shorter events, 38.4 us)
Async XLA Ops:
  2.2 12.5 %copy-start.40 = (s32[8]{0:T(128)S(1)}, s32[8]{0:T(128)}, u32[]{:S(2)}) copy-start(s32[8]{0:T(128)} %constant.99.clone) | copy-start | bytes 100
  6.6 34.8 %collective-permute-start = (f32[256,256]{1,0:T(8,128)}, f32[256,256]{1,0:T(8,128)}, u32[]{:S(2)}, u32[]{:S(2)}) collective-permute-start(f32[256,256]{1,0:T(8,128)} %get-tuple-element.123.refs_3_), channel_id=1, source_target_pairs={{0,8},{8,24},{24,16},{16,0},{1,9},{9,25},{25,17},{17,1},{10,2},{2,... | collective-permute-start | bytes 786440 | tf_op jit(solution)/shard_map/ppermute | solution.py:401
  9.6 31.8 %collective-permute-start.1 = (f32[256,256]{1,0:T(8,128)}, f32[256,256]{1,0:T(8,128)}, u32[]{:S(2)}, u32[]{:S(2)}) collective-permute-start(f32[256,256]{1,0:T(8,128)} %get-tuple-element.124.refs_7_), channel_id=1, source_target_pairs={{8,0},{24,8},{16,24},{0,16},{9,1},{25,9},{17,25},{1,17},{2,10},{18... | collective-permute-start | bytes 786440 | tf_op jit(solution)/shard_map/ppermute | solution.py:401
  9.7 15.7 %collective-permute-start.2 = (f32[256,256]{1,0:T(8,128)}, f32[256,256]{1,0:T(8,128)}, u32[]{:S(2)}, u32[]{:S(2)}) collective-permute-start(f32[256,256]{1,0:T(8,128)} %get-tuple-element.113.refs_2_.refs_3_), channel_id=1, source_target_pairs={{0,8},{8,24},{24,16},{16,0},{1,9},{9,25},{25,17},{17,1},{10,2},{2,... | collective-permute-start | bytes 786440 | tf_op jit(solution)/shard_map/ppermute | solution.py:401
  11.6 13.7 %collective-permute-start.3 = (f32[256,256]{1,0:T(8,128)}, f32[256,256]{1,0:T(8,128)}, u32[]{:S(2)}, u32[]{:S(2)}) collective-permute-start(f32[256,256]{1,0:T(8,128)} %get-tuple-element.127.refs_7_), channel_id=1, source_target_pairs={{8,0},{24,8},{16,24},{0,16},{9,1},{25,9},{17,25},{1,17},{2,10},{18... | collective-permute-start | bytes 786440 | tf_op jit(solution)/shard_map/ppermute | solution.py:401
  11.7 14.1 %collective-permute-start.4 = (f32[1,2,64,512]{3,2,1,0:T(8,128)}, f32[1,2,64,512]{3,2,1,0:T(8,128)}, u32[]{:S(2)}, u32[]{:S(2)}) collective-permute-start(f32[1,2,64,512]{3,2,1,0:T(8,128)} %bitcast.4.refs_5_), channel_id=1, source_target_pairs={{0,4},{1,5},{2,6},{3,7},{4,0},{5,1},{6,2},{7,3},{8,12},{9,13},{10,... | collective-permute-start | bytes 786440 | tf_op jit(solution)/shard_map/ppermute | solution.py:65
  31.3 15.6 %collective-permute-start.9 = (f32[2,2,64,512]{3,2,1,0:T(8,128)}, f32[2,2,64,512]{3,2,1,0:T(8,128)}, u32[]{:S(2)}, u32[]{:S(2)}) collective-permute-start(f32[2,2,64,512]{3,2,1,0:T(8,128)} %get-tuple-element.135.refs_5_), channel_id=1, source_target_pairs={{0,2},{1,3},{2,0},{3,1},{4,6},{5,7},{6,4},{7,5},{8,10},{9,11},{10,... | collective-permute-start | bytes 1572872 | tf_op jit(solution)/shard_map/ppermute | solution.py:65
  32.9 14.0 %collective-permute-start.7 = (f32[256,256]{1,0:T(8,128)}, f32[256,256]{1,0:T(8,128)S(1)}, u32[]{:S(2)}, u32[]{:S(2)}) collective-permute-start(f32[256,256]{1,0:T(8,128)} %copy-done.21), channel_id=1, source_target_pairs={{0,8},{8,24},{24,16},{16,0},{1,9},{9,25},{25,17},{17,1},{10,2},{2,... | collective-permute-start | bytes 786440 | tf_op jit(solution)/shard_map/ppermute | solution.py:401
  34.5 12.4 %collective-permute-start.8 = (f32[256,256]{1,0:T(8,128)}, f32[256,256]{1,0:T(8,128)S(1)}, u32[]{:S(2)}, u32[]{:S(2)}) collective-permute-start(f32[256,256]{1,0:T(8,128)} %copy-done.28), channel_id=1, source_target_pairs={{8,0},{24,8},{16,24},{0,16},{9,1},{25,9},{17,25},{1,17},{2,10},{18... | collective-permute-start | bytes 786440 | tf_op jit(solution)/shard_map/ppermute | solution.py:401
  50.8 11.0 %collective-permute-start.10 = (f32[4,2,64,512]{3,2,1,0:T(8,128)}, f32[4,2,64,512]{3,2,1,0:T(8,128)}, u32[]{:S(2)}, u32[]{:S(2)}) collective-permute-start(f32[4,2,64,512]{3,2,1,0:T(8,128)} %get-tuple-element.137.refs_5_), channel_id=1, source_target_pairs={{0,1},{1,0},{2,3},{3,2},{4,5},{5,4},{6,7},{7,6},{8,9},{9,8},{10,11... | collective-permute-start | bytes 3145736 | tf_op jit(solution)/shard_map/ppermute | solution.py:65
  50.9 9.5 %collective-permute-start.5 = (f32[256,256]{1,0:T(8,128)}, f32[256,256]{1,0:T(8,128)}, u32[]{:S(2)}, u32[]{:S(2)}) collective-permute-start(f32[256,256]{1,0:T(8,128)} %get-tuple-element.130.refs_3_), channel_id=1, source_target_pairs={{0,8},{8,24},{24,16},{16,0},{1,9},{9,25},{25,17},{17,1},{10,2},{2,... | collective-permute-start | bytes 786440 | tf_op jit(solution)/shard_map/ppermute | solution.py:401
  52.4 9.5 %collective-permute-start.6 = (f32[256,256]{1,0:T(8,128)}, f32[256,256]{1,0:T(8,128)}, u32[]{:S(2)}, u32[]{:S(2)}) collective-permute-start(f32[256,256]{1,0:T(8,128)} %get-tuple-element.131.refs_7_), channel_id=1, source_target_pairs={{8,0},{24,8},{16,24},{0,16},{9,1},{25,9},{17,25},{1,17},{2,10},{18... | collective-permute-start | bytes 786440 | tf_op jit(solution)/shard_map/ppermute | solution.py:401
  52.9 18.8 %collective-permute-start.11 = (f32[256,256]{1,0:T(8,128)}, f32[256,256]{1,0:T(8,128)}, u32[]{:S(2)}, u32[]{:S(2)}) collective-permute-start(f32[256,256]{1,0:T(8,128)} %get-tuple-element.138.refs_7_.refs_3_), channel_id=1, source_target_pairs={{0,8},{8,24},{24,16},{16,0},{1,9},{9,25},{25,17},{17,1},{10,2},{2,... | collective-permute-start | bytes 786440 | tf_op jit(solution)/shard_map/ppermute | solution.py:401
  54.4 17.3 %collective-permute-start.12 = (f32[256,256]{1,0:T(8,128)}, f32[256,256]{1,0:T(8,128)}, u32[]{:S(2)}, u32[]{:S(2)}) collective-permute-start(f32[256,256]{1,0:T(8,128)} %get-tuple-element.144.refs_7_), channel_id=1, source_target_pairs={{8,0},{24,8},{16,24},{0,16},{9,1},{25,9},{17,25},{1,17},{2,10},{18... | collective-permute-start | bytes 786440 | tf_op jit(solution)/shard_map/ppermute | solution.py:401
  55.0 12.3 %copy-start.16 = (f32[3,64,512]{2,1,0:T(8,128)S(1)}, f32[3,64,512]{2,1,0:T(8,128)}, u32[]{:S(2)}) copy-start(f32[3,64,512]{2,1,0:T(8,128)} %refs_1_.9) | copy-start | bytes 1179652
  65.7 9.1 %collective-permute-start.14 = (f32[256,256]{1,0:T(8,128)S(1)}, f32[256,256]{1,0:T(8,128)S(1)}, u32[]{:S(2)}, u32[]{:S(2)}) collective-permute-start(f32[256,256]{1,0:T(8,128)S(1)} %get-tuple-element.140.refs_7_.refs_3_), channel_id=1, source_target_pairs={{0,8},{8,24},{24,16},{16,0},{1,9},{9,25},{25,17},{17,1},{10,2},{2,... | collective-permute-start | bytes 786440 | tf_op jit(solution)/shard_map/ppermute | solution.py:401
  71.8 11.1 %copy-start.26 = (f32[256,256]{1,0:T(8,128)S(1)}, f32[256,256]{1,0:T(8,128)}, u32[]{:S(2)}) copy-start(f32[256,256]{1,0:T(8,128)} %get-tuple-element.123.refs_3_) | copy-start | bytes 786436
  74.1 13.4 %collective-permute-start.13 = (f32[512,256]{1,0:T(8,128)S(1)}, f32[512,256]{1,0:T(8,128)S(1)}, u32[]{:S(2)}, u32[]{:S(2)}) collective-permute-start(f32[512,256]{1,0:T(8,128)S(1)} %get-tuple-element.146), channel_id=1, source_target_pairs={{0,1},{1,0},{2,3},{3,2},{4,5},{5,4},{6,7},{7,6},{8,9},{9,8},{10,11... | collective-permute-start | bytes 1572872 | tf_op jit(solution)/shard_map/ppermute | solution.py:65
  74.2 8.7 %collective-permute-start.15 = (f32[256,256]{1,0:T(8,128)S(1)}, f32[256,256]{1,0:T(8,128)S(1)}, u32[]{:S(2)}, u32[]{:S(2)}) collective-permute-start(f32[256,256]{1,0:T(8,128)S(1)} %get-tuple-element.147.refs_7_), channel_id=1, source_target_pairs={{8,0},{24,8},{16,24},{0,16},{9,1},{25,9},{17,25},{1,17},{2,10},{18... | collective-permute-start | bytes 786440 | tf_op jit(solution)/shard_map/ppermute | solution.py:401
  82.9 12.0 %copy-start.23 = (f32[256,256]{1,0:T(8,128)S(1)}, f32[256,256]{1,0:T(8,128)}, u32[]{:S(2)}) copy-start(f32[256,256]{1,0:T(8,128)} %copy-done.21) | copy-start | bytes 786436
  82.9 12.0 %copy-start.29 = (f32[256,256]{1,0:T(8,128)S(1)}, f32[256,256]{1,0:T(8,128)}, u32[]{:S(2)}) copy-start(f32[256,256]{1,0:T(8,128)} %copy-done.28) | copy-start | bytes 786436
  85.2 14.1 %collective-permute-start.17 = (f32[512,256]{1,0:T(8,128)S(1)}, f32[512,256]{1,0:T(8,128)S(1)}, u32[]{:S(2)}, u32[]{:S(2)}) collective-permute-start(f32[512,256]{1,0:T(8,128)S(1)} %get-tuple-element.151), channel_id=1, source_target_pairs={{0,1},{1,0},{2,3},{3,2},{4,5},{5,4},{6,7},{7,6},{8,9},{9,8},{10,11... | collective-permute-start | bytes 1572872 | tf_op jit(solution)/shard_map/ppermute | solution.py:65
  85.3 9.6 %collective-permute-start.18 = (f32[256,256]{1,0:T(8,128)}, f32[256,256]{1,0:T(8,128)S(1)}, u32[]{:S(2)}, u32[]{:S(2)}) collective-permute-start(f32[256,256]{1,0:T(8,128)} %collective-permute-done.11.refs_6_.refs_5_.refs_4_), channel_id=1, source_target_pairs={{0,8},{8,24},{24,16},{16,0},{1,9},{9,25},{25,17},{17,1},{10,2},{2,... | collective-permute-start | bytes 786440 | tf_op jit(solution)/shard_map/ppermute | solution.py:401
  86.1 8.8 %collective-permute-start.19 = (f32[256,256]{1,0:T(8,128)}, f32[256,256]{1,0:T(8,128)S(1)}, u32[]{:S(2)}, u32[]{:S(2)}) collective-permute-start(f32[256,256]{1,0:T(8,128)} %collective-permute-done.12.refs_10_.refs_9_.refs_8_), channel_id=1, source_target_pairs={{8,0},{24,8},{16,24},{0,16},{9,1},{25,9},{17,25},{1,17},{2,10},{18... | collective-permute-start | bytes 786440 | tf_op jit(solution)/shard_map/ppermute | solution.py:401
  87.6 11.7 %collective-permute-start.16 = (f32[256,256]{1,0:T(8,128)S(1)}, f32[256,256]{1,0:T(8,128)S(1)}, u32[]{:S(2)}, u32[]{:S(2)}) collective-permute-start(f32[256,256]{1,0:T(8,128)S(1)} %get-tuple-element.150), channel_id=1, source_target_pairs={{0,2},{1,3},{2,0},{3,1},{4,6},{5,7},{6,4},{7,5},{8,10},{9,11},{10,... | collective-permute-start | bytes 786440 | tf_op jit(solution)/shard_map/ppermute | solution.py:65
  88.7 13.9 %collective-permute-start.23 = (f32[256,256]{1,0:T(8,128)S(1)}, f32[256,256]{1,0:T(8,128)S(1)}, u32[]{:S(2)}, u32[]{:S(2)}) collective-permute-start(f32[256,256]{1,0:T(8,128)S(1)} %collective-permute-done.14.refs_6_.refs_5_.refs_4_), channel_id=1, source_target_pairs={{0,8},{8,24},{24,16},{16,0},{1,9},{9,25},{25,17},{17,1},{10,2},{2,... | collective-permute-start | bytes 786440 | tf_op jit(solution)/shard_map/ppermute | solution.py:401
  97.1 16.2 %collective-permute-start.22 = (f32[512,256]{1,0:T(8,128)S(1)}, f32[512,256]{1,0:T(8,128)S(1)}, u32[]{:S(2)}, u32[]{:S(2)}) collective-permute-start(f32[512,256]{1,0:T(8,128)S(1)} %get-tuple-element.154.refs_3_), channel_id=1, source_target_pairs={{0,1},{1,0},{2,3},{3,2},{4,5},{5,4},{6,7},{7,6},{8,9},{9,8},{10,11... | collective-permute-start | bytes 1572872 | tf_op jit(solution)/shard_map/ppermute | solution.py:65
  97.2 8.7 %collective-permute-start.24 = (f32[256,256]{1,0:T(8,128)S(1)}, f32[256,256]{1,0:T(8,128)S(1)}, u32[]{:S(2)}, u32[]{:S(2)}) collective-permute-start(f32[256,256]{1,0:T(8,128)S(1)} %collective-permute-done.15.refs_10_.refs_9_.refs_8_), channel_id=1, source_target_pairs={{8,0},{24,8},{16,24},{0,16},{9,1},{25,9},{17,25},{1,17},{2,10},{18... | collective-permute-start | bytes 786440 | tf_op jit(solution)/shard_map/ppermute | solution.py:401
  99.4 9.8 %collective-permute-start.20 = (f32[128,256]{1,0:T(8,128)S(1)}, f32[128,256]{1,0:T(8,128)S(1)}, u32[]{:S(2)}, u32[]{:S(2)}) collective-permute-start(f32[128,256]{1,0:T(8,128)S(1)} %get-tuple-element.156), channel_id=1, source_target_pairs={{0,4},{1,5},{2,6},{3,7},{4,0},{5,1},{6,2},{7,3},{8,12},{9,13},{10,... | collective-permute-start | bytes 393224 | tf_op jit(solution)/shard_map/ppermute | solution.py:65
  102.5 10.8 %collective-permute-start.21 = (f32[256,256]{1,0:T(8,128)S(1)}, f32[256,256]{1,0:T(8,128)S(1)}, u32[]{:S(2)}, u32[]{:S(2)}) collective-permute-start(f32[256,256]{1,0:T(8,128)S(1)} %get-tuple-element.158), channel_id=1, source_target_pairs={{0,2},{1,3},{2,0},{3,1},{4,6},{5,7},{6,4},{7,5},{8,10},{9,11},{10,... | collective-permute-start | bytes 786440 | tf_op jit(solution)/shard_map/ppermute | solution.py:65
  108.2 18.7 %collective-permute-start.27 = (f32[512,256]{1,0:T(8,128)S(1)}, f32[512,256]{1,0:T(8,128)S(1)}, u32[]{:S(2)}, u32[]{:S(2)}) collective-permute-start(f32[512,256]{1,0:T(8,128)S(1)} %get-tuple-element.160.refs_3_), channel_id=1, source_target_pairs={{0,1},{1,0},{2,3},{3,2},{4,5},{5,4},{6,7},{7,6},{8,9},{9,8},{10,11... | collective-permute-start | bytes 1572872 | tf_op jit(solution)/shard_map/ppermute | solution.py:65
  108.2 9.2 %collective-permute-start.28 = (f32[256,256]{1,0:T(8,128)S(1)}, f32[256,256]{1,0:T(8,128)S(1)}, u32[]{:S(2)}, u32[]{:S(2)}) collective-permute-start(f32[256,256]{1,0:T(8,128)S(1)} %collective-permute-done.18.refs_6_.refs_5_), channel_id=1, source_target_pairs={{0,8},{8,24},{24,16},{16,0},{1,9},{9,25},{25,17},{17,1},{10,2},{2,... | collective-permute-start | bytes 786440 | tf_op jit(solution)/shard_map/ppermute | solution.py:401
  109.3 9.2 %collective-permute-start.29 = (f32[256,256]{1,0:T(8,128)S(1)}, f32[256,256]{1,0:T(8,128)S(1)}, u32[]{:S(2)}, u32[]{:S(2)}) collective-permute-start(f32[256,256]{1,0:T(8,128)S(1)} %collective-permute-done.19.refs_10_.refs_9_), channel_id=1, source_target_pairs={{8,0},{24,8},{16,24},{0,16},{9,1},{25,9},{17,25},{1,17},{2,10},{18... | collective-permute-start | bytes 786440 | tf_op jit(solution)/shard_map/ppermute | solution.py:401
  113.4 13.5 %collective-permute-start.26 = (f32[256,256]{1,0:T(8,128)S(1)}, f32[256,256]{1,0:T(8,128)S(1)}, u32[]{:S(2)}, u32[]{:S(2)}) collective-permute-start(f32[256,256]{1,0:T(8,128)S(1)} %get-tuple-element.165), channel_id=1, source_target_pairs={{0,2},{1,3},{2,0},{3,1},{4,6},{5,7},{6,4},{7,5},{8,10},{9,11},{10,... | collective-permute-start | bytes 786440 | tf_op jit(solution)/shard_map/ppermute | solution.py:65
  113.9 13.1 %collective-permute-start.30 = (f32[256,256]{1,0:T(8,128)S(1)}, f32[256,256]{1,0:T(8,128)S(1)}, u32[]{:S(2)}, u32[]{:S(2)}) collective-permute-start(f32[256,256]{1,0:T(8,128)S(1)} %collective-permute-done.23.refs_6_.refs_5_), channel_id=1, source_target_pairs={{0,8},{8,24},{24,16},{16,0},{1,9},{9,25},{25,17},{17,1},{10,2},{2,... | collective-permute-start | bytes 786440 | tf_op jit(solution)/shard_map/ppermute | solution.py:401
  117.4 9.6 %collective-permute-start.31 = (f32[256,256]{1,0:T(8,128)S(1)}, f32[256,256]{1,0:T(8,128)S(1)}, u32[]{:S(2)}, u32[]{:S(2)}) collective-permute-start(f32[256,256]{1,0:T(8,128)S(1)} %collective-permute-done.24.refs_10_.refs_9_), channel_id=1, source_target_pairs={{8,0},{24,8},{16,24},{0,16},{9,1},{25,9},{17,25},{1,17},{2,10},{18... | collective-permute-start | bytes 786440 | tf_op jit(solution)/shard_map/ppermute | solution.py:401
  118.5 8.4 %collective-permute-start.25 = (f32[128,256]{1,0:T(8,128)S(1)}, f32[128,256]{1,0:T(8,128)S(1)}, u32[]{:S(2)}, u32[]{:S(2)}) collective-permute-start(f32[128,256]{1,0:T(8,128)S(1)} %get-tuple-element.163), channel_id=1, source_target_pairs={{0,4},{1,5},{2,6},{3,7},{4,0},{5,1},{6,2},{7,3},{8,12},{9,13},{10,... | collective-permute-start | bytes 393224 | tf_op jit(solution)/shard_map/ppermute | solution.py:65
  134.1 38.5 %collective-permute-start.39 = (f32[3,256,512]{2,1,0:T(8,128)S(1)}, f32[3,256,512]{2,1,0:T(8,128)S(1)}, u32[]{:S(2)}, u32[]{:S(2)}) collective-permute-start(f32[3,256,512]{2,1,0:T(8,128)S(1)} %get-tuple-element.193), channel_id=1, source_target_pairs={{0,1},{1,0},{2,3},{3,2},{4,5},{5,4},{6,7},{7,6},{8,9},{9,8},{10,11... | collective-permute-start | bytes 4718600 | tf_op jit(solution)/shard_map/ppermute | solution.py:65
  136.9 18.0 %collective-permute-start.35 = (f32[2,256,512]{2,1,0:T(8,128)S(1)}, f32[2,256,512]{2,1,0:T(8,128)S(1)}, u32[]{:S(2)}, u32[]{:S(2)}) collective-permute-start(f32[2,256,512]{2,1,0:T(8,128)S(1)} %get-tuple-element.186), channel_id=1, source_target_pairs={{0,1},{1,0},{2,3},{3,2},{4,5},{5,4},{6,7},{7,6},{8,9},{9,8},{10,11... | collective-permute-start | bytes 3145736 | tf_op jit(solution)/shard_map/ppermute | solution.py:65
  137.5 17.4 %collective-permute-start.34 = (f32[512,256]{1,0:T(8,128)S(1)}, f32[512,256]{1,0:T(8,128)S(1)}, u32[]{:S(2)}, u32[]{:S(2)}) collective-permute-start(f32[512,256]{1,0:T(8,128)S(1)} %get-tuple-element.168.refs_3_), channel_id=1, source_target_pairs={{0,1},{1,0},{2,3},{3,2},{4,5},{5,4},{6,7},{7,6},{8,9},{9,8},{10,11... | collective-permute-start | bytes 1572872 | tf_op jit(solution)/shard_map/ppermute | solution.py:65
  137.5 9.0 %collective-permute-start.32 = (f32[128,256]{1,0:T(8,128)S(1)}, f32[128,256]{1,0:T(8,128)S(1)}, u32[]{:S(2)}, u32[]{:S(2)}) collective-permute-start(f32[128,256]{1,0:T(8,128)S(1)} %get-tuple-element.175), channel_id=1, source_target_pairs={{0,4},{1,5},{2,6},{3,7},{4,0},{5,1},{6,2},{7,3},{8,12},{9,13},{10,... | collective-permute-start | bytes 393224 | tf_op jit(solution)/shard_map/ppermute | solution.py:65
  138.3 20.7 %collective-permute-start.38 = (f32[512,256]{1,0:T(8,128)S(1)}, f32[512,256]{1,0:T(8,128)S(1)}, u32[]{:S(2)}, u32[]{:S(2)}) collective-permute-start(f32[512,256]{1,0:T(8,128)S(1)} %get-tuple-element.171.refs_3_), channel_id=1, source_target_pairs={{0,1},{1,0},{2,3},{3,2},{4,5},{5,4},{6,7},{7,6},{8,9},{9,8},{10,11... | collective-permute-start | bytes 1572872 | tf_op jit(solution)/shard_map/ppermute | solution.py:65
  146.6 8.3 %collective-permute-start.33 = (f32[256,256]{1,0:T(8,128)S(1)}, f32[256,256]{1,0:T(8,128)S(1)}, u32[]{:S(2)}, u32[]{:S(2)}) collective-permute-start(f32[256,256]{1,0:T(8,128)S(1)} %get-tuple-element.177), channel_id=1, source_target_pairs={{0,2},{1,3},{2,0},{3,1},{4,6},{5,7},{6,4},{7,5},{8,10},{9,11},{10,... | collective-permute-start | bytes 786440 | tf_op jit(solution)/shard_map/ppermute | solution.py:65
  155.1 8.5 %collective-permute-start.36 = (f32[128,256]{1,0:T(8,128)S(1)}, f32[128,256]{1,0:T(8,128)S(1)}, u32[]{:S(2)}, u32[]{:S(2)}) collective-permute-start(f32[128,256]{1,0:T(8,128)S(1)} %get-tuple-element.189), channel_id=1, source_target_pairs={{0,4},{1,5},{2,6},{3,7},{4,0},{5,1},{6,2},{7,3},{8,12},{9,13},{10,... | collective-permute-start | bytes 393224 | tf_op jit(solution)/shard_map/ppermute | solution.py:65
  156.2 10.1 %collective-permute-start.37 = (f32[256,256]{1,0:T(8,128)S(1)}, f32[256,256]{1,0:T(8,128)S(1)}, u32[]{:S(2)}, u32[]{:S(2)}) collective-permute-start(f32[256,256]{1,0:T(8,128)S(1)} %get-tuple-element.191), channel_id=1, source_target_pairs={{0,2},{1,3},{2,0},{3,1},{4,6},{5,7},{6,4},{7,5},{8,10},{9,11},{10,... | collective-permute-start | bytes 786440 | tf_op jit(solution)/shard_map/ppermute | solution.py:65
  158.0 8.4 %collective-permute-start.40 = (f32[2,64,512]{2,1,0:T(8,128)S(1)}, f32[2,64,512]{2,1,0:T(8,128)S(1)}, u32[]{:S(2)}, u32[]{:S(2)}) collective-permute-start(f32[2,64,512]{2,1,0:T(8,128)S(1)} %get-tuple-element.195), channel_id=1, source_target_pairs={{0,8},{8,0},{16,24},{24,16},{1,9},{9,1},{17,25},{25,17},{2,10},{10... | collective-permute-start | bytes 786440 | tf_op jit(solution)/shard_map/ppermute | solution.py:65
  159.1 7.3 %collective-permute-start.41 = (f32[2,64,512]{2,1,0:T(8,128)S(1)}, f32[2,64,512]{2,1,0:T(8,128)S(1)}, u32[]{:S(2)}, u32[]{:S(2)}) collective-permute-start(f32[2,64,512]{2,1,0:T(8,128)S(1)} %get-tuple-element.196), channel_id=1, source_target_pairs={{0,16},{8,24},{16,0},{24,8},{1,17},{9,25},{17,1},{25,9},{2,18},{10... | collective-permute-start | bytes 786440 | tf_op jit(solution)/shard_map/ppermute | solution.py:65
  163.6 8.9 %collective-permute-start.42 = (f32[2,64,512]{2,1,0:T(8,128)S(1)}, f32[2,64,512]{2,1,0:T(8,128)S(1)}, u32[]{:S(2)}, u32[]{:S(2)}) collective-permute-start(f32[2,64,512]{2,1,0:T(8,128)S(1)} %get-tuple-element.197), channel_id=1, source_target_pairs={{0,24},{8,16},{16,8},{24,0},{1,25},{9,17},{17,9},{25,1},{2,26},{10... | collective-permute-start | bytes 786440 | tf_op jit(solution)/shard_map/ppermute | solution.py:65
  172.9 16.3 %collective-permute-start.45 = (f32[3,64,512]{2,1,0:T(8,128)S(1)}, f32[3,64,512]{2,1,0:T(8,128)S(1)}, u32[]{:S(2)}, u32[]{:S(2)}) collective-permute-start(f32[3,64,512]{2,1,0:T(8,128)S(1)} %get-tuple-element.204), channel_id=1, source_target_pairs={{0,8},{8,0},{16,24},{24,16},{1,9},{9,1},{17,25},{25,17},{2,10},{10... | collective-permute-start | bytes 1179656 | tf_op jit(solution)/shard_map/ppermute | solution.py:65
  173.9 18.1 %collective-permute-start.46 = (f32[3,64,512]{2,1,0:T(8,128)S(1)}, f32[3,64,512]{2,1,0:T(8,128)S(1)}, u32[]{:S(2)}, u32[]{:S(2)}) collective-permute-start(f32[3,64,512]{2,1,0:T(8,128)S(1)} %get-tuple-element.205), channel_id=1, source_target_pairs={{0,16},{8,24},{16,0},{24,8},{1,17},{9,25},{17,1},{25,9},{2,18},{10... | collective-permute-start | bytes 1179656 | tf_op jit(solution)/shard_map/ppermute | solution.py:65
  174.7 17.3 %collective-permute-start.47 = (f32[3,64,512]{2,1,0:T(8,128)S(1)}, f32[3,64,512]{2,1,0:T(8,128)S(1)}, u32[]{:S(2)}, u32[]{:S(2)}) collective-permute-start(f32[3,64,512]{2,1,0:T(8,128)S(1)} %get-tuple-element.206), channel_id=1, source_target_pairs={{0,24},{8,16},{16,8},{24,0},{1,25},{9,17},{17,9},{25,1},{2,26},{10... | collective-permute-start | bytes 1179656 | tf_op jit(solution)/shard_map/ppermute | solution.py:65
  176.5 7.0 %collective-permute-start.43 = (f32[128,256]{1,0:T(8,128)S(1)}, f32[128,256]{1,0:T(8,128)S(1)}, u32[]{:S(2)}, u32[]{:S(2)}) collective-permute-start(f32[128,256]{1,0:T(8,128)S(1)} %get-tuple-element.200), channel_id=1, source_target_pairs={{0,4},{1,5},{2,6},{3,7},{4,0},{5,1},{6,2},{7,3},{8,12},{9,13},{10,... | collective-permute-start | bytes 393224 | tf_op jit(solution)/shard_map/ppermute | solution.py:65
  176.5 12.7 %collective-permute-start.44 = (f32[256,256]{1,0:T(8,128)S(1)}, f32[256,256]{1,0:T(8,128)S(1)}, u32[]{:S(2)}, u32[]{:S(2)}) collective-permute-start(f32[256,256]{1,0:T(8,128)S(1)} %get-tuple-element.202), channel_id=1, source_target_pairs={{0,2},{1,3},{2,0},{3,1},{4,6},{5,7},{6,4},{7,5},{8,10},{9,11},{10,... | collective-permute-start | bytes 786440 | tf_op jit(solution)/shard_map/ppermute | solution.py:65
  183.4 5.7 %collective-permute-start.48 = (f32[2,32,512]{2,1,0:T(8,128)S(1)}, f32[2,32,512]{2,1,0:T(8,128)S(1)}, u32[]{:S(2)}, u32[]{:S(2)}) collective-permute-start(f32[2,32,512]{2,1,0:T(8,128)S(1)} %get-tuple-element.208), channel_id=1, source_target_pairs={{0,2},{1,3},{2,0},{3,1},{4,6},{5,7},{6,4},{7,5},{8,10},{9,11},{10,... | collective-permute-start | bytes 393224 | tf_op jit(solution)/shard_map/ppermute | solution.py:65
  192.2 11.7 %collective-permute-start.50 = (f32[3,32,512]{2,1,0:T(8,128)S(1)}, f32[3,32,512]{2,1,0:T(8,128)S(1)}, u32[]{:S(2)}, u32[]{:S(2)}) collective-permute-start(f32[3,32,512]{2,1,0:T(8,128)S(1)} %get-tuple-element.213), channel_id=1, source_target_pairs={{0,2},{1,3},{2,0},{3,1},{4,6},{5,7},{6,4},{7,5},{8,10},{9,11},{10,... | collective-permute-start | bytes 589832 | tf_op jit(solution)/shard_map/ppermute | solution.py:65
  192.3 11.7 %collective-permute-start.49 = (f32[128,256]{1,0:T(8,128)S(1)}, f32[128,256]{1,0:T(8,128)S(1)}, u32[]{:S(2)}, u32[]{:S(2)}) collective-permute-start(f32[128,256]{1,0:T(8,128)S(1)} %get-tuple-element.211), channel_id=1, source_target_pairs={{0,4},{1,5},{2,6},{3,7},{4,0},{5,1},{6,2},{7,3},{8,12},{9,13},{10,... | collective-permute-start | bytes 393224 | tf_op jit(solution)/shard_map/ppermute | solution.py:65
  195.2 8.7 %collective-permute-start.51 = (f32[2,16,512]{2,1,0:T(8,128)S(1)}, f32[2,16,512]{2,1,0:T(8,128)S(1)}, u32[]{:S(2)}, u32[]{:S(2)}) collective-permute-start(f32[2,16,512]{2,1,0:T(8,128)S(1)} %get-tuple-element.215), channel_id=1, source_target_pairs={{0,4},{1,5},{2,6},{3,7},{4,0},{5,1},{6,2},{7,3},{8,12},{9,13},{10,... | collective-permute-start | bytes 196616 | tf_op jit(solution)/shard_map/ppermute | solution.py:65
  204.0 5.6 %collective-permute-start.52 = (f32[3,16,512]{2,1,0:T(8,128)S(1)}, f32[3,16,512]{2,1,0:T(8,128)S(1)}, u32[]{:S(2)}, u32[]{:S(2)}) collective-permute-start(f32[3,16,512]{2,1,0:T(8,128)S(1)} %get-tuple-element.219), channel_id=1, source_target_pairs={{0,4},{1,5},{2,6},{3,7},{4,0},{5,1},{6,2},{7,3},{8,12},{9,13},{10,... | collective-permute-start | bytes 294920 | tf_op jit(solution)/shard_map/ppermute | solution.py:65
  204.0 11.5 %collective-permute-start.56 = (f32[2,16,512]{2,1,0:T(8,128)S(1)}, f32[2,16,512]{2,1,0:T(8,128)S(1)}, u32[]{:S(2)}, u32[]{:S(2)}) collective-permute-start(f32[2,16,512]{2,1,0:T(8,128)S(1)} %get-tuple-element.220.refs_7_), channel_id=1, source_target_pairs={{0,8},{8,0},{16,24},{24,16},{1,9},{9,1},{17,25},{25,17},{2,10},{10... | collective-permute-start | bytes 196616 | tf_op jit(solution)/shard_map/ppermute | solution.py:65
  210.7 10.0 %collective-permute-start.53 = (f32[3,16,512]{2,1,0:T(8,128)S(1)}, f32[3,16,512]{2,1,0:T(8,128)S(1)}, u32[]{:S(2)}, u32[]{:S(2)}) collective-permute-start(f32[3,16,512]{2,1,0:T(8,128)S(1)} %shard_map.125.refs_3_.refs_11_), channel_id=1, source_target_pairs={{0,8},{8,0},{16,24},{24,16},{1,9},{9,1},{17,25},{25,17},{2,10},{10... | collective-permute-start | bytes 294920 | tf_op jit(solution)/shard_map/ppermute | solution.py:65
  211.8 8.9 %collective-permute-start.54 = (f32[3,16,512]{2,1,0:T(8,128)S(1)}, f32[3,16,512]{2,1,0:T(8,128)S(1)}, u32[]{:S(2)}, u32[]{:S(2)}) collective-permute-start(f32[3,16,512]{2,1,0:T(8,128)S(1)} %shard_map.125.refs_3_.refs_11_), channel_id=1, source_target_pairs={{0,16},{8,24},{16,0},{24,8},{1,17},{9,25},{17,1},{25,9},{2,18},{10... | collective-permute-start | bytes 294920 | tf_op jit(solution)/shard_map/ppermute | solution.py:65
  212.8 7.9 %collective-permute-start.55 = (f32[3,16,512]{2,1,0:T(8,128)S(1)}, f32[3,16,512]{2,1,0:T(8,128)S(1)}, u32[]{:S(2)}, u32[]{:S(2)}) collective-permute-start(f32[3,16,512]{2,1,0:T(8,128)S(1)} %shard_map.125.refs_3_.refs_11_), channel_id=1, source_target_pairs={{0,24},{8,16},{16,8},{24,0},{1,25},{9,17},{17,9},{25,1},{2,26},{10... | collective-permute-start | bytes 294920 | tf_op jit(solution)/shard_map/ppermute | solution.py:65
  214.2 4.8 %collective-permute-start.57 = (f32[2,16,512]{2,1,0:T(8,128)S(1)}, f32[2,16,512]{2,1,0:T(8,128)S(1)}, u32[]{:S(2)}, u32[]{:S(2)}) collective-permute-start(f32[2,16,512]{2,1,0:T(8,128)S(1)} %get-tuple-element.220.refs_7_), channel_id=1, source_target_pairs={{0,16},{8,24},{16,0},{24,8},{1,17},{9,25},{17,1},{25,9},{2,18},{10... | collective-permute-start | bytes 196616 | tf_op jit(solution)/shard_map/ppermute | solution.py:65
  215.5 5.2 %collective-permute-start.58 = (f32[2,16,512]{2,1,0:T(8,128)S(1)}, f32[2,16,512]{2,1,0:T(8,128)S(1)}, u32[]{:S(2)}, u32[]{:S(2)}) collective-permute-start(f32[2,16,512]{2,1,0:T(8,128)S(1)} %get-tuple-element.220.refs_7_), channel_id=1, source_target_pairs={{0,24},{8,16},{16,8},{24,0},{1,25},{9,17},{17,9},{25,1},{2,26},{10... | collective-permute-start | bytes 196616 | tf_op jit(solution)/shard_map/ppermute | solution.py:65
  (36 other events, 88.9 us)

commit v6 on v5

--- a/solution.py
+++ b/solution.py
@@ -90,21 +90,21 @@
     return list(results)
 
 
-def cut_kernel(members, lanes, info_ref, factors_ref, *refs):
+def cut_kernel(cuts, info_ref, factors_ref, *refs):
     *outs, sems = refs
     half, unit = outs[0].shape
     first = pl.multiple_of(info_ref[0] * (2 * half), 2 * half)
     copies = []
     for at, out_ref in enumerate(outs):
-        member, lane, way = at // (2 * lanes), at // 2 % lanes, at % 2
+        member, cut, way = at // (2 * cuts), at // 2 % cuts, at % 2
         source = factors_ref.at[
-            member, pl.ds(first + way * half, half), lane * unit : (lane + 1) * unit
+            member, pl.ds(first + way * half, half), cut * unit : (cut + 1) * unit
         ]
         copies.append(pltpu.make_async_copy(source, out_ref, sems.at[at]))
         copies[-1].start()
     for at, out_ref in enumerate(outs):
         copies[at].wait()
-        out_ref[...] = out_ref[...] * info_ref[1 + at // (2 * lanes)].astype(F32)
+        out_ref[...] = out_ref[...] * info_ref[1 + at // (2 * cuts)].astype(F32)
 
 
 def fetch_groups(order_ref, source_ref, target_ref, sems, groups):
@@ -181,19 +181,22 @@
         corner_ref[c] = share * product(turn(chooser, split(slices_ref[c])), split(framed))
 
 
-def unit_kernel(count, place_ref, high_ref, low_ref, *refs):
+def unit_kernel(count, cuts, place_ref, high_ref, low_ref, *refs):
     keep_ref, send_ref = refs[-2:]
     middle = keep_ref.shape[0]
-    chosen = []
-    for way in range(2):
-        candidates = refs[way * count :][:count]
-        value = candidates[0][...]
-        for at in range(1, count):
-            value = jnp.where(place_ref[way] == at, candidates[at][...], value)
-        chosen.append(value)
-    right = split(jnp.concatenate(chosen))
-    send_ref[...] = product((high_ref[middle:], low_ref[middle:]), right)
-    keep_ref[...] = product((high_ref[:middle], low_ref[:middle]), right)
+    for cut in range(cuts):
+        chosen = []
+        for way in range(2):
+            candidates = refs[(2 * cut + way) * count :][:count]
+            value = candidates[0][...]
+            for at in range(1, count):
+                value = jnp.where(place_ref[way] == at, candidates[at][...], value)
+            chosen.append(value)
+        right = split(jnp.concatenate(chosen))
+        unit = right[0].shape[1]
+        columns = slice(cut * unit, (cut + 1) * unit)
+        send_ref[:, columns] = product((high_ref[middle:], low_ref[middle:]), right)
+        keep_ref[:, columns] = product((high_ref[:middle], low_ref[:middle]), right)
 
 
 def unit_gram_kernel(high_ref, low_ref, keep_ref, send_ref, out_ref):
@@ -211,12 +214,11 @@
 
 def parent_kernel(
     children, weight_ref, chooser_ref, own_high_ref, own_low_ref, own_thigh_ref, own_tlow_ref,
-    link_high_ref, link_low_ref, left_ref, right_ref,
+    link_high_ref, link_low_ref, sum_ref,
     col_ref, turned_ref, high_ref, low_ref, thigh_ref, tlow_ref, keep_ref, send_ref,
 ):
     chooser = chooser_ref[...]
-    column = -jnp.concatenate([left_ref[...], right_ref[...]], axis=1)
-    column = column * weight_ref[0].astype(F32)
+    column = -sum_ref[...] * weight_ref[0].astype(F32)
     col_ref[...] = column
     pair = split(column)
     turned_pair = turn(chooser, pair)
@@ -235,14 +237,13 @@
 
 
 def child_kernel(
-    children, lanes, own_high_ref, own_low_ref, own_thigh_ref, own_tlow_ref,
+    children, own_high_ref, own_low_ref, own_thigh_ref, own_tlow_ref,
     high_ref, low_ref, thigh_ref, tlow_ref, lift_high_ref, lift_low_ref, corner_ref, *refs
 ):
     keep_ref, send_ref = refs[-2:]
     for c in range(children):
-        grams = [ref[...] for ref in refs[c * lanes : (c + 1) * lanes]]
         turned = pair_of(high_ref, low_ref, c)
-        total = corner_ref[c] + jnp.concatenate(grams, axis=1)
+        total = corner_ref[c] + refs[c][...]
         total += product(pair_of(own_thigh_ref, own_tlow_ref, c + 1), turned)
         total += product(
             pair_of(thigh_ref, tlow_ref, c), pair_of(own_high_ref, own_low_ref, c + 1)
@@ -251,12 +252,11 @@
         store_halves(keep_ref, send_ref, c, total)
 
 
-def column_kernel(children, lanes, weight_ref, col_ref, turned_ref, *refs):
+def column_kernel(children, weight_ref, col_ref, turned_ref, *refs):
     out_ref = refs[-1]
     out_ref[0] = col_ref[...]
     for c in range(children):
-        total = jnp.concatenate([ref[...] for ref in refs[c * lanes : (c + 1) * lanes]], axis=1)
-        out_ref[c + 1] = -(total + turned_ref[c]) * weight_ref[c + 1].astype(F32)
+        out_ref[c + 1] = -(refs[c][...] + turned_ref[c]) * weight_ref[c + 1].astype(F32)
 
 
 def finish_kernel(rows, place_ref, diag_ref, framed_ref, *refs):
@@ -324,8 +324,9 @@
     part = diag_width // row_count
     first_row = row_place * rows_here
     source = col_place // ratio
-    lanes = 2
-    unit = width // lanes
+    cuts = 2
+    unit = width // cuts
+    chunk_count = members * cuts
     half = cols_here // 2
 
     def ring(forward):
@@ -344,15 +345,13 @@
         [(col_place % ratio)[None], listed[:, col_place * cols_here // width]]
     ).astype(jnp.int32)
     flat = call(
-        functools.partial(cut_kernel, members, lanes),
-        [shape(half, unit)] * (members * lanes * 2),
+        functools.partial(cut_kernel, cuts),
+        [shape(half, unit)] * (chunk_count * 2),
         [column_info, factor_cols],
-        smem=1, hbm=1, vmem=56,
-        scratch=[pltpu.SemaphoreType.DMA((members * lanes * 2,))],
+        smem=1, hbm=1, vmem=48,
+        scratch=[pltpu.SemaphoreType.DMA((chunk_count * 2,))],
     )
-    chunks = [
-        [flat[(j * lanes + lane) * 2 :][:2] for lane in range(lanes)] for j in range(members)
-    ]
+    chunks = [flat[at * 2 :][:2] for at in range(chunk_count)]
 
     source_flag = (row_place == source).astype(jnp.int32)[None]
     forward_place = row_place ^ source
@@ -375,35 +374,27 @@
 
     last = [flat[0]]
     held = {}
-    moved = [[] for _ in range(lanes)]
-    received = [[] for _ in range(lanes)]
+    moved = []
+    received = []
+    stages = chunk_count + row_count - 2
 
     def heavy(body, outs, args, **options):
         results = call(body, outs, args, after=last[0], **options)
         last[0] = results[0]
         return results
 
-    def ring_flow(lane):
-        for _ in range(lane):
-            yield WAIT
-        stages = members + row_count - 2
+    def ring_flow():
         for stage in range(stages):
-            arrived = received[lane][-1] if stage else None
             if stage == 0:
-                moving = chunks[0][lane]
-            elif stage < members:
-                moving = yield (select_step, chunks[stage][lane] + arrived, [shape(half, unit)] * 2)
+                moving = chunks[0]
+            elif stage < chunk_count:
+                wish = (select_step, chunks[stage] + received[-1], [shape(half, unit)] * 2)
+                moving = yield wish
             else:
+                moving = received[-1]
                 yield WAIT
-                moving = arrived
-            moved[lane].append(moving)
-            received[lane].append(
-                [lax.ppermute(moving[way], AXES, rings[way]) for way in range(2)]
-            )
-            for _ in range(lanes - 1):
-                yield WAIT
-            if stage > row_count - 3:
-                held["ready", stage - row_count + 2, lane] = True
+            moved.append(moving)
+            received.append([lax.ppermute(moving[way], AXES, rings[way]) for way in range(2)])
 
     def link_flow():
         gathered = parent_factor[None]
@@ -457,34 +448,45 @@
                 ],
             )
 
-    def unit_flow(member, lane):
-        while ("ready", member, lane) not in held:
+    def unit_flow(member):
+        chunk = (member + 1) * cuts - 1
+        while len(received) < chunk + row_count - 1:
             yield WAIT
         candidates = []
-        for way in range(2):
-            candidates.append(moved[lane][member][way])
-            candidates += [received[lane][member + at][way] for at in range(row_count - 1)]
+        for at in range(member * cuts, (member + 1) * cuts):
+            for way in range(2):
+                candidates.append(moved[at][way])
+                candidates += [received[at + hop][way] for hop in range(row_count - 1)]
         size = rows_here // 2
         keep, send = heavy(
-            functools.partial(unit_kernel, row_count),
-            [shape(size, unit)] * 2,
+            functools.partial(unit_kernel, row_count, cuts),
+            [shape(size, width)] * 2,
             [places, *held["region"], *candidates],
-            smem=1, vmem=12,
+            smem=1, vmem=16,
         )
         arrived = swap(send, "col", col_count, 1)
         if member:
-            held["gram", member, lane] = heavy(
+            held["gram", member] = heavy(
                 unit_gram_kernel,
-                [shape(width, unit)],
+                [shape(width, width)],
                 [*held["turned", member], keep, send],
-                vmem=12,
+                vmem=16,
             )[0]
-        yield WAIT
+        size //= 2
+        keep, send = heavy(
+            functools.partial(step_kernel, [(halve_step, 2, 2)]),
+            [shape(size, width)] * 2,
+            [source_flag, keep, arrived],
+            smem=1,
+        )
         for bit in range(1, col_bits):
-            size //= 2
-            keep, send = yield (halve_step, [keep, arrived], [shape(size, unit)] * 2)
             arrived = swap(send, "col", col_count, 1 << bit)
-        held["sum", member, lane] = (yield (halve_step, [keep, arrived], [shape(size, unit)]))[0]
+            if len(received) < stages:
+                yield WAIT
+            if bit + 1 < col_bits:
+                size //= 2
+                keep, send = yield (halve_step, [keep, arrived], [shape(size, width)] * 2)
+        held["sum", member] = (yield (halve_step, [keep, arrived], [shape(size, width)]))[0]
 
     def total_flow(keep, send):
         count = keep.shape[0]
@@ -501,7 +503,7 @@
         return [piece] + [swap(piece, "row", row_count, d) for d in range(1, row_count)]
 
     def parent_flow():
-        names = [("sum", 0, lane) for lane in range(lanes)] + ["links"]
+        names = [("sum", 0), "links"]
         while any(name not in held for name in names):
             yield WAIT
         col, turned, *pairs, keep, send = heavy(
@@ -510,20 +512,18 @@
             + [shape(children, group, width, dtype=BF16)] * 2
             + [shape(children, width, group, dtype=BF16)] * 2
             + [shape(members, width // 2, width)] * 2,
-            [own_weights, chooser, *held["own"], *held["links"][:2]]
-            + [held["sum", 0, lane] for lane in range(lanes)],
+            [own_weights, chooser, *held["own"], *held["links"][:2], held["sum", 0]],
             smem=1, vmem=20,
         )
         held["parent"] = (col, turned, pairs)
-        yield WAIT
         held["parent totals"] = yield from total_flow(keep, send)
 
     def child_flow():
-        names = [("gram", 1 + c, lane) for c in range(children) for lane in range(lanes)]
+        names = [("gram", 1 + c) for c in range(children)]
         while any(name not in held for name in names + ["parent"]):
             yield WAIT
         keep, send = heavy(
-            functools.partial(child_kernel, children, lanes),
+            functools.partial(child_kernel, children),
             [shape(children, width // 2, width)] * 2,
             [*held["own"], *held["parent"][2], *held["links"][2:4], held["links"][5]]
             + [held[name] for name in names],
@@ -532,19 +532,19 @@
         held["child totals"] = yield from total_flow(keep, send)
 
     def column_flow():
-        names = [("sum", 1 + c, lane) for c in range(children) for lane in range(lanes)]
+        names = [("sum", 1 + c) for c in range(children)]
         while any(name not in held for name in names + ["parent"]):
             yield WAIT
         col, turned, _ = held["parent"]
         held["columns"] = heavy(
-            functools.partial(column_kernel, children, lanes),
+            functools.partial(column_kernel, children),
             [shape(members, group, width)],
             [own_weights, col, turned] + [held[name] for name in names],
             smem=1,
         )[0]
 
-    flows = [ring_flow(lane) for lane in range(lanes)] + [link_flow(), prepare_flow()]
-    flows += [unit_flow(j, lane) for j in range(members) for lane in range(lanes)]
+    flows = [ring_flow(), link_flow(), prepare_flow()]
+    flows += [unit_flow(member) for member in range(members)]
     flows += [parent_flow(), child_flow(), column_flow()]
     waiting = [(flow, None) for flow in flows]
     while waiting:

time: 223 us -> 221 us (level)
  waiting for transfers between devices: 88.3 us -> 101 us
  Pallas kernels: 53.3 us -> 41.3 us
  starting transfers between devices: 56.5 us -> 53.9 us
    ppermute x39 -> x30, waiting for transfers between devices: 61.4 us -> 83.4 us  [swap(): lax.ppermute(value, axis, [(place, place ^ change) for place in range(siz...]
    pallas_call x33 -> x28, Pallas kernels: 53.3 us -> 41.3 us  [call(): pl.pallas_call(inner, out_shape=outs, in_specs=[pl.BlockSpec(memory_space...]
    ppermute x20 -> x16, waiting for transfers between devices: 26.9 us -> 17.5 us  [ring_flow(): lax.ppermute(moving[way], AXES, rings[way])]
    ppermute x20 -> x16, starting transfers between devices: 20.6 us -> 17.2 us  [ring_flow(): lax.ppermute(moving[way], AXES, rings[way])]
    unnamed x83 -> x111, local copies, waits for them, and re-layouts: 19.2 us -> 20.3 us
    ppermute x39 -> x30, starting transfers between devices: 35.9 us -> 36.7 us  [swap(): lax.ppermute(value, axis, [(place, place ^ change) for place in range(siz...]
  transfers between devices with their start and end apart: 59 -> 46, of which waited for: 22 -> 24; matrix products, arithmetic and copies ran while one was open for 1% -> 1% of each run, Pallas kernels for 17% -> 10%
where the time goes in v6:
time: 221 us; the launch traced here: 220 us
  waiting for transfers between devices  101 us (46%)
  starting transfers between devices  53.9 us (24%)
  Pallas kernels  41.3 us (19%)
  local copies, waits for them, and re-layouts  22.2 us (10%)
    ppermute x30, waiting for transfers between devices, swap(): lax.ppermute(value, axis, [(place, place ^ change) for place in range(siz...  83.4 us
    pallas_call x28, Pallas kernels, call(): pl.pallas_call(inner, out_shape=outs, in_specs=[pl.BlockSpec(memory_space...  41.3 us
    ppermute x30, starting transfers between devices, swap(): lax.ppermute(value, axis, [(place, place ^ change) for place in range(siz...  36.7 us
    unnamed x111, local copies, waits for them, and re-layouts  20.3 us
    ppermute x16, waiting for transfers between devices, ring_flow(): lax.ppermute(moving[way], AXES, rings[way])  17.5 us
    ppermute x16, starting transfers between devices, ring_flow(): lax.ppermute(moving[way], AXES, rings[way])  17.2 us
  transfers between devices with their start and end apart: 46, of which 24 were waited for; matrix products, arithmetic and copies ran while one was open for 1% of the time, Pallas kernels for 10%

profile of v6, /device:TPU:0, one launch (start us, length us, event | category | flops | bytes accessed | tf_op | source)
XLA Modules:
  0.0 220.5 jit_solution(8675242222921457190)
XLA Ops:
  1.7 3.2 %shard_map.94 = (f32[256,256]{1,0:T(8,128)S(1)}, f32[256,256]{1,0:T(8,128)}, f32[256,256]{1,0:T(8,128)S(1)}, f32[256,256]{1,0:T(8,128)S(1)}, f32[256,256]{1,0:T(...) custom-call(s32[4]{0:T(128)S(1)} %pad_add_fusion.1.info_ref, ...), custom_call_target="tpu_custom_call" | custom-call | flops 1024 | bytes 1024 | tf_op jit(solution)/shard_map/pallas_call | solution.py:81
  11.9 2.9 %collective-permute-start = (f32[256,256]{1,0:T(8,128)S(1)}, f32[256,256]{1,0:T(8,128)}, u32[]{:S(2)}, u32[]{:S(2)}) collective-permute-start(f32[256,256]{1,0:T(8,128)S(1)} %get-tuple-element.97.refs_2_.refs_3_), channel_id=1, source_target_pairs={{0,8},{8,24},{24,16},{16,0},{1,9},{9,25},{25,17},{17,1},{10,2},{2,... | collective-permute-start | bytes 786440 | tf_op jit(solution)/shard_map/ppermute | solution.py:397
  14.9 3.1 %collective-permute-start.4 = (f32[1,2,64,512]{3,2,1,0:T(8,128)}, f32[1,2,64,512]{3,2,1,0:T(8,128)}, u32[]{:S(2)}, u32[]{:S(2)}) collective-permute-start(f32[1,2,64,512]{3,2,1,0:T(8,128)} %bitcast.3.refs_5_), channel_id=1, source_target_pairs={{0,4},{1,5},{2,6},{3,7},{4,0},{5,1},{6,2},{7,3},{8,12},{9,13},{10,... | collective-permute-start | bytes 786440 | tf_op jit(solution)/shard_map/ppermute | solution.py:65
  18.2 1.6 copy-done.13
  19.8 1.1 shard_map.95
  24.9 1.9 shard_map.96
  26.8 1.5 collective-permute-start.2
  29.8 2.8 %copy-done = f32[3,1024,512]{2,1,0:T(8,128)S(1)} copy-done((f32[3,1024,512]{2,1,0:T(8,128)S(1)}, f32[3,1024,512]{2,1,0:T(8,128)}, u32[]{:S(2)}) %copy-start) | copy-done | bytes 6291480
  32.6 2.0 shard_map.97
  35.2 1.2 shard_map.98
  37.2 1.4 collective-permute-start.5
  39.7 2.3 %shard_map.99 = (bf16[512,1024]{1,0:T(8,128)(2,1)S(1)}, bf16[512,1024]{1,0:T(8,128)(2,1)S(1)}) custom-call(s32[16]{0:T(128)S(1)} %get-tuple-element.194.refs_0_, f32[3,1024,512]{2,1,0:T(8,128)S(1)} %bitcast.10, bf16[512,512]{1,0:T(8,128)(2,1)S(1)} %fusion.refs_2_.refs_4_.refs_1_, f32[256,256]{1,0:T(8,128)S(1)} %get-tuple-element.114.refs_3_), custom_call_target="tpu_custom_call" | custom-call | flops 1024 | bytes 1024 | tf_op jit(solution)/shard_map/pallas_call | solution.py:81
  42.0 1.6 collective-permute-done.5.refs_3_.refs_6_.refs_13_.refs_4_
  43.6 1.4 collective-permute-done.6.refs_4_.refs_10_.refs_17_.refs_8_
  46.8 1.3 collective-permute-start.8
  48.1 2.8 %copy-done.1 = f32[3,1024,512]{2,1,0:T(8,128)S(1)} copy-done((f32[3,1024,512]{2,1,0:T(8,128)S(1)}, f32[3,1024,512]{2,1,0:T(8,128)}, u32[]{:S(2)}) %copy-start.1) | copy-done | bytes 6291480
  50.9 2.3 %shard_map.101 = (bf16[512,1024]{1,0:T(8,128)(2,1)S(1)}, bf16[512,1024]{1,0:T(8,128)(2,1)S(1)}) custom-call(s32[16]{0:T(128)S(1)} %get-tuple-element.193.refs_0_, f32[3,1024,512]{2,1,0:T(8,128)S(1)} %copy-done.1, bf16[512,512]{1,0:T(8,128)(2,1)S(1)} %fusion.refs_2_.refs_4_.refs_1_, f32[256,256]{1,0:T(8,128)S(1)} %get-tuple-element.117.refs_3_.refs_11_), custom_call_target="tpu_custom_call" | custom-call | flops 1024 | bytes 1024 | tf_op jit(solution)/shard_map/pallas_call | solution.py:81
  53.3 3.4 %shard_map.102 = (f32[512,512]{1,0:T(8,128)S(1)}, f32[512,512]{1,0:T(8,128)S(1)}) custom-call(s32[2]{0:T(128)S(1)} %pad_add_fusion.3.refs_0_, bf16[1024,512]{1,0:T(8,128)(2,1)S(1)} %copy-done.3, bf16[1024,512]{1,0:T(8,128)(2,1)S(1)} %copy-done.5, f32[256,256]{1,0:T(8,128)S(1)} %copy-done.24, f32[256,256]{1,0:T(8,128)} %collective-permute-done.refs_3_.refs_4_, ...), custom_call_target="tpu_custom_call" | custom-call | flops 1024 | bytes 1024 | tf_op jit(solution)/shard_map/pallas_call | solution.py:81
  56.8 1.6 collective-permute-start.9
  58.4 1.0 collective-permute-done.10.refs_2_
  59.5 11.6 %collective-permute-done.9.refs_6_ = f32[2,2,64,512]{3,2,1,0:T(8,128)S(1)} collective-permute-done((f32[2,2,64,512]{3,2,1,0:T(8,128)S(1)}, f32[2,2,64,512]{3,2,1,0:T(8,128)S(1)}, u32[]{:S(2)}, u32[]{:S(2)}) %collective-permute-start.9) | collective-permute-done | bytes 524320 | tf_op jit(solution)/shard_map/ppermute | solution.py:65
  71.3 1.6 collective-permute-start.14
  72.9 1.2 collective-permute-start.11
  75.0 6.3 %collective-permute-done.11.refs_3_.refs_6_.refs_13_.refs_4_ = f32[256,256]{1,0:T(8,128)S(1)} collective-permute-done((f32[256,256]{1,0:T(8,128)S(1)}, f32[256,256]{1,0:T(8,128)S(1)}, u32[]{:S(2)}, u32[]{:S(2)}) %collective-permute-start.11) | collective-permute-done | bytes 262176 | tf_op jit(solution)/shard_map/ppermute | solution.py:397
  82.2 3.4 %collective-permute-done.14.refs_8_ = f32[256,512]{1,0:T(8,128)S(1)} collective-permute-done((f32[256,512]{1,0:T(8,128)S(1)}, f32[256,512]{1,0:T(8,128)S(1)}, u32[]{:S(2)}, u32[]{:S(2)}) %collective-permute-start.14) | collective-permute-done | bytes 524320 | tf_op jit(solution)/shard_map/ppermute | solution.py:65
  85.9 1.1 collective-permute-start.16
  87.0 1.0 collective-permute-start.17
  88.1 4.5 %shard_map.106 = (bf16[2,512,512]{2,1,0:T(8,128)(2,1)S(1)}, bf16[2,512,512]{2,1,0:T(8,128)(2,1)S(1)}, bf16[2,512,128]{2,1,0:T(8,128)(2,1)S(1)}, bf16[2,512,128]{...) custom-call(s32[8]{0:T(128)S(1)} %iota_xor_fusion.refs_0_, ...), custom_call_target="tpu_custom_call" | custom-call | flops 1024 | bytes 1024 | tf_op jit(solution)/shard_map/pallas_call | solution.py:81
  92.5 1.3 collective-permute-done.16.refs_14_.refs_5_.refs_12_
  94.6 2.5 %shard_map.107 = (f32[512,512]{1,0:T(8,128)S(1)}, f32[512,512]{1,0:T(8,128)S(1)}) custom-call(s32[2]{0:T(128)S(1)} %pad_add_fusion.3.refs_0_, bf16[1024,512]{1,0:T(8,128)(2,1)S(1)} %copy-done.3, bf16[1024,512]{1,0:T(8,128)(2,1)S(1)} %copy-done.5, f32[256,256]{1,0:T(8,128)S(1)} %copy-done.22, ...), custom_call_target="tpu_custom_call" | custom-call | flops 1024 | bytes 1024 | tf_op jit(solution)/shard_map/pallas_call | solution.py:81
  97.2 1.8 shard_map.108.refs_3_.refs_11_
  99.9 1.4 collective-permute-start.19
  101.3 1.3 collective-permute-start.20
  103.4 2.4 %collective-permute-start.15 = (f32[128,512]{1,0:T(8,128)S(1)}, f32[128,512]{1,0:T(8,128)S(1)}, u32[]{:S(2)}, u32[]{:S(2)}) collective-permute-start(f32[128,512]{1,0:T(8,128)S(1)} %get-tuple-element.134), channel_id=1, source_target_pairs={{0,4},{1,5},{2,6},{3,7},{4,0},{5,1},{6,2},{7,3},{8,12},{9,13},{10,... | collective-permute-start | bytes 786440 | tf_op jit(solution)/shard_map/ppermute | solution.py:65
  105.7 3.7 %collective-permute-done.20.refs_6_.refs_13_ = f32[256,256]{1,0:T(8,128)S(1)} collective-permute-done((f32[256,256]{1,0:T(8,128)S(1)}, f32[256,256]{1,0:T(8,128)S(1)}, u32[]{:S(2)}, u32[]{:S(2)}) %collective-permute-start.20) | collective-permute-done | bytes 262176 | tf_op jit(solution)/shard_map/ppermute | solution.py:397
  109.4 1.3 collective-permute-start.22
  111.4 7.0 %collective-permute-done.15.refs_2_ = f32[128,512]{1,0:T(8,128)S(1)} collective-permute-done((f32[128,512]{1,0:T(8,128)S(1)}, f32[128,512]{1,0:T(8,128)S(1)}, u32[]{:S(2)}, u32[]{:S(2)}) %collective-permute-start.15) | collective-permute-done | bytes 262176 | tf_op jit(solution)/shard_map/ppermute | solution.py:65
  118.4 1.1 collective-permute-done.19.refs_4_
  119.7 2.5 %shard_map.111 = (f32[512,512]{1,0:T(8,128)S(1)}, f32[512,512]{1,0:T(8,128)S(1)}) custom-call(s32[2]{0:T(128)S(1)} %pad_add_fusion.3.refs_0_, bf16[1024,512]{1,0:T(8,128)(2,1)S(1)} %copy-done.3, bf16[1024,512]{1,0:T(8,128)(2,1)S(1)} %copy-done.5, f32[256,256]{1,0:T(8,128)S(1)} %get-tuple-element.125.refs_9_.refs_3_, ...), custom_call_target="tpu_custom_call" | custom-call | flops 1024 | bytes 1024 | tf_op jit(solution)/shard_map/pallas_call | solution.py:81
  122.2 1.8 shard_map.112.refs_3_.refs_12_
  125.2 4.3 %shard_map.114 = (f32[128,512]{1,0:T(8,128)S(1)}, f32[2,128,512]{2,1,0:T(8,128)S(1)}, bf16[2,128,512]{2,1,0:T(8,128)(2,1)S(1)}, bf16[2,128,512]{2,1,0:T(8,128)(2...) custom-call(s32[3]{0:T(128)S(1)} %get-tuple-element.190.refs_0_, ...), custom_call_target="tpu_custom_call" | custom-call | flops 1024 | bytes 1024 | tf_op jit(solution)/shard_map/pallas_call | solution.py:81
  130.1 2.7 %shard_map.115 = (f32[2,256,512]{2,1,0:T(8,128)S(1)}, f32[2,256,512]{2,1,0:T(8,128)S(1)}) custom-call(bf16[3,128,512]{2,1,0:T(8,128)(2,1)S(1)} %get-tuple-element.101.refs_7_.refs_5_.refs_2_.refs_0_, bf16[3,128,512]{2,1,0:T(8,128)(2,1)S(1)} %copy-done.9, bf16[3,512,128]{2,1,0:T(8,128)(2,1)S(1)} %copy-done.16, bf16[3,512,128]{2,1,0:T(8,128)(2,1)S(1)} %copy-done.18, ...), custom_call_target="tpu_custom_call" | custom-call | flops 1024 | bytes 1024 | tf_op jit(solution)/shard_map/pallas_call | solution.py:81
  132.9 2.7 %collective-permute-start.26 = (f32[256,512]{1,0:T(8,128)S(1)}, f32[256,512]{1,0:T(8,128)S(1)}, u32[]{:S(2)}, u32[]{:S(2)}) collective-permute-start(f32[256,512]{1,0:T(8,128)S(1)} %get-tuple-element.150), channel_id=1, source_target_pairs={{0,2},{1,3},{2,0},{3,1},{4,6},{5,7},{6,4},{7,5},{8,10},{9,11},{10,... | collective-permute-start | bytes 1572872 | tf_op jit(solution)/shard_map/ppermute | solution.py:65
  135.6 1.1 collective-permute-start.25
  136.7 16.3 %collective-permute-done.25.refs_2_ = f32[128,512]{1,0:T(8,128)S(1)} collective-permute-done((f32[128,512]{1,0:T(8,128)S(1)}, f32[128,512]{1,0:T(8,128)S(1)}, u32[]{:S(2)}, u32[]{:S(2)}) %collective-permute-start.25) | collective-permute-done | bytes 262176 | tf_op jit(solution)/shard_map/ppermute | solution.py:65
  154.1 2.7 %collective-permute-start.29 = (f32[128,512]{1,0:T(8,128)S(1)}, f32[128,512]{1,0:T(8,128)S(1)}, u32[]{:S(2)}, u32[]{:S(2)}) collective-permute-start(f32[128,512]{1,0:T(8,128)S(1)} %get-tuple-element.164), channel_id=1, source_target_pairs={{0,4},{1,5},{2,6},{3,7},{4,0},{5,1},{6,2},{7,3},{8,12},{9,13},{10,... | collective-permute-start | bytes 786440 | tf_op jit(solution)/shard_map/ppermute | solution.py:65
  156.8 1.0 collective-permute-start.33
  157.9 1.0 collective-permute-start.30
  159.7 1.6 collective-permute-start.32
  161.4 7.4 %collective-permute-done.29.refs_2_ = f32[128,512]{1,0:T(8,128)S(1)} collective-permute-done((f32[128,512]{1,0:T(8,128)S(1)}, f32[128,512]{1,0:T(8,128)S(1)}, u32[]{:S(2)}, u32[]{:S(2)}) %collective-permute-start.29) | collective-permute-done | bytes 262176 | tf_op jit(solution)/shard_map/ppermute | solution.py:65
  169.6 1.6 collective-permute-start.35
  171.3 19.1 %collective-permute-done.34.refs_9_ = f32[2,64,512]{2,1,0:T(8,128)S(1)} collective-permute-done((f32[2,64,512]{2,1,0:T(8,128)S(1)}, f32[2,64,512]{2,1,0:T(8,128)S(1)}, u32[]{:S(2)}, u32[]{:S(2)}) %collective-permute-start.34) | collective-permute-done | bytes 262176 | tf_op jit(solution)/shard_map/ppermute | solution.py:65
  190.6 2.0 collective-permute-start.37
  192.6 1.5 shard_map.118.refs_5_
  194.1 4.9 %collective-permute-done.37.refs_4_ = f32[2,32,512]{2,1,0:T(8,128)S(1)} collective-permute-done((f32[2,32,512]{2,1,0:T(8,128)S(1)}, f32[2,32,512]{2,1,0:T(8,128)S(1)}, u32[]{:S(2)}, u32[]{:S(2)}) %collective-permute-start.37) | collective-permute-done | bytes 131104 | tf_op jit(solution)/shard_map/ppermute | solution.py:65
  199.0 1.1 copy-done.10
  200.9 2.3 %collective-permute-start.39 = (f32[2,16,512]{2,1,0:T(8,128)S(1)}, f32[2,16,512]{2,1,0:T(8,128)S(1)}, u32[]{:S(2)}, u32[]{:S(2)}) collective-permute-start(f32[2,16,512]{2,1,0:T(8,128)S(1)} %get-tuple-element.182), channel_id=1, source_target_pairs={{0,4},{1,5},{2,6},{3,7},{4,0},{5,1},{6,2},{7,3},{8,12},{9,13},{10,... | collective-permute-start | bytes 196616 | tf_op jit(solution)/shard_map/ppermute | solution.py:65
  203.2 5.5 %collective-permute-done.39.refs_4_ = f32[2,16,512]{2,1,0:T(8,128)S(1)} collective-permute-done((f32[2,16,512]{2,1,0:T(8,128)S(1)}, f32[2,16,512]{2,1,0:T(8,128)S(1)}, u32[]{:S(2)}, u32[]{:S(2)}) %collective-permute-start.39) | collective-permute-done | bytes 65568 | tf_op jit(solution)/shard_map/ppermute | solution.py:65
  208.8 2.0 collective-permute-start.40
  212.3 1.9 collective-permute-start.44
  214.3 1.5 collective-permute-start.45
  215.8 2.3 %collective-permute-done.44.refs_9_ = f32[2,16,512]{2,1,0:T(8,128)S(1)} collective-permute-done((f32[2,16,512]{2,1,0:T(8,128)S(1)}, f32[2,16,512]{2,1,0:T(8,128)S(1)}, u32[]{:S(2)}, u32[]{:S(2)}) %collective-permute-start.44) | collective-permute-done | bytes 65568 | tf_op jit(solution)/shard_map/ppermute | solution.py:65
  218.1 1.4 collective-permute-done.45.refs_10_
  219.5 1.0 shard_map.121
  (186 shorter events, 31.0 us)
Async XLA Ops:
  1.7 16.3 %copy-start.52 = (s32[8]{0:T(128)S(1)}, s32[8]{0:T(128)}, u32[]{:S(2)}) copy-start(s32[8]{0:T(128)} %constant.99.clone) | copy-start | bytes 100
  11.9 14.8 %copy-start.23 = (f32[256,256]{1,0:T(8,128)}, f32[256,256]{1,0:T(8,128)S(1)}, u32[]{:S(2)}) copy-start(f32[256,256]{1,0:T(8,128)S(1)} %get-tuple-element.97.refs_2_.refs_3_) | copy-start | bytes 786436
  11.9 10.1 %collective-permute-start = (f32[256,256]{1,0:T(8,128)S(1)}, f32[256,256]{1,0:T(8,128)}, u32[]{:S(2)}, u32[]{:S(2)}) collective-permute-start(f32[256,256]{1,0:T(8,128)S(1)} %get-tuple-element.97.refs_2_.refs_3_), channel_id=1, source_target_pairs={{0,8},{8,24},{24,16},{16,0},{1,9},{9,25},{25,17},{17,1},{10,2},{2,... | collective-permute-start | bytes 786440 | tf_op jit(solution)/shard_map/ppermute | solution.py:397
  14.9 8.1 %collective-permute-start.1 = (f32[256,256]{1,0:T(8,128)}, f32[256,256]{1,0:T(8,128)}, u32[]{:S(2)}, u32[]{:S(2)}) collective-permute-start(f32[256,256]{1,0:T(8,128)} %get-tuple-element.98.refs_7_), channel_id=1, source_target_pairs={{8,0},{24,8},{16,24},{0,16},{9,1},{25,9},{17,25},{1,17},{2,10},{18... | collective-permute-start | bytes 786440 | tf_op jit(solution)/shard_map/ppermute | solution.py:397
  14.9 19.7 %collective-permute-start.4 = (f32[1,2,64,512]{3,2,1,0:T(8,128)}, f32[1,2,64,512]{3,2,1,0:T(8,128)}, u32[]{:S(2)}, u32[]{:S(2)}) collective-permute-start(f32[1,2,64,512]{3,2,1,0:T(8,128)} %bitcast.3.refs_5_), channel_id=1, source_target_pairs={{0,4},{1,5},{2,6},{3,7},{4,0},{5,1},{6,2},{7,3},{8,12},{9,13},{10,... | collective-permute-start | bytes 786440 | tf_op jit(solution)/shard_map/ppermute | solution.py:65
  19.8 9.1 %copy-start.51 = (s32[3,8]{1,0:T(4,128)S(1)}, s32[3,8]{1,0:T(4,128)}, u32[]{:S(2)}) copy-start(s32[3,8]{1,0:T(4,128)} %param.11) | copy-start | bytes 292
  19.8 19.8 %slice-start = ((s8[6291456]{0:T(1024)(128)(4,1)}), s8[2097152]{0:T(1024)(128)(4,1)S(1)}, s32[]{:S(2)}) async-start(s8[6291456]{0:T(1024)(128)(4,1)} %bitcast.9), calls=%async_computation | async-start | bytes 4194304
  21.9 7.0 %copy-start.2 = (bf16[1024,512]{1,0:T(8,128)(2,1)}, bf16[1024,512]{1,0:T(8,128)(2,1)S(1)}, u32[]{:S(2)}) copy-start(bf16[1024,512]{1,0:T(8,128)(2,1)S(1)} %get-tuple-element.99.refs_5_.refs_1_) | copy-start | bytes 3145732
  26.8 7.8 %collective-permute-start.2 = (f32[256,256]{1,0:T(8,128)}, f32[256,256]{1,0:T(8,128)S(1)}, u32[]{:S(2)}, u32[]{:S(2)}) collective-permute-start(f32[256,256]{1,0:T(8,128)} %get-tuple-element.100.refs_3_.refs_11_), channel_id=1, source_target_pairs={{0,8},{8,24},{24,16},{16,0},{1,9},{9,25},{25,17},{17,1},{10,2},{2,... | collective-permute-start | bytes 786440 | tf_op jit(solution)/shard_map/ppermute | solution.py:397
  28.3 6.9 %collective-permute-start.3 = (f32[256,256]{1,0:T(8,128)}, f32[256,256]{1,0:T(8,128)}, u32[]{:S(2)}, u32[]{:S(2)}) collective-permute-start(f32[256,256]{1,0:T(8,128)} %get-tuple-element.113.refs_15_), channel_id=1, source_target_pairs={{8,0},{24,8},{16,24},{0,16},{9,1},{25,9},{17,25},{1,17},{2,10},{18... | collective-permute-start | bytes 786440 | tf_op jit(solution)/shard_map/ppermute | solution.py:397
  32.6 7.1 %slice-start.1 = ((s8[6291456]{0:T(1024)(128)(4,1)}), s8[4194304]{0:T(1024)(128)(4,1)S(1)}, s32[]{:S(2)}) async-start(s8[6291456]{0:T(1024)(128)(4,1)} %bitcast.9), calls=%async_computation.1 | async-start | bytes 8388608
  34.6 5.1 %copy-start.8 = (bf16[3,128,512]{2,1,0:T(8,128)(2,1)}, bf16[3,128,512]{2,1,0:T(8,128)(2,1)S(1)}, u32[]{:S(2)}) copy-start(bf16[3,128,512]{2,1,0:T(8,128)(2,1)S(1)} %get-tuple-element.102.refs_6_.refs_3_.refs_1_) | copy-start | bytes 1179652
  34.6 5.0 %copy-start.15 = (bf16[3,512,128]{2,1,0:T(8,128)(2,1)}, bf16[3,512,128]{2,1,0:T(8,128)(2,1)S(1)}, u32[]{:S(2)}) copy-start(bf16[3,512,128]{2,1,0:T(8,128)(2,1)S(1)} %get-tuple-element.103.refs_4_.refs_2_) | copy-start | bytes 1179652
  37.2 6.4 %collective-permute-start.5 = (f32[256,256]{1,0:T(8,128)S(1)}, f32[256,256]{1,0:T(8,128)S(1)}, u32[]{:S(2)}, u32[]{:S(2)}) collective-permute-start(f32[256,256]{1,0:T(8,128)S(1)} %get-tuple-element.114.refs_3_), channel_id=1, source_target_pairs={{0,8},{8,24},{24,16},{16,0},{1,9},{9,25},{25,17},{17,1},{10,2},{2,... | collective-permute-start | bytes 786440 | tf_op jit(solution)/shard_map/ppermute | solution.py:397
  38.6 6.4 %collective-permute-start.6 = (f32[256,256]{1,0:T(8,128)S(1)}, f32[256,256]{1,0:T(8,128)S(1)}, u32[]{:S(2)}, u32[]{:S(2)}) collective-permute-start(f32[256,256]{1,0:T(8,128)S(1)} %get-tuple-element.115.refs_7_), channel_id=1, source_target_pairs={{8,0},{24,8},{16,24},{0,16},{9,1},{25,9},{17,25},{1,17},{2,10},{18... | collective-permute-start | bytes 786440 | tf_op jit(solution)/shard_map/ppermute | solution.py:397
  39.7 5.3 %copy-start.32 = (f32[256,256]{1,0:T(8,128)S(1)}, f32[256,256]{1,0:T(8,128)}, u32[]{:S(2)}) copy-start(f32[256,256]{1,0:T(8,128)} %copy-done.31) | copy-start | bytes 786436
  39.7 5.3 %copy-start.34 = (f32[256,256]{1,0:T(8,128)S(1)}, f32[256,256]{1,0:T(8,128)}, u32[]{:S(2)}) copy-start(f32[256,256]{1,0:T(8,128)} %copy-done.33) | copy-start | bytes 786436
  46.0 7.2 %copy-start.49 = (f32[256,256]{1,0:T(8,128)}, f32[256,256]{1,0:T(8,128)S(1)}, u32[]{:S(2)}) copy-start(f32[256,256]{1,0:T(8,128)S(1)} %get-tuple-element.118.refs_15_) | copy-start | bytes 786436
  46.0 7.2 %collective-permute-start.7 = (f32[256,256]{1,0:T(8,128)S(1)}, f32[256,256]{1,0:T(8,128)S(1)}, u32[]{:S(2)}, u32[]{:S(2)}) collective-permute-start(f32[256,256]{1,0:T(8,128)S(1)} %get-tuple-element.117.refs_3_.refs_11_), channel_id=1, source_target_pairs={{0,8},{8,24},{24,16},{16,0},{1,9},{9,25},{25,17},{17,1},{10,2},{2,... | collective-permute-start | bytes 786440 | tf_op jit(solution)/shard_map/ppermute | solution.py:397
  46.8 6.4 %collective-permute-start.8 = (f32[256,256]{1,0:T(8,128)S(1)}, f32[256,256]{1,0:T(8,128)S(1)}, u32[]{:S(2)}, u32[]{:S(2)}) collective-permute-start(f32[256,256]{1,0:T(8,128)S(1)} %get-tuple-element.118.refs_15_), channel_id=1, source_target_pairs={{8,0},{24,8},{16,24},{0,16},{9,1},{25,9},{17,25},{1,17},{2,10},{18... | collective-permute-start | bytes 786440 | tf_op jit(solution)/shard_map/ppermute | solution.py:397
  56.6 14.4 %copy-start.44 = (f32[256,256]{1,0:T(8,128)S(1)}, f32[256,256]{1,0:T(8,128)}, u32[]{:S(2)}) copy-start(f32[256,256]{1,0:T(8,128)} %copy-done.43) | copy-start | bytes 786436
  56.7 14.4 %copy-start.46 = (f32[256,256]{1,0:T(8,128)S(1)}, f32[256,256]{1,0:T(8,128)}, u32[]{:S(2)}) copy-start(f32[256,256]{1,0:T(8,128)} %copy-done.45) | copy-start | bytes 786436
  56.7 2.7 %collective-permute-start.10 = (f32[512,512]{1,0:T(8,128)S(1)}, f32[512,512]{1,0:T(8,128)S(1)}, u32[]{:S(2)}, u32[]{:S(2)}) collective-permute-start(f32[512,512]{1,0:T(8,128)S(1)} %get-tuple-element.123), channel_id=1, source_target_pairs={{0,1},{1,0},{2,3},{3,2},{4,5},{5,4},{6,7},{7,6},{8,9},{9,8},{10,11... | collective-permute-start | bytes 3145736 | tf_op jit(solution)/shard_map/ppermute | solution.py:65
  56.8 14.3 %collective-permute-start.9 = (f32[2,2,64,512]{3,2,1,0:T(8,128)S(1)}, f32[2,2,64,512]{3,2,1,0:T(8,128)S(1)}, u32[]{:S(2)}, u32[]{:S(2)}) collective-permute-start(f32[2,2,64,512]{3,2,1,0:T(8,128)S(1)} %copy-done.26), channel_id=1, source_target_pairs={{0,2},{1,3},{2,0},{3,1},{4,6},{5,7},{6,4},{7,5},{8,10},{9,11},{10,... | collective-permute-start | bytes 1572872 | tf_op jit(solution)/shard_map/ppermute | solution.py:65
  59.5 26.1 %copy-start.28 = (f32[256,256]{1,0:T(8,128)S(1)}, f32[256,256]{1,0:T(8,128)}, u32[]{:S(2)}) copy-start(f32[256,256]{1,0:T(8,128)} %copy-done.27) | copy-start | bytes 786436
  59.5 26.1 %copy-start.30 = (f32[256,256]{1,0:T(8,128)S(1)}, f32[256,256]{1,0:T(8,128)}, u32[]{:S(2)}) copy-start(f32[256,256]{1,0:T(8,128)} %copy-done.29) | copy-start | bytes 786436
  71.2 14.4 %collective-permute-start.13 = (f32[4,2,64,512]{3,2,1,0:T(8,128)S(1)}, f32[4,2,64,512]{3,2,1,0:T(8,128)S(1)}, u32[]{:S(2)}, u32[]{:S(2)}) collective-permute-start(f32[4,2,64,512]{3,2,1,0:T(8,128)S(1)} %get-tuple-element.127.refs_5_), channel_id=1, source_target_pairs={{0,1},{1,0},{2,3},{3,2},{4,5},{5,4},{6,7},{7,6},{8,9},{9,8},{10,11... | collective-permute-start | bytes 3145736 | tf_op jit(solution)/shard_map/ppermute | solution.py:65
  71.3 14.3 %collective-permute-start.14 = (f32[256,512]{1,0:T(8,128)S(1)}, f32[256,512]{1,0:T(8,128)S(1)}, u32[]{:S(2)}, u32[]{:S(2)}) collective-permute-start(f32[256,512]{1,0:T(8,128)S(1)} %get-tuple-element.128), channel_id=1, source_target_pairs={{0,2},{1,3},{2,0},{3,1},{4,6},{5,7},{6,4},{7,5},{8,10},{9,11},{10,... | collective-permute-start | bytes 1572872 | tf_op jit(solution)/shard_map/ppermute | solution.py:65
  72.9 8.4 %collective-permute-start.11 = (f32[256,256]{1,0:T(8,128)S(1)}, f32[256,256]{1,0:T(8,128)S(1)}, u32[]{:S(2)}, u32[]{:S(2)}) collective-permute-start(f32[256,256]{1,0:T(8,128)S(1)} %get-tuple-element.125.refs_9_.refs_3_), channel_id=1, source_target_pairs={{0,8},{8,24},{24,16},{16,0},{1,9},{9,25},{25,17},{17,1},{10,2},{2,... | collective-permute-start | bytes 786440 | tf_op jit(solution)/shard_map/ppermute | solution.py:397
  74.1 8.1 %collective-permute-start.12 = (f32[256,256]{1,0:T(8,128)S(1)}, f32[256,256]{1,0:T(8,128)S(1)}, u32[]{:S(2)}, u32[]{:S(2)}) collective-permute-start(f32[256,256]{1,0:T(8,128)S(1)} %get-tuple-element.126.refs_7_), channel_id=1, source_target_pairs={{8,0},{24,8},{16,24},{0,16},{9,1},{25,9},{17,25},{1,17},{2,10},{18... | collective-permute-start | bytes 786440 | tf_op jit(solution)/shard_map/ppermute | solution.py:397
  85.9 7.9 %collective-permute-start.16 = (f32[256,256]{1,0:T(8,128)S(1)}, f32[256,256]{1,0:T(8,128)S(1)}, u32[]{:S(2)}, u32[]{:S(2)}) collective-permute-start(f32[256,256]{1,0:T(8,128)S(1)} %get-tuple-element.130.refs_7_.refs_11_), channel_id=1, source_target_pairs={{0,8},{8,24},{24,16},{16,0},{1,9},{9,25},{25,17},{17,1},{10,2},{2,... | collective-permute-start | bytes 786440 | tf_op jit(solution)/shard_map/ppermute | solution.py:397
  87.0 7.6 %collective-permute-start.17 = (f32[256,256]{1,0:T(8,128)S(1)}, f32[256,256]{1,0:T(8,128)S(1)}, u32[]{:S(2)}, u32[]{:S(2)}) collective-permute-start(f32[256,256]{1,0:T(8,128)S(1)} %get-tuple-element.135.refs_15_), channel_id=1, source_target_pairs={{8,0},{24,8},{16,24},{0,16},{9,1},{25,9},{17,25},{1,17},{2,10},{18... | collective-permute-start | bytes 786440 | tf_op jit(solution)/shard_map/ppermute | solution.py:397
  88.0 6.6 %copy-start.22 = (f32[256,256]{1,0:T(8,128)S(1)}, f32[256,256]{1,0:T(8,128)}, u32[]{:S(2)}) copy-start(f32[256,256]{1,0:T(8,128)} %copy-done.21) | copy-start | bytes 786436
  88.0 6.5 %copy-start.48 = (f32[256,256]{1,0:T(8,128)S(1)}, f32[256,256]{1,0:T(8,128)}, u32[]{:S(2)}) copy-start(f32[256,256]{1,0:T(8,128)} %copy-done.47) | copy-start | bytes 786436
  88.1 6.5 %copy-start.50 = (f32[256,256]{1,0:T(8,128)S(1)}, f32[256,256]{1,0:T(8,128)}, u32[]{:S(2)}) copy-start(f32[256,256]{1,0:T(8,128)} %copy-done.49) | copy-start | bytes 786436
  97.1 2.7 %collective-permute-start.18 = (f32[512,512]{1,0:T(8,128)S(1)}, f32[512,512]{1,0:T(8,128)S(1)}, u32[]{:S(2)}, u32[]{:S(2)}) collective-permute-start(f32[512,512]{1,0:T(8,128)S(1)} %get-tuple-element.137.refs_3_), channel_id=1, source_target_pairs={{0,1},{1,0},{2,3},{3,2},{4,5},{5,4},{6,7},{7,6},{8,9},{9,8},{10,11... | collective-permute-start | bytes 3145736 | tf_op jit(solution)/shard_map/ppermute | solution.py:65
  99.9 19.6 %collective-permute-start.19 = (f32[256,512]{1,0:T(8,128)S(1)}, f32[256,512]{1,0:T(8,128)S(1)}, u32[]{:S(2)}, u32[]{:S(2)}) collective-permute-start(f32[256,512]{1,0:T(8,128)S(1)} %get-tuple-element.140), channel_id=1, source_target_pairs={{0,2},{1,3},{2,0},{3,1},{4,6},{5,7},{6,4},{7,5},{8,10},{9,11},{10,... | collective-permute-start | bytes 1572872 | tf_op jit(solution)/shard_map/ppermute | solution.py:65
  101.3 8.1 %collective-permute-start.20 = (f32[256,256]{1,0:T(8,128)S(1)}, f32[256,256]{1,0:T(8,128)S(1)}, u32[]{:S(2)}, u32[]{:S(2)}) collective-permute-start(f32[256,256]{1,0:T(8,128)S(1)} %collective-permute-done.16.refs_14_.refs_5_.refs_12_), channel_id=1, source_target_pairs={{0,8},{8,24},{24,16},{16,0},{1,9},{9,25},{25,17},{17,1},{10,2},{2,... | collective-permute-start | bytes 786440 | tf_op jit(solution)/shard_map/ppermute | solution.py:397
  102.6 8.1 %collective-permute-start.21 = (f32[256,256]{1,0:T(8,128)S(1)}, f32[256,256]{1,0:T(8,128)S(1)}, u32[]{:S(2)}, u32[]{:S(2)}) collective-permute-start(f32[256,256]{1,0:T(8,128)S(1)} %collective-permute-done.17.refs_18_.refs_9_.refs_16_), channel_id=1, source_target_pairs={{8,0},{24,8},{16,24},{0,16},{9,1},{25,9},{17,25},{1,17},{2,10},{18... | collective-permute-start | bytes 786440 | tf_op jit(solution)/shard_map/ppermute | solution.py:397
  103.4 15.1 %collective-permute-start.15 = (f32[128,512]{1,0:T(8,128)S(1)}, f32[128,512]{1,0:T(8,128)S(1)}, u32[]{:S(2)}, u32[]{:S(2)}) collective-permute-start(f32[128,512]{1,0:T(8,128)S(1)} %get-tuple-element.134), channel_id=1, source_target_pairs={{0,4},{1,5},{2,6},{3,7},{4,0},{5,1},{6,2},{7,3},{8,12},{9,13},{10,... | collective-permute-start | bytes 786440 | tf_op jit(solution)/shard_map/ppermute | solution.py:65
  109.4 10.3 %collective-permute-start.22 = (f32[256,256]{1,0:T(8,128)S(1)}, f32[256,256]{1,0:T(8,128)S(1)}, u32[]{:S(2)}, u32[]{:S(2)}) collective-permute-start(f32[256,256]{1,0:T(8,128)S(1)} %collective-permute-done.20.refs_6_.refs_13_), channel_id=1, source_target_pairs={{0,8},{8,24},{24,16},{16,0},{1,9},{9,25},{25,17},{17,1},{10,2},{2,... | collective-permute-start | bytes 786440 | tf_op jit(solution)/shard_map/ppermute | solution.py:397
  110.7 9.0 %collective-permute-start.23 = (f32[256,256]{1,0:T(8,128)S(1)}, f32[256,256]{1,0:T(8,128)S(1)}, u32[]{:S(2)}, u32[]{:S(2)}) collective-permute-start(f32[256,256]{1,0:T(8,128)S(1)} %collective-permute-done.21.refs_10_.refs_17_), channel_id=1, source_target_pairs={{8,0},{24,8},{16,24},{0,16},{9,1},{25,9},{17,25},{1,17},{2,10},{18... | collective-permute-start | bytes 786440 | tf_op jit(solution)/shard_map/ppermute | solution.py:397
  122.2 2.7 %collective-permute-start.24 = (f32[512,512]{1,0:T(8,128)S(1)}, f32[512,512]{1,0:T(8,128)S(1)}, u32[]{:S(2)}, u32[]{:S(2)}) collective-permute-start(f32[512,512]{1,0:T(8,128)S(1)} %get-tuple-element.143.refs_3_), channel_id=1, source_target_pairs={{0,1},{1,0},{2,3},{3,2},{4,5},{5,4},{6,7},{7,6},{8,9},{9,8},{10,11... | collective-permute-start | bytes 3145736 | tf_op jit(solution)/shard_map/ppermute | solution.py:65
  129.5 24.2 %collective-permute-start.27 = (f32[3,256,512]{2,1,0:T(8,128)S(1)}, f32[3,256,512]{2,1,0:T(8,128)S(1)}, u32[]{:S(2)}, u32[]{:S(2)}) collective-permute-start(f32[3,256,512]{2,1,0:T(8,128)S(1)} %get-tuple-element.152), channel_id=1, source_target_pairs={{0,1},{1,0},{2,3},{3,2},{4,5},{5,4},{6,7},{7,6},{8,9},{9,8},{10,11... | collective-permute-start | bytes 4718600 | tf_op jit(solution)/shard_map/ppermute | solution.py:65
  132.8 20.9 %collective-permute-start.28 = (f32[2,256,512]{2,1,0:T(8,128)S(1)}, f32[2,256,512]{2,1,0:T(8,128)S(1)}, u32[]{:S(2)}, u32[]{:S(2)}) collective-permute-start(f32[2,256,512]{2,1,0:T(8,128)S(1)} %get-tuple-element.161), channel_id=1, source_target_pairs={{0,1},{1,0},{2,3},{3,2},{4,5},{5,4},{6,7},{7,6},{8,9},{9,8},{10,11... | collective-permute-start | bytes 3145736 | tf_op jit(solution)/shard_map/ppermute | solution.py:65
  132.9 20.8 %collective-permute-start.26 = (f32[256,512]{1,0:T(8,128)S(1)}, f32[256,512]{1,0:T(8,128)S(1)}, u32[]{:S(2)}, u32[]{:S(2)}) collective-permute-start(f32[256,512]{1,0:T(8,128)S(1)} %get-tuple-element.150), channel_id=1, source_target_pairs={{0,2},{1,3},{2,0},{3,1},{4,6},{5,7},{6,4},{7,5},{8,10},{9,11},{10,... | collective-permute-start | bytes 1572872 | tf_op jit(solution)/shard_map/ppermute | solution.py:65
  135.6 17.4 %collective-permute-start.25 = (f32[128,512]{1,0:T(8,128)S(1)}, f32[128,512]{1,0:T(8,128)S(1)}, u32[]{:S(2)}, u32[]{:S(2)}) collective-permute-start(f32[128,512]{1,0:T(8,128)S(1)} %get-tuple-element.149), channel_id=1, source_target_pairs={{0,4},{1,5},{2,6},{3,7},{4,0},{5,1},{6,2},{7,3},{8,12},{9,13},{10,... | collective-permute-start | bytes 786440 | tf_op jit(solution)/shard_map/ppermute | solution.py:65
  154.1 14.6 %collective-permute-start.29 = (f32[128,512]{1,0:T(8,128)S(1)}, f32[128,512]{1,0:T(8,128)S(1)}, u32[]{:S(2)}, u32[]{:S(2)}) collective-permute-start(f32[128,512]{1,0:T(8,128)S(1)} %get-tuple-element.164), channel_id=1, source_target_pairs={{0,4},{1,5},{2,6},{3,7},{4,0},{5,1},{6,2},{7,3},{8,12},{9,13},{10,... | collective-permute-start | bytes 786440 | tf_op jit(solution)/shard_map/ppermute | solution.py:65
  156.8 12.8 %collective-permute-start.33 = (f32[2,64,512]{2,1,0:T(8,128)S(1)}, f32[2,64,512]{2,1,0:T(8,128)S(1)}, u32[]{:S(2)}, u32[]{:S(2)}) collective-permute-start(f32[2,64,512]{2,1,0:T(8,128)S(1)} %get-tuple-element.170), channel_id=1, source_target_pairs={{0,8},{8,0},{16,24},{24,16},{1,9},{9,1},{17,25},{25,17},{2,10},{10... | collective-permute-start | bytes 786440 | tf_op jit(solution)/shard_map/ppermute | solution.py:65
  157.9 32.5 %collective-permute-start.30 = (f32[3,64,512]{2,1,0:T(8,128)S(1)}, f32[3,64,512]{2,1,0:T(8,128)S(1)}, u32[]{:S(2)}, u32[]{:S(2)}) collective-permute-start(f32[3,64,512]{2,1,0:T(8,128)S(1)} %get-tuple-element.166), channel_id=1, source_target_pairs={{0,8},{8,0},{16,24},{24,16},{1,9},{9,1},{17,25},{25,17},{2,10},{10... | collective-permute-start | bytes 1179656 | tf_op jit(solution)/shard_map/ppermute | solution.py:65
  158.9 31.5 %collective-permute-start.31 = (f32[3,64,512]{2,1,0:T(8,128)S(1)}, f32[3,64,512]{2,1,0:T(8,128)S(1)}, u32[]{:S(2)}, u32[]{:S(2)}) collective-permute-start(f32[3,64,512]{2,1,0:T(8,128)S(1)} %get-tuple-element.167), channel_id=1, source_target_pairs={{0,16},{8,24},{16,0},{24,8},{1,17},{9,25},{17,1},{25,9},{2,18},{10... | collective-permute-start | bytes 1179656 | tf_op jit(solution)/shard_map/ppermute | solution.py:65
  159.7 30.6 %collective-permute-start.32 = (f32[3,64,512]{2,1,0:T(8,128)S(1)}, f32[3,64,512]{2,1,0:T(8,128)S(1)}, u32[]{:S(2)}, u32[]{:S(2)}) collective-permute-start(f32[3,64,512]{2,1,0:T(8,128)S(1)} %get-tuple-element.168), channel_id=1, source_target_pairs={{0,24},{8,16},{16,8},{24,0},{1,25},{9,17},{17,9},{25,1},{2,26},{10... | collective-permute-start | bytes 1179656 | tf_op jit(solution)/shard_map/ppermute | solution.py:65
  168.8 21.6 %collective-permute-start.34 = (f32[2,64,512]{2,1,0:T(8,128)S(1)}, f32[2,64,512]{2,1,0:T(8,128)S(1)}, u32[]{:S(2)}, u32[]{:S(2)}) collective-permute-start(f32[2,64,512]{2,1,0:T(8,128)S(1)} %get-tuple-element.171), channel_id=1, source_target_pairs={{0,16},{8,24},{16,0},{24,8},{1,17},{9,25},{17,1},{25,9},{2,18},{10... | collective-permute-start | bytes 786440 | tf_op jit(solution)/shard_map/ppermute | solution.py:65
  169.6 20.7 %collective-permute-start.35 = (f32[2,64,512]{2,1,0:T(8,128)S(1)}, f32[2,64,512]{2,1,0:T(8,128)S(1)}, u32[]{:S(2)}, u32[]{:S(2)}) collective-permute-start(f32[2,64,512]{2,1,0:T(8,128)S(1)} %get-tuple-element.172), channel_id=1, source_target_pairs={{0,24},{8,16},{16,8},{24,0},{1,25},{9,17},{17,9},{25,1},{2,26},{10... | collective-permute-start | bytes 786440 | tf_op jit(solution)/shard_map/ppermute | solution.py:65
  190.5 8.5 %collective-permute-start.36 = (f32[3,32,512]{2,1,0:T(8,128)S(1)}, f32[3,32,512]{2,1,0:T(8,128)S(1)}, u32[]{:S(2)}, u32[]{:S(2)}) collective-permute-start(f32[3,32,512]{2,1,0:T(8,128)S(1)} %get-tuple-element.176), channel_id=1, source_target_pairs={{0,2},{1,3},{2,0},{3,1},{4,6},{5,7},{6,4},{7,5},{8,10},{9,11},{10,... | collective-permute-start | bytes 589832 | tf_op jit(solution)/shard_map/ppermute | solution.py:65
  190.6 8.4 %collective-permute-start.37 = (f32[2,32,512]{2,1,0:T(8,128)S(1)}, f32[2,32,512]{2,1,0:T(8,128)S(1)}, u32[]{:S(2)}, u32[]{:S(2)}) collective-permute-start(f32[2,32,512]{2,1,0:T(8,128)S(1)} %get-tuple-element.178), channel_id=1, source_target_pairs={{0,2},{1,3},{2,0},{3,1},{4,6},{5,7},{6,4},{7,5},{8,10},{9,11},{10,... | collective-permute-start | bytes 393224 | tf_op jit(solution)/shard_map/ppermute | solution.py:65
  200.2 8.5 %collective-permute-start.38 = (f32[3,16,512]{2,1,0:T(8,128)S(1)}, f32[3,16,512]{2,1,0:T(8,128)S(1)}, u32[]{:S(2)}, u32[]{:S(2)}) collective-permute-start(f32[3,16,512]{2,1,0:T(8,128)S(1)} %get-tuple-element.180), channel_id=1, source_target_pairs={{0,4},{1,5},{2,6},{3,7},{4,0},{5,1},{6,2},{7,3},{8,12},{9,13},{10,... | collective-permute-start | bytes 294920 | tf_op jit(solution)/shard_map/ppermute | solution.py:65
  200.9 7.8 %collective-permute-start.39 = (f32[2,16,512]{2,1,0:T(8,128)S(1)}, f32[2,16,512]{2,1,0:T(8,128)S(1)}, u32[]{:S(2)}, u32[]{:S(2)}) collective-permute-start(f32[2,16,512]{2,1,0:T(8,128)S(1)} %get-tuple-element.182), channel_id=1, source_target_pairs={{0,4},{1,5},{2,6},{3,7},{4,0},{5,1},{6,2},{7,3},{8,12},{9,13},{10,... | collective-permute-start | bytes 196616 | tf_op jit(solution)/shard_map/ppermute | solution.py:65
  208.7 5.6 %collective-permute-start.43 = (f32[2,16,512]{2,1,0:T(8,128)S(1)}, f32[2,16,512]{2,1,0:T(8,128)S(1)}, u32[]{:S(2)}, u32[]{:S(2)}) collective-permute-start(f32[2,16,512]{2,1,0:T(8,128)S(1)} %get-tuple-element.184.refs_7_), channel_id=1, source_target_pairs={{0,8},{8,0},{16,24},{24,16},{1,9},{9,1},{17,25},{25,17},{2,10},{10... | collective-permute-start | bytes 196616 | tf_op jit(solution)/shard_map/ppermute | solution.py:65
  208.8 10.7 %collective-permute-start.40 = (f32[3,16,512]{2,1,0:T(8,128)S(1)}, f32[3,16,512]{2,1,0:T(8,128)S(1)}, u32[]{:S(2)}, u32[]{:S(2)}) collective-permute-start(f32[3,16,512]{2,1,0:T(8,128)S(1)} %get-tuple-element.183.refs_3_.refs_11_), channel_id=1, source_target_pairs={{0,8},{8,0},{16,24},{24,16},{1,9},{9,1},{17,25},{25,17},{2,10},{10... | collective-permute-start | bytes 294920 | tf_op jit(solution)/shard_map/ppermute | solution.py:65
  210.8 8.7 %collective-permute-start.41 = (f32[3,16,512]{2,1,0:T(8,128)S(1)}, f32[3,16,512]{2,1,0:T(8,128)S(1)}, u32[]{:S(2)}, u32[]{:S(2)}) collective-permute-start(f32[3,16,512]{2,1,0:T(8,128)S(1)} %get-tuple-element.183.refs_3_.refs_11_), channel_id=1, source_target_pairs={{0,16},{8,24},{16,0},{24,8},{1,17},{9,25},{17,1},{25,9},{2,18},{10... | collective-permute-start | bytes 294920 | tf_op jit(solution)/shard_map/ppermute | solution.py:65
  211.7 7.8 %collective-permute-start.42 = (f32[3,16,512]{2,1,0:T(8,128)S(1)}, f32[3,16,512]{2,1,0:T(8,128)S(1)}, u32[]{:S(2)}, u32[]{:S(2)}) collective-permute-start(f32[3,16,512]{2,1,0:T(8,128)S(1)} %get-tuple-element.183.refs_3_.refs_11_), channel_id=1, source_target_pairs={{0,24},{8,16},{16,8},{24,0},{1,25},{9,17},{17,9},{25,1},{2,26},{10... | collective-permute-start | bytes 294920 | tf_op jit(solution)/shard_map/ppermute | solution.py:65
  212.3 5.7 %collective-permute-start.44 = (f32[2,16,512]{2,1,0:T(8,128)S(1)}, f32[2,16,512]{2,1,0:T(8,128)S(1)}, u32[]{:S(2)}, u32[]{:S(2)}) collective-permute-start(f32[2,16,512]{2,1,0:T(8,128)S(1)} %get-tuple-element.184.refs_7_), channel_id=1, source_target_pairs={{0,16},{8,24},{16,0},{24,8},{1,17},{9,25},{17,1},{25,9},{2,18},{10... | collective-permute-start | bytes 196616 | tf_op jit(solution)/shard_map/ppermute | solution.py:65
  214.3 5.2 %collective-permute-start.45 = (f32[2,16,512]{2,1,0:T(8,128)S(1)}, f32[2,16,512]{2,1,0:T(8,128)S(1)}, u32[]{:S(2)}, u32[]{:S(2)}) collective-permute-start(f32[2,16,512]{2,1,0:T(8,128)S(1)} %get-tuple-element.184.refs_7_), channel_id=1, source_target_pairs={{0,24},{8,16},{16,8},{24,0},{1,25},{9,17},{17,9},{25,1},{2,26},{10... | collective-permute-start | bytes 196616 | tf_op jit(solution)/shard_map/ppermute | solution.py:65
  (37 other events, 71.2 us)

commit v7 on v6

v7 whole, which is shorter than its diff:
```python
import functools

import jax
import jax.numpy as jnp
from jax import lax
from jax.experimental import pallas as pl
from jax.experimental.pallas import tpu as pltpu
from jax.sharding import PartitionSpec as P

AXES = ("row", "col")
F32 = jnp.float32
BF16 = jnp.bfloat16
NN = (((1,), (0,)), ((), ()))
NT = (((1,), (1,)), ((), ()))
MIB = 1024 * 1024
WAIT = ("wait",)


def split(value):
    high = value.astype(BF16)
    return high, (value - high.astype(F32)).astype(BF16)


def one_pass(left, right, dims=NN):
    return lax.dot_general(left, right, dims, preferred_element_type=F32)


def product(left, right):
    return one_pass(left[0], right[0]) + (
        one_pass(left[0], right[1]) + one_pass(left[1], right[0])
    )


def turn(chooser, pair):
    return [one_pass(chooser, half, NT).astype(BF16) for half in pair]


def pair_of(high_ref, low_ref, *index):
    return (high_ref[index], low_ref[index]) if index else (high_ref[...], low_ref[...])


def store_pair(high_ref, low_ref, pair, *index):
    index = index if index else ...
    high_ref[index], low_ref[index] = pair


def shape(*dims, dtype=F32):
    return jax.ShapeDtypeStruct(dims, dtype)


def gray(place):
    return place ^ (place >> 1)


def reversed_bits(count):
    order = [0]
    step = 1
    while step < count:
        order = [value + bit * step for value in order for bit in (0, 1)]
        step *= 2
    return order


def swap(value, axis, size, change):
    return lax.ppermute(value, axis, [(place, place ^ change) for place in range(size)])


def block(index, size):
    return pl.ds(pl.multiple_of(index * size, size), size)


def core_of(info_ref):
    return info_ref[1] & 1


def call(body, outs, args, smem=0, hbm=0, scratch=(), vmem=8, after=None):
    places = [pltpu.SMEM] * smem + [pltpu.HBM] * hbm
    places += [pltpu.VMEM] * (len(args) - len(places))
    count = len(args)
    args = list(args)
    inner = body
    if after is not None:
        args.append(after)
        places.append(pl.ANY)

        def inner(*refs):
            body(*refs[:count], *refs[count + 1 :])

    results = pl.pallas_call(
        inner,
        out_shape=outs,
        in_specs=[pl.BlockSpec(memory_space=place) for place in places],
        out_specs=[pl.BlockSpec(memory_space=pltpu.VMEM)] * len(outs),
        scratch_shapes=scratch,
        compiler_params=pltpu.CompilerParams(vmem_limit_bytes=vmem * MIB),
        cost_estimate=pl.CostEstimate(flops=1024, bytes_accessed=1024, transcendentals=0),
    )(*args)
    return list(results)


def cut_kernel(ratio, cuts, info_ref, listed_ref, factors_ref, *refs):
    *outs, sems = refs
    size, unit = outs[0].shape
    width = factors_ref.shape[2]
    column = info_ref[1]
    pair = (column % ratio) // 2
    copies = []
    for at, out_ref in enumerate(outs):
        member, cut, way = at // (2 * cuts), at // 2 % cuts, at % 2
        source = factors_ref.at[
            member, block(2 * pair + way, size), block(core_of(info_ref) * cuts + cut, unit)
        ]
        copies.append(pltpu.make_async_copy(source, out_ref, sems.at[at]))
        copies[-1].start()
    for at, out_ref in enumerate(outs):
        copies[at].wait()
        owner = column - core_of(info_ref) + at % 2
        weight = listed_ref[at // (2 * cuts), owner * size // width]
        out_ref[...] = out_ref[...] * weight.astype(F32)


def chooser_kernel(rows, columns, info_ref, out_ref):
    width = out_ref.shape[0]
    size = width // columns
    part = size // rows
    place = lax.broadcasted_iota(jnp.int32, out_ref.shape, 0)
    inner = place % part
    core = place // part % 2
    level = place // (2 * part) % (columns // 2)
    by_row = place // (2 * part * (columns // 2))
    turned = jnp.zeros_like(level)
    bits = (columns // 2).bit_length() - 1
    for bit in range(bits):
        turned = turned | (((level >> bit) & 1) << (bits - 1 - bit))
    column = (turned * 2 + core) ^ info_ref[1]
    wanted = column * size + (by_row ^ info_ref[0]) * part + inner
    hit = wanted == lax.broadcasted_iota(jnp.int32, out_ref.shape, 1)
    out_ref[...] = hit.astype(F32).astype(BF16)


def region_kernel(order, info_ref, own_ref, other_ref, high_ref, low_ref, held_ref, sems):
    groups = len(order)
    size = own_ref.shape[0] // groups
    width = own_ref.shape[1]
    column = info_ref[1] >> 1
    copies = []
    for g in range(groups):
        for side, source_ref in enumerate((own_ref, other_ref)):
            copies.append(
                pltpu.make_async_copy(
                    source_ref.at[block(order[g] ^ column, size), :],
                    held_ref.at[side, pl.ds(g * size, size), :],
                    sems.at[side, g],
                )
            )
            copies[-1].start()
    for g in range(groups):
        rows = slice(g * size, (g + 1) * size)
        for side in range(2):
            copies[2 * g + side].wait()
            columns = block(core_of(info_ref) ^ side, width)
            high, low = split(held_ref[side, rows, :])
            high_ref[rows, columns] = high
            low_ref[rows, columns] = low


def factor_kernel(
    order, member, info_ref, listed_ref, factors_ref, chooser_ref, high_ref, low_ref, held_ref, sems
):
    groups = len(order)
    _, rows_here, width = factors_ref.shape
    size = rows_here // groups
    column = info_ref[1] >> 1
    copies = []
    for g in range(groups):
        copies.append(
            pltpu.make_async_copy(
                factors_ref.at[member, block(order[g] ^ column, size), :],
                held_ref.at[pl.ds(g * size, size), :],
                sems.at[g],
            )
        )
        copies[-1].start()
    for g in range(groups):
        copies[g].wait()
        rows = slice(g * size, (g + 1) * size)
        first = info_ref[0] * rows_here + (order[g] ^ column) * size
        held_ref[rows, :] = held_ref[rows, :] * listed_ref[member, first // width].astype(F32)
    store_pair(high_ref, low_ref, turn(chooser_ref[...], split(held_ref[...])))


def own_weight(info_ref, listed_ref, member, size, rows_here, width):
    first = info_ref[0] * rows_here + (info_ref[1] >> 1) * size
    return listed_ref[member, first // width].astype(F32)


def own_kernel(
    info_ref, listed_ref, factors_ref, chooser_ref, high_ref, low_ref, thigh_ref, tlow_ref,
    held_ref, sems,
):
    members, rows, width = held_ref.shape
    copies = []
    for j in range(members):
        copies.append(
            pltpu.make_async_copy(
                factors_ref.at[j, block(info_ref[1] >> 1, rows), :], held_ref.at[j], sems.at[j]
            )
        )
        copies[-1].start()
    for j in range(members):
        copies[j].wait()
        weight = own_weight(info_ref, listed_ref, j, rows, factors_ref.shape[1], width)
        pair = split(held_ref[j] * weight)
        store_pair(high_ref, low_ref, pair, j)
        store_pair(thigh_ref, tlow_ref, turn(chooser_ref[...], pair), j)


def link_kernel(
    children, share, info_ref, gathered_ref, diag_ref, other_ref, chooser_ref,
    own_high_ref, own_low_ref, high_ref, low_ref, lift_high_ref, lift_low_ref, framed_ref,
    corner_ref, held_ref, rows_ref, frame_ref,
):
    groups, _, size, width = gathered_ref.shape
    half = corner_ref.shape[2]
    core = core_of(info_ref)
    chooser = chooser_ref[...]
    for g in range(groups):
        for c in range(children):
            held_ref[c, block(info_ref[1] ^ g, size), :] = gathered_ref[g, c]
    rows_ref[block(core, size), :] = diag_ref[0]
    rows_ref[block(1 - core, size), :] = other_ref[0]
    diag = split(rows_ref[...])
    for c in range(children):
        pair = split(held_ref[c])
        store_pair(high_ref, low_ref, pair, c)
        lifted = product(pair_of(own_high_ref, own_low_ref, 0), pair)
        store_pair(lift_high_ref, lift_low_ref, turn(chooser, split(lifted)), c)
        frame_ref[...] = product(diag, pair)
        framed_ref[c] = frame_ref[block(core, size), :]
        slices = split(held_ref[c, block(info_ref[1] >> 1, 2 * size), :])
        corner = product(turn(chooser, slices), split(frame_ref[:, block(core, half)]))
        corner_ref[c] = share * corner


def unit_kernel(count, ratio, cuts, info_ref, high_ref, low_ref, *refs):
    keep_ref, send_ref = refs[-2:]
    middle = keep_ref.shape[0]
    place = info_ref[0] ^ (info_ref[1] // ratio)
    shift = 1
    while shift < count:
        place = place ^ (place >> shift)
        shift *= 2
    places = (place, (count - place) % count)
    parts = []
    for cut in range(cuts):
        chosen = []
        for way in range(2):
            candidates = refs[(2 * cut + way) * count :][:count]
            value = candidates[0][...]
            for at in range(1, count):
                value = jnp.where(places[way] == at, candidates[at][...], value)
            chosen.append(value)
        parts.append(jnp.concatenate(chosen))
    right = split(jnp.concatenate(parts, axis=1))
    send_ref[...] = product((high_ref[middle:], low_ref[middle:]), right)
    keep_ref[...] = product((high_ref[:middle], low_ref[:middle]), right)


def unit_gram_kernel(high_ref, low_ref, keep_ref, send_ref, out_ref):
    middle = keep_ref.shape[0]
    out_ref[...] = product(
        (high_ref[:, :middle], low_ref[:, :middle]), split(keep_ref[...])
    ) + product((high_ref[:, middle:], low_ref[:, middle:]), split(send_ref[...]))


def store_parts(refs, index, value):
    size = refs[0].shape[1]
    for at, ref in enumerate(refs):
        ref[index] = value[at * size : (at + 1) * size]


def parent_kernel(
    children, rows_here, info_ref, listed_ref, chooser_ref, own_high_ref, own_low_ref,
    own_thigh_ref, own_tlow_ref, link_high_ref, link_low_ref, mine_ref, other_ref,
    col_ref, turned_ref, high_ref, low_ref, thigh_ref, tlow_ref, *refs
):
    *outs, full_ref = refs
    chooser = chooser_ref[...]
    rows, half = mine_ref.shape
    core = core_of(info_ref)
    weight = own_weight(info_ref, listed_ref, 0, rows, rows_here, chooser.shape[0])
    mine = -mine_ref[...] * weight
    full_ref[:, block(core, half)] = mine
    full_ref[:, block(1 - core, half)] = -other_ref[...] * weight
    output_rows = block(core, rows // 2)
    col_ref[...] = full_ref[output_rows, :]
    pair = split(full_ref[...])
    turned_pair = turn(chooser, pair)
    parent = pair_of(own_thigh_ref, own_tlow_ref, 0)
    columns = block(core, half)
    store_parts(outs, 0, -product(parent, split(mine)))
    for c in range(children):
        full_ref[...] = product(pair, pair_of(link_high_ref, link_low_ref, c))
        turned_ref[c] = full_ref[output_rows, :]
        lifted = split(full_ref[:, columns])
        store_pair(high_ref, low_ref, lifted, c)
        store_pair(thigh_ref, tlow_ref, turn(chooser, split(full_ref[...])), c)
        own = (own_high_ref[c + 1, :, columns], own_low_ref[c + 1, :, columns])
        store_parts(outs, 1 + c, product(parent, lifted) - product(turned_pair, own))


def child_kernel(
    children, info_ref, own_high_ref, own_low_ref, own_thigh_ref, own_tlow_ref,
    high_ref, low_ref, thigh_ref, tlow_ref, lift_high_ref, lift_low_ref, corner_ref, *refs
):
    outs = refs[children:]
    columns = block(core_of(info_ref), corner_ref.shape[2])
    for c in range(children):
        lifted = pair_of(high_ref, low_ref, c)
        own = (own_high_ref[c + 1, :, columns], own_low_ref[c + 1, :, columns])
        total = corner_ref[c] + refs[c][...]
        total += product(pair_of(own_thigh_ref, own_tlow_ref, c + 1), lifted)
        total += product(pair_of(thigh_ref, tlow_ref, c), own)
        total -= product(pair_of(lift_high_ref, lift_low_ref, c), lifted)
        store_parts(outs, c, total)


def column_kernel(children, rows_here, info_ref, listed_ref, col_ref, turned_ref, *refs):
    out_ref = refs[-1]
    rows, width = col_ref.shape
    half = width // 2
    core = core_of(info_ref)
    out_ref[0] = col_ref[...]
    for c in range(children):
        weight = own_weight(info_ref, listed_ref, c + 1, 2 * rows, rows_here, width)
        for side in range(2):
            columns = block(core ^ side, half)
            total = refs[2 * c + side][...] + turned_ref[c, :, columns]
            out_ref[c + 1, :, columns] = -total * weight


def finish_kernel(rows, info_ref, diag_ref, framed_ref, *refs):
    parents, offspring = refs[:rows], refs[rows : 2 * rows]
    diags_ref, uppers_ref = refs[2 * rows :]
    part = parents[0].shape[1]

    def chosen(pieces, row):
        value = pieces[0][...]
        for change in range(1, rows):
            value = jnp.where(info_ref[0] ^ change == row, pieces[change][...], value)
        return value

    for row in range(rows):
        at = slice(row * part, (row + 1) * part)
        above, below = chosen(parents, row), chosen(offspring, row)
        diags_ref[0, at] = diag_ref[0, at] + above[0]
        diags_ref[1:, at] = diag_ref[1:, at] + below
        uppers_ref[:, at] = above[1:] - framed_ref[:, at]


def select_step(ratio, info_ref, ins, outs):
    source = info_ref[0] == info_ref[1] // ratio
    for way in range(2):
        outs[way][...] = jnp.where(source, ins[way][...], ins[2 + way][...])


def pass_step(info_ref, ins, outs):
    for way in range(2):
        outs[way][...] = ins[way][...]


def stack_step(info_ref, ins, outs):
    for at in range(ins[0].shape[0]):
        for side in range(2):
            outs[0][2 * at + side] = ins[side][at]


def halve_step(info_ref, ins, outs):
    size = outs[0].shape[-2]
    for at, out in enumerate(outs):
        rows = pl.ds(at * size, size)
        index = (rows,) if len(out.shape) == 2 else (slice(None), rows)
        total = ins[0][index]
        for other in ins[1:]:
            total = total + other[index]
        out[...] = total


def part_step(info_ref, ins, outs):
    size = outs[0].shape[0]
    for side, out in enumerate(outs):
        rows = block(core_of(info_ref) ^ side, size)
        total = ins[0][rows, :]
        for other in ins[1:]:
            total = total + other[rows, :]
        out[...] = total


def join_step(info_ref, ins, outs):
    half = ins[0].shape[-1]
    for side, value in enumerate(ins):
        outs[0][:, :, block(core_of(info_ref) ^ side, half)] = value[...]


def step_kernel(tasks, info_ref, *refs):
    start = 0
    end = sum(ins for _, ins, _ in tasks)
    for body, ins, outs in tasks:
        body(info_ref, refs[start : start + ins], refs[end : end + outs])
        start += ins
        end += outs


def shards(region_inverse, factor_cols, parent_factor, diag_inverse, listed):
    row_count = lax.axis_size("row")
    col_count = lax.axis_size("col")
    col_bits = col_count.bit_length() - 1
    rows_here, cols_here = region_inverse.shape
    members, _, width = factor_cols.shape
    children = members - 1
    levels = col_count // 2
    group = rows_here // levels
    ratio = col_count // row_count
    diag_width = width // col_count
    part = diag_width // row_count
    half = width // 2
    cuts = 2
    unit = half // cuts
    chunk_count = members * cuts
    order = reversed_bits(levels)
    stages = chunk_count + row_count - 2

    def ring(forward):
        pairs = []
        for col in range(col_count):
            start = col // ratio
            for place in range(row_count):
                at = (start ^ gray(place)) * col_count + col
                to = (start ^ gray((place + 1) % row_count)) * col_count + col
                pairs.append((at, to) if forward else (to, at))
        return pairs

    rings = (ring(True), ring(False))
    info = jnp.stack([lax.axis_index("row"), lax.axis_index("col")]).astype(jnp.int32)

    flat = call(
        functools.partial(cut_kernel, ratio, cuts),
        [shape(cols_here, unit)] * (chunk_count * 2),
        [info, listed, factor_cols],
        smem=2, hbm=1, vmem=48,
        scratch=[pltpu.SemaphoreType.DMA((chunk_count * 2,))],
    )
    chunks = [flat[at * 2 :][:2] for at in range(chunk_count)]

    last = [flat[0]]
    held = {}
    moved = []
    received = []

    def heavy(body, outs, args, **options):
        results = call(body, outs, args, after=last[0], **options)
        last[0] = results[0]
        return results

    def ring_flow():
        shapes = [shape(cols_here, unit)] * 2
        for stage in range(stages):
            if stage == 0:
                moving = chunks[0]
            elif stage < chunk_count:
                step = functools.partial(select_step, ratio)
                moving = yield (step, chunks[stage] + received[-1], shapes)
            else:
                moving = yield (pass_step, received[-1], shapes)
            moved.append(moving)
            received.append([lax.ppermute(moving[way], AXES, rings[way]) for way in range(2)])

    def link_flow():
        gathered = parent_factor[None]
        for bit in reversed(range(col_bits)):
            arrived = swap(gathered, "col", col_count, 1 << bit)
            dims = (2 * gathered.shape[0],) + parent_factor.shape
            (gathered,) = yield (stack_step, [gathered, arrived], [shape(*dims)])
        held["links"] = heavy(
            functools.partial(link_kernel, children, 1.0 / row_count),
            [shape(children, width, width, dtype=BF16)] * 2
            + [shape(children, width, group, dtype=BF16)] * 2
            + [shape(children, diag_width, width), shape(children, width, half)],
            [info, gathered, diag_inverse, held["other diag"], held["chooser"], *held["own"][:2]],
            smem=1, vmem=20,
            scratch=[
                pltpu.VMEM((children, width, width), F32),
                pltpu.VMEM((2 * diag_width, width), F32),
                pltpu.VMEM((2 * diag_width, width), F32),
            ],
        )

    def prepare_flow():
        other_region = swap(region_inverse, "col", col_count, 1)
        held["other diag"] = swap(diag_inverse[:1], "col", col_count, 1)
        (held["chooser"],) = heavy(
            functools.partial(chooser_kernel, row_count, col_count),
            [shape(width, width, dtype=BF16)],
            [info],
            smem=1,
        )
        held["own"] = heavy(
            own_kernel,
            [shape(members, group, width, dtype=BF16)] * 2
            + [shape(members, width, group, dtype=BF16)] * 2,
            [info, listed, factor_cols, held["chooser"]],
            smem=2, hbm=1,
            scratch=[
                pltpu.VMEM((members, group, width), F32), pltpu.SemaphoreType.DMA((members,))
            ],
        )
        yield WAIT
        held["region"] = heavy(
            functools.partial(region_kernel, order),
            [shape(rows_here, 2 * cols_here, dtype=BF16)] * 2,
            [info, region_inverse, other_region],
            smem=1, hbm=2, vmem=12,
            scratch=[
                pltpu.VMEM((2, rows_here, cols_here), F32),
                pltpu.SemaphoreType.DMA((2, levels)),
            ],
        )
        for member in range(1, members):
            yield WAIT
            held["turned", member] = heavy(
                functools.partial(factor_kernel, order, member),
                [shape(width, rows_here, dtype=BF16)] * 2,
                [info, listed, factor_cols, held["chooser"]],
                smem=2, hbm=1, vmem=20,
                scratch=[
                    pltpu.VMEM((rows_here, width), F32), pltpu.SemaphoreType.DMA((levels,))
                ],
            )

    def unit_flow(member):
        chunk = (member + 1) * cuts - 1
        while len(received) < chunk + row_count - 1:
            yield WAIT
        candidates = []
        for at in range(member * cuts, (member + 1) * cuts):
            for way in range(2):
                candidates.append(moved[at][way])
                candidates += [received[at + hop][way] for hop in range(row_count - 1)]
        size = rows_here // 2
        keep, send = heavy(
            functools.partial(unit_kernel, row_count, ratio, cuts),
            [shape(size, half)] * 2,
            [info, *held["region"], *candidates],
            smem=1, vmem=16,
        )
        first = (keep, send)
        for bit in range(1, col_bits):
            arrived = swap(send, "col", col_count, 1 << bit)
            if bit == 1:
                yield WAIT
                if member:
                    held["gram", member] = heavy(
                        unit_gram_kernel,
                        [shape(width, half)],
                        [*held["turned", member], *first],
                        vmem=16,
                    )[0]
            if bit + 1 < col_bits:
                size //= 2
                keep, send = yield (halve_step, [keep, arrived], [shape(size, half)] * 2)
        if member == 0:
            (mine,) = yield (halve_step, [keep, arrived], [shape(size, half)])
            other = swap(mine, "col", col_count, 1)
        else:
            mine, theirs = yield (part_step, [keep, arrived], [shape(size // 2, half)] * 2)
            other = swap(theirs, "col", col_count, 1)
        held["sum", member] = [mine, other]

    def total_flow(pieces):
        count, size, _ = pieces[0].shape
        inputs = [pieces[0]] + [swap(pieces[d], "row", row_count, d) for d in range(1, row_count)]
        for bit in [*range(1, col_bits), 0]:
            size //= 2
            keep, send = yield (halve_step, inputs, [shape(count, size, half)] * 2)
            inputs = [keep, swap(send, "col", col_count, 1 << bit)]
        (piece,) = yield (join_step, inputs, [shape(count, size, width)])
        return [piece] + [swap(piece, "row", row_count, d) for d in range(1, row_count)]

    def parent_flow():
        names = [("sum", 0), "links"]
        while any(name not in held for name in names):
            yield WAIT
        col, turned, *rest = heavy(
            functools.partial(parent_kernel, children, rows_here),
            [shape(group // 2, width), shape(children, group // 2, width)]
            + [shape(children, group, half, dtype=BF16)] * 2
            + [shape(children, width, group, dtype=BF16)] * 2
            + [shape(members, width // row_count, half)] * row_count,
            [info, listed, held["chooser"], *held["own"], *held["links"][:2], *held["sum", 0]],
            smem=2, vmem=20,
            scratch=[pltpu.VMEM((group, width), F32)],
        )
        held["parent"] = (col, turned, rest[:4])
        held["parent totals"] = yield from total_flow(rest[4:])

    def child_flow():
        names = [("gram", 1 + c) for c in range(children)]
        while any(name not in held for name in names + ["parent"]):
            yield WAIT
        pieces = heavy(
            functools.partial(child_kernel, children),
            [shape(children, width // row_count, half)] * row_count,
            [info, *held["own"], *held["parent"][2], *held["links"][2:4], held["links"][5]]
            + [held[name] for name in names],
            smem=1, vmem=20,
        )
        held["child totals"] = yield from total_flow(pieces)

    def column_flow():
        names = [("sum", 1 + c) for c in range(children)]
        while any(name not in held for name in names + ["parent"]):
            yield WAIT
        yield WAIT
        col, turned, _ = held["parent"]
        held["columns"] = heavy(
            functools.partial(column_kernel, children, rows_here),
            [shape(members, group // 2, width)],
            [info, listed, col, turned] + [value for name in names for value in held[name]],
            smem=2,
        )[0]

    flows = [ring_flow(), link_flow(), prepare_flow()]
    flows += [unit_flow(member) for member in range(members)]
    flows += [parent_flow(), child_flow(), column_flow()]
    waiting = [(flow, None) for flow in flows]
    while waiting:
        tasks = [wish for _, wish in waiting if wish not in (None, WAIT)]
        results = iter(())
        if tasks:
            outs = [out for _, _, shapes in tasks for out in shapes]
            args = [value for _, values, _ in tasks for value in values]
            sizes = [(body, len(values), len(shapes)) for body, values, shapes in tasks]
            results = iter(
                heavy(functools.partial(step_kernel, sizes), outs, [info, *args], smem=1)
            )
        answered = []
        for flow, wish in waiting:
            answer = None
            if wish not in (None, WAIT):
                answer = [next(results) for _ in wish[2]]
            answered.append((flow, answer))
        waiting = []
        for flow, answer in answered:
            try:
                waiting.append((flow, flow.send(answer)))
            except StopIteration:
                pass

    diags, uppers = heavy(
        functools.partial(finish_kernel, row_count),
        [shape(members, diag_width, width), shape(children, diag_width, width)],
        [info, diag_inverse, held["links"][4]] + held["parent totals"] + held["child totals"],
        smem=1,
    )
    return held["columns"], diags, uppers


def solution(mesh):
    in_specs = (
        P("row", "col"),
        P(None, "row", None),
        P(None, "col", None),
        P(None, "col", None),
        P(),
    )
    out_specs = (P(None, ("row", "col"), None), P(None, "col", None), P(None, "col", None))
    return jax.shard_map(shards, mesh=mesh, in_specs=in_specs, out_specs=out_specs, check_vma=False)
```

time: 221 us -> 204 us (0.923)
  local copies, waits for them, and re-layouts: 22.2 us -> 1.85 us
  waiting for transfers between devices: 101 us -> 104 us
    ppermute x16, waiting for transfers between devices: 17.5 us -> 43.4 us  [ring_flow(): lax.ppermute(moving[way], AXES, rings[way])]
    ppermute x30 -> x32, waiting for transfers between devices: 83.4 us -> 61.1 us  [swap(): lax.ppermute(value, axis, [(place, place ^ change) for place in range(siz...]
    unnamed x111 -> x14, local copies, waits for them, and re-layouts: 20.3 us -> 1.84 us
    ppermute x30 -> x32, starting transfers between devices: 36.7 us -> 36.3 us  [swap(): lax.ppermute(value, axis, [(place, place ^ change) for place in range(siz...]
  transfers between devices with their start and end apart: 46 -> 48, of which waited for: 24 -> 26; matrix products, arithmetic and copies ran while one was open for 1% -> 0% of each run, Pallas kernels for 10% -> 17%
where the time goes in v7:
time: 204 us
  waiting for transfers between devices  104 us (51%)
  starting transfers between devices  53.7 us (26%)
  Pallas kernels  43 us (21%)
    ppermute x32, waiting for transfers between devices, swap(): lax.ppermute(value, axis, [(place, place ^ change) for place in range(siz...  61.1 us
    ppermute x16, waiting for transfers between devices, ring_flow(): lax.ppermute(moving[way], AXES, rings[way])  43.4 us
    pallas_call x28, Pallas kernels, call(): pl.pallas_call(inner, out_shape=outs, in_specs=[pl.BlockSpec(memory_space...  43 us
    ppermute x32, starting transfers between devices, swap(): lax.ppermute(value, axis, [(place, place ^ change) for place in range(siz...  36.3 us
    ppermute x16, starting transfers between devices, ring_flow(): lax.ppermute(moving[way], AXES, rings[way])  17.5 us
  transfers between devices with their start and end apart: 48, of which 26 were waited for; matrix products, arithmetic and copies ran while one was open for 0% of the time, Pallas kernels for 17%

profile of v7, /device:TPU:0, one launch (start us, length us, event | category | flops | bytes accessed | tf_op | source)
XLA Modules:
  0.0 204.1 jit_solution(17669008539286365677)
XLA Ops:
  1.1 3.7 %collective-permute-start.2 = (f32[1,2,64,512]{3,2,1,0:T(8,128)}, f32[1,2,64,512]{3,2,1,0:T(8,128)S(1)}, u32[]{:S(2)}, u32[]{:S(2)}) collective-permute-start(f32[1,2,64,512]{3,2,1,0:T(8,128)} %bitcast.3), channel_id=1, source_target_pairs={{0,4},{1,5},{2,6},{3,7},{4,0},{5,1},{6,2},{7,3},{8,12},{9,13},{10,... | collective-permute-start | bytes 786440 | tf_op jit(solution)/shard_map/ppermute | solution.py:65
  5.6 2.8 %shard_map.76 = (f32[512,128]{1,0:T(8,128)S(1)}, f32[512,128]{1,0:T(8,128)S(1)}, f32[512,128]{1,0:T(8,128)S(1)}, f32[512,128]{1,0:T(8,128)S(1)}, f32[512,128]{1,...) custom-call(s32[2]{0:T(128)S(1)} %pad_add_fusion.info_ref.refs_0_, ...), custom_call_target="tpu_custom_call" | custom-call | flops 1024 | bytes 1024 | tf_op jit(solution)/shard_map/pallas_call | solution.py:89
  8.4 1.6 collective-permute-start.1
  11.3 2.2 %shard_map.78 = (bf16[3,256,512]{2,1,0:T(8,128)(2,1)S(1)}, bf16[3,256,512]{2,1,0:T(8,128)(2,1)S(1)}, bf16[3,512,256]{2,1,0:T(8,128)(2,1)S(1)}, bf16[3,512,256]{2,1,0:T(8,128)(2,1)S(1)}) custom-call(s32[2]{0:T(128)S(1)} %pad_add_fusion.info_ref.refs_0_, s32[3,8]{1,0:T(4,128)S(1)} %copy-done.5, f32[3,1024,512]{2,1,0:T(8,128)S(1)} %copy-done, ...), custom_call_target="tpu_custom_call" | custom-call | flops 1024 | bytes 1024 | tf_op jit(solution)/shard_map/pallas_call | solution.py:89
  13.6 4.0 %collective-permute-done.2.refs_6_ = f32[1,2,64,512]{3,2,1,0:T(8,128)S(1)} collective-permute-done((f32[1,2,64,512]{3,2,1,0:T(8,128)}, f32[1,2,64,512]{3,2,1,0:T(8,128)S(1)}, u32[]{:S(2)}, u32[]{:S(2)}) %collective-permute-start.2) | collective-permute-done | bytes 262176 | tf_op jit(solution)/shard_map/ppermute | solution.py:65
  18.7 1.6 collective-permute-start.5
  20.9 1.5 collective-permute-start.3
  22.4 1.7 shard_map.80
  24.0 3.2 %collective-permute-done.4.refs_4_.refs_9_.refs_16_ = f32[512,128]{1,0:T(8,128)S(1)} collective-permute-done((f32[512,128]{1,0:T(8,128)S(1)}, f32[512,128]{1,0:T(8,128)S(1)}, u32[]{:S(2)}, u32[]{:S(2)}) %collective-permute-start.4) | collective-permute-done | bytes 262176 | tf_op jit(solution)/shard_map/ppermute | solution.py:476
  27.3 1.1 collective-permute-done.3.refs_3_.refs_5_.refs_12_
  28.3 3.6 %collective-permute-done.5.refs_6_ = f32[2,2,64,512]{3,2,1,0:T(8,128)S(1)} collective-permute-done((f32[2,2,64,512]{3,2,1,0:T(8,128)S(1)}, f32[2,2,64,512]{3,2,1,0:T(8,128)S(1)}, u32[]{:S(2)}, u32[]{:S(2)}) %collective-permute-start.5) | collective-permute-done | bytes 524320 | tf_op jit(solution)/shard_map/ppermute | solution.py:65
  32.7 1.5 collective-permute-start.8
  34.8 2.2 %shard_map.82 = (bf16[512,1024]{1,0:T(8,128)(2,1)S(1)}, bf16[512,1024]{1,0:T(8,128)(2,1)S(1)}) custom-call(s32[2]{0:T(128)S(1)} %pad_add_fusion.info_ref.refs_0_, s32[3,8]{1,0:T(4,128)S(1)} %copy-done.5, f32[3,1024,512]{2,1,0:T(8,128)S(1)} %copy-done, bf16[512,512]{1,0:T(8,128)(2,1)S(1)} %shard_map.77.refs_3_.refs_4_.refs_2_, ...), custom_call_target="tpu_custom_call" | custom-call | flops 1024 | bytes 1024 | tf_op jit(solution)/shard_map/pallas_call | solution.py:89
  37.0 4.4 %collective-permute-done.8.refs_4_.refs_10_.refs_17_.refs_8_ = f32[512,128]{1,0:T(8,128)S(1)} collective-permute-done((f32[512,128]{1,0:T(8,128)S(1)}, f32[512,128]{1,0:T(8,128)S(1)}, u32[]{:S(2)}, u32[]{:S(2)}) %collective-permute-start.8) | collective-permute-done | bytes 262176 | tf_op jit(solution)/shard_map/ppermute | solution.py:476
  41.4 1.1 collective-permute-done.7.refs_3_.refs_6_.refs_13_.refs_4_
  43.3 1.5 collective-permute-start.12
  45.4 1.3 collective-permute-done.10.refs_3_
  46.8 4.5 %shard_map.84 = (bf16[2,512,512]{2,1,0:T(8,128)(2,1)S(1)}, bf16[2,512,512]{2,1,0:T(8,128)(2,1)S(1)}, bf16[2,512,256]{2,1,0:T(8,128)(2,1)S(1)}, bf16[2,512,256]{2...) custom-call(s32[2]{0:T(128)S(1)} %pad_add_fusion.info_ref.refs_0_, ...), custom_call_target="tpu_custom_call" | custom-call | flops 1024 | bytes 1024 | tf_op jit(solution)/shard_map/pallas_call | solution.py:89
  51.3 2.2 %shard_map.85 = (bf16[512,1024]{1,0:T(8,128)(2,1)S(1)}, bf16[512,1024]{1,0:T(8,128)(2,1)S(1)}) custom-call(s32[2]{0:T(128)S(1)} %pad_add_fusion.info_ref.refs_0_, s32[3,8]{1,0:T(4,128)S(1)} %copy-done.5, f32[3,1024,512]{2,1,0:T(8,128)S(1)} %copy-done, bf16[512,512]{1,0:T(8,128)(2,1)S(1)} %shard_map.77.refs_3_.refs_4_.refs_2_, ...), custom_call_target="tpu_custom_call" | custom-call | flops 1024 | bytes 1024 | tf_op jit(solution)/shard_map/pallas_call | solution.py:89
  53.5 2.5 %shard_map.86 = (f32[512,256]{1,0:T(8,128)S(1)}, f32[512,256]{1,0:T(8,128)S(1)}) custom-call(s32[2]{0:T(128)S(1)} %pad_add_fusion.info_ref.refs_0_, bf16[1024,1024]{1,0:T(8,128)(2,1)S(1)} %get-tuple-element.109.refs_7_.refs_1_, bf16[1024,1024]{1,0:T(8,128)(2,1)S(1)} %get-tuple-element.123.refs_2_, f32[512,128]{1,0:T(8,128)S(1)} %get-tuple-element.94.refs_1_.refs_3_, ...), custom_call_target="tpu_custom_call" | custom-call | flops 1024 | bytes 1024 | tf_op jit(solution)/shard_map/pallas_call | solution.py:89
  56.0 1.4 collective-permute-start.15
  58.6 1.5 collective-permute-start.13
  60.1 6.1 %collective-permute-done.14.refs_4_.refs_10_.refs_17_.refs_8_ = f32[512,128]{1,0:T(8,128)S(1)} collective-permute-done((f32[512,128]{1,0:T(8,128)S(1)}, f32[512,128]{1,0:T(8,128)S(1)}, u32[]{:S(2)}, u32[]{:S(2)}) %collective-permute-start.14) | collective-permute-done | bytes 262176 | tf_op jit(solution)/shard_map/ppermute | solution.py:476
  66.4 3.7 %collective-permute-done.15.refs_6_ = f32[512,256]{1,0:T(8,128)S(1)} collective-permute-done((f32[512,256]{1,0:T(8,128)S(1)}, f32[512,256]{1,0:T(8,128)S(1)}, u32[]{:S(2)}, u32[]{:S(2)}) %collective-permute-start.15) | collective-permute-done | bytes 524320 | tf_op jit(solution)/shard_map/ppermute | solution.py:65
  70.7 1.5 collective-permute-start.17
  72.8 2.7 %collective-permute-start.18 = (f32[256,256]{1,0:T(8,128)S(1)}, f32[256,256]{1,0:T(8,128)S(1)}, u32[]{:S(2)}, u32[]{:S(2)}) collective-permute-start(f32[256,256]{1,0:T(8,128)S(1)} %get-tuple-element.132), channel_id=1, source_target_pairs={{0,4},{1,5},{2,6},{3,7},{4,0},{5,1},{6,2},{7,3},{8,12},{9,13},{10,... | collective-permute-start | bytes 786440 | tf_op jit(solution)/shard_map/ppermute | solution.py:65
  75.5 2.8 %collective-permute-done.17.refs_18_.refs_2_.refs_9_.refs_16_ = f32[512,128]{1,0:T(8,128)S(1)} collective-permute-done((f32[512,128]{1,0:T(8,128)S(1)}, f32[512,128]{1,0:T(8,128)S(1)}, u32[]{:S(2)}, u32[]{:S(2)}) %collective-permute-start.17) | collective-permute-done | bytes 262176 | tf_op jit(solution)/shard_map/ppermute | solution.py:476
  78.3 1.2 collective-permute-done.16.refs_14_.refs_1_.refs_5_.refs_12_
  79.5 2.4 %shard_map.89 = (f32[512,256]{1,0:T(8,128)S(1)}, f32[512,256]{1,0:T(8,128)S(1)}) custom-call(s32[2]{0:T(128)S(1)} %pad_add_fusion.info_ref.refs_0_, bf16[1024,1024]{1,0:T(8,128)(2,1)S(1)} %get-tuple-element.109.refs_7_.refs_1_, bf16[1024,1024]{1,0:T(8,128)(2,1)S(1)} %get-tuple-element.123.refs_2_, f32[512,128]{1,0:T(8,128)S(1)} %get-tuple-element.110.refs_4_.refs_3_, ...), custom_call_target="tpu_custom_call" | custom-call | flops 1024 | bytes 1024 | tf_op jit(solution)/shard_map/pallas_call | solution.py:89
  82.0 4.5 %collective-permute-done.18.refs_4_ = f32[256,256]{1,0:T(8,128)S(1)} collective-permute-done((f32[256,256]{1,0:T(8,128)S(1)}, f32[256,256]{1,0:T(8,128)S(1)}, u32[]{:S(2)}, u32[]{:S(2)}) %collective-permute-start.18) | collective-permute-done | bytes 262176 | tf_op jit(solution)/shard_map/ppermute | solution.py:65
  87.2 2.0 collective-permute-start.21
  89.2 1.1 shard_map.91.refs_11_.refs_12_
  90.2 4.5 %shard_map.92 = (f32[128,512]{1,0:T(8,128)S(1)}, f32[2,128,512]{2,1,0:T(8,128)S(1)}, bf16[2,256,256]{2,1,0:T(8,128)(2,1)S(1)}, bf16[2,256,256]{2,1,0:T(8,128)(2,...) custom-call(s32[2]{0:T(128)S(1)} %pad_add_fusion.info_ref.refs_0_, ...), custom_call_target="tpu_custom_call" | custom-call | flops 1024 | bytes 1024 | tf_op jit(solution)/shard_map/pallas_call | solution.py:89
  94.7 1.1 collective-permute-start.23
  95.8 1.7 collective-permute-start.24
  98.3 1.0 collective-permute-start.20
  99.3 21.0 %collective-permute-done.20.refs_1_.refs_6_.refs_13_ = f32[512,128]{1,0:T(8,128)S(1)} collective-permute-done((f32[512,128]{1,0:T(8,128)S(1)}, f32[512,128]{1,0:T(8,128)S(1)}, u32[]{:S(2)}, u32[]{:S(2)}) %collective-permute-start.20) | collective-permute-done | bytes 262176 | tf_op jit(solution)/shard_map/ppermute | solution.py:476
  121.5 1.6 collective-permute-start.28
  123.1 3.4 %collective-permute-start.26 = (f32[256,256]{1,0:T(8,128)S(1)}, f32[256,256]{1,0:T(8,128)S(1)}, u32[]{:S(2)}, u32[]{:S(2)}) collective-permute-start(f32[256,256]{1,0:T(8,128)S(1)} %get-tuple-element.146), channel_id=1, source_target_pairs={{0,4},{1,5},{2,6},{3,7},{4,0},{5,1},{6,2},{7,3},{8,12},{9,13},{10,... | collective-permute-start | bytes 786440 | tf_op jit(solution)/shard_map/ppermute | solution.py:65
  126.5 1.3 collective-permute-done.29.refs_18_
  128.2 2.4 %shard_map.94 = (f32[512,256]{1,0:T(8,128)S(1)}, f32[512,256]{1,0:T(8,128)S(1)}) custom-call(s32[2]{0:T(128)S(1)} %pad_add_fusion.info_ref.refs_0_, bf16[1024,1024]{1,0:T(8,128)(2,1)S(1)} %get-tuple-element.109.refs_7_.refs_1_, bf16[1024,1024]{1,0:T(8,128)(2,1)S(1)} %get-tuple-element.123.refs_2_, f32[512,128]{1,0:T(8,128)S(1)} %get-tuple-element.126.refs_7_.refs_3_, ...), custom_call_target="tpu_custom_call" | custom-call | flops 1024 | bytes 1024 | tf_op jit(solution)/shard_map/pallas_call | solution.py:89
  130.7 2.4 %collective-permute-start.31 = (f32[512,256]{1,0:T(8,128)S(1)}, f32[512,256]{1,0:T(8,128)S(1)}, u32[]{:S(2)}, u32[]{:S(2)}) collective-permute-start(f32[512,256]{1,0:T(8,128)S(1)} %get-tuple-element.154.refs_3_), channel_id=1, source_target_pairs={{0,2},{1,3},{2,0},{3,1},{4,6},{5,7},{6,4},{7,5},{8,10},{9,11},{10,... | collective-permute-start | bytes 1572872 | tf_op jit(solution)/shard_map/ppermute | solution.py:65
  133.2 19.0 %collective-permute-done.27.refs_4_ = f32[3,64,256]{2,1,0:T(8,128)S(1)} collective-permute-done((f32[3,64,256]{2,1,0:T(8,128)S(1)}, f32[3,64,256]{2,1,0:T(8,128)S(1)}, u32[]{:S(2)}, u32[]{:S(2)}) %collective-permute-start.27) | collective-permute-done | bytes 196640 | tf_op jit(solution)/shard_map/ppermute | solution.py:65
  152.8 1.0 shard_map.96.refs_13_.refs_14_
  153.8 2.0 shard_map.97
  156.5 1.1 collective-permute-start.34
  157.6 1.8 collective-permute-start.35
  159.9 6.0 %collective-permute-done.32.refs_4_ = f32[3,32,256]{2,1,0:T(8,128)S(1)} collective-permute-done((f32[3,32,256]{2,1,0:T(8,128)S(1)}, f32[3,32,256]{2,1,0:T(8,128)S(1)}, u32[]{:S(2)}, u32[]{:S(2)}) %collective-permute-start.32) | collective-permute-done | bytes 98336 | tf_op jit(solution)/shard_map/ppermute | solution.py:65
  165.9 3.8 %collective-permute-done.34.refs_7_ = f32[2,128,256]{2,1,0:T(8,128)S(1)} collective-permute-done((f32[2,128,256]{2,1,0:T(8,128)S(1)}, f32[2,128,256]{2,1,0:T(8,128)S(1)}, u32[]{:S(2)}, u32[]{:S(2)}) %collective-permute-start.34) | collective-permute-done | bytes 262176 | tf_op jit(solution)/shard_map/ppermute | solution.py:65
  170.3 0.8 collective-permute-start.36
  171.2 2.5 %collective-permute-start.38 = (f32[2,64,256]{2,1,0:T(8,128)S(1)}, f32[2,64,256]{2,1,0:T(8,128)S(1)}, u32[]{:S(2)}, u32[]{:S(2)}) collective-permute-start(f32[2,64,256]{2,1,0:T(8,128)S(1)} %get-tuple-element.174), channel_id=1, source_target_pairs={{0,2},{1,3},{2,0},{3,1},{4,6},{5,7},{6,4},{7,5},{8,10},{9,11},{10,... | collective-permute-start | bytes 393224 | tf_op jit(solution)/shard_map/ppermute | solution.py:65
  174.9 4.0 %collective-permute-done.38.refs_6_ = f32[2,64,256]{2,1,0:T(8,128)S(1)} collective-permute-done((f32[2,64,256]{2,1,0:T(8,128)S(1)}, f32[2,64,256]{2,1,0:T(8,128)S(1)}, u32[]{:S(2)}, u32[]{:S(2)}) %collective-permute-start.38) | collective-permute-done | bytes 131104 | tf_op jit(solution)/shard_map/ppermute | solution.py:65
  178.9 4.3 %collective-permute-done.36.refs_2_ = f32[256,256]{1,0:T(8,128)S(1)} collective-permute-done((f32[256,256]{1,0:T(8,128)S(1)}, f32[256,256]{1,0:T(8,128)S(1)}, u32[]{:S(2)}, u32[]{:S(2)}) %collective-permute-start.36) | collective-permute-done | bytes 262176 | tf_op jit(solution)/shard_map/ppermute | solution.py:65
  183.9 1.8 collective-permute-start.43
  185.8 1.7 collective-permute-start.42
  187.4 3.2 %collective-permute-done.40.refs_2_ = f32[2,32,256]{2,1,0:T(8,128)S(1)} collective-permute-done((f32[2,32,256]{2,1,0:T(8,128)S(1)}, f32[2,32,256]{2,1,0:T(8,128)S(1)}, u32[]{:S(2)}, u32[]{:S(2)}) %collective-permute-start.40) | collective-permute-done | bytes 65568 | tf_op jit(solution)/shard_map/ppermute | solution.py:65
  191.3 1.6 collective-permute-start.41
  192.9 1.5 shard_map.101.refs_3_
  194.4 1.1 copy-done.1
  196.1 1.2 collective-permute-start.47
  197.3 0.9 collective-permute-start.46
  198.2 1.5 collective-permute-start.45
  199.7 2.1 %collective-permute-done.47.refs_10_ = f32[2,16,512]{2,1,0:T(8,128)S(1)} collective-permute-done((f32[2,16,512]{2,1,0:T(8,128)S(1)}, f32[2,16,512]{2,1,0:T(8,128)S(1)}, u32[]{:S(2)}, u32[]{:S(2)}) %collective-permute-start.47) | collective-permute-done | bytes 65568 | tf_op jit(solution)/shard_map/ppermute | solution.py:65
  202.6 1.5 shard_map.103
  (76 shorter events, 19.2 us)
Async XLA Ops:
  0.6 21.7 %collective-permute-start.6 = (f32[1024,512]{1,0:T(8,128)}, f32[1024,512]{1,0:T(8,128)S(1)}, u32[]{:S(2)}, u32[]{:S(2)}) collective-permute-start(f32[1024,512]{1,0:T(8,128)} %refs_1_.8), channel_id=1, source_target_pairs={{0,1},{1,0},{2,3},{3,2},{4,5},{5,4},{6,7},{7,6},{8,9},{9,8},{10,11... | collective-permute-start | bytes 6291464 | tf_op jit(solution)/shard_map/ppermute | solution.py:65
  1.1 16.4 %collective-permute-start.2 = (f32[1,2,64,512]{3,2,1,0:T(8,128)}, f32[1,2,64,512]{3,2,1,0:T(8,128)S(1)}, u32[]{:S(2)}, u32[]{:S(2)}) collective-permute-start(f32[1,2,64,512]{3,2,1,0:T(8,128)} %bitcast.3), channel_id=1, source_target_pairs={{0,4},{1,5},{2,6},{3,7},{4,0},{5,1},{6,2},{7,3},{8,12},{9,13},{10,... | collective-permute-start | bytes 786440 | tf_op jit(solution)/shard_map/ppermute | solution.py:65
  4.9 0.7 copy-start.5
  5.6 5.7 %copy-start = (f32[3,1024,512]{2,1,0:T(8,128)S(1)}, f32[3,1024,512]{2,1,0:T(8,128)}, u32[]{:S(2)}) copy-start(f32[3,1024,512]{2,1,0:T(8,128)} %refs_2_.7) | copy-start | bytes 18874372
  8.4 9.1 %collective-permute-start.1 = (f32[512,128]{1,0:T(8,128)S(1)}, f32[512,128]{1,0:T(8,128)S(1)}, u32[]{:S(2)}, u32[]{:S(2)}) collective-permute-start(f32[512,128]{1,0:T(8,128)S(1)} %get-tuple-element.105.refs_7_), channel_id=1, source_target_pairs={{8,0},{24,8},{16,24},{0,16},{9,1},{25,9},{17,25},{1,17},{2,10},{18... | collective-permute-start | bytes 786440 | tf_op jit(solution)/shard_map/ppermute | solution.py:476
  10.0 8.1 %collective-permute-start = (f32[512,128]{1,0:T(8,128)S(1)}, f32[512,128]{1,0:T(8,128)S(1)}, u32[]{:S(2)}, u32[]{:S(2)}) collective-permute-start(f32[512,128]{1,0:T(8,128)S(1)} %get-tuple-element.94.refs_1_.refs_3_), channel_id=1, source_target_pairs={{0,8},{8,24},{24,16},{16,0},{1,9},{9,25},{25,17},{17,1},{10,2},{2,... | collective-permute-start | bytes 786440 | tf_op jit(solution)/shard_map/ppermute | solution.py:476
  11.3 6.8 %copy-start.4 = (f32[2,64,512]{2,1,0:T(8,128)S(1)}, f32[2,64,512]{2,1,0:T(8,128)}, u32[]{:S(2)}) copy-start(f32[2,64,512]{2,1,0:T(8,128)} %param.7) | copy-start | bytes 786436
  13.5 8.8 %copy-start.3 = (f32[1024,512]{1,0:T(8,128)S(1)}, f32[1024,512]{1,0:T(8,128)}, u32[]{:S(2)}) copy-start(f32[1024,512]{1,0:T(8,128)} %refs_1_.8) | copy-start | bytes 6291460
  18.7 13.2 %collective-permute-start.5 = (f32[2,2,64,512]{3,2,1,0:T(8,128)S(1)}, f32[2,2,64,512]{3,2,1,0:T(8,128)S(1)}, u32[]{:S(2)}, u32[]{:S(2)}) collective-permute-start(f32[2,2,64,512]{3,2,1,0:T(8,128)S(1)} %get-tuple-element.108.refs_5_), channel_id=1, source_target_pairs={{0,2},{1,3},{2,0},{3,1},{4,6},{5,7},{6,4},{7,5},{8,10},{9,11},{10,... | collective-permute-start | bytes 1572872 | tf_op jit(solution)/shard_map/ppermute | solution.py:65
  20.3 6.9 %collective-permute-start.4 = (f32[512,128]{1,0:T(8,128)S(1)}, f32[512,128]{1,0:T(8,128)S(1)}, u32[]{:S(2)}, u32[]{:S(2)}) collective-permute-start(f32[512,128]{1,0:T(8,128)S(1)} %get-tuple-element.107.refs_15_), channel_id=1, source_target_pairs={{8,0},{24,8},{16,24},{0,16},{9,1},{25,9},{17,25},{1,17},{2,10},{18... | collective-permute-start | bytes 786440 | tf_op jit(solution)/shard_map/ppermute | solution.py:476
  20.9 7.5 %collective-permute-start.3 = (f32[512,128]{1,0:T(8,128)S(1)}, f32[512,128]{1,0:T(8,128)S(1)}, u32[]{:S(2)}, u32[]{:S(2)}) collective-permute-start(f32[512,128]{1,0:T(8,128)S(1)} %get-tuple-element.106.refs_3_.refs_11_), channel_id=1, source_target_pairs={{0,8},{8,24},{24,16},{16,0},{1,9},{9,25},{25,17},{17,1},{10,2},{2,... | collective-permute-start | bytes 786440 | tf_op jit(solution)/shard_map/ppermute | solution.py:476
  32.6 9.9 %collective-permute-start.9 = (f32[4,2,64,512]{3,2,1,0:T(8,128)S(1)}, f32[4,2,64,512]{3,2,1,0:T(8,128)S(1)}, u32[]{:S(2)}, u32[]{:S(2)}) collective-permute-start(f32[4,2,64,512]{3,2,1,0:T(8,128)S(1)} %get-tuple-element.112.refs_5_), channel_id=1, source_target_pairs={{0,1},{1,0},{2,3},{3,2},{4,5},{5,4},{6,7},{7,6},{8,9},{9,8},{10,11... | collective-permute-start | bytes 3145736 | tf_op jit(solution)/shard_map/ppermute | solution.py:65
  32.7 8.7 %collective-permute-start.8 = (f32[512,128]{1,0:T(8,128)S(1)}, f32[512,128]{1,0:T(8,128)S(1)}, u32[]{:S(2)}, u32[]{:S(2)}) collective-permute-start(f32[512,128]{1,0:T(8,128)S(1)} %get-tuple-element.111.refs_7_), channel_id=1, source_target_pairs={{8,0},{24,8},{16,24},{0,16},{9,1},{25,9},{17,25},{1,17},{2,10},{18... | collective-permute-start | bytes 786440 | tf_op jit(solution)/shard_map/ppermute | solution.py:476
  34.1 8.4 %collective-permute-start.7 = (f32[512,128]{1,0:T(8,128)S(1)}, f32[512,128]{1,0:T(8,128)S(1)}, u32[]{:S(2)}, u32[]{:S(2)}) collective-permute-start(f32[512,128]{1,0:T(8,128)S(1)} %get-tuple-element.110.refs_4_.refs_3_), channel_id=1, source_target_pairs={{0,8},{8,24},{24,16},{16,0},{1,9},{9,25},{25,17},{17,1},{10,2},{2,... | collective-permute-start | bytes 786440 | tf_op jit(solution)/shard_map/ppermute | solution.py:476
  42.5 2.8 %copy-start.2 = (f32[3,64,512]{2,1,0:T(8,128)S(1)}, f32[3,64,512]{2,1,0:T(8,128)}, u32[]{:S(2)}) copy-start(f32[3,64,512]{2,1,0:T(8,128)} %refs_1_.13) | copy-start | bytes 1179652
  43.3 10.3 %collective-permute-start.12 = (f32[512,128]{1,0:T(8,128)S(1)}, f32[512,128]{1,0:T(8,128)S(1)}, u32[]{:S(2)}, u32[]{:S(2)}) collective-permute-start(f32[512,128]{1,0:T(8,128)S(1)} %get-tuple-element.122.refs_15_), channel_id=1, source_target_pairs={{8,0},{24,8},{16,24},{0,16},{9,1},{25,9},{17,25},{1,17},{2,10},{18... | collective-permute-start | bytes 786440 | tf_op jit(solution)/shard_map/ppermute | solution.py:476
  44.8 8.7 %collective-permute-start.11 = (f32[512,128]{1,0:T(8,128)S(1)}, f32[512,128]{1,0:T(8,128)S(1)}, u32[]{:S(2)}, u32[]{:S(2)}) collective-permute-start(f32[512,128]{1,0:T(8,128)S(1)} %get-tuple-element.115.refs_7_.refs_11_), channel_id=1, source_target_pairs={{0,8},{8,24},{24,16},{16,0},{1,9},{9,25},{25,17},{17,1},{10,2},{2,... | collective-permute-start | bytes 786440 | tf_op jit(solution)/shard_map/ppermute | solution.py:476
  45.4 1.4 collective-permute-start.10
  56.0 14.1 %collective-permute-start.15 = (f32[512,256]{1,0:T(8,128)S(1)}, f32[512,256]{1,0:T(8,128)S(1)}, u32[]{:S(2)}, u32[]{:S(2)}) collective-permute-start(f32[512,256]{1,0:T(8,128)S(1)} %get-tuple-element.128), channel_id=1, source_target_pairs={{0,2},{1,3},{2,0},{3,1},{4,6},{5,7},{6,4},{7,5},{8,10},{9,11},{10,... | collective-permute-start | bytes 1572872 | tf_op jit(solution)/shard_map/ppermute | solution.py:65
  58.0 8.1 %collective-permute-start.14 = (f32[512,128]{1,0:T(8,128)S(1)}, f32[512,128]{1,0:T(8,128)S(1)}, u32[]{:S(2)}, u32[]{:S(2)}) collective-permute-start(f32[512,128]{1,0:T(8,128)S(1)} %get-tuple-element.127.refs_7_), channel_id=1, source_target_pairs={{8,0},{24,8},{16,24},{0,16},{9,1},{25,9},{17,25},{1,17},{2,10},{18... | collective-permute-start | bytes 786440 | tf_op jit(solution)/shard_map/ppermute | solution.py:476
  58.6 7.8 %collective-permute-start.13 = (f32[512,128]{1,0:T(8,128)S(1)}, f32[512,128]{1,0:T(8,128)S(1)}, u32[]{:S(2)}, u32[]{:S(2)}) collective-permute-start(f32[512,128]{1,0:T(8,128)S(1)} %get-tuple-element.126.refs_7_.refs_3_), channel_id=1, source_target_pairs={{0,8},{8,24},{24,16},{16,0},{1,9},{9,25},{25,17},{17,1},{10,2},{2,... | collective-permute-start | bytes 786440 | tf_op jit(solution)/shard_map/ppermute | solution.py:476
  70.7 7.6 %collective-permute-start.17 = (f32[512,128]{1,0:T(8,128)S(1)}, f32[512,128]{1,0:T(8,128)S(1)}, u32[]{:S(2)}, u32[]{:S(2)}) collective-permute-start(f32[512,128]{1,0:T(8,128)S(1)} %get-tuple-element.130.refs_15_), channel_id=1, source_target_pairs={{8,0},{24,8},{16,24},{0,16},{9,1},{25,9},{17,25},{1,17},{2,10},{18... | collective-permute-start | bytes 786440 | tf_op jit(solution)/shard_map/ppermute | solution.py:476
  72.3 7.3 %collective-permute-start.16 = (f32[512,128]{1,0:T(8,128)S(1)}, f32[512,128]{1,0:T(8,128)S(1)}, u32[]{:S(2)}, u32[]{:S(2)}) collective-permute-start(f32[512,128]{1,0:T(8,128)S(1)} %get-tuple-element.129.refs_19_.refs_11_), channel_id=1, source_target_pairs={{0,8},{8,24},{24,16},{16,0},{1,9},{9,25},{25,17},{17,1},{10,2},{2,... | collective-permute-start | bytes 786440 | tf_op jit(solution)/shard_map/ppermute | solution.py:476
  72.8 13.7 %collective-permute-start.18 = (f32[256,256]{1,0:T(8,128)S(1)}, f32[256,256]{1,0:T(8,128)S(1)}, u32[]{:S(2)}, u32[]{:S(2)}) collective-permute-start(f32[256,256]{1,0:T(8,128)S(1)} %get-tuple-element.132), channel_id=1, source_target_pairs={{0,4},{1,5},{2,6},{3,7},{4,0},{5,1},{6,2},{7,3},{8,12},{9,13},{10,... | collective-permute-start | bytes 786440 | tf_op jit(solution)/shard_map/ppermute | solution.py:65
  87.1 3.1 %copy-start.6 = (s32[3,8]{1,0:T(4,128)S(1)}, s32[3,8]{1,0:T(4,128)}, u32[]{:S(2)}) copy-start(s32[3,8]{1,0:T(4,128)} %refs_1_.12) | copy-start | bytes 292
  87.1 3.1 %collective-permute-start.19 = (f32[256,256]{1,0:T(8,128)S(1)}, f32[256,256]{1,0:T(8,128)S(1)}, u32[]{:S(2)}, u32[]{:S(2)}) collective-permute-start(f32[256,256]{1,0:T(8,128)S(1)} %get-tuple-element.134.refs_9_), channel_id=1, source_target_pairs={{0,1},{1,0},{2,3},{3,2},{4,5},{5,4},{6,7},{7,6},{8,9},{9,8},{10,11... | collective-permute-start | bytes 786440 | tf_op jit(solution)/shard_map/ppermute | solution.py:65
  87.2 11.1 %collective-permute-start.21 = (f32[512,128]{1,0:T(8,128)S(1)}, f32[512,128]{1,0:T(8,128)S(1)}, u32[]{:S(2)}, u32[]{:S(2)}) collective-permute-start(f32[512,128]{1,0:T(8,128)S(1)} %get-tuple-element.140), channel_id=1, source_target_pairs={{8,0},{24,8},{16,24},{0,16},{9,1},{25,9},{17,25},{1,17},{2,10},{18... | collective-permute-start | bytes 786440 | tf_op jit(solution)/shard_map/ppermute | solution.py:476
  89.2 31.1 %collective-permute-start.22 = (f32[512,256]{1,0:T(8,128)S(1)}, f32[512,256]{1,0:T(8,128)S(1)}, u32[]{:S(2)}, u32[]{:S(2)}) collective-permute-start(f32[512,256]{1,0:T(8,128)S(1)} %get-tuple-element.136.refs_3_), channel_id=1, source_target_pairs={{0,2},{1,3},{2,0},{3,1},{4,6},{5,7},{6,4},{7,5},{8,10},{9,11},{10,... | collective-permute-start | bytes 1572872 | tf_op jit(solution)/shard_map/ppermute | solution.py:65
  94.7 25.6 %collective-permute-start.23 = (f32[3,128,256]{2,1,0:T(8,128)S(1)}, f32[3,128,256]{2,1,0:T(8,128)S(1)}, u32[]{:S(2)}, u32[]{:S(2)}) collective-permute-start(f32[3,128,256]{2,1,0:T(8,128)S(1)} %get-tuple-element.142), channel_id=1, source_target_pairs={{0,8},{8,0},{16,24},{24,16},{1,9},{9,1},{17,25},{25,17},{2,10},{10... | collective-permute-start | bytes 1179656 | tf_op jit(solution)/shard_map/ppermute | solution.py:65
  95.8 24.5 %collective-permute-start.24 = (f32[3,128,256]{2,1,0:T(8,128)S(1)}, f32[3,128,256]{2,1,0:T(8,128)S(1)}, u32[]{:S(2)}, u32[]{:S(2)}) collective-permute-start(f32[3,128,256]{2,1,0:T(8,128)S(1)} %get-tuple-element.143), channel_id=1, source_target_pairs={{0,16},{8,24},{16,0},{24,8},{1,17},{9,25},{17,1},{25,9},{2,18},{10... | collective-permute-start | bytes 1179656 | tf_op jit(solution)/shard_map/ppermute | solution.py:65
  97.5 22.8 %collective-permute-start.25 = (f32[3,128,256]{2,1,0:T(8,128)S(1)}, f32[3,128,256]{2,1,0:T(8,128)S(1)}, u32[]{:S(2)}, u32[]{:S(2)}) collective-permute-start(f32[3,128,256]{2,1,0:T(8,128)S(1)} %get-tuple-element.144), channel_id=1, source_target_pairs={{0,24},{8,16},{16,8},{24,0},{1,25},{9,17},{17,9},{25,1},{2,26},{10... | collective-permute-start | bytes 1179656 | tf_op jit(solution)/shard_map/ppermute | solution.py:65
  98.3 22.0 %collective-permute-start.20 = (f32[512,128]{1,0:T(8,128)S(1)}, f32[512,128]{1,0:T(8,128)S(1)}, u32[]{:S(2)}, u32[]{:S(2)}) collective-permute-start(f32[512,128]{1,0:T(8,128)S(1)} %get-tuple-element.137.refs_4_), channel_id=1, source_target_pairs={{0,8},{8,24},{24,16},{16,0},{1,9},{9,25},{25,17},{17,1},{10,2},{2,... | collective-permute-start | bytes 786440 | tf_op jit(solution)/shard_map/ppermute | solution.py:476
  121.1 6.8 %collective-permute-start.29 = (f32[512,128]{1,0:T(8,128)S(1)}, f32[512,128]{1,0:T(8,128)S(1)}, u32[]{:S(2)}, u32[]{:S(2)}) collective-permute-start(f32[512,128]{1,0:T(8,128)S(1)} %get-tuple-element.150), channel_id=1, source_target_pairs={{8,0},{24,8},{16,24},{0,16},{9,1},{25,9},{17,25},{1,17},{2,10},{18... | collective-permute-start | bytes 786440 | tf_op jit(solution)/shard_map/ppermute | solution.py:476
  121.5 6.7 %collective-permute-start.28 = (f32[512,128]{1,0:T(8,128)S(1)}, f32[512,128]{1,0:T(8,128)S(1)}, u32[]{:S(2)}, u32[]{:S(2)}) collective-permute-start(f32[512,128]{1,0:T(8,128)S(1)} %get-tuple-element.149.refs_19_), channel_id=1, source_target_pairs={{0,8},{8,24},{24,16},{16,0},{1,9},{9,25},{25,17},{17,1},{10,2},{2,... | collective-permute-start | bytes 786440 | tf_op jit(solution)/shard_map/ppermute | solution.py:476
  123.1 29.0 %collective-permute-start.26 = (f32[256,256]{1,0:T(8,128)S(1)}, f32[256,256]{1,0:T(8,128)S(1)}, u32[]{:S(2)}, u32[]{:S(2)}) collective-permute-start(f32[256,256]{1,0:T(8,128)S(1)} %get-tuple-element.146), channel_id=1, source_target_pairs={{0,4},{1,5},{2,6},{3,7},{4,0},{5,1},{6,2},{7,3},{8,12},{9,13},{10,... | collective-permute-start | bytes 786440 | tf_op jit(solution)/shard_map/ppermute | solution.py:65
  130.7 39.0 %collective-permute-start.31 = (f32[512,256]{1,0:T(8,128)S(1)}, f32[512,256]{1,0:T(8,128)S(1)}, u32[]{:S(2)}, u32[]{:S(2)}) collective-permute-start(f32[512,256]{1,0:T(8,128)S(1)} %get-tuple-element.154.refs_3_), channel_id=1, source_target_pairs={{0,2},{1,3},{2,0},{3,1},{4,6},{5,7},{6,4},{7,5},{8,10},{9,11},{10,... | collective-permute-start | bytes 1572872 | tf_op jit(solution)/shard_map/ppermute | solution.py:65
  133.1 19.1 %collective-permute-start.27 = (f32[3,64,256]{2,1,0:T(8,128)S(1)}, f32[3,64,256]{2,1,0:T(8,128)S(1)}, u32[]{:S(2)}, u32[]{:S(2)}) collective-permute-start(f32[3,64,256]{2,1,0:T(8,128)S(1)} %get-tuple-element.148), channel_id=1, source_target_pairs={{0,2},{1,3},{2,0},{3,1},{4,6},{5,7},{6,4},{7,5},{8,10},{9,11},{10,... | collective-permute-start | bytes 589832 | tf_op jit(solution)/shard_map/ppermute | solution.py:65
  155.8 10.1 %collective-permute-start.33 = (f32[2,128,256]{2,1,0:T(8,128)S(1)}, f32[2,128,256]{2,1,0:T(8,128)S(1)}, u32[]{:S(2)}, u32[]{:S(2)}) collective-permute-start(f32[2,128,256]{2,1,0:T(8,128)S(1)} %get-tuple-element.166), channel_id=1, source_target_pairs={{0,8},{8,0},{16,24},{24,16},{1,9},{9,1},{17,25},{25,17},{2,10},{10... | collective-permute-start | bytes 786440 | tf_op jit(solution)/shard_map/ppermute | solution.py:65
  156.5 13.2 %collective-permute-start.34 = (f32[2,128,256]{2,1,0:T(8,128)S(1)}, f32[2,128,256]{2,1,0:T(8,128)S(1)}, u32[]{:S(2)}, u32[]{:S(2)}) collective-permute-start(f32[2,128,256]{2,1,0:T(8,128)S(1)} %get-tuple-element.167), channel_id=1, source_target_pairs={{0,16},{8,24},{16,0},{24,8},{1,17},{9,25},{17,1},{25,9},{2,18},{10... | collective-permute-start | bytes 786440 | tf_op jit(solution)/shard_map/ppermute | solution.py:65
  157.6 12.1 %collective-permute-start.35 = (f32[2,128,256]{2,1,0:T(8,128)S(1)}, f32[2,128,256]{2,1,0:T(8,128)S(1)}, u32[]{:S(2)}, u32[]{:S(2)}) collective-permute-start(f32[2,128,256]{2,1,0:T(8,128)S(1)} %get-tuple-element.168), channel_id=1, source_target_pairs={{0,24},{8,16},{16,8},{24,0},{1,25},{9,17},{17,9},{25,1},{2,26},{10... | collective-permute-start | bytes 786440 | tf_op jit(solution)/shard_map/ppermute | solution.py:65
  159.4 6.5 %collective-permute-start.32 = (f32[3,32,256]{2,1,0:T(8,128)S(1)}, f32[3,32,256]{2,1,0:T(8,128)S(1)}, u32[]{:S(2)}, u32[]{:S(2)}) collective-permute-start(f32[3,32,256]{2,1,0:T(8,128)S(1)} %get-tuple-element.156), channel_id=1, source_target_pairs={{0,4},{1,5},{2,6},{3,7},{4,0},{5,1},{6,2},{7,3},{8,12},{9,13},{10,... | collective-permute-start | bytes 294920 | tf_op jit(solution)/shard_map/ppermute | solution.py:65
  170.3 12.9 %collective-permute-start.36 = (f32[256,256]{1,0:T(8,128)S(1)}, f32[256,256]{1,0:T(8,128)S(1)}, u32[]{:S(2)}, u32[]{:S(2)}) collective-permute-start(f32[256,256]{1,0:T(8,128)S(1)} %get-tuple-element.170), channel_id=1, source_target_pairs={{0,4},{1,5},{2,6},{3,7},{4,0},{5,1},{6,2},{7,3},{8,12},{9,13},{10,... | collective-permute-start | bytes 786440 | tf_op jit(solution)/shard_map/ppermute | solution.py:65
  171.2 7.8 %collective-permute-start.38 = (f32[2,64,256]{2,1,0:T(8,128)S(1)}, f32[2,64,256]{2,1,0:T(8,128)S(1)}, u32[]{:S(2)}, u32[]{:S(2)}) collective-permute-start(f32[2,64,256]{2,1,0:T(8,128)S(1)} %get-tuple-element.174), channel_id=1, source_target_pairs={{0,2},{1,3},{2,0},{3,1},{4,6},{5,7},{6,4},{7,5},{8,10},{9,11},{10,... | collective-permute-start | bytes 393224 | tf_op jit(solution)/shard_map/ppermute | solution.py:65
  173.6 1.2 collective-permute-start.37
  173.6 17.7 %collective-permute-start.30 = (f32[128,256]{1,0:T(8,128)S(1)}, f32[128,256]{1,0:T(8,128)S(1)}, u32[]{:S(2)}, u32[]{:S(2)}) collective-permute-start(f32[128,256]{1,0:T(8,128)S(1)} %get-tuple-element.153), channel_id=1, source_target_pairs={{0,1},{1,0},{2,3},{3,2},{4,5},{5,4},{6,7},{7,6},{8,9},{9,8},{10,11... | collective-permute-start | bytes 393224 | tf_op jit(solution)/shard_map/ppermute | solution.py:65
  183.8 9.1 %collective-permute-start.39 = (f32[128,256]{1,0:T(8,128)S(1)}, f32[128,256]{1,0:T(8,128)S(1)}, u32[]{:S(2)}, u32[]{:S(2)}) collective-permute-start(f32[128,256]{1,0:T(8,128)S(1)} %get-tuple-element.176), channel_id=1, source_target_pairs={{0,1},{1,0},{2,3},{3,2},{4,5},{5,4},{6,7},{7,6},{8,9},{9,8},{10,11... | collective-permute-start | bytes 393224 | tf_op jit(solution)/shard_map/ppermute | solution.py:65
  183.9 6.8 %collective-permute-start.40 = (f32[2,32,256]{2,1,0:T(8,128)S(1)}, f32[2,32,256]{2,1,0:T(8,128)S(1)}, u32[]{:S(2)}, u32[]{:S(2)}) collective-permute-start(f32[2,32,256]{2,1,0:T(8,128)S(1)} %get-tuple-element.178), channel_id=1, source_target_pairs={{0,4},{1,5},{2,6},{3,7},{4,0},{5,1},{6,2},{7,3},{8,12},{9,13},{10,... | collective-permute-start | bytes 196616 | tf_op jit(solution)/shard_map/ppermute | solution.py:65
  183.9 14.2 %collective-permute-start.43 = (f32[3,16,512]{2,1,0:T(8,128)S(1)}, f32[3,16,512]{2,1,0:T(8,128)S(1)}, u32[]{:S(2)}, u32[]{:S(2)}) collective-permute-start(f32[3,16,512]{2,1,0:T(8,128)S(1)} %get-tuple-element.181.refs_3_), channel_id=1, source_target_pairs={{0,24},{8,16},{16,8},{24,0},{1,25},{9,17},{17,9},{25,1},{2,26},{10... | collective-permute-start | bytes 294920 | tf_op jit(solution)/shard_map/ppermute | solution.py:65
  185.8 13.9 %collective-permute-start.42 = (f32[3,16,512]{2,1,0:T(8,128)S(1)}, f32[3,16,512]{2,1,0:T(8,128)S(1)}, u32[]{:S(2)}, u32[]{:S(2)}) collective-permute-start(f32[3,16,512]{2,1,0:T(8,128)S(1)} %get-tuple-element.181.refs_3_), channel_id=1, source_target_pairs={{0,16},{8,24},{16,0},{24,8},{1,17},{9,25},{17,1},{25,9},{2,18},{10... | collective-permute-start | bytes 294920 | tf_op jit(solution)/shard_map/ppermute | solution.py:65
  191.2 3.2 %collective-permute-start.44 = (f32[2,16,256]{2,1,0:T(8,128)S(1)}, f32[2,16,256]{2,1,0:T(8,128)S(1)}, u32[]{:S(2)}, u32[]{:S(2)}) collective-permute-start(f32[2,16,256]{2,1,0:T(8,128)S(1)} %get-tuple-element.182), channel_id=1, source_target_pairs={{0,1},{1,0},{2,3},{3,2},{4,5},{5,4},{6,7},{7,6},{8,9},{9,8},{10,11... | collective-permute-start | bytes 98312 | tf_op jit(solution)/shard_map/ppermute | solution.py:65
  191.3 8.4 %collective-permute-start.41 = (f32[3,16,512]{2,1,0:T(8,128)S(1)}, f32[3,16,512]{2,1,0:T(8,128)S(1)}, u32[]{:S(2)}, u32[]{:S(2)}) collective-permute-start(f32[3,16,512]{2,1,0:T(8,128)S(1)} %get-tuple-element.181.refs_3_), channel_id=1, source_target_pairs={{0,8},{8,0},{16,24},{24,16},{1,9},{9,1},{17,25},{25,17},{2,10},{10... | collective-permute-start | bytes 294920 | tf_op jit(solution)/shard_map/ppermute | solution.py:65
  194.4 1.1 copy-start.1
  196.1 5.6 %collective-permute-start.47 = (f32[2,16,512]{2,1,0:T(8,128)S(1)}, f32[2,16,512]{2,1,0:T(8,128)S(1)}, u32[]{:S(2)}, u32[]{:S(2)}) collective-permute-start(f32[2,16,512]{2,1,0:T(8,128)S(1)} %shard_map.102.refs_7_.refs_11_), channel_id=1, source_target_pairs={{0,24},{8,16},{16,8},{24,0},{1,25},{9,17},{17,9},{25,1},{2,26},{10... | collective-permute-start | bytes 196616 | tf_op jit(solution)/shard_map/ppermute | solution.py:65
  197.3 5.3 %collective-permute-start.46 = (f32[2,16,512]{2,1,0:T(8,128)S(1)}, f32[2,16,512]{2,1,0:T(8,128)S(1)}, u32[]{:S(2)}, u32[]{:S(2)}) collective-permute-start(f32[2,16,512]{2,1,0:T(8,128)S(1)} %shard_map.102.refs_7_.refs_11_), channel_id=1, source_target_pairs={{0,16},{8,24},{16,0},{24,8},{1,17},{9,25},{17,1},{25,9},{2,18},{10... | collective-permute-start | bytes 196616 | tf_op jit(solution)/shard_map/ppermute | solution.py:65
  198.2 4.4 %collective-permute-start.45 = (f32[2,16,512]{2,1,0:T(8,128)S(1)}, f32[2,16,512]{2,1,0:T(8,128)S(1)}, u32[]{:S(2)}, u32[]{:S(2)}) collective-permute-start(f32[2,16,512]{2,1,0:T(8,128)S(1)} %shard_map.102.refs_7_.refs_11_), channel_id=1, source_target_pairs={{0,8},{8,0},{16,24},{24,16},{1,9},{9,1},{17,25},{25,17},{2,10},{10... | collective-permute-start | bytes 196616 | tf_op jit(solution)/shard_map/ppermute | solution.py:65

commit v8 on v7

--- a/solution.py
+++ b/solution.py
@@ -98,8 +98,9 @@
     return list(results)
 
 
-def cut_kernel(ratio, cuts, info_ref, listed_ref, factors_ref, *refs):
-    *outs, sems = refs
+def cut_kernel(ratio, cuts, info_ref, listed_ref, factors_ref, slices_ref, *refs):
+    *outs, through_ref, sems = refs
+    through_ref[0] = slices_ref[...]
     size, unit = outs[0].shape
     width = factors_ref.shape[2]
     column = info_ref[1]
@@ -424,7 +425,7 @@
     diag_width = width // col_count
     part = diag_width // row_count
     half = width // 2
-    cuts = 2
+    cuts = 1
     unit = half // cuts
     chunk_count = members * cuts
     order = reversed_bits(levels)
@@ -445,8 +446,8 @@
 
     flat = call(
         functools.partial(cut_kernel, ratio, cuts),
-        [shape(cols_here, unit)] * (chunk_count * 2),
-        [info, listed, factor_cols],
+        [shape(cols_here, unit)] * (chunk_count * 2) + [shape(1, *parent_factor.shape)],
+        [info, listed, factor_cols, parent_factor],
         smem=2, hbm=1, vmem=48,
         scratch=[pltpu.SemaphoreType.DMA((chunk_count * 2,))],
     )
@@ -476,7 +477,7 @@
             received.append([lax.ppermute(moving[way], AXES, rings[way]) for way in range(2)])
 
     def link_flow():
-        gathered = parent_factor[None]
+        gathered = flat[-1]
         for bit in reversed(range(col_bits)):
             arrived = swap(gathered, "col", col_count, 1 << bit)
             dims = (2 * gathered.shape[0],) + parent_factor.shape
@@ -579,10 +580,14 @@
     def total_flow(pieces):
         count, size, _ = pieces[0].shape
         inputs = [pieces[0]] + [swap(pieces[d], "row", row_count, d) for d in range(1, row_count)]
-        for bit in [*range(1, col_bits), 0]:
-            size //= 2
-            keep, send = yield (halve_step, inputs, [shape(count, size, half)] * 2)
-            inputs = [keep, swap(send, "col", col_count, 1 << bit)]
+        size //= levels
+        pieces = yield (halve_step, inputs, [shape(count, size, half)] * levels)
+        inputs = [pieces[0]]
+        for at in range(1, levels):
+            inputs.append(swap(pieces[at], "col", col_count, order[at] << 1))
+        size //= 2
+        keep, send = yield (halve_step, inputs, [shape(count, size, half)] * 2)
+        inputs = [keep, swap(send, "col", col_count, 1)]
         (piece,) = yield (join_step, inputs, [shape(count, size, width)])
         return [piece] + [swap(piece, "row", row_count, d) for d in range(1, row_count)]
 
@@ -614,6 +619,7 @@
             + [held[name] for name in names],
             smem=1, vmem=20,
         )
+        yield WAIT
         held["child totals"] = yield from total_flow(pieces)
 
     def column_flow():

time: 204 us -> 173 us (0.85)
  waiting for transfers between devices: 104 us -> 79.6 us
  starting transfers between devices: 53.7 us -> 48.1 us
    ppermute x16 -> x10, waiting for transfers between devices: 43.4 us -> 28.7 us  [ring_flow(): lax.ppermute(moving[way], AXES, rings[way])]
    ppermute x32 -> x34, waiting for transfers between devices: 61.1 us -> 50.9 us  [swap(): lax.ppermute(value, axis, [(place, place ^ change) for place in range(siz...]
    ppermute x16 -> x10, starting transfers between devices: 17.5 us -> 12 us  [ring_flow(): lax.ppermute(moving[way], AXES, rings[way])]
    pallas_call x28 -> x25, Pallas kernels: 43 us -> 41.2 us  [call(): pl.pallas_call(inner, out_shape=outs, in_specs=[pl.BlockSpec(memory_space...]
    ppermute x32 -> x34, starting transfers between devices: 36.3 us -> 36.1 us  [swap(): lax.ppermute(value, axis, [(place, place ^ change) for place in range(siz...]
  transfers between devices with their start and end apart: 48 -> 44, of which waited for: 26 -> 22; matrix products, arithmetic and copies ran while one was open for 0% -> 0% of each run, Pallas kernels for 17% -> 21%
where the time goes in v8:
time: 173 us
  waiting for transfers between devices  79.6 us (46%)
  starting transfers between devices  48.1 us (28%)
  Pallas kernels  41.2 us (24%)
  local copies, waits for them, and re-layouts  2.79 us (2%)
    ppermute x34, waiting for transfers between devices, swap(): lax.ppermute(value, axis, [(place, place ^ change) for place in range(siz...  50.9 us
    pallas_call x25, Pallas kernels, call(): pl.pallas_call(inner, out_shape=outs, in_specs=[pl.BlockSpec(memory_space...  41.2 us
    ppermute x34, starting transfers between devices, swap(): lax.ppermute(value, axis, [(place, place ^ change) for place in range(siz...  36.1 us
    ppermute x10, waiting for transfers between devices, ring_flow(): lax.ppermute(moving[way], AXES, rings[way])  28.7 us
    ppermute x10, starting transfers between devices, ring_flow(): lax.ppermute(moving[way], AXES, rings[way])  12 us
  transfers between devices with their start and end apart: 44, of which 22 were waited for; matrix products, arithmetic and copies ran while one was open for 0% of the time, Pallas kernels for 21%

profile of v8, /device:TPU:0, one launch (start us, length us, event | category | flops | bytes accessed | tf_op | source)
XLA Modules:
  0.0 172.7 jit_solution(7733985590955354403)
XLA Ops:
  1.2 0.9 copy-done.4
  2.2 0.7 copy-done.5
  2.9 2.8 %shard_map.76 = (f32[512,256]{1,0:T(8,128)S(1)}, f32[512,256]{1,0:T(8,128)S(1)}, f32[512,256]{1,0:T(8,128)S(1)}, f32[512,256]{1,0:T(8,128)S(1)}, f32[512,256]{1,...) custom-call(s32[2]{0:T(128)S(1)} %pad_add_fusion.info_ref.refs_0_, s32[3,8]{1,0:T(4,128)S(1)} %copy-done.5, ...), custom_call_target="tpu_custom_call" | custom-call | flops 1024 | bytes 1024 | tf_op jit(solution)/shard_map/pallas_call | solution.py:89
  5.6 2.6 %collective-permute-start.1 = (f32[512,256]{1,0:T(8,128)S(1)}, f32[512,256]{1,0:T(8,128)S(1)}, u32[]{:S(2)}, u32[]{:S(2)}) collective-permute-start(f32[512,256]{1,0:T(8,128)S(1)} %get-tuple-element.92.refs_7_), channel_id=1, source_target_pairs={{8,0},{24,8},{16,24},{0,16},{9,1},{25,9},{17,25},{1,17},{2,10},{18... | collective-permute-start | bytes 1572872 | tf_op jit(solution)/shard_map/ppermute | solution.py:477
  8.3 3.1 %collective-permute-start.2 = (f32[1,2,64,512]{3,2,1,0:T(8,128)S(1)}, f32[1,2,64,512]{3,2,1,0:T(8,128)S(1)}, u32[]{:S(2)}, u32[]{:S(2)}) collective-permute-start(f32[1,2,64,512]{3,2,1,0:T(8,128)S(1)} %get-tuple-element.93.refs_5_), channel_id=1, source_target_pairs={{0,4},{1,5},{2,6},{3,7},{4,0},{5,1},{6,2},{7,3},{8,12},{9,13},{10,... | collective-permute-start | bytes 786440 | tf_op jit(solution)/shard_map/ppermute | solution.py:65
  11.3 0.8 shard_map.77.refs_3_.refs_4_.refs_2_
  12.1 2.2 %shard_map.78 = (bf16[3,256,512]{2,1,0:T(8,128)(2,1)S(1)}, bf16[3,256,512]{2,1,0:T(8,128)(2,1)S(1)}, bf16[3,512,256]{2,1,0:T(8,128)(2,1)S(1)}, bf16[3,512,256]{2,1,0:T(8,128)(2,1)S(1)}) custom-call(s32[2]{0:T(128)S(1)} %pad_add_fusion.info_ref.refs_0_, s32[3,8]{1,0:T(4,128)S(1)} %copy-done.6, f32[3,1024,512]{2,1,0:T(8,128)S(1)} %copy-done, ...), custom_call_target="tpu_custom_call" | custom-call | flops 1024 | bytes 1024 | tf_op jit(solution)/shard_map/pallas_call | solution.py:89
  14.4 8.9 %collective-permute-done.2.refs_6_ = f32[1,2,64,512]{3,2,1,0:T(8,128)S(1)} collective-permute-done((f32[1,2,64,512]{3,2,1,0:T(8,128)S(1)}, f32[1,2,64,512]{3,2,1,0:T(8,128)S(1)}, u32[]{:S(2)}, u32[]{:S(2)}) %collective-permute-start.2) | collective-permute-done | bytes 262176 | tf_op jit(solution)/shard_map/ppermute | solution.py:65
  23.3 0.7 shard_map.79
  24.0 1.6 collective-permute-start.4
  26.3 1.5 collective-permute-start.3
  27.8 1.7 shard_map.80
  29.5 7.8 %collective-permute-done.4.refs_4_.refs_9_.refs_8_ = f32[512,256]{1,0:T(8,128)S(1)} collective-permute-done((f32[512,256]{1,0:T(8,128)S(1)}, f32[512,256]{1,0:T(8,128)S(1)}, u32[]{:S(2)}, u32[]{:S(2)}) %collective-permute-start.4) | collective-permute-done | bytes 524320 | tf_op jit(solution)/shard_map/ppermute | solution.py:477
  37.3 1.0 collective-permute-done.5.refs_6_
  38.3 1.3 collective-permute-done.3.refs_3_.refs_5_.refs_4_
  39.6 0.7 shard_map.81
  41.0 1.5 collective-permute-start.7
  42.5 2.2 %shard_map.82 = (bf16[512,1024]{1,0:T(8,128)(2,1)S(1)}, bf16[512,1024]{1,0:T(8,128)(2,1)S(1)}) custom-call(s32[2]{0:T(128)S(1)} %pad_add_fusion.info_ref.refs_0_, s32[3,8]{1,0:T(4,128)S(1)} %copy-done.6, f32[3,1024,512]{2,1,0:T(8,128)S(1)} %copy-done, bf16[512,512]{1,0:T(8,128)(2,1)S(1)} %shard_map.77.refs_3_.refs_4_.refs_2_, ...), custom_call_target="tpu_custom_call" | custom-call | flops 1024 | bytes 1024 | tf_op jit(solution)/shard_map/pallas_call | solution.py:89
  44.7 10.0 %collective-permute-done.8.refs_10_.refs_2_.refs_9_.refs_8_ = f32[512,256]{1,0:T(8,128)S(1)} collective-permute-done((f32[512,256]{1,0:T(8,128)S(1)}, f32[512,256]{1,0:T(8,128)S(1)}, u32[]{:S(2)}, u32[]{:S(2)}) %collective-permute-start.8) | collective-permute-done | bytes 524320 | tf_op jit(solution)/shard_map/ppermute | solution.py:477
  55.0 2.4 %shard_map.83 = (f32[512,256]{1,0:T(8,128)S(1)}, f32[512,256]{1,0:T(8,128)S(1)}) custom-call(s32[2]{0:T(128)S(1)} %pad_add_fusion.info_ref.refs_0_, bf16[1024,1024]{1,0:T(8,128)(2,1)S(1)} %get-tuple-element.97.refs_7_.refs_1_, bf16[1024,1024]{1,0:T(8,128)(2,1)S(1)} %get-tuple-element.101.refs_2_, f32[512,256]{1,0:T(8,128)S(1)} %get-tuple-element.83.refs_1_.refs_3_, ...), custom_call_target="tpu_custom_call" | custom-call | flops 1024 | bytes 1024 | tf_op jit(solution)/shard_map/pallas_call | solution.py:89
  57.4 0.7 shard_map.84
  58.2 1.6 collective-permute-start.12
  60.3 1.3 collective-permute-start.13
  61.6 1.3 collective-permute-done.10.refs_3_
  63.0 4.5 %shard_map.85 = (bf16[2,512,512]{2,1,0:T(8,128)(2,1)S(1)}, bf16[2,512,512]{2,1,0:T(8,128)(2,1)S(1)}, bf16[2,512,256]{2,1,0:T(8,128)(2,1)S(1)}, bf16[2,512,256]{2...) custom-call(s32[2]{0:T(128)S(1)} %pad_add_fusion.info_ref.refs_0_, ...), custom_call_target="tpu_custom_call" | custom-call | flops 1024 | bytes 1024 | tf_op jit(solution)/shard_map/pallas_call | solution.py:89
  67.5 2.2 %shard_map.86 = (bf16[512,1024]{1,0:T(8,128)(2,1)S(1)}, bf16[512,1024]{1,0:T(8,128)(2,1)S(1)}) custom-call(s32[2]{0:T(128)S(1)} %pad_add_fusion.info_ref.refs_0_, s32[3,8]{1,0:T(4,128)S(1)} %copy-done.6, f32[3,1024,512]{2,1,0:T(8,128)S(1)} %copy-done, bf16[512,512]{1,0:T(8,128)(2,1)S(1)} %shard_map.77.refs_3_.refs_4_.refs_2_, ...), custom_call_target="tpu_custom_call" | custom-call | flops 1024 | bytes 1024 | tf_op jit(solution)/shard_map/pallas_call | solution.py:89
  69.7 1.8 %collective-permute-done.12.refs_10_.refs_2_.refs_9_ = f32[512,256]{1,0:T(8,128)S(1)} collective-permute-done((f32[512,256]{1,0:T(8,128)S(1)}, f32[512,256]{1,0:T(8,128)S(1)}, u32[]{:S(2)}, u32[]{:S(2)}) %collective-permute-start.12) | collective-permute-done | bytes 524320 | tf_op jit(solution)/shard_map/ppermute | solution.py:477
  71.5 1.2 collective-permute-done.11.refs_6_.refs_1_.refs_5_
  72.6 2.4 %shard_map.87 = (f32[512,256]{1,0:T(8,128)S(1)}, f32[512,256]{1,0:T(8,128)S(1)}) custom-call(s32[2]{0:T(128)S(1)} %pad_add_fusion.info_ref.refs_0_, bf16[1024,1024]{1,0:T(8,128)(2,1)S(1)} %get-tuple-element.97.refs_7_.refs_1_, bf16[1024,1024]{1,0:T(8,128)(2,1)S(1)} %get-tuple-element.101.refs_2_, f32[512,256]{1,0:T(8,128)S(1)} %get-tuple-element.94.refs_3_, ...), custom_call_target="tpu_custom_call" | custom-call | flops 1024 | bytes 1024 | tf_op jit(solution)/shard_map/pallas_call | solution.py:89
  75.7 1.5 collective-permute-start.17
  78.2 3.4 %collective-permute-start.14 = (f32[256,256]{1,0:T(8,128)S(1)}, f32[256,256]{1,0:T(8,128)S(1)}, u32[]{:S(2)}, u32[]{:S(2)}) collective-permute-start(f32[256,256]{1,0:T(8,128)S(1)} %get-tuple-element.113), channel_id=1, source_target_pairs={{0,4},{1,5},{2,6},{3,7},{4,0},{5,1},{6,2},{7,3},{8,12},{9,13},{10,... | collective-permute-start | bytes 786440 | tf_op jit(solution)/shard_map/ppermute | solution.py:65
  81.5 1.0 shard_map.89.refs_11_.refs_12_
  82.6 5.2 %collective-permute-done.17.refs_10_ = f32[512,256]{1,0:T(8,128)S(1)} collective-permute-done((f32[512,256]{1,0:T(8,128)S(1)}, f32[512,256]{1,0:T(8,128)S(1)}, u32[]{:S(2)}, u32[]{:S(2)}) %collective-permute-start.17) | collective-permute-done | bytes 524320 | tf_op jit(solution)/shard_map/ppermute | solution.py:477
  87.7 1.2 collective-permute-done.16.refs_6_
  89.0 2.5 %shard_map.90 = (f32[512,256]{1,0:T(8,128)S(1)}, f32[512,256]{1,0:T(8,128)S(1)}) custom-call(s32[2]{0:T(128)S(1)} %pad_add_fusion.info_ref.refs_0_, bf16[1024,1024]{1,0:T(8,128)(2,1)S(1)} %get-tuple-element.97.refs_7_.refs_1_, bf16[1024,1024]{1,0:T(8,128)(2,1)S(1)} %get-tuple-element.101.refs_2_, f32[512,256]{1,0:T(8,128)S(1)} %get-tuple-element.98.refs_4_.refs_3_, ...), custom_call_target="tpu_custom_call" | custom-call | flops 1024 | bytes 1024 | tf_op jit(solution)/shard_map/pallas_call | solution.py:89
  91.4 1.3 collective-permute-done.14.refs_2_
  92.7 2.1 %collective-permute-done.15.refs_4_ = f32[512,256]{1,0:T(8,128)S(1)} collective-permute-done((f32[512,256]{1,0:T(8,128)S(1)}, f32[512,256]{1,0:T(8,128)S(1)}, u32[]{:S(2)}, u32[]{:S(2)}) %collective-permute-start.15) | collective-permute-done | bytes 524320 | tf_op jit(solution)/shard_map/ppermute | solution.py:65
  95.5 3.4 %collective-permute-start.20 = (f32[512,256]{1,0:T(8,128)S(1)}, f32[512,256]{1,0:T(8,128)S(1)}, u32[]{:S(2)}, u32[]{:S(2)}) collective-permute-start(f32[512,256]{1,0:T(8,128)S(1)} %get-tuple-element.121.refs_3_), channel_id=1, source_target_pairs={{0,2},{1,3},{2,0},{3,1},{4,6},{5,7},{6,4},{7,5},{8,10},{9,11},{10,... | collective-permute-start | bytes 1572872 | tf_op jit(solution)/shard_map/ppermute | solution.py:65
  99.0 1.0 shard_map.92.refs_11_.refs_13_
  100.0 4.5 %shard_map.93 = (f32[128,512]{1,0:T(8,128)S(1)}, f32[2,128,512]{2,1,0:T(8,128)S(1)}, bf16[2,256,256]{2,1,0:T(8,128)(2,1)S(1)}, bf16[2,256,256]{2,1,0:T(8,128)(2,...) custom-call(s32[2]{0:T(128)S(1)} %pad_add_fusion.info_ref.refs_0_, ...), custom_call_target="tpu_custom_call" | custom-call | flops 1024 | bytes 1024 | tf_op jit(solution)/shard_map/pallas_call | solution.py:89
  104.5 1.6 collective-permute-start.21
  106.7 1.3 collective-permute-start.23
  108.5 2.0 %shard_map.94 = (f32[2,128,256]{2,1,0:T(8,128)S(1)}, f32[2,128,256]{2,1,0:T(8,128)S(1)}, f32[2,128,256]{2,1,0:T(8,128)S(1)}, f32[2,128,256]{2,1,0:T(8,128)S(1)}) custom-call(s32[2]{0:T(128)S(1)} %pad_add_fusion.info_ref.refs_0_, bf16[3,256,512]{2,1,0:T(8,128)(2,1)S(1)} %get-tuple-element.84.refs_7_.refs_5_.refs_3_.refs_1_, ...), custom_call_target="tpu_custom_call" | custom-call | flops 1024 | bytes 1024 | tf_op jit(solution)/shard_map/pallas_call | solution.py:89
  110.5 11.6 %collective-permute-done.19.refs_2_ = f32[256,256]{1,0:T(8,128)S(1)} collective-permute-done((f32[256,256]{1,0:T(8,128)S(1)}, f32[256,256]{1,0:T(8,128)S(1)}, u32[]{:S(2)}, u32[]{:S(2)}) %collective-permute-start.19) | collective-permute-done | bytes 262176 | tf_op jit(solution)/shard_map/ppermute | solution.py:65
  122.1 1.5 collective-permute-start.29
  124.3 1.3 collective-permute-start.31
  125.6 0.8 shard_map.95
  126.7 2.7 %collective-permute-start.26 = (f32[3,32,256]{2,1,0:T(8,128)S(1)}, f32[3,32,256]{2,1,0:T(8,128)S(1)}, u32[]{:S(2)}, u32[]{:S(2)}) collective-permute-start(f32[3,32,256]{2,1,0:T(8,128)S(1)} %get-tuple-element.143), channel_id=1, source_target_pairs={{0,4},{1,5},{2,6},{3,7},{4,0},{5,1},{6,2},{7,3},{8,12},{9,13},{10,... | collective-permute-start | bytes 294920 | tf_op jit(solution)/shard_map/ppermute | solution.py:65
  129.4 2.0 %collective-permute-done.29.refs_8_ = f32[2,128,256]{2,1,0:T(8,128)S(1)} collective-permute-done((f32[2,128,256]{2,1,0:T(8,128)S(1)}, f32[2,128,256]{2,1,0:T(8,128)S(1)}, u32[]{:S(2)}, u32[]{:S(2)}) %collective-permute-start.29) | collective-permute-done | bytes 262176 | tf_op jit(solution)/shard_map/ppermute | solution.py:65
  131.4 5.5 %collective-permute-done.30.refs_9_ = f32[2,128,256]{2,1,0:T(8,128)S(1)} collective-permute-done((f32[2,128,256]{2,1,0:T(8,128)S(1)}, f32[2,128,256]{2,1,0:T(8,128)S(1)}, u32[]{:S(2)}, u32[]{:S(2)}) %collective-permute-start.30) | collective-permute-done | bytes 262176 | tf_op jit(solution)/shard_map/ppermute | solution.py:65
  136.8 8.7 %collective-permute-done.26.refs_4_ = f32[3,32,256]{2,1,0:T(8,128)S(1)} collective-permute-done((f32[3,32,256]{2,1,0:T(8,128)S(1)}, f32[3,32,256]{2,1,0:T(8,128)S(1)}, u32[]{:S(2)}, u32[]{:S(2)}) %collective-permute-start.26) | collective-permute-done | bytes 98336 | tf_op jit(solution)/shard_map/ppermute | solution.py:65
  146.3 1.9 %collective-permute-start.34 = (f32[2,32,256]{2,1,0:T(8,128)S(1)}, f32[2,32,256]{2,1,0:T(8,128)S(1)}, u32[]{:S(2)}, u32[]{:S(2)}) collective-permute-start(f32[2,32,256]{2,1,0:T(8,128)S(1)} %get-tuple-element.154), channel_id=1, source_target_pairs={{0,4},{1,5},{2,6},{3,7},{4,0},{5,1},{6,2},{7,3},{8,12},{9,13},{10,... | collective-permute-start | bytes 196616 | tf_op jit(solution)/shard_map/ppermute | solution.py:65
  148.2 0.8 collective-permute-start.35
  149.0 2.3 %collective-permute-start.36 = (f32[2,32,256]{2,1,0:T(8,128)S(1)}, f32[2,32,256]{2,1,0:T(8,128)S(1)}, u32[]{:S(2)}, u32[]{:S(2)}) collective-permute-start(f32[2,32,256]{2,1,0:T(8,128)S(1)} %get-tuple-element.156), channel_id=1, source_target_pairs={{0,6},{1,7},{2,4},{3,5},{4,2},{5,3},{6,0},{7,1},{8,14},{9,15},{10,... | collective-permute-start | bytes 196616 | tf_op jit(solution)/shard_map/ppermute | solution.py:65
  151.8 1.3 collective-permute-done.35.refs_5_
  153.1 3.4 %collective-permute-done.36.refs_6_ = f32[2,32,256]{2,1,0:T(8,128)S(1)} collective-permute-done((f32[2,32,256]{2,1,0:T(8,128)S(1)}, f32[2,32,256]{2,1,0:T(8,128)S(1)}, u32[]{:S(2)}, u32[]{:S(2)}) %collective-permute-start.36) | collective-permute-done | bytes 65568 | tf_op jit(solution)/shard_map/ppermute | solution.py:65
  157.1 2.3 %collective-permute-start.39 = (f32[3,16,512]{2,1,0:T(8,128)S(1)}, f32[3,16,512]{2,1,0:T(8,128)S(1)}, u32[]{:S(2)}, u32[]{:S(2)}) collective-permute-start(f32[3,16,512]{2,1,0:T(8,128)S(1)} %get-tuple-element.157.refs_8_.refs_3_), channel_id=1, source_target_pairs={{0,24},{8,16},{16,8},{24,0},{1,25},{9,17},{17,9},{25,1},{2,26},{10... | collective-permute-start | bytes 294920 | tf_op jit(solution)/shard_map/ppermute | solution.py:65
  159.4 0.7 collective-permute-start.38
  160.7 1.5 shard_map.98.refs_3_
  162.2 1.1 copy-done.1
  163.9 2.3 %collective-permute-start.43 = (f32[2,16,512]{2,1,0:T(8,128)S(1)}, f32[2,16,512]{2,1,0:T(8,128)S(1)}, u32[]{:S(2)}, u32[]{:S(2)}) collective-permute-start(f32[2,16,512]{2,1,0:T(8,128)S(1)} %shard_map.99.refs_7_.refs_11_), channel_id=1, source_target_pairs={{0,24},{8,16},{16,8},{24,0},{1,25},{9,17},{17,9},{25,1},{2,26},{10... | collective-permute-start | bytes 196616 | tf_op jit(solution)/shard_map/ppermute | solution.py:65
  167.5 1.7 %collective-permute-done.43.refs_10_ = f32[2,16,512]{2,1,0:T(8,128)S(1)} collective-permute-done((f32[2,16,512]{2,1,0:T(8,128)S(1)}, f32[2,16,512]{2,1,0:T(8,128)S(1)}, u32[]{:S(2)}, u32[]{:S(2)}) %collective-permute-start.43) | collective-permute-done | bytes 65568 | tf_op jit(solution)/shard_map/ppermute | solution.py:65
  169.2 1.3 collective-permute-done.42.refs_9_
  171.1 1.6 shard_map.100
  (65 shorter events, 12.1 us)
Async XLA Ops:
  0.6 27.2 %collective-permute-start.6 = (f32[1024,512]{1,0:T(8,128)}, f32[1024,512]{1,0:T(8,128)S(1)}, u32[]{:S(2)}, u32[]{:S(2)}) collective-permute-start(f32[1024,512]{1,0:T(8,128)} %refs_1_.8), channel_id=1, source_target_pairs={{0,1},{1,0},{2,3},{3,2},{4,5},{5,4},{6,7},{7,6},{8,9},{9,8},{10,11... | collective-permute-start | bytes 6291464 | tf_op jit(solution)/shard_map/ppermute | solution.py:65
  1.2 0.9 copy-start.4
  2.2 0.7 copy-start.5
  2.9 9.3 %copy-start = (f32[3,1024,512]{2,1,0:T(8,128)S(1)}, f32[3,1024,512]{2,1,0:T(8,128)}, u32[]{:S(2)}) copy-start(f32[3,1024,512]{2,1,0:T(8,128)} %refs_2_.7) | copy-start | bytes 18874372
  2.9 9.3 %copy-start.6 = (s32[3,8]{1,0:T(4,128)S(1)}, s32[3,8]{1,0:T(4,128)}, u32[]{:S(2)}) copy-start(s32[3,8]{1,0:T(4,128)} %refs_1_.12) | copy-start | bytes 292
  5.6 17.7 %collective-permute-start.1 = (f32[512,256]{1,0:T(8,128)S(1)}, f32[512,256]{1,0:T(8,128)S(1)}, u32[]{:S(2)}, u32[]{:S(2)}) collective-permute-start(f32[512,256]{1,0:T(8,128)S(1)} %get-tuple-element.92.refs_7_), channel_id=1, source_target_pairs={{8,0},{24,8},{16,24},{0,16},{9,1},{25,9},{17,25},{1,17},{2,10},{18... | collective-permute-start | bytes 1572872 | tf_op jit(solution)/shard_map/ppermute | solution.py:477
  8.2 15.1 %collective-permute-start = (f32[512,256]{1,0:T(8,128)S(1)}, f32[512,256]{1,0:T(8,128)S(1)}, u32[]{:S(2)}, u32[]{:S(2)}) collective-permute-start(f32[512,256]{1,0:T(8,128)S(1)} %get-tuple-element.83.refs_1_.refs_3_), channel_id=1, source_target_pairs={{0,8},{8,24},{24,16},{16,0},{1,9},{9,25},{25,17},{17,1},{10,2},{2,... | collective-permute-start | bytes 1572872 | tf_op jit(solution)/shard_map/ppermute | solution.py:477
  8.3 15.1 %collective-permute-start.2 = (f32[1,2,64,512]{3,2,1,0:T(8,128)S(1)}, f32[1,2,64,512]{3,2,1,0:T(8,128)S(1)}, u32[]{:S(2)}, u32[]{:S(2)}) collective-permute-start(f32[1,2,64,512]{3,2,1,0:T(8,128)S(1)} %get-tuple-element.93.refs_5_), channel_id=1, source_target_pairs={{0,4},{1,5},{2,6},{3,7},{4,0},{5,1},{6,2},{7,3},{8,12},{9,13},{10,... | collective-permute-start | bytes 786440 | tf_op jit(solution)/shard_map/ppermute | solution.py:65
  14.4 13.5 %copy-start.3 = (f32[1024,512]{1,0:T(8,128)S(1)}, f32[1024,512]{1,0:T(8,128)}, u32[]{:S(2)}) copy-start(f32[1024,512]{1,0:T(8,128)} %refs_1_.8) | copy-start | bytes 6291460
  24.0 13.3 %collective-permute-start.4 = (f32[512,256]{1,0:T(8,128)S(1)}, f32[512,256]{1,0:T(8,128)S(1)}, u32[]{:S(2)}, u32[]{:S(2)}) collective-permute-start(f32[512,256]{1,0:T(8,128)S(1)} %get-tuple-element.95.refs_7_), channel_id=1, source_target_pairs={{8,0},{24,8},{16,24},{0,16},{9,1},{25,9},{17,25},{1,17},{2,10},{18... | collective-permute-start | bytes 1572872 | tf_op jit(solution)/shard_map/ppermute | solution.py:477
  25.7 12.6 %collective-permute-start.5 = (f32[2,2,64,512]{3,2,1,0:T(8,128)S(1)}, f32[2,2,64,512]{3,2,1,0:T(8,128)S(1)}, u32[]{:S(2)}, u32[]{:S(2)}) collective-permute-start(f32[2,2,64,512]{3,2,1,0:T(8,128)S(1)} %get-tuple-element.96.refs_5_), channel_id=1, source_target_pairs={{0,2},{1,3},{2,0},{3,1},{4,6},{5,7},{6,4},{7,5},{8,10},{9,11},{10,... | collective-permute-start | bytes 1572872 | tf_op jit(solution)/shard_map/ppermute | solution.py:65
  26.3 13.3 %collective-permute-start.3 = (f32[512,256]{1,0:T(8,128)S(1)}, f32[512,256]{1,0:T(8,128)S(1)}, u32[]{:S(2)}, u32[]{:S(2)}) collective-permute-start(f32[512,256]{1,0:T(8,128)S(1)} %get-tuple-element.94.refs_3_), channel_id=1, source_target_pairs={{0,8},{8,24},{24,16},{16,0},{1,9},{9,25},{25,17},{17,1},{10,2},{2,... | collective-permute-start | bytes 1572872 | tf_op jit(solution)/shard_map/ppermute | solution.py:477
  40.3 17.1 %collective-permute-start.9 = (f32[4,2,64,512]{3,2,1,0:T(8,128)S(1)}, f32[4,2,64,512]{3,2,1,0:T(8,128)S(1)}, u32[]{:S(2)}, u32[]{:S(2)}) collective-permute-start(f32[4,2,64,512]{3,2,1,0:T(8,128)S(1)} %get-tuple-element.100.refs_3_), channel_id=1, source_target_pairs={{0,1},{1,0},{2,3},{3,2},{4,5},{5,4},{6,7},{7,6},{8,9},{9,8},{10,11... | collective-permute-start | bytes 3145736 | tf_op jit(solution)/shard_map/ppermute | solution.py:65
  40.4 14.3 %collective-permute-start.8 = (f32[512,256]{1,0:T(8,128)S(1)}, f32[512,256]{1,0:T(8,128)S(1)}, u32[]{:S(2)}, u32[]{:S(2)}) collective-permute-start(f32[512,256]{1,0:T(8,128)S(1)} %get-tuple-element.99.refs_7_), channel_id=1, source_target_pairs={{8,0},{24,8},{16,24},{0,16},{9,1},{25,9},{17,25},{1,17},{2,10},{18... | collective-permute-start | bytes 1572872 | tf_op jit(solution)/shard_map/ppermute | solution.py:477
  41.0 14.0 %collective-permute-start.7 = (f32[512,256]{1,0:T(8,128)S(1)}, f32[512,256]{1,0:T(8,128)S(1)}, u32[]{:S(2)}, u32[]{:S(2)}) collective-permute-start(f32[512,256]{1,0:T(8,128)S(1)} %get-tuple-element.98.refs_4_.refs_3_), channel_id=1, source_target_pairs={{0,8},{8,24},{24,16},{16,0},{1,9},{9,25},{25,17},{17,1},{10,2},{2,... | collective-permute-start | bytes 1572872 | tf_op jit(solution)/shard_map/ppermute | solution.py:477
  57.4 4.1 %copy-start.2 = (f32[3,64,512]{2,1,0:T(8,128)S(1)}, f32[3,64,512]{2,1,0:T(8,128)}, u32[]{:S(2)}) copy-start(f32[3,64,512]{2,1,0:T(8,128)} %refs_1_.13) | copy-start | bytes 1179652
  58.2 13.3 %collective-permute-start.12 = (f32[512,256]{1,0:T(8,128)S(1)}, f32[512,256]{1,0:T(8,128)S(1)}, u32[]{:S(2)}, u32[]{:S(2)}) collective-permute-start(f32[512,256]{1,0:T(8,128)S(1)} %get-tuple-element.108), channel_id=1, source_target_pairs={{8,0},{24,8},{16,24},{0,16},{9,1},{25,9},{17,25},{1,17},{2,10},{18... | collective-permute-start | bytes 1572872 | tf_op jit(solution)/shard_map/ppermute | solution.py:477
  59.7 12.9 %collective-permute-start.11 = (f32[512,256]{1,0:T(8,128)S(1)}, f32[512,256]{1,0:T(8,128)S(1)}, u32[]{:S(2)}, u32[]{:S(2)}) collective-permute-start(f32[512,256]{1,0:T(8,128)S(1)} %get-tuple-element.105.refs_7_), channel_id=1, source_target_pairs={{0,8},{8,24},{24,16},{16,0},{1,9},{9,25},{25,17},{17,1},{10,2},{2,... | collective-permute-start | bytes 1572872 | tf_op jit(solution)/shard_map/ppermute | solution.py:477
  60.3 14.8 %collective-permute-start.13 = (f32[512,256]{1,0:T(8,128)S(1)}, f32[512,256]{1,0:T(8,128)S(1)}, u32[]{:S(2)}, u32[]{:S(2)}) collective-permute-start(f32[512,256]{1,0:T(8,128)S(1)} %get-tuple-element.109), channel_id=1, source_target_pairs={{0,2},{1,3},{2,0},{3,1},{4,6},{5,7},{6,4},{7,5},{8,10},{9,11},{10,... | collective-permute-start | bytes 1572872 | tf_op jit(solution)/shard_map/ppermute | solution.py:65
  61.5 1.4 collective-permute-start.10
  75.7 12.0 %collective-permute-start.17 = (f32[512,256]{1,0:T(8,128)S(1)}, f32[512,256]{1,0:T(8,128)S(1)}, u32[]{:S(2)}, u32[]{:S(2)}) collective-permute-start(f32[512,256]{1,0:T(8,128)S(1)} %get-tuple-element.116), channel_id=1, source_target_pairs={{8,0},{24,8},{16,24},{0,16},{9,1},{25,9},{17,25},{1,17},{2,10},{18... | collective-permute-start | bytes 1572872 | tf_op jit(solution)/shard_map/ppermute | solution.py:477
  77.3 11.7 %collective-permute-start.16 = (f32[512,256]{1,0:T(8,128)S(1)}, f32[512,256]{1,0:T(8,128)S(1)}, u32[]{:S(2)}, u32[]{:S(2)}) collective-permute-start(f32[512,256]{1,0:T(8,128)S(1)} %get-tuple-element.115.refs_4_), channel_id=1, source_target_pairs={{0,8},{8,24},{24,16},{16,0},{1,9},{9,25},{25,17},{17,1},{10,2},{2,... | collective-permute-start | bytes 1572872 | tf_op jit(solution)/shard_map/ppermute | solution.py:477
  77.8 17.0 %collective-permute-start.15 = (f32[512,256]{1,0:T(8,128)S(1)}, f32[512,256]{1,0:T(8,128)S(1)}, u32[]{:S(2)}, u32[]{:S(2)}) collective-permute-start(f32[512,256]{1,0:T(8,128)S(1)} %get-tuple-element.114.refs_3_), channel_id=1, source_target_pairs={{0,2},{1,3},{2,0},{3,1},{4,6},{5,7},{6,4},{7,5},{8,10},{9,11},{10,... | collective-permute-start | bytes 1572872 | tf_op jit(solution)/shard_map/ppermute | solution.py:65
  78.2 14.5 %collective-permute-start.14 = (f32[256,256]{1,0:T(8,128)S(1)}, f32[256,256]{1,0:T(8,128)S(1)}, u32[]{:S(2)}, u32[]{:S(2)}) collective-permute-start(f32[256,256]{1,0:T(8,128)S(1)} %get-tuple-element.113), channel_id=1, source_target_pairs={{0,4},{1,5},{2,6},{3,7},{4,0},{5,1},{6,2},{7,3},{8,12},{9,13},{10,... | collective-permute-start | bytes 786440 | tf_op jit(solution)/shard_map/ppermute | solution.py:65
  95.5 4.5 %collective-permute-start.18 = (f32[256,256]{1,0:T(8,128)S(1)}, f32[256,256]{1,0:T(8,128)S(1)}, u32[]{:S(2)}, u32[]{:S(2)}) collective-permute-start(f32[256,256]{1,0:T(8,128)S(1)} %get-tuple-element.119.refs_4_.refs_9_), channel_id=1, source_target_pairs={{0,1},{1,0},{2,3},{3,2},{4,5},{5,4},{6,7},{7,6},{8,9},{9,8},{10,11... | collective-permute-start | bytes 786440 | tf_op jit(solution)/shard_map/ppermute | solution.py:65
  95.5 28.1 %collective-permute-start.20 = (f32[512,256]{1,0:T(8,128)S(1)}, f32[512,256]{1,0:T(8,128)S(1)}, u32[]{:S(2)}, u32[]{:S(2)}) collective-permute-start(f32[512,256]{1,0:T(8,128)S(1)} %get-tuple-element.121.refs_3_), channel_id=1, source_target_pairs={{0,2},{1,3},{2,0},{3,1},{4,6},{5,7},{6,4},{7,5},{8,10},{9,11},{10,... | collective-permute-start | bytes 1572872 | tf_op jit(solution)/shard_map/ppermute | solution.py:65
  104.5 19.9 %collective-permute-start.21 = (f32[3,128,256]{2,1,0:T(8,128)S(1)}, f32[3,128,256]{2,1,0:T(8,128)S(1)}, u32[]{:S(2)}, u32[]{:S(2)}) collective-permute-start(f32[3,128,256]{2,1,0:T(8,128)S(1)} %get-tuple-element.127), channel_id=1, source_target_pairs={{0,8},{8,0},{16,24},{24,16},{1,9},{9,1},{17,25},{25,17},{2,10},{10... | collective-permute-start | bytes 1179656 | tf_op jit(solution)/shard_map/ppermute | solution.py:65
  106.0 19.6 %collective-permute-start.22 = (f32[3,128,256]{2,1,0:T(8,128)S(1)}, f32[3,128,256]{2,1,0:T(8,128)S(1)}, u32[]{:S(2)}, u32[]{:S(2)}) collective-permute-start(f32[3,128,256]{2,1,0:T(8,128)S(1)} %get-tuple-element.128), channel_id=1, source_target_pairs={{0,16},{8,24},{16,0},{24,8},{1,17},{9,25},{17,1},{25,9},{2,18},{10... | collective-permute-start | bytes 1179656 | tf_op jit(solution)/shard_map/ppermute | solution.py:65
  106.7 18.9 %collective-permute-start.23 = (f32[3,128,256]{2,1,0:T(8,128)S(1)}, f32[3,128,256]{2,1,0:T(8,128)S(1)}, u32[]{:S(2)}, u32[]{:S(2)}) collective-permute-start(f32[3,128,256]{2,1,0:T(8,128)S(1)} %get-tuple-element.129), channel_id=1, source_target_pairs={{0,24},{8,16},{16,8},{24,0},{1,25},{9,17},{17,9},{25,1},{2,26},{10... | collective-permute-start | bytes 1179656 | tf_op jit(solution)/shard_map/ppermute | solution.py:65
  108.0 14.1 %collective-permute-start.19 = (f32[256,256]{1,0:T(8,128)S(1)}, f32[256,256]{1,0:T(8,128)S(1)}, u32[]{:S(2)}, u32[]{:S(2)}) collective-permute-start(f32[256,256]{1,0:T(8,128)S(1)} %get-tuple-element.125), channel_id=1, source_target_pairs={{0,4},{1,5},{2,6},{3,7},{4,0},{5,1},{6,2},{7,3},{8,12},{9,13},{10,... | collective-permute-start | bytes 786440 | tf_op jit(solution)/shard_map/ppermute | solution.py:65
  122.1 9.2 %collective-permute-start.29 = (f32[2,128,256]{2,1,0:T(8,128)S(1)}, f32[2,128,256]{2,1,0:T(8,128)S(1)}, u32[]{:S(2)}, u32[]{:S(2)}) collective-permute-start(f32[2,128,256]{2,1,0:T(8,128)S(1)} %get-tuple-element.146), channel_id=1, source_target_pairs={{0,8},{8,0},{16,24},{24,16},{1,9},{9,1},{17,25},{25,17},{2,10},{10... | collective-permute-start | bytes 786440 | tf_op jit(solution)/shard_map/ppermute | solution.py:65
  123.6 13.2 %collective-permute-start.30 = (f32[2,128,256]{2,1,0:T(8,128)S(1)}, f32[2,128,256]{2,1,0:T(8,128)S(1)}, u32[]{:S(2)}, u32[]{:S(2)}) collective-permute-start(f32[2,128,256]{2,1,0:T(8,128)S(1)} %get-tuple-element.147), channel_id=1, source_target_pairs={{0,16},{8,24},{16,0},{24,8},{1,17},{9,25},{17,1},{25,9},{2,18},{10... | collective-permute-start | bytes 786440 | tf_op jit(solution)/shard_map/ppermute | solution.py:65
  124.3 12.5 %collective-permute-start.31 = (f32[2,128,256]{2,1,0:T(8,128)S(1)}, f32[2,128,256]{2,1,0:T(8,128)S(1)}, u32[]{:S(2)}, u32[]{:S(2)}) collective-permute-start(f32[2,128,256]{2,1,0:T(8,128)S(1)} %get-tuple-element.148), channel_id=1, source_target_pairs={{0,24},{8,16},{16,8},{24,0},{1,25},{9,17},{17,9},{25,1},{2,26},{10... | collective-permute-start | bytes 786440 | tf_op jit(solution)/shard_map/ppermute | solution.py:65
  126.4 19.2 %collective-permute-start.25 = (f32[256,256]{1,0:T(8,128)S(1)}, f32[256,256]{1,0:T(8,128)S(1)}, u32[]{:S(2)}, u32[]{:S(2)}) collective-permute-start(f32[256,256]{1,0:T(8,128)S(1)} %get-tuple-element.141), channel_id=1, source_target_pairs={{0,4},{1,5},{2,6},{3,7},{4,0},{5,1},{6,2},{7,3},{8,12},{9,13},{10,... | collective-permute-start | bytes 786440 | tf_op jit(solution)/shard_map/ppermute | solution.py:65
  126.7 18.9 %collective-permute-start.26 = (f32[3,32,256]{2,1,0:T(8,128)S(1)}, f32[3,32,256]{2,1,0:T(8,128)S(1)}, u32[]{:S(2)}, u32[]{:S(2)}) collective-permute-start(f32[3,32,256]{2,1,0:T(8,128)S(1)} %get-tuple-element.143), channel_id=1, source_target_pairs={{0,4},{1,5},{2,6},{3,7},{4,0},{5,1},{6,2},{7,3},{8,12},{9,13},{10,... | collective-permute-start | bytes 294920 | tf_op jit(solution)/shard_map/ppermute | solution.py:65
  131.4 14.2 %collective-permute-start.27 = (f32[3,32,256]{2,1,0:T(8,128)S(1)}, f32[3,32,256]{2,1,0:T(8,128)S(1)}, u32[]{:S(2)}, u32[]{:S(2)}) collective-permute-start(f32[3,32,256]{2,1,0:T(8,128)S(1)} %get-tuple-element.144), channel_id=1, source_target_pairs={{0,2},{1,3},{2,0},{3,1},{4,6},{5,7},{6,4},{7,5},{8,10},{9,11},{10,... | collective-permute-start | bytes 294920 | tf_op jit(solution)/shard_map/ppermute | solution.py:65
  136.8 8.7 %collective-permute-start.28 = (f32[3,32,256]{2,1,0:T(8,128)S(1)}, f32[3,32,256]{2,1,0:T(8,128)S(1)}, u32[]{:S(2)}, u32[]{:S(2)}) collective-permute-start(f32[3,32,256]{2,1,0:T(8,128)S(1)} %get-tuple-element.145), channel_id=1, source_target_pairs={{0,6},{1,7},{2,4},{3,5},{4,2},{5,3},{6,0},{7,1},{8,14},{9,15},{10,... | collective-permute-start | bytes 294920 | tf_op jit(solution)/shard_map/ppermute | solution.py:65
  146.2 5.1 %collective-permute-start.33 = (f32[3,16,256]{2,1,0:T(8,128)S(1)}, f32[3,16,256]{2,1,0:T(8,128)S(1)}, u32[]{:S(2)}, u32[]{:S(2)}) collective-permute-start(f32[3,16,256]{2,1,0:T(8,128)S(1)} %get-tuple-element.152), channel_id=1, source_target_pairs={{0,1},{1,0},{2,3},{3,2},{4,5},{5,4},{6,7},{7,6},{8,9},{9,8},{10,11... | collective-permute-start | bytes 147464 | tf_op jit(solution)/shard_map/ppermute | solution.py:65
  146.3 5.5 %collective-permute-start.34 = (f32[2,32,256]{2,1,0:T(8,128)S(1)}, f32[2,32,256]{2,1,0:T(8,128)S(1)}, u32[]{:S(2)}, u32[]{:S(2)}) collective-permute-start(f32[2,32,256]{2,1,0:T(8,128)S(1)} %get-tuple-element.154), channel_id=1, source_target_pairs={{0,4},{1,5},{2,6},{3,7},{4,0},{5,1},{6,2},{7,3},{8,12},{9,13},{10,... | collective-permute-start | bytes 196616 | tf_op jit(solution)/shard_map/ppermute | solution.py:65
  148.2 4.9 %collective-permute-start.35 = (f32[2,32,256]{2,1,0:T(8,128)S(1)}, f32[2,32,256]{2,1,0:T(8,128)S(1)}, u32[]{:S(2)}, u32[]{:S(2)}) collective-permute-start(f32[2,32,256]{2,1,0:T(8,128)S(1)} %get-tuple-element.155), channel_id=1, source_target_pairs={{0,2},{1,3},{2,0},{3,1},{4,6},{5,7},{6,4},{7,5},{8,10},{9,11},{10,... | collective-permute-start | bytes 196616 | tf_op jit(solution)/shard_map/ppermute | solution.py:65
  149.0 7.5 %collective-permute-start.36 = (f32[2,32,256]{2,1,0:T(8,128)S(1)}, f32[2,32,256]{2,1,0:T(8,128)S(1)}, u32[]{:S(2)}, u32[]{:S(2)}) collective-permute-start(f32[2,32,256]{2,1,0:T(8,128)S(1)} %get-tuple-element.156), channel_id=1, source_target_pairs={{0,6},{1,7},{2,4},{3,5},{4,2},{5,3},{6,0},{7,1},{8,14},{9,15},{10,... | collective-permute-start | bytes 196616 | tf_op jit(solution)/shard_map/ppermute | solution.py:65
  151.3 8.8 %collective-permute-start.24 = (f32[128,256]{1,0:T(8,128)S(1)}, f32[128,256]{1,0:T(8,128)S(1)}, u32[]{:S(2)}, u32[]{:S(2)}) collective-permute-start(f32[128,256]{1,0:T(8,128)S(1)} %get-tuple-element.139), channel_id=1, source_target_pairs={{0,1},{1,0},{2,3},{3,2},{4,5},{5,4},{6,7},{7,6},{8,9},{9,8},{10,11... | collective-permute-start | bytes 393224 | tf_op jit(solution)/shard_map/ppermute | solution.py:65
  151.3 9.4 %collective-permute-start.32 = (f32[128,256]{1,0:T(8,128)S(1)}, f32[128,256]{1,0:T(8,128)S(1)}, u32[]{:S(2)}, u32[]{:S(2)}) collective-permute-start(f32[128,256]{1,0:T(8,128)S(1)} %get-tuple-element.150), channel_id=1, source_target_pairs={{0,1},{1,0},{2,3},{3,2},{4,5},{5,4},{6,7},{7,6},{8,9},{9,8},{10,11... | collective-permute-start | bytes 393224 | tf_op jit(solution)/shard_map/ppermute | solution.py:65
  157.1 9.8 %collective-permute-start.39 = (f32[3,16,512]{2,1,0:T(8,128)S(1)}, f32[3,16,512]{2,1,0:T(8,128)S(1)}, u32[]{:S(2)}, u32[]{:S(2)}) collective-permute-start(f32[3,16,512]{2,1,0:T(8,128)S(1)} %get-tuple-element.157.refs_8_.refs_3_), channel_id=1, source_target_pairs={{0,24},{8,16},{16,8},{24,0},{1,25},{9,17},{17,9},{25,1},{2,26},{10... | collective-permute-start | bytes 294920 | tf_op jit(solution)/shard_map/ppermute | solution.py:65
  159.4 2.8 %collective-permute-start.40 = (f32[2,16,256]{2,1,0:T(8,128)S(1)}, f32[2,16,256]{2,1,0:T(8,128)S(1)}, u32[]{:S(2)}, u32[]{:S(2)}) collective-permute-start(f32[2,16,256]{2,1,0:T(8,128)S(1)} %get-tuple-element.160), channel_id=1, source_target_pairs={{0,1},{1,0},{2,3},{3,2},{4,5},{5,4},{6,7},{7,6},{8,9},{9,8},{10,11... | collective-permute-start | bytes 98312 | tf_op jit(solution)/shard_map/ppermute | solution.py:65
  159.4 8.0 %collective-permute-start.38 = (f32[3,16,512]{2,1,0:T(8,128)S(1)}, f32[3,16,512]{2,1,0:T(8,128)S(1)}, u32[]{:S(2)}, u32[]{:S(2)}) collective-permute-start(f32[3,16,512]{2,1,0:T(8,128)S(1)} %get-tuple-element.157.refs_8_.refs_3_), channel_id=1, source_target_pairs={{0,16},{8,24},{16,0},{24,8},{1,17},{9,25},{17,1},{25,9},{2,18},{10... | collective-permute-start | bytes 294920 | tf_op jit(solution)/shard_map/ppermute | solution.py:65
  160.1 7.4 %collective-permute-start.37 = (f32[3,16,512]{2,1,0:T(8,128)S(1)}, f32[3,16,512]{2,1,0:T(8,128)S(1)}, u32[]{:S(2)}, u32[]{:S(2)}) collective-permute-start(f32[3,16,512]{2,1,0:T(8,128)S(1)} %get-tuple-element.157.refs_8_.refs_3_), channel_id=1, source_target_pairs={{0,8},{8,0},{16,24},{24,16},{1,9},{9,1},{17,25},{25,17},{2,10},{10... | collective-permute-start | bytes 294920 | tf_op jit(solution)/shard_map/ppermute | solution.py:65
  162.2 1.1 copy-start.1
  163.9 5.3 %collective-permute-start.43 = (f32[2,16,512]{2,1,0:T(8,128)S(1)}, f32[2,16,512]{2,1,0:T(8,128)S(1)}, u32[]{:S(2)}, u32[]{:S(2)}) collective-permute-start(f32[2,16,512]{2,1,0:T(8,128)S(1)} %shard_map.99.refs_7_.refs_11_), channel_id=1, source_target_pairs={{0,24},{8,16},{16,8},{24,0},{1,25},{9,17},{17,9},{25,1},{2,26},{10... | collective-permute-start | bytes 196616 | tf_op jit(solution)/shard_map/ppermute | solution.py:65
  166.2 4.3 %collective-permute-start.42 = (f32[2,16,512]{2,1,0:T(8,128)S(1)}, f32[2,16,512]{2,1,0:T(8,128)S(1)}, u32[]{:S(2)}, u32[]{:S(2)}) collective-permute-start(f32[2,16,512]{2,1,0:T(8,128)S(1)} %shard_map.99.refs_7_.refs_11_), channel_id=1, source_target_pairs={{0,16},{8,24},{16,0},{24,8},{1,17},{9,25},{17,1},{25,9},{2,18},{10... | collective-permute-start | bytes 196616 | tf_op jit(solution)/shard_map/ppermute | solution.py:65
  166.9 4.3 %collective-permute-start.41 = (f32[2,16,512]{2,1,0:T(8,128)S(1)}, f32[2,16,512]{2,1,0:T(8,128)S(1)}, u32[]{:S(2)}, u32[]{:S(2)}) collective-permute-start(f32[2,16,512]{2,1,0:T(8,128)S(1)} %shard_map.99.refs_7_.refs_11_), channel_id=1, source_target_pairs={{0,8},{8,0},{16,24},{24,16},{1,9},{9,1},{17,25},{25,17},{2,10},{10... | collective-permute-start | bytes 196616 | tf_op jit(solution)/shard_map/ppermute | solution.py:65

commit v9 on v8

--- a/solution.py
+++ b/solution.py
@@ -98,16 +98,15 @@
     return list(results)
 
 
-def cut_kernel(ratio, cuts, info_ref, listed_ref, factors_ref, slices_ref, *refs):
-    *outs, through_ref, sems = refs
-    through_ref[0] = slices_ref[...]
+def cut_kernel(ratio, cuts, members, info_ref, listed_ref, factors_ref, *refs):
+    *outs, sems = refs
     size, unit = outs[0].shape
     width = factors_ref.shape[2]
     column = info_ref[1]
     pair = (column % ratio) // 2
     copies = []
     for at, out_ref in enumerate(outs):
-        member, cut, way = at // (2 * cuts), at // 2 % cuts, at % 2
+        member, cut, way = members[at // (2 * cuts)], at // 2 % cuts, at % 2
         source = factors_ref.at[
             member, block(2 * pair + way, size), block(core_of(info_ref) * cuts + cut, unit)
         ]
@@ -116,7 +115,7 @@
     for at, out_ref in enumerate(outs):
         copies[at].wait()
         owner = column - core_of(info_ref) + at % 2
-        weight = listed_ref[at // (2 * cuts), owner * size // width]
+        weight = listed_ref[members[at // (2 * cuts)], owner * size // width]
         out_ref[...] = out_ref[...] * weight.astype(F32)
 
 
@@ -283,7 +282,7 @@
 def parent_kernel(
     children, rows_here, info_ref, listed_ref, chooser_ref, own_high_ref, own_low_ref,
     own_thigh_ref, own_tlow_ref, link_high_ref, link_low_ref, mine_ref, other_ref,
-    col_ref, turned_ref, high_ref, low_ref, thigh_ref, tlow_ref, *refs
+    col_ref, turned_ref, high_ref, low_ref, *refs
 ):
     *outs, full_ref = refs
     chooser = chooser_ref[...]
@@ -304,24 +303,24 @@
         full_ref[...] = product(pair, pair_of(link_high_ref, link_low_ref, c))
         turned_ref[c] = full_ref[output_rows, :]
         lifted = split(full_ref[:, columns])
-        store_pair(high_ref, low_ref, lifted, c)
-        store_pair(thigh_ref, tlow_ref, turn(chooser, split(full_ref[...])), c)
+        store_pair(high_ref, low_ref, split(full_ref[...]), c)
         own = (own_high_ref[c + 1, :, columns], own_low_ref[c + 1, :, columns])
         store_parts(outs, 1 + c, product(parent, lifted) - product(turned_pair, own))
 
 
 def child_kernel(
-    children, info_ref, own_high_ref, own_low_ref, own_thigh_ref, own_tlow_ref,
-    high_ref, low_ref, thigh_ref, tlow_ref, lift_high_ref, lift_low_ref, corner_ref, *refs
+    children, info_ref, chooser_ref, own_high_ref, own_low_ref, own_thigh_ref, own_tlow_ref,
+    high_ref, low_ref, lift_high_ref, lift_low_ref, corner_ref, *refs
 ):
     outs = refs[children:]
     columns = block(core_of(info_ref), corner_ref.shape[2])
     for c in range(children):
-        lifted = pair_of(high_ref, low_ref, c)
+        lifted = (high_ref[c, :, columns], low_ref[c, :, columns])
+        turned_pair = turn(chooser_ref[...], pair_of(high_ref, low_ref, c))
         own = (own_high_ref[c + 1, :, columns], own_low_ref[c + 1, :, columns])
         total = corner_ref[c] + refs[c][...]
         total += product(pair_of(own_thigh_ref, own_tlow_ref, c + 1), lifted)
-        total += product(pair_of(thigh_ref, tlow_ref, c), own)
+        total += product(turned_pair, own)
         total -= product(pair_of(lift_high_ref, lift_low_ref, c), lifted)
         store_parts(outs, c, total)
 
@@ -444,16 +443,20 @@
     rings = (ring(True), ring(False))
     info = jnp.stack([lax.axis_index("row"), lax.axis_index("col")]).astype(jnp.int32)
 
-    flat = call(
-        functools.partial(cut_kernel, ratio, cuts),
-        [shape(cols_here, unit)] * (chunk_count * 2) + [shape(1, *parent_factor.shape)],
-        [info, listed, factor_cols, parent_factor],
-        smem=2, hbm=1, vmem=48,
-        scratch=[pltpu.SemaphoreType.DMA((chunk_count * 2,))],
-    )
-    chunks = [flat[at * 2 :][:2] for at in range(chunk_count)]
-
-    last = [flat[0]]
+    def cut(chosen, run):
+        count = len(chosen) * cuts * 2
+        flat = run(
+            functools.partial(cut_kernel, ratio, cuts, chosen),
+            [shape(cols_here, unit)] * count,
+            [info, listed, factor_cols],
+            smem=2, hbm=1, vmem=48,
+            scratch=[pltpu.SemaphoreType.DMA((count,))],
+        )
+        return [flat[at : at + 2] for at in range(0, count, 2)]
+
+    chunks = cut((0,), call)
+
+    last = [chunks[0][0]]
     held = {}
     moved = []
     received = []
@@ -462,6 +465,8 @@
         results = call(body, outs, args, after=last[0], **options)
         last[0] = results[0]
         return results
+
+    chunks.extend(cut(tuple(range(1, members)), heavy))
 
     def ring_flow():
         shapes = [shape(cols_here, unit)] * 2
@@ -477,7 +482,7 @@
             received.append([lax.ppermute(moving[way], AXES, rings[way]) for way in range(2)])
 
     def link_flow():
-        gathered = flat[-1]
+        gathered = parent_factor[None]
         for bit in reversed(range(col_bits)):
             arrived = swap(gathered, "col", col_count, 1 << bit)
             dims = (2 * gathered.shape[0],) + parent_factor.shape
@@ -542,6 +547,9 @@
         chunk = (member + 1) * cuts - 1
         while len(received) < chunk + row_count - 1:
             yield WAIT
+        final = member == members - 1
+        if not final:
+            yield WAIT
         candidates = []
         for at in range(member * cuts, (member + 1) * cuts):
             for way in range(2):
@@ -558,7 +566,8 @@
         for bit in range(1, col_bits):
             arrived = swap(send, "col", col_count, 1 << bit)
             if bit == 1:
-                yield WAIT
+                if final:
+                    yield WAIT
                 if member:
                     held["gram", member] = heavy(
                         unit_gram_kernel,
@@ -570,12 +579,10 @@
                 size //= 2
                 keep, send = yield (halve_step, [keep, arrived], [shape(size, half)] * 2)
         if member == 0:
-            (mine,) = yield (halve_step, [keep, arrived], [shape(size, half)])
-            other = swap(mine, "col", col_count, 1)
-        else:
-            mine, theirs = yield (part_step, [keep, arrived], [shape(size // 2, half)] * 2)
-            other = swap(theirs, "col", col_count, 1)
-        held["sum", member] = [mine, other]
+            held["last", 0] = [keep, arrived]
+            return
+        mine, theirs = yield (part_step, [keep, arrived], [shape(size // 2, half)] * 2)
+        held["sum", member] = [mine, swap(theirs, "col", col_count, 1)]
 
     def total_flow(pieces):
         count, size, _ = pieces[0].shape
@@ -592,21 +599,28 @@
         return [piece] + [swap(piece, "row", row_count, d) for d in range(1, row_count)]
 
     def parent_flow():
-        names = [("sum", 0), "links"]
+        names = [("last", 0), "links"]
         while any(name not in held for name in names):
             yield WAIT
+        (mine,) = heavy(
+            functools.partial(step_kernel, [(halve_step, 2, 1)]),
+            [shape(group, half)],
+            [info, *held["last", 0]],
+            smem=1,
+        )
+        other = swap(mine, "col", col_count, 1)
         col, turned, *rest = heavy(
             functools.partial(parent_kernel, children, rows_here),
             [shape(group // 2, width), shape(children, group // 2, width)]
-            + [shape(children, group, half, dtype=BF16)] * 2
-            + [shape(children, width, group, dtype=BF16)] * 2
+            + [shape(children, group, width, dtype=BF16)] * 2
             + [shape(members, width // row_count, half)] * row_count,
-            [info, listed, held["chooser"], *held["own"], *held["links"][:2], *held["sum", 0]],
+            [info, listed, held["chooser"], *held["own"], *held["links"][:2], mine, other],
             smem=2, vmem=20,
             scratch=[pltpu.VMEM((group, width), F32)],
         )
-        held["parent"] = (col, turned, rest[:4])
-        held["parent totals"] = yield from total_flow(rest[4:])
+        held["parent"] = (col, turned, rest[:2])
+        yield WAIT
+        held["parent totals"] = yield from total_flow(rest[2:])
 
     def child_flow():
         names = [("gram", 1 + c) for c in range(children)]
@@ -615,7 +629,8 @@
         pieces = heavy(
             functools.partial(child_kernel, children),
             [shape(children, width // row_count, half)] * row_count,
-            [info, *held["own"], *held["parent"][2], *held["links"][2:4], held["links"][5]]
+            [info, held["chooser"], *held["own"], *held["parent"][2], *held["links"][2:4]]
+            + [held["links"][5]]
             + [held[name] for name in names],
             smem=1, vmem=20,
         )
@@ -635,9 +650,9 @@
             smem=2,
         )[0]
 
-    flows = [ring_flow(), link_flow(), prepare_flow()]
-    flows += [unit_flow(member) for member in range(members)]
-    flows += [parent_flow(), child_flow(), column_flow()]
+    flows = [ring_flow()] + [unit_flow(member) for member in range(children)]
+    flows += [link_flow(), prepare_flow(), parent_flow()]
+    flows += [unit_flow(children), child_flow(), column_flow()]
     waiting = [(flow, None) for flow in flows]
     while waiting:
         tasks = [wish for _, wish in waiting if wish not in (None, WAIT)]

time: 173 us -> 166 us (0.960)
  waiting for transfers between devices: 79.6 us -> 62.1 us
  starting transfers between devices: 48.1 us -> 56.5 us
  Pallas kernels: 41.2 us -> 43.9 us
    ppermute x10, waiting for transfers between devices: 28.7 us -> 19.6 us  [ring_flow(): lax.ppermute(moving[way], AXES, rings[way])]
    ppermute x34, waiting for transfers between devices: 50.9 us -> 42.5 us  [swap(): lax.ppermute(value, axis, [(place, place ^ change) for place in range(siz...]
    ppermute x34, starting transfers between devices: 36.1 us -> 43.6 us  [swap(): lax.ppermute(value, axis, [(place, place ^ change) for place in range(siz...]
    pallas_call x25 -> x27, Pallas kernels: 41.2 us -> 43.9 us  [call(): pl.pallas_call(inner, out_shape=outs, in_specs=[pl.BlockSpec(memory_space...]
  transfers between devices with their start and end apart: 44 -> 44, of which waited for: 22 -> 21; matrix products, arithmetic and copies ran while one was open for 0% -> 0% of each run, Pallas kernels for 21% -> 24%
where the time goes in v9:
time: 166 us; the launch traced here: 165 us
  waiting for transfers between devices  62.1 us (37%)
  starting transfers between devices  56.5 us (34%)
  Pallas kernels  43.9 us (26%)
  local copies, waits for them, and re-layouts  1.85 us (1%)
    pallas_call x27, Pallas kernels, call(): pl.pallas_call(inner, out_shape=outs, in_specs=[pl.BlockSpec(memory_space...  43.9 us
    ppermute x34, starting transfers between devices, swap(): lax.ppermute(value, axis, [(place, place ^ change) for place in range(siz...  43.6 us
    ppermute x34, waiting for transfers between devices, swap(): lax.ppermute(value, axis, [(place, place ^ change) for place in range(siz...  42.5 us
    ppermute x10, waiting for transfers between devices, ring_flow(): lax.ppermute(moving[way], AXES, rings[way])  19.6 us
    ppermute x10, starting transfers between devices, ring_flow(): lax.ppermute(moving[way], AXES, rings[way])  13 us
  transfers between devices with their start and end apart: 44, of which 21 were waited for; matrix products, arithmetic and copies ran while one was open for 0% of the time, Pallas kernels for 24%

profile of v9, /device:TPU:0, one launch (start us, length us, event | category | flops | bytes accessed | tf_op | source)
XLA Modules:
  0.0 165.4 jit_solution(11426834988388522513)
XLA Ops:
  1.9 2.1 %shard_map.76 = (f32[512,256]{1,0:T(8,128)S(1)}, f32[512,256]{1,0:T(8,128)S(1)}) custom-call(s32[2]{0:T(128)S(1)} %pad_add_fusion.info_ref.refs_0_, s32[3,8]{1,0:T(4,128)S(1)} %copy-done.4, f32[3,1024,512]{2,1,0:T(8,128)} %refs_2_.9), custom_call_target="tpu_custom_call" | custom-call | flops 1024 | bytes 1024 | tf_op jit(solution)/shard_map/pallas_call | solution.py:89
  4.1 2.6 %collective-permute-start.1 = (f32[512,256]{1,0:T(8,128)S(1)}, f32[512,256]{1,0:T(8,128)S(1)}, u32[]{:S(2)}, u32[]{:S(2)}) collective-permute-start(f32[512,256]{1,0:T(8,128)S(1)} %get-tuple-element.88.refs_7_), channel_id=1, source_target_pairs={{8,0},{24,8},{16,24},{0,16},{9,1},{25,9},{17,25},{1,17},{2,10},{18... | collective-permute-start | bytes 1572872 | tf_op jit(solution)/shard_map/ppermute | solution.py:482
  6.7 3.1 %collective-permute-start.2 = (f32[1,2,64,512]{3,2,1,0:T(8,128)S(1)}, f32[1,2,64,512]{3,2,1,0:T(8,128)S(1)}, u32[]{:S(2)}, u32[]{:S(2)}) collective-permute-start(f32[1,2,64,512]{3,2,1,0:T(8,128)S(1)} %bitcast.5), channel_id=1, source_target_pairs={{0,4},{1,5},{2,6},{3,7},{4,0},{5,1},{6,2},{7,3},{8,12},{9,13},{10,... | collective-permute-start | bytes 786440 | tf_op jit(solution)/shard_map/ppermute | solution.py:65
  9.8 2.2 %shard_map.77 = (f32[512,256]{1,0:T(8,128)S(1)}, f32[512,256]{1,0:T(8,128)S(1)}, f32[512,256]{1,0:T(8,128)S(1)}, f32[512,256]{1,0:T(8,128)S(1)}) custom-call(s32[2]{0:T(128)S(1)} %pad_add_fusion.info_ref.refs_0_, s32[3,8]{1,0:T(4,128)S(1)} %copy-done.5, f32[3,1024,512]{2,1,0:T(8,128)} %refs_2_.9, f32[512,256]{1,0:T(8,128)S(1)} %get-tuple-element.79.refs_3_), custom_call_target="tpu_custom_call" | custom-call | flops 1024 | bytes 1024 | tf_op jit(solution)/shard_map/pallas_call | solution.py:89
  11.9 0.8 shard_map.78.refs_3_.refs_4_.refs_2_.refs_1_
  12.8 2.2 %shard_map.79 = (bf16[3,256,512]{2,1,0:T(8,128)(2,1)S(1)}, bf16[3,256,512]{2,1,0:T(8,128)(2,1)S(1)}, bf16[3,512,256]{2,1,0:T(8,128)(2,1)S(1)}, bf16[3,512,256]{2,1,0:T(8,128)(2,1)S(1)}) custom-call(s32[2]{0:T(128)S(1)} %pad_add_fusion.info_ref.refs_0_, s32[3,8]{1,0:T(4,128)S(1)} %copy-done.5, f32[3,1024,512]{2,1,0:T(8,128)S(1)} %bitcast.4, ...), custom_call_target="tpu_custom_call" | custom-call | flops 1024 | bytes 1024 | tf_op jit(solution)/shard_map/pallas_call | solution.py:89
  15.0 6.8 %collective-permute-done.2.refs_6_ = f32[1,2,64,512]{3,2,1,0:T(8,128)S(1)} collective-permute-done((f32[1,2,64,512]{3,2,1,0:T(8,128)S(1)}, f32[1,2,64,512]{3,2,1,0:T(8,128)S(1)}, u32[]{:S(2)}, u32[]{:S(2)}) %collective-permute-start.2) | collective-permute-done | bytes 262176 | tf_op jit(solution)/shard_map/ppermute | solution.py:65
  22.5 1.6 collective-permute-start.4
  24.7 1.5 collective-permute-start.3
  26.3 1.7 %shard_map.81 = (bf16[1024,1024]{1,0:T(8,128)(2,1)S(1)}, bf16[1024,1024]{1,0:T(8,128)(2,1)S(1)}) custom-call(s32[2]{0:T(128)S(1)} %pad_add_fusion.info_ref.refs_0_, f32[1024,512]{1,0:T(8,128)S(1)} %copy-done.2, f32[1024,512]{1,0:T(8,128)S(1)} %collective-permute-done.6.refs_2_, f32[512,256]{1,0:T(8,128)S(1)} %get-tuple-element.89.refs_3_), custom_call_target="tpu_custom_call" | custom-call | flops 1024 | bytes 1024 | tf_op jit(solution)/shard_map/pallas_call | solution.py:89
  27.9 7.8 %collective-permute-done.4.refs_4_.refs_9_.refs_8_ = f32[512,256]{1,0:T(8,128)S(1)} collective-permute-done((f32[512,256]{1,0:T(8,128)S(1)}, f32[512,256]{1,0:T(8,128)S(1)}, u32[]{:S(2)}, u32[]{:S(2)}) %collective-permute-start.4) | collective-permute-done | bytes 524320 | tf_op jit(solution)/shard_map/ppermute | solution.py:482
  35.7 1.0 collective-permute-done.5.refs_6_
  36.7 1.3 collective-permute-done.3.refs_3_.refs_5_.refs_4_
  38.0 0.7 shard_map.82
  39.4 1.5 collective-permute-start.7
  40.9 2.2 %shard_map.83 = (bf16[512,1024]{1,0:T(8,128)(2,1)S(1)}, bf16[512,1024]{1,0:T(8,128)(2,1)S(1)}) custom-call(s32[2]{0:T(128)S(1)} %pad_add_fusion.info_ref.refs_0_, s32[3,8]{1,0:T(4,128)S(1)} %copy-done.5, f32[3,1024,512]{2,1,0:T(8,128)S(1)} %bitcast.4, bf16[512,512]{1,0:T(8,128)(2,1)S(1)} %shard_map.78.refs_3_.refs_4_.refs_2_.refs_1_, ...), custom_call_target="tpu_custom_call" | custom-call | flops 1024 | bytes 1024 | tf_op jit(solution)/shard_map/pallas_call | solution.py:89
  43.1 10.0 %collective-permute-done.8.refs_2_.refs_10_.refs_9_.refs_8_ = f32[512,256]{1,0:T(8,128)S(1)} collective-permute-done((f32[512,256]{1,0:T(8,128)S(1)}, f32[512,256]{1,0:T(8,128)S(1)}, u32[]{:S(2)}, u32[]{:S(2)}) %collective-permute-start.8) | collective-permute-done | bytes 524320 | tf_op jit(solution)/shard_map/ppermute | solution.py:482
  53.4 0.7 shard_map.84
  54.2 1.6 collective-permute-start.12
  55.7 2.4 %shard_map.85 = (f32[512,256]{1,0:T(8,128)S(1)}, f32[512,256]{1,0:T(8,128)S(1)}) custom-call(s32[2]{0:T(128)S(1)} %pad_add_fusion.info_ref.refs_0_, bf16[1024,1024]{1,0:T(8,128)(2,1)S(1)} %get-tuple-element.92.refs_7_.refs_1_, bf16[1024,1024]{1,0:T(8,128)(2,1)S(1)} %get-tuple-element.98.refs_2_, f32[512,256]{1,0:T(8,128)S(1)} %get-tuple-element.79.refs_3_, ...), custom_call_target="tpu_custom_call" | custom-call | flops 1024 | bytes 1024 | tf_op jit(solution)/shard_map/pallas_call | solution.py:89
  58.6 1.5 collective-permute-start.11
  60.2 1.3 collective-permute-done.10.refs_3_
  61.6 4.5 %shard_map.86 = (bf16[2,512,512]{2,1,0:T(8,128)(2,1)S(1)}, bf16[2,512,512]{2,1,0:T(8,128)(2,1)S(1)}, bf16[2,512,256]{2,1,0:T(8,128)(2,1)S(1)}, bf16[2,512,256]{2...) custom-call(s32[2]{0:T(128)S(1)} %pad_add_fusion.info_ref.refs_0_, ...), custom_call_target="tpu_custom_call" | custom-call | flops 1024 | bytes 1024 | tf_op jit(solution)/shard_map/pallas_call | solution.py:89
  66.1 2.2 %shard_map.87 = (bf16[512,1024]{1,0:T(8,128)(2,1)S(1)}, bf16[512,1024]{1,0:T(8,128)(2,1)S(1)}) custom-call(s32[2]{0:T(128)S(1)} %pad_add_fusion.info_ref.refs_0_, s32[3,8]{1,0:T(4,128)S(1)} %copy-done.5, f32[3,1024,512]{2,1,0:T(8,128)S(1)} %bitcast.4, bf16[512,512]{1,0:T(8,128)(2,1)S(1)} %shard_map.78.refs_3_.refs_4_.refs_2_.refs_1_, ...), custom_call_target="tpu_custom_call" | custom-call | flops 1024 | bytes 1024 | tf_op jit(solution)/shard_map/pallas_call | solution.py:89
  68.3 2.8 %collective-permute-done.13.refs_4_ = f32[512,256]{1,0:T(8,128)S(1)} collective-permute-done((f32[512,256]{1,0:T(8,128)S(1)}, f32[512,256]{1,0:T(8,128)S(1)}, u32[]{:S(2)}, u32[]{:S(2)}) %collective-permute-start.13) | collective-permute-done | bytes 524320 | tf_op jit(solution)/shard_map/ppermute | solution.py:65
  72.0 3.4 %collective-permute-start.14 = (f32[256,256]{1,0:T(8,128)S(1)}, f32[256,256]{1,0:T(8,128)S(1)}, u32[]{:S(2)}, u32[]{:S(2)}) collective-permute-start(f32[256,256]{1,0:T(8,128)S(1)} %get-tuple-element.107), channel_id=1, source_target_pairs={{0,4},{1,5},{2,6},{3,7},{4,0},{5,1},{6,2},{7,3},{8,12},{9,13},{10,... | collective-permute-start | bytes 786440 | tf_op jit(solution)/shard_map/ppermute | solution.py:65
  76.1 1.4 collective-permute-start.17
  77.5 2.4 %shard_map.89 = (f32[512,256]{1,0:T(8,128)S(1)}, f32[512,256]{1,0:T(8,128)S(1)}) custom-call(s32[2]{0:T(128)S(1)} %pad_add_fusion.info_ref.refs_0_, bf16[1024,1024]{1,0:T(8,128)(2,1)S(1)} %get-tuple-element.92.refs_7_.refs_1_, bf16[1024,1024]{1,0:T(8,128)(2,1)S(1)} %get-tuple-element.98.refs_2_, f32[512,256]{1,0:T(8,128)S(1)} %get-tuple-element.89.refs_3_, ...), custom_call_target="tpu_custom_call" | custom-call | flops 1024 | bytes 1024 | tf_op jit(solution)/shard_map/pallas_call | solution.py:89
  79.9 1.6 collective-permute-start.16
  81.5 1.0 shard_map.90.refs_3_.refs_11_
  82.5 3.2 %collective-permute-done.14.refs_2_ = f32[256,256]{1,0:T(8,128)S(1)} collective-permute-done((f32[256,256]{1,0:T(8,128)S(1)}, f32[256,256]{1,0:T(8,128)S(1)}, u32[]{:S(2)}, u32[]{:S(2)}) %collective-permute-start.14) | collective-permute-done | bytes 262176 | tf_op jit(solution)/shard_map/ppermute | solution.py:65
  86.4 1.5 collective-permute-done.15.refs_10_
  87.9 4.4 %shard_map.92 = (f32[128,512]{1,0:T(8,128)S(1)}, f32[2,128,512]{2,1,0:T(8,128)S(1)}, bf16[2,256,512]{2,1,0:T(8,128)(2,1)S(1)}, bf16[2,256,512]{2,1,0:T(8,128)(2,...) custom-call(s32[2]{0:T(128)S(1)} %pad_add_fusion.info_ref.refs_0_, ...), custom_call_target="tpu_custom_call" | custom-call | flops 1024 | bytes 1024 | tf_op jit(solution)/shard_map/pallas_call | solution.py:89
  92.3 2.4 %shard_map.93 = (f32[512,256]{1,0:T(8,128)S(1)}, f32[512,256]{1,0:T(8,128)S(1)}) custom-call(s32[2]{0:T(128)S(1)} %pad_add_fusion.info_ref.refs_0_, bf16[1024,1024]{1,0:T(8,128)(2,1)S(1)} %get-tuple-element.92.refs_7_.refs_1_, bf16[1024,1024]{1,0:T(8,128)(2,1)S(1)} %get-tuple-element.98.refs_2_, f32[512,256]{1,0:T(8,128)S(1)} %get-tuple-element.93.refs_4_.refs_3_, ...), custom_call_target="tpu_custom_call" | custom-call | flops 1024 | bytes 1024 | tf_op jit(solution)/shard_map/pallas_call | solution.py:89
  95.3 1.5 collective-permute-start.20
  97.5 1.3 collective-permute-start.22
  99.4 3.5 %collective-permute-start.19 = (f32[256,256]{1,0:T(8,128)S(1)}, f32[256,256]{1,0:T(8,128)S(1)}, u32[]{:S(2)}, u32[]{:S(2)}) collective-permute-start(f32[256,256]{1,0:T(8,128)S(1)} %get-tuple-element.117), channel_id=1, source_target_pairs={{0,4},{1,5},{2,6},{3,7},{4,0},{5,1},{6,2},{7,3},{8,12},{9,13},{10,... | collective-permute-start | bytes 786440 | tf_op jit(solution)/shard_map/ppermute | solution.py:65
  102.9 1.0 shard_map.95.refs_12_.refs_13_
  103.9 2.6 %shard_map.96 = (f32[2,128,256]{2,1,0:T(8,128)S(1)}, f32[2,128,256]{2,1,0:T(8,128)S(1)}, f32[2,128,256]{2,1,0:T(8,128)S(1)}, f32[2,128,256]{2,1,0:T(8,128)S(1)}) custom-call(s32[2]{0:T(128)S(1)} %pad_add_fusion.info_ref.refs_0_, bf16[512,512]{1,0:T(8,128)(2,1)S(1)} %shard_map.78.refs_3_.refs_4_.refs_2_.refs_1_, ...), custom_call_target="tpu_custom_call" | custom-call | flops 1024 | bytes 1024 | tf_op jit(solution)/shard_map/pallas_call | solution.py:89
  106.5 5.9 %collective-permute-done.19.refs_2_ = f32[256,256]{1,0:T(8,128)S(1)} collective-permute-done((f32[256,256]{1,0:T(8,128)S(1)}, f32[256,256]{1,0:T(8,128)S(1)}, u32[]{:S(2)}, u32[]{:S(2)}) %collective-permute-start.19) | collective-permute-done | bytes 262176 | tf_op jit(solution)/shard_map/ppermute | solution.py:65
  112.4 1.5 collective-permute-start.29
  114.0 0.7 collective-permute-start.30
  114.7 1.4 collective-permute-done.21.refs_5_
  116.1 0.8 shard_map.97
  116.9 3.6 %collective-permute-start.28 = (f32[256,256]{1,0:T(8,128)S(1)}, f32[256,256]{1,0:T(8,128)S(1)}, u32[]{:S(2)}, u32[]{:S(2)}) collective-permute-start(f32[256,256]{1,0:T(8,128)S(1)} %get-tuple-element.137), channel_id=1, source_target_pairs={{0,4},{1,5},{2,6},{3,7},{4,0},{5,1},{6,2},{7,3},{8,12},{9,13},{10,... | collective-permute-start | bytes 786440 | tf_op jit(solution)/shard_map/ppermute | solution.py:65
  120.5 1.2 collective-permute-done.29.refs_8_
  121.7 4.2 %collective-permute-start.26 = (f32[3,32,256]{2,1,0:T(8,128)S(1)}, f32[3,32,256]{2,1,0:T(8,128)S(1)}, u32[]{:S(2)}, u32[]{:S(2)}) collective-permute-start(f32[3,32,256]{2,1,0:T(8,128)S(1)} %get-tuple-element.134), channel_id=1, source_target_pairs={{0,2},{1,3},{2,0},{3,1},{4,6},{5,7},{6,4},{7,5},{8,10},{9,11},{10,... | collective-permute-start | bytes 294920 | tf_op jit(solution)/shard_map/ppermute | solution.py:65
  125.9 1.3 collective-permute-done.30.refs_9_
  127.1 3.2 %collective-permute-start.27 = (f32[3,32,256]{2,1,0:T(8,128)S(1)}, f32[3,32,256]{2,1,0:T(8,128)S(1)}, u32[]{:S(2)}, u32[]{:S(2)}) collective-permute-start(f32[3,32,256]{2,1,0:T(8,128)S(1)} %get-tuple-element.135), channel_id=1, source_target_pairs={{0,6},{1,7},{2,4},{3,5},{4,2},{5,3},{6,0},{7,1},{8,14},{9,15},{10,... | collective-permute-start | bytes 294920 | tf_op jit(solution)/shard_map/ppermute | solution.py:65
  130.4 7.7 %collective-permute-done.25.refs_2_ = f32[3,32,256]{2,1,0:T(8,128)S(1)} collective-permute-done((f32[3,32,256]{2,1,0:T(8,128)S(1)}, f32[3,32,256]{2,1,0:T(8,128)S(1)}, u32[]{:S(2)}, u32[]{:S(2)}) %collective-permute-start.25) | collective-permute-done | bytes 98336 | tf_op jit(solution)/shard_map/ppermute | solution.py:65
  138.9 3.7 %collective-permute-start.34 = (f32[2,32,256]{2,1,0:T(8,128)S(1)}, f32[2,32,256]{2,1,0:T(8,128)S(1)}, u32[]{:S(2)}, u32[]{:S(2)}) collective-permute-start(f32[2,32,256]{2,1,0:T(8,128)S(1)} %get-tuple-element.146), channel_id=1, source_target_pairs={{0,4},{1,5},{2,6},{3,7},{4,0},{5,1},{6,2},{7,3},{8,12},{9,13},{10,... | collective-permute-start | bytes 196616 | tf_op jit(solution)/shard_map/ppermute | solution.py:65
  142.6 1.5 collective-permute-start.36
  144.6 2.1 %collective-permute-done.34.refs_4_ = f32[2,32,256]{2,1,0:T(8,128)S(1)} collective-permute-done((f32[2,32,256]{2,1,0:T(8,128)S(1)}, f32[2,32,256]{2,1,0:T(8,128)S(1)}, u32[]{:S(2)}, u32[]{:S(2)}) %collective-permute-start.34) | collective-permute-done | bytes 65568 | tf_op jit(solution)/shard_map/ppermute | solution.py:65
  146.7 2.4 %collective-permute-done.35.refs_5_ = f32[2,32,256]{2,1,0:T(8,128)S(1)} collective-permute-done((f32[2,32,256]{2,1,0:T(8,128)S(1)}, f32[2,32,256]{2,1,0:T(8,128)S(1)}, u32[]{:S(2)}, u32[]{:S(2)}) %collective-permute-start.35) | collective-permute-done | bytes 65568 | tf_op jit(solution)/shard_map/ppermute | solution.py:65
  149.7 1.7 %collective-permute-start.39 = (f32[3,16,512]{2,1,0:T(8,128)S(1)}, f32[3,16,512]{2,1,0:T(8,128)S(1)}, u32[]{:S(2)}, u32[]{:S(2)}) collective-permute-start(f32[3,16,512]{2,1,0:T(8,128)S(1)} %get-tuple-element.149.refs_8_.refs_3_), channel_id=1, source_target_pairs={{0,24},{8,16},{16,8},{24,0},{1,25},{9,17},{17,9},{25,1},{2,26},{10... | collective-permute-start | bytes 294920 | tf_op jit(solution)/shard_map/ppermute | solution.py:65
  151.4 1.3 collective-permute-start.38
  153.3 1.5 shard_map.100.refs_3_
  154.8 1.1 copy-done
  156.5 1.7 %collective-permute-start.43 = (f32[2,16,512]{2,1,0:T(8,128)S(1)}, f32[2,16,512]{2,1,0:T(8,128)S(1)}, u32[]{:S(2)}, u32[]{:S(2)}) collective-permute-start(f32[2,16,512]{2,1,0:T(8,128)S(1)} %shard_map.101.refs_7_.refs_11_), channel_id=1, source_target_pairs={{0,24},{8,16},{16,8},{24,0},{1,25},{9,17},{17,9},{25,1},{2,26},{10... | collective-permute-start | bytes 196616 | tf_op jit(solution)/shard_map/ppermute | solution.py:65
  158.2 1.3 collective-permute-start.42
  160.1 1.8 %collective-permute-done.43.refs_10_ = f32[2,16,512]{2,1,0:T(8,128)S(1)} collective-permute-done((f32[2,16,512]{2,1,0:T(8,128)S(1)}, f32[2,16,512]{2,1,0:T(8,128)S(1)}, u32[]{:S(2)}, u32[]{:S(2)}) %collective-permute-start.43) | collective-permute-done | bytes 65568 | tf_op jit(solution)/shard_map/ppermute | solution.py:65
  161.9 0.9 collective-permute-done.42.refs_9_
  162.8 1.0 collective-permute-done.41.refs_8_
  163.8 1.6 shard_map.102
  (70 shorter events, 11.7 us)
Async XLA Ops:
  0.6 25.6 %collective-permute-start.6 = (f32[1024,512]{1,0:T(8,128)}, f32[1024,512]{1,0:T(8,128)S(1)}, u32[]{:S(2)}, u32[]{:S(2)}) collective-permute-start(f32[1024,512]{1,0:T(8,128)} %refs_1_.10), channel_id=1, source_target_pairs={{0,1},{1,0},{2,3},{3,2},{4,5},{5,4},{6,7},{7,6},{8,9},{9,8},{10,11... | collective-permute-start | bytes 6291464 | tf_op jit(solution)/shard_map/ppermute | solution.py:65
  1.2 0.7 copy-start.4
  1.9 4.8 %copy-start.3 = (f32[2,64,512]{2,1,0:T(8,128)S(1)}, f32[2,64,512]{2,1,0:T(8,128)}, u32[]{:S(2)}) copy-start(f32[2,64,512]{2,1,0:T(8,128)} %param.7) | copy-start | bytes 786436
  1.9 7.8 %copy-start.5 = (s32[3,8]{1,0:T(4,128)S(1)}, s32[3,8]{1,0:T(4,128)}, u32[]{:S(2)}) copy-start(s32[3,8]{1,0:T(4,128)} %refs_1_.14) | copy-start | bytes 292
  1.9 10.8 %slice-start = ((s8[6291456]{0:T(1024)(128)(4,1)}), s8[4194304]{0:T(1024)(128)(4,1)S(1)}, s32[]{:S(2)}) async-start(s8[6291456]{0:T(1024)(128)(4,1)} %bitcast.3), calls=%async_computation | async-start | bytes 8388608
  4.1 17.7 %collective-permute-start.1 = (f32[512,256]{1,0:T(8,128)S(1)}, f32[512,256]{1,0:T(8,128)S(1)}, u32[]{:S(2)}, u32[]{:S(2)}) collective-permute-start(f32[512,256]{1,0:T(8,128)S(1)} %get-tuple-element.88.refs_7_), channel_id=1, source_target_pairs={{8,0},{24,8},{16,24},{0,16},{9,1},{25,9},{17,25},{1,17},{2,10},{18... | collective-permute-start | bytes 1572872 | tf_op jit(solution)/shard_map/ppermute | solution.py:482
  6.7 15.1 %collective-permute-start = (f32[512,256]{1,0:T(8,128)S(1)}, f32[512,256]{1,0:T(8,128)S(1)}, u32[]{:S(2)}, u32[]{:S(2)}) collective-permute-start(f32[512,256]{1,0:T(8,128)S(1)} %get-tuple-element.79.refs_3_), channel_id=1, source_target_pairs={{0,8},{8,24},{24,16},{16,0},{1,9},{9,25},{25,17},{17,1},{10,2},{2,... | collective-permute-start | bytes 1572872 | tf_op jit(solution)/shard_map/ppermute | solution.py:482
  6.7 6.1 %slice-start.1 = ((s8[6291456]{0:T(1024)(128)(4,1)}), s8[2097152]{0:T(1024)(128)(4,1)S(1)}, s32[]{:S(2)}) async-start(s8[6291456]{0:T(1024)(128)(4,1)} %bitcast.3), calls=%async_computation.1 | async-start | bytes 4194304
  6.7 15.1 %collective-permute-start.2 = (f32[1,2,64,512]{3,2,1,0:T(8,128)S(1)}, f32[1,2,64,512]{3,2,1,0:T(8,128)S(1)}, u32[]{:S(2)}, u32[]{:S(2)}) collective-permute-start(f32[1,2,64,512]{3,2,1,0:T(8,128)S(1)} %bitcast.5), channel_id=1, source_target_pairs={{0,4},{1,5},{2,6},{3,7},{4,0},{5,1},{6,2},{7,3},{8,12},{9,13},{10,... | collective-permute-start | bytes 786440 | tf_op jit(solution)/shard_map/ppermute | solution.py:65
  15.0 11.3 %copy-start.2 = (f32[1024,512]{1,0:T(8,128)S(1)}, f32[1024,512]{1,0:T(8,128)}, u32[]{:S(2)}) copy-start(f32[1024,512]{1,0:T(8,128)} %refs_1_.10) | copy-start | bytes 6291460
  22.5 13.3 %collective-permute-start.4 = (f32[512,256]{1,0:T(8,128)S(1)}, f32[512,256]{1,0:T(8,128)S(1)}, u32[]{:S(2)}, u32[]{:S(2)}) collective-permute-start(f32[512,256]{1,0:T(8,128)S(1)} %get-tuple-element.90.refs_7_), channel_id=1, source_target_pairs={{8,0},{24,8},{16,24},{0,16},{9,1},{25,9},{17,25},{1,17},{2,10},{18... | collective-permute-start | bytes 1572872 | tf_op jit(solution)/shard_map/ppermute | solution.py:482
  24.1 12.6 %collective-permute-start.5 = (f32[2,2,64,512]{3,2,1,0:T(8,128)S(1)}, f32[2,2,64,512]{3,2,1,0:T(8,128)S(1)}, u32[]{:S(2)}, u32[]{:S(2)}) collective-permute-start(f32[2,2,64,512]{3,2,1,0:T(8,128)S(1)} %get-tuple-element.91.refs_5_), channel_id=1, source_target_pairs={{0,2},{1,3},{2,0},{3,1},{4,6},{5,7},{6,4},{7,5},{8,10},{9,11},{10,... | collective-permute-start | bytes 1572872 | tf_op jit(solution)/shard_map/ppermute | solution.py:65
  24.7 13.3 %collective-permute-start.3 = (f32[512,256]{1,0:T(8,128)S(1)}, f32[512,256]{1,0:T(8,128)S(1)}, u32[]{:S(2)}, u32[]{:S(2)}) collective-permute-start(f32[512,256]{1,0:T(8,128)S(1)} %get-tuple-element.89.refs_3_), channel_id=1, source_target_pairs={{0,8},{8,24},{24,16},{16,0},{1,9},{9,25},{25,17},{17,1},{10,2},{2,... | collective-permute-start | bytes 1572872 | tf_op jit(solution)/shard_map/ppermute | solution.py:482
  38.8 14.7 %collective-permute-start.9 = (f32[4,2,64,512]{3,2,1,0:T(8,128)S(1)}, f32[4,2,64,512]{3,2,1,0:T(8,128)S(1)}, u32[]{:S(2)}, u32[]{:S(2)}) collective-permute-start(f32[4,2,64,512]{3,2,1,0:T(8,128)S(1)} %get-tuple-element.95.refs_3_), channel_id=1, source_target_pairs={{0,1},{1,0},{2,3},{3,2},{4,5},{5,4},{6,7},{7,6},{8,9},{9,8},{10,11... | collective-permute-start | bytes 3145736 | tf_op jit(solution)/shard_map/ppermute | solution.py:65
  38.8 14.3 %collective-permute-start.8 = (f32[512,256]{1,0:T(8,128)S(1)}, f32[512,256]{1,0:T(8,128)S(1)}, u32[]{:S(2)}, u32[]{:S(2)}) collective-permute-start(f32[512,256]{1,0:T(8,128)S(1)} %get-tuple-element.94.refs_7_), channel_id=1, source_target_pairs={{8,0},{24,8},{16,24},{0,16},{9,1},{25,9},{17,25},{1,17},{2,10},{18... | collective-permute-start | bytes 1572872 | tf_op jit(solution)/shard_map/ppermute | solution.py:482
  39.4 14.0 %collective-permute-start.7 = (f32[512,256]{1,0:T(8,128)S(1)}, f32[512,256]{1,0:T(8,128)S(1)}, u32[]{:S(2)}, u32[]{:S(2)}) collective-permute-start(f32[512,256]{1,0:T(8,128)S(1)} %get-tuple-element.93.refs_4_.refs_3_), channel_id=1, source_target_pairs={{0,8},{8,24},{24,16},{16,0},{1,9},{9,25},{25,17},{17,1},{10,2},{2,... | collective-permute-start | bytes 1572872 | tf_op jit(solution)/shard_map/ppermute | solution.py:482
  54.2 14.1 %collective-permute-start.12 = (f32[512,256]{1,0:T(8,128)S(1)}, f32[512,256]{1,0:T(8,128)S(1)}, u32[]{:S(2)}, u32[]{:S(2)}) collective-permute-start(f32[512,256]{1,0:T(8,128)S(1)} %get-tuple-element.103), channel_id=1, source_target_pairs={{8,0},{24,8},{16,24},{0,16},{9,1},{25,9},{17,25},{1,17},{2,10},{18... | collective-permute-start | bytes 1572872 | tf_op jit(solution)/shard_map/ppermute | solution.py:482
  55.7 4.4 %copy-start.1 = (f32[3,64,512]{2,1,0:T(8,128)S(1)}, f32[3,64,512]{2,1,0:T(8,128)}, u32[]{:S(2)}) copy-start(f32[3,64,512]{2,1,0:T(8,128)} %refs_1_.15) | copy-start | bytes 1179652
  58.1 12.9 %collective-permute-start.13 = (f32[512,256]{1,0:T(8,128)S(1)}, f32[512,256]{1,0:T(8,128)S(1)}, u32[]{:S(2)}, u32[]{:S(2)}) collective-permute-start(f32[512,256]{1,0:T(8,128)S(1)} %get-tuple-element.104), channel_id=1, source_target_pairs={{0,2},{1,3},{2,0},{3,1},{4,6},{5,7},{6,4},{7,5},{8,10},{9,11},{10,... | collective-permute-start | bytes 1572872 | tf_op jit(solution)/shard_map/ppermute | solution.py:65
  58.6 12.7 %collective-permute-start.11 = (f32[512,256]{1,0:T(8,128)S(1)}, f32[512,256]{1,0:T(8,128)S(1)}, u32[]{:S(2)}, u32[]{:S(2)}) collective-permute-start(f32[512,256]{1,0:T(8,128)S(1)} %get-tuple-element.99.refs_11_), channel_id=1, source_target_pairs={{0,8},{8,24},{24,16},{16,0},{1,9},{9,25},{25,17},{17,1},{10,2},{2,... | collective-permute-start | bytes 1572872 | tf_op jit(solution)/shard_map/ppermute | solution.py:482
  60.1 1.4 collective-permute-start.10
  72.0 13.7 %collective-permute-start.14 = (f32[256,256]{1,0:T(8,128)S(1)}, f32[256,256]{1,0:T(8,128)S(1)}, u32[]{:S(2)}, u32[]{:S(2)}) collective-permute-start(f32[256,256]{1,0:T(8,128)S(1)} %get-tuple-element.107), channel_id=1, source_target_pairs={{0,4},{1,5},{2,6},{3,7},{4,0},{5,1},{6,2},{7,3},{8,12},{9,13},{10,... | collective-permute-start | bytes 786440 | tf_op jit(solution)/shard_map/ppermute | solution.py:65
  75.4 16.9 %collective-permute-start.18 = (f32[512,256]{1,0:T(8,128)S(1)}, f32[512,256]{1,0:T(8,128)S(1)}, u32[]{:S(2)}, u32[]{:S(2)}) collective-permute-start(f32[512,256]{1,0:T(8,128)S(1)} %get-tuple-element.114), channel_id=1, source_target_pairs={{8,0},{24,8},{16,24},{0,16},{9,1},{25,9},{17,25},{1,17},{2,10},{18... | collective-permute-start | bytes 1572872 | tf_op jit(solution)/shard_map/ppermute | solution.py:482
  76.1 16.3 %collective-permute-start.17 = (f32[512,256]{1,0:T(8,128)S(1)}, f32[512,256]{1,0:T(8,128)S(1)}, u32[]{:S(2)}, u32[]{:S(2)}) collective-permute-start(f32[512,256]{1,0:T(8,128)S(1)} %get-tuple-element.109.refs_11_), channel_id=1, source_target_pairs={{0,8},{8,24},{24,16},{16,0},{1,9},{9,25},{25,17},{17,1},{10,2},{2,... | collective-permute-start | bytes 1572872 | tf_op jit(solution)/shard_map/ppermute | solution.py:482
  79.9 18.9 %collective-permute-start.16 = (f32[512,256]{1,0:T(8,128)S(1)}, f32[512,256]{1,0:T(8,128)S(1)}, u32[]{:S(2)}, u32[]{:S(2)}) collective-permute-start(f32[512,256]{1,0:T(8,128)S(1)} %get-tuple-element.111.refs_3_), channel_id=1, source_target_pairs={{0,2},{1,3},{2,0},{3,1},{4,6},{5,7},{6,4},{7,5},{8,10},{9,11},{10,... | collective-permute-start | bytes 1572872 | tf_op jit(solution)/shard_map/ppermute | solution.py:65
  86.3 1.6 collective-permute-start.15
  94.8 21.3 %collective-permute-start.23 = (f32[512,256]{1,0:T(8,128)S(1)}, f32[512,256]{1,0:T(8,128)S(1)}, u32[]{:S(2)}, u32[]{:S(2)}) collective-permute-start(f32[512,256]{1,0:T(8,128)S(1)} %get-tuple-element.122.refs_3_), channel_id=1, source_target_pairs={{0,2},{1,3},{2,0},{3,1},{4,6},{5,7},{6,4},{7,5},{8,10},{9,11},{10,... | collective-permute-start | bytes 1572872 | tf_op jit(solution)/shard_map/ppermute | solution.py:65
  95.3 18.6 %collective-permute-start.20 = (f32[3,128,256]{2,1,0:T(8,128)S(1)}, f32[3,128,256]{2,1,0:T(8,128)S(1)}, u32[]{:S(2)}, u32[]{:S(2)}) collective-permute-start(f32[3,128,256]{2,1,0:T(8,128)S(1)} %get-tuple-element.119), channel_id=1, source_target_pairs={{0,8},{8,0},{16,24},{24,16},{1,9},{9,1},{17,25},{25,17},{2,10},{10... | collective-permute-start | bytes 1179656 | tf_op jit(solution)/shard_map/ppermute | solution.py:65
  96.8 19.3 %collective-permute-start.21 = (f32[3,128,256]{2,1,0:T(8,128)S(1)}, f32[3,128,256]{2,1,0:T(8,128)S(1)}, u32[]{:S(2)}, u32[]{:S(2)}) collective-permute-start(f32[3,128,256]{2,1,0:T(8,128)S(1)} %get-tuple-element.120), channel_id=1, source_target_pairs={{0,16},{8,24},{16,0},{24,8},{1,17},{9,25},{17,1},{25,9},{2,18},{10... | collective-permute-start | bytes 1179656 | tf_op jit(solution)/shard_map/ppermute | solution.py:65
  97.5 18.6 %collective-permute-start.22 = (f32[3,128,256]{2,1,0:T(8,128)S(1)}, f32[3,128,256]{2,1,0:T(8,128)S(1)}, u32[]{:S(2)}, u32[]{:S(2)}) collective-permute-start(f32[3,128,256]{2,1,0:T(8,128)S(1)} %get-tuple-element.121), channel_id=1, source_target_pairs={{0,24},{8,16},{16,8},{24,0},{1,25},{9,17},{17,9},{25,1},{2,26},{10... | collective-permute-start | bytes 1179656 | tf_op jit(solution)/shard_map/ppermute | solution.py:65
  99.4 13.0 %collective-permute-start.19 = (f32[256,256]{1,0:T(8,128)S(1)}, f32[256,256]{1,0:T(8,128)S(1)}, u32[]{:S(2)}, u32[]{:S(2)}) collective-permute-start(f32[256,256]{1,0:T(8,128)S(1)} %get-tuple-element.117), channel_id=1, source_target_pairs={{0,4},{1,5},{2,6},{3,7},{4,0},{5,1},{6,2},{7,3},{8,12},{9,13},{10,... | collective-permute-start | bytes 786440 | tf_op jit(solution)/shard_map/ppermute | solution.py:65
  112.4 9.2 %collective-permute-start.29 = (f32[2,128,256]{2,1,0:T(8,128)S(1)}, f32[2,128,256]{2,1,0:T(8,128)S(1)}, u32[]{:S(2)}, u32[]{:S(2)}) collective-permute-start(f32[2,128,256]{2,1,0:T(8,128)S(1)} %get-tuple-element.138), channel_id=1, source_target_pairs={{0,8},{8,0},{16,24},{24,16},{1,9},{9,1},{17,25},{25,17},{2,10},{10... | collective-permute-start | bytes 786440 | tf_op jit(solution)/shard_map/ppermute | solution.py:65
  114.0 13.2 %collective-permute-start.30 = (f32[2,128,256]{2,1,0:T(8,128)S(1)}, f32[2,128,256]{2,1,0:T(8,128)S(1)}, u32[]{:S(2)}, u32[]{:S(2)}) collective-permute-start(f32[2,128,256]{2,1,0:T(8,128)S(1)} %get-tuple-element.139), channel_id=1, source_target_pairs={{0,16},{8,24},{16,0},{24,8},{1,17},{9,25},{17,1},{25,9},{2,18},{10... | collective-permute-start | bytes 786440 | tf_op jit(solution)/shard_map/ppermute | solution.py:65
  116.1 14.3 %collective-permute-start.31 = (f32[2,128,256]{2,1,0:T(8,128)S(1)}, f32[2,128,256]{2,1,0:T(8,128)S(1)}, u32[]{:S(2)}, u32[]{:S(2)}) collective-permute-start(f32[2,128,256]{2,1,0:T(8,128)S(1)} %get-tuple-element.140), channel_id=1, source_target_pairs={{0,24},{8,16},{16,8},{24,0},{1,25},{9,17},{17,9},{25,1},{2,26},{10... | collective-permute-start | bytes 786440 | tf_op jit(solution)/shard_map/ppermute | solution.py:65
  116.9 21.2 %collective-permute-start.28 = (f32[256,256]{1,0:T(8,128)S(1)}, f32[256,256]{1,0:T(8,128)S(1)}, u32[]{:S(2)}, u32[]{:S(2)}) collective-permute-start(f32[256,256]{1,0:T(8,128)S(1)} %get-tuple-element.137), channel_id=1, source_target_pairs={{0,4},{1,5},{2,6},{3,7},{4,0},{5,1},{6,2},{7,3},{8,12},{9,13},{10,... | collective-permute-start | bytes 786440 | tf_op jit(solution)/shard_map/ppermute | solution.py:65
  120.4 17.7 %collective-permute-start.25 = (f32[3,32,256]{2,1,0:T(8,128)S(1)}, f32[3,32,256]{2,1,0:T(8,128)S(1)}, u32[]{:S(2)}, u32[]{:S(2)}) collective-permute-start(f32[3,32,256]{2,1,0:T(8,128)S(1)} %get-tuple-element.133), channel_id=1, source_target_pairs={{0,4},{1,5},{2,6},{3,7},{4,0},{5,1},{6,2},{7,3},{8,12},{9,13},{10,... | collective-permute-start | bytes 294920 | tf_op jit(solution)/shard_map/ppermute | solution.py:65
  121.7 16.4 %collective-permute-start.26 = (f32[3,32,256]{2,1,0:T(8,128)S(1)}, f32[3,32,256]{2,1,0:T(8,128)S(1)}, u32[]{:S(2)}, u32[]{:S(2)}) collective-permute-start(f32[3,32,256]{2,1,0:T(8,128)S(1)} %get-tuple-element.134), channel_id=1, source_target_pairs={{0,2},{1,3},{2,0},{3,1},{4,6},{5,7},{6,4},{7,5},{8,10},{9,11},{10,... | collective-permute-start | bytes 294920 | tf_op jit(solution)/shard_map/ppermute | solution.py:65
  127.1 11.0 %collective-permute-start.27 = (f32[3,32,256]{2,1,0:T(8,128)S(1)}, f32[3,32,256]{2,1,0:T(8,128)S(1)}, u32[]{:S(2)}, u32[]{:S(2)}) collective-permute-start(f32[3,32,256]{2,1,0:T(8,128)S(1)} %get-tuple-element.135), channel_id=1, source_target_pairs={{0,6},{1,7},{2,4},{3,5},{4,2},{5,3},{6,0},{7,1},{8,14},{9,15},{10,... | collective-permute-start | bytes 294920 | tf_op jit(solution)/shard_map/ppermute | solution.py:65
  138.8 5.3 %collective-permute-start.33 = (f32[3,16,256]{2,1,0:T(8,128)S(1)}, f32[3,16,256]{2,1,0:T(8,128)S(1)}, u32[]{:S(2)}, u32[]{:S(2)}) collective-permute-start(f32[3,16,256]{2,1,0:T(8,128)S(1)} %get-tuple-element.144), channel_id=1, source_target_pairs={{0,1},{1,0},{2,3},{3,2},{4,5},{5,4},{6,7},{7,6},{8,9},{9,8},{10,11... | collective-permute-start | bytes 147464 | tf_op jit(solution)/shard_map/ppermute | solution.py:65
  138.9 7.9 %collective-permute-start.34 = (f32[2,32,256]{2,1,0:T(8,128)S(1)}, f32[2,32,256]{2,1,0:T(8,128)S(1)}, u32[]{:S(2)}, u32[]{:S(2)}) collective-permute-start(f32[2,32,256]{2,1,0:T(8,128)S(1)} %get-tuple-element.146), channel_id=1, source_target_pairs={{0,4},{1,5},{2,6},{3,7},{4,0},{5,1},{6,2},{7,3},{8,12},{9,13},{10,... | collective-permute-start | bytes 196616 | tf_op jit(solution)/shard_map/ppermute | solution.py:65
  142.5 6.6 %collective-permute-start.35 = (f32[2,32,256]{2,1,0:T(8,128)S(1)}, f32[2,32,256]{2,1,0:T(8,128)S(1)}, u32[]{:S(2)}, u32[]{:S(2)}) collective-permute-start(f32[2,32,256]{2,1,0:T(8,128)S(1)} %get-tuple-element.147), channel_id=1, source_target_pairs={{0,2},{1,3},{2,0},{3,1},{4,6},{5,7},{6,4},{7,5},{8,10},{9,11},{10,... | collective-permute-start | bytes 196616 | tf_op jit(solution)/shard_map/ppermute | solution.py:65
  142.6 6.6 %collective-permute-start.36 = (f32[2,32,256]{2,1,0:T(8,128)S(1)}, f32[2,32,256]{2,1,0:T(8,128)S(1)}, u32[]{:S(2)}, u32[]{:S(2)}) collective-permute-start(f32[2,32,256]{2,1,0:T(8,128)S(1)} %get-tuple-element.148), channel_id=1, source_target_pairs={{0,6},{1,7},{2,4},{3,5},{4,2},{5,3},{6,0},{7,1},{8,14},{9,15},{10,... | collective-permute-start | bytes 196616 | tf_op jit(solution)/shard_map/ppermute | solution.py:65
  144.1 8.7 %collective-permute-start.24 = (f32[128,256]{1,0:T(8,128)S(1)}, f32[128,256]{1,0:T(8,128)S(1)}, u32[]{:S(2)}, u32[]{:S(2)}) collective-permute-start(f32[128,256]{1,0:T(8,128)S(1)} %get-tuple-element.131), channel_id=1, source_target_pairs={{0,1},{1,0},{2,3},{3,2},{4,5},{5,4},{6,7},{7,6},{8,9},{9,8},{10,11... | collective-permute-start | bytes 393224 | tf_op jit(solution)/shard_map/ppermute | solution.py:65
  144.1 9.2 %collective-permute-start.32 = (f32[128,256]{1,0:T(8,128)S(1)}, f32[128,256]{1,0:T(8,128)S(1)}, u32[]{:S(2)}, u32[]{:S(2)}) collective-permute-start(f32[128,256]{1,0:T(8,128)S(1)} %get-tuple-element.142), channel_id=1, source_target_pairs={{0,1},{1,0},{2,3},{3,2},{4,5},{5,4},{6,7},{7,6},{8,9},{9,8},{10,11... | collective-permute-start | bytes 393224 | tf_op jit(solution)/shard_map/ppermute | solution.py:65
  149.7 9.8 %collective-permute-start.39 = (f32[3,16,512]{2,1,0:T(8,128)S(1)}, f32[3,16,512]{2,1,0:T(8,128)S(1)}, u32[]{:S(2)}, u32[]{:S(2)}) collective-permute-start(f32[3,16,512]{2,1,0:T(8,128)S(1)} %get-tuple-element.149.refs_8_.refs_3_), channel_id=1, source_target_pairs={{0,24},{8,16},{16,8},{24,0},{1,25},{9,17},{17,9},{25,1},{2,26},{10... | collective-permute-start | bytes 294920 | tf_op jit(solution)/shard_map/ppermute | solution.py:65
  151.4 3.4 %collective-permute-start.40 = (f32[2,16,256]{2,1,0:T(8,128)S(1)}, f32[2,16,256]{2,1,0:T(8,128)S(1)}, u32[]{:S(2)}, u32[]{:S(2)}) collective-permute-start(f32[2,16,256]{2,1,0:T(8,128)S(1)} %get-tuple-element.152), channel_id=1, source_target_pairs={{0,1},{1,0},{2,3},{3,2},{4,5},{5,4},{6,7},{7,6},{8,9},{9,8},{10,11... | collective-permute-start | bytes 98312 | tf_op jit(solution)/shard_map/ppermute | solution.py:65
  151.4 8.7 %collective-permute-start.38 = (f32[3,16,512]{2,1,0:T(8,128)S(1)}, f32[3,16,512]{2,1,0:T(8,128)S(1)}, u32[]{:S(2)}, u32[]{:S(2)}) collective-permute-start(f32[3,16,512]{2,1,0:T(8,128)S(1)} %get-tuple-element.149.refs_8_.refs_3_), channel_id=1, source_target_pairs={{0,16},{8,24},{16,0},{24,8},{1,17},{9,25},{17,1},{25,9},{2,18},{10... | collective-permute-start | bytes 294920 | tf_op jit(solution)/shard_map/ppermute | solution.py:65
  152.8 7.3 %collective-permute-start.37 = (f32[3,16,512]{2,1,0:T(8,128)S(1)}, f32[3,16,512]{2,1,0:T(8,128)S(1)}, u32[]{:S(2)}, u32[]{:S(2)}) collective-permute-start(f32[3,16,512]{2,1,0:T(8,128)S(1)} %get-tuple-element.149.refs_8_.refs_3_), channel_id=1, source_target_pairs={{0,8},{8,0},{16,24},{24,16},{1,9},{9,1},{17,25},{25,17},{2,10},{10... | collective-permute-start | bytes 294920 | tf_op jit(solution)/shard_map/ppermute | solution.py:65
  154.8 1.1 copy-start
  156.5 5.4 %collective-permute-start.43 = (f32[2,16,512]{2,1,0:T(8,128)S(1)}, f32[2,16,512]{2,1,0:T(8,128)S(1)}, u32[]{:S(2)}, u32[]{:S(2)}) collective-permute-start(f32[2,16,512]{2,1,0:T(8,128)S(1)} %shard_map.101.refs_7_.refs_11_), channel_id=1, source_target_pairs={{0,24},{8,16},{16,8},{24,0},{1,25},{9,17},{17,9},{25,1},{2,26},{10... | collective-permute-start | bytes 196616 | tf_op jit(solution)/shard_map/ppermute | solution.py:65
  158.2 4.6 %collective-permute-start.42 = (f32[2,16,512]{2,1,0:T(8,128)S(1)}, f32[2,16,512]{2,1,0:T(8,128)S(1)}, u32[]{:S(2)}, u32[]{:S(2)}) collective-permute-start(f32[2,16,512]{2,1,0:T(8,128)S(1)} %shard_map.101.refs_7_.refs_11_), channel_id=1, source_target_pairs={{0,16},{8,24},{16,0},{24,8},{1,17},{9,25},{17,1},{25,9},{2,18},{10... | collective-permute-start | bytes 196616 | tf_op jit(solution)/shard_map/ppermute | solution.py:65
  159.6 4.3 %collective-permute-start.41 = (f32[2,16,512]{2,1,0:T(8,128)S(1)}, f32[2,16,512]{2,1,0:T(8,128)S(1)}, u32[]{:S(2)}, u32[]{:S(2)}) collective-permute-start(f32[2,16,512]{2,1,0:T(8,128)S(1)} %shard_map.101.refs_7_.refs_11_), channel_id=1, source_target_pairs={{0,8},{8,0},{16,24},{24,16},{1,9},{9,1},{17,25},{25,17},{2,10},{10... | collective-permute-start | bytes 196616 | tf_op jit(solution)/shard_map/ppermute | solution.py:65

commit v10 on v9

--- a/solution.py
+++ b/solution.py
@@ -124,16 +124,9 @@
     size = width // columns
     part = size // rows
     place = lax.broadcasted_iota(jnp.int32, out_ref.shape, 0)
-    inner = place % part
-    core = place // part % 2
-    level = place // (2 * part) % (columns // 2)
-    by_row = place // (2 * part * (columns // 2))
-    turned = jnp.zeros_like(level)
-    bits = (columns // 2).bit_length() - 1
-    for bit in range(bits):
-        turned = turned | (((level >> bit) & 1) << (bits - 1 - bit))
-    column = (turned * 2 + core) ^ info_ref[1]
-    wanted = column * size + (by_row ^ info_ref[0]) * part + inner
+    column = place // part % columns
+    by_row = place // (part * columns)
+    wanted = column * size + (by_row ^ info_ref[0]) * part + place % part
     hit = wanted == lax.broadcasted_iota(jnp.int32, out_ref.shape, 1)
     out_ref[...] = hit.astype(F32).astype(BF16)
 
@@ -396,10 +389,23 @@
         out[...] = total
 
 
+def pieces_step(info_ref, ins, outs):
+    columns, _, size, _ = outs[0].shape
+    for at in range(columns):
+        rows = pl.ds(at * size, size)
+        total = ins[0][:, rows]
+        for other in ins[1:]:
+            total = total + other[:, rows]
+        outs[0][at] = total
+
+
 def join_step(info_ref, ins, outs):
-    half = ins[0].shape[-1]
-    for side, value in enumerate(ins):
-        outs[0][:, :, block(core_of(info_ref) ^ side, half)] = value[...]
+    columns, _, _, half = ins[0].shape
+    for core in range(2):
+        total = ins[0][core]
+        for at in range(2 + core, columns, 2):
+            total = total + ins[0][at]
+        outs[0][:, :, core * half : (core + 1) * half] = total
 
 
 def step_kernel(tasks, info_ref, *refs):
@@ -587,15 +593,9 @@
     def total_flow(pieces):
         count, size, _ = pieces[0].shape
         inputs = [pieces[0]] + [swap(pieces[d], "row", row_count, d) for d in range(1, row_count)]
-        size //= levels
-        pieces = yield (halve_step, inputs, [shape(count, size, half)] * levels)
-        inputs = [pieces[0]]
-        for at in range(1, levels):
-            inputs.append(swap(pieces[at], "col", col_count, order[at] << 1))
-        size //= 2
-        keep, send = yield (halve_step, inputs, [shape(count, size, half)] * 2)
-        inputs = [keep, swap(send, "col", col_count, 1)]
-        (piece,) = yield (join_step, inputs, [shape(count, size, width)])
+        (sent,) = yield (pieces_step, inputs, [shape(col_count, count, part, half)])
+        arrived = lax.all_to_all(sent, "col", 0, 0, tiled=True)
+        (piece,) = yield (join_step, [arrived], [shape(count, part, width)])
         return [piece] + [swap(piece, "row", row_count, d) for d in range(1, row_count)]
 
     def parent_flow():
@@ -641,6 +641,7 @@
         names = [("sum", 1 + c) for c in range(children)]
         while any(name not in held for name in names + ["parent"]):
             yield WAIT
+        yield WAIT
         yield WAIT
         col, turned, _ = held["parent"]
         held["columns"] = heavy(

time: 166 us -> 176 us (1.060)
  waiting for transfers between devices: 62.1 us -> 74.1 us
  starting transfers between devices: 56.5 us -> 50 us
  local copies, waits for them, and re-layouts: 1.85 us -> 5.58 us
    ppermute x34 -> x26, starting transfers between devices: 43.6 us -> 29.1 us  [swap(): lax.ppermute(value, axis, [(place, place ^ change) for place in range(siz...]
    all_to_all x0 -> x2, starting transfers between devices: none -> 8.02 us  [total_flow(): arrived = lax.all_to_all(sent, 'col', 0, 0, tiled=True)]
    ppermute x34 -> x26, waiting for transfers between devices: 42.5 us -> 48.9 us  [swap(): lax.ppermute(value, axis, [(place, place ^ change) for place in range(siz...]
    all_to_all x0 -> x2, waiting for transfers between devices: none -> 5.6 us  [total_flow(): arrived = lax.all_to_all(sent, 'col', 0, 0, tiled=True)]
    unnamed x16 -> x30, local copies, waits for them, and re-layouts: 1.84 us -> 5.57 us
    pallas_call x27 -> x26, Pallas kernels: 43.9 us -> 44.6 us  [call(): pl.pallas_call(inner, out_shape=outs, in_specs=[pl.BlockSpec(memory_space...]
  transfers between devices with their start and end apart: 44 -> 38, of which waited for: 21 -> 22; matrix products, arithmetic and copies ran while one was open for 0% -> 0% of each run, Pallas kernels for 24% -> 22%
where the time goes in v10:
time: 176 us; the launch traced here: 175 us
  waiting for transfers between devices  74.1 us (42%)
  starting transfers between devices  50 us (28%)
  Pallas kernels  44.6 us (25%)
  local copies, waits for them, and re-layouts  5.58 us (3%)
    ppermute x26, waiting for transfers between devices, swap(): lax.ppermute(value, axis, [(place, place ^ change) for place in range(siz...  48.9 us
    pallas_call x26, Pallas kernels, call(): pl.pallas_call(inner, out_shape=outs, in_specs=[pl.BlockSpec(memory_space...  44.6 us
    ppermute x26, starting transfers between devices, swap(): lax.ppermute(value, axis, [(place, place ^ change) for place in range(siz...  29.1 us
    ppermute x10, waiting for transfers between devices, ring_flow(): lax.ppermute(moving[way], AXES, rings[way])  19.6 us
    ppermute x10, starting transfers between devices, ring_flow(): lax.ppermute(moving[way], AXES, rings[way])  13 us
    all_to_all x2, starting transfers between devices, total_flow(): arrived = lax.all_to_all(sent, 'col', 0, 0, tiled=True)  8.02 us
    all_to_all x2, waiting for transfers between devices, total_flow(): arrived = lax.all_to_all(sent, 'col', 0, 0, tiled=True)  5.6 us
    unnamed x30, local copies, waits for them, and re-layouts  5.57 us
  transfers between devices with their start and end apart: 38, of which 22 were waited for; matrix products, arithmetic and copies ran while one was open for 0% of the time, Pallas kernels for 22%

profile of v10, /device:TPU:0, one launch (start us, length us, event | category | flops | bytes accessed | tf_op | source)
XLA Modules:
  0.0 175.4 jit_solution(8257537263173707398)
XLA Ops:
  1.9 2.1 %shard_map.76 = (f32[512,256]{1,0:T(8,128)S(1)}, f32[512,256]{1,0:T(8,128)S(1)}) custom-call(s32[2]{0:T(128)S(1)} %pad_add_fusion.info_ref.refs_0_, s32[3,8]{1,0:T(4,128)S(1)} %copy-done.7, f32[3,1024,512]{2,1,0:T(8,128)} %refs_2_.9), custom_call_target="tpu_custom_call" | custom-call | flops 1024 | bytes 1024 | tf_op jit(solution)/shard_map/pallas_call | solution.py:89
  4.1 2.6 %collective-permute-start.1 = (f32[512,256]{1,0:T(8,128)S(1)}, f32[512,256]{1,0:T(8,128)S(1)}, u32[]{:S(2)}, u32[]{:S(2)}) collective-permute-start(f32[512,256]{1,0:T(8,128)S(1)} %get-tuple-element.78.refs_7_), channel_id=1, source_target_pairs={{8,0},{24,8},{16,24},{0,16},{9,1},{25,9},{17,25},{1,17},{2,10},{18... | collective-permute-start | bytes 1572872 | tf_op jit(solution)/shard_map/ppermute | solution.py:488
  6.7 3.1 %collective-permute-start.2 = (f32[1,2,64,512]{3,2,1,0:T(8,128)S(1)}, f32[1,2,64,512]{3,2,1,0:T(8,128)S(1)}, u32[]{:S(2)}, u32[]{:S(2)}) collective-permute-start(f32[1,2,64,512]{3,2,1,0:T(8,128)S(1)} %bitcast.5), channel_id=1, source_target_pairs={{0,4},{1,5},{2,6},{3,7},{4,0},{5,1},{6,2},{7,3},{8,12},{9,13},{10,... | collective-permute-start | bytes 786440 | tf_op jit(solution)/shard_map/ppermute | solution.py:65
  9.8 2.2 %shard_map.77 = (f32[512,256]{1,0:T(8,128)S(1)}, f32[512,256]{1,0:T(8,128)S(1)}, f32[512,256]{1,0:T(8,128)S(1)}, f32[512,256]{1,0:T(8,128)S(1)}) custom-call(s32[2]{0:T(128)S(1)} %pad_add_fusion.info_ref.refs_0_, s32[3,8]{1,0:T(4,128)S(1)} %copy-done.8, f32[3,1024,512]{2,1,0:T(8,128)} %refs_2_.9, f32[512,256]{1,0:T(8,128)S(1)} %get-tuple-element.69.refs_3_), custom_call_target="tpu_custom_call" | custom-call | flops 1024 | bytes 1024 | tf_op jit(solution)/shard_map/pallas_call | solution.py:89
  11.9 0.7 shard_map.78.refs_3_.refs_4_.refs_2_.refs_1_
  12.7 2.2 %shard_map.79 = (bf16[3,256,512]{2,1,0:T(8,128)(2,1)S(1)}, bf16[3,256,512]{2,1,0:T(8,128)(2,1)S(1)}, bf16[3,512,256]{2,1,0:T(8,128)(2,1)S(1)}, bf16[3,512,256]{2,1,0:T(8,128)(2,1)S(1)}) custom-call(s32[2]{0:T(128)S(1)} %pad_add_fusion.info_ref.refs_0_, s32[3,8]{1,0:T(4,128)S(1)} %copy-done.8, f32[3,1024,512]{2,1,0:T(8,128)S(1)} %bitcast.4, ...), custom_call_target="tpu_custom_call" | custom-call | flops 1024 | bytes 1024 | tf_op jit(solution)/shard_map/pallas_call | solution.py:89
  14.9 6.8 %collective-permute-done.2.refs_6_ = f32[1,2,64,512]{3,2,1,0:T(8,128)S(1)} collective-permute-done((f32[1,2,64,512]{3,2,1,0:T(8,128)S(1)}, f32[1,2,64,512]{3,2,1,0:T(8,128)S(1)}, u32[]{:S(2)}, u32[]{:S(2)}) %collective-permute-start.2) | collective-permute-done | bytes 262176 | tf_op jit(solution)/shard_map/ppermute | solution.py:65
  21.8 0.7 shard_map.80
  22.5 1.6 collective-permute-start.4
  24.7 1.5 collective-permute-start.3
  26.3 1.7 shard_map.81
  27.9 7.8 %collective-permute-done.4.refs_4_.refs_9_.refs_8_ = f32[512,256]{1,0:T(8,128)S(1)} collective-permute-done((f32[512,256]{1,0:T(8,128)S(1)}, f32[512,256]{1,0:T(8,128)S(1)}, u32[]{:S(2)}, u32[]{:S(2)}) %collective-permute-start.4) | collective-permute-done | bytes 524320 | tf_op jit(solution)/shard_map/ppermute | solution.py:488
  35.7 1.0 collective-permute-done.5.refs_6_
  36.7 1.3 collective-permute-done.3.refs_3_.refs_5_.refs_4_
  38.0 0.7 shard_map.82
  39.4 1.5 collective-permute-start.7
  40.9 2.2 %shard_map.83 = (bf16[512,1024]{1,0:T(8,128)(2,1)S(1)}, bf16[512,1024]{1,0:T(8,128)(2,1)S(1)}) custom-call(s32[2]{0:T(128)S(1)} %pad_add_fusion.info_ref.refs_0_, s32[3,8]{1,0:T(4,128)S(1)} %copy-done.8, f32[3,1024,512]{2,1,0:T(8,128)S(1)} %bitcast.4, bf16[512,512]{1,0:T(8,128)(2,1)S(1)} %shard_map.78.refs_3_.refs_4_.refs_2_.refs_1_, ...), custom_call_target="tpu_custom_call" | custom-call | flops 1024 | bytes 1024 | tf_op jit(solution)/shard_map/pallas_call | solution.py:89
  43.1 10.0 %collective-permute-done.8.refs_2_.refs_10_.refs_9_.refs_8_ = f32[512,256]{1,0:T(8,128)S(1)} collective-permute-done((f32[512,256]{1,0:T(8,128)S(1)}, f32[512,256]{1,0:T(8,128)S(1)}, u32[]{:S(2)}, u32[]{:S(2)}) %collective-permute-start.8) | collective-permute-done | bytes 524320 | tf_op jit(solution)/shard_map/ppermute | solution.py:488
  53.4 0.7 shard_map.84
  54.2 1.6 collective-permute-start.12
  55.7 2.4 %shard_map.85 = (f32[512,256]{1,0:T(8,128)S(1)}, f32[512,256]{1,0:T(8,128)S(1)}) custom-call(s32[2]{0:T(128)S(1)} %pad_add_fusion.info_ref.refs_0_, bf16[1024,1024]{1,0:T(8,128)(2,1)S(1)} %get-tuple-element.82.refs_7_.refs_1_, bf16[1024,1024]{1,0:T(8,128)(2,1)S(1)} %get-tuple-element.88.refs_2_, f32[512,256]{1,0:T(8,128)S(1)} %get-tuple-element.69.refs_3_, ...), custom_call_target="tpu_custom_call" | custom-call | flops 1024 | bytes 1024 | tf_op jit(solution)/shard_map/pallas_call | solution.py:89
  58.6 1.5 collective-permute-start.11
  60.2 1.3 collective-permute-done.10.refs_3_
  61.6 4.5 %shard_map.86 = (bf16[2,512,512]{2,1,0:T(8,128)(2,1)S(1)}, bf16[2,512,512]{2,1,0:T(8,128)(2,1)S(1)}, bf16[2,512,256]{2,1,0:T(8,128)(2,1)S(1)}, bf16[2,512,256]{2...) custom-call(s32[2]{0:T(128)S(1)} %pad_add_fusion.info_ref.refs_0_, ...), custom_call_target="tpu_custom_call" | custom-call | flops 1024 | bytes 1024 | tf_op jit(solution)/shard_map/pallas_call | solution.py:89
  66.1 2.2 %shard_map.87 = (bf16[512,1024]{1,0:T(8,128)(2,1)S(1)}, bf16[512,1024]{1,0:T(8,128)(2,1)S(1)}) custom-call(s32[2]{0:T(128)S(1)} %pad_add_fusion.info_ref.refs_0_, s32[3,8]{1,0:T(4,128)S(1)} %copy-done.8, f32[3,1024,512]{2,1,0:T(8,128)S(1)} %bitcast.4, bf16[512,512]{1,0:T(8,128)(2,1)S(1)} %shard_map.78.refs_3_.refs_4_.refs_2_.refs_1_, ...), custom_call_target="tpu_custom_call" | custom-call | flops 1024 | bytes 1024 | tf_op jit(solution)/shard_map/pallas_call | solution.py:89
  68.3 2.8 %collective-permute-done.13.refs_4_ = f32[512,256]{1,0:T(8,128)S(1)} collective-permute-done((f32[512,256]{1,0:T(8,128)S(1)}, f32[512,256]{1,0:T(8,128)S(1)}, u32[]{:S(2)}, u32[]{:S(2)}) %collective-permute-start.13) | collective-permute-done | bytes 524320 | tf_op jit(solution)/shard_map/ppermute | solution.py:65
  72.0 3.4 %collective-permute-start.14 = (f32[256,256]{1,0:T(8,128)S(1)}, f32[256,256]{1,0:T(8,128)S(1)}, u32[]{:S(2)}, u32[]{:S(2)}) collective-permute-start(f32[256,256]{1,0:T(8,128)S(1)} %get-tuple-element.97), channel_id=1, source_target_pairs={{0,4},{1,5},{2,6},{3,7},{4,0},{5,1},{6,2},{7,3},{8,12},{9,13},{10,... | collective-permute-start | bytes 786440 | tf_op jit(solution)/shard_map/ppermute | solution.py:65
  76.1 1.4 collective-permute-start.17
  77.5 2.4 %shard_map.89 = (f32[512,256]{1,0:T(8,128)S(1)}, f32[512,256]{1,0:T(8,128)S(1)}) custom-call(s32[2]{0:T(128)S(1)} %pad_add_fusion.info_ref.refs_0_, bf16[1024,1024]{1,0:T(8,128)(2,1)S(1)} %get-tuple-element.82.refs_7_.refs_1_, bf16[1024,1024]{1,0:T(8,128)(2,1)S(1)} %get-tuple-element.88.refs_2_, f32[512,256]{1,0:T(8,128)S(1)} %get-tuple-element.79.refs_3_, ...), custom_call_target="tpu_custom_call" | custom-call | flops 1024 | bytes 1024 | tf_op jit(solution)/shard_map/pallas_call | solution.py:89
  79.9 1.0 shard_map.90.refs_3_.refs_11_
  80.9 4.7 %collective-permute-done.14.refs_2_ = f32[256,256]{1,0:T(8,128)S(1)} collective-permute-done((f32[256,256]{1,0:T(8,128)S(1)}, f32[256,256]{1,0:T(8,128)S(1)}, u32[]{:S(2)}, u32[]{:S(2)}) %collective-permute-start.14) | collective-permute-done | bytes 262176 | tf_op jit(solution)/shard_map/ppermute | solution.py:65
  86.9 0.9 collective-permute-done.15.refs_10_
  87.8 4.4 %shard_map.92 = (f32[128,512]{1,0:T(8,128)S(1)}, f32[2,128,512]{2,1,0:T(8,128)S(1)}, bf16[2,256,512]{2,1,0:T(8,128)(2,1)S(1)}, bf16[2,256,512]{2,1,0:T(8,128)(2,...) custom-call(s32[2]{0:T(128)S(1)} %pad_add_fusion.info_ref.refs_0_, ...), custom_call_target="tpu_custom_call" | custom-call | flops 1024 | bytes 1024 | tf_op jit(solution)/shard_map/pallas_call | solution.py:89
  92.2 2.4 %shard_map.93 = (f32[512,256]{1,0:T(8,128)S(1)}, f32[512,256]{1,0:T(8,128)S(1)}) custom-call(s32[2]{0:T(128)S(1)} %pad_add_fusion.info_ref.refs_0_, bf16[1024,1024]{1,0:T(8,128)(2,1)S(1)} %get-tuple-element.82.refs_7_.refs_1_, bf16[1024,1024]{1,0:T(8,128)(2,1)S(1)} %get-tuple-element.88.refs_2_, f32[512,256]{1,0:T(8,128)S(1)} %get-tuple-element.83.refs_4_.refs_3_, ...), custom_call_target="tpu_custom_call" | custom-call | flops 1024 | bytes 1024 | tf_op jit(solution)/shard_map/pallas_call | solution.py:89
  95.3 1.5 collective-permute-start.20
  97.5 1.3 collective-permute-start.22
  98.8 2.2 %collective-permute-done.16.refs_2_ = f32[512,256]{1,0:T(8,128)S(1)} collective-permute-done((f32[512,256]{1,0:T(8,128)S(1)}, f32[512,256]{1,0:T(8,128)S(1)}, u32[]{:S(2)}, u32[]{:S(2)}) %collective-permute-start.16) | collective-permute-done | bytes 524320 | tf_op jit(solution)/shard_map/ppermute | solution.py:65
  101.7 2.0 %collective-permute-start.19 = (f32[256,256]{1,0:T(8,128)S(1)}, f32[256,256]{1,0:T(8,128)S(1)}, u32[]{:S(2)}, u32[]{:S(2)}) collective-permute-start(f32[256,256]{1,0:T(8,128)S(1)} %get-tuple-element.107), channel_id=1, source_target_pairs={{0,4},{1,5},{2,6},{3,7},{4,0},{5,1},{6,2},{7,3},{8,12},{9,13},{10,... | collective-permute-start | bytes 786440 | tf_op jit(solution)/shard_map/ppermute | solution.py:65
  103.7 1.0 shard_map.95.refs_12_.refs_13_
  104.7 3.3 %shard_map.96 = (f32[2,128,256]{2,1,0:T(8,128)S(1)}, f32[2,128,256]{2,1,0:T(8,128)}, f32[2,128,256]{2,1,0:T(8,128)}, f32[2,128,256]{2,1,0:T(8,128)S(1)}) custom-call(s32[2]{0:T(128)S(1)} %pad_add_fusion.info_ref.refs_0_, bf16[512,512]{1,0:T(8,128)(2,1)S(1)} %shard_map.78.refs_3_.refs_4_.refs_2_.refs_1_, ...), custom_call_target="tpu_custom_call" | custom-call | flops 1024 | bytes 1024 | tf_op jit(solution)/shard_map/pallas_call | solution.py:89
  108.0 7.5 %collective-permute-done.19.refs_2_ = f32[256,256]{1,0:T(8,128)S(1)} collective-permute-done((f32[256,256]{1,0:T(8,128)S(1)}, f32[256,256]{1,0:T(8,128)S(1)}, u32[]{:S(2)}, u32[]{:S(2)}) %collective-permute-start.19) | collective-permute-done | bytes 262176 | tf_op jit(solution)/shard_map/ppermute | solution.py:65
  115.9 1.5 collective-permute-done.23.refs_8_
  117.5 1.5 shard_map.97
  118.9 0.7 copy-done.10
  119.7 4.6 %all-to-all-start = ((f32[8,3,16,256]{3,2,1,0:T(8,128)}), f32[8,3,16,256]{3,2,1,0:T(8,128)S(1)}, u32[]{:S(2)}, u32[]{:S(2)}) async-start(f32[8,3,16,256]{3,2,1,0:T(8,128)} %get-tuple-element.122), calls=%async_computation | async-start | bytes 786432 | tf_op jit(solution)/shard_map/all_to_all | solution.py:597
  124.3 1.5 collective-permute-start.26
  126.5 1.3 collective-permute-start.28
  127.8 2.9 %collective-permute-start.25 = (f32[256,256]{1,0:T(8,128)}, f32[256,256]{1,0:T(8,128)S(1)}, u32[]{:S(2)}, u32[]{:S(2)}) collective-permute-start(f32[256,256]{1,0:T(8,128)} %copy-done.10), channel_id=1, source_target_pairs={{0,4},{1,5},{2,6},{3,7},{4,0},{5,1},{6,2},{7,3},{8,12},{9,13},{10,... | collective-permute-start | bytes 786440 | tf_op jit(solution)/shard_map/ppermute | solution.py:65
  130.7 2.9 %collective-permute-done.26.refs_5_ = f32[2,128,256]{2,1,0:T(8,128)S(1)} collective-permute-done((f32[2,128,256]{2,1,0:T(8,128)}, f32[2,128,256]{2,1,0:T(8,128)S(1)}, u32[]{:S(2)}, u32[]{:S(2)}) %collective-permute-start.26) | collective-permute-done | bytes 262176 | tf_op jit(solution)/shard_map/ppermute | solution.py:65
  133.6 6.5 %collective-permute-done.27.refs_6_ = f32[2,128,256]{2,1,0:T(8,128)S(1)} collective-permute-done((f32[2,128,256]{2,1,0:T(8,128)}, f32[2,128,256]{2,1,0:T(8,128)S(1)}, u32[]{:S(2)}, u32[]{:S(2)}) %collective-permute-start.27) | collective-permute-done | bytes 262176 | tf_op jit(solution)/shard_map/ppermute | solution.py:65
  140.1 8.0 %collective-permute-done.25.refs_3_ = f32[256,256]{1,0:T(8,128)S(1)} collective-permute-done((f32[256,256]{1,0:T(8,128)}, f32[256,256]{1,0:T(8,128)S(1)}, u32[]{:S(2)}, u32[]{:S(2)}) %collective-permute-start.25) | collective-permute-done | bytes 262176 | tf_op jit(solution)/shard_map/ppermute | solution.py:65
  148.1 0.7 copy-done.4
  148.8 0.9 copy-done.5
  150.4 0.7 copy-done.6
  151.7 3.4 %all-to-all-start.1 = ((f32[8,2,16,256]{3,2,1,0:T(8,128)}), f32[8,2,16,256]{3,2,1,0:T(8,128)S(1)}, u32[]{:S(2)}, u32[]{:S(2)}) async-start(f32[8,2,16,256]{3,2,1,0:T(8,128)} %copy-done.6), calls=%async_computation.1 | async-start | bytes 524288 | tf_op jit(solution)/shard_map/all_to_all | solution.py:597
  155.7 1.6 collective-permute-start.32
  157.4 1.3 collective-permute-start.31
  159.2 5.6 %all-to-all-done.1.refs_1_ = f32[8,2,16,256]{3,2,1,0:T(8,128)S(1)} async-done(((f32[8,2,16,256]{3,2,1,0:T(8,128)}), f32[8,2,16,256]{3,2,1,0:T(8,128)S(1)}, u32[]{:S(2)}, u32[]{:S(2)}) %all-to-all-start.1) | async-done | bytes 262176 | tf_op jit(solution)/shard_map/all_to_all | solution.py:597
  165.4 1.7 collective-permute-start.35
  167.1 1.3 collective-permute-start.34
  169.0 1.5 shard_map.100.refs_11_
  171.6 1.1 collective-permute-done.33.refs_8_
  172.7 1.1 copy-done
  173.9 1.5 shard_map.101
  (71 shorter events, 13.9 us)
Async XLA Ops:
  0.6 25.6 %collective-permute-start.6 = (f32[1024,512]{1,0:T(8,128)}, f32[1024,512]{1,0:T(8,128)S(1)}, u32[]{:S(2)}, u32[]{:S(2)}) collective-permute-start(f32[1024,512]{1,0:T(8,128)} %refs_1_.10), channel_id=1, source_target_pairs={{0,1},{1,0},{2,3},{3,2},{4,5},{5,4},{6,7},{7,6},{8,9},{9,8},{10,11... | collective-permute-start | bytes 6291464 | tf_op jit(solution)/shard_map/ppermute | solution.py:65
  1.2 0.7 copy-start.7
  1.9 4.8 %copy-start.3 = (f32[2,64,512]{2,1,0:T(8,128)S(1)}, f32[2,64,512]{2,1,0:T(8,128)}, u32[]{:S(2)}) copy-start(f32[2,64,512]{2,1,0:T(8,128)} %param.7) | copy-start | bytes 786436
  1.9 7.8 %copy-start.8 = (s32[3,8]{1,0:T(4,128)S(1)}, s32[3,8]{1,0:T(4,128)}, u32[]{:S(2)}) copy-start(s32[3,8]{1,0:T(4,128)} %refs_1_.14) | copy-start | bytes 292
  1.9 10.8 %slice-start = ((s8[6291456]{0:T(1024)(128)(4,1)}), s8[4194304]{0:T(1024)(128)(4,1)S(1)}, s32[]{:S(2)}) async-start(s8[6291456]{0:T(1024)(128)(4,1)} %bitcast.3), calls=%async_computation.2 | async-start | bytes 8388608
  4.1 17.7 %collective-permute-start.1 = (f32[512,256]{1,0:T(8,128)S(1)}, f32[512,256]{1,0:T(8,128)S(1)}, u32[]{:S(2)}, u32[]{:S(2)}) collective-permute-start(f32[512,256]{1,0:T(8,128)S(1)} %get-tuple-element.78.refs_7_), channel_id=1, source_target_pairs={{8,0},{24,8},{16,24},{0,16},{9,1},{25,9},{17,25},{1,17},{2,10},{18... | collective-permute-start | bytes 1572872 | tf_op jit(solution)/shard_map/ppermute | solution.py:488
  6.7 15.1 %collective-permute-start = (f32[512,256]{1,0:T(8,128)S(1)}, f32[512,256]{1,0:T(8,128)S(1)}, u32[]{:S(2)}, u32[]{:S(2)}) collective-permute-start(f32[512,256]{1,0:T(8,128)S(1)} %get-tuple-element.69.refs_3_), channel_id=1, source_target_pairs={{0,8},{8,24},{24,16},{16,0},{1,9},{9,25},{25,17},{17,1},{10,2},{2,... | collective-permute-start | bytes 1572872 | tf_op jit(solution)/shard_map/ppermute | solution.py:488
  6.7 6.0 %slice-start.1 = ((s8[6291456]{0:T(1024)(128)(4,1)}), s8[2097152]{0:T(1024)(128)(4,1)S(1)}, s32[]{:S(2)}) async-start(s8[6291456]{0:T(1024)(128)(4,1)} %bitcast.3), calls=%async_computation.3 | async-start | bytes 4194304
  6.7 15.1 %collective-permute-start.2 = (f32[1,2,64,512]{3,2,1,0:T(8,128)S(1)}, f32[1,2,64,512]{3,2,1,0:T(8,128)S(1)}, u32[]{:S(2)}, u32[]{:S(2)}) collective-permute-start(f32[1,2,64,512]{3,2,1,0:T(8,128)S(1)} %bitcast.5), channel_id=1, source_target_pairs={{0,4},{1,5},{2,6},{3,7},{4,0},{5,1},{6,2},{7,3},{8,12},{9,13},{10,... | collective-permute-start | bytes 786440 | tf_op jit(solution)/shard_map/ppermute | solution.py:65
  14.9 11.3 %copy-start.2 = (f32[1024,512]{1,0:T(8,128)S(1)}, f32[1024,512]{1,0:T(8,128)}, u32[]{:S(2)}) copy-start(f32[1024,512]{1,0:T(8,128)} %refs_1_.10) | copy-start | bytes 6291460
  22.5 13.3 %collective-permute-start.4 = (f32[512,256]{1,0:T(8,128)S(1)}, f32[512,256]{1,0:T(8,128)S(1)}, u32[]{:S(2)}, u32[]{:S(2)}) collective-permute-start(f32[512,256]{1,0:T(8,128)S(1)} %get-tuple-element.80.refs_7_), channel_id=1, source_target_pairs={{8,0},{24,8},{16,24},{0,16},{9,1},{25,9},{17,25},{1,17},{2,10},{18... | collective-permute-start | bytes 1572872 | tf_op jit(solution)/shard_map/ppermute | solution.py:488
  24.1 12.6 %collective-permute-start.5 = (f32[2,2,64,512]{3,2,1,0:T(8,128)S(1)}, f32[2,2,64,512]{3,2,1,0:T(8,128)S(1)}, u32[]{:S(2)}, u32[]{:S(2)}) collective-permute-start(f32[2,2,64,512]{3,2,1,0:T(8,128)S(1)} %get-tuple-element.81.refs_5_), channel_id=1, source_target_pairs={{0,2},{1,3},{2,0},{3,1},{4,6},{5,7},{6,4},{7,5},{8,10},{9,11},{10,... | collective-permute-start | bytes 1572872 | tf_op jit(solution)/shard_map/ppermute | solution.py:65
  24.7 13.3 %collective-permute-start.3 = (f32[512,256]{1,0:T(8,128)S(1)}, f32[512,256]{1,0:T(8,128)S(1)}, u32[]{:S(2)}, u32[]{:S(2)}) collective-permute-start(f32[512,256]{1,0:T(8,128)S(1)} %get-tuple-element.79.refs_3_), channel_id=1, source_target_pairs={{0,8},{8,24},{24,16},{16,0},{1,9},{9,25},{25,17},{17,1},{10,2},{2,... | collective-permute-start | bytes 1572872 | tf_op jit(solution)/shard_map/ppermute | solution.py:488
  38.8 14.7 %collective-permute-start.9 = (f32[4,2,64,512]{3,2,1,0:T(8,128)S(1)}, f32[4,2,64,512]{3,2,1,0:T(8,128)S(1)}, u32[]{:S(2)}, u32[]{:S(2)}) collective-permute-start(f32[4,2,64,512]{3,2,1,0:T(8,128)S(1)} %get-tuple-element.85.refs_3_), channel_id=1, source_target_pairs={{0,1},{1,0},{2,3},{3,2},{4,5},{5,4},{6,7},{7,6},{8,9},{9,8},{10,11... | collective-permute-start | bytes 3145736 | tf_op jit(solution)/shard_map/ppermute | solution.py:65
  38.8 14.3 %collective-permute-start.8 = (f32[512,256]{1,0:T(8,128)S(1)}, f32[512,256]{1,0:T(8,128)S(1)}, u32[]{:S(2)}, u32[]{:S(2)}) collective-permute-start(f32[512,256]{1,0:T(8,128)S(1)} %get-tuple-element.84.refs_7_), channel_id=1, source_target_pairs={{8,0},{24,8},{16,24},{0,16},{9,1},{25,9},{17,25},{1,17},{2,10},{18... | collective-permute-start | bytes 1572872 | tf_op jit(solution)/shard_map/ppermute | solution.py:488
  39.4 14.0 %collective-permute-start.7 = (f32[512,256]{1,0:T(8,128)S(1)}, f32[512,256]{1,0:T(8,128)S(1)}, u32[]{:S(2)}, u32[]{:S(2)}) collective-permute-start(f32[512,256]{1,0:T(8,128)S(1)} %get-tuple-element.83.refs_4_.refs_3_), channel_id=1, source_target_pairs={{0,8},{8,24},{24,16},{16,0},{1,9},{9,25},{25,17},{17,1},{10,2},{2,... | collective-permute-start | bytes 1572872 | tf_op jit(solution)/shard_map/ppermute | solution.py:488
  54.2 14.2 %collective-permute-start.12 = (f32[512,256]{1,0:T(8,128)S(1)}, f32[512,256]{1,0:T(8,128)S(1)}, u32[]{:S(2)}, u32[]{:S(2)}) collective-permute-start(f32[512,256]{1,0:T(8,128)S(1)} %get-tuple-element.93), channel_id=1, source_target_pairs={{8,0},{24,8},{16,24},{0,16},{9,1},{25,9},{17,25},{1,17},{2,10},{18... | collective-permute-start | bytes 1572872 | tf_op jit(solution)/shard_map/ppermute | solution.py:488
  55.7 4.4 %copy-start.1 = (f32[3,64,512]{2,1,0:T(8,128)S(1)}, f32[3,64,512]{2,1,0:T(8,128)}, u32[]{:S(2)}) copy-start(f32[3,64,512]{2,1,0:T(8,128)} %refs_1_.15) | copy-start | bytes 1179652
  58.1 12.9 %collective-permute-start.13 = (f32[512,256]{1,0:T(8,128)S(1)}, f32[512,256]{1,0:T(8,128)S(1)}, u32[]{:S(2)}, u32[]{:S(2)}) collective-permute-start(f32[512,256]{1,0:T(8,128)S(1)} %get-tuple-element.94), channel_id=1, source_target_pairs={{0,2},{1,3},{2,0},{3,1},{4,6},{5,7},{6,4},{7,5},{8,10},{9,11},{10,... | collective-permute-start | bytes 1572872 | tf_op jit(solution)/shard_map/ppermute | solution.py:65
  58.6 12.7 %collective-permute-start.11 = (f32[512,256]{1,0:T(8,128)S(1)}, f32[512,256]{1,0:T(8,128)S(1)}, u32[]{:S(2)}, u32[]{:S(2)}) collective-permute-start(f32[512,256]{1,0:T(8,128)S(1)} %get-tuple-element.89.refs_11_), channel_id=1, source_target_pairs={{0,8},{8,24},{24,16},{16,0},{1,9},{9,25},{25,17},{17,1},{10,2},{2,... | collective-permute-start | bytes 1572872 | tf_op jit(solution)/shard_map/ppermute | solution.py:488
  60.1 1.4 collective-permute-start.10
  72.0 13.6 %collective-permute-start.14 = (f32[256,256]{1,0:T(8,128)S(1)}, f32[256,256]{1,0:T(8,128)S(1)}, u32[]{:S(2)}, u32[]{:S(2)}) collective-permute-start(f32[256,256]{1,0:T(8,128)S(1)} %get-tuple-element.97), channel_id=1, source_target_pairs={{0,4},{1,5},{2,6},{3,7},{4,0},{5,1},{6,2},{7,3},{8,12},{9,13},{10,... | collective-permute-start | bytes 786440 | tf_op jit(solution)/shard_map/ppermute | solution.py:65
  75.4 16.8 %collective-permute-start.18 = (f32[512,256]{1,0:T(8,128)S(1)}, f32[512,256]{1,0:T(8,128)S(1)}, u32[]{:S(2)}, u32[]{:S(2)}) collective-permute-start(f32[512,256]{1,0:T(8,128)S(1)} %get-tuple-element.104), channel_id=1, source_target_pairs={{8,0},{24,8},{16,24},{0,16},{9,1},{25,9},{17,25},{1,17},{2,10},{18... | collective-permute-start | bytes 1572872 | tf_op jit(solution)/shard_map/ppermute | solution.py:488
  76.1 16.2 %collective-permute-start.17 = (f32[512,256]{1,0:T(8,128)S(1)}, f32[512,256]{1,0:T(8,128)S(1)}, u32[]{:S(2)}, u32[]{:S(2)}) collective-permute-start(f32[512,256]{1,0:T(8,128)S(1)} %get-tuple-element.99.refs_11_), channel_id=1, source_target_pairs={{0,8},{8,24},{24,16},{16,0},{1,9},{9,25},{25,17},{17,1},{10,2},{2,... | collective-permute-start | bytes 1572872 | tf_op jit(solution)/shard_map/ppermute | solution.py:488
  86.2 1.6 collective-permute-start.15
  86.3 14.8 %collective-permute-start.16 = (f32[512,256]{1,0:T(8,128)S(1)}, f32[512,256]{1,0:T(8,128)S(1)}, u32[]{:S(2)}, u32[]{:S(2)}) collective-permute-start(f32[512,256]{1,0:T(8,128)S(1)} %get-tuple-element.101.refs_3_), channel_id=1, source_target_pairs={{0,2},{1,3},{2,0},{3,1},{4,6},{5,7},{6,4},{7,5},{8,10},{9,11},{10,... | collective-permute-start | bytes 1572872 | tf_op jit(solution)/shard_map/ppermute | solution.py:65
  94.7 22.8 %collective-permute-start.23 = (f32[512,256]{1,0:T(8,128)S(1)}, f32[512,256]{1,0:T(8,128)S(1)}, u32[]{:S(2)}, u32[]{:S(2)}) collective-permute-start(f32[512,256]{1,0:T(8,128)S(1)} %get-tuple-element.112.refs_3_), channel_id=1, source_target_pairs={{0,2},{1,3},{2,0},{3,1},{4,6},{5,7},{6,4},{7,5},{8,10},{9,11},{10,... | collective-permute-start | bytes 1572872 | tf_op jit(solution)/shard_map/ppermute | solution.py:65
  95.3 20.2 %collective-permute-start.20 = (f32[3,128,256]{2,1,0:T(8,128)S(1)}, f32[3,128,256]{2,1,0:T(8,128)S(1)}, u32[]{:S(2)}, u32[]{:S(2)}) collective-permute-start(f32[3,128,256]{2,1,0:T(8,128)S(1)} %get-tuple-element.109), channel_id=1, source_target_pairs={{0,8},{8,0},{16,24},{24,16},{1,9},{9,1},{17,25},{25,17},{2,10},{10... | collective-permute-start | bytes 1179656 | tf_op jit(solution)/shard_map/ppermute | solution.py:65
  96.8 19.1 %collective-permute-start.21 = (f32[3,128,256]{2,1,0:T(8,128)S(1)}, f32[3,128,256]{2,1,0:T(8,128)S(1)}, u32[]{:S(2)}, u32[]{:S(2)}) collective-permute-start(f32[3,128,256]{2,1,0:T(8,128)S(1)} %get-tuple-element.110), channel_id=1, source_target_pairs={{0,16},{8,24},{16,0},{24,8},{1,17},{9,25},{17,1},{25,9},{2,18},{10... | collective-permute-start | bytes 1179656 | tf_op jit(solution)/shard_map/ppermute | solution.py:65
  97.5 18.4 %collective-permute-start.22 = (f32[3,128,256]{2,1,0:T(8,128)S(1)}, f32[3,128,256]{2,1,0:T(8,128)S(1)}, u32[]{:S(2)}, u32[]{:S(2)}) collective-permute-start(f32[3,128,256]{2,1,0:T(8,128)S(1)} %get-tuple-element.111), channel_id=1, source_target_pairs={{0,24},{8,16},{16,8},{24,0},{1,25},{9,17},{17,9},{25,1},{2,26},{10... | collective-permute-start | bytes 1179656 | tf_op jit(solution)/shard_map/ppermute | solution.py:65
  101.7 13.8 %collective-permute-start.19 = (f32[256,256]{1,0:T(8,128)S(1)}, f32[256,256]{1,0:T(8,128)S(1)}, u32[]{:S(2)}, u32[]{:S(2)}) collective-permute-start(f32[256,256]{1,0:T(8,128)S(1)} %get-tuple-element.107), channel_id=1, source_target_pairs={{0,4},{1,5},{2,6},{3,7},{4,0},{5,1},{6,2},{7,3},{8,12},{9,13},{10,... | collective-permute-start | bytes 786440 | tf_op jit(solution)/shard_map/ppermute | solution.py:65
  108.0 10.9 %copy-start.9 = (f32[2,128,256]{2,1,0:T(8,128)}, f32[2,128,256]{2,1,0:T(8,128)S(1)}, u32[]{:S(2)}) copy-start(f32[2,128,256]{2,1,0:T(8,128)S(1)} %get-tuple-element.127) | copy-start | bytes 786436
  118.9 0.7 copy-start.10
  119.7 29.1 %copy-start.11 = (f32[128,256]{1,0:T(8,128)}, f32[128,256]{1,0:T(8,128)S(1)}, u32[]{:S(2)}) copy-start(f32[128,256]{1,0:T(8,128)S(1)} %get-tuple-element.121) | copy-start | bytes 393220
  119.7 29.1 %all-to-all-start = ((f32[8,3,16,256]{3,2,1,0:T(8,128)}), f32[8,3,16,256]{3,2,1,0:T(8,128)S(1)}, u32[]{:S(2)}, u32[]{:S(2)}) async-start(f32[8,3,16,256]{3,2,1,0:T(8,128)} %get-tuple-element.122), calls=%async_computation | async-start | bytes 786432 | tf_op jit(solution)/shard_map/all_to_all | solution.py:597
  124.3 9.3 %collective-permute-start.26 = (f32[2,128,256]{2,1,0:T(8,128)}, f32[2,128,256]{2,1,0:T(8,128)S(1)}, u32[]{:S(2)}, u32[]{:S(2)}) collective-permute-start(f32[2,128,256]{2,1,0:T(8,128)} %get-tuple-element.125), channel_id=1, source_target_pairs={{0,8},{8,0},{16,24},{24,16},{1,9},{9,1},{17,25},{25,17},{2,10},{10... | collective-permute-start | bytes 786440 | tf_op jit(solution)/shard_map/ppermute | solution.py:65
  125.8 14.3 %collective-permute-start.27 = (f32[2,128,256]{2,1,0:T(8,128)}, f32[2,128,256]{2,1,0:T(8,128)S(1)}, u32[]{:S(2)}, u32[]{:S(2)}) collective-permute-start(f32[2,128,256]{2,1,0:T(8,128)} %get-tuple-element.126), channel_id=1, source_target_pairs={{0,16},{8,24},{16,0},{24,8},{1,17},{9,25},{17,1},{25,9},{2,18},{10... | collective-permute-start | bytes 786440 | tf_op jit(solution)/shard_map/ppermute | solution.py:65
  126.5 13.6 %collective-permute-start.28 = (f32[2,128,256]{2,1,0:T(8,128)}, f32[2,128,256]{2,1,0:T(8,128)S(1)}, u32[]{:S(2)}, u32[]{:S(2)}) collective-permute-start(f32[2,128,256]{2,1,0:T(8,128)} %copy-done.9), channel_id=1, source_target_pairs={{0,24},{8,16},{16,8},{24,0},{1,25},{9,17},{17,9},{25,1},{2,26},{10... | collective-permute-start | bytes 786440 | tf_op jit(solution)/shard_map/ppermute | solution.py:65
  127.8 20.3 %collective-permute-start.25 = (f32[256,256]{1,0:T(8,128)}, f32[256,256]{1,0:T(8,128)S(1)}, u32[]{:S(2)}, u32[]{:S(2)}) collective-permute-start(f32[256,256]{1,0:T(8,128)} %copy-done.10), channel_id=1, source_target_pairs={{0,4},{1,5},{2,6},{3,7},{4,0},{5,1},{6,2},{7,3},{8,12},{9,13},{10,... | collective-permute-start | bytes 786440 | tf_op jit(solution)/shard_map/ppermute | solution.py:65
  148.1 0.7 copy-start.4
  148.8 1.0 copy-start.5
  150.4 0.7 copy-start.6
  151.1 0.7 copy-start.12
  151.7 13.1 %all-to-all-start.1 = ((f32[8,2,16,256]{3,2,1,0:T(8,128)}), f32[8,2,16,256]{3,2,1,0:T(8,128)S(1)}, u32[]{:S(2)}, u32[]{:S(2)}) async-start(f32[8,2,16,256]{3,2,1,0:T(8,128)} %copy-done.6), calls=%async_computation.1 | async-start | bytes 524288 | tf_op jit(solution)/shard_map/all_to_all | solution.py:597
  155.2 10.2 %collective-permute-start.24 = (f32[128,256]{1,0:T(8,128)}, f32[128,256]{1,0:T(8,128)S(1)}, u32[]{:S(2)}, u32[]{:S(2)}) collective-permute-start(f32[128,256]{1,0:T(8,128)} %copy-done.11), channel_id=1, source_target_pairs={{0,1},{1,0},{2,3},{3,2},{4,5},{5,4},{6,7},{7,6},{8,9},{9,8},{10,11... | collective-permute-start | bytes 393224 | tf_op jit(solution)/shard_map/ppermute | solution.py:65
  155.6 12.9 %collective-permute-start.29 = (f32[128,256]{1,0:T(8,128)}, f32[128,256]{1,0:T(8,128)S(1)}, u32[]{:S(2)}, u32[]{:S(2)}) collective-permute-start(f32[128,256]{1,0:T(8,128)} %copy-done.12), channel_id=1, source_target_pairs={{0,1},{1,0},{2,3},{3,2},{4,5},{5,4},{6,7},{7,6},{8,9},{9,8},{10,11... | collective-permute-start | bytes 393224 | tf_op jit(solution)/shard_map/ppermute | solution.py:65
  155.7 11.4 %collective-permute-start.32 = (f32[3,16,512]{2,1,0:T(8,128)S(1)}, f32[3,16,512]{2,1,0:T(8,128)S(1)}, u32[]{:S(2)}, u32[]{:S(2)}) collective-permute-start(f32[3,16,512]{2,1,0:T(8,128)S(1)} %get-tuple-element.131.refs_2_.refs_3_), channel_id=1, source_target_pairs={{0,24},{8,16},{16,8},{24,0},{1,25},{9,17},{17,9},{25,1},{2,26},{10... | collective-permute-start | bytes 294920 | tf_op jit(solution)/shard_map/ppermute | solution.py:65
  157.4 13.1 %collective-permute-start.31 = (f32[3,16,512]{2,1,0:T(8,128)S(1)}, f32[3,16,512]{2,1,0:T(8,128)S(1)}, u32[]{:S(2)}, u32[]{:S(2)}) collective-permute-start(f32[3,16,512]{2,1,0:T(8,128)S(1)} %get-tuple-element.131.refs_2_.refs_3_), channel_id=1, source_target_pairs={{0,16},{8,24},{16,0},{24,8},{1,17},{9,25},{17,1},{25,9},{2,18},{10... | collective-permute-start | bytes 294920 | tf_op jit(solution)/shard_map/ppermute | solution.py:65
  158.7 11.8 %collective-permute-start.30 = (f32[3,16,512]{2,1,0:T(8,128)S(1)}, f32[3,16,512]{2,1,0:T(8,128)S(1)}, u32[]{:S(2)}, u32[]{:S(2)}) collective-permute-start(f32[3,16,512]{2,1,0:T(8,128)S(1)} %get-tuple-element.131.refs_2_.refs_3_), channel_id=1, source_target_pairs={{0,8},{8,0},{16,24},{24,16},{1,9},{9,1},{17,25},{25,17},{2,10},{10... | collective-permute-start | bytes 294920 | tf_op jit(solution)/shard_map/ppermute | solution.py:65
  165.4 5.8 %collective-permute-start.35 = (f32[2,16,512]{2,1,0:T(8,128)S(1)}, f32[2,16,512]{2,1,0:T(8,128)S(1)}, u32[]{:S(2)}, u32[]{:S(2)}) collective-permute-start(f32[2,16,512]{2,1,0:T(8,128)S(1)} %shard_map.99.refs_8_.refs_7_), channel_id=1, source_target_pairs={{0,24},{8,16},{16,8},{24,0},{1,25},{9,17},{17,9},{25,1},{2,26},{10... | collective-permute-start | bytes 196616 | tf_op jit(solution)/shard_map/ppermute | solution.py:65
  167.1 4.5 %collective-permute-start.34 = (f32[2,16,512]{2,1,0:T(8,128)S(1)}, f32[2,16,512]{2,1,0:T(8,128)S(1)}, u32[]{:S(2)}, u32[]{:S(2)}) collective-permute-start(f32[2,16,512]{2,1,0:T(8,128)S(1)} %shard_map.99.refs_8_.refs_7_), channel_id=1, source_target_pairs={{0,16},{8,24},{16,0},{24,8},{1,17},{9,25},{17,1},{25,9},{2,18},{10... | collective-permute-start | bytes 196616 | tf_op jit(solution)/shard_map/ppermute | solution.py:65
  168.4 4.3 %collective-permute-start.33 = (f32[2,16,512]{2,1,0:T(8,128)S(1)}, f32[2,16,512]{2,1,0:T(8,128)S(1)}, u32[]{:S(2)}, u32[]{:S(2)}) collective-permute-start(f32[2,16,512]{2,1,0:T(8,128)S(1)} %shard_map.99.refs_8_.refs_7_), channel_id=1, source_target_pairs={{0,8},{8,0},{16,24},{24,16},{1,9},{9,1},{17,25},{25,17},{2,10},{10... | collective-permute-start | bytes 196616 | tf_op jit(solution)/shard_map/ppermute | solution.py:65
  172.7 1.1 copy-start

commit v11 on v9

--- a/solution.py
+++ b/solution.py
@@ -340,22 +340,18 @@
 
 
 def finish_kernel(rows, info_ref, diag_ref, framed_ref, *refs):
-    parents, offspring = refs[:rows], refs[rows : 2 * rows]
-    diags_ref, uppers_ref = refs[2 * rows :]
-    part = parents[0].shape[1]
-
-    def chosen(pieces, row):
+    pieces = refs[:rows]
+    diags_ref, uppers_ref = refs[rows:]
+    part = pieces[0].shape[1]
+    children = uppers_ref.shape[0]
+    for row in range(rows):
+        at = slice(row * part, (row + 1) * part)
         value = pieces[0][...]
         for change in range(1, rows):
             value = jnp.where(info_ref[0] ^ change == row, pieces[change][...], value)
-        return value
-
-    for row in range(rows):
-        at = slice(row * part, (row + 1) * part)
-        above, below = chosen(parents, row), chosen(offspring, row)
-        diags_ref[0, at] = diag_ref[0, at] + above[0]
-        diags_ref[1:, at] = diag_ref[1:, at] + below
-        uppers_ref[:, at] = above[1:] - framed_ref[:, at]
+        diags_ref[0, at] = diag_ref[0, at] + value[0]
+        uppers_ref[:, at] = value[1 : 1 + children] - framed_ref[:, at]
+        diags_ref[1:, at] = diag_ref[1:, at] + value[1 + children :]
 
 
 def select_step(ratio, info_ref, ins, outs):
@@ -397,9 +393,13 @@
 
 
 def join_step(info_ref, ins, outs):
-    half = ins[0].shape[-1]
-    for side, value in enumerate(ins):
-        outs[0][:, :, block(core_of(info_ref) ^ side, half)] = value[...]
+    first = 0
+    for at in range(0, len(ins), 2):
+        count, _, half = ins[at].shape
+        for side in range(2):
+            columns = block(core_of(info_ref) ^ side, half)
+            outs[0][first : first + count, :, columns] = ins[at + side][...]
+        first += count
 
 
 def step_kernel(tasks, info_ref, *refs):
@@ -584,19 +584,30 @@
         mine, theirs = yield (part_step, [keep, arrived], [shape(size // 2, half)] * 2)
         held["sum", member] = [mine, swap(theirs, "col", col_count, 1)]
 
-    def total_flow(pieces):
+    def total_flow(name, pieces, direct):
         count, size, _ = pieces[0].shape
         inputs = [pieces[0]] + [swap(pieces[d], "row", row_count, d) for d in range(1, row_count)]
-        size //= levels
-        pieces = yield (halve_step, inputs, [shape(count, size, half)] * levels)
-        inputs = [pieces[0]]
-        for at in range(1, levels):
-            inputs.append(swap(pieces[at], "col", col_count, order[at] << 1))
+        if direct:
+            size //= levels
+            pieces = yield (halve_step, inputs, [shape(count, size, half)] * levels)
+            inputs = [pieces[0]]
+            for at in range(1, levels):
+                inputs.append(swap(pieces[at], "col", col_count, order[at] << 1))
+        else:
+            for bit in range(1, col_bits):
+                size //= 2
+                keep, send = yield (halve_step, inputs, [shape(count, size, half)] * 2)
+                inputs = [keep, swap(send, "col", col_count, 1 << bit)]
         size //= 2
         keep, send = yield (halve_step, inputs, [shape(count, size, half)] * 2)
-        inputs = [keep, swap(send, "col", col_count, 1)]
-        (piece,) = yield (join_step, inputs, [shape(count, size, width)])
-        return [piece] + [swap(piece, "row", row_count, d) for d in range(1, row_count)]
+        held[name] = [keep, swap(send, "col", col_count, 1)]
+
+    def gather_flow():
+        while "parent totals" not in held or "child totals" not in held:
+            yield WAIT
+        pairs = held["parent totals"] + held["child totals"]
+        (piece,) = yield (join_step, pairs, [shape(members + children, part, width)])
+        held["totals"] = [piece] + [swap(piece, "row", row_count, d) for d in range(1, row_count)]
 
     def parent_flow():
         names = [("last", 0), "links"]
@@ -620,7 +631,7 @@
         )
         held["parent"] = (col, turned, rest[:2])
         yield WAIT
-        held["parent totals"] = yield from total_flow(rest[2:])
+        yield from total_flow("parent totals", rest[2:], False)
 
     def child_flow():
         names = [("gram", 1 + c) for c in range(children)]
@@ -635,13 +646,14 @@
             smem=1, vmem=20,
         )
         yield WAIT
-        held["child totals"] = yield from total_flow(pieces)
+        yield from total_flow("child totals", pieces, True)
 
     def column_flow():
         names = [("sum", 1 + c) for c in range(children)]
         while any(name not in held for name in names + ["parent"]):
             yield WAIT
-        yield WAIT
+        while "totals" not in held:
+            yield WAIT
         col, turned, _ = held["parent"]
         held["columns"] = heavy(
             functools.partial(column_kernel, children, rows_here),
@@ -652,7 +664,7 @@
 
     flows = [ring_flow()] + [unit_flow(member) for member in range(children)]
     flows += [link_flow(), prepare_flow(), parent_flow()]
-    flows += [unit_flow(children), child_flow(), column_flow()]
+    flows += [unit_flow(children), child_flow(), gather_flow(), column_flow()]
     waiting = [(flow, None) for flow in flows]
     while waiting:
         tasks = [wish for _, wish in waiting if wish not in (None, WAIT)]
@@ -680,7 +692,7 @@
     diags, uppers = heavy(
         functools.partial(finish_kernel, row_count),
         [shape(members, diag_width, width), shape(children, diag_width, width)],
-        [info, diag_inverse, held["links"][4]] + held["parent totals"] + held["child totals"],
+        [info, diag_inverse, held["links"][4]] + held["totals"],
         smem=1,
     )
     return held["columns"], diags, uppers

time: 166 us -> 160 us (0.964)
  starting transfers between devices: 56.5 us -> 48.2 us
  waiting for transfers between devices: 62.1 us -> 64.4 us
    ppermute x34 -> x30, starting transfers between devices: 43.6 us -> 35.2 us  [swap(): lax.ppermute(value, axis, [(place, place ^ change) for place in range(siz...]
    ppermute x34 -> x30, waiting for transfers between devices: 42.5 us -> 44.8 us  [swap(): lax.ppermute(value, axis, [(place, place ^ change) for place in range(siz...]
  transfers between devices with their start and end apart: 44 -> 40, of which waited for: 21 -> 23; matrix products, arithmetic and copies ran while one was open for 0% -> 0% of each run, Pallas kernels for 24% -> 24%
where the time goes in v11:
time: 160 us; the launch traced here: 159 us
  waiting for transfers between devices  64.4 us (40%)
  starting transfers between devices  48.2 us (30%)
  Pallas kernels  43.9 us (27%)
  local copies, waits for them, and re-layouts  1.85 us (1%)
    ppermute x30, waiting for transfers between devices, swap(): lax.ppermute(value, axis, [(place, place ^ change) for place in range(siz...  44.8 us
    pallas_call x27, Pallas kernels, call(): pl.pallas_call(inner, out_shape=outs, in_specs=[pl.BlockSpec(memory_space...  43.9 us
    ppermute x30, starting transfers between devices, swap(): lax.ppermute(value, axis, [(place, place ^ change) for place in range(siz...  35.2 us
    ppermute x10, waiting for transfers between devices, ring_flow(): lax.ppermute(moving[way], AXES, rings[way])  19.6 us
    ppermute x10, starting transfers between devices, ring_flow(): lax.ppermute(moving[way], AXES, rings[way])  13 us
  transfers between devices with their start and end apart: 40, of which 23 were waited for; matrix products, arithmetic and copies ran while one was open for 0% of the time, Pallas kernels for 24%

profile of v11, /device:TPU:0, one launch (start us, length us, event | category | flops | bytes accessed | tf_op | source)
XLA Modules:
  0.0 159.3 jit_solution(6714443078953742487)
XLA Ops:
  1.2 0.7 copy-done.4
  1.9 2.1 %shard_map.76 = (f32[512,256]{1,0:T(8,128)S(1)}, f32[512,256]{1,0:T(8,128)S(1)}) custom-call(s32[2]{0:T(128)S(1)} %pad_add_fusion.info_ref.refs_0_, s32[3,8]{1,0:T(4,128)S(1)} %copy-done.4, f32[3,1024,512]{2,1,0:T(8,128)} %refs_2_.9), custom_call_target="tpu_custom_call" | custom-call | flops 1024 | bytes 1024 | tf_op jit(solution)/shard_map/pallas_call | solution.py:89
  4.1 2.6 %collective-permute-start.1 = (f32[512,256]{1,0:T(8,128)S(1)}, f32[512,256]{1,0:T(8,128)S(1)}, u32[]{:S(2)}, u32[]{:S(2)}) collective-permute-start(f32[512,256]{1,0:T(8,128)S(1)} %get-tuple-element.87.refs_7_), channel_id=1, source_target_pairs={{8,0},{24,8},{16,24},{0,16},{9,1},{25,9},{17,25},{1,17},{2,10},{18... | collective-permute-start | bytes 1572872 | tf_op jit(solution)/shard_map/ppermute | solution.py:482
  6.7 3.1 %collective-permute-start.2 = (f32[1,2,64,512]{3,2,1,0:T(8,128)S(1)}, f32[1,2,64,512]{3,2,1,0:T(8,128)S(1)}, u32[]{:S(2)}, u32[]{:S(2)}) collective-permute-start(f32[1,2,64,512]{3,2,1,0:T(8,128)S(1)} %bitcast.5), channel_id=1, source_target_pairs={{0,4},{1,5},{2,6},{3,7},{4,0},{5,1},{6,2},{7,3},{8,12},{9,13},{10,... | collective-permute-start | bytes 786440 | tf_op jit(solution)/shard_map/ppermute | solution.py:65
  9.8 2.2 %shard_map.77 = (f32[512,256]{1,0:T(8,128)S(1)}, f32[512,256]{1,0:T(8,128)S(1)}, f32[512,256]{1,0:T(8,128)S(1)}, f32[512,256]{1,0:T(8,128)S(1)}) custom-call(s32[2]{0:T(128)S(1)} %pad_add_fusion.info_ref.refs_0_, s32[3,8]{1,0:T(4,128)S(1)} %copy-done.5, f32[3,1024,512]{2,1,0:T(8,128)} %refs_2_.9, f32[512,256]{1,0:T(8,128)S(1)} %get-tuple-element.78.refs_3_), custom_call_target="tpu_custom_call" | custom-call | flops 1024 | bytes 1024 | tf_op jit(solution)/shard_map/pallas_call | solution.py:89
  11.9 0.8 shard_map.78.refs_3_.refs_4_.refs_2_.refs_1_
  12.8 2.2 %shard_map.79 = (bf16[3,256,512]{2,1,0:T(8,128)(2,1)S(1)}, bf16[3,256,512]{2,1,0:T(8,128)(2,1)S(1)}, bf16[3,512,256]{2,1,0:T(8,128)(2,1)S(1)}, bf16[3,512,256]{2,1,0:T(8,128)(2,1)S(1)}) custom-call(s32[2]{0:T(128)S(1)} %pad_add_fusion.info_ref.refs_0_, s32[3,8]{1,0:T(4,128)S(1)} %copy-done.5, f32[3,1024,512]{2,1,0:T(8,128)S(1)} %bitcast.4, ...), custom_call_target="tpu_custom_call" | custom-call | flops 1024 | bytes 1024 | tf_op jit(solution)/shard_map/pallas_call | solution.py:89
  15.0 6.8 %collective-permute-done.2.refs_6_ = f32[1,2,64,512]{3,2,1,0:T(8,128)S(1)} collective-permute-done((f32[1,2,64,512]{3,2,1,0:T(8,128)S(1)}, f32[1,2,64,512]{3,2,1,0:T(8,128)S(1)}, u32[]{:S(2)}, u32[]{:S(2)}) %collective-permute-start.2) | collective-permute-done | bytes 262176 | tf_op jit(solution)/shard_map/ppermute | solution.py:65
  21.8 0.7 shard_map.80
  22.5 1.6 %collective-permute-start.4 = (f32[512,256]{1,0:T(8,128)S(1)}, f32[512,256]{1,0:T(8,128)S(1)}, u32[]{:S(2)}, u32[]{:S(2)}) collective-permute-start(f32[512,256]{1,0:T(8,128)S(1)} %get-tuple-element.89.refs_7_), channel_id=1, source_target_pairs={{8,0},{24,8},{16,24},{0,16},{9,1},{25,9},{17,25},{1,17},{2,10},{18... | collective-permute-start | bytes 1572872 | tf_op jit(solution)/shard_map/ppermute | solution.py:482
  24.7 1.5 collective-permute-start.3
  26.3 1.7 %shard_map.81 = (bf16[1024,1024]{1,0:T(8,128)(2,1)S(1)}, bf16[1024,1024]{1,0:T(8,128)(2,1)S(1)}) custom-call(s32[2]{0:T(128)S(1)} %pad_add_fusion.info_ref.refs_0_, f32[1024,512]{1,0:T(8,128)S(1)} %copy-done.2, f32[1024,512]{1,0:T(8,128)S(1)} %collective-permute-done.6.refs_2_, f32[512,256]{1,0:T(8,128)S(1)} %get-tuple-element.88.refs_3_), custom_call_target="tpu_custom_call" | custom-call | flops 1024 | bytes 1024 | tf_op jit(solution)/shard_map/pallas_call | solution.py:89
  27.9 7.8 %collective-permute-done.4.refs_4_.refs_9_.refs_8_ = f32[512,256]{1,0:T(8,128)S(1)} collective-permute-done((f32[512,256]{1,0:T(8,128)S(1)}, f32[512,256]{1,0:T(8,128)S(1)}, u32[]{:S(2)}, u32[]{:S(2)}) %collective-permute-start.4) | collective-permute-done | bytes 524320 | tf_op jit(solution)/shard_map/ppermute | solution.py:482
  35.7 1.0 collective-permute-done.5.refs_6_
  36.7 1.3 collective-permute-done.3.refs_3_.refs_5_.refs_4_
  38.0 0.7 shard_map.82
  39.4 1.5 collective-permute-start.7
  40.9 2.2 %shard_map.83 = (bf16[512,1024]{1,0:T(8,128)(2,1)S(1)}, bf16[512,1024]{1,0:T(8,128)(2,1)S(1)}) custom-call(s32[2]{0:T(128)S(1)} %pad_add_fusion.info_ref.refs_0_, s32[3,8]{1,0:T(4,128)S(1)} %copy-done.5, f32[3,1024,512]{2,1,0:T(8,128)S(1)} %bitcast.4, bf16[512,512]{1,0:T(8,128)(2,1)S(1)} %shard_map.78.refs_3_.refs_4_.refs_2_.refs_1_, ...), custom_call_target="tpu_custom_call" | custom-call | flops 1024 | bytes 1024 | tf_op jit(solution)/shard_map/pallas_call | solution.py:89
  43.1 10.0 %collective-permute-done.8.refs_2_.refs_10_.refs_9_.refs_8_ = f32[512,256]{1,0:T(8,128)S(1)} collective-permute-done((f32[512,256]{1,0:T(8,128)S(1)}, f32[512,256]{1,0:T(8,128)S(1)}, u32[]{:S(2)}, u32[]{:S(2)}) %collective-permute-start.8) | collective-permute-done | bytes 524320 | tf_op jit(solution)/shard_map/ppermute | solution.py:482
  53.4 0.7 shard_map.84
  54.2 1.6 collective-permute-start.12
  55.7 2.4 %shard_map.85 = (f32[512,256]{1,0:T(8,128)S(1)}, f32[512,256]{1,0:T(8,128)S(1)}) custom-call(s32[2]{0:T(128)S(1)} %pad_add_fusion.info_ref.refs_0_, bf16[1024,1024]{1,0:T(8,128)(2,1)S(1)} %get-tuple-element.91.refs_7_.refs_1_, bf16[1024,1024]{1,0:T(8,128)(2,1)S(1)} %get-tuple-element.97.refs_2_, f32[512,256]{1,0:T(8,128)S(1)} %get-tuple-element.78.refs_3_, ...), custom_call_target="tpu_custom_call" | custom-call | flops 1024 | bytes 1024 | tf_op jit(solution)/shard_map/pallas_call | solution.py:89
  58.6 1.5 collective-permute-start.11
  60.2 1.3 collective-permute-done.10.refs_3_
  61.6 4.5 %shard_map.86 = (bf16[2,512,512]{2,1,0:T(8,128)(2,1)S(1)}, bf16[2,512,512]{2,1,0:T(8,128)(2,1)S(1)}, bf16[2,512,256]{2,1,0:T(8,128)(2,1)S(1)}, bf16[2,512,256]{2...) custom-call(s32[2]{0:T(128)S(1)} %pad_add_fusion.info_ref.refs_0_, ...), custom_call_target="tpu_custom_call" | custom-call | flops 1024 | bytes 1024 | tf_op jit(solution)/shard_map/pallas_call | solution.py:89
  66.1 2.2 %shard_map.87 = (bf16[512,1024]{1,0:T(8,128)(2,1)S(1)}, bf16[512,1024]{1,0:T(8,128)(2,1)S(1)}) custom-call(s32[2]{0:T(128)S(1)} %pad_add_fusion.info_ref.refs_0_, s32[3,8]{1,0:T(4,128)S(1)} %copy-done.5, f32[3,1024,512]{2,1,0:T(8,128)S(1)} %bitcast.4, bf16[512,512]{1,0:T(8,128)(2,1)S(1)} %shard_map.78.refs_3_.refs_4_.refs_2_.refs_1_, ...), custom_call_target="tpu_custom_call" | custom-call | flops 1024 | bytes 1024 | tf_op jit(solution)/shard_map/pallas_call | solution.py:89
  68.3 2.8 %collective-permute-done.13.refs_4_ = f32[512,256]{1,0:T(8,128)S(1)} collective-permute-done((f32[512,256]{1,0:T(8,128)S(1)}, f32[512,256]{1,0:T(8,128)S(1)}, u32[]{:S(2)}, u32[]{:S(2)}) %collective-permute-start.13) | collective-permute-done | bytes 524320 | tf_op jit(solution)/shard_map/ppermute | solution.py:65
  72.0 3.4 %collective-permute-start.14 = (f32[256,256]{1,0:T(8,128)S(1)}, f32[256,256]{1,0:T(8,128)S(1)}, u32[]{:S(2)}, u32[]{:S(2)}) collective-permute-start(f32[256,256]{1,0:T(8,128)S(1)} %get-tuple-element.106), channel_id=1, source_target_pairs={{0,4},{1,5},{2,6},{3,7},{4,0},{5,1},{6,2},{7,3},{8,12},{9,13},{10,... | collective-permute-start | bytes 786440 | tf_op jit(solution)/shard_map/ppermute | solution.py:65
  76.1 1.4 collective-permute-start.17
  77.5 2.4 %shard_map.89 = (f32[512,256]{1,0:T(8,128)S(1)}, f32[512,256]{1,0:T(8,128)S(1)}) custom-call(s32[2]{0:T(128)S(1)} %pad_add_fusion.info_ref.refs_0_, bf16[1024,1024]{1,0:T(8,128)(2,1)S(1)} %get-tuple-element.91.refs_7_.refs_1_, bf16[1024,1024]{1,0:T(8,128)(2,1)S(1)} %get-tuple-element.97.refs_2_, f32[512,256]{1,0:T(8,128)S(1)} %get-tuple-element.88.refs_3_, ...), custom_call_target="tpu_custom_call" | custom-call | flops 1024 | bytes 1024 | tf_op jit(solution)/shard_map/pallas_call | solution.py:89
  79.9 1.6 collective-permute-start.16
  81.5 1.0 shard_map.90.refs_3_.refs_11_
  82.5 3.2 %collective-permute-done.14.refs_2_ = f32[256,256]{1,0:T(8,128)S(1)} collective-permute-done((f32[256,256]{1,0:T(8,128)S(1)}, f32[256,256]{1,0:T(8,128)S(1)}, u32[]{:S(2)}, u32[]{:S(2)}) %collective-permute-start.14) | collective-permute-done | bytes 262176 | tf_op jit(solution)/shard_map/ppermute | solution.py:65
  86.4 1.5 collective-permute-done.15.refs_10_
  87.9 4.4 %shard_map.92 = (f32[128,512]{1,0:T(8,128)S(1)}, f32[2,128,512]{2,1,0:T(8,128)S(1)}, bf16[2,256,512]{2,1,0:T(8,128)(2,1)S(1)}, bf16[2,256,512]{2,1,0:T(8,128)(2,...) custom-call(s32[2]{0:T(128)S(1)} %pad_add_fusion.info_ref.refs_0_, ...), custom_call_target="tpu_custom_call" | custom-call | flops 1024 | bytes 1024 | tf_op jit(solution)/shard_map/pallas_call | solution.py:89
  92.3 2.4 %shard_map.93 = (f32[512,256]{1,0:T(8,128)S(1)}, f32[512,256]{1,0:T(8,128)S(1)}) custom-call(s32[2]{0:T(128)S(1)} %pad_add_fusion.info_ref.refs_0_, bf16[1024,1024]{1,0:T(8,128)(2,1)S(1)} %get-tuple-element.91.refs_7_.refs_1_, bf16[1024,1024]{1,0:T(8,128)(2,1)S(1)} %get-tuple-element.97.refs_2_, f32[512,256]{1,0:T(8,128)S(1)} %get-tuple-element.92.refs_4_.refs_3_, ...), custom_call_target="tpu_custom_call" | custom-call | flops 1024 | bytes 1024 | tf_op jit(solution)/shard_map/pallas_call | solution.py:89
  95.3 1.5 collective-permute-start.20
  96.8 0.7 collective-permute-start.21
  97.5 1.3 collective-permute-start.22
  99.4 3.5 %collective-permute-start.19 = (f32[256,256]{1,0:T(8,128)S(1)}, f32[256,256]{1,0:T(8,128)S(1)}, u32[]{:S(2)}, u32[]{:S(2)}) collective-permute-start(f32[256,256]{1,0:T(8,128)S(1)} %get-tuple-element.116), channel_id=1, source_target_pairs={{0,4},{1,5},{2,6},{3,7},{4,0},{5,1},{6,2},{7,3},{8,12},{9,13},{10,... | collective-permute-start | bytes 786440 | tf_op jit(solution)/shard_map/ppermute | solution.py:65
  102.9 1.0 shard_map.95.refs_12_.refs_13_
  103.9 2.6 %shard_map.96 = (f32[2,128,256]{2,1,0:T(8,128)S(1)}, f32[2,128,256]{2,1,0:T(8,128)S(1)}, f32[2,128,256]{2,1,0:T(8,128)S(1)}, f32[2,128,256]{2,1,0:T(8,128)S(1)}) custom-call(s32[2]{0:T(128)S(1)} %pad_add_fusion.info_ref.refs_0_, bf16[512,512]{1,0:T(8,128)(2,1)S(1)} %shard_map.78.refs_3_.refs_4_.refs_2_.refs_1_, ...), custom_call_target="tpu_custom_call" | custom-call | flops 1024 | bytes 1024 | tf_op jit(solution)/shard_map/pallas_call | solution.py:89
  106.5 5.9 %collective-permute-done.19.refs_2_ = f32[256,256]{1,0:T(8,128)S(1)} collective-permute-done((f32[256,256]{1,0:T(8,128)S(1)}, f32[256,256]{1,0:T(8,128)S(1)}, u32[]{:S(2)}, u32[]{:S(2)}) %collective-permute-start.19) | collective-permute-done | bytes 262176 | tf_op jit(solution)/shard_map/ppermute | solution.py:65
  112.4 1.5 collective-permute-start.27
  113.9 0.7 collective-permute-start.28
  114.6 1.4 collective-permute-done.21.refs_5_
  116.1 0.8 shard_map.97
  116.8 3.6 %collective-permute-start.26 = (f32[256,256]{1,0:T(8,128)S(1)}, f32[256,256]{1,0:T(8,128)S(1)}, u32[]{:S(2)}, u32[]{:S(2)}) collective-permute-start(f32[256,256]{1,0:T(8,128)S(1)} %get-tuple-element.134), channel_id=1, source_target_pairs={{0,4},{1,5},{2,6},{3,7},{4,0},{5,1},{6,2},{7,3},{8,12},{9,13},{10,... | collective-permute-start | bytes 786440 | tf_op jit(solution)/shard_map/ppermute | solution.py:65
  121.7 5.4 %collective-permute-done.28.refs_7_ = f32[2,128,256]{2,1,0:T(8,128)S(1)} collective-permute-done((f32[2,128,256]{2,1,0:T(8,128)S(1)}, f32[2,128,256]{2,1,0:T(8,128)S(1)}, u32[]{:S(2)}, u32[]{:S(2)}) %collective-permute-start.28) | collective-permute-done | bytes 262176 | tf_op jit(solution)/shard_map/ppermute | solution.py:65
  127.1 1.5 collective-permute-done.25.refs_2_
  128.6 2.1 %collective-permute-done.26.refs_4_ = f32[256,256]{1,0:T(8,128)S(1)} collective-permute-done((f32[256,256]{1,0:T(8,128)S(1)}, f32[256,256]{1,0:T(8,128)S(1)}, u32[]{:S(2)}, u32[]{:S(2)}) %collective-permute-start.26) | collective-permute-done | bytes 262176 | tf_op jit(solution)/shard_map/ppermute | solution.py:65
  131.4 2.4 %collective-permute-start.31 = (f32[3,32,256]{2,1,0:T(8,128)S(1)}, f32[3,32,256]{2,1,0:T(8,128)S(1)}, u32[]{:S(2)}, u32[]{:S(2)}) collective-permute-start(f32[3,32,256]{2,1,0:T(8,128)S(1)} %get-tuple-element.141), channel_id=1, source_target_pairs={{0,4},{1,5},{2,6},{3,7},{4,0},{5,1},{6,2},{7,3},{8,12},{9,13},{10,... | collective-permute-start | bytes 294920 | tf_op jit(solution)/shard_map/ppermute | solution.py:65
  134.4 1.2 collective-permute-start.33
  135.6 2.7 %collective-permute-start.34 = (f32[2,32,256]{2,1,0:T(8,128)S(1)}, f32[2,32,256]{2,1,0:T(8,128)S(1)}, u32[]{:S(2)}, u32[]{:S(2)}) collective-permute-start(f32[2,32,256]{2,1,0:T(8,128)S(1)} %get-tuple-element.145), channel_id=1, source_target_pairs={{0,6},{1,7},{2,4},{3,5},{4,2},{5,3},{6,0},{7,1},{8,14},{9,15},{10,... | collective-permute-start | bytes 196616 | tf_op jit(solution)/shard_map/ppermute | solution.py:65
  138.2 4.9 %collective-permute-done.32.refs_4_ = f32[2,32,256]{2,1,0:T(8,128)S(1)} collective-permute-done((f32[2,32,256]{2,1,0:T(8,128)S(1)}, f32[2,32,256]{2,1,0:T(8,128)S(1)}, u32[]{:S(2)}, u32[]{:S(2)}) %collective-permute-start.32) | collective-permute-done | bytes 65568 | tf_op jit(solution)/shard_map/ppermute | solution.py:65
  144.3 0.9 collective-permute-done.36.refs_4_
  145.7 1.7 %collective-permute-start.39 = (f32[5,16,512]{2,1,0:T(8,128)S(1)}, f32[5,16,512]{2,1,0:T(8,128)S(1)}, u32[]{:S(2)}, u32[]{:S(2)}) collective-permute-start(f32[5,16,512]{2,1,0:T(8,128)S(1)} %shard_map.100.refs_8_.refs_3_), channel_id=1, source_target_pairs={{0,24},{8,16},{16,8},{24,0},{1,25},{9,17},{17,9},{25,1},{2,26},{10... | collective-permute-start | bytes 491528 | tf_op jit(solution)/shard_map/ppermute | solution.py:65
  147.4 1.4 collective-permute-start.38
  149.8 0.8 collective-permute-done.24.refs_5_
  150.8 1.5 shard_map.101.refs_7_
  152.3 1.4 collective-permute-done.39.refs_6_
  153.7 2.9 %collective-permute-done.38.refs_5_ = f32[5,16,512]{2,1,0:T(8,128)S(1)} collective-permute-done((f32[5,16,512]{2,1,0:T(8,128)S(1)}, f32[5,16,512]{2,1,0:T(8,128)S(1)}, u32[]{:S(2)}, u32[]{:S(2)}) %collective-permute-start.38) | collective-permute-done | bytes 163872 | tf_op jit(solution)/shard_map/ppermute | solution.py:65
  156.6 1.1 copy-done
  157.8 1.6 shard_map.102
  (62 shorter events, 11.4 us)
Async XLA Ops:
  0.6 25.6 %collective-permute-start.6 = (f32[1024,512]{1,0:T(8,128)}, f32[1024,512]{1,0:T(8,128)S(1)}, u32[]{:S(2)}, u32[]{:S(2)}) collective-permute-start(f32[1024,512]{1,0:T(8,128)} %refs_1_.10), channel_id=1, source_target_pairs={{0,1},{1,0},{2,3},{3,2},{4,5},{5,4},{6,7},{7,6},{8,9},{9,8},{10,11... | collective-permute-start | bytes 6291464 | tf_op jit(solution)/shard_map/ppermute | solution.py:65
  1.2 0.7 copy-start.4
  1.9 4.8 %copy-start.3 = (f32[2,64,512]{2,1,0:T(8,128)S(1)}, f32[2,64,512]{2,1,0:T(8,128)}, u32[]{:S(2)}) copy-start(f32[2,64,512]{2,1,0:T(8,128)} %param.7) | copy-start | bytes 786436
  1.9 7.8 %copy-start.5 = (s32[3,8]{1,0:T(4,128)S(1)}, s32[3,8]{1,0:T(4,128)}, u32[]{:S(2)}) copy-start(s32[3,8]{1,0:T(4,128)} %refs_1_.14) | copy-start | bytes 292
  1.9 10.8 %slice-start = ((s8[6291456]{0:T(1024)(128)(4,1)}), s8[4194304]{0:T(1024)(128)(4,1)S(1)}, s32[]{:S(2)}) async-start(s8[6291456]{0:T(1024)(128)(4,1)} %bitcast.3), calls=%async_computation | async-start | bytes 8388608
  4.1 17.7 %collective-permute-start.1 = (f32[512,256]{1,0:T(8,128)S(1)}, f32[512,256]{1,0:T(8,128)S(1)}, u32[]{:S(2)}, u32[]{:S(2)}) collective-permute-start(f32[512,256]{1,0:T(8,128)S(1)} %get-tuple-element.87.refs_7_), channel_id=1, source_target_pairs={{8,0},{24,8},{16,24},{0,16},{9,1},{25,9},{17,25},{1,17},{2,10},{18... | collective-permute-start | bytes 1572872 | tf_op jit(solution)/shard_map/ppermute | solution.py:482
  6.7 15.1 %collective-permute-start = (f32[512,256]{1,0:T(8,128)S(1)}, f32[512,256]{1,0:T(8,128)S(1)}, u32[]{:S(2)}, u32[]{:S(2)}) collective-permute-start(f32[512,256]{1,0:T(8,128)S(1)} %get-tuple-element.78.refs_3_), channel_id=1, source_target_pairs={{0,8},{8,24},{24,16},{16,0},{1,9},{9,25},{25,17},{17,1},{10,2},{2,... | collective-permute-start | bytes 1572872 | tf_op jit(solution)/shard_map/ppermute | solution.py:482
  6.7 6.1 %slice-start.1 = ((s8[6291456]{0:T(1024)(128)(4,1)}), s8[2097152]{0:T(1024)(128)(4,1)S(1)}, s32[]{:S(2)}) async-start(s8[6291456]{0:T(1024)(128)(4,1)} %bitcast.3), calls=%async_computation.1 | async-start | bytes 4194304
  6.7 15.1 %collective-permute-start.2 = (f32[1,2,64,512]{3,2,1,0:T(8,128)S(1)}, f32[1,2,64,512]{3,2,1,0:T(8,128)S(1)}, u32[]{:S(2)}, u32[]{:S(2)}) collective-permute-start(f32[1,2,64,512]{3,2,1,0:T(8,128)S(1)} %bitcast.5), channel_id=1, source_target_pairs={{0,4},{1,5},{2,6},{3,7},{4,0},{5,1},{6,2},{7,3},{8,12},{9,13},{10,... | collective-permute-start | bytes 786440 | tf_op jit(solution)/shard_map/ppermute | solution.py:65
  15.0 11.3 %copy-start.2 = (f32[1024,512]{1,0:T(8,128)S(1)}, f32[1024,512]{1,0:T(8,128)}, u32[]{:S(2)}) copy-start(f32[1024,512]{1,0:T(8,128)} %refs_1_.10) | copy-start | bytes 6291460
  22.5 13.3 %collective-permute-start.4 = (f32[512,256]{1,0:T(8,128)S(1)}, f32[512,256]{1,0:T(8,128)S(1)}, u32[]{:S(2)}, u32[]{:S(2)}) collective-permute-start(f32[512,256]{1,0:T(8,128)S(1)} %get-tuple-element.89.refs_7_), channel_id=1, source_target_pairs={{8,0},{24,8},{16,24},{0,16},{9,1},{25,9},{17,25},{1,17},{2,10},{18... | collective-permute-start | bytes 1572872 | tf_op jit(solution)/shard_map/ppermute | solution.py:482
  24.1 12.6 %collective-permute-start.5 = (f32[2,2,64,512]{3,2,1,0:T(8,128)S(1)}, f32[2,2,64,512]{3,2,1,0:T(8,128)S(1)}, u32[]{:S(2)}, u32[]{:S(2)}) collective-permute-start(f32[2,2,64,512]{3,2,1,0:T(8,128)S(1)} %get-tuple-element.90.refs_5_), channel_id=1, source_target_pairs={{0,2},{1,3},{2,0},{3,1},{4,6},{5,7},{6,4},{7,5},{8,10},{9,11},{10,... | collective-permute-start | bytes 1572872 | tf_op jit(solution)/shard_map/ppermute | solution.py:65
  24.7 13.3 %collective-permute-start.3 = (f32[512,256]{1,0:T(8,128)S(1)}, f32[512,256]{1,0:T(8,128)S(1)}, u32[]{:S(2)}, u32[]{:S(2)}) collective-permute-start(f32[512,256]{1,0:T(8,128)S(1)} %get-tuple-element.88.refs_3_), channel_id=1, source_target_pairs={{0,8},{8,24},{24,16},{16,0},{1,9},{9,25},{25,17},{17,1},{10,2},{2,... | collective-permute-start | bytes 1572872 | tf_op jit(solution)/shard_map/ppermute | solution.py:482
  38.8 14.7 %collective-permute-start.9 = (f32[4,2,64,512]{3,2,1,0:T(8,128)S(1)}, f32[4,2,64,512]{3,2,1,0:T(8,128)S(1)}, u32[]{:S(2)}, u32[]{:S(2)}) collective-permute-start(f32[4,2,64,512]{3,2,1,0:T(8,128)S(1)} %get-tuple-element.94.refs_3_), channel_id=1, source_target_pairs={{0,1},{1,0},{2,3},{3,2},{4,5},{5,4},{6,7},{7,6},{8,9},{9,8},{10,11... | collective-permute-start | bytes 3145736 | tf_op jit(solution)/shard_map/ppermute | solution.py:65
  38.8 14.3 %collective-permute-start.8 = (f32[512,256]{1,0:T(8,128)S(1)}, f32[512,256]{1,0:T(8,128)S(1)}, u32[]{:S(2)}, u32[]{:S(2)}) collective-permute-start(f32[512,256]{1,0:T(8,128)S(1)} %get-tuple-element.93.refs_7_), channel_id=1, source_target_pairs={{8,0},{24,8},{16,24},{0,16},{9,1},{25,9},{17,25},{1,17},{2,10},{18... | collective-permute-start | bytes 1572872 | tf_op jit(solution)/shard_map/ppermute | solution.py:482
  39.4 14.0 %collective-permute-start.7 = (f32[512,256]{1,0:T(8,128)S(1)}, f32[512,256]{1,0:T(8,128)S(1)}, u32[]{:S(2)}, u32[]{:S(2)}) collective-permute-start(f32[512,256]{1,0:T(8,128)S(1)} %get-tuple-element.92.refs_4_.refs_3_), channel_id=1, source_target_pairs={{0,8},{8,24},{24,16},{16,0},{1,9},{9,25},{25,17},{17,1},{10,2},{2,... | collective-permute-start | bytes 1572872 | tf_op jit(solution)/shard_map/ppermute | solution.py:482
  54.2 14.1 %collective-permute-start.12 = (f32[512,256]{1,0:T(8,128)S(1)}, f32[512,256]{1,0:T(8,128)S(1)}, u32[]{:S(2)}, u32[]{:S(2)}) collective-permute-start(f32[512,256]{1,0:T(8,128)S(1)} %get-tuple-element.102), channel_id=1, source_target_pairs={{8,0},{24,8},{16,24},{0,16},{9,1},{25,9},{17,25},{1,17},{2,10},{18... | collective-permute-start | bytes 1572872 | tf_op jit(solution)/shard_map/ppermute | solution.py:482
  55.7 4.4 %copy-start.1 = (f32[3,64,512]{2,1,0:T(8,128)S(1)}, f32[3,64,512]{2,1,0:T(8,128)}, u32[]{:S(2)}) copy-start(f32[3,64,512]{2,1,0:T(8,128)} %refs_1_.15) | copy-start | bytes 1179652
  58.1 12.9 %collective-permute-start.13 = (f32[512,256]{1,0:T(8,128)S(1)}, f32[512,256]{1,0:T(8,128)S(1)}, u32[]{:S(2)}, u32[]{:S(2)}) collective-permute-start(f32[512,256]{1,0:T(8,128)S(1)} %get-tuple-element.103), channel_id=1, source_target_pairs={{0,2},{1,3},{2,0},{3,1},{4,6},{5,7},{6,4},{7,5},{8,10},{9,11},{10,... | collective-permute-start | bytes 1572872 | tf_op jit(solution)/shard_map/ppermute | solution.py:65
  58.6 12.7 %collective-permute-start.11 = (f32[512,256]{1,0:T(8,128)S(1)}, f32[512,256]{1,0:T(8,128)S(1)}, u32[]{:S(2)}, u32[]{:S(2)}) collective-permute-start(f32[512,256]{1,0:T(8,128)S(1)} %get-tuple-element.98.refs_11_), channel_id=1, source_target_pairs={{0,8},{8,24},{24,16},{16,0},{1,9},{9,25},{25,17},{17,1},{10,2},{2,... | collective-permute-start | bytes 1572872 | tf_op jit(solution)/shard_map/ppermute | solution.py:482
  60.1 1.4 collective-permute-start.10
  72.0 13.7 %collective-permute-start.14 = (f32[256,256]{1,0:T(8,128)S(1)}, f32[256,256]{1,0:T(8,128)S(1)}, u32[]{:S(2)}, u32[]{:S(2)}) collective-permute-start(f32[256,256]{1,0:T(8,128)S(1)} %get-tuple-element.106), channel_id=1, source_target_pairs={{0,4},{1,5},{2,6},{3,7},{4,0},{5,1},{6,2},{7,3},{8,12},{9,13},{10,... | collective-permute-start | bytes 786440 | tf_op jit(solution)/shard_map/ppermute | solution.py:65
  75.4 16.9 %collective-permute-start.18 = (f32[512,256]{1,0:T(8,128)S(1)}, f32[512,256]{1,0:T(8,128)S(1)}, u32[]{:S(2)}, u32[]{:S(2)}) collective-permute-start(f32[512,256]{1,0:T(8,128)S(1)} %get-tuple-element.113), channel_id=1, source_target_pairs={{8,0},{24,8},{16,24},{0,16},{9,1},{25,9},{17,25},{1,17},{2,10},{18... | collective-permute-start | bytes 1572872 | tf_op jit(solution)/shard_map/ppermute | solution.py:482
  76.1 16.3 %collective-permute-start.17 = (f32[512,256]{1,0:T(8,128)S(1)}, f32[512,256]{1,0:T(8,128)S(1)}, u32[]{:S(2)}, u32[]{:S(2)}) collective-permute-start(f32[512,256]{1,0:T(8,128)S(1)} %get-tuple-element.108.refs_11_), channel_id=1, source_target_pairs={{0,8},{8,24},{24,16},{16,0},{1,9},{9,25},{25,17},{17,1},{10,2},{2,... | collective-permute-start | bytes 1572872 | tf_op jit(solution)/shard_map/ppermute | solution.py:482
  79.9 18.9 %collective-permute-start.16 = (f32[512,256]{1,0:T(8,128)S(1)}, f32[512,256]{1,0:T(8,128)S(1)}, u32[]{:S(2)}, u32[]{:S(2)}) collective-permute-start(f32[512,256]{1,0:T(8,128)S(1)} %get-tuple-element.110.refs_3_), channel_id=1, source_target_pairs={{0,2},{1,3},{2,0},{3,1},{4,6},{5,7},{6,4},{7,5},{8,10},{9,11},{10,... | collective-permute-start | bytes 1572872 | tf_op jit(solution)/shard_map/ppermute | solution.py:65
  86.3 1.6 %collective-permute-start.15 = (f32[256,256]{1,0:T(8,128)S(1)}, f32[256,256]{1,0:T(8,128)S(1)}, u32[]{:S(2)}, u32[]{:S(2)}) collective-permute-start(f32[256,256]{1,0:T(8,128)S(1)} %shard_map.91.refs_9_.refs_11_), channel_id=1, source_target_pairs={{0,1},{1,0},{2,3},{3,2},{4,5},{5,4},{6,7},{7,6},{8,9},{9,8},{10,11... | collective-permute-start | bytes 786440 | tf_op jit(solution)/shard_map/ppermute | solution.py:65
  94.8 21.3 %collective-permute-start.23 = (f32[512,256]{1,0:T(8,128)S(1)}, f32[512,256]{1,0:T(8,128)S(1)}, u32[]{:S(2)}, u32[]{:S(2)}) collective-permute-start(f32[512,256]{1,0:T(8,128)S(1)} %get-tuple-element.121.refs_3_), channel_id=1, source_target_pairs={{0,2},{1,3},{2,0},{3,1},{4,6},{5,7},{6,4},{7,5},{8,10},{9,11},{10,... | collective-permute-start | bytes 1572872 | tf_op jit(solution)/shard_map/ppermute | solution.py:65
  95.3 18.7 %collective-permute-start.20 = (f32[3,128,256]{2,1,0:T(8,128)S(1)}, f32[3,128,256]{2,1,0:T(8,128)S(1)}, u32[]{:S(2)}, u32[]{:S(2)}) collective-permute-start(f32[3,128,256]{2,1,0:T(8,128)S(1)} %get-tuple-element.118), channel_id=1, source_target_pairs={{0,8},{8,0},{16,24},{24,16},{1,9},{9,1},{17,25},{25,17},{2,10},{10... | collective-permute-start | bytes 1179656 | tf_op jit(solution)/shard_map/ppermute | solution.py:65
  96.8 19.2 %collective-permute-start.21 = (f32[3,128,256]{2,1,0:T(8,128)S(1)}, f32[3,128,256]{2,1,0:T(8,128)S(1)}, u32[]{:S(2)}, u32[]{:S(2)}) collective-permute-start(f32[3,128,256]{2,1,0:T(8,128)S(1)} %get-tuple-element.119), channel_id=1, source_target_pairs={{0,16},{8,24},{16,0},{24,8},{1,17},{9,25},{17,1},{25,9},{2,18},{10... | collective-permute-start | bytes 1179656 | tf_op jit(solution)/shard_map/ppermute | solution.py:65
  97.5 18.6 %collective-permute-start.22 = (f32[3,128,256]{2,1,0:T(8,128)S(1)}, f32[3,128,256]{2,1,0:T(8,128)S(1)}, u32[]{:S(2)}, u32[]{:S(2)}) collective-permute-start(f32[3,128,256]{2,1,0:T(8,128)S(1)} %get-tuple-element.120), channel_id=1, source_target_pairs={{0,24},{8,16},{16,8},{24,0},{1,25},{9,17},{17,9},{25,1},{2,26},{10... | collective-permute-start | bytes 1179656 | tf_op jit(solution)/shard_map/ppermute | solution.py:65
  99.4 13.0 %collective-permute-start.19 = (f32[256,256]{1,0:T(8,128)S(1)}, f32[256,256]{1,0:T(8,128)S(1)}, u32[]{:S(2)}, u32[]{:S(2)}) collective-permute-start(f32[256,256]{1,0:T(8,128)S(1)} %get-tuple-element.116), channel_id=1, source_target_pairs={{0,4},{1,5},{2,6},{3,7},{4,0},{5,1},{6,2},{7,3},{8,12},{9,13},{10,... | collective-permute-start | bytes 786440 | tf_op jit(solution)/shard_map/ppermute | solution.py:65
  112.4 9.2 %collective-permute-start.27 = (f32[2,128,256]{2,1,0:T(8,128)S(1)}, f32[2,128,256]{2,1,0:T(8,128)S(1)}, u32[]{:S(2)}, u32[]{:S(2)}) collective-permute-start(f32[2,128,256]{2,1,0:T(8,128)S(1)} %get-tuple-element.135), channel_id=1, source_target_pairs={{0,8},{8,0},{16,24},{24,16},{1,9},{9,1},{17,25},{25,17},{2,10},{10... | collective-permute-start | bytes 786440 | tf_op jit(solution)/shard_map/ppermute | solution.py:65
  113.9 13.2 %collective-permute-start.28 = (f32[2,128,256]{2,1,0:T(8,128)S(1)}, f32[2,128,256]{2,1,0:T(8,128)S(1)}, u32[]{:S(2)}, u32[]{:S(2)}) collective-permute-start(f32[2,128,256]{2,1,0:T(8,128)S(1)} %get-tuple-element.136), channel_id=1, source_target_pairs={{0,16},{8,24},{16,0},{24,8},{1,17},{9,25},{17,1},{25,9},{2,18},{10... | collective-permute-start | bytes 786440 | tf_op jit(solution)/shard_map/ppermute | solution.py:65
  116.1 11.0 %collective-permute-start.29 = (f32[2,128,256]{2,1,0:T(8,128)S(1)}, f32[2,128,256]{2,1,0:T(8,128)S(1)}, u32[]{:S(2)}, u32[]{:S(2)}) collective-permute-start(f32[2,128,256]{2,1,0:T(8,128)S(1)} %get-tuple-element.137), channel_id=1, source_target_pairs={{0,24},{8,16},{16,8},{24,0},{1,25},{9,17},{17,9},{25,1},{2,26},{10... | collective-permute-start | bytes 786440 | tf_op jit(solution)/shard_map/ppermute | solution.py:65
  116.8 13.9 %collective-permute-start.26 = (f32[256,256]{1,0:T(8,128)S(1)}, f32[256,256]{1,0:T(8,128)S(1)}, u32[]{:S(2)}, u32[]{:S(2)}) collective-permute-start(f32[256,256]{1,0:T(8,128)S(1)} %get-tuple-element.134), channel_id=1, source_target_pairs={{0,4},{1,5},{2,6},{3,7},{4,0},{5,1},{6,2},{7,3},{8,12},{9,13},{10,... | collective-permute-start | bytes 786440 | tf_op jit(solution)/shard_map/ppermute | solution.py:65
  120.4 8.2 %collective-permute-start.25 = (f32[3,64,256]{2,1,0:T(8,128)S(1)}, f32[3,64,256]{2,1,0:T(8,128)S(1)}, u32[]{:S(2)}, u32[]{:S(2)}) collective-permute-start(f32[3,64,256]{2,1,0:T(8,128)S(1)} %get-tuple-element.132), channel_id=1, source_target_pairs={{0,2},{1,3},{2,0},{3,1},{4,6},{5,7},{6,4},{7,5},{8,10},{9,11},{10,... | collective-permute-start | bytes 589832 | tf_op jit(solution)/shard_map/ppermute | solution.py:65
  131.4 11.7 %collective-permute-start.31 = (f32[3,32,256]{2,1,0:T(8,128)S(1)}, f32[3,32,256]{2,1,0:T(8,128)S(1)}, u32[]{:S(2)}, u32[]{:S(2)}) collective-permute-start(f32[3,32,256]{2,1,0:T(8,128)S(1)} %get-tuple-element.141), channel_id=1, source_target_pairs={{0,4},{1,5},{2,6},{3,7},{4,0},{5,1},{6,2},{7,3},{8,12},{9,13},{10,... | collective-permute-start | bytes 294920 | tf_op jit(solution)/shard_map/ppermute | solution.py:65
  133.9 9.3 %collective-permute-start.32 = (f32[2,32,256]{2,1,0:T(8,128)S(1)}, f32[2,32,256]{2,1,0:T(8,128)S(1)}, u32[]{:S(2)}, u32[]{:S(2)}) collective-permute-start(f32[2,32,256]{2,1,0:T(8,128)S(1)} %get-tuple-element.143), channel_id=1, source_target_pairs={{0,4},{1,5},{2,6},{3,7},{4,0},{5,1},{6,2},{7,3},{8,12},{9,13},{10,... | collective-permute-start | bytes 196616 | tf_op jit(solution)/shard_map/ppermute | solution.py:65
  134.4 8.7 %collective-permute-start.33 = (f32[2,32,256]{2,1,0:T(8,128)S(1)}, f32[2,32,256]{2,1,0:T(8,128)S(1)}, u32[]{:S(2)}, u32[]{:S(2)}) collective-permute-start(f32[2,32,256]{2,1,0:T(8,128)S(1)} %get-tuple-element.144), channel_id=1, source_target_pairs={{0,2},{1,3},{2,0},{3,1},{4,6},{5,7},{6,4},{7,5},{8,10},{9,11},{10,... | collective-permute-start | bytes 196616 | tf_op jit(solution)/shard_map/ppermute | solution.py:65
  135.6 7.5 %collective-permute-start.34 = (f32[2,32,256]{2,1,0:T(8,128)S(1)}, f32[2,32,256]{2,1,0:T(8,128)S(1)}, u32[]{:S(2)}, u32[]{:S(2)}) collective-permute-start(f32[2,32,256]{2,1,0:T(8,128)S(1)} %get-tuple-element.145), channel_id=1, source_target_pairs={{0,6},{1,7},{2,4},{3,5},{4,2},{5,3},{6,0},{7,1},{8,14},{9,15},{10,... | collective-permute-start | bytes 196616 | tf_op jit(solution)/shard_map/ppermute | solution.py:65
  143.7 1.4 collective-permute-start.35
  143.8 1.4 collective-permute-start.36
  145.7 8.0 %collective-permute-start.39 = (f32[5,16,512]{2,1,0:T(8,128)S(1)}, f32[5,16,512]{2,1,0:T(8,128)S(1)}, u32[]{:S(2)}, u32[]{:S(2)}) collective-permute-start(f32[5,16,512]{2,1,0:T(8,128)S(1)} %shard_map.100.refs_8_.refs_3_), channel_id=1, source_target_pairs={{0,24},{8,16},{16,8},{24,0},{1,25},{9,17},{17,9},{25,1},{2,26},{10... | collective-permute-start | bytes 491528 | tf_op jit(solution)/shard_map/ppermute | solution.py:65
  147.4 9.2 %collective-permute-start.38 = (f32[5,16,512]{2,1,0:T(8,128)S(1)}, f32[5,16,512]{2,1,0:T(8,128)S(1)}, u32[]{:S(2)}, u32[]{:S(2)}) collective-permute-start(f32[5,16,512]{2,1,0:T(8,128)S(1)} %shard_map.100.refs_8_.refs_3_), channel_id=1, source_target_pairs={{0,16},{8,24},{16,0},{24,8},{1,17},{9,25},{17,1},{25,9},{2,18},{10... | collective-permute-start | bytes 491528 | tf_op jit(solution)/shard_map/ppermute | solution.py:65
  148.8 7.9 %collective-permute-start.37 = (f32[5,16,512]{2,1,0:T(8,128)S(1)}, f32[5,16,512]{2,1,0:T(8,128)S(1)}, u32[]{:S(2)}, u32[]{:S(2)}) collective-permute-start(f32[5,16,512]{2,1,0:T(8,128)S(1)} %shard_map.100.refs_8_.refs_3_), channel_id=1, source_target_pairs={{0,8},{8,0},{16,24},{24,16},{1,9},{9,1},{17,25},{25,17},{2,10},{10... | collective-permute-start | bytes 491528 | tf_op jit(solution)/shard_map/ppermute | solution.py:65
  149.3 1.3 collective-permute-start.24
  149.3 1.5 collective-permute-start.30
  156.6 1.1 copy-start

commit v12 on v11

--- a/solution.py
+++ b/solution.py
@@ -73,7 +73,7 @@
     return info_ref[1] & 1
 
 
-def call(body, outs, args, smem=0, hbm=0, scratch=(), vmem=8, after=None):
+def call(body, outs, args, smem=0, hbm=0, scratch=(), vmem=8, after=None, target=pltpu.VMEM):
     places = [pltpu.SMEM] * smem + [pltpu.HBM] * hbm
     places += [pltpu.VMEM] * (len(args) - len(places))
     count = len(args)
@@ -90,7 +90,7 @@
         inner,
         out_shape=outs,
         in_specs=[pl.BlockSpec(memory_space=place) for place in places],
-        out_specs=[pl.BlockSpec(memory_space=pltpu.VMEM)] * len(outs),
+        out_specs=[pl.BlockSpec(memory_space=target)] * len(outs),
         scratch_shapes=scratch,
         compiler_params=pltpu.CompilerParams(vmem_limit_bytes=vmem * MIB),
         cost_estimate=pl.CostEstimate(flops=1024, bytes_accessed=1024, transcendentals=0),
@@ -326,17 +326,20 @@
 
 
 def column_kernel(children, rows_here, info_ref, listed_ref, col_ref, turned_ref, *refs):
-    out_ref = refs[-1]
+    *refs, out_ref, held_ref, sem = refs
     rows, width = col_ref.shape
     half = width // 2
     core = core_of(info_ref)
-    out_ref[0] = col_ref[...]
+    held_ref[0] = col_ref[...]
     for c in range(children):
         weight = own_weight(info_ref, listed_ref, c + 1, 2 * rows, rows_here, width)
         for side in range(2):
             columns = block(core ^ side, half)
             total = refs[2 * c + side][...] + turned_ref[c, :, columns]
-            out_ref[c + 1, :, columns] = -total * weight
+            held_ref[c + 1, :, columns] = -total * weight
+    copy = pltpu.make_async_copy(held_ref, out_ref, sem)
+    copy.start()
+    copy.wait()
 
 
 def finish_kernel(rows, info_ref, diag_ref, framed_ref, *refs):
@@ -424,7 +427,7 @@
     diag_width = width // col_count
     part = diag_width // row_count
     half = width // 2
-    cuts = 1
+    cuts = 2
     unit = half // cuts
     chunk_count = members * cuts
     order = reversed_bits(levels)
@@ -485,6 +488,8 @@
         gathered = parent_factor[None]
         for bit in reversed(range(col_bits)):
             arrived = swap(gathered, "col", col_count, 1 << bit)
+            if 0 < bit < col_bits - 1:
+                yield WAIT
             dims = (2 * gathered.shape[0],) + parent_factor.shape
             (gathered,) = yield (stack_step, [gathered, arrived], [shape(*dims)])
         held["links"] = heavy(
@@ -575,6 +580,8 @@
                         [*held["turned", member], *first],
                         vmem=16,
                     )[0]
+                if not final:
+                    yield WAIT
             if bit + 1 < col_bits:
                 size //= 2
                 keep, send = yield (halve_step, [keep, arrived], [shape(size, half)] * 2)
@@ -613,12 +620,7 @@
         names = [("last", 0), "links"]
         while any(name not in held for name in names):
             yield WAIT
-        (mine,) = heavy(
-            functools.partial(step_kernel, [(halve_step, 2, 1)]),
-            [shape(group, half)],
-            [info, *held["last", 0]],
-            smem=1,
-        )
+        (mine,) = yield (halve_step, held["last", 0], [shape(group, half)])
         other = swap(mine, "col", col_count, 1)
         col, turned, *rest = heavy(
             functools.partial(parent_kernel, children, rows_here),
@@ -659,7 +661,10 @@
             functools.partial(column_kernel, children, rows_here),
             [shape(members, group // 2, width)],
             [info, listed, col, turned] + [value for name in names for value in held[name]],
-            smem=2,
+            smem=2, target=pltpu.HBM,
+            scratch=[
+                pltpu.VMEM((members, group // 2, width), F32), pltpu.SemaphoreType.DMA(())
+            ],
         )[0]
 
     flows = [ring_flow()] + [unit_flow(member) for member in range(children)]

time: 160 us -> 163 us (1.019)
  starting transfers between devices: 48.2 us -> 54.3 us
  waiting for transfers between devices: 64.4 us -> 60.7 us
    ppermute x10 -> x16, starting transfers between devices: 13 us -> 17.2 us  [ring_flow(): lax.ppermute(moving[way], AXES, rings[way])]
    ppermute x30, waiting for transfers between devices: 44.8 us -> 42.3 us  [swap(): lax.ppermute(value, axis, [(place, place ^ change) for place in range(siz...]
    ppermute x30, starting transfers between devices: 35.2 us -> 37.1 us  [swap(): lax.ppermute(value, axis, [(place, place ^ change) for place in range(siz...]
    ppermute x10 -> x16, waiting for transfers between devices: 19.6 us -> 18.4 us  [ring_flow(): lax.ppermute(moving[way], AXES, rings[way])]
    pallas_call x27 -> x29, Pallas kernels: 43.9 us -> 44.7 us  [call(): pl.pallas_call(inner, out_shape=outs, in_specs=[pl.BlockSpec(memory_space...]
  transfers between devices with their start and end apart: 40 -> 46, of which waited for: 23 -> 26; matrix products, arithmetic and copies ran while one was open for 0% -> 0% of each run, Pallas kernels for 24% -> 24%
where the time goes in v12:
time: 163 us
  waiting for transfers between devices  60.7 us (37%)
  starting transfers between devices  54.3 us (33%)
  Pallas kernels  44.7 us (27%)
  local copies, waits for them, and re-layouts  1.84 us (1%)
    pallas_call x29, Pallas kernels, call(): pl.pallas_call(inner, out_shape=outs, in_specs=[pl.BlockSpec(memory_space...  44.7 us
    ppermute x30, waiting for transfers between devices, swap(): lax.ppermute(value, axis, [(place, place ^ change) for place in range(siz...  42.3 us
    ppermute x30, starting transfers between devices, swap(): lax.ppermute(value, axis, [(place, place ^ change) for place in range(siz...  37.1 us
    ppermute x16, waiting for transfers between devices, ring_flow(): lax.ppermute(moving[way], AXES, rings[way])  18.4 us
    ppermute x16, starting transfers between devices, ring_flow(): lax.ppermute(moving[way], AXES, rings[way])  17.2 us
  transfers between devices with their start and end apart: 46, of which 26 were waited for; matrix products, arithmetic and copies ran while one was open for 0% of the time, Pallas kernels for 24%

profile of v12, /device:TPU:0, one launch (start us, length us, event | category | flops | bytes accessed | tf_op | source)
XLA Modules:
  0.0 162.5 jit_solution(16943786134255038903)
XLA Ops:
  1.9 1.8 %shard_map.76 = (f32[512,128]{1,0:T(8,128)S(1)}, f32[512,128]{1,0:T(8,128)S(1)}, f32[512,128]{1,0:T(8,128)S(1)}, f32[512,128]{1,0:T(8,128)S(1)}) custom-call(s32[2]{0:T(128)S(1)} %pad_add_fusion.info_ref.refs_0_, s32[3,8]{1,0:T(4,128)S(1)} %copy-done.5, f32[3,1024,512]{2,1,0:T(8,128)} %refs_2_.8), custom_call_target="tpu_custom_call" | custom-call | flops 1024 | bytes 1024 | tf_op jit(solution)/shard_map/pallas_call | solution.py:89
  3.8 2.6 %collective-permute-start = (f32[512,128]{1,0:T(8,128)S(1)}, f32[512,128]{1,0:T(8,128)S(1)}, u32[]{:S(2)}, u32[]{:S(2)}) collective-permute-start(f32[512,128]{1,0:T(8,128)S(1)} %get-tuple-element.91.refs_3_), channel_id=1, source_target_pairs={{0,8},{8,24},{24,16},{16,0},{1,9},{9,25},{25,17},{17,1},{10,2},{2,... | collective-permute-start | bytes 786440 | tf_op jit(solution)/shard_map/ppermute | solution.py:485
  6.4 3.0 %collective-permute-start.2 = (f32[1,2,64,512]{3,2,1,0:T(8,128)S(1)}, f32[1,2,64,512]{3,2,1,0:T(8,128)S(1)}, u32[]{:S(2)}, u32[]{:S(2)}) collective-permute-start(f32[1,2,64,512]{3,2,1,0:T(8,128)S(1)} %bitcast.3), channel_id=1, source_target_pairs={{0,4},{1,5},{2,6},{3,7},{4,0},{5,1},{6,2},{7,3},{8,12},{9,13},{10,... | collective-permute-start | bytes 786440 | tf_op jit(solution)/shard_map/ppermute | solution.py:65
  9.4 2.2 %shard_map.77 = (f32[512,128]{1,0:T(8,128)S(1)}, f32[512,128]{1,0:T(8,128)S(1)}, f32[512,128]{1,0:T(8,128)S(1)}, f32[512,128]{1,0:T(8,128)S(1)}, f32[512,128]{1,...) custom-call(s32[2]{0:T(128)S(1)} %pad_add_fusion.info_ref.refs_0_, ...), custom_call_target="tpu_custom_call" | custom-call | flops 1024 | bytes 1024 | tf_op jit(solution)/shard_map/pallas_call | solution.py:89
  11.7 0.8 shard_map.78.refs_3_.refs_4_.refs_2_.refs_1_
  12.5 2.2 %shard_map.79 = (bf16[3,256,512]{2,1,0:T(8,128)(2,1)S(1)}, bf16[3,256,512]{2,1,0:T(8,128)(2,1)S(1)}, bf16[3,512,256]{2,1,0:T(8,128)(2,1)S(1)}, bf16[3,512,256]{2,1,0:T(8,128)(2,1)S(1)}) custom-call(s32[2]{0:T(128)S(1)} %pad_add_fusion.info_ref.refs_0_, s32[3,8]{1,0:T(4,128)S(1)} %copy-done.6, f32[3,1024,512]{2,1,0:T(8,128)S(1)} %copy-done, ...), custom_call_target="tpu_custom_call" | custom-call | flops 1024 | bytes 1024 | tf_op jit(solution)/shard_map/pallas_call | solution.py:89
  14.7 6.7 %collective-permute-done.2.refs_6_ = f32[1,2,64,512]{3,2,1,0:T(8,128)S(1)} collective-permute-done((f32[1,2,64,512]{3,2,1,0:T(8,128)S(1)}, f32[1,2,64,512]{3,2,1,0:T(8,128)S(1)}, u32[]{:S(2)}, u32[]{:S(2)}) %collective-permute-start.2) | collective-permute-done | bytes 262176 | tf_op jit(solution)/shard_map/ppermute | solution.py:65
  22.1 1.6 collective-permute-start.3
  24.9 1.7 %shard_map.81 = (bf16[1024,1024]{1,0:T(8,128)(2,1)S(1)}, bf16[1024,1024]{1,0:T(8,128)(2,1)S(1)}) custom-call(s32[2]{0:T(128)S(1)} %pad_add_fusion.info_ref.refs_0_, f32[1024,512]{1,0:T(8,128)S(1)} %copy-done.3, f32[1024,512]{1,0:T(8,128)S(1)} %collective-permute-done.5.refs_2_, f32[512,128]{1,0:T(8,128)S(1)} %get-tuple-element.105.refs_3_.refs_11_), custom_call_target="tpu_custom_call" | custom-call | flops 1024 | bytes 1024 | tf_op jit(solution)/shard_map/pallas_call | solution.py:89
  26.6 3.2 %collective-permute-done.3.refs_3_.refs_5_.refs_12_ = f32[512,128]{1,0:T(8,128)S(1)} collective-permute-done((f32[512,128]{1,0:T(8,128)S(1)}, f32[512,128]{1,0:T(8,128)S(1)}, u32[]{:S(2)}, u32[]{:S(2)}) %collective-permute-start.3) | collective-permute-done | bytes 262176 | tf_op jit(solution)/shard_map/ppermute | solution.py:485
  29.8 1.0 collective-permute-done.4.refs_4_.refs_9_.refs_16_
  31.3 1.6 collective-permute-start.6
  33.4 2.2 %shard_map.83 = (bf16[512,1024]{1,0:T(8,128)(2,1)S(1)}, bf16[512,1024]{1,0:T(8,128)(2,1)S(1)}) custom-call(s32[2]{0:T(128)S(1)} %pad_add_fusion.info_ref.refs_0_, s32[3,8]{1,0:T(4,128)S(1)} %copy-done.6, f32[3,1024,512]{2,1,0:T(8,128)S(1)} %copy-done, bf16[512,512]{1,0:T(8,128)(2,1)S(1)} %shard_map.78.refs_3_.refs_4_.refs_2_.refs_1_, ...), custom_call_target="tpu_custom_call" | custom-call | flops 1024 | bytes 1024 | tf_op jit(solution)/shard_map/pallas_call | solution.py:89
  35.6 1.2 collective-permute-done.8.refs_6_
  36.8 0.9 collective-permute-done.6.refs_3_.refs_6_.refs_13_.refs_4_
  37.7 1.5 collective-permute-done.7.refs_4_.refs_10_.refs_17_.refs_8_
  40.6 1.5 collective-permute-start.9
  42.1 2.2 %shard_map.85 = (bf16[512,1024]{1,0:T(8,128)(2,1)S(1)}, bf16[512,1024]{1,0:T(8,128)(2,1)S(1)}) custom-call(s32[2]{0:T(128)S(1)} %pad_add_fusion.info_ref.refs_0_, s32[3,8]{1,0:T(4,128)S(1)} %copy-done.6, f32[3,1024,512]{2,1,0:T(8,128)S(1)} %copy-done, bf16[512,512]{1,0:T(8,128)(2,1)S(1)} %shard_map.78.refs_3_.refs_4_.refs_2_.refs_1_, ...), custom_call_target="tpu_custom_call" | custom-call | flops 1024 | bytes 1024 | tf_op jit(solution)/shard_map/pallas_call | solution.py:89
  44.3 4.4 %collective-permute-done.10.refs_4_.refs_18_.refs_9_.refs_16_ = f32[512,128]{1,0:T(8,128)S(1)} collective-permute-done((f32[512,128]{1,0:T(8,128)S(1)}, f32[512,128]{1,0:T(8,128)S(1)}, u32[]{:S(2)}, u32[]{:S(2)}) %collective-permute-start.10) | collective-permute-done | bytes 262176 | tf_op jit(solution)/shard_map/ppermute | solution.py:485
  49.7 1.6 collective-permute-start.13
  51.8 2.4 %shard_map.87 = (f32[512,256]{1,0:T(8,128)S(1)}, f32[512,256]{1,0:T(8,128)S(1)}) custom-call(s32[2]{0:T(128)S(1)} %pad_add_fusion.info_ref.refs_0_, bf16[1024,1024]{1,0:T(8,128)(2,1)S(1)} %get-tuple-element.107.refs_5_.refs_1_, bf16[1024,1024]{1,0:T(8,128)(2,1)S(1)} %get-tuple-element.117.refs_2_, f32[512,128]{1,0:T(8,128)S(1)} %get-tuple-element.91.refs_3_, ...), custom_call_target="tpu_custom_call" | custom-call | flops 1024 | bytes 1024 | tf_op jit(solution)/shard_map/pallas_call | solution.py:89
  54.2 2.1 %collective-permute-start.17 = (f32[512,256]{1,0:T(8,128)S(1)}, f32[512,256]{1,0:T(8,128)S(1)}, u32[]{:S(2)}, u32[]{:S(2)}) collective-permute-start(f32[512,256]{1,0:T(8,128)S(1)} %get-tuple-element.127), channel_id=1, source_target_pairs={{0,2},{1,3},{2,0},{3,1},{4,6},{5,7},{6,4},{7,5},{8,10},{9,11},{10,... | collective-permute-start | bytes 1572872 | tf_op jit(solution)/shard_map/ppermute | solution.py:65
  56.4 1.3 collective-permute-done.12.refs_3_
  57.8 4.5 %shard_map.88 = (bf16[2,512,512]{2,1,0:T(8,128)(2,1)S(1)}, bf16[2,512,512]{2,1,0:T(8,128)(2,1)S(1)}, bf16[2,512,256]{2,1,0:T(8,128)(2,1)S(1)}, bf16[2,512,256]{2...) custom-call(s32[2]{0:T(128)S(1)} %pad_add_fusion.info_ref.refs_0_, ...), custom_call_target="tpu_custom_call" | custom-call | flops 1024 | bytes 1024 | tf_op jit(solution)/shard_map/pallas_call | solution.py:89
  63.5 1.4 collective-permute-start.16
  65.0 2.3 %collective-permute-done.17.refs_4_ = f32[512,256]{1,0:T(8,128)S(1)} collective-permute-done((f32[512,256]{1,0:T(8,128)S(1)}, f32[512,256]{1,0:T(8,128)S(1)}, u32[]{:S(2)}, u32[]{:S(2)}) %collective-permute-start.17) | collective-permute-done | bytes 524320 | tf_op jit(solution)/shard_map/ppermute | solution.py:65
  67.3 4.1 %collective-permute-done.15.refs_1_.refs_14_.refs_5_.refs_12_ = f32[512,128]{1,0:T(8,128)S(1)} collective-permute-done((f32[512,128]{1,0:T(8,128)S(1)}, f32[512,128]{1,0:T(8,128)S(1)}, u32[]{:S(2)}, u32[]{:S(2)}) %collective-permute-start.15) | collective-permute-done | bytes 262176 | tf_op jit(solution)/shard_map/ppermute | solution.py:485
  72.3 1.6 collective-permute-start.18
  74.4 3.4 %collective-permute-start.20 = (f32[256,256]{1,0:T(8,128)S(1)}, f32[256,256]{1,0:T(8,128)S(1)}, u32[]{:S(2)}, u32[]{:S(2)}) collective-permute-start(f32[256,256]{1,0:T(8,128)S(1)} %get-tuple-element.131), channel_id=1, source_target_pairs={{0,4},{1,5},{2,6},{3,7},{4,0},{5,1},{6,2},{7,3},{8,12},{9,13},{10,... | collective-permute-start | bytes 786440 | tf_op jit(solution)/shard_map/ppermute | solution.py:65
  77.8 2.5 %shard_map.91 = (f32[512,256]{1,0:T(8,128)S(1)}, f32[512,256]{1,0:T(8,128)S(1)}) custom-call(s32[2]{0:T(128)S(1)} %pad_add_fusion.info_ref.refs_0_, bf16[1024,1024]{1,0:T(8,128)(2,1)S(1)} %get-tuple-element.107.refs_5_.refs_1_, bf16[1024,1024]{1,0:T(8,128)(2,1)S(1)} %get-tuple-element.117.refs_2_, f32[512,128]{1,0:T(8,128)S(1)} %get-tuple-element.108.refs_4_.refs_3_, ...), custom_call_target="tpu_custom_call" | custom-call | flops 1024 | bytes 1024 | tf_op jit(solution)/shard_map/pallas_call | solution.py:89
  80.2 1.0 collective-permute-start.22
  81.2 1.0 shard_map.92.refs_5_.refs_11_
  82.2 6.2 %collective-permute-done.20.refs_4_ = f32[256,256]{1,0:T(8,128)S(1)} collective-permute-done((f32[256,256]{1,0:T(8,128)S(1)}, f32[256,256]{1,0:T(8,128)S(1)}, u32[]{:S(2)}, u32[]{:S(2)}) %collective-permute-start.20) | collective-permute-done | bytes 262176 | tf_op jit(solution)/shard_map/ppermute | solution.py:65
  89.1 1.0 collective-permute-start.23
  90.1 1.1 collective-permute-start.24
  91.2 4.4 %shard_map.94 = (f32[128,512]{1,0:T(8,128)S(1)}, f32[2,128,512]{2,1,0:T(8,128)S(1)}, bf16[2,256,512]{2,1,0:T(8,128)(2,1)S(1)}, bf16[2,256,512]{2,1,0:T(8,128)(2,...) custom-call(s32[2]{0:T(128)S(1)} %pad_add_fusion.info_ref.refs_0_, ...), custom_call_target="tpu_custom_call" | custom-call | flops 1024 | bytes 1024 | tf_op jit(solution)/shard_map/pallas_call | solution.py:89
  95.6 2.2 %collective-permute-done.23.refs_14_ = f32[512,128]{1,0:T(8,128)S(1)} collective-permute-done((f32[512,128]{1,0:T(8,128)S(1)}, f32[512,128]{1,0:T(8,128)S(1)}, u32[]{:S(2)}, u32[]{:S(2)}) %collective-permute-start.23) | collective-permute-done | bytes 262176 | tf_op jit(solution)/shard_map/ppermute | solution.py:485
  98.5 2.4 %shard_map.95 = (f32[512,256]{1,0:T(8,128)S(1)}, f32[512,256]{1,0:T(8,128)S(1)}) custom-call(s32[2]{0:T(128)S(1)} %pad_add_fusion.info_ref.refs_0_, bf16[1024,1024]{1,0:T(8,128)(2,1)S(1)} %get-tuple-element.107.refs_5_.refs_1_, bf16[1024,1024]{1,0:T(8,128)(2,1)S(1)} %get-tuple-element.117.refs_2_, f32[512,128]{1,0:T(8,128)S(1)} %get-tuple-element.118.refs_19_.refs_3_, ...), custom_call_target="tpu_custom_call" | custom-call | flops 1024 | bytes 1024 | tf_op jit(solution)/shard_map/pallas_call | solution.py:89
  101.0 1.2 collective-permute-start.26
  102.2 0.8 collective-permute-start.27
  103.0 1.6 collective-permute-start.28
  105.2 3.2 %collective-permute-start.25 = (f32[256,256]{1,0:T(8,128)S(1)}, f32[256,256]{1,0:T(8,128)S(1)}, u32[]{:S(2)}, u32[]{:S(2)}) collective-permute-start(f32[256,256]{1,0:T(8,128)S(1)} %get-tuple-element.142), channel_id=1, source_target_pairs={{0,4},{1,5},{2,6},{3,7},{4,0},{5,1},{6,2},{7,3},{8,12},{9,13},{10,... | collective-permute-start | bytes 786440 | tf_op jit(solution)/shard_map/ppermute | solution.py:65
  108.4 1.0 shard_map.97.refs_12_.refs_13_
  109.4 2.6 %shard_map.98 = (f32[2,128,256]{2,1,0:T(8,128)S(1)}, f32[2,128,256]{2,1,0:T(8,128)S(1)}, f32[2,128,256]{2,1,0:T(8,128)S(1)}, f32[2,128,256]{2,1,0:T(8,128)S(1)}) custom-call(s32[2]{0:T(128)S(1)} %pad_add_fusion.info_ref.refs_0_, bf16[512,512]{1,0:T(8,128)(2,1)S(1)} %shard_map.78.refs_3_.refs_4_.refs_2_.refs_1_, ...), custom_call_target="tpu_custom_call" | custom-call | flops 1024 | bytes 1024 | tf_op jit(solution)/shard_map/pallas_call | solution.py:89
  112.0 5.6 %collective-permute-done.25.refs_2_ = f32[256,256]{1,0:T(8,128)S(1)} collective-permute-done((f32[256,256]{1,0:T(8,128)S(1)}, f32[256,256]{1,0:T(8,128)S(1)}, u32[]{:S(2)}, u32[]{:S(2)}) %collective-permute-start.25) | collective-permute-done | bytes 262176 | tf_op jit(solution)/shard_map/ppermute | solution.py:65
  117.6 0.9 collective-permute-start.33
  118.5 1.0 collective-permute-start.34
  119.5 2.0 %collective-permute-start.35 = (f32[2,128,256]{2,1,0:T(8,128)S(1)}, f32[2,128,256]{2,1,0:T(8,128)S(1)}, u32[]{:S(2)}, u32[]{:S(2)}) collective-permute-start(f32[2,128,256]{2,1,0:T(8,128)S(1)} %get-tuple-element.163), channel_id=1, source_target_pairs={{0,24},{8,16},{16,8},{24,0},{1,25},{9,17},{17,9},{25,1},{2,26},{10... | collective-permute-start | bytes 786440 | tf_op jit(solution)/shard_map/ppermute | solution.py:65
  122.3 4.4 %collective-permute-start.32 = (f32[256,256]{1,0:T(8,128)S(1)}, f32[256,256]{1,0:T(8,128)S(1)}, u32[]{:S(2)}, u32[]{:S(2)}) collective-permute-start(f32[256,256]{1,0:T(8,128)S(1)} %get-tuple-element.160), channel_id=1, source_target_pairs={{0,4},{1,5},{2,6},{3,7},{4,0},{5,1},{6,2},{7,3},{8,12},{9,13},{10,... | collective-permute-start | bytes 786440 | tf_op jit(solution)/shard_map/ppermute | solution.py:65
  127.4 4.3 %collective-permute-done.35.refs_8_ = f32[2,128,256]{2,1,0:T(8,128)S(1)} collective-permute-done((f32[2,128,256]{2,1,0:T(8,128)S(1)}, f32[2,128,256]{2,1,0:T(8,128)S(1)}, u32[]{:S(2)}, u32[]{:S(2)}) %collective-permute-start.35) | collective-permute-done | bytes 262176 | tf_op jit(solution)/shard_map/ppermute | solution.py:65
  131.6 2.2 %collective-permute-done.31.refs_2_ = f32[3,64,256]{2,1,0:T(8,128)S(1)} collective-permute-done((f32[3,64,256]{2,1,0:T(8,128)S(1)}, f32[3,64,256]{2,1,0:T(8,128)S(1)}, u32[]{:S(2)}, u32[]{:S(2)}) %collective-permute-start.31) | collective-permute-done | bytes 196640 | tf_op jit(solution)/shard_map/ppermute | solution.py:65
  133.8 1.4 collective-permute-done.32.refs_4_
  135.9 1.6 %collective-permute-start.37 = (f32[3,32,256]{2,1,0:T(8,128)S(1)}, f32[3,32,256]{2,1,0:T(8,128)S(1)}, u32[]{:S(2)}, u32[]{:S(2)}) collective-permute-start(f32[3,32,256]{2,1,0:T(8,128)S(1)} %get-tuple-element.167), channel_id=1, source_target_pairs={{0,4},{1,5},{2,6},{3,7},{4,0},{5,1},{6,2},{7,3},{8,12},{9,13},{10,... | collective-permute-start | bytes 294920 | tf_op jit(solution)/shard_map/ppermute | solution.py:65
  137.5 1.4 collective-permute-start.38
  139.3 2.6 %collective-permute-start.40 = (f32[2,32,256]{2,1,0:T(8,128)S(1)}, f32[2,32,256]{2,1,0:T(8,128)S(1)}, u32[]{:S(2)}, u32[]{:S(2)}) collective-permute-start(f32[2,32,256]{2,1,0:T(8,128)S(1)} %get-tuple-element.171), channel_id=1, source_target_pairs={{0,6},{1,7},{2,4},{3,5},{4,2},{5,3},{6,0},{7,1},{8,14},{9,15},{10,... | collective-permute-start | bytes 196616 | tf_op jit(solution)/shard_map/ppermute | solution.py:65
  141.9 4.7 %collective-permute-done.38.refs_4_ = f32[2,32,256]{2,1,0:T(8,128)S(1)} collective-permute-done((f32[2,32,256]{2,1,0:T(8,128)S(1)}, f32[2,32,256]{2,1,0:T(8,128)S(1)}, u32[]{:S(2)}, u32[]{:S(2)}) %collective-permute-start.38) | collective-permute-done | bytes 65568 | tf_op jit(solution)/shard_map/ppermute | solution.py:65
  147.8 0.9 collective-permute-done.42.refs_4_
  149.9 1.3 collective-permute-start.44
  151.1 1.6 collective-permute-start.45
  153.3 0.8 collective-permute-done.30.refs_5_
  154.3 1.5 shard_map.103.refs_7_
  156.3 3.6 %collective-permute-done.45.refs_6_ = f32[5,16,512]{2,1,0:T(8,128)S(1)} collective-permute-done((f32[5,16,512]{2,1,0:T(8,128)S(1)}, f32[5,16,512]{2,1,0:T(8,128)S(1)}, u32[]{:S(2)}, u32[]{:S(2)}) %collective-permute-start.45) | collective-permute-done | bytes 163872 | tf_op jit(solution)/shard_map/ppermute | solution.py:65
  159.9 1.1 copy-done.1
  161.0 1.6 shard_map.104
  (73 shorter events, 17.9 us)
Async XLA Ops:
  0.6 24.3 %collective-permute-start.5 = (f32[1024,512]{1,0:T(8,128)}, f32[1024,512]{1,0:T(8,128)S(1)}, u32[]{:S(2)}, u32[]{:S(2)}) collective-permute-start(f32[1024,512]{1,0:T(8,128)} %refs_1_.10), channel_id=1, source_target_pairs={{0,1},{1,0},{2,3},{3,2},{4,5},{5,4},{6,7},{7,6},{8,9},{9,8},{10,11... | collective-permute-start | bytes 6291464 | tf_op jit(solution)/shard_map/ppermute | solution.py:65
  1.2 0.7 copy-start.5
  1.9 4.5 %copy-start.4 = (f32[2,64,512]{2,1,0:T(8,128)S(1)}, f32[2,64,512]{2,1,0:T(8,128)}, u32[]{:S(2)}) copy-start(f32[2,64,512]{2,1,0:T(8,128)} %param.7) | copy-start | bytes 786436
  1.9 7.5 %copy-start.6 = (s32[3,8]{1,0:T(4,128)S(1)}, s32[3,8]{1,0:T(4,128)}, u32[]{:S(2)}) copy-start(s32[3,8]{1,0:T(4,128)} %refs_1_.14) | copy-start | bytes 292
  3.8 11.0 %collective-permute-start = (f32[512,128]{1,0:T(8,128)S(1)}, f32[512,128]{1,0:T(8,128)S(1)}, u32[]{:S(2)}, u32[]{:S(2)}) collective-permute-start(f32[512,128]{1,0:T(8,128)S(1)} %get-tuple-element.91.refs_3_), channel_id=1, source_target_pairs={{0,8},{8,24},{24,16},{16,0},{1,9},{9,25},{25,17},{17,1},{10,2},{2,... | collective-permute-start | bytes 786440 | tf_op jit(solution)/shard_map/ppermute | solution.py:485
  6.3 8.4 %collective-permute-start.1 = (f32[512,128]{1,0:T(8,128)S(1)}, f32[512,128]{1,0:T(8,128)S(1)}, u32[]{:S(2)}, u32[]{:S(2)}) collective-permute-start(f32[512,128]{1,0:T(8,128)S(1)} %get-tuple-element.104.refs_7_), channel_id=1, source_target_pairs={{8,0},{24,8},{16,24},{0,16},{9,1},{25,9},{17,25},{1,17},{2,10},{18... | collective-permute-start | bytes 786440 | tf_op jit(solution)/shard_map/ppermute | solution.py:485
  6.4 6.1 %copy-start = (f32[3,1024,512]{2,1,0:T(8,128)S(1)}, f32[3,1024,512]{2,1,0:T(8,128)}, u32[]{:S(2)}) copy-start(f32[3,1024,512]{2,1,0:T(8,128)} %refs_2_.8) | copy-start | bytes 18874372
  6.4 15.0 %collective-permute-start.2 = (f32[1,2,64,512]{3,2,1,0:T(8,128)S(1)}, f32[1,2,64,512]{3,2,1,0:T(8,128)S(1)}, u32[]{:S(2)}, u32[]{:S(2)}) collective-permute-start(f32[1,2,64,512]{3,2,1,0:T(8,128)S(1)} %bitcast.3), channel_id=1, source_target_pairs={{0,4},{1,5},{2,6},{3,7},{4,0},{5,1},{6,2},{7,3},{8,12},{9,13},{10,... | collective-permute-start | bytes 786440 | tf_op jit(solution)/shard_map/ppermute | solution.py:65
  14.7 10.2 %copy-start.3 = (f32[1024,512]{1,0:T(8,128)S(1)}, f32[1024,512]{1,0:T(8,128)}, u32[]{:S(2)}) copy-start(f32[1024,512]{1,0:T(8,128)} %refs_1_.10) | copy-start | bytes 6291460
  22.1 7.7 %collective-permute-start.3 = (f32[512,128]{1,0:T(8,128)S(1)}, f32[512,128]{1,0:T(8,128)S(1)}, u32[]{:S(2)}, u32[]{:S(2)}) collective-permute-start(f32[512,128]{1,0:T(8,128)S(1)} %get-tuple-element.105.refs_3_.refs_11_), channel_id=1, source_target_pairs={{0,8},{8,24},{24,16},{16,0},{1,9},{9,25},{25,17},{17,1},{10,2},{2,... | collective-permute-start | bytes 786440 | tf_op jit(solution)/shard_map/ppermute | solution.py:485
  23.7 7.0 %collective-permute-start.4 = (f32[512,128]{1,0:T(8,128)S(1)}, f32[512,128]{1,0:T(8,128)S(1)}, u32[]{:S(2)}, u32[]{:S(2)}) collective-permute-start(f32[512,128]{1,0:T(8,128)S(1)} %get-tuple-element.106.refs_15_), channel_id=1, source_target_pairs={{8,0},{24,8},{16,24},{0,16},{9,1},{25,9},{17,25},{1,17},{2,10},{18... | collective-permute-start | bytes 786440 | tf_op jit(solution)/shard_map/ppermute | solution.py:485
  24.2 12.7 %collective-permute-start.8 = (f32[2,2,64,512]{3,2,1,0:T(8,128)S(1)}, f32[2,2,64,512]{3,2,1,0:T(8,128)S(1)}, u32[]{:S(2)}, u32[]{:S(2)}) collective-permute-start(f32[2,2,64,512]{3,2,1,0:T(8,128)S(1)} %get-tuple-element.110.refs_5_), channel_id=1, source_target_pairs={{0,2},{1,3},{2,0},{3,1},{4,6},{5,7},{6,4},{7,5},{8,10},{9,11},{10,... | collective-permute-start | bytes 1572872 | tf_op jit(solution)/shard_map/ppermute | solution.py:65
  31.3 6.4 %collective-permute-start.6 = (f32[512,128]{1,0:T(8,128)S(1)}, f32[512,128]{1,0:T(8,128)S(1)}, u32[]{:S(2)}, u32[]{:S(2)}) collective-permute-start(f32[512,128]{1,0:T(8,128)S(1)} %get-tuple-element.108.refs_4_.refs_3_), channel_id=1, source_target_pairs={{0,8},{8,24},{24,16},{16,0},{1,9},{9,25},{25,17},{17,1},{10,2},{2,... | collective-permute-start | bytes 786440 | tf_op jit(solution)/shard_map/ppermute | solution.py:485
  32.9 6.4 %collective-permute-start.7 = (f32[512,128]{1,0:T(8,128)S(1)}, f32[512,128]{1,0:T(8,128)S(1)}, u32[]{:S(2)}, u32[]{:S(2)}) collective-permute-start(f32[512,128]{1,0:T(8,128)S(1)} %get-tuple-element.109.refs_7_), channel_id=1, source_target_pairs={{8,0},{24,8},{16,24},{0,16},{9,1},{25,9},{17,25},{1,17},{2,10},{18... | collective-permute-start | bytes 786440 | tf_op jit(solution)/shard_map/ppermute | solution.py:485
  39.9 9.0 %collective-permute-start.11 = (f32[4,2,64,512]{3,2,1,0:T(8,128)S(1)}, f32[4,2,64,512]{3,2,1,0:T(8,128)S(1)}, u32[]{:S(2)}, u32[]{:S(2)}) collective-permute-start(f32[4,2,64,512]{3,2,1,0:T(8,128)S(1)} %get-tuple-element.114.refs_5_), channel_id=1, source_target_pairs={{0,1},{1,0},{2,3},{3,2},{4,5},{5,4},{6,7},{7,6},{8,9},{9,8},{10,11... | collective-permute-start | bytes 3145736 | tf_op jit(solution)/shard_map/ppermute | solution.py:65
  40.0 8.7 %collective-permute-start.10 = (f32[512,128]{1,0:T(8,128)S(1)}, f32[512,128]{1,0:T(8,128)S(1)}, u32[]{:S(2)}, u32[]{:S(2)}) collective-permute-start(f32[512,128]{1,0:T(8,128)S(1)} %get-tuple-element.113.refs_15_), channel_id=1, source_target_pairs={{8,0},{24,8},{16,24},{0,16},{9,1},{25,9},{17,25},{1,17},{2,10},{18... | collective-permute-start | bytes 786440 | tf_op jit(solution)/shard_map/ppermute | solution.py:485
  40.6 8.4 %collective-permute-start.9 = (f32[512,128]{1,0:T(8,128)S(1)}, f32[512,128]{1,0:T(8,128)S(1)}, u32[]{:S(2)}, u32[]{:S(2)}) collective-permute-start(f32[512,128]{1,0:T(8,128)S(1)} %get-tuple-element.112.refs_4_.refs_11_), channel_id=1, source_target_pairs={{0,8},{8,24},{24,16},{16,0},{1,9},{9,25},{25,17},{17,1},{10,2},{2,... | collective-permute-start | bytes 786440 | tf_op jit(solution)/shard_map/ppermute | solution.py:485
  49.7 12.6 %collective-permute-start.13 = (f32[512,128]{1,0:T(8,128)S(1)}, f32[512,128]{1,0:T(8,128)S(1)}, u32[]{:S(2)}, u32[]{:S(2)}) collective-permute-start(f32[512,128]{1,0:T(8,128)S(1)} %get-tuple-element.118.refs_19_.refs_3_), channel_id=1, source_target_pairs={{0,8},{8,24},{24,16},{16,0},{1,9},{9,25},{25,17},{17,1},{10,2},{2,... | collective-permute-start | bytes 786440 | tf_op jit(solution)/shard_map/ppermute | solution.py:485
  51.3 11.0 %collective-permute-start.14 = (f32[512,128]{1,0:T(8,128)S(1)}, f32[512,128]{1,0:T(8,128)S(1)}, u32[]{:S(2)}, u32[]{:S(2)}) collective-permute-start(f32[512,128]{1,0:T(8,128)S(1)} %get-tuple-element.124.refs_7_), channel_id=1, source_target_pairs={{8,0},{24,8},{16,24},{0,16},{9,1},{25,9},{17,25},{1,17},{2,10},{18... | collective-permute-start | bytes 786440 | tf_op jit(solution)/shard_map/ppermute | solution.py:485
  51.8 4.6 %copy-start.2 = (f32[3,64,512]{2,1,0:T(8,128)S(1)}, f32[3,64,512]{2,1,0:T(8,128)}, u32[]{:S(2)}) copy-start(f32[3,64,512]{2,1,0:T(8,128)} %refs_1_.15) | copy-start | bytes 1179652
  54.2 13.1 %collective-permute-start.17 = (f32[512,256]{1,0:T(8,128)S(1)}, f32[512,256]{1,0:T(8,128)S(1)}, u32[]{:S(2)}, u32[]{:S(2)}) collective-permute-start(f32[512,256]{1,0:T(8,128)S(1)} %get-tuple-element.127), channel_id=1, source_target_pairs={{0,2},{1,3},{2,0},{3,1},{4,6},{5,7},{6,4},{7,5},{8,10},{9,11},{10,... | collective-permute-start | bytes 1572872 | tf_op jit(solution)/shard_map/ppermute | solution.py:65
  56.3 1.4 collective-permute-start.12
  62.9 8.4 %collective-permute-start.15 = (f32[512,128]{1,0:T(8,128)S(1)}, f32[512,128]{1,0:T(8,128)S(1)}, u32[]{:S(2)}, u32[]{:S(2)}) collective-permute-start(f32[512,128]{1,0:T(8,128)S(1)} %get-tuple-element.125.refs_5_.refs_11_), channel_id=1, source_target_pairs={{0,8},{8,24},{24,16},{16,0},{1,9},{9,25},{25,17},{17,1},{10,2},{2,... | collective-permute-start | bytes 786440 | tf_op jit(solution)/shard_map/ppermute | solution.py:485
  63.5 8.1 %collective-permute-start.16 = (f32[512,128]{1,0:T(8,128)S(1)}, f32[512,128]{1,0:T(8,128)S(1)}, u32[]{:S(2)}, u32[]{:S(2)}) collective-permute-start(f32[512,128]{1,0:T(8,128)S(1)} %get-tuple-element.126.refs_15_), channel_id=1, source_target_pairs={{8,0},{24,8},{16,24},{0,16},{9,1},{25,9},{17,25},{1,17},{2,10},{18... | collective-permute-start | bytes 786440 | tf_op jit(solution)/shard_map/ppermute | solution.py:485
  72.3 9.9 %collective-permute-start.18 = (f32[512,128]{1,0:T(8,128)S(1)}, f32[512,128]{1,0:T(8,128)S(1)}, u32[]{:S(2)}, u32[]{:S(2)}) collective-permute-start(f32[512,128]{1,0:T(8,128)S(1)} %get-tuple-element.128.refs_19_), channel_id=1, source_target_pairs={{0,8},{8,24},{24,16},{16,0},{1,9},{9,25},{25,17},{17,1},{10,2},{2,... | collective-permute-start | bytes 786440 | tf_op jit(solution)/shard_map/ppermute | solution.py:485
  73.9 8.4 %collective-permute-start.19 = (f32[512,128]{1,0:T(8,128)S(1)}, f32[512,128]{1,0:T(8,128)S(1)}, u32[]{:S(2)}, u32[]{:S(2)}) collective-permute-start(f32[512,128]{1,0:T(8,128)S(1)} %get-tuple-element.129), channel_id=1, source_target_pairs={{8,0},{24,8},{16,24},{0,16},{9,1},{25,9},{17,25},{1,17},{2,10},{18... | collective-permute-start | bytes 786440 | tf_op jit(solution)/shard_map/ppermute | solution.py:485
  74.4 14.1 %collective-permute-start.20 = (f32[256,256]{1,0:T(8,128)S(1)}, f32[256,256]{1,0:T(8,128)S(1)}, u32[]{:S(2)}, u32[]{:S(2)}) collective-permute-start(f32[256,256]{1,0:T(8,128)S(1)} %get-tuple-element.131), channel_id=1, source_target_pairs={{0,4},{1,5},{2,6},{3,7},{4,0},{5,1},{6,2},{7,3},{8,12},{9,13},{10,... | collective-permute-start | bytes 786440 | tf_op jit(solution)/shard_map/ppermute | solution.py:65
  80.2 24.3 %collective-permute-start.22 = (f32[512,256]{1,0:T(8,128)S(1)}, f32[512,256]{1,0:T(8,128)S(1)}, u32[]{:S(2)}, u32[]{:S(2)}) collective-permute-start(f32[512,256]{1,0:T(8,128)S(1)} %get-tuple-element.134.refs_3_), channel_id=1, source_target_pairs={{0,2},{1,3},{2,0},{3,1},{4,6},{5,7},{6,4},{7,5},{8,10},{9,11},{10,... | collective-permute-start | bytes 1572872 | tf_op jit(solution)/shard_map/ppermute | solution.py:65
  89.0 2.2 %collective-permute-start.21 = (f32[256,256]{1,0:T(8,128)S(1)}, f32[256,256]{1,0:T(8,128)S(1)}, u32[]{:S(2)}, u32[]{:S(2)}) collective-permute-start(f32[256,256]{1,0:T(8,128)S(1)} %get-tuple-element.135.refs_9_), channel_id=1, source_target_pairs={{0,1},{1,0},{2,3},{3,2},{4,5},{5,4},{6,7},{7,6},{8,9},{9,8},{10,11... | collective-permute-start | bytes 786440 | tf_op jit(solution)/shard_map/ppermute | solution.py:65
  89.1 8.7 %collective-permute-start.23 = (f32[512,128]{1,0:T(8,128)S(1)}, f32[512,128]{1,0:T(8,128)S(1)}, u32[]{:S(2)}, u32[]{:S(2)}) collective-permute-start(f32[512,128]{1,0:T(8,128)S(1)} %get-tuple-element.136.refs_11_), channel_id=1, source_target_pairs={{0,8},{8,24},{24,16},{16,0},{1,9},{9,25},{25,17},{17,1},{10,2},{2,... | collective-permute-start | bytes 786440 | tf_op jit(solution)/shard_map/ppermute | solution.py:485
  90.1 8.4 %collective-permute-start.24 = (f32[512,128]{1,0:T(8,128)S(1)}, f32[512,128]{1,0:T(8,128)S(1)}, u32[]{:S(2)}, u32[]{:S(2)}) collective-permute-start(f32[512,128]{1,0:T(8,128)S(1)} %get-tuple-element.139), channel_id=1, source_target_pairs={{8,0},{24,8},{16,24},{0,16},{9,1},{25,9},{17,25},{1,17},{2,10},{18... | collective-permute-start | bytes 786440 | tf_op jit(solution)/shard_map/ppermute | solution.py:485
  100.9 20.6 %collective-permute-start.29 = (f32[512,256]{1,0:T(8,128)S(1)}, f32[512,256]{1,0:T(8,128)S(1)}, u32[]{:S(2)}, u32[]{:S(2)}) collective-permute-start(f32[512,256]{1,0:T(8,128)S(1)} %get-tuple-element.147.refs_3_), channel_id=1, source_target_pairs={{0,2},{1,3},{2,0},{3,1},{4,6},{5,7},{6,4},{7,5},{8,10},{9,11},{10,... | collective-permute-start | bytes 1572872 | tf_op jit(solution)/shard_map/ppermute | solution.py:65
  101.0 17.5 %collective-permute-start.26 = (f32[3,128,256]{2,1,0:T(8,128)S(1)}, f32[3,128,256]{2,1,0:T(8,128)S(1)}, u32[]{:S(2)}, u32[]{:S(2)}) collective-permute-start(f32[3,128,256]{2,1,0:T(8,128)S(1)} %get-tuple-element.144), channel_id=1, source_target_pairs={{0,8},{8,0},{16,24},{24,16},{1,9},{9,1},{17,25},{25,17},{2,10},{10... | collective-permute-start | bytes 1179656 | tf_op jit(solution)/shard_map/ppermute | solution.py:65
  102.2 17.3 %collective-permute-start.27 = (f32[3,128,256]{2,1,0:T(8,128)S(1)}, f32[3,128,256]{2,1,0:T(8,128)S(1)}, u32[]{:S(2)}, u32[]{:S(2)}) collective-permute-start(f32[3,128,256]{2,1,0:T(8,128)S(1)} %get-tuple-element.145), channel_id=1, source_target_pairs={{0,16},{8,24},{16,0},{24,8},{1,17},{9,25},{17,1},{25,9},{2,18},{10... | collective-permute-start | bytes 1179656 | tf_op jit(solution)/shard_map/ppermute | solution.py:65
  103.0 18.6 %collective-permute-start.28 = (f32[3,128,256]{2,1,0:T(8,128)S(1)}, f32[3,128,256]{2,1,0:T(8,128)S(1)}, u32[]{:S(2)}, u32[]{:S(2)}) collective-permute-start(f32[3,128,256]{2,1,0:T(8,128)S(1)} %get-tuple-element.146), channel_id=1, source_target_pairs={{0,24},{8,16},{16,8},{24,0},{1,25},{9,17},{17,9},{25,1},{2,26},{10... | collective-permute-start | bytes 1179656 | tf_op jit(solution)/shard_map/ppermute | solution.py:65
  105.2 12.4 %collective-permute-start.25 = (f32[256,256]{1,0:T(8,128)S(1)}, f32[256,256]{1,0:T(8,128)S(1)}, u32[]{:S(2)}, u32[]{:S(2)}) collective-permute-start(f32[256,256]{1,0:T(8,128)S(1)} %get-tuple-element.142), channel_id=1, source_target_pairs={{0,4},{1,5},{2,6},{3,7},{4,0},{5,1},{6,2},{7,3},{8,12},{9,13},{10,... | collective-permute-start | bytes 786440 | tf_op jit(solution)/shard_map/ppermute | solution.py:65
  117.6 9.4 %collective-permute-start.33 = (f32[2,128,256]{2,1,0:T(8,128)S(1)}, f32[2,128,256]{2,1,0:T(8,128)S(1)}, u32[]{:S(2)}, u32[]{:S(2)}) collective-permute-start(f32[2,128,256]{2,1,0:T(8,128)S(1)} %get-tuple-element.161), channel_id=1, source_target_pairs={{0,8},{8,0},{16,24},{24,16},{1,9},{9,1},{17,25},{25,17},{2,10},{10... | collective-permute-start | bytes 786440 | tf_op jit(solution)/shard_map/ppermute | solution.py:65
  118.5 8.9 %collective-permute-start.34 = (f32[2,128,256]{2,1,0:T(8,128)S(1)}, f32[2,128,256]{2,1,0:T(8,128)S(1)}, u32[]{:S(2)}, u32[]{:S(2)}) collective-permute-start(f32[2,128,256]{2,1,0:T(8,128)S(1)} %get-tuple-element.162), channel_id=1, source_target_pairs={{0,16},{8,24},{16,0},{24,8},{1,17},{9,25},{17,1},{25,9},{2,18},{10... | collective-permute-start | bytes 786440 | tf_op jit(solution)/shard_map/ppermute | solution.py:65
  119.5 12.1 %collective-permute-start.35 = (f32[2,128,256]{2,1,0:T(8,128)S(1)}, f32[2,128,256]{2,1,0:T(8,128)S(1)}, u32[]{:S(2)}, u32[]{:S(2)}) collective-permute-start(f32[2,128,256]{2,1,0:T(8,128)S(1)} %get-tuple-element.163), channel_id=1, source_target_pairs={{0,24},{8,16},{16,8},{24,0},{1,25},{9,17},{17,9},{25,1},{2,26},{10... | collective-permute-start | bytes 786440 | tf_op jit(solution)/shard_map/ppermute | solution.py:65
  122.3 12.9 %collective-permute-start.32 = (f32[256,256]{1,0:T(8,128)S(1)}, f32[256,256]{1,0:T(8,128)S(1)}, u32[]{:S(2)}, u32[]{:S(2)}) collective-permute-start(f32[256,256]{1,0:T(8,128)S(1)} %get-tuple-element.160), channel_id=1, source_target_pairs={{0,4},{1,5},{2,6},{3,7},{4,0},{5,1},{6,2},{7,3},{8,12},{9,13},{10,... | collective-permute-start | bytes 786440 | tf_op jit(solution)/shard_map/ppermute | solution.py:65
  126.8 7.1 %collective-permute-start.31 = (f32[3,64,256]{2,1,0:T(8,128)S(1)}, f32[3,64,256]{2,1,0:T(8,128)S(1)}, u32[]{:S(2)}, u32[]{:S(2)}) collective-permute-start(f32[3,64,256]{2,1,0:T(8,128)S(1)} %get-tuple-element.158), channel_id=1, source_target_pairs={{0,2},{1,3},{2,0},{3,1},{4,6},{5,7},{6,4},{7,5},{8,10},{9,11},{10,... | collective-permute-start | bytes 589832 | tf_op jit(solution)/shard_map/ppermute | solution.py:65
  135.9 10.7 %collective-permute-start.37 = (f32[3,32,256]{2,1,0:T(8,128)S(1)}, f32[3,32,256]{2,1,0:T(8,128)S(1)}, u32[]{:S(2)}, u32[]{:S(2)}) collective-permute-start(f32[3,32,256]{2,1,0:T(8,128)S(1)} %get-tuple-element.167), channel_id=1, source_target_pairs={{0,4},{1,5},{2,6},{3,7},{4,0},{5,1},{6,2},{7,3},{8,12},{9,13},{10,... | collective-permute-start | bytes 294920 | tf_op jit(solution)/shard_map/ppermute | solution.py:65
  137.5 9.1 %collective-permute-start.38 = (f32[2,32,256]{2,1,0:T(8,128)S(1)}, f32[2,32,256]{2,1,0:T(8,128)S(1)}, u32[]{:S(2)}, u32[]{:S(2)}) collective-permute-start(f32[2,32,256]{2,1,0:T(8,128)S(1)} %get-tuple-element.169), channel_id=1, source_target_pairs={{0,4},{1,5},{2,6},{3,7},{4,0},{5,1},{6,2},{7,3},{8,12},{9,13},{10,... | collective-permute-start | bytes 196616 | tf_op jit(solution)/shard_map/ppermute | solution.py:65
  138.9 7.7 %collective-permute-start.39 = (f32[2,32,256]{2,1,0:T(8,128)S(1)}, f32[2,32,256]{2,1,0:T(8,128)S(1)}, u32[]{:S(2)}, u32[]{:S(2)}) collective-permute-start(f32[2,32,256]{2,1,0:T(8,128)S(1)} %get-tuple-element.170), channel_id=1, source_target_pairs={{0,2},{1,3},{2,0},{3,1},{4,6},{5,7},{6,4},{7,5},{8,10},{9,11},{10,... | collective-permute-start | bytes 196616 | tf_op jit(solution)/shard_map/ppermute | solution.py:65
  139.3 7.3 %collective-permute-start.40 = (f32[2,32,256]{2,1,0:T(8,128)S(1)}, f32[2,32,256]{2,1,0:T(8,128)S(1)}, u32[]{:S(2)}, u32[]{:S(2)}) collective-permute-start(f32[2,32,256]{2,1,0:T(8,128)S(1)} %get-tuple-element.171), channel_id=1, source_target_pairs={{0,6},{1,7},{2,4},{3,5},{4,2},{5,3},{6,0},{7,1},{8,14},{9,15},{10,... | collective-permute-start | bytes 196616 | tf_op jit(solution)/shard_map/ppermute | solution.py:65
  147.2 1.4 collective-permute-start.41
  147.3 1.4 collective-permute-start.42
  149.2 7.1 %collective-permute-start.43 = (f32[5,16,512]{2,1,0:T(8,128)S(1)}, f32[5,16,512]{2,1,0:T(8,128)S(1)}, u32[]{:S(2)}, u32[]{:S(2)}) collective-permute-start(f32[5,16,512]{2,1,0:T(8,128)S(1)} %shard_map.102.refs_8_.refs_3_), channel_id=1, source_target_pairs={{0,8},{8,0},{16,24},{24,16},{1,9},{9,1},{17,25},{25,17},{2,10},{10... | collective-permute-start | bytes 491528 | tf_op jit(solution)/shard_map/ppermute | solution.py:65
  149.9 6.4 %collective-permute-start.44 = (f32[5,16,512]{2,1,0:T(8,128)S(1)}, f32[5,16,512]{2,1,0:T(8,128)S(1)}, u32[]{:S(2)}, u32[]{:S(2)}) collective-permute-start(f32[5,16,512]{2,1,0:T(8,128)S(1)} %shard_map.102.refs_8_.refs_3_), channel_id=1, source_target_pairs={{0,16},{8,24},{16,0},{24,8},{1,17},{9,25},{17,1},{25,9},{2,18},{10... | collective-permute-start | bytes 491528 | tf_op jit(solution)/shard_map/ppermute | solution.py:65
  151.1 8.7 %collective-permute-start.45 = (f32[5,16,512]{2,1,0:T(8,128)S(1)}, f32[5,16,512]{2,1,0:T(8,128)S(1)}, u32[]{:S(2)}, u32[]{:S(2)}) collective-permute-start(f32[5,16,512]{2,1,0:T(8,128)S(1)} %shard_map.102.refs_8_.refs_3_), channel_id=1, source_target_pairs={{0,24},{8,16},{16,8},{24,0},{1,25},{9,17},{17,9},{25,1},{2,26},{10... | collective-permute-start | bytes 491528 | tf_op jit(solution)/shard_map/ppermute | solution.py:65
  152.7 1.3 collective-permute-start.30
  152.7 1.5 collective-permute-start.36
  159.9 1.1 copy-start.1

commit v13 on v12

--- a/solution.py
+++ b/solution.py
@@ -216,7 +216,7 @@
 
 
 def link_kernel(
-    children, share, info_ref, gathered_ref, diag_ref, other_ref, chooser_ref,
+    children, share, order, info_ref, gathered_ref, diag_ref, other_ref, chooser_ref,
     own_high_ref, own_low_ref, high_ref, low_ref, lift_high_ref, lift_low_ref, framed_ref,
     corner_ref, held_ref, rows_ref, frame_ref,
 ):
@@ -226,7 +226,7 @@
     chooser = chooser_ref[...]
     for g in range(groups):
         for c in range(children):
-            held_ref[c, block(info_ref[1] ^ g, size), :] = gathered_ref[g, c]
+            held_ref[c, block(info_ref[1] ^ order[g], size), :] = gathered_ref[g, c]
     rows_ref[block(core, size), :] = diag_ref[0]
     rows_ref[block(1 - core, size), :] = other_ref[0]
     diag = split(rows_ref[...])
@@ -444,6 +444,10 @@
         return pairs
 
     rings = (ring(True), ring(False))
+    link_bits = [*range(1, col_bits), 0]
+    link_order = [0]
+    for bit in link_bits:
+        link_order = [value ^ (side << bit) for value in link_order for side in range(2)]
     info = jnp.stack([lax.axis_index("row"), lax.axis_index("col")]).astype(jnp.int32)
 
     def cut(chosen, run):
@@ -486,14 +490,14 @@
 
     def link_flow():
         gathered = parent_factor[None]
-        for bit in reversed(range(col_bits)):
+        for bit in link_bits:
             arrived = swap(gathered, "col", col_count, 1 << bit)
-            if 0 < bit < col_bits - 1:
+            if bit > 1:
                 yield WAIT
             dims = (2 * gathered.shape[0],) + parent_factor.shape
             (gathered,) = yield (stack_step, [gathered, arrived], [shape(*dims)])
         held["links"] = heavy(
-            functools.partial(link_kernel, children, 1.0 / row_count),
+            functools.partial(link_kernel, children, 1.0 / row_count, link_order),
             [shape(children, width, width, dtype=BF16)] * 2
             + [shape(children, width, group, dtype=BF16)] * 2
             + [shape(children, diag_width, width), shape(children, width, half)],
@@ -620,7 +624,13 @@
         names = [("last", 0), "links"]
         while any(name not in held for name in names):
             yield WAIT
-        (mine,) = yield (halve_step, held["last", 0], [shape(group, half)])
+        yield WAIT
+        (mine,) = heavy(
+            functools.partial(step_kernel, [(halve_step, 2, 1)]),
+            [shape(group, half)],
+            [info, *held["last", 0]],
+            smem=1,
+        )
         other = swap(mine, "col", col_count, 1)
         col, turned, *rest = heavy(
             functools.partial(parent_kernel, children, rows_here),
@@ -653,8 +663,6 @@
     def column_flow():
         names = [("sum", 1 + c) for c in range(children)]
         while any(name not in held for name in names + ["parent"]):
-            yield WAIT
-        while "totals" not in held:
             yield WAIT
         col, turned, _ = held["parent"]
         held["columns"] = heavy(

time: 163 us -> 168 us (1.031)
  waiting for transfers between devices: 60.7 us -> 69.8 us
  starting transfers between devices: 54.3 us -> 49.6 us
    ppermute x30, waiting for transfers between devices: 42.3 us -> 54.1 us  [swap(): lax.ppermute(value, axis, [(place, place ^ change) for place in range(siz...]
    ppermute x30, starting transfers between devices: 37.1 us -> 32.4 us  [swap(): lax.ppermute(value, axis, [(place, place ^ change) for place in range(siz...]
    ppermute x16, waiting for transfers between devices: 18.4 us -> 15.6 us  [ring_flow(): lax.ppermute(moving[way], AXES, rings[way])]
    pallas_call x29 -> x30, Pallas kernels: 44.7 us -> 45.2 us  [call(): pl.pallas_call(inner, out_shape=outs, in_specs=[pl.BlockSpec(memory_space...]
  transfers between devices with their start and end apart: 46 -> 46, of which waited for: 26 -> 25; matrix products, arithmetic and copies ran while one was open for 0% -> 0% of each run, Pallas kernels for 24% -> 24%
where the time goes in v13:
time: 168 us; the launch traced here: 167 us
  waiting for transfers between devices  69.8 us (42%)
  starting transfers between devices  49.6 us (30%)
  Pallas kernels  45.2 us (27%)
  local copies, waits for them, and re-layouts  1.84 us (1%)
    ppermute x30, waiting for transfers between devices, swap(): lax.ppermute(value, axis, [(place, place ^ change) for place in range(siz...  54.1 us
    pallas_call x30, Pallas kernels, call(): pl.pallas_call(inner, out_shape=outs, in_specs=[pl.BlockSpec(memory_space...  45.2 us
    ppermute x30, starting transfers between devices, swap(): lax.ppermute(value, axis, [(place, place ^ change) for place in range(siz...  32.4 us
    ppermute x16, starting transfers between devices, ring_flow(): lax.ppermute(moving[way], AXES, rings[way])  17.2 us
    ppermute x16, waiting for transfers between devices, ring_flow(): lax.ppermute(moving[way], AXES, rings[way])  15.6 us
  transfers between devices with their start and end apart: 46, of which 25 were waited for; matrix products, arithmetic and copies ran while one was open for 0% of the time, Pallas kernels for 24%

profile of v13, /device:TPU:0, one launch (start us, length us, event | category | flops | bytes accessed | tf_op | source)
XLA Modules:
  0.0 167.5 jit_solution(764598013677201121)
XLA Ops:
  1.9 1.8 %shard_map.76 = (f32[512,128]{1,0:T(8,128)S(1)}, f32[512,128]{1,0:T(8,128)S(1)}, f32[512,128]{1,0:T(8,128)S(1)}, f32[512,128]{1,0:T(8,128)S(1)}) custom-call(s32[2]{0:T(128)S(1)} %pad_add_fusion.info_ref.refs_0_, s32[3,8]{1,0:T(4,128)S(1)} %copy-done.5, f32[3,1024,512]{2,1,0:T(8,128)} %refs_2_.8), custom_call_target="tpu_custom_call" | custom-call | flops 1024 | bytes 1024 | tf_op jit(solution)/shard_map/pallas_call | solution.py:89
  3.8 2.6 %collective-permute-start = (f32[512,128]{1,0:T(8,128)S(1)}, f32[512,128]{1,0:T(8,128)S(1)}, u32[]{:S(2)}, u32[]{:S(2)}) collective-permute-start(f32[512,128]{1,0:T(8,128)S(1)} %get-tuple-element.90.refs_3_), channel_id=1, source_target_pairs={{0,8},{8,24},{24,16},{16,0},{1,9},{9,25},{25,17},{17,1},{10,2},{2,... | collective-permute-start | bytes 786440 | tf_op jit(solution)/shard_map/ppermute | solution.py:489
  6.4 2.0 %collective-permute-start.2 = (f32[1,2,64,512]{3,2,1,0:T(8,128)S(1)}, f32[1,2,64,512]{3,2,1,0:T(8,128)S(1)}, u32[]{:S(2)}, u32[]{:S(2)}) collective-permute-start(f32[1,2,64,512]{3,2,1,0:T(8,128)S(1)} %bitcast.3), channel_id=1, source_target_pairs={{0,2},{1,3},{2,0},{3,1},{4,6},{5,7},{6,4},{7,5},{8,10},{9,11},{10,... | collective-permute-start | bytes 786440 | tf_op jit(solution)/shard_map/ppermute | solution.py:65
  8.4 2.2 %shard_map.77 = (f32[512,128]{1,0:T(8,128)S(1)}, f32[512,128]{1,0:T(8,128)S(1)}, f32[512,128]{1,0:T(8,128)S(1)}, f32[512,128]{1,0:T(8,128)S(1)}, f32[512,128]{1,...) custom-call(s32[2]{0:T(128)S(1)} %pad_add_fusion.info_ref.refs_0_, ...), custom_call_target="tpu_custom_call" | custom-call | flops 1024 | bytes 1024 | tf_op jit(solution)/shard_map/pallas_call | solution.py:89
  10.7 0.8 shard_map.78.refs_3_.refs_4_.refs_2_.refs_1_
  11.5 2.2 %shard_map.79 = (bf16[3,256,512]{2,1,0:T(8,128)(2,1)S(1)}, bf16[3,256,512]{2,1,0:T(8,128)(2,1)S(1)}, bf16[3,512,256]{2,1,0:T(8,128)(2,1)S(1)}, bf16[3,512,256]{2,1,0:T(8,128)(2,1)S(1)}) custom-call(s32[2]{0:T(128)S(1)} %pad_add_fusion.info_ref.refs_0_, s32[3,8]{1,0:T(4,128)S(1)} %copy-done.6, f32[3,1024,512]{2,1,0:T(8,128)S(1)} %copy-done, ...), custom_call_target="tpu_custom_call" | custom-call | flops 1024 | bytes 1024 | tf_op jit(solution)/shard_map/pallas_call | solution.py:89
  13.7 1.0 collective-permute-done.1.refs_4_.refs_8_
  15.5 1.7 %collective-permute-start.3 = (f32[512,128]{1,0:T(8,128)S(1)}, f32[512,128]{1,0:T(8,128)S(1)}, u32[]{:S(2)}, u32[]{:S(2)}) collective-permute-start(f32[512,128]{1,0:T(8,128)S(1)} %get-tuple-element.104.refs_3_.refs_11_), channel_id=1, source_target_pairs={{0,8},{8,24},{24,16},{16,0},{1,9},{9,25},{25,17},{17,1},{10,2},{2,... | collective-permute-start | bytes 786440 | tf_op jit(solution)/shard_map/ppermute | solution.py:489
  17.6 2.8 %collective-permute-start.8 = (f32[2,2,64,512]{3,2,1,0:T(8,128)S(1)}, f32[2,2,64,512]{3,2,1,0:T(8,128)S(1)}, u32[]{:S(2)}, u32[]{:S(2)}) collective-permute-start(f32[2,2,64,512]{3,2,1,0:T(8,128)S(1)} %get-tuple-element.109.refs_5_), channel_id=1, source_target_pairs={{0,4},{1,5},{2,6},{3,7},{4,0},{5,1},{6,2},{7,3},{8,12},{9,13},{10,... | collective-permute-start | bytes 1572872 | tf_op jit(solution)/shard_map/ppermute | solution.py:65
  20.3 1.7 shard_map.81
  22.0 1.1 collective-permute-done.3.refs_3_.refs_5_.refs_12_
  23.1 1.1 collective-permute-done.4.refs_4_.refs_9_.refs_16_
  24.9 1.5 collective-permute-start.6
  27.0 2.2 %shard_map.83 = (bf16[512,1024]{1,0:T(8,128)(2,1)S(1)}, bf16[512,1024]{1,0:T(8,128)(2,1)S(1)}) custom-call(s32[2]{0:T(128)S(1)} %pad_add_fusion.info_ref.refs_0_, s32[3,8]{1,0:T(4,128)S(1)} %copy-done.6, f32[3,1024,512]{2,1,0:T(8,128)S(1)} %copy-done, bf16[512,512]{1,0:T(8,128)(2,1)S(1)} %shard_map.78.refs_3_.refs_4_.refs_2_.refs_1_, ...), custom_call_target="tpu_custom_call" | custom-call | flops 1024 | bytes 1024 | tf_op jit(solution)/shard_map/pallas_call | solution.py:89
  29.2 13.2 %collective-permute-done.8.refs_6_ = f32[2,2,64,512]{3,2,1,0:T(8,128)S(1)} collective-permute-done((f32[2,2,64,512]{3,2,1,0:T(8,128)S(1)}, f32[2,2,64,512]{3,2,1,0:T(8,128)S(1)}, u32[]{:S(2)}, u32[]{:S(2)}) %collective-permute-start.8) | collective-permute-done | bytes 524320 | tf_op jit(solution)/shard_map/ppermute | solution.py:65
  43.1 1.4 collective-permute-start.10
  45.2 2.2 %shard_map.85 = (bf16[512,1024]{1,0:T(8,128)(2,1)S(1)}, bf16[512,1024]{1,0:T(8,128)(2,1)S(1)}) custom-call(s32[2]{0:T(128)S(1)} %pad_add_fusion.info_ref.refs_0_, s32[3,8]{1,0:T(4,128)S(1)} %copy-done.6, f32[3,1024,512]{2,1,0:T(8,128)S(1)} %copy-done, bf16[512,512]{1,0:T(8,128)(2,1)S(1)} %shard_map.78.refs_3_.refs_4_.refs_2_.refs_1_, ...), custom_call_target="tpu_custom_call" | custom-call | flops 1024 | bytes 1024 | tf_op jit(solution)/shard_map/pallas_call | solution.py:89
  47.4 4.4 %collective-permute-done.10.refs_4_.refs_18_.refs_9_.refs_16_ = f32[512,128]{1,0:T(8,128)S(1)} collective-permute-done((f32[512,128]{1,0:T(8,128)S(1)}, f32[512,128]{1,0:T(8,128)S(1)}, u32[]{:S(2)}, u32[]{:S(2)}) %collective-permute-start.10) | collective-permute-done | bytes 262176 | tf_op jit(solution)/shard_map/ppermute | solution.py:489
  51.8 1.1 collective-permute-done.9.refs_3_.refs_14_.refs_5_.refs_12_
  54.4 1.4 collective-permute-start.14
  55.7 2.4 %shard_map.87 = (f32[512,256]{1,0:T(8,128)S(1)}, f32[512,256]{1,0:T(8,128)S(1)}) custom-call(s32[2]{0:T(128)S(1)} %pad_add_fusion.info_ref.refs_0_, bf16[1024,1024]{1,0:T(8,128)(2,1)S(1)} %get-tuple-element.106.refs_5_.refs_1_, bf16[1024,1024]{1,0:T(8,128)(2,1)S(1)} %get-tuple-element.116.refs_2_, f32[512,128]{1,0:T(8,128)S(1)} %get-tuple-element.90.refs_3_, ...), custom_call_target="tpu_custom_call" | custom-call | flops 1024 | bytes 1024 | tf_op jit(solution)/shard_map/pallas_call | solution.py:89
  59.0 1.3 collective-permute-done.12.refs_3_
  60.3 4.5 %shard_map.88 = (bf16[2,512,512]{2,1,0:T(8,128)(2,1)S(1)}, bf16[2,512,512]{2,1,0:T(8,128)(2,1)S(1)}, bf16[2,512,256]{2,1,0:T(8,128)(2,1)S(1)}, bf16[2,512,256]{2...) custom-call(s32[2]{0:T(128)S(1)} %pad_add_fusion.info_ref.refs_0_, ...), custom_call_target="tpu_custom_call" | custom-call | flops 1024 | bytes 1024 | tf_op jit(solution)/shard_map/pallas_call | solution.py:89
  65.5 1.6 collective-permute-start.15
  67.6 3.3 %collective-permute-done.17.refs_4_ = f32[512,256]{1,0:T(8,128)S(1)} collective-permute-done((f32[512,256]{1,0:T(8,128)S(1)}, f32[512,256]{1,0:T(8,128)S(1)}, u32[]{:S(2)}, u32[]{:S(2)}) %collective-permute-start.17) | collective-permute-done | bytes 524320 | tf_op jit(solution)/shard_map/ppermute | solution.py:65
  70.9 3.0 %collective-permute-done.15.refs_1_.refs_14_.refs_5_.refs_12_ = f32[512,128]{1,0:T(8,128)S(1)} collective-permute-done((f32[512,128]{1,0:T(8,128)S(1)}, f32[512,128]{1,0:T(8,128)S(1)}, u32[]{:S(2)}, u32[]{:S(2)}) %collective-permute-start.15) | collective-permute-done | bytes 262176 | tf_op jit(solution)/shard_map/ppermute | solution.py:489
  73.9 1.2 collective-permute-done.16.refs_2_.refs_18_.refs_9_.refs_16_
  76.4 1.4 collective-permute-start.20
  77.9 3.4 %collective-permute-start.18 = (f32[256,256]{1,0:T(8,128)S(1)}, f32[256,256]{1,0:T(8,128)S(1)}, u32[]{:S(2)}, u32[]{:S(2)}) collective-permute-start(f32[256,256]{1,0:T(8,128)S(1)} %get-tuple-element.128), channel_id=1, source_target_pairs={{0,4},{1,5},{2,6},{3,7},{4,0},{5,1},{6,2},{7,3},{8,12},{9,13},{10,... | collective-permute-start | bytes 786440 | tf_op jit(solution)/shard_map/ppermute | solution.py:65
  81.2 2.4 %shard_map.91 = (f32[512,256]{1,0:T(8,128)S(1)}, f32[512,256]{1,0:T(8,128)S(1)}) custom-call(s32[2]{0:T(128)S(1)} %pad_add_fusion.info_ref.refs_0_, bf16[1024,1024]{1,0:T(8,128)(2,1)S(1)} %get-tuple-element.106.refs_5_.refs_1_, bf16[1024,1024]{1,0:T(8,128)(2,1)S(1)} %get-tuple-element.116.refs_2_, f32[512,128]{1,0:T(8,128)S(1)} %get-tuple-element.107.refs_4_.refs_3_, ...), custom_call_target="tpu_custom_call" | custom-call | flops 1024 | bytes 1024 | tf_op jit(solution)/shard_map/pallas_call | solution.py:89
  83.8 1.0 shard_map.92.refs_3_.refs_11_
  85.4 6.5 %collective-permute-done.18.refs_2_ = f32[256,256]{1,0:T(8,128)S(1)} collective-permute-done((f32[256,256]{1,0:T(8,128)S(1)}, f32[256,256]{1,0:T(8,128)S(1)}, u32[]{:S(2)}, u32[]{:S(2)}) %collective-permute-start.18) | collective-permute-done | bytes 262176 | tf_op jit(solution)/shard_map/ppermute | solution.py:65
  93.2 1.4 collective-permute-start.24
  94.6 4.4 %shard_map.95 = (f32[128,512]{1,0:T(8,128)S(1)}, f32[2,128,512]{2,1,0:T(8,128)S(1)}, bf16[2,256,512]{2,1,0:T(8,128)(2,1)S(1)}, bf16[2,256,512]{2,1,0:T(8,128)(2,...) custom-call(s32[2]{0:T(128)S(1)} %pad_add_fusion.info_ref.refs_0_, ...), custom_call_target="tpu_custom_call" | custom-call | flops 1024 | bytes 1024 | tf_op jit(solution)/shard_map/pallas_call | solution.py:89
  99.0 2.2 %collective-permute-done.23.refs_14_ = f32[512,128]{1,0:T(8,128)S(1)} collective-permute-done((f32[512,128]{1,0:T(8,128)S(1)}, f32[512,128]{1,0:T(8,128)S(1)}, u32[]{:S(2)}, u32[]{:S(2)}) %collective-permute-start.23) | collective-permute-done | bytes 262176 | tf_op jit(solution)/shard_map/ppermute | solution.py:489
  101.6 2.4 %shard_map.96 = (f32[512,256]{1,0:T(8,128)S(1)}, f32[512,256]{1,0:T(8,128)S(1)}) custom-call(s32[2]{0:T(128)S(1)} %pad_add_fusion.info_ref.refs_0_, bf16[1024,1024]{1,0:T(8,128)(2,1)S(1)} %get-tuple-element.106.refs_5_.refs_1_, bf16[1024,1024]{1,0:T(8,128)(2,1)S(1)} %get-tuple-element.116.refs_2_, f32[512,128]{1,0:T(8,128)S(1)} %get-tuple-element.117.refs_19_.refs_3_, ...), custom_call_target="tpu_custom_call" | custom-call | flops 1024 | bytes 1024 | tf_op jit(solution)/shard_map/pallas_call | solution.py:89
  104.7 1.5 collective-permute-start.27
  106.2 1.5 collective-permute-start.28
  108.2 2.6 %collective-permute-start.25 = (f32[256,256]{1,0:T(8,128)S(1)}, f32[256,256]{1,0:T(8,128)S(1)}, u32[]{:S(2)}, u32[]{:S(2)}) collective-permute-start(f32[256,256]{1,0:T(8,128)S(1)} %get-tuple-element.140), channel_id=1, source_target_pairs={{0,4},{1,5},{2,6},{3,7},{4,0},{5,1},{6,2},{7,3},{8,12},{9,13},{10,... | collective-permute-start | bytes 786440 | tf_op jit(solution)/shard_map/ppermute | solution.py:65
  110.8 1.0 shard_map.98.refs_12_.refs_13_
  111.8 2.6 %shard_map.99 = (f32[2,128,256]{2,1,0:T(8,128)S(1)}, f32[2,128,256]{2,1,0:T(8,128)S(1)}, f32[2,128,256]{2,1,0:T(8,128)S(1)}, f32[2,128,256]{2,1,0:T(8,128)S(1)}) custom-call(s32[2]{0:T(128)S(1)} %pad_add_fusion.info_ref.refs_0_, bf16[512,512]{1,0:T(8,128)(2,1)S(1)} %shard_map.78.refs_3_.refs_4_.refs_2_.refs_1_, ...), custom_call_target="tpu_custom_call" | custom-call | flops 1024 | bytes 1024 | tf_op jit(solution)/shard_map/pallas_call | solution.py:89
  114.4 6.3 %collective-permute-done.25.refs_2_ = f32[256,256]{1,0:T(8,128)S(1)} collective-permute-done((f32[256,256]{1,0:T(8,128)S(1)}, f32[256,256]{1,0:T(8,128)S(1)}, u32[]{:S(2)}, u32[]{:S(2)}) %collective-permute-start.25) | collective-permute-done | bytes 262176 | tf_op jit(solution)/shard_map/ppermute | solution.py:65
  121.3 1.4 collective-permute-start.34
  122.7 3.4 %collective-permute-start.35 = (f32[2,128,256]{2,1,0:T(8,128)S(1)}, f32[2,128,256]{2,1,0:T(8,128)S(1)}, u32[]{:S(2)}, u32[]{:S(2)}) collective-permute-start(f32[2,128,256]{2,1,0:T(8,128)S(1)} %get-tuple-element.161), channel_id=1, source_target_pairs={{0,24},{8,16},{16,8},{24,0},{1,25},{9,17},{17,9},{25,1},{2,26},{10... | collective-permute-start | bytes 786440 | tf_op jit(solution)/shard_map/ppermute | solution.py:65
  126.8 1.6 collective-permute-start.32
  128.3 1.6 collective-permute-done.33.refs_6_
  129.9 0.9 collective-permute-done.34.refs_7_
  130.8 4.3 %collective-permute-done.35.refs_8_ = f32[2,128,256]{2,1,0:T(8,128)S(1)} collective-permute-done((f32[2,128,256]{2,1,0:T(8,128)S(1)}, f32[2,128,256]{2,1,0:T(8,128)S(1)}, u32[]{:S(2)}, u32[]{:S(2)}) %collective-permute-start.35) | collective-permute-done | bytes 262176 | tf_op jit(solution)/shard_map/ppermute | solution.py:65
  135.0 1.1 collective-permute-done.31.refs_2_
  136.2 2.1 %collective-permute-done.32.refs_4_ = f32[256,256]{1,0:T(8,128)S(1)} collective-permute-done((f32[256,256]{1,0:T(8,128)S(1)}, f32[256,256]{1,0:T(8,128)S(1)}, u32[]{:S(2)}, u32[]{:S(2)}) %collective-permute-start.32) | collective-permute-done | bytes 262176 | tf_op jit(solution)/shard_map/ppermute | solution.py:65
  139.0 1.0 collective-permute-start.37
  140.1 2.0 %collective-permute-start.38 = (f32[2,32,256]{2,1,0:T(8,128)S(1)}, f32[2,32,256]{2,1,0:T(8,128)S(1)}, u32[]{:S(2)}, u32[]{:S(2)}) collective-permute-start(f32[2,32,256]{2,1,0:T(8,128)S(1)} %get-tuple-element.168), channel_id=1, source_target_pairs={{0,4},{1,5},{2,6},{3,7},{4,0},{5,1},{6,2},{7,3},{8,12},{9,13},{10,... | collective-permute-start | bytes 196616 | tf_op jit(solution)/shard_map/ppermute | solution.py:65
  142.4 2.0 %collective-permute-start.40 = (f32[2,32,256]{2,1,0:T(8,128)S(1)}, f32[2,32,256]{2,1,0:T(8,128)S(1)}, u32[]{:S(2)}, u32[]{:S(2)}) collective-permute-start(f32[2,32,256]{2,1,0:T(8,128)S(1)} %get-tuple-element.170), channel_id=1, source_target_pairs={{0,6},{1,7},{2,4},{3,5},{4,2},{5,3},{6,0},{7,1},{8,14},{9,15},{10,... | collective-permute-start | bytes 196616 | tf_op jit(solution)/shard_map/ppermute | solution.py:65
  144.5 1.6 shard_map.102.refs_7_
  146.0 5.3 %collective-permute-done.38.refs_4_ = f32[2,32,256]{2,1,0:T(8,128)S(1)} collective-permute-done((f32[2,32,256]{2,1,0:T(8,128)S(1)}, f32[2,32,256]{2,1,0:T(8,128)S(1)}, u32[]{:S(2)}, u32[]{:S(2)}) %collective-permute-start.38) | collective-permute-done | bytes 65568 | tf_op jit(solution)/shard_map/ppermute | solution.py:65
  151.3 1.1 copy-done.1
  153.6 0.9 collective-permute-done.42.refs_4_
  155.0 1.2 collective-permute-start.43
  156.2 1.0 collective-permute-start.44
  157.2 1.4 collective-permute-start.45
  158.6 3.5 %collective-permute-done.43.refs_4_ = f32[5,16,512]{2,1,0:T(8,128)S(1)} collective-permute-done((f32[5,16,512]{2,1,0:T(8,128)S(1)}, f32[5,16,512]{2,1,0:T(8,128)S(1)}, u32[]{:S(2)}, u32[]{:S(2)}) %collective-permute-start.43) | collective-permute-done | bytes 163872 | tf_op jit(solution)/shard_map/ppermute | solution.py:65
  162.1 2.3 %collective-permute-done.44.refs_5_ = f32[5,16,512]{2,1,0:T(8,128)S(1)} collective-permute-done((f32[5,16,512]{2,1,0:T(8,128)S(1)}, f32[5,16,512]{2,1,0:T(8,128)S(1)}, u32[]{:S(2)}, u32[]{:S(2)}) %collective-permute-start.44) | collective-permute-done | bytes 163872 | tf_op jit(solution)/shard_map/ppermute | solution.py:65
  164.4 1.5 collective-permute-done.45.refs_6_
  165.9 1.6 shard_map.105
  (74 shorter events, 17.4 us)
Async XLA Ops:
  0.6 19.7 %collective-permute-start.5 = (f32[1024,512]{1,0:T(8,128)}, f32[1024,512]{1,0:T(8,128)S(1)}, u32[]{:S(2)}, u32[]{:S(2)}) collective-permute-start(f32[1024,512]{1,0:T(8,128)} %refs_1_.10), channel_id=1, source_target_pairs={{0,1},{1,0},{2,3},{3,2},{4,5},{5,4},{6,7},{7,6},{8,9},{9,8},{10,11... | collective-permute-start | bytes 6291464 | tf_op jit(solution)/shard_map/ppermute | solution.py:65
  1.2 0.7 copy-start.5
  1.9 4.5 %copy-start.4 = (f32[2,64,512]{2,1,0:T(8,128)S(1)}, f32[2,64,512]{2,1,0:T(8,128)}, u32[]{:S(2)}) copy-start(f32[2,64,512]{2,1,0:T(8,128)} %param.7) | copy-start | bytes 786436
  1.9 6.5 %copy-start.6 = (s32[3,8]{1,0:T(4,128)S(1)}, s32[3,8]{1,0:T(4,128)}, u32[]{:S(2)}) copy-start(s32[3,8]{1,0:T(4,128)} %refs_1_.14) | copy-start | bytes 292
  3.8 10.0 %collective-permute-start = (f32[512,128]{1,0:T(8,128)S(1)}, f32[512,128]{1,0:T(8,128)S(1)}, u32[]{:S(2)}, u32[]{:S(2)}) collective-permute-start(f32[512,128]{1,0:T(8,128)S(1)} %get-tuple-element.90.refs_3_), channel_id=1, source_target_pairs={{0,8},{8,24},{24,16},{16,0},{1,9},{9,25},{25,17},{17,1},{10,2},{2,... | collective-permute-start | bytes 786440 | tf_op jit(solution)/shard_map/ppermute | solution.py:489
  6.3 8.4 %collective-permute-start.1 = (f32[512,128]{1,0:T(8,128)S(1)}, f32[512,128]{1,0:T(8,128)S(1)}, u32[]{:S(2)}, u32[]{:S(2)}) collective-permute-start(f32[512,128]{1,0:T(8,128)S(1)} %get-tuple-element.103.refs_7_), channel_id=1, source_target_pairs={{8,0},{24,8},{16,24},{0,16},{9,1},{25,9},{17,25},{1,17},{2,10},{18... | collective-permute-start | bytes 786440 | tf_op jit(solution)/shard_map/ppermute | solution.py:489
  6.4 5.1 %copy-start = (f32[3,1024,512]{2,1,0:T(8,128)S(1)}, f32[3,1024,512]{2,1,0:T(8,128)}, u32[]{:S(2)}) copy-start(f32[3,1024,512]{2,1,0:T(8,128)} %refs_2_.8) | copy-start | bytes 18874372
  6.4 8.4 %collective-permute-start.2 = (f32[1,2,64,512]{3,2,1,0:T(8,128)S(1)}, f32[1,2,64,512]{3,2,1,0:T(8,128)S(1)}, u32[]{:S(2)}, u32[]{:S(2)}) collective-permute-start(f32[1,2,64,512]{3,2,1,0:T(8,128)S(1)} %bitcast.3), channel_id=1, source_target_pairs={{0,2},{1,3},{2,0},{3,1},{4,6},{5,7},{6,4},{7,5},{8,10},{9,11},{10,... | collective-permute-start | bytes 786440 | tf_op jit(solution)/shard_map/ppermute | solution.py:65
  13.7 6.6 %copy-start.3 = (f32[1024,512]{1,0:T(8,128)S(1)}, f32[1024,512]{1,0:T(8,128)}, u32[]{:S(2)}) copy-start(f32[1024,512]{1,0:T(8,128)} %refs_1_.10) | copy-start | bytes 6291460
  15.5 7.7 %collective-permute-start.3 = (f32[512,128]{1,0:T(8,128)S(1)}, f32[512,128]{1,0:T(8,128)S(1)}, u32[]{:S(2)}, u32[]{:S(2)}) collective-permute-start(f32[512,128]{1,0:T(8,128)S(1)} %get-tuple-element.104.refs_3_.refs_11_), channel_id=1, source_target_pairs={{0,8},{8,24},{24,16},{16,0},{1,9},{9,25},{25,17},{17,1},{10,2},{2,... | collective-permute-start | bytes 786440 | tf_op jit(solution)/shard_map/ppermute | solution.py:489
  17.2 7.1 %collective-permute-start.4 = (f32[512,128]{1,0:T(8,128)S(1)}, f32[512,128]{1,0:T(8,128)S(1)}, u32[]{:S(2)}, u32[]{:S(2)}) collective-permute-start(f32[512,128]{1,0:T(8,128)S(1)} %get-tuple-element.105.refs_15_), channel_id=1, source_target_pairs={{8,0},{24,8},{16,24},{0,16},{9,1},{25,9},{17,25},{1,17},{2,10},{18... | collective-permute-start | bytes 786440 | tf_op jit(solution)/shard_map/ppermute | solution.py:489
  17.6 24.8 %collective-permute-start.8 = (f32[2,2,64,512]{3,2,1,0:T(8,128)S(1)}, f32[2,2,64,512]{3,2,1,0:T(8,128)S(1)}, u32[]{:S(2)}, u32[]{:S(2)}) collective-permute-start(f32[2,2,64,512]{3,2,1,0:T(8,128)S(1)} %get-tuple-element.109.refs_5_), channel_id=1, source_target_pairs={{0,4},{1,5},{2,6},{3,7},{4,0},{5,1},{6,2},{7,3},{8,12},{9,13},{10,... | collective-permute-start | bytes 1572872 | tf_op jit(solution)/shard_map/ppermute | solution.py:65
  24.9 17.5 %collective-permute-start.6 = (f32[512,128]{1,0:T(8,128)S(1)}, f32[512,128]{1,0:T(8,128)S(1)}, u32[]{:S(2)}, u32[]{:S(2)}) collective-permute-start(f32[512,128]{1,0:T(8,128)S(1)} %get-tuple-element.107.refs_4_.refs_3_), channel_id=1, source_target_pairs={{0,8},{8,24},{24,16},{16,0},{1,9},{9,25},{25,17},{17,1},{10,2},{2,... | collective-permute-start | bytes 786440 | tf_op jit(solution)/shard_map/ppermute | solution.py:489
  26.4 16.0 %collective-permute-start.7 = (f32[512,128]{1,0:T(8,128)S(1)}, f32[512,128]{1,0:T(8,128)S(1)}, u32[]{:S(2)}, u32[]{:S(2)}) collective-permute-start(f32[512,128]{1,0:T(8,128)S(1)} %get-tuple-element.108.refs_7_), channel_id=1, source_target_pairs={{8,0},{24,8},{16,24},{0,16},{9,1},{25,9},{17,25},{1,17},{2,10},{18... | collective-permute-start | bytes 786440 | tf_op jit(solution)/shard_map/ppermute | solution.py:489
  43.0 9.9 %collective-permute-start.11 = (f32[4,2,64,512]{3,2,1,0:T(8,128)S(1)}, f32[4,2,64,512]{3,2,1,0:T(8,128)S(1)}, u32[]{:S(2)}, u32[]{:S(2)}) collective-permute-start(f32[4,2,64,512]{3,2,1,0:T(8,128)S(1)} %get-tuple-element.113.refs_5_), channel_id=1, source_target_pairs={{0,1},{1,0},{2,3},{3,2},{4,5},{5,4},{6,7},{7,6},{8,9},{9,8},{10,11... | collective-permute-start | bytes 3145736 | tf_op jit(solution)/shard_map/ppermute | solution.py:65
  43.1 8.7 %collective-permute-start.10 = (f32[512,128]{1,0:T(8,128)S(1)}, f32[512,128]{1,0:T(8,128)S(1)}, u32[]{:S(2)}, u32[]{:S(2)}) collective-permute-start(f32[512,128]{1,0:T(8,128)S(1)} %get-tuple-element.112.refs_15_), channel_id=1, source_target_pairs={{8,0},{24,8},{16,24},{0,16},{9,1},{25,9},{17,25},{1,17},{2,10},{18... | collective-permute-start | bytes 786440 | tf_op jit(solution)/shard_map/ppermute | solution.py:489
  44.5 8.4 %collective-permute-start.9 = (f32[512,128]{1,0:T(8,128)S(1)}, f32[512,128]{1,0:T(8,128)S(1)}, u32[]{:S(2)}, u32[]{:S(2)}) collective-permute-start(f32[512,128]{1,0:T(8,128)S(1)} %get-tuple-element.111.refs_4_.refs_11_), channel_id=1, source_target_pairs={{0,8},{8,24},{24,16},{16,0},{1,9},{9,25},{25,17},{17,1},{10,2},{2,... | collective-permute-start | bytes 786440 | tf_op jit(solution)/shard_map/ppermute | solution.py:489
  53.7 11.2 %collective-permute-start.13 = (f32[512,128]{1,0:T(8,128)S(1)}, f32[512,128]{1,0:T(8,128)S(1)}, u32[]{:S(2)}, u32[]{:S(2)}) collective-permute-start(f32[512,128]{1,0:T(8,128)S(1)} %get-tuple-element.117.refs_19_.refs_3_), channel_id=1, source_target_pairs={{0,8},{8,24},{24,16},{16,0},{1,9},{9,25},{25,17},{17,1},{10,2},{2,... | collective-permute-start | bytes 786440 | tf_op jit(solution)/shard_map/ppermute | solution.py:489
  54.4 10.5 %collective-permute-start.14 = (f32[512,128]{1,0:T(8,128)S(1)}, f32[512,128]{1,0:T(8,128)S(1)}, u32[]{:S(2)}, u32[]{:S(2)}) collective-permute-start(f32[512,128]{1,0:T(8,128)S(1)} %get-tuple-element.123.refs_7_), channel_id=1, source_target_pairs={{8,0},{24,8},{16,24},{0,16},{9,1},{25,9},{17,25},{1,17},{2,10},{18... | collective-permute-start | bytes 786440 | tf_op jit(solution)/shard_map/ppermute | solution.py:489
  55.7 3.2 %copy-start.2 = (f32[3,64,512]{2,1,0:T(8,128)S(1)}, f32[3,64,512]{2,1,0:T(8,128)}, u32[]{:S(2)}) copy-start(f32[3,64,512]{2,1,0:T(8,128)} %refs_1_.15) | copy-start | bytes 1179652
  58.2 12.7 %collective-permute-start.17 = (f32[512,256]{1,0:T(8,128)S(1)}, f32[512,256]{1,0:T(8,128)S(1)}, u32[]{:S(2)}, u32[]{:S(2)}) collective-permute-start(f32[512,256]{1,0:T(8,128)S(1)} %get-tuple-element.126), channel_id=1, source_target_pairs={{0,2},{1,3},{2,0},{3,1},{4,6},{5,7},{6,4},{7,5},{8,10},{9,11},{10,... | collective-permute-start | bytes 1572872 | tf_op jit(solution)/shard_map/ppermute | solution.py:65
  58.9 1.4 collective-permute-start.12
  65.5 8.4 %collective-permute-start.15 = (f32[512,128]{1,0:T(8,128)S(1)}, f32[512,128]{1,0:T(8,128)S(1)}, u32[]{:S(2)}, u32[]{:S(2)}) collective-permute-start(f32[512,128]{1,0:T(8,128)S(1)} %get-tuple-element.124.refs_5_.refs_11_), channel_id=1, source_target_pairs={{0,8},{8,24},{24,16},{16,0},{1,9},{9,25},{25,17},{17,1},{10,2},{2,... | collective-permute-start | bytes 786440 | tf_op jit(solution)/shard_map/ppermute | solution.py:489
  67.0 8.1 %collective-permute-start.16 = (f32[512,128]{1,0:T(8,128)S(1)}, f32[512,128]{1,0:T(8,128)S(1)}, u32[]{:S(2)}, u32[]{:S(2)}) collective-permute-start(f32[512,128]{1,0:T(8,128)S(1)} %get-tuple-element.125.refs_15_), channel_id=1, source_target_pairs={{8,0},{24,8},{16,24},{0,16},{9,1},{25,9},{17,25},{1,17},{2,10},{18... | collective-permute-start | bytes 786440 | tf_op jit(solution)/shard_map/ppermute | solution.py:489
  75.8 9.0 %collective-permute-start.19 = (f32[512,128]{1,0:T(8,128)S(1)}, f32[512,128]{1,0:T(8,128)S(1)}, u32[]{:S(2)}, u32[]{:S(2)}) collective-permute-start(f32[512,128]{1,0:T(8,128)S(1)} %get-tuple-element.129.refs_19_), channel_id=1, source_target_pairs={{0,8},{8,24},{24,16},{16,0},{1,9},{9,25},{25,17},{17,1},{10,2},{2,... | collective-permute-start | bytes 786440 | tf_op jit(solution)/shard_map/ppermute | solution.py:489
  76.4 8.4 %collective-permute-start.20 = (f32[512,128]{1,0:T(8,128)S(1)}, f32[512,128]{1,0:T(8,128)S(1)}, u32[]{:S(2)}, u32[]{:S(2)}) collective-permute-start(f32[512,128]{1,0:T(8,128)S(1)} %get-tuple-element.130), channel_id=1, source_target_pairs={{8,0},{24,8},{16,24},{0,16},{9,1},{25,9},{17,25},{1,17},{2,10},{18... | collective-permute-start | bytes 786440 | tf_op jit(solution)/shard_map/ppermute | solution.py:489
  77.9 14.0 %collective-permute-start.18 = (f32[256,256]{1,0:T(8,128)S(1)}, f32[256,256]{1,0:T(8,128)S(1)}, u32[]{:S(2)}, u32[]{:S(2)}) collective-permute-start(f32[256,256]{1,0:T(8,128)S(1)} %get-tuple-element.128), channel_id=1, source_target_pairs={{0,4},{1,5},{2,6},{3,7},{4,0},{5,1},{6,2},{7,3},{8,12},{9,13},{10,... | collective-permute-start | bytes 786440 | tf_op jit(solution)/shard_map/ppermute | solution.py:65
  83.7 24.0 %collective-permute-start.22 = (f32[512,256]{1,0:T(8,128)S(1)}, f32[512,256]{1,0:T(8,128)S(1)}, u32[]{:S(2)}, u32[]{:S(2)}) collective-permute-start(f32[512,256]{1,0:T(8,128)S(1)} %get-tuple-element.133.refs_3_), channel_id=1, source_target_pairs={{0,2},{1,3},{2,0},{3,1},{4,6},{5,7},{6,4},{7,5},{8,10},{9,11},{10,... | collective-permute-start | bytes 1572872 | tf_op jit(solution)/shard_map/ppermute | solution.py:65
  92.5 2.2 %collective-permute-start.21 = (f32[256,256]{1,0:T(8,128)S(1)}, f32[256,256]{1,0:T(8,128)S(1)}, u32[]{:S(2)}, u32[]{:S(2)}) collective-permute-start(f32[256,256]{1,0:T(8,128)S(1)} %shard_map.94.refs_9_.refs_11_), channel_id=1, source_target_pairs={{0,1},{1,0},{2,3},{3,2},{4,5},{5,4},{6,7},{7,6},{8,9},{9,8},{10,11... | collective-permute-start | bytes 786440 | tf_op jit(solution)/shard_map/ppermute | solution.py:65
  92.5 8.7 %collective-permute-start.23 = (f32[512,128]{1,0:T(8,128)S(1)}, f32[512,128]{1,0:T(8,128)S(1)}, u32[]{:S(2)}, u32[]{:S(2)}) collective-permute-start(f32[512,128]{1,0:T(8,128)S(1)} %get-tuple-element.134.refs_3_), channel_id=1, source_target_pairs={{0,8},{8,24},{24,16},{16,0},{1,9},{9,25},{25,17},{17,1},{10,2},{2,... | collective-permute-start | bytes 786440 | tf_op jit(solution)/shard_map/ppermute | solution.py:489
  93.2 8.4 %collective-permute-start.24 = (f32[512,128]{1,0:T(8,128)S(1)}, f32[512,128]{1,0:T(8,128)S(1)}, u32[]{:S(2)}, u32[]{:S(2)}) collective-permute-start(f32[512,128]{1,0:T(8,128)S(1)} %get-tuple-element.137), channel_id=1, source_target_pairs={{8,0},{24,8},{16,24},{0,16},{9,1},{25,9},{17,25},{1,17},{2,10},{18... | collective-permute-start | bytes 786440 | tf_op jit(solution)/shard_map/ppermute | solution.py:489
  104.0 22.1 %collective-permute-start.29 = (f32[512,256]{1,0:T(8,128)S(1)}, f32[512,256]{1,0:T(8,128)S(1)}, u32[]{:S(2)}, u32[]{:S(2)}) collective-permute-start(f32[512,256]{1,0:T(8,128)S(1)} %get-tuple-element.145.refs_3_), channel_id=1, source_target_pairs={{0,2},{1,3},{2,0},{3,1},{4,6},{5,7},{6,4},{7,5},{8,10},{9,11},{10,... | collective-permute-start | bytes 1572872 | tf_op jit(solution)/shard_map/ppermute | solution.py:65
  104.1 17.2 %collective-permute-start.26 = (f32[3,128,256]{2,1,0:T(8,128)S(1)}, f32[3,128,256]{2,1,0:T(8,128)S(1)}, u32[]{:S(2)}, u32[]{:S(2)}) collective-permute-start(f32[3,128,256]{2,1,0:T(8,128)S(1)} %get-tuple-element.142), channel_id=1, source_target_pairs={{0,8},{8,0},{16,24},{24,16},{1,9},{9,1},{17,25},{25,17},{2,10},{10... | collective-permute-start | bytes 1179656 | tf_op jit(solution)/shard_map/ppermute | solution.py:65
  104.7 18.0 %collective-permute-start.27 = (f32[3,128,256]{2,1,0:T(8,128)S(1)}, f32[3,128,256]{2,1,0:T(8,128)S(1)}, u32[]{:S(2)}, u32[]{:S(2)}) collective-permute-start(f32[3,128,256]{2,1,0:T(8,128)S(1)} %get-tuple-element.143), channel_id=1, source_target_pairs={{0,16},{8,24},{16,0},{24,8},{1,17},{9,25},{17,1},{25,9},{2,18},{10... | collective-permute-start | bytes 1179656 | tf_op jit(solution)/shard_map/ppermute | solution.py:65
  106.2 19.9 %collective-permute-start.28 = (f32[3,128,256]{2,1,0:T(8,128)S(1)}, f32[3,128,256]{2,1,0:T(8,128)S(1)}, u32[]{:S(2)}, u32[]{:S(2)}) collective-permute-start(f32[3,128,256]{2,1,0:T(8,128)S(1)} %get-tuple-element.144), channel_id=1, source_target_pairs={{0,24},{8,16},{16,8},{24,0},{1,25},{9,17},{17,9},{25,1},{2,26},{10... | collective-permute-start | bytes 1179656 | tf_op jit(solution)/shard_map/ppermute | solution.py:65
  108.2 12.4 %collective-permute-start.25 = (f32[256,256]{1,0:T(8,128)S(1)}, f32[256,256]{1,0:T(8,128)S(1)}, u32[]{:S(2)}, u32[]{:S(2)}) collective-permute-start(f32[256,256]{1,0:T(8,128)S(1)} %get-tuple-element.140), channel_id=1, source_target_pairs={{0,4},{1,5},{2,6},{3,7},{4,0},{5,1},{6,2},{7,3},{8,12},{9,13},{10,... | collective-permute-start | bytes 786440 | tf_op jit(solution)/shard_map/ppermute | solution.py:65
  120.7 9.2 %collective-permute-start.33 = (f32[2,128,256]{2,1,0:T(8,128)S(1)}, f32[2,128,256]{2,1,0:T(8,128)S(1)}, u32[]{:S(2)}, u32[]{:S(2)}) collective-permute-start(f32[2,128,256]{2,1,0:T(8,128)S(1)} %get-tuple-element.159), channel_id=1, source_target_pairs={{0,8},{8,0},{16,24},{24,16},{1,9},{9,1},{17,25},{25,17},{2,10},{10... | collective-permute-start | bytes 786440 | tf_op jit(solution)/shard_map/ppermute | solution.py:65
  121.3 9.5 %collective-permute-start.34 = (f32[2,128,256]{2,1,0:T(8,128)S(1)}, f32[2,128,256]{2,1,0:T(8,128)S(1)}, u32[]{:S(2)}, u32[]{:S(2)}) collective-permute-start(f32[2,128,256]{2,1,0:T(8,128)S(1)} %get-tuple-element.160), channel_id=1, source_target_pairs={{0,16},{8,24},{16,0},{24,8},{1,17},{9,25},{17,1},{25,9},{2,18},{10... | collective-permute-start | bytes 786440 | tf_op jit(solution)/shard_map/ppermute | solution.py:65
  122.7 12.3 %collective-permute-start.35 = (f32[2,128,256]{2,1,0:T(8,128)S(1)}, f32[2,128,256]{2,1,0:T(8,128)S(1)}, u32[]{:S(2)}, u32[]{:S(2)}) collective-permute-start(f32[2,128,256]{2,1,0:T(8,128)S(1)} %get-tuple-element.161), channel_id=1, source_target_pairs={{0,24},{8,16},{16,8},{24,0},{1,25},{9,17},{17,9},{25,1},{2,26},{10... | collective-permute-start | bytes 786440 | tf_op jit(solution)/shard_map/ppermute | solution.py:65
  126.8 11.5 %collective-permute-start.32 = (f32[256,256]{1,0:T(8,128)S(1)}, f32[256,256]{1,0:T(8,128)S(1)}, u32[]{:S(2)}, u32[]{:S(2)}) collective-permute-start(f32[256,256]{1,0:T(8,128)S(1)} %get-tuple-element.158), channel_id=1, source_target_pairs={{0,4},{1,5},{2,6},{3,7},{4,0},{5,1},{6,2},{7,3},{8,12},{9,13},{10,... | collective-permute-start | bytes 786440 | tf_op jit(solution)/shard_map/ppermute | solution.py:65
  128.3 7.9 %collective-permute-start.31 = (f32[3,64,256]{2,1,0:T(8,128)S(1)}, f32[3,64,256]{2,1,0:T(8,128)S(1)}, u32[]{:S(2)}, u32[]{:S(2)}) collective-permute-start(f32[3,64,256]{2,1,0:T(8,128)S(1)} %get-tuple-element.156), channel_id=1, source_target_pairs={{0,2},{1,3},{2,0},{3,1},{4,6},{5,7},{6,4},{7,5},{8,10},{9,11},{10,... | collective-permute-start | bytes 589832 | tf_op jit(solution)/shard_map/ppermute | solution.py:65
  129.9 12.5 %collective-permute-start.30 = (f32[128,256]{1,0:T(8,128)S(1)}, f32[128,256]{1,0:T(8,128)S(1)}, u32[]{:S(2)}, u32[]{:S(2)}) collective-permute-start(f32[128,256]{1,0:T(8,128)S(1)} %get-tuple-element.154), channel_id=1, source_target_pairs={{0,1},{1,0},{2,3},{3,2},{4,5},{5,4},{6,7},{7,6},{8,9},{9,8},{10,11... | collective-permute-start | bytes 393224 | tf_op jit(solution)/shard_map/ppermute | solution.py:65
  138.9 5.5 %collective-permute-start.36 = (f32[128,256]{1,0:T(8,128)S(1)}, f32[128,256]{1,0:T(8,128)S(1)}, u32[]{:S(2)}, u32[]{:S(2)}) collective-permute-start(f32[128,256]{1,0:T(8,128)S(1)} %get-tuple-element.163), channel_id=1, source_target_pairs={{0,1},{1,0},{2,3},{3,2},{4,5},{5,4},{6,7},{7,6},{8,9},{9,8},{10,11... | collective-permute-start | bytes 393224 | tf_op jit(solution)/shard_map/ppermute | solution.py:65
  139.0 12.3 %collective-permute-start.37 = (f32[3,32,256]{2,1,0:T(8,128)S(1)}, f32[3,32,256]{2,1,0:T(8,128)S(1)}, u32[]{:S(2)}, u32[]{:S(2)}) collective-permute-start(f32[3,32,256]{2,1,0:T(8,128)S(1)} %get-tuple-element.166), channel_id=1, source_target_pairs={{0,4},{1,5},{2,6},{3,7},{4,0},{5,1},{6,2},{7,3},{8,12},{9,13},{10,... | collective-permute-start | bytes 294920 | tf_op jit(solution)/shard_map/ppermute | solution.py:65
  140.1 11.3 %collective-permute-start.38 = (f32[2,32,256]{2,1,0:T(8,128)S(1)}, f32[2,32,256]{2,1,0:T(8,128)S(1)}, u32[]{:S(2)}, u32[]{:S(2)}) collective-permute-start(f32[2,32,256]{2,1,0:T(8,128)S(1)} %get-tuple-element.168), channel_id=1, source_target_pairs={{0,4},{1,5},{2,6},{3,7},{4,0},{5,1},{6,2},{7,3},{8,12},{9,13},{10,... | collective-permute-start | bytes 196616 | tf_op jit(solution)/shard_map/ppermute | solution.py:65
  142.0 9.3 %collective-permute-start.39 = (f32[2,32,256]{2,1,0:T(8,128)S(1)}, f32[2,32,256]{2,1,0:T(8,128)S(1)}, u32[]{:S(2)}, u32[]{:S(2)}) collective-permute-start(f32[2,32,256]{2,1,0:T(8,128)S(1)} %get-tuple-element.169), channel_id=1, source_target_pairs={{0,2},{1,3},{2,0},{3,1},{4,6},{5,7},{6,4},{7,5},{8,10},{9,11},{10,... | collective-permute-start | bytes 196616 | tf_op jit(solution)/shard_map/ppermute | solution.py:65
  142.4 8.9 %collective-permute-start.40 = (f32[2,32,256]{2,1,0:T(8,128)S(1)}, f32[2,32,256]{2,1,0:T(8,128)S(1)}, u32[]{:S(2)}, u32[]{:S(2)}) collective-permute-start(f32[2,32,256]{2,1,0:T(8,128)S(1)} %get-tuple-element.170), channel_id=1, source_target_pairs={{0,6},{1,7},{2,4},{3,5},{4,2},{5,3},{6,0},{7,1},{8,14},{9,15},{10,... | collective-permute-start | bytes 196616 | tf_op jit(solution)/shard_map/ppermute | solution.py:65
  151.3 1.1 copy-start.1
  153.0 1.4 collective-permute-start.41
  153.1 1.3 collective-permute-start.42
  155.0 7.1 %collective-permute-start.43 = (f32[5,16,512]{2,1,0:T(8,128)S(1)}, f32[5,16,512]{2,1,0:T(8,128)S(1)}, u32[]{:S(2)}, u32[]{:S(2)}) collective-permute-start(f32[5,16,512]{2,1,0:T(8,128)S(1)} %shard_map.104.refs_3_.refs_7_), channel_id=1, source_target_pairs={{0,8},{8,0},{16,24},{24,16},{1,9},{9,1},{17,25},{25,17},{2,10},{10... | collective-permute-start | bytes 491528 | tf_op jit(solution)/shard_map/ppermute | solution.py:65
  156.2 8.2 %collective-permute-start.44 = (f32[5,16,512]{2,1,0:T(8,128)S(1)}, f32[5,16,512]{2,1,0:T(8,128)S(1)}, u32[]{:S(2)}, u32[]{:S(2)}) collective-permute-start(f32[5,16,512]{2,1,0:T(8,128)S(1)} %shard_map.104.refs_3_.refs_7_), channel_id=1, source_target_pairs={{0,16},{8,24},{16,0},{24,8},{1,17},{9,25},{17,1},{25,9},{2,18},{10... | collective-permute-start | bytes 491528 | tf_op jit(solution)/shard_map/ppermute | solution.py:65
  157.2 8.7 %collective-permute-start.45 = (f32[5,16,512]{2,1,0:T(8,128)S(1)}, f32[5,16,512]{2,1,0:T(8,128)S(1)}, u32[]{:S(2)}, u32[]{:S(2)}) collective-permute-start(f32[5,16,512]{2,1,0:T(8,128)S(1)} %shard_map.104.refs_3_.refs_7_), channel_id=1, source_target_pairs={{0,24},{8,16},{16,8},{24,0},{1,25},{9,17},{17,9},{25,1},{2,26},{10... | collective-permute-start | bytes 491528 | tf_op jit(solution)/shard_map/ppermute | solution.py:65

commit v14 on v11

--- a/solution.py
+++ b/solution.py
@@ -216,7 +216,7 @@
 
 
 def link_kernel(
-    children, share, info_ref, gathered_ref, diag_ref, other_ref, chooser_ref,
+    children, share, order, info_ref, gathered_ref, diag_ref, other_ref, chooser_ref,
     own_high_ref, own_low_ref, high_ref, low_ref, lift_high_ref, lift_low_ref, framed_ref,
     corner_ref, held_ref, rows_ref, frame_ref,
 ):
@@ -226,7 +226,7 @@
     chooser = chooser_ref[...]
     for g in range(groups):
         for c in range(children):
-            held_ref[c, block(info_ref[1] ^ g, size), :] = gathered_ref[g, c]
+            held_ref[c, block(info_ref[1] ^ order[g], size), :] = gathered_ref[g, c]
     rows_ref[block(core, size), :] = diag_ref[0]
     rows_ref[block(1 - core, size), :] = other_ref[0]
     diag = split(rows_ref[...])
@@ -282,7 +282,7 @@
 def parent_kernel(
     children, rows_here, info_ref, listed_ref, chooser_ref, own_high_ref, own_low_ref,
     own_thigh_ref, own_tlow_ref, link_high_ref, link_low_ref, mine_ref, other_ref,
-    col_ref, turned_ref, high_ref, low_ref, *refs
+    col_ref, high_ref, low_ref, *refs
 ):
     *outs, full_ref = refs
     chooser = chooser_ref[...]
@@ -292,33 +292,36 @@
     mine = -mine_ref[...] * weight
     full_ref[:, block(core, half)] = mine
     full_ref[:, block(1 - core, half)] = -other_ref[...] * weight
-    output_rows = block(core, rows // 2)
-    col_ref[...] = full_ref[output_rows, :]
+    col_ref[...] = full_ref[block(core, rows // 2), :]
     pair = split(full_ref[...])
+    store_pair(high_ref, low_ref, pair)
     turned_pair = turn(chooser, pair)
     parent = pair_of(own_thigh_ref, own_tlow_ref, 0)
     columns = block(core, half)
     store_parts(outs, 0, -product(parent, split(mine)))
     for c in range(children):
-        full_ref[...] = product(pair, pair_of(link_high_ref, link_low_ref, c))
-        turned_ref[c] = full_ref[output_rows, :]
-        lifted = split(full_ref[:, columns])
-        store_pair(high_ref, low_ref, split(full_ref[...]), c)
+        link = (link_high_ref[c, :, columns], link_low_ref[c, :, columns])
+        lifted = split(product(pair, link))
         own = (own_high_ref[c + 1, :, columns], own_low_ref[c + 1, :, columns])
         store_parts(outs, 1 + c, product(parent, lifted) - product(turned_pair, own))
 
 
 def child_kernel(
     children, info_ref, chooser_ref, own_high_ref, own_low_ref, own_thigh_ref, own_tlow_ref,
-    high_ref, low_ref, lift_high_ref, lift_low_ref, corner_ref, *refs
+    high_ref, low_ref, link_high_ref, link_low_ref, lift_high_ref, lift_low_ref, corner_ref, *refs
 ):
-    outs = refs[children:]
-    columns = block(core_of(info_ref), corner_ref.shape[2])
+    *refs, full_ref = refs
+    grams, outs, turned_ref = refs[:children], refs[children:-1], refs[-1]
+    core = core_of(info_ref)
+    columns = block(core, corner_ref.shape[2])
+    pair = pair_of(high_ref, low_ref)
     for c in range(children):
-        lifted = (high_ref[c, :, columns], low_ref[c, :, columns])
-        turned_pair = turn(chooser_ref[...], pair_of(high_ref, low_ref, c))
+        full_ref[...] = product(pair, pair_of(link_high_ref, link_low_ref, c))
+        turned_ref[c] = full_ref[block(core, full_ref.shape[0] // 2), :]
+        lifted = split(full_ref[:, columns])
+        turned_pair = turn(chooser_ref[...], split(full_ref[...]))
         own = (own_high_ref[c + 1, :, columns], own_low_ref[c + 1, :, columns])
-        total = corner_ref[c] + refs[c][...]
+        total = corner_ref[c] + grams[c][...]
         total += product(pair_of(own_thigh_ref, own_tlow_ref, c + 1), lifted)
         total += product(turned_pair, own)
         total -= product(pair_of(lift_high_ref, lift_low_ref, c), lifted)
@@ -441,6 +444,10 @@
         return pairs
 
     rings = (ring(True), ring(False))
+    link_bits = [*range(1, col_bits), 0]
+    link_order = [0]
+    for bit in link_bits:
+        link_order = [value ^ (side << bit) for value in link_order for side in range(2)]
     info = jnp.stack([lax.axis_index("row"), lax.axis_index("col")]).astype(jnp.int32)
 
     def cut(chosen, run):
@@ -483,12 +490,22 @@
 
     def link_flow():
         gathered = parent_factor[None]
-        for bit in reversed(range(col_bits)):
+        for bit in link_bits:
             arrived = swap(gathered, "col", col_count, 1 << bit)
             dims = (2 * gathered.shape[0],) + parent_factor.shape
-            (gathered,) = yield (stack_step, [gathered, arrived], [shape(*dims)])
+            if bit:
+                if bit > 1:
+                    yield WAIT
+                (gathered,) = yield (stack_step, [gathered, arrived], [shape(*dims)])
+            else:
+                (gathered,) = heavy(
+                    functools.partial(step_kernel, [(stack_step, 2, 1)]),
+                    [shape(*dims)],
+                    [info, gathered, arrived],
+                    smem=1,
+                )
         held["links"] = heavy(
-            functools.partial(link_kernel, children, 1.0 / row_count),
+            functools.partial(link_kernel, children, 1.0 / row_count, link_order),
             [shape(children, width, width, dtype=BF16)] * 2
             + [shape(children, width, group, dtype=BF16)] * 2
             + [shape(children, diag_width, width), shape(children, width, half)],
@@ -620,16 +637,16 @@
             smem=1,
         )
         other = swap(mine, "col", col_count, 1)
-        col, turned, *rest = heavy(
+        col, *rest = heavy(
             functools.partial(parent_kernel, children, rows_here),
-            [shape(group // 2, width), shape(children, group // 2, width)]
-            + [shape(children, group, width, dtype=BF16)] * 2
+            [shape(group // 2, width)]
+            + [shape(group, width, dtype=BF16)] * 2
             + [shape(members, width // row_count, half)] * row_count,
             [info, listed, held["chooser"], *held["own"], *held["links"][:2], mine, other],
             smem=2, vmem=20,
             scratch=[pltpu.VMEM((group, width), F32)],
         )
-        held["parent"] = (col, turned, rest[:2])
+        held["parent"] = (col, rest[:2])
         yield WAIT
         yield from total_flow("parent totals", rest[2:], False)
 
@@ -637,13 +654,15 @@
         names = [("gram", 1 + c) for c in range(children)]
         while any(name not in held for name in names + ["parent"]):
             yield WAIT
-        pieces = heavy(
+        *pieces, held["lifted"] = heavy(
             functools.partial(child_kernel, children),
-            [shape(children, width // row_count, half)] * row_count,
-            [info, held["chooser"], *held["own"], *held["parent"][2], *held["links"][2:4]]
+            [shape(children, width // row_count, half)] * row_count
+            + [shape(children, group // 2, width)],
+            [info, held["chooser"], *held["own"], *held["parent"][1], *held["links"][:4]]
             + [held["links"][5]]
             + [held[name] for name in names],
             smem=1, vmem=20,
+            scratch=[pltpu.VMEM((group, width), F32)],
         )
         yield WAIT
         yield from total_flow("child totals", pieces, True)
@@ -654,7 +673,7 @@
             yield WAIT
         while "totals" not in held:
             yield WAIT
-        col, turned, _ = held["parent"]
+        col, turned = held["parent"][0], held["lifted"]
         held["columns"] = heavy(
             functools.partial(column_kernel, children, rows_here),
             [shape(members, group // 2, width)],

time: 160 us -> 155 us (0.969)
  starting transfers between devices: 48.2 us -> 45.3 us
  waiting for transfers between devices: 64.4 us -> 61.6 us
    ppermute x10, waiting for transfers between devices: 19.6 us -> 15.7 us  [ring_flow(): lax.ppermute(moving[way], AXES, rings[way])]
    ppermute x10, starting transfers between devices: 13 us -> 11 us  [ring_flow(): lax.ppermute(moving[way], AXES, rings[way])]
    pallas_call x27 -> x28, Pallas kernels: 43.9 us -> 44.6 us  [call(): pl.pallas_call(inner, out_shape=outs, in_specs=[pl.BlockSpec(memory_space...]
  transfers between devices with their start and end apart: 40 -> 40, of which waited for: 23 -> 26; matrix products, arithmetic and copies ran while one was open for 0% -> 0% of each run, Pallas kernels for 24% -> 26%
where the time goes in v14:
time: 155 us; the launch traced here: 154 us
  waiting for transfers between devices  61.6 us (40%)
  starting transfers between devices  45.3 us (29%)
  Pallas kernels  44.6 us (29%)
  local copies, waits for them, and re-layouts  1.85 us (1%)
    ppermute x30, waiting for transfers between devices, swap(): lax.ppermute(value, axis, [(place, place ^ change) for place in range(siz...  45.9 us
    pallas_call x28, Pallas kernels, call(): pl.pallas_call(inner, out_shape=outs, in_specs=[pl.BlockSpec(memory_space...  44.6 us
    ppermute x30, starting transfers between devices, swap(): lax.ppermute(value, axis, [(place, place ^ change) for place in range(siz...  34.3 us
    ppermute x10, waiting for transfers between devices, ring_flow(): lax.ppermute(moving[way], AXES, rings[way])  15.7 us
    ppermute x10, starting transfers between devices, ring_flow(): lax.ppermute(moving[way], AXES, rings[way])  11 us
  transfers between devices with their start and end apart: 40, of which 26 were waited for; matrix products, arithmetic and copies ran while one was open for 0% of the time, Pallas kernels for 26%

profile of v14, /device:TPU:0, one launch (start us, length us, event | category | flops | bytes accessed | tf_op | source)
XLA Modules:
  0.0 154.4 jit_solution(13095113307990037028)
XLA Ops:
  1.2 0.7 copy-done.4
  1.9 2.1 %shard_map.76 = (f32[512,256]{1,0:T(8,128)S(1)}, f32[512,256]{1,0:T(8,128)S(1)}) custom-call(s32[2]{0:T(128)S(1)} %pad_add_fusion.info_ref.refs_0_, s32[3,8]{1,0:T(4,128)S(1)} %copy-done.4, f32[3,1024,512]{2,1,0:T(8,128)} %refs_2_.9), custom_call_target="tpu_custom_call" | custom-call | flops 1024 | bytes 1024 | tf_op jit(solution)/shard_map/pallas_call | solution.py:89
  4.1 2.6 %collective-permute-start.1 = (f32[512,256]{1,0:T(8,128)S(1)}, f32[512,256]{1,0:T(8,128)S(1)}, u32[]{:S(2)}, u32[]{:S(2)}) collective-permute-start(f32[512,256]{1,0:T(8,128)S(1)} %get-tuple-element.86.refs_7_), channel_id=1, source_target_pairs={{8,0},{24,8},{16,24},{0,16},{9,1},{25,9},{17,25},{1,17},{2,10},{18... | collective-permute-start | bytes 1572872 | tf_op jit(solution)/shard_map/ppermute | solution.py:489
  6.7 2.0 %collective-permute-start.2 = (f32[1,2,64,512]{3,2,1,0:T(8,128)S(1)}, f32[1,2,64,512]{3,2,1,0:T(8,128)S(1)}, u32[]{:S(2)}, u32[]{:S(2)}) collective-permute-start(f32[1,2,64,512]{3,2,1,0:T(8,128)S(1)} %bitcast.5), channel_id=1, source_target_pairs={{0,2},{1,3},{2,0},{3,1},{4,6},{5,7},{6,4},{7,5},{8,10},{9,11},{10,... | collective-permute-start | bytes 786440 | tf_op jit(solution)/shard_map/ppermute | solution.py:65
  8.7 2.2 %shard_map.77 = (f32[512,256]{1,0:T(8,128)S(1)}, f32[512,256]{1,0:T(8,128)S(1)}, f32[512,256]{1,0:T(8,128)S(1)}, f32[512,256]{1,0:T(8,128)S(1)}) custom-call(s32[2]{0:T(128)S(1)} %pad_add_fusion.info_ref.refs_0_, s32[3,8]{1,0:T(4,128)S(1)} %copy-done.5, f32[3,1024,512]{2,1,0:T(8,128)} %refs_2_.9, f32[512,256]{1,0:T(8,128)S(1)} %get-tuple-element.77.refs_3_), custom_call_target="tpu_custom_call" | custom-call | flops 1024 | bytes 1024 | tf_op jit(solution)/shard_map/pallas_call | solution.py:89
  10.9 0.8 shard_map.78.refs_3_.refs_4_.refs_2_.refs_1_
  11.8 2.2 %shard_map.79 = (bf16[3,256,512]{2,1,0:T(8,128)(2,1)S(1)}, bf16[3,256,512]{2,1,0:T(8,128)(2,1)S(1)}, bf16[3,512,256]{2,1,0:T(8,128)(2,1)S(1)}, bf16[3,512,256]{2,1,0:T(8,128)(2,1)S(1)}) custom-call(s32[2]{0:T(128)S(1)} %pad_add_fusion.info_ref.refs_0_, s32[3,8]{1,0:T(4,128)S(1)} %copy-done.5, f32[3,1024,512]{2,1,0:T(8,128)S(1)} %bitcast.4, ...), custom_call_target="tpu_custom_call" | custom-call | flops 1024 | bytes 1024 | tf_op jit(solution)/shard_map/pallas_call | solution.py:89
  14.0 1.1 collective-permute-done.2.refs_6_
  15.1 4.1 %collective-permute-done.1.refs_4_.refs_8_ = f32[512,256]{1,0:T(8,128)S(1)} collective-permute-done((f32[512,256]{1,0:T(8,128)S(1)}, f32[512,256]{1,0:T(8,128)S(1)}, u32[]{:S(2)}, u32[]{:S(2)}) %collective-permute-start.1) | collective-permute-done | bytes 524320 | tf_op jit(solution)/shard_map/ppermute | solution.py:489
  19.2 1.5 collective-permute-done.refs_3_.refs_4_
  20.7 0.7 shard_map.80
  21.4 1.5 collective-permute-start.4
  23.5 2.6 %collective-permute-start.8 = (f32[2,2,64,512]{3,2,1,0:T(8,128)S(1)}, f32[2,2,64,512]{3,2,1,0:T(8,128)S(1)}, u32[]{:S(2)}, u32[]{:S(2)}) collective-permute-start(f32[2,2,64,512]{3,2,1,0:T(8,128)S(1)} %get-tuple-element.92.refs_3_), channel_id=1, source_target_pairs={{0,4},{1,5},{2,6},{3,7},{4,0},{5,1},{6,2},{7,3},{8,12},{9,13},{10,... | collective-permute-start | bytes 1572872 | tf_op jit(solution)/shard_map/ppermute | solution.py:65
  26.0 1.7 %shard_map.81 = (bf16[1024,1024]{1,0:T(8,128)(2,1)S(1)}, bf16[1024,1024]{1,0:T(8,128)(2,1)S(1)}) custom-call(s32[2]{0:T(128)S(1)} %pad_add_fusion.info_ref.refs_0_, f32[1024,512]{1,0:T(8,128)S(1)} %copy-done.2, f32[1024,512]{1,0:T(8,128)S(1)} %collective-permute-done.5.refs_2_, f32[512,256]{1,0:T(8,128)S(1)} %get-tuple-element.87.refs_3_), custom_call_target="tpu_custom_call" | custom-call | flops 1024 | bytes 1024 | tf_op jit(solution)/shard_map/pallas_call | solution.py:89
  27.7 6.9 %collective-permute-done.4.refs_4_.refs_9_.refs_8_ = f32[512,256]{1,0:T(8,128)S(1)} collective-permute-done((f32[512,256]{1,0:T(8,128)S(1)}, f32[512,256]{1,0:T(8,128)S(1)}, u32[]{:S(2)}, u32[]{:S(2)}) %collective-permute-start.4) | collective-permute-done | bytes 524320 | tf_op jit(solution)/shard_map/ppermute | solution.py:489
  34.7 1.2 collective-permute-done.3.refs_3_.refs_5_.refs_4_
  37.2 1.4 collective-permute-start.6
  38.6 2.2 %shard_map.83 = (bf16[512,1024]{1,0:T(8,128)(2,1)S(1)}, bf16[512,1024]{1,0:T(8,128)(2,1)S(1)}) custom-call(s32[2]{0:T(128)S(1)} %pad_add_fusion.info_ref.refs_0_, s32[3,8]{1,0:T(4,128)S(1)} %copy-done.5, f32[3,1024,512]{2,1,0:T(8,128)S(1)} %bitcast.4, bf16[512,512]{1,0:T(8,128)(2,1)S(1)} %shard_map.78.refs_3_.refs_4_.refs_2_.refs_1_, ...), custom_call_target="tpu_custom_call" | custom-call | flops 1024 | bytes 1024 | tf_op jit(solution)/shard_map/pallas_call | solution.py:89
  40.8 7.4 %collective-permute-done.8.refs_4_ = f32[2,2,64,512]{3,2,1,0:T(8,128)S(1)} collective-permute-done((f32[2,2,64,512]{3,2,1,0:T(8,128)S(1)}, f32[2,2,64,512]{3,2,1,0:T(8,128)S(1)}, u32[]{:S(2)}, u32[]{:S(2)}) %collective-permute-start.8) | collective-permute-done | bytes 524320 | tf_op jit(solution)/shard_map/ppermute | solution.py:65
  49.8 0.8 collective-permute-start.12
  50.6 2.4 %shard_map.85 = (f32[512,256]{1,0:T(8,128)S(1)}, f32[512,256]{1,0:T(8,128)S(1)}) custom-call(s32[2]{0:T(128)S(1)} %pad_add_fusion.info_ref.refs_0_, bf16[1024,1024]{1,0:T(8,128)(2,1)S(1)} %get-tuple-element.89.refs_5_.refs_1_, bf16[1024,1024]{1,0:T(8,128)(2,1)S(1)} %get-tuple-element.95.refs_2_, f32[512,256]{1,0:T(8,128)S(1)} %get-tuple-element.77.refs_3_, ...), custom_call_target="tpu_custom_call" | custom-call | flops 1024 | bytes 1024 | tf_op jit(solution)/shard_map/pallas_call | solution.py:89
  53.0 1.4 collective-permute-start.13
  54.4 1.3 collective-permute-start.11
  57.1 4.5 %shard_map.87 = (bf16[2,512,512]{2,1,0:T(8,128)(2,1)S(1)}, bf16[2,512,512]{2,1,0:T(8,128)(2,1)S(1)}, bf16[2,512,256]{2,1,0:T(8,128)(2,1)S(1)}, bf16[2,512,256]{2...) custom-call(s32[2]{0:T(128)S(1)} %pad_add_fusion.info_ref.refs_0_, ...), custom_call_target="tpu_custom_call" | custom-call | flops 1024 | bytes 1024 | tf_op jit(solution)/shard_map/pallas_call | solution.py:89
  61.7 2.2 %shard_map.88 = (bf16[512,1024]{1,0:T(8,128)(2,1)S(1)}, bf16[512,1024]{1,0:T(8,128)(2,1)S(1)}) custom-call(s32[2]{0:T(128)S(1)} %pad_add_fusion.info_ref.refs_0_, s32[3,8]{1,0:T(4,128)S(1)} %copy-done.5, f32[3,1024,512]{2,1,0:T(8,128)S(1)} %bitcast.4, bf16[512,512]{1,0:T(8,128)(2,1)S(1)} %shard_map.78.refs_3_.refs_4_.refs_2_.refs_1_, ...), custom_call_target="tpu_custom_call" | custom-call | flops 1024 | bytes 1024 | tf_op jit(solution)/shard_map/pallas_call | solution.py:89
  64.1 3.0 %collective-permute-done.13.refs_4_ = f32[512,256]{1,0:T(8,128)S(1)} collective-permute-done((f32[512,256]{1,0:T(8,128)S(1)}, f32[512,256]{1,0:T(8,128)S(1)}, u32[]{:S(2)}, u32[]{:S(2)}) %collective-permute-start.13) | collective-permute-done | bytes 524320 | tf_op jit(solution)/shard_map/ppermute | solution.py:65
  67.1 1.0 collective-permute-done.11.refs_1_.refs_6_.refs_5_
  68.8 2.7 %collective-permute-start.14 = (f32[256,256]{1,0:T(8,128)S(1)}, f32[256,256]{1,0:T(8,128)S(1)}, u32[]{:S(2)}, u32[]{:S(2)}) collective-permute-start(f32[256,256]{1,0:T(8,128)S(1)} %get-tuple-element.104), channel_id=1, source_target_pairs={{0,4},{1,5},{2,6},{3,7},{4,0},{5,1},{6,2},{7,3},{8,12},{9,13},{10,... | collective-permute-start | bytes 786440 | tf_op jit(solution)/shard_map/ppermute | solution.py:65
  71.5 1.3 collective-permute-start.17
  72.8 0.7 collective-permute-start.16
  73.5 2.5 %shard_map.90 = (f32[512,256]{1,0:T(8,128)S(1)}, f32[512,256]{1,0:T(8,128)S(1)}) custom-call(s32[2]{0:T(128)S(1)} %pad_add_fusion.info_ref.refs_0_, bf16[1024,1024]{1,0:T(8,128)(2,1)S(1)} %get-tuple-element.89.refs_5_.refs_1_, bf16[1024,1024]{1,0:T(8,128)(2,1)S(1)} %get-tuple-element.95.refs_2_, f32[512,256]{1,0:T(8,128)S(1)} %get-tuple-element.87.refs_3_, ...), custom_call_target="tpu_custom_call" | custom-call | flops 1024 | bytes 1024 | tf_op jit(solution)/shard_map/pallas_call | solution.py:89
  76.6 1.0 shard_map.91.refs_3_.refs_13_
  77.6 5.1 %collective-permute-done.14.refs_2_ = f32[256,256]{1,0:T(8,128)S(1)} collective-permute-done((f32[256,256]{1,0:T(8,128)S(1)}, f32[256,256]{1,0:T(8,128)S(1)}, u32[]{:S(2)}, u32[]{:S(2)}) %collective-permute-start.14) | collective-permute-done | bytes 262176 | tf_op jit(solution)/shard_map/ppermute | solution.py:65
  83.4 1.5 collective-permute-done.15.refs_10_
  84.9 3.3 %shard_map.93 = (f32[128,512]{1,0:T(8,128)S(1)}, bf16[256,512]{1,0:T(8,128)(2,1)S(1)}, bf16[256,512]{1,0:T(8,128)(2,1)S(1)}, f32[3,128,256]{2,1,0:T(8,128)S(1)},...) custom-call(s32[2]{0:T(128)S(1)} %pad_add_fusion.info_ref.refs_0_, ...), custom_call_target="tpu_custom_call" | custom-call | flops 1024 | bytes 1024 | tf_op jit(solution)/shard_map/pallas_call | solution.py:89
  88.2 2.4 %shard_map.94 = (f32[512,256]{1,0:T(8,128)S(1)}, f32[512,256]{1,0:T(8,128)S(1)}) custom-call(s32[2]{0:T(128)S(1)} %pad_add_fusion.info_ref.refs_0_, bf16[1024,1024]{1,0:T(8,128)(2,1)S(1)} %get-tuple-element.89.refs_5_.refs_1_, bf16[1024,1024]{1,0:T(8,128)(2,1)S(1)} %get-tuple-element.95.refs_2_, f32[512,256]{1,0:T(8,128)S(1)} %get-tuple-element.90.refs_4_.refs_3_, ...), custom_call_target="tpu_custom_call" | custom-call | flops 1024 | bytes 1024 | tf_op jit(solution)/shard_map/pallas_call | solution.py:89
  90.7 1.5 collective-permute-start.20
  92.2 1.4 collective-permute-start.21
  94.9 3.3 %collective-permute-start.19 = (f32[256,256]{1,0:T(8,128)S(1)}, f32[256,256]{1,0:T(8,128)S(1)}, u32[]{:S(2)}, u32[]{:S(2)}) collective-permute-start(f32[256,256]{1,0:T(8,128)S(1)} %get-tuple-element.121), channel_id=1, source_target_pairs={{0,4},{1,5},{2,6},{3,7},{4,0},{5,1},{6,2},{7,3},{8,12},{9,13},{10,... | collective-permute-start | bytes 786440 | tf_op jit(solution)/shard_map/ppermute | solution.py:65
  98.1 1.0 shard_map.96.refs_14_.refs_15_
  99.1 3.9 %shard_map.97 = (f32[2,128,256]{2,1,0:T(8,128)S(1)}, f32[2,128,256]{2,1,0:T(8,128)S(1)}, f32[2,128,256]{2,1,0:T(8,128)S(1)}, f32[2,128,256]{2,1,0:T(8,128)S(1)}, f32[2,128,512]{2,1,0:T(8,128)S(1)}) custom-call(s32[2]{0:T(128)S(1)} %pad_add_fusion.info_ref.refs_0_, bf16[512,512]{1,0:T(8,128)(2,1)S(1)} %shard_map.78.refs_3_.refs_4_.refs_2_.refs_1_, ...), custom_call_target="tpu_custom_call" | custom-call | flops 1024 | bytes 1024 | tf_op jit(solution)/shard_map/pallas_call | solution.py:89
  103.0 5.1 %collective-permute-done.19.refs_2_ = f32[256,256]{1,0:T(8,128)S(1)} collective-permute-done((f32[256,256]{1,0:T(8,128)S(1)}, f32[256,256]{1,0:T(8,128)S(1)}, u32[]{:S(2)}, u32[]{:S(2)}) %collective-permute-start.19) | collective-permute-done | bytes 262176 | tf_op jit(solution)/shard_map/ppermute | solution.py:65
  108.1 1.4 collective-permute-start.27
  109.5 1.4 collective-permute-start.28
  111.5 1.5 collective-permute-start.29
  113.0 0.7 shard_map.98
  113.8 2.0 %collective-permute-start.26 = (f32[256,256]{1,0:T(8,128)S(1)}, f32[256,256]{1,0:T(8,128)S(1)}, u32[]{:S(2)}, u32[]{:S(2)}) collective-permute-start(f32[256,256]{1,0:T(8,128)S(1)} %get-tuple-element.132), channel_id=1, source_target_pairs={{0,4},{1,5},{2,6},{3,7},{4,0},{5,1},{6,2},{7,3},{8,12},{9,13},{10,... | collective-permute-start | bytes 786440 | tf_op jit(solution)/shard_map/ppermute | solution.py:65
  116.2 1.1 collective-permute-done.27.refs_6_
  117.3 5.4 %collective-permute-done.28.refs_7_ = f32[2,128,256]{2,1,0:T(8,128)S(1)} collective-permute-done((f32[2,128,256]{2,1,0:T(8,128)S(1)}, f32[2,128,256]{2,1,0:T(8,128)S(1)}, u32[]{:S(2)}, u32[]{:S(2)}) %collective-permute-start.28) | collective-permute-done | bytes 262176 | tf_op jit(solution)/shard_map/ppermute | solution.py:65
  122.8 1.8 %collective-permute-done.25.refs_2_ = f32[3,64,256]{2,1,0:T(8,128)S(1)} collective-permute-done((f32[3,64,256]{2,1,0:T(8,128)S(1)}, f32[3,64,256]{2,1,0:T(8,128)S(1)}, u32[]{:S(2)}, u32[]{:S(2)}) %collective-permute-start.25) | collective-permute-done | bytes 196640 | tf_op jit(solution)/shard_map/ppermute | solution.py:65
  124.6 2.1 %collective-permute-done.26.refs_4_ = f32[256,256]{1,0:T(8,128)S(1)} collective-permute-done((f32[256,256]{1,0:T(8,128)S(1)}, f32[256,256]{1,0:T(8,128)S(1)}, u32[]{:S(2)}, u32[]{:S(2)}) %collective-permute-start.26) | collective-permute-done | bytes 262176 | tf_op jit(solution)/shard_map/ppermute | solution.py:65
  127.3 1.7 %collective-permute-start.31 = (f32[3,32,256]{2,1,0:T(8,128)S(1)}, f32[3,32,256]{2,1,0:T(8,128)S(1)}, u32[]{:S(2)}, u32[]{:S(2)}) collective-permute-start(f32[3,32,256]{2,1,0:T(8,128)S(1)} %get-tuple-element.139), channel_id=1, source_target_pairs={{0,4},{1,5},{2,6},{3,7},{4,0},{5,1},{6,2},{7,3},{8,12},{9,13},{10,... | collective-permute-start | bytes 294920 | tf_op jit(solution)/shard_map/ppermute | solution.py:65
  129.0 1.3 collective-permute-start.32
  130.7 2.7 %collective-permute-start.34 = (f32[2,32,256]{2,1,0:T(8,128)S(1)}, f32[2,32,256]{2,1,0:T(8,128)S(1)}, u32[]{:S(2)}, u32[]{:S(2)}) collective-permute-start(f32[2,32,256]{2,1,0:T(8,128)S(1)} %get-tuple-element.143), channel_id=1, source_target_pairs={{0,6},{1,7},{2,4},{3,5},{4,2},{5,3},{6,0},{7,1},{8,14},{9,15},{10,... | collective-permute-start | bytes 196616 | tf_op jit(solution)/shard_map/ppermute | solution.py:65
  133.4 4.7 %collective-permute-done.32.refs_4_ = f32[2,32,256]{2,1,0:T(8,128)S(1)} collective-permute-done((f32[2,32,256]{2,1,0:T(8,128)S(1)}, f32[2,32,256]{2,1,0:T(8,128)S(1)}, u32[]{:S(2)}, u32[]{:S(2)}) %collective-permute-start.32) | collective-permute-done | bytes 65568 | tf_op jit(solution)/shard_map/ppermute | solution.py:65
  139.3 0.9 collective-permute-done.36.refs_4_
  140.7 2.2 %collective-permute-start.39 = (f32[5,16,512]{2,1,0:T(8,128)S(1)}, f32[5,16,512]{2,1,0:T(8,128)S(1)}, u32[]{:S(2)}, u32[]{:S(2)}) collective-permute-start(f32[5,16,512]{2,1,0:T(8,128)S(1)} %shard_map.101.refs_8_.refs_3_), channel_id=1, source_target_pairs={{0,24},{8,16},{16,8},{24,0},{1,25},{9,17},{17,9},{25,1},{2,26},{10... | collective-permute-start | bytes 491528 | tf_op jit(solution)/shard_map/ppermute | solution.py:65
  142.9 0.8 collective-permute-start.38
  144.8 0.8 collective-permute-done.24.refs_5_
  145.8 1.5 shard_map.102.refs_7_
  147.4 1.4 collective-permute-done.39.refs_6_
  148.8 2.9 %collective-permute-done.38.refs_5_ = f32[5,16,512]{2,1,0:T(8,128)S(1)} collective-permute-done((f32[5,16,512]{2,1,0:T(8,128)S(1)}, f32[5,16,512]{2,1,0:T(8,128)S(1)}, u32[]{:S(2)}, u32[]{:S(2)}) %collective-permute-start.38) | collective-permute-done | bytes 163872 | tf_op jit(solution)/shard_map/ppermute | solution.py:65
  151.7 1.1 copy-done
  152.8 1.6 %shard_map.103 = (f32[3,64,512]{2,1,0:T(8,128)}, f32[2,64,512]{2,1,0:T(8,128)}) custom-call(s32[2]{0:T(128)S(1)} %pad_add_fusion.info_ref.refs_0_, f32[3,64,512]{2,1,0:T(8,128)S(1)} %copy-done.1, f32[2,64,512]{2,1,0:T(8,128)S(1)} %get-tuple-element.148.refs_2_, f32[5,16,512]{2,1,0:T(8,128)S(1)} %shard_map.101.refs_8_.refs_3_, ...), custom_call_target="tpu_custom_call" | custom-call | flops 1024 | bytes 1024 | tf_op jit(solution)/shard_map/pallas_call | solution.py:89
  (63 shorter events, 13.9 us)
Async XLA Ops:
  0.6 25.4 %collective-permute-start.5 = (f32[1024,512]{1,0:T(8,128)}, f32[1024,512]{1,0:T(8,128)S(1)}, u32[]{:S(2)}, u32[]{:S(2)}) collective-permute-start(f32[1024,512]{1,0:T(8,128)} %refs_1_.10), channel_id=1, source_target_pairs={{0,1},{1,0},{2,3},{3,2},{4,5},{5,4},{6,7},{7,6},{8,9},{9,8},{10,11... | collective-permute-start | bytes 6291464 | tf_op jit(solution)/shard_map/ppermute | solution.py:65
  1.2 0.7 copy-start.4
  1.9 4.8 %copy-start.3 = (f32[2,64,512]{2,1,0:T(8,128)S(1)}, f32[2,64,512]{2,1,0:T(8,128)}, u32[]{:S(2)}) copy-start(f32[2,64,512]{2,1,0:T(8,128)} %param.7) | copy-start | bytes 786436
  1.9 6.8 %copy-start.5 = (s32[3,8]{1,0:T(4,128)S(1)}, s32[3,8]{1,0:T(4,128)}, u32[]{:S(2)}) copy-start(s32[3,8]{1,0:T(4,128)} %refs_1_.14) | copy-start | bytes 292
  1.9 9.8 %slice-start = ((s8[6291456]{0:T(1024)(128)(4,1)}), s8[4194304]{0:T(1024)(128)(4,1)S(1)}, s32[]{:S(2)}) async-start(s8[6291456]{0:T(1024)(128)(4,1)} %bitcast.3), calls=%async_computation | async-start | bytes 8388608
  4.1 15.1 %collective-permute-start.1 = (f32[512,256]{1,0:T(8,128)S(1)}, f32[512,256]{1,0:T(8,128)S(1)}, u32[]{:S(2)}, u32[]{:S(2)}) collective-permute-start(f32[512,256]{1,0:T(8,128)S(1)} %get-tuple-element.86.refs_7_), channel_id=1, source_target_pairs={{8,0},{24,8},{16,24},{0,16},{9,1},{25,9},{17,25},{1,17},{2,10},{18... | collective-permute-start | bytes 1572872 | tf_op jit(solution)/shard_map/ppermute | solution.py:489
  6.7 14.0 %collective-permute-start = (f32[512,256]{1,0:T(8,128)S(1)}, f32[512,256]{1,0:T(8,128)S(1)}, u32[]{:S(2)}, u32[]{:S(2)}) collective-permute-start(f32[512,256]{1,0:T(8,128)S(1)} %get-tuple-element.77.refs_3_), channel_id=1, source_target_pairs={{0,8},{8,24},{24,16},{16,0},{1,9},{9,25},{25,17},{17,1},{10,2},{2,... | collective-permute-start | bytes 1572872 | tf_op jit(solution)/shard_map/ppermute | solution.py:489
  6.7 5.1 %slice-start.1 = ((s8[6291456]{0:T(1024)(128)(4,1)}), s8[2097152]{0:T(1024)(128)(4,1)S(1)}, s32[]{:S(2)}) async-start(s8[6291456]{0:T(1024)(128)(4,1)} %bitcast.3), calls=%async_computation.1 | async-start | bytes 4194304
  6.7 8.4 %collective-permute-start.2 = (f32[1,2,64,512]{3,2,1,0:T(8,128)S(1)}, f32[1,2,64,512]{3,2,1,0:T(8,128)S(1)}, u32[]{:S(2)}, u32[]{:S(2)}) collective-permute-start(f32[1,2,64,512]{3,2,1,0:T(8,128)S(1)} %bitcast.5), channel_id=1, source_target_pairs={{0,2},{1,3},{2,0},{3,1},{4,6},{5,7},{6,4},{7,5},{8,10},{9,11},{10,... | collective-permute-start | bytes 786440 | tf_op jit(solution)/shard_map/ppermute | solution.py:65
  14.0 12.0 %copy-start.2 = (f32[1024,512]{1,0:T(8,128)S(1)}, f32[1024,512]{1,0:T(8,128)}, u32[]{:S(2)}) copy-start(f32[1024,512]{1,0:T(8,128)} %refs_1_.10) | copy-start | bytes 6291460
  21.4 13.3 %collective-permute-start.4 = (f32[512,256]{1,0:T(8,128)S(1)}, f32[512,256]{1,0:T(8,128)S(1)}, u32[]{:S(2)}, u32[]{:S(2)}) collective-permute-start(f32[512,256]{1,0:T(8,128)S(1)} %get-tuple-element.88.refs_7_), channel_id=1, source_target_pairs={{8,0},{24,8},{16,24},{0,16},{9,1},{25,9},{17,25},{1,17},{2,10},{18... | collective-permute-start | bytes 1572872 | tf_op jit(solution)/shard_map/ppermute | solution.py:489
  22.9 12.9 %collective-permute-start.3 = (f32[512,256]{1,0:T(8,128)S(1)}, f32[512,256]{1,0:T(8,128)S(1)}, u32[]{:S(2)}, u32[]{:S(2)}) collective-permute-start(f32[512,256]{1,0:T(8,128)S(1)} %get-tuple-element.87.refs_3_), channel_id=1, source_target_pairs={{0,8},{8,24},{24,16},{16,0},{1,9},{9,25},{25,17},{17,1},{10,2},{2,... | collective-permute-start | bytes 1572872 | tf_op jit(solution)/shard_map/ppermute | solution.py:489
  23.5 24.8 %collective-permute-start.8 = (f32[2,2,64,512]{3,2,1,0:T(8,128)S(1)}, f32[2,2,64,512]{3,2,1,0:T(8,128)S(1)}, u32[]{:S(2)}, u32[]{:S(2)}) collective-permute-start(f32[2,2,64,512]{3,2,1,0:T(8,128)S(1)} %get-tuple-element.92.refs_3_), channel_id=1, source_target_pairs={{0,4},{1,5},{2,6},{3,7},{4,0},{5,1},{6,2},{7,3},{8,12},{9,13},{10,... | collective-permute-start | bytes 1572872 | tf_op jit(solution)/shard_map/ppermute | solution.py:65
  36.5 12.1 %collective-permute-start.7 = (f32[512,256]{1,0:T(8,128)S(1)}, f32[512,256]{1,0:T(8,128)S(1)}, u32[]{:S(2)}, u32[]{:S(2)}) collective-permute-start(f32[512,256]{1,0:T(8,128)S(1)} %get-tuple-element.91.refs_7_), channel_id=1, source_target_pairs={{8,0},{24,8},{16,24},{0,16},{9,1},{25,9},{17,25},{1,17},{2,10},{18... | collective-permute-start | bytes 1572872 | tf_op jit(solution)/shard_map/ppermute | solution.py:489
  37.2 11.8 %collective-permute-start.6 = (f32[512,256]{1,0:T(8,128)S(1)}, f32[512,256]{1,0:T(8,128)S(1)}, u32[]{:S(2)}, u32[]{:S(2)}) collective-permute-start(f32[512,256]{1,0:T(8,128)S(1)} %get-tuple-element.90.refs_4_.refs_3_), channel_id=1, source_target_pairs={{0,8},{8,24},{24,16},{16,0},{1,9},{9,25},{25,17},{17,1},{10,2},{2,... | collective-permute-start | bytes 1572872 | tf_op jit(solution)/shard_map/ppermute | solution.py:489
  49.7 6.1 %collective-permute-start.9 = (f32[4,2,64,512]{3,2,1,0:T(8,128)S(1)}, f32[4,2,64,512]{3,2,1,0:T(8,128)S(1)}, u32[]{:S(2)}, u32[]{:S(2)}) collective-permute-start(f32[4,2,64,512]{3,2,1,0:T(8,128)S(1)} %get-tuple-element.94.refs_1_), channel_id=1, source_target_pairs={{0,1},{1,0},{2,3},{3,2},{4,5},{5,4},{6,7},{7,6},{8,9},{9,8},{10,11... | collective-permute-start | bytes 3145736 | tf_op jit(solution)/shard_map/ppermute | solution.py:65
  49.8 14.3 %collective-permute-start.12 = (f32[512,256]{1,0:T(8,128)S(1)}, f32[512,256]{1,0:T(8,128)S(1)}, u32[]{:S(2)}, u32[]{:S(2)}) collective-permute-start(f32[512,256]{1,0:T(8,128)S(1)} %get-tuple-element.100), channel_id=1, source_target_pairs={{8,0},{24,8},{16,24},{0,16},{9,1},{25,9},{17,25},{1,17},{2,10},{18... | collective-permute-start | bytes 1572872 | tf_op jit(solution)/shard_map/ppermute | solution.py:489
  50.6 5.1 %copy-start.1 = (f32[3,64,512]{2,1,0:T(8,128)S(1)}, f32[3,64,512]{2,1,0:T(8,128)}, u32[]{:S(2)}) copy-start(f32[3,64,512]{2,1,0:T(8,128)} %refs_1_.15) | copy-start | bytes 1179652
  53.0 14.1 %collective-permute-start.13 = (f32[512,256]{1,0:T(8,128)S(1)}, f32[512,256]{1,0:T(8,128)S(1)}, u32[]{:S(2)}, u32[]{:S(2)}) collective-permute-start(f32[512,256]{1,0:T(8,128)S(1)} %get-tuple-element.101), channel_id=1, source_target_pairs={{0,2},{1,3},{2,0},{3,1},{4,6},{5,7},{6,4},{7,5},{8,10},{9,11},{10,... | collective-permute-start | bytes 1572872 | tf_op jit(solution)/shard_map/ppermute | solution.py:65
  54.4 13.7 %collective-permute-start.11 = (f32[512,256]{1,0:T(8,128)S(1)}, f32[512,256]{1,0:T(8,128)S(1)}, u32[]{:S(2)}, u32[]{:S(2)}) collective-permute-start(f32[512,256]{1,0:T(8,128)S(1)} %get-tuple-element.96.refs_11_), channel_id=1, source_target_pairs={{0,8},{8,24},{24,16},{16,0},{1,9},{9,25},{25,17},{17,1},{10,2},{2,... | collective-permute-start | bytes 1572872 | tf_op jit(solution)/shard_map/ppermute | solution.py:489
  55.7 1.4 collective-permute-start.10
  68.8 13.9 %collective-permute-start.14 = (f32[256,256]{1,0:T(8,128)S(1)}, f32[256,256]{1,0:T(8,128)S(1)}, u32[]{:S(2)}, u32[]{:S(2)}) collective-permute-start(f32[256,256]{1,0:T(8,128)S(1)} %get-tuple-element.104), channel_id=1, source_target_pairs={{0,4},{1,5},{2,6},{3,7},{4,0},{5,1},{6,2},{7,3},{8,12},{9,13},{10,... | collective-permute-start | bytes 786440 | tf_op jit(solution)/shard_map/ppermute | solution.py:65
  71.5 16.7 %collective-permute-start.17 = (f32[512,256]{1,0:T(8,128)S(1)}, f32[512,256]{1,0:T(8,128)S(1)}, u32[]{:S(2)}, u32[]{:S(2)}) collective-permute-start(f32[512,256]{1,0:T(8,128)S(1)} %get-tuple-element.116), channel_id=1, source_target_pairs={{8,0},{24,8},{16,24},{0,16},{9,1},{25,9},{17,25},{1,17},{2,10},{18... | collective-permute-start | bytes 1572872 | tf_op jit(solution)/shard_map/ppermute | solution.py:489
  72.8 15.4 %collective-permute-start.16 = (f32[512,256]{1,0:T(8,128)S(1)}, f32[512,256]{1,0:T(8,128)S(1)}, u32[]{:S(2)}, u32[]{:S(2)}) collective-permute-start(f32[512,256]{1,0:T(8,128)S(1)} %get-tuple-element.106.refs_11_), channel_id=1, source_target_pairs={{0,8},{8,24},{24,16},{16,0},{1,9},{9,25},{25,17},{17,1},{10,2},{2,... | collective-permute-start | bytes 1572872 | tf_op jit(solution)/shard_map/ppermute | solution.py:489
  76.0 18.3 %collective-permute-start.18 = (f32[512,256]{1,0:T(8,128)S(1)}, f32[512,256]{1,0:T(8,128)S(1)}, u32[]{:S(2)}, u32[]{:S(2)}) collective-permute-start(f32[512,256]{1,0:T(8,128)S(1)} %get-tuple-element.108.refs_3_), channel_id=1, source_target_pairs={{0,2},{1,3},{2,0},{3,1},{4,6},{5,7},{6,4},{7,5},{8,10},{9,11},{10,... | collective-permute-start | bytes 1572872 | tf_op jit(solution)/shard_map/ppermute | solution.py:65
  83.3 1.6 %collective-permute-start.15 = (f32[256,256]{1,0:T(8,128)S(1)}, f32[256,256]{1,0:T(8,128)S(1)}, u32[]{:S(2)}, u32[]{:S(2)}) collective-permute-start(f32[256,256]{1,0:T(8,128)S(1)} %shard_map.92.refs_9_.refs_11_), channel_id=1, source_target_pairs={{0,1},{1,0},{2,3},{3,2},{4,5},{5,4},{6,7},{7,6},{8,9},{9,8},{10,11... | collective-permute-start | bytes 786440 | tf_op jit(solution)/shard_map/ppermute | solution.py:65
  90.6 22.4 %collective-permute-start.23 = (f32[512,256]{1,0:T(8,128)S(1)}, f32[512,256]{1,0:T(8,128)S(1)}, u32[]{:S(2)}, u32[]{:S(2)}) collective-permute-start(f32[512,256]{1,0:T(8,128)S(1)} %get-tuple-element.118.refs_3_), channel_id=1, source_target_pairs={{0,2},{1,3},{2,0},{3,1},{4,6},{5,7},{6,4},{7,5},{8,10},{9,11},{10,... | collective-permute-start | bytes 1572872 | tf_op jit(solution)/shard_map/ppermute | solution.py:65
  90.7 18.8 %collective-permute-start.20 = (f32[3,128,256]{2,1,0:T(8,128)S(1)}, f32[3,128,256]{2,1,0:T(8,128)S(1)}, u32[]{:S(2)}, u32[]{:S(2)}) collective-permute-start(f32[3,128,256]{2,1,0:T(8,128)S(1)} %get-tuple-element.123), channel_id=1, source_target_pairs={{0,8},{8,0},{16,24},{24,16},{1,9},{9,1},{17,25},{25,17},{2,10},{10... | collective-permute-start | bytes 1179656 | tf_op jit(solution)/shard_map/ppermute | solution.py:65
  92.2 19.3 %collective-permute-start.21 = (f32[3,128,256]{2,1,0:T(8,128)S(1)}, f32[3,128,256]{2,1,0:T(8,128)S(1)}, u32[]{:S(2)}, u32[]{:S(2)}) collective-permute-start(f32[3,128,256]{2,1,0:T(8,128)S(1)} %get-tuple-element.124), channel_id=1, source_target_pairs={{0,16},{8,24},{16,0},{24,8},{1,17},{9,25},{17,1},{25,9},{2,18},{10... | collective-permute-start | bytes 1179656 | tf_op jit(solution)/shard_map/ppermute | solution.py:65
  93.6 19.4 %collective-permute-start.22 = (f32[3,128,256]{2,1,0:T(8,128)S(1)}, f32[3,128,256]{2,1,0:T(8,128)S(1)}, u32[]{:S(2)}, u32[]{:S(2)}) collective-permute-start(f32[3,128,256]{2,1,0:T(8,128)S(1)} %get-tuple-element.125), channel_id=1, source_target_pairs={{0,24},{8,16},{16,8},{24,0},{1,25},{9,17},{17,9},{25,1},{2,26},{10... | collective-permute-start | bytes 1179656 | tf_op jit(solution)/shard_map/ppermute | solution.py:65
  94.9 13.2 %collective-permute-start.19 = (f32[256,256]{1,0:T(8,128)S(1)}, f32[256,256]{1,0:T(8,128)S(1)}, u32[]{:S(2)}, u32[]{:S(2)}) collective-permute-start(f32[256,256]{1,0:T(8,128)S(1)} %get-tuple-element.121), channel_id=1, source_target_pairs={{0,4},{1,5},{2,6},{3,7},{4,0},{5,1},{6,2},{7,3},{8,12},{9,13},{10,... | collective-permute-start | bytes 786440 | tf_op jit(solution)/shard_map/ppermute | solution.py:65
  108.1 9.2 %collective-permute-start.27 = (f32[2,128,256]{2,1,0:T(8,128)S(1)}, f32[2,128,256]{2,1,0:T(8,128)S(1)}, u32[]{:S(2)}, u32[]{:S(2)}) collective-permute-start(f32[2,128,256]{2,1,0:T(8,128)S(1)} %get-tuple-element.133), channel_id=1, source_target_pairs={{0,8},{8,0},{16,24},{24,16},{1,9},{9,1},{17,25},{25,17},{2,10},{10... | collective-permute-start | bytes 786440 | tf_op jit(solution)/shard_map/ppermute | solution.py:65
  109.5 13.2 %collective-permute-start.28 = (f32[2,128,256]{2,1,0:T(8,128)S(1)}, f32[2,128,256]{2,1,0:T(8,128)S(1)}, u32[]{:S(2)}, u32[]{:S(2)}) collective-permute-start(f32[2,128,256]{2,1,0:T(8,128)S(1)} %get-tuple-element.134), channel_id=1, source_target_pairs={{0,16},{8,24},{16,0},{24,8},{1,17},{9,25},{17,1},{25,9},{2,18},{10... | collective-permute-start | bytes 786440 | tf_op jit(solution)/shard_map/ppermute | solution.py:65
  111.5 11.2 %collective-permute-start.29 = (f32[2,128,256]{2,1,0:T(8,128)S(1)}, f32[2,128,256]{2,1,0:T(8,128)S(1)}, u32[]{:S(2)}, u32[]{:S(2)}) collective-permute-start(f32[2,128,256]{2,1,0:T(8,128)S(1)} %get-tuple-element.135), channel_id=1, source_target_pairs={{0,24},{8,16},{16,8},{24,0},{1,25},{9,17},{17,9},{25,1},{2,26},{10... | collective-permute-start | bytes 786440 | tf_op jit(solution)/shard_map/ppermute | solution.py:65
  113.8 12.9 %collective-permute-start.26 = (f32[256,256]{1,0:T(8,128)S(1)}, f32[256,256]{1,0:T(8,128)S(1)}, u32[]{:S(2)}, u32[]{:S(2)}) collective-permute-start(f32[256,256]{1,0:T(8,128)S(1)} %get-tuple-element.132), channel_id=1, source_target_pairs={{0,4},{1,5},{2,6},{3,7},{4,0},{5,1},{6,2},{7,3},{8,12},{9,13},{10,... | collective-permute-start | bytes 786440 | tf_op jit(solution)/shard_map/ppermute | solution.py:65
  115.8 8.8 %collective-permute-start.25 = (f32[3,64,256]{2,1,0:T(8,128)S(1)}, f32[3,64,256]{2,1,0:T(8,128)S(1)}, u32[]{:S(2)}, u32[]{:S(2)}) collective-permute-start(f32[3,64,256]{2,1,0:T(8,128)S(1)} %get-tuple-element.130), channel_id=1, source_target_pairs={{0,2},{1,3},{2,0},{3,1},{4,6},{5,7},{6,4},{7,5},{8,10},{9,11},{10,... | collective-permute-start | bytes 589832 | tf_op jit(solution)/shard_map/ppermute | solution.py:65
  127.3 10.8 %collective-permute-start.31 = (f32[3,32,256]{2,1,0:T(8,128)S(1)}, f32[3,32,256]{2,1,0:T(8,128)S(1)}, u32[]{:S(2)}, u32[]{:S(2)}) collective-permute-start(f32[3,32,256]{2,1,0:T(8,128)S(1)} %get-tuple-element.139), channel_id=1, source_target_pairs={{0,4},{1,5},{2,6},{3,7},{4,0},{5,1},{6,2},{7,3},{8,12},{9,13},{10,... | collective-permute-start | bytes 294920 | tf_op jit(solution)/shard_map/ppermute | solution.py:65
  129.0 9.1 %collective-permute-start.32 = (f32[2,32,256]{2,1,0:T(8,128)S(1)}, f32[2,32,256]{2,1,0:T(8,128)S(1)}, u32[]{:S(2)}, u32[]{:S(2)}) collective-permute-start(f32[2,32,256]{2,1,0:T(8,128)S(1)} %get-tuple-element.141), channel_id=1, source_target_pairs={{0,4},{1,5},{2,6},{3,7},{4,0},{5,1},{6,2},{7,3},{8,12},{9,13},{10,... | collective-permute-start | bytes 196616 | tf_op jit(solution)/shard_map/ppermute | solution.py:65
  130.3 7.8 %collective-permute-start.33 = (f32[2,32,256]{2,1,0:T(8,128)S(1)}, f32[2,32,256]{2,1,0:T(8,128)S(1)}, u32[]{:S(2)}, u32[]{:S(2)}) collective-permute-start(f32[2,32,256]{2,1,0:T(8,128)S(1)} %get-tuple-element.142), channel_id=1, source_target_pairs={{0,2},{1,3},{2,0},{3,1},{4,6},{5,7},{6,4},{7,5},{8,10},{9,11},{10,... | collective-permute-start | bytes 196616 | tf_op jit(solution)/shard_map/ppermute | solution.py:65
  130.7 7.4 %collective-permute-start.34 = (f32[2,32,256]{2,1,0:T(8,128)S(1)}, f32[2,32,256]{2,1,0:T(8,128)S(1)}, u32[]{:S(2)}, u32[]{:S(2)}) collective-permute-start(f32[2,32,256]{2,1,0:T(8,128)S(1)} %get-tuple-element.143), channel_id=1, source_target_pairs={{0,6},{1,7},{2,4},{3,5},{4,2},{5,3},{6,0},{7,1},{8,14},{9,15},{10,... | collective-permute-start | bytes 196616 | tf_op jit(solution)/shard_map/ppermute | solution.py:65
  138.7 1.4 collective-permute-start.35
  138.8 1.4 collective-permute-start.36
  140.7 8.0 %collective-permute-start.39 = (f32[5,16,512]{2,1,0:T(8,128)S(1)}, f32[5,16,512]{2,1,0:T(8,128)S(1)}, u32[]{:S(2)}, u32[]{:S(2)}) collective-permute-start(f32[5,16,512]{2,1,0:T(8,128)S(1)} %shard_map.101.refs_8_.refs_3_), channel_id=1, source_target_pairs={{0,24},{8,16},{16,8},{24,0},{1,25},{9,17},{17,9},{25,1},{2,26},{10... | collective-permute-start | bytes 491528 | tf_op jit(solution)/shard_map/ppermute | solution.py:65
  142.9 8.8 %collective-permute-start.38 = (f32[5,16,512]{2,1,0:T(8,128)S(1)}, f32[5,16,512]{2,1,0:T(8,128)S(1)}, u32[]{:S(2)}, u32[]{:S(2)}) collective-permute-start(f32[5,16,512]{2,1,0:T(8,128)S(1)} %shard_map.101.refs_8_.refs_3_), channel_id=1, source_target_pairs={{0,16},{8,24},{16,0},{24,8},{1,17},{9,25},{17,1},{25,9},{2,18},{10... | collective-permute-start | bytes 491528 | tf_op jit(solution)/shard_map/ppermute | solution.py:65
  143.7 8.0 %collective-permute-start.37 = (f32[5,16,512]{2,1,0:T(8,128)S(1)}, f32[5,16,512]{2,1,0:T(8,128)S(1)}, u32[]{:S(2)}, u32[]{:S(2)}) collective-permute-start(f32[5,16,512]{2,1,0:T(8,128)S(1)} %shard_map.101.refs_8_.refs_3_), channel_id=1, source_target_pairs={{0,8},{8,0},{16,24},{24,16},{1,9},{9,1},{17,25},{25,17},{2,10},{10... | collective-permute-start | bytes 491528 | tf_op jit(solution)/shard_map/ppermute | solution.py:65
  144.3 1.3 collective-permute-start.24
  144.3 1.5 collective-permute-start.30
  151.7 1.1 copy-start

commit v15 on v14

--- a/solution.py
+++ b/solution.py
@@ -98,12 +98,10 @@
     return list(results)
 
 
-def cut_kernel(ratio, cuts, members, info_ref, listed_ref, factors_ref, *refs):
+def cut_kernel(ratio, cuts, members, info_ref, factors_ref, *refs):
     *outs, sems = refs
     size, unit = outs[0].shape
-    width = factors_ref.shape[2]
-    column = info_ref[1]
-    pair = (column % ratio) // 2
+    pair = (info_ref[1] % ratio) // 2
     copies = []
     for at, out_ref in enumerate(outs):
         member, cut, way = members[at // (2 * cuts)], at // 2 % cuts, at % 2
@@ -112,11 +110,8 @@
         ]
         copies.append(pltpu.make_async_copy(source, out_ref, sems.at[at]))
         copies[-1].start()
-    for at, out_ref in enumerate(outs):
-        copies[at].wait()
-        owner = column - core_of(info_ref) + at % 2
-        weight = listed_ref[members[at // (2 * cuts)], owner * size // width]
-        out_ref[...] = out_ref[...] * weight.astype(F32)
+    for copy in copies:
+        copy.wait()
 
 
 def chooser_kernel(rows, columns, info_ref, out_ref):
@@ -242,7 +237,7 @@
         corner_ref[c] = share * corner
 
 
-def unit_kernel(count, ratio, cuts, info_ref, high_ref, low_ref, *refs):
+def unit_kernel(count, ratio, cuts, member, info_ref, listed_ref, high_ref, low_ref, *refs):
     keep_ref, send_ref = refs[-2:]
     middle = keep_ref.shape[0]
     place = info_ref[0] ^ (info_ref[1] // ratio)
@@ -259,7 +254,9 @@
             value = candidates[0][...]
             for at in range(1, count):
                 value = jnp.where(places[way] == at, candidates[at][...], value)
-            chosen.append(value)
+            owner = info_ref[1] - core_of(info_ref) + way
+            weight = listed_ref[member, owner * value.shape[0] // (2 * cuts * value.shape[1])]
+            chosen.append(value * weight.astype(F32))
         parts.append(jnp.concatenate(chosen))
     right = split(jnp.concatenate(parts, axis=1))
     send_ref[...] = product((high_ref[middle:], low_ref[middle:]), right)
@@ -455,8 +452,8 @@
         flat = run(
             functools.partial(cut_kernel, ratio, cuts, chosen),
             [shape(cols_here, unit)] * count,
-            [info, listed, factor_cols],
-            smem=2, hbm=1, vmem=48,
+            [info, factor_cols],
+            smem=1, hbm=1, vmem=48,
             scratch=[pltpu.SemaphoreType.DMA((count,))],
         )
         return [flat[at : at + 2] for at in range(0, count, 2)]
@@ -574,10 +571,10 @@
                 candidates += [received[at + hop][way] for hop in range(row_count - 1)]
         size = rows_here // 2
         keep, send = heavy(
-            functools.partial(unit_kernel, row_count, ratio, cuts),
+            functools.partial(unit_kernel, row_count, ratio, cuts, member),
             [shape(size, half)] * 2,
-            [info, *held["region"], *candidates],
-            smem=1, vmem=16,
+            [info, listed, *held["region"], *candidates],
+            smem=2, vmem=16,
         )
         first = (keep, send)
         for bit in range(1, col_bits):
@@ -598,6 +595,8 @@
         if member == 0:
             held["last", 0] = [keep, arrived]
             return
+        if final:
+            yield WAIT
         mine, theirs = yield (part_step, [keep, arrived], [shape(size // 2, half)] * 2)
         held["sum", member] = [mine, swap(theirs, "col", col_count, 1)]
 

time: 155 us -> 154 us (level)
  starting transfers between devices: 45.3 us -> 46.9 us
    ppermute x30, starting transfers between devices: 34.3 us -> 35.9 us  [swap(): lax.ppermute(value, axis, [(place, place ^ change) for place in range(siz...]
  transfers between devices with their start and end apart: 40 -> 40, of which waited for: 26 -> 24; matrix products, arithmetic and copies ran while one was open for 0% -> 0% of each run, Pallas kernels for 26% -> 26%
where the time goes in v15:
time: 154 us
  waiting for transfers between devices  60.5 us (39%)
  starting transfers between devices  46.9 us (30%)
  Pallas kernels  44.5 us (29%)
    ppermute x30, waiting for transfers between devices, swap(): lax.ppermute(value, axis, [(place, place ^ change) for place in range(siz...  44.9 us
    pallas_call x28, Pallas kernels, call(): pl.pallas_call(inner, out_shape=outs, in_specs=[pl.BlockSpec(memory_space...  44.5 us
    ppermute x30, starting transfers between devices, swap(): lax.ppermute(value, axis, [(place, place ^ change) for place in range(siz...  35.9 us
    ppermute x10, waiting for transfers between devices, ring_flow(): lax.ppermute(moving[way], AXES, rings[way])  15.6 us
    ppermute x10, starting transfers between devices, ring_flow(): lax.ppermute(moving[way], AXES, rings[way])  11 us
  transfers between devices with their start and end apart: 40, of which 24 were waited for; matrix products, arithmetic and copies ran while one was open for 0% of the time, Pallas kernels for 26%

profile of v15, /device:TPU:0, one launch (start us, length us, event | category | flops | bytes accessed | tf_op | source)
XLA Modules:
  0.0 154.1 jit_solution(6697418651588177591)
XLA Ops:
  1.2 2.0 %shard_map.76 = (f32[512,256]{1,0:T(8,128)S(1)}, f32[512,256]{1,0:T(8,128)S(1)}) custom-call(s32[2]{0:T(128)S(1)} %pad_add_fusion.info_ref.refs_0_, f32[3,1024,512]{2,1,0:T(8,128)} %refs_2_.7), custom_call_target="tpu_custom_call" | custom-call | flops 1024 | bytes 1024 | tf_op jit(solution)/shard_map/pallas_call | solution.py:89
  3.3 2.6 %collective-permute-start.1 = (f32[512,256]{1,0:T(8,128)S(1)}, f32[512,256]{1,0:T(8,128)S(1)}, u32[]{:S(2)}, u32[]{:S(2)}) collective-permute-start(f32[512,256]{1,0:T(8,128)S(1)} %get-tuple-element.86.refs_8_), channel_id=1, source_target_pairs={{8,0},{24,8},{16,24},{0,16},{9,1},{25,9},{17,25},{1,17},{2,10},{18... | collective-permute-start | bytes 1572872 | tf_op jit(solution)/shard_map/ppermute | solution.py:486
  5.9 2.0 %collective-permute-start.2 = (f32[1,2,64,512]{3,2,1,0:T(8,128)S(1)}, f32[1,2,64,512]{3,2,1,0:T(8,128)S(1)}, u32[]{:S(2)}, u32[]{:S(2)}) collective-permute-start(f32[1,2,64,512]{3,2,1,0:T(8,128)S(1)} %bitcast.5), channel_id=1, source_target_pairs={{0,2},{1,3},{2,0},{3,1},{4,6},{5,7},{6,4},{7,5},{8,10},{9,11},{10,... | collective-permute-start | bytes 786440 | tf_op jit(solution)/shard_map/ppermute | solution.py:65
  8.0 2.1 %shard_map.77 = (f32[512,256]{1,0:T(8,128)S(1)}, f32[512,256]{1,0:T(8,128)S(1)}, f32[512,256]{1,0:T(8,128)S(1)}, f32[512,256]{1,0:T(8,128)S(1)}) custom-call(s32[2]{0:T(128)S(1)} %pad_add_fusion.info_ref.refs_0_, f32[3,1024,512]{2,1,0:T(8,128)} %refs_2_.7, f32[512,256]{1,0:T(8,128)S(1)} %get-tuple-element.77.refs_2_.refs_4_), custom_call_target="tpu_custom_call" | custom-call | flops 1024 | bytes 1024 | tf_op jit(solution)/shard_map/pallas_call | solution.py:89
  10.1 0.8 shard_map.78.refs_3_.refs_4_.refs_2_.refs_1_
  10.9 2.2 %shard_map.79 = (bf16[3,256,512]{2,1,0:T(8,128)(2,1)S(1)}, bf16[3,256,512]{2,1,0:T(8,128)(2,1)S(1)}, bf16[3,512,256]{2,1,0:T(8,128)(2,1)S(1)}, bf16[3,512,256]{2,1,0:T(8,128)(2,1)S(1)}) custom-call(s32[2]{0:T(128)S(1)} %pad_add_fusion.info_ref.refs_0_, s32[3,8]{1,0:T(4,128)S(1)} %copy-done.4, f32[3,1024,512]{2,1,0:T(8,128)S(1)} %bitcast.4, ...), custom_call_target="tpu_custom_call" | custom-call | flops 1024 | bytes 1024 | tf_op jit(solution)/shard_map/pallas_call | solution.py:89
  13.2 1.2 collective-permute-done.2.refs_6_
  14.4 4.0 %collective-permute-done.1.refs_4_.refs_9_ = f32[512,256]{1,0:T(8,128)S(1)} collective-permute-done((f32[512,256]{1,0:T(8,128)S(1)}, f32[512,256]{1,0:T(8,128)S(1)}, u32[]{:S(2)}, u32[]{:S(2)}) %collective-permute-start.1) | collective-permute-done | bytes 524320 | tf_op jit(solution)/shard_map/ppermute | solution.py:486
  18.4 1.5 collective-permute-done.refs_3_.refs_5_
  19.9 0.7 shard_map.80
  20.6 1.5 %collective-permute-start.4 = (f32[512,256]{1,0:T(8,128)S(1)}, f32[512,256]{1,0:T(8,128)S(1)}, u32[]{:S(2)}, u32[]{:S(2)}) collective-permute-start(f32[512,256]{1,0:T(8,128)S(1)} %get-tuple-element.88.refs_8_), channel_id=1, source_target_pairs={{8,0},{24,8},{16,24},{0,16},{9,1},{25,9},{17,25},{1,17},{2,10},{18... | collective-permute-start | bytes 1572872 | tf_op jit(solution)/shard_map/ppermute | solution.py:486
  22.7 2.6 %collective-permute-start.8 = (f32[2,2,64,512]{3,2,1,0:T(8,128)S(1)}, f32[2,2,64,512]{3,2,1,0:T(8,128)S(1)}, u32[]{:S(2)}, u32[]{:S(2)}) collective-permute-start(f32[2,2,64,512]{3,2,1,0:T(8,128)S(1)} %get-tuple-element.92.refs_3_), channel_id=1, source_target_pairs={{0,4},{1,5},{2,6},{3,7},{4,0},{5,1},{6,2},{7,3},{8,12},{9,13},{10,... | collective-permute-start | bytes 1572872 | tf_op jit(solution)/shard_map/ppermute | solution.py:65
  25.2 1.7 %shard_map.81 = (bf16[1024,1024]{1,0:T(8,128)(2,1)S(1)}, bf16[1024,1024]{1,0:T(8,128)(2,1)S(1)}) custom-call(s32[2]{0:T(128)S(1)} %pad_add_fusion.info_ref.refs_0_, f32[1024,512]{1,0:T(8,128)S(1)} %copy-done.2, f32[1024,512]{1,0:T(8,128)S(1)} %collective-permute-done.5.refs_2_, f32[512,256]{1,0:T(8,128)S(1)} %get-tuple-element.87.refs_3_.refs_4_), custom_call_target="tpu_custom_call" | custom-call | flops 1024 | bytes 1024 | tf_op jit(solution)/shard_map/pallas_call | solution.py:89
  26.9 6.9 %collective-permute-done.4.refs_4_.refs_10_.refs_9_ = f32[512,256]{1,0:T(8,128)S(1)} collective-permute-done((f32[512,256]{1,0:T(8,128)S(1)}, f32[512,256]{1,0:T(8,128)S(1)}, u32[]{:S(2)}, u32[]{:S(2)}) %collective-permute-start.4) | collective-permute-done | bytes 524320 | tf_op jit(solution)/shard_map/ppermute | solution.py:486
  33.9 1.2 collective-permute-done.3.refs_3_.refs_6_.refs_5_
  36.4 1.4 collective-permute-start.6
  37.8 2.2 %shard_map.83 = (bf16[512,1024]{1,0:T(8,128)(2,1)S(1)}, bf16[512,1024]{1,0:T(8,128)(2,1)S(1)}) custom-call(s32[2]{0:T(128)S(1)} %pad_add_fusion.info_ref.refs_0_, s32[3,8]{1,0:T(4,128)S(1)} %copy-done.4, f32[3,1024,512]{2,1,0:T(8,128)S(1)} %bitcast.4, bf16[512,512]{1,0:T(8,128)(2,1)S(1)} %shard_map.78.refs_3_.refs_4_.refs_2_.refs_1_, ...), custom_call_target="tpu_custom_call" | custom-call | flops 1024 | bytes 1024 | tf_op jit(solution)/shard_map/pallas_call | solution.py:89
  40.0 7.4 %collective-permute-done.8.refs_4_ = f32[2,2,64,512]{3,2,1,0:T(8,128)S(1)} collective-permute-done((f32[2,2,64,512]{3,2,1,0:T(8,128)S(1)}, f32[2,2,64,512]{3,2,1,0:T(8,128)S(1)}, u32[]{:S(2)}, u32[]{:S(2)}) %collective-permute-start.8) | collective-permute-done | bytes 524320 | tf_op jit(solution)/shard_map/ppermute | solution.py:65
  48.2 0.7 shard_map.84
  49.0 0.8 collective-permute-start.12
  49.8 2.5 %shard_map.85 = (f32[512,256]{1,0:T(8,128)S(1)}, f32[512,256]{1,0:T(8,128)S(1)}) custom-call(s32[2]{0:T(128)S(1)} %pad_add_fusion.info_ref.refs_0_, s32[3,8]{1,0:T(4,128)S(1)} %copy-done.4, bf16[1024,1024]{1,0:T(8,128)(2,1)S(1)} %get-tuple-element.89.refs_5_.refs_2_, bf16[1024,1024]{1,0:T(8,128)(2,1)S(1)} %get-tuple-element.95.refs_3_, ...), custom_call_target="tpu_custom_call" | custom-call | flops 1024 | bytes 1024 | tf_op jit(solution)/shard_map/pallas_call | solution.py:89
  52.3 1.4 collective-permute-start.13
  53.7 1.3 collective-permute-start.11
  55.1 0.7 shard_map.86.refs_1_.refs_7_
  56.4 4.5 %shard_map.87 = (bf16[2,512,512]{2,1,0:T(8,128)(2,1)S(1)}, bf16[2,512,512]{2,1,0:T(8,128)(2,1)S(1)}, bf16[2,512,256]{2,1,0:T(8,128)(2,1)S(1)}, bf16[2,512,256]{2...) custom-call(s32[2]{0:T(128)S(1)} %pad_add_fusion.info_ref.refs_0_, ...), custom_call_target="tpu_custom_call" | custom-call | flops 1024 | bytes 1024 | tf_op jit(solution)/shard_map/pallas_call | solution.py:89
  61.0 2.2 %shard_map.88 = (bf16[512,1024]{1,0:T(8,128)(2,1)S(1)}, bf16[512,1024]{1,0:T(8,128)(2,1)S(1)}) custom-call(s32[2]{0:T(128)S(1)} %pad_add_fusion.info_ref.refs_0_, s32[3,8]{1,0:T(4,128)S(1)} %copy-done.4, f32[3,1024,512]{2,1,0:T(8,128)S(1)} %bitcast.4, bf16[512,512]{1,0:T(8,128)(2,1)S(1)} %shard_map.78.refs_3_.refs_4_.refs_2_.refs_1_, ...), custom_call_target="tpu_custom_call" | custom-call | flops 1024 | bytes 1024 | tf_op jit(solution)/shard_map/pallas_call | solution.py:89
  63.3 3.1 %collective-permute-done.13.refs_4_ = f32[512,256]{1,0:T(8,128)S(1)} collective-permute-done((f32[512,256]{1,0:T(8,128)S(1)}, f32[512,256]{1,0:T(8,128)S(1)}, u32[]{:S(2)}, u32[]{:S(2)}) %collective-permute-start.13) | collective-permute-done | bytes 524320 | tf_op jit(solution)/shard_map/ppermute | solution.py:65
  66.4 1.0 collective-permute-done.11.refs_1_.refs_7_.refs_6_
  68.1 2.7 %collective-permute-start.14 = (f32[256,256]{1,0:T(8,128)S(1)}, f32[256,256]{1,0:T(8,128)S(1)}, u32[]{:S(2)}, u32[]{:S(2)}) collective-permute-start(f32[256,256]{1,0:T(8,128)S(1)} %get-tuple-element.104), channel_id=1, source_target_pairs={{0,4},{1,5},{2,6},{3,7},{4,0},{5,1},{6,2},{7,3},{8,12},{9,13},{10,... | collective-permute-start | bytes 786440 | tf_op jit(solution)/shard_map/ppermute | solution.py:65
  70.8 1.3 collective-permute-start.17
  72.1 0.7 collective-permute-start.16
  72.8 2.5 %shard_map.90 = (f32[512,256]{1,0:T(8,128)S(1)}, f32[512,256]{1,0:T(8,128)S(1)}) custom-call(s32[2]{0:T(128)S(1)} %pad_add_fusion.info_ref.refs_0_, s32[3,8]{1,0:T(4,128)S(1)} %copy-done.4, bf16[1024,1024]{1,0:T(8,128)(2,1)S(1)} %get-tuple-element.89.refs_5_.refs_2_, bf16[1024,1024]{1,0:T(8,128)(2,1)S(1)} %get-tuple-element.95.refs_3_, ...), custom_call_target="tpu_custom_call" | custom-call | flops 1024 | bytes 1024 | tf_op jit(solution)/shard_map/pallas_call | solution.py:89
  75.8 1.0 shard_map.91.refs_3_.refs_13_
  76.9 5.1 %collective-permute-done.14.refs_2_ = f32[256,256]{1,0:T(8,128)S(1)} collective-permute-done((f32[256,256]{1,0:T(8,128)S(1)}, f32[256,256]{1,0:T(8,128)S(1)}, u32[]{:S(2)}, u32[]{:S(2)}) %collective-permute-start.14) | collective-permute-done | bytes 262176 | tf_op jit(solution)/shard_map/ppermute | solution.py:65
  82.7 1.5 collective-permute-done.15.refs_10_
  84.2 3.3 %shard_map.93 = (f32[128,512]{1,0:T(8,128)S(1)}, bf16[256,512]{1,0:T(8,128)(2,1)S(1)}, bf16[256,512]{1,0:T(8,128)(2,1)S(1)}, f32[3,128,256]{2,1,0:T(8,128)S(1)},...) custom-call(s32[2]{0:T(128)S(1)} %pad_add_fusion.info_ref.refs_0_, ...), custom_call_target="tpu_custom_call" | custom-call | flops 1024 | bytes 1024 | tf_op jit(solution)/shard_map/pallas_call | solution.py:89
  87.5 2.4 %shard_map.94 = (f32[512,256]{1,0:T(8,128)S(1)}, f32[512,256]{1,0:T(8,128)S(1)}) custom-call(s32[2]{0:T(128)S(1)} %pad_add_fusion.info_ref.refs_0_, s32[3,8]{1,0:T(4,128)S(1)} %copy-done.4, bf16[1024,1024]{1,0:T(8,128)(2,1)S(1)} %get-tuple-element.89.refs_5_.refs_2_, bf16[1024,1024]{1,0:T(8,128)(2,1)S(1)} %get-tuple-element.95.refs_3_, ...), custom_call_target="tpu_custom_call" | custom-call | flops 1024 | bytes 1024 | tf_op jit(solution)/shard_map/pallas_call | solution.py:89
  90.0 1.5 collective-permute-start.20
  91.5 1.4 collective-permute-start.21
  92.9 0.7 collective-permute-start.22
  94.2 3.2 %collective-permute-start.19 = (f32[256,256]{1,0:T(8,128)S(1)}, f32[256,256]{1,0:T(8,128)S(1)}, u32[]{:S(2)}, u32[]{:S(2)}) collective-permute-start(f32[256,256]{1,0:T(8,128)S(1)} %get-tuple-element.121), channel_id=1, source_target_pairs={{0,4},{1,5},{2,6},{3,7},{4,0},{5,1},{6,2},{7,3},{8,12},{9,13},{10,... | collective-permute-start | bytes 786440 | tf_op jit(solution)/shard_map/ppermute | solution.py:65
  97.4 1.0 shard_map.96.refs_14_.refs_15_
  98.5 3.9 %shard_map.97 = (f32[2,128,256]{2,1,0:T(8,128)S(1)}, f32[2,128,256]{2,1,0:T(8,128)S(1)}, f32[2,128,256]{2,1,0:T(8,128)S(1)}, f32[2,128,256]{2,1,0:T(8,128)S(1)}, f32[2,128,512]{2,1,0:T(8,128)S(1)}) custom-call(s32[2]{0:T(128)S(1)} %pad_add_fusion.info_ref.refs_0_, bf16[512,512]{1,0:T(8,128)(2,1)S(1)} %shard_map.78.refs_3_.refs_4_.refs_2_.refs_1_, ...), custom_call_target="tpu_custom_call" | custom-call | flops 1024 | bytes 1024 | tf_op jit(solution)/shard_map/pallas_call | solution.py:89
  102.3 5.1 %collective-permute-done.19.refs_2_ = f32[256,256]{1,0:T(8,128)S(1)} collective-permute-done((f32[256,256]{1,0:T(8,128)S(1)}, f32[256,256]{1,0:T(8,128)S(1)}, u32[]{:S(2)}, u32[]{:S(2)}) %collective-permute-start.19) | collective-permute-done | bytes 262176 | tf_op jit(solution)/shard_map/ppermute | solution.py:65
  107.4 1.4 collective-permute-start.26
  108.8 1.4 collective-permute-start.27
  110.8 1.5 collective-permute-start.28
  112.3 0.8 shard_map.98
  113.1 2.3 %collective-permute-start.25 = (f32[3,64,256]{2,1,0:T(8,128)S(1)}, f32[3,64,256]{2,1,0:T(8,128)S(1)}, u32[]{:S(2)}, u32[]{:S(2)}) collective-permute-start(f32[3,64,256]{2,1,0:T(8,128)S(1)} %get-tuple-element.130), channel_id=1, source_target_pairs={{0,2},{1,3},{2,0},{3,1},{4,6},{5,7},{6,4},{7,5},{8,10},{9,11},{10,... | collective-permute-start | bytes 589832 | tf_op jit(solution)/shard_map/ppermute | solution.py:65
  115.4 1.2 collective-permute-done.26.refs_4_
  116.6 5.5 %collective-permute-done.27.refs_5_ = f32[2,128,256]{2,1,0:T(8,128)S(1)} collective-permute-done((f32[2,128,256]{2,1,0:T(8,128)S(1)}, f32[2,128,256]{2,1,0:T(8,128)S(1)}, u32[]{:S(2)}, u32[]{:S(2)}) %collective-permute-start.27) | collective-permute-done | bytes 262176 | tf_op jit(solution)/shard_map/ppermute | solution.py:65
  122.7 3.4 %collective-permute-start.29 = (f32[3,32,256]{2,1,0:T(8,128)S(1)}, f32[3,32,256]{2,1,0:T(8,128)S(1)}, u32[]{:S(2)}, u32[]{:S(2)}) collective-permute-start(f32[3,32,256]{2,1,0:T(8,128)S(1)} %get-tuple-element.135), channel_id=1, source_target_pairs={{0,4},{1,5},{2,6},{3,7},{4,0},{5,1},{6,2},{7,3},{8,12},{9,13},{10,... | collective-permute-start | bytes 294920 | tf_op jit(solution)/shard_map/ppermute | solution.py:65
  126.2 3.4 %collective-permute-start.32 = (f32[2,32,256]{2,1,0:T(8,128)S(1)}, f32[2,32,256]{2,1,0:T(8,128)S(1)}, u32[]{:S(2)}, u32[]{:S(2)}) collective-permute-start(f32[2,32,256]{2,1,0:T(8,128)S(1)} %get-tuple-element.140), channel_id=1, source_target_pairs={{0,2},{1,3},{2,0},{3,1},{4,6},{5,7},{6,4},{7,5},{8,10},{9,11},{10,... | collective-permute-start | bytes 196616 | tf_op jit(solution)/shard_map/ppermute | solution.py:65
  129.6 0.9 collective-permute-start.33
  130.5 7.3 %collective-permute-done.31.refs_6_ = f32[2,32,256]{2,1,0:T(8,128)S(1)} collective-permute-done((f32[2,32,256]{2,1,0:T(8,128)S(1)}, f32[2,32,256]{2,1,0:T(8,128)S(1)}, u32[]{:S(2)}, u32[]{:S(2)}) %collective-permute-start.31) | collective-permute-done | bytes 65568 | tf_op jit(solution)/shard_map/ppermute | solution.py:65
  139.0 0.9 collective-permute-done.36.refs_4_
  140.4 2.3 %collective-permute-start.39 = (f32[5,16,512]{2,1,0:T(8,128)S(1)}, f32[5,16,512]{2,1,0:T(8,128)S(1)}, u32[]{:S(2)}, u32[]{:S(2)}) collective-permute-start(f32[5,16,512]{2,1,0:T(8,128)S(1)} %shard_map.101.refs_8_.refs_3_), channel_id=1, source_target_pairs={{0,24},{8,16},{16,8},{24,0},{1,25},{9,17},{17,9},{25,1},{2,26},{10... | collective-permute-start | bytes 491528 | tf_op jit(solution)/shard_map/ppermute | solution.py:65
  142.7 0.9 collective-permute-start.38
  144.5 0.8 collective-permute-done.24.refs_5_
  145.5 1.5 %shard_map.102.refs_7_ = f32[3,128,512]{2,1,0:T(8,128)} custom-call(s32[2]{0:T(128)S(1)} %pad_add_fusion.info_ref.refs_0_, s32[3,8]{1,0:T(4,128)S(1)} %copy-done.4, f32[128,512]{1,0:T(8,128)S(1)} %get-tuple-element.109.refs_12_.refs_2_, f32[2,128,512]{2,1,0:T(8,128)S(1)} %get-tuple-element.120.refs_3_, f32[128,256]{1,0:T(8,128)S(1)} %get-tuple-element.127.refs_7_.refs_4_, ...), custom_call_target="tpu_custom_call" | custom-call | flops 1024 | bytes 1024 | tf_op jit(solution)/shard_map/pallas_call | solution.py:89
  147.1 1.4 collective-permute-done.39.refs_6_
  148.5 2.9 %collective-permute-done.38.refs_5_ = f32[5,16,512]{2,1,0:T(8,128)S(1)} collective-permute-done((f32[5,16,512]{2,1,0:T(8,128)S(1)}, f32[5,16,512]{2,1,0:T(8,128)S(1)}, u32[]{:S(2)}, u32[]{:S(2)}) %collective-permute-start.38) | collective-permute-done | bytes 163872 | tf_op jit(solution)/shard_map/ppermute | solution.py:65
  151.4 1.1 copy-done
  152.5 1.6 %shard_map.103 = (f32[3,64,512]{2,1,0:T(8,128)}, f32[2,64,512]{2,1,0:T(8,128)}) custom-call(s32[2]{0:T(128)S(1)} %pad_add_fusion.info_ref.refs_0_, f32[3,64,512]{2,1,0:T(8,128)S(1)} %copy-done.1, f32[2,64,512]{2,1,0:T(8,128)S(1)} %get-tuple-element.148.refs_2_, f32[5,16,512]{2,1,0:T(8,128)S(1)} %shard_map.101.refs_8_.refs_3_, ...), custom_call_target="tpu_custom_call" | custom-call | flops 1024 | bytes 1024 | tf_op jit(solution)/shard_map/pallas_call | solution.py:89
  (61 shorter events, 10.9 us)
Async XLA Ops:
  0.6 24.6 %collective-permute-start.5 = (f32[1024,512]{1,0:T(8,128)}, f32[1024,512]{1,0:T(8,128)S(1)}, u32[]{:S(2)}, u32[]{:S(2)}) collective-permute-start(f32[1024,512]{1,0:T(8,128)} %refs_1_.13), channel_id=1, source_target_pairs={{0,1},{1,0},{2,3},{3,2},{4,5},{5,4},{6,7},{7,6},{8,9},{9,8},{10,11... | collective-permute-start | bytes 6291464 | tf_op jit(solution)/shard_map/ppermute | solution.py:65
  1.2 4.7 %copy-start.3 = (f32[2,64,512]{2,1,0:T(8,128)S(1)}, f32[2,64,512]{2,1,0:T(8,128)}, u32[]{:S(2)}) copy-start(f32[2,64,512]{2,1,0:T(8,128)} %param.7) | copy-start | bytes 786436
  1.2 9.7 %slice-start = ((s8[6291456]{0:T(1024)(128)(4,1)}), s8[4194304]{0:T(1024)(128)(4,1)S(1)}, s32[]{:S(2)}) async-start(s8[6291456]{0:T(1024)(128)(4,1)} %bitcast.3), calls=%async_computation | async-start | bytes 8388608
  3.3 15.1 %collective-permute-start.1 = (f32[512,256]{1,0:T(8,128)S(1)}, f32[512,256]{1,0:T(8,128)S(1)}, u32[]{:S(2)}, u32[]{:S(2)}) collective-permute-start(f32[512,256]{1,0:T(8,128)S(1)} %get-tuple-element.86.refs_8_), channel_id=1, source_target_pairs={{8,0},{24,8},{16,24},{0,16},{9,1},{25,9},{17,25},{1,17},{2,10},{18... | collective-permute-start | bytes 1572872 | tf_op jit(solution)/shard_map/ppermute | solution.py:486
  5.9 14.0 %collective-permute-start = (f32[512,256]{1,0:T(8,128)S(1)}, f32[512,256]{1,0:T(8,128)S(1)}, u32[]{:S(2)}, u32[]{:S(2)}) collective-permute-start(f32[512,256]{1,0:T(8,128)S(1)} %get-tuple-element.77.refs_2_.refs_4_), channel_id=1, source_target_pairs={{0,8},{8,24},{24,16},{16,0},{1,9},{9,25},{25,17},{17,1},{10,2},{2,... | collective-permute-start | bytes 1572872 | tf_op jit(solution)/shard_map/ppermute | solution.py:486
  5.9 5.0 %slice-start.1 = ((s8[6291456]{0:T(1024)(128)(4,1)}), s8[2097152]{0:T(1024)(128)(4,1)S(1)}, s32[]{:S(2)}) async-start(s8[6291456]{0:T(1024)(128)(4,1)} %bitcast.3), calls=%async_computation.1 | async-start | bytes 4194304
  5.9 5.0 %copy-start.4 = (s32[3,8]{1,0:T(4,128)S(1)}, s32[3,8]{1,0:T(4,128)}, u32[]{:S(2)}) copy-start(s32[3,8]{1,0:T(4,128)} %refs_1_.20) | copy-start | bytes 292
  5.9 8.5 %collective-permute-start.2 = (f32[1,2,64,512]{3,2,1,0:T(8,128)S(1)}, f32[1,2,64,512]{3,2,1,0:T(8,128)S(1)}, u32[]{:S(2)}, u32[]{:S(2)}) collective-permute-start(f32[1,2,64,512]{3,2,1,0:T(8,128)S(1)} %bitcast.5), channel_id=1, source_target_pairs={{0,2},{1,3},{2,0},{3,1},{4,6},{5,7},{6,4},{7,5},{8,10},{9,11},{10,... | collective-permute-start | bytes 786440 | tf_op jit(solution)/shard_map/ppermute | solution.py:65
  13.1 12.1 %copy-start.2 = (f32[1024,512]{1,0:T(8,128)S(1)}, f32[1024,512]{1,0:T(8,128)}, u32[]{:S(2)}) copy-start(f32[1024,512]{1,0:T(8,128)} %refs_1_.13) | copy-start | bytes 6291460
  20.6 13.3 %collective-permute-start.4 = (f32[512,256]{1,0:T(8,128)S(1)}, f32[512,256]{1,0:T(8,128)S(1)}, u32[]{:S(2)}, u32[]{:S(2)}) collective-permute-start(f32[512,256]{1,0:T(8,128)S(1)} %get-tuple-element.88.refs_8_), channel_id=1, source_target_pairs={{8,0},{24,8},{16,24},{0,16},{9,1},{25,9},{17,25},{1,17},{2,10},{18... | collective-permute-start | bytes 1572872 | tf_op jit(solution)/shard_map/ppermute | solution.py:486
  22.1 12.9 %collective-permute-start.3 = (f32[512,256]{1,0:T(8,128)S(1)}, f32[512,256]{1,0:T(8,128)S(1)}, u32[]{:S(2)}, u32[]{:S(2)}) collective-permute-start(f32[512,256]{1,0:T(8,128)S(1)} %get-tuple-element.87.refs_3_.refs_4_), channel_id=1, source_target_pairs={{0,8},{8,24},{24,16},{16,0},{1,9},{9,25},{25,17},{17,1},{10,2},{2,... | collective-permute-start | bytes 1572872 | tf_op jit(solution)/shard_map/ppermute | solution.py:486
  22.7 24.8 %collective-permute-start.8 = (f32[2,2,64,512]{3,2,1,0:T(8,128)S(1)}, f32[2,2,64,512]{3,2,1,0:T(8,128)S(1)}, u32[]{:S(2)}, u32[]{:S(2)}) collective-permute-start(f32[2,2,64,512]{3,2,1,0:T(8,128)S(1)} %get-tuple-element.92.refs_3_), channel_id=1, source_target_pairs={{0,4},{1,5},{2,6},{3,7},{4,0},{5,1},{6,2},{7,3},{8,12},{9,13},{10,... | collective-permute-start | bytes 1572872 | tf_op jit(solution)/shard_map/ppermute | solution.py:65
  35.7 12.1 %collective-permute-start.7 = (f32[512,256]{1,0:T(8,128)S(1)}, f32[512,256]{1,0:T(8,128)S(1)}, u32[]{:S(2)}, u32[]{:S(2)}) collective-permute-start(f32[512,256]{1,0:T(8,128)S(1)} %get-tuple-element.91.refs_8_), channel_id=1, source_target_pairs={{8,0},{24,8},{16,24},{0,16},{9,1},{25,9},{17,25},{1,17},{2,10},{18... | collective-permute-start | bytes 1572872 | tf_op jit(solution)/shard_map/ppermute | solution.py:486
  36.4 11.8 %collective-permute-start.6 = (f32[512,256]{1,0:T(8,128)S(1)}, f32[512,256]{1,0:T(8,128)S(1)}, u32[]{:S(2)}, u32[]{:S(2)}) collective-permute-start(f32[512,256]{1,0:T(8,128)S(1)} %get-tuple-element.90.refs_4_), channel_id=1, source_target_pairs={{0,8},{8,24},{24,16},{16,0},{1,9},{9,25},{25,17},{17,1},{10,2},{2,... | collective-permute-start | bytes 1572872 | tf_op jit(solution)/shard_map/ppermute | solution.py:486
  48.9 6.2 %collective-permute-start.9 = (f32[4,2,64,512]{3,2,1,0:T(8,128)S(1)}, f32[4,2,64,512]{3,2,1,0:T(8,128)S(1)}, u32[]{:S(2)}, u32[]{:S(2)}) collective-permute-start(f32[4,2,64,512]{3,2,1,0:T(8,128)S(1)} %get-tuple-element.94.refs_1_), channel_id=1, source_target_pairs={{0,1},{1,0},{2,3},{3,2},{4,5},{5,4},{6,7},{7,6},{8,9},{9,8},{10,11... | collective-permute-start | bytes 3145736 | tf_op jit(solution)/shard_map/ppermute | solution.py:65
  49.0 14.3 %collective-permute-start.12 = (f32[512,256]{1,0:T(8,128)S(1)}, f32[512,256]{1,0:T(8,128)S(1)}, u32[]{:S(2)}, u32[]{:S(2)}) collective-permute-start(f32[512,256]{1,0:T(8,128)S(1)} %get-tuple-element.100), channel_id=1, source_target_pairs={{8,0},{24,8},{16,24},{0,16},{9,1},{25,9},{17,25},{1,17},{2,10},{18... | collective-permute-start | bytes 1572872 | tf_op jit(solution)/shard_map/ppermute | solution.py:486
  49.8 5.2 %copy-start.1 = (f32[3,64,512]{2,1,0:T(8,128)S(1)}, f32[3,64,512]{2,1,0:T(8,128)}, u32[]{:S(2)}) copy-start(f32[3,64,512]{2,1,0:T(8,128)} %refs_1_.21) | copy-start | bytes 1179652
  52.3 14.1 %collective-permute-start.13 = (f32[512,256]{1,0:T(8,128)S(1)}, f32[512,256]{1,0:T(8,128)S(1)}, u32[]{:S(2)}, u32[]{:S(2)}) collective-permute-start(f32[512,256]{1,0:T(8,128)S(1)} %get-tuple-element.101), channel_id=1, source_target_pairs={{0,2},{1,3},{2,0},{3,1},{4,6},{5,7},{6,4},{7,5},{8,10},{9,11},{10,... | collective-permute-start | bytes 1572872 | tf_op jit(solution)/shard_map/ppermute | solution.py:65
  53.7 13.7 %collective-permute-start.11 = (f32[512,256]{1,0:T(8,128)S(1)}, f32[512,256]{1,0:T(8,128)S(1)}, u32[]{:S(2)}, u32[]{:S(2)}) collective-permute-start(f32[512,256]{1,0:T(8,128)S(1)} %get-tuple-element.96.refs_12_), channel_id=1, source_target_pairs={{0,8},{8,24},{24,16},{16,0},{1,9},{9,25},{25,17},{17,1},{10,2},{2,... | collective-permute-start | bytes 1572872 | tf_op jit(solution)/shard_map/ppermute | solution.py:486
  55.0 1.4 collective-permute-start.10
  68.1 13.9 %collective-permute-start.14 = (f32[256,256]{1,0:T(8,128)S(1)}, f32[256,256]{1,0:T(8,128)S(1)}, u32[]{:S(2)}, u32[]{:S(2)}) collective-permute-start(f32[256,256]{1,0:T(8,128)S(1)} %get-tuple-element.104), channel_id=1, source_target_pairs={{0,4},{1,5},{2,6},{3,7},{4,0},{5,1},{6,2},{7,3},{8,12},{9,13},{10,... | collective-permute-start | bytes 786440 | tf_op jit(solution)/shard_map/ppermute | solution.py:65
  70.8 16.7 %collective-permute-start.17 = (f32[512,256]{1,0:T(8,128)S(1)}, f32[512,256]{1,0:T(8,128)S(1)}, u32[]{:S(2)}, u32[]{:S(2)}) collective-permute-start(f32[512,256]{1,0:T(8,128)S(1)} %get-tuple-element.116), channel_id=1, source_target_pairs={{8,0},{24,8},{16,24},{0,16},{9,1},{25,9},{17,25},{1,17},{2,10},{18... | collective-permute-start | bytes 1572872 | tf_op jit(solution)/shard_map/ppermute | solution.py:486
  72.1 15.4 %collective-permute-start.16 = (f32[512,256]{1,0:T(8,128)S(1)}, f32[512,256]{1,0:T(8,128)S(1)}, u32[]{:S(2)}, u32[]{:S(2)}) collective-permute-start(f32[512,256]{1,0:T(8,128)S(1)} %get-tuple-element.106.refs_12_), channel_id=1, source_target_pairs={{0,8},{8,24},{24,16},{16,0},{1,9},{9,25},{25,17},{17,1},{10,2},{2,... | collective-permute-start | bytes 1572872 | tf_op jit(solution)/shard_map/ppermute | solution.py:486
  75.3 18.3 %collective-permute-start.18 = (f32[512,256]{1,0:T(8,128)S(1)}, f32[512,256]{1,0:T(8,128)S(1)}, u32[]{:S(2)}, u32[]{:S(2)}) collective-permute-start(f32[512,256]{1,0:T(8,128)S(1)} %get-tuple-element.108.refs_3_), channel_id=1, source_target_pairs={{0,2},{1,3},{2,0},{3,1},{4,6},{5,7},{6,4},{7,5},{8,10},{9,11},{10,... | collective-permute-start | bytes 1572872 | tf_op jit(solution)/shard_map/ppermute | solution.py:65
  82.6 1.6 %collective-permute-start.15 = (f32[256,256]{1,0:T(8,128)S(1)}, f32[256,256]{1,0:T(8,128)S(1)}, u32[]{:S(2)}, u32[]{:S(2)}) collective-permute-start(f32[256,256]{1,0:T(8,128)S(1)} %shard_map.92.refs_9_.refs_11_), channel_id=1, source_target_pairs={{0,1},{1,0},{2,3},{3,2},{4,5},{5,4},{6,7},{7,6},{8,9},{9,8},{10,11... | collective-permute-start | bytes 786440 | tf_op jit(solution)/shard_map/ppermute | solution.py:65
  89.9 22.4 %collective-permute-start.23 = (f32[512,256]{1,0:T(8,128)S(1)}, f32[512,256]{1,0:T(8,128)S(1)}, u32[]{:S(2)}, u32[]{:S(2)}) collective-permute-start(f32[512,256]{1,0:T(8,128)S(1)} %get-tuple-element.118.refs_3_), channel_id=1, source_target_pairs={{0,2},{1,3},{2,0},{3,1},{4,6},{5,7},{6,4},{7,5},{8,10},{9,11},{10,... | collective-permute-start | bytes 1572872 | tf_op jit(solution)/shard_map/ppermute | solution.py:65
  90.0 18.8 %collective-permute-start.20 = (f32[3,128,256]{2,1,0:T(8,128)S(1)}, f32[3,128,256]{2,1,0:T(8,128)S(1)}, u32[]{:S(2)}, u32[]{:S(2)}) collective-permute-start(f32[3,128,256]{2,1,0:T(8,128)S(1)} %get-tuple-element.123), channel_id=1, source_target_pairs={{0,8},{8,0},{16,24},{24,16},{1,9},{9,1},{17,25},{25,17},{2,10},{10... | collective-permute-start | bytes 1179656 | tf_op jit(solution)/shard_map/ppermute | solution.py:65
  91.5 19.3 %collective-permute-start.21 = (f32[3,128,256]{2,1,0:T(8,128)S(1)}, f32[3,128,256]{2,1,0:T(8,128)S(1)}, u32[]{:S(2)}, u32[]{:S(2)}) collective-permute-start(f32[3,128,256]{2,1,0:T(8,128)S(1)} %get-tuple-element.124), channel_id=1, source_target_pairs={{0,16},{8,24},{16,0},{24,8},{1,17},{9,25},{17,1},{25,9},{2,18},{10... | collective-permute-start | bytes 1179656 | tf_op jit(solution)/shard_map/ppermute | solution.py:65
  92.9 19.4 %collective-permute-start.22 = (f32[3,128,256]{2,1,0:T(8,128)S(1)}, f32[3,128,256]{2,1,0:T(8,128)S(1)}, u32[]{:S(2)}, u32[]{:S(2)}) collective-permute-start(f32[3,128,256]{2,1,0:T(8,128)S(1)} %get-tuple-element.125), channel_id=1, source_target_pairs={{0,24},{8,16},{16,8},{24,0},{1,25},{9,17},{17,9},{25,1},{2,26},{10... | collective-permute-start | bytes 1179656 | tf_op jit(solution)/shard_map/ppermute | solution.py:65
  94.2 13.2 %collective-permute-start.19 = (f32[256,256]{1,0:T(8,128)S(1)}, f32[256,256]{1,0:T(8,128)S(1)}, u32[]{:S(2)}, u32[]{:S(2)}) collective-permute-start(f32[256,256]{1,0:T(8,128)S(1)} %get-tuple-element.121), channel_id=1, source_target_pairs={{0,4},{1,5},{2,6},{3,7},{4,0},{5,1},{6,2},{7,3},{8,12},{9,13},{10,... | collective-permute-start | bytes 786440 | tf_op jit(solution)/shard_map/ppermute | solution.py:65
  107.4 9.2 %collective-permute-start.26 = (f32[2,128,256]{2,1,0:T(8,128)S(1)}, f32[2,128,256]{2,1,0:T(8,128)S(1)}, u32[]{:S(2)}, u32[]{:S(2)}) collective-permute-start(f32[2,128,256]{2,1,0:T(8,128)S(1)} %get-tuple-element.131), channel_id=1, source_target_pairs={{0,8},{8,0},{16,24},{24,16},{1,9},{9,1},{17,25},{25,17},{2,10},{10... | collective-permute-start | bytes 786440 | tf_op jit(solution)/shard_map/ppermute | solution.py:65
  108.8 13.2 %collective-permute-start.27 = (f32[2,128,256]{2,1,0:T(8,128)S(1)}, f32[2,128,256]{2,1,0:T(8,128)S(1)}, u32[]{:S(2)}, u32[]{:S(2)}) collective-permute-start(f32[2,128,256]{2,1,0:T(8,128)S(1)} %get-tuple-element.132), channel_id=1, source_target_pairs={{0,16},{8,24},{16,0},{24,8},{1,17},{9,25},{17,1},{25,9},{2,18},{10... | collective-permute-start | bytes 786440 | tf_op jit(solution)/shard_map/ppermute | solution.py:65
  110.8 11.2 %collective-permute-start.28 = (f32[2,128,256]{2,1,0:T(8,128)S(1)}, f32[2,128,256]{2,1,0:T(8,128)S(1)}, u32[]{:S(2)}, u32[]{:S(2)}) collective-permute-start(f32[2,128,256]{2,1,0:T(8,128)S(1)} %get-tuple-element.133), channel_id=1, source_target_pairs={{0,24},{8,16},{16,8},{24,0},{1,25},{9,17},{17,9},{25,1},{2,26},{10... | collective-permute-start | bytes 786440 | tf_op jit(solution)/shard_map/ppermute | solution.py:65
  113.1 9.0 %collective-permute-start.25 = (f32[3,64,256]{2,1,0:T(8,128)S(1)}, f32[3,64,256]{2,1,0:T(8,128)S(1)}, u32[]{:S(2)}, u32[]{:S(2)}) collective-permute-start(f32[3,64,256]{2,1,0:T(8,128)S(1)} %get-tuple-element.130), channel_id=1, source_target_pairs={{0,2},{1,3},{2,0},{3,1},{4,6},{5,7},{6,4},{7,5},{8,10},{9,11},{10,... | collective-permute-start | bytes 589832 | tf_op jit(solution)/shard_map/ppermute | solution.py:65
  115.4 22.4 %collective-permute-start.30 = (f32[256,256]{1,0:T(8,128)S(1)}, f32[256,256]{1,0:T(8,128)S(1)}, u32[]{:S(2)}, u32[]{:S(2)}) collective-permute-start(f32[256,256]{1,0:T(8,128)S(1)} %get-tuple-element.137), channel_id=1, source_target_pairs={{0,4},{1,5},{2,6},{3,7},{4,0},{5,1},{6,2},{7,3},{8,12},{9,13},{10,... | collective-permute-start | bytes 786440 | tf_op jit(solution)/shard_map/ppermute | solution.py:65
  122.7 15.1 %collective-permute-start.29 = (f32[3,32,256]{2,1,0:T(8,128)S(1)}, f32[3,32,256]{2,1,0:T(8,128)S(1)}, u32[]{:S(2)}, u32[]{:S(2)}) collective-permute-start(f32[3,32,256]{2,1,0:T(8,128)S(1)} %get-tuple-element.135), channel_id=1, source_target_pairs={{0,4},{1,5},{2,6},{3,7},{4,0},{5,1},{6,2},{7,3},{8,12},{9,13},{10,... | collective-permute-start | bytes 294920 | tf_op jit(solution)/shard_map/ppermute | solution.py:65
  126.1 11.7 %collective-permute-start.31 = (f32[2,32,256]{2,1,0:T(8,128)S(1)}, f32[2,32,256]{2,1,0:T(8,128)S(1)}, u32[]{:S(2)}, u32[]{:S(2)}) collective-permute-start(f32[2,32,256]{2,1,0:T(8,128)S(1)} %get-tuple-element.139), channel_id=1, source_target_pairs={{0,4},{1,5},{2,6},{3,7},{4,0},{5,1},{6,2},{7,3},{8,12},{9,13},{10,... | collective-permute-start | bytes 196616 | tf_op jit(solution)/shard_map/ppermute | solution.py:65
  126.2 11.6 %collective-permute-start.32 = (f32[2,32,256]{2,1,0:T(8,128)S(1)}, f32[2,32,256]{2,1,0:T(8,128)S(1)}, u32[]{:S(2)}, u32[]{:S(2)}) collective-permute-start(f32[2,32,256]{2,1,0:T(8,128)S(1)} %get-tuple-element.140), channel_id=1, source_target_pairs={{0,2},{1,3},{2,0},{3,1},{4,6},{5,7},{6,4},{7,5},{8,10},{9,11},{10,... | collective-permute-start | bytes 196616 | tf_op jit(solution)/shard_map/ppermute | solution.py:65
  129.6 8.2 %collective-permute-start.33 = (f32[2,32,256]{2,1,0:T(8,128)S(1)}, f32[2,32,256]{2,1,0:T(8,128)S(1)}, u32[]{:S(2)}, u32[]{:S(2)}) collective-permute-start(f32[2,32,256]{2,1,0:T(8,128)S(1)} %get-tuple-element.141), channel_id=1, source_target_pairs={{0,6},{1,7},{2,4},{3,5},{4,2},{5,3},{6,0},{7,1},{8,14},{9,15},{10,... | collective-permute-start | bytes 196616 | tf_op jit(solution)/shard_map/ppermute | solution.py:65
  138.4 1.4 collective-permute-start.35
  138.5 1.4 collective-permute-start.36
  140.4 8.0 %collective-permute-start.39 = (f32[5,16,512]{2,1,0:T(8,128)S(1)}, f32[5,16,512]{2,1,0:T(8,128)S(1)}, u32[]{:S(2)}, u32[]{:S(2)}) collective-permute-start(f32[5,16,512]{2,1,0:T(8,128)S(1)} %shard_map.101.refs_8_.refs_3_), channel_id=1, source_target_pairs={{0,24},{8,16},{16,8},{24,0},{1,25},{9,17},{17,9},{25,1},{2,26},{10... | collective-permute-start | bytes 491528 | tf_op jit(solution)/shard_map/ppermute | solution.py:65
  142.7 8.7 %collective-permute-start.38 = (f32[5,16,512]{2,1,0:T(8,128)S(1)}, f32[5,16,512]{2,1,0:T(8,128)S(1)}, u32[]{:S(2)}, u32[]{:S(2)}) collective-permute-start(f32[5,16,512]{2,1,0:T(8,128)S(1)} %shard_map.101.refs_8_.refs_3_), channel_id=1, source_target_pairs={{0,16},{8,24},{16,0},{24,8},{1,17},{9,25},{17,1},{25,9},{2,18},{10... | collective-permute-start | bytes 491528 | tf_op jit(solution)/shard_map/ppermute | solution.py:65
  143.6 7.8 %collective-permute-start.37 = (f32[5,16,512]{2,1,0:T(8,128)S(1)}, f32[5,16,512]{2,1,0:T(8,128)S(1)}, u32[]{:S(2)}, u32[]{:S(2)}) collective-permute-start(f32[5,16,512]{2,1,0:T(8,128)S(1)} %shard_map.101.refs_8_.refs_3_), channel_id=1, source_target_pairs={{0,8},{8,0},{16,24},{24,16},{1,9},{9,1},{17,25},{25,17},{2,10},{10... | collective-permute-start | bytes 491528 | tf_op jit(solution)/shard_map/ppermute | solution.py:65
  144.0 1.3 collective-permute-start.24
  144.0 1.5 collective-permute-start.34
  151.4 1.1 copy-start

commit v16 on v15

--- a/solution.py
+++ b/solution.py
@@ -595,9 +595,16 @@
         if member == 0:
             held["last", 0] = [keep, arrived]
             return
+        yield WAIT
         if final:
-            yield WAIT
-        mine, theirs = yield (part_step, [keep, arrived], [shape(size // 2, half)] * 2)
+            mine, theirs = yield (part_step, [keep, arrived], [shape(size // 2, half)] * 2)
+        else:
+            mine, theirs = heavy(
+                functools.partial(step_kernel, [(part_step, 2, 2)]),
+                [shape(size // 2, half)] * 2,
+                [info, keep, arrived],
+                smem=1,
+            )
         held["sum", member] = [mine, swap(theirs, "col", col_count, 1)]
 
     def total_flow(name, pieces, direct):
@@ -707,7 +714,7 @@
             except StopIteration:
                 pass
 
-    diags, uppers = heavy(
+    diags, uppers = call(
         functools.partial(finish_kernel, row_count),
         [shape(members, diag_width, width), shape(children, diag_width, width)],
         [info, diag_inverse, held["links"][4]] + held["totals"],

time: 154 us -> 154 us (level)
  starting transfers between devices: 46.9 us -> 43.9 us
  waiting for transfers between devices: 60.5 us -> 63.5 us
    ppermute x30, waiting for transfers between devices: 44.9 us -> 47.9 us  [swap(): lax.ppermute(value, axis, [(place, place ^ change) for place in range(siz...]
    ppermute x30, starting transfers between devices: 35.9 us -> 33 us  [swap(): lax.ppermute(value, axis, [(place, place ^ change) for place in range(siz...]
    pallas_call x28 -> x29, Pallas kernels: 44.5 us -> 45 us  [call(): pl.pallas_call(inner, out_shape=outs, in_specs=[pl.BlockSpec(memory_space...]
  transfers between devices with their start and end apart: 40 -> 40, of which waited for: 24 -> 25; matrix products, arithmetic and copies ran while one was open for 0% -> 0% of each run, Pallas kernels for 26% -> 27%
where the time goes in v16:
time: 154 us
  waiting for transfers between devices  63.5 us (41%)
  Pallas kernels  45 us (29%)
  starting transfers between devices  43.9 us (29%)
    ppermute x30, waiting for transfers between devices, swap(): lax.ppermute(value, axis, [(place, place ^ change) for place in range(siz...  47.9 us
    pallas_call x29, Pallas kernels, call(): pl.pallas_call(inner, out_shape=outs, in_specs=[pl.BlockSpec(memory_space...  45 us
    ppermute x30, starting transfers between devices, swap(): lax.ppermute(value, axis, [(place, place ^ change) for place in range(siz...  33 us
    ppermute x10, waiting for transfers between devices, ring_flow(): lax.ppermute(moving[way], AXES, rings[way])  15.6 us
    ppermute x10, starting transfers between devices, ring_flow(): lax.ppermute(moving[way], AXES, rings[way])  11 us
  transfers between devices with their start and end apart: 40, of which 25 were waited for; matrix products, arithmetic and copies ran while one was open for 0% of the time, Pallas kernels for 27%

profile of v16, /device:TPU:0, one launch (start us, length us, event | category | flops | bytes accessed | tf_op | source)
XLA Modules:
  0.0 153.5 jit_solution(12751631123254494543)
XLA Ops:
  1.2 2.0 %shard_map.76 = (f32[512,256]{1,0:T(8,128)S(1)}, f32[512,256]{1,0:T(8,128)S(1)}) custom-call(s32[2]{0:T(128)S(1)} %pad_add_fusion.info_ref.refs_0_, f32[3,1024,512]{2,1,0:T(8,128)} %refs_2_.7), custom_call_target="tpu_custom_call" | custom-call | flops 1024 | bytes 1024 | tf_op jit(solution)/shard_map/pallas_call | solution.py:89
  3.3 2.6 %collective-permute-start.1 = (f32[512,256]{1,0:T(8,128)S(1)}, f32[512,256]{1,0:T(8,128)S(1)}, u32[]{:S(2)}, u32[]{:S(2)}) collective-permute-start(f32[512,256]{1,0:T(8,128)S(1)} %get-tuple-element.86.refs_8_), channel_id=1, source_target_pairs={{8,0},{24,8},{16,24},{0,16},{9,1},{25,9},{17,25},{1,17},{2,10},{18... | collective-permute-start | bytes 1572872 | tf_op jit(solution)/shard_map/ppermute | solution.py:486
  5.9 2.0 %collective-permute-start.2 = (f32[1,2,64,512]{3,2,1,0:T(8,128)S(1)}, f32[1,2,64,512]{3,2,1,0:T(8,128)S(1)}, u32[]{:S(2)}, u32[]{:S(2)}) collective-permute-start(f32[1,2,64,512]{3,2,1,0:T(8,128)S(1)} %bitcast.5), channel_id=1, source_target_pairs={{0,2},{1,3},{2,0},{3,1},{4,6},{5,7},{6,4},{7,5},{8,10},{9,11},{10,... | collective-permute-start | bytes 786440 | tf_op jit(solution)/shard_map/ppermute | solution.py:65
  8.0 2.1 %shard_map.77 = (f32[512,256]{1,0:T(8,128)S(1)}, f32[512,256]{1,0:T(8,128)S(1)}, f32[512,256]{1,0:T(8,128)S(1)}, f32[512,256]{1,0:T(8,128)S(1)}) custom-call(s32[2]{0:T(128)S(1)} %pad_add_fusion.info_ref.refs_0_, f32[3,1024,512]{2,1,0:T(8,128)} %refs_2_.7, f32[512,256]{1,0:T(8,128)S(1)} %get-tuple-element.77.refs_2_.refs_4_), custom_call_target="tpu_custom_call" | custom-call | flops 1024 | bytes 1024 | tf_op jit(solution)/shard_map/pallas_call | solution.py:89
  10.1 0.8 shard_map.78.refs_3_.refs_4_.refs_2_.refs_1_
  10.9 2.2 %shard_map.79 = (bf16[3,256,512]{2,1,0:T(8,128)(2,1)S(1)}, bf16[3,256,512]{2,1,0:T(8,128)(2,1)S(1)}, bf16[3,512,256]{2,1,0:T(8,128)(2,1)S(1)}, bf16[3,512,256]{2,1,0:T(8,128)(2,1)S(1)}) custom-call(s32[2]{0:T(128)S(1)} %pad_add_fusion.info_ref.refs_0_, s32[3,8]{1,0:T(4,128)S(1)} %copy-done.3, f32[3,1024,512]{2,1,0:T(8,128)S(1)} %bitcast.4, ...), custom_call_target="tpu_custom_call" | custom-call | flops 1024 | bytes 1024 | tf_op jit(solution)/shard_map/pallas_call | solution.py:89
  13.2 1.2 collective-permute-done.2.refs_6_
  14.4 4.0 %collective-permute-done.1.refs_4_.refs_9_ = f32[512,256]{1,0:T(8,128)S(1)} collective-permute-done((f32[512,256]{1,0:T(8,128)S(1)}, f32[512,256]{1,0:T(8,128)S(1)}, u32[]{:S(2)}, u32[]{:S(2)}) %collective-permute-start.1) | collective-permute-done | bytes 524320 | tf_op jit(solution)/shard_map/ppermute | solution.py:486
  18.4 1.5 collective-permute-done.refs_3_.refs_5_
  19.9 0.7 shard_map.80
  20.6 1.5 %collective-permute-start.4 = (f32[512,256]{1,0:T(8,128)S(1)}, f32[512,256]{1,0:T(8,128)S(1)}, u32[]{:S(2)}, u32[]{:S(2)}) collective-permute-start(f32[512,256]{1,0:T(8,128)S(1)} %get-tuple-element.88.refs_8_), channel_id=1, source_target_pairs={{8,0},{24,8},{16,24},{0,16},{9,1},{25,9},{17,25},{1,17},{2,10},{18... | collective-permute-start | bytes 1572872 | tf_op jit(solution)/shard_map/ppermute | solution.py:486
  22.7 2.6 %collective-permute-start.8 = (f32[2,2,64,512]{3,2,1,0:T(8,128)S(1)}, f32[2,2,64,512]{3,2,1,0:T(8,128)S(1)}, u32[]{:S(2)}, u32[]{:S(2)}) collective-permute-start(f32[2,2,64,512]{3,2,1,0:T(8,128)S(1)} %get-tuple-element.92.refs_3_), channel_id=1, source_target_pairs={{0,4},{1,5},{2,6},{3,7},{4,0},{5,1},{6,2},{7,3},{8,12},{9,13},{10,... | collective-permute-start | bytes 1572872 | tf_op jit(solution)/shard_map/ppermute | solution.py:65
  25.2 1.7 %shard_map.81 = (bf16[1024,1024]{1,0:T(8,128)(2,1)S(1)}, bf16[1024,1024]{1,0:T(8,128)(2,1)S(1)}) custom-call(s32[2]{0:T(128)S(1)} %pad_add_fusion.info_ref.refs_0_, f32[1024,512]{1,0:T(8,128)S(1)} %copy-done.1, f32[1024,512]{1,0:T(8,128)S(1)} %collective-permute-done.5.refs_2_, f32[512,256]{1,0:T(8,128)S(1)} %get-tuple-element.87.refs_3_.refs_4_), custom_call_target="tpu_custom_call" | custom-call | flops 1024 | bytes 1024 | tf_op jit(solution)/shard_map/pallas_call | solution.py:89
  26.9 6.9 %collective-permute-done.4.refs_4_.refs_10_.refs_9_ = f32[512,256]{1,0:T(8,128)S(1)} collective-permute-done((f32[512,256]{1,0:T(8,128)S(1)}, f32[512,256]{1,0:T(8,128)S(1)}, u32[]{:S(2)}, u32[]{:S(2)}) %collective-permute-start.4) | collective-permute-done | bytes 524320 | tf_op jit(solution)/shard_map/ppermute | solution.py:486
  33.9 1.2 collective-permute-done.3.refs_3_.refs_6_.refs_5_
  36.4 1.4 collective-permute-start.6
  37.8 2.2 %shard_map.83 = (bf16[512,1024]{1,0:T(8,128)(2,1)S(1)}, bf16[512,1024]{1,0:T(8,128)(2,1)S(1)}) custom-call(s32[2]{0:T(128)S(1)} %pad_add_fusion.info_ref.refs_0_, s32[3,8]{1,0:T(4,128)S(1)} %copy-done.3, f32[3,1024,512]{2,1,0:T(8,128)S(1)} %bitcast.4, bf16[512,512]{1,0:T(8,128)(2,1)S(1)} %shard_map.78.refs_3_.refs_4_.refs_2_.refs_1_, ...), custom_call_target="tpu_custom_call" | custom-call | flops 1024 | bytes 1024 | tf_op jit(solution)/shard_map/pallas_call | solution.py:89
  40.0 7.4 %collective-permute-done.8.refs_4_ = f32[2,2,64,512]{3,2,1,0:T(8,128)S(1)} collective-permute-done((f32[2,2,64,512]{3,2,1,0:T(8,128)S(1)}, f32[2,2,64,512]{3,2,1,0:T(8,128)S(1)}, u32[]{:S(2)}, u32[]{:S(2)}) %collective-permute-start.8) | collective-permute-done | bytes 524320 | tf_op jit(solution)/shard_map/ppermute | solution.py:65
  48.2 0.7 shard_map.84
  49.0 0.8 collective-permute-start.12
  49.8 2.5 %shard_map.85 = (f32[512,256]{1,0:T(8,128)S(1)}, f32[512,256]{1,0:T(8,128)S(1)}) custom-call(s32[2]{0:T(128)S(1)} %pad_add_fusion.info_ref.refs_0_, s32[3,8]{1,0:T(4,128)S(1)} %copy-done.3, bf16[1024,1024]{1,0:T(8,128)(2,1)S(1)} %get-tuple-element.89.refs_5_.refs_2_, bf16[1024,1024]{1,0:T(8,128)(2,1)S(1)} %get-tuple-element.95.refs_3_, ...), custom_call_target="tpu_custom_call" | custom-call | flops 1024 | bytes 1024 | tf_op jit(solution)/shard_map/pallas_call | solution.py:89
  52.3 1.4 collective-permute-start.13
  53.7 1.3 collective-permute-start.11
  55.1 0.7 shard_map.86.refs_1_.refs_7_
  56.4 4.5 %shard_map.87 = (bf16[2,512,512]{2,1,0:T(8,128)(2,1)S(1)}, bf16[2,512,512]{2,1,0:T(8,128)(2,1)S(1)}, bf16[2,512,256]{2,1,0:T(8,128)(2,1)S(1)}, bf16[2,512,256]{2...) custom-call(s32[2]{0:T(128)S(1)} %pad_add_fusion.info_ref.refs_0_, ...), custom_call_target="tpu_custom_call" | custom-call | flops 1024 | bytes 1024 | tf_op jit(solution)/shard_map/pallas_call | solution.py:89
  61.0 2.2 %shard_map.88 = (bf16[512,1024]{1,0:T(8,128)(2,1)S(1)}, bf16[512,1024]{1,0:T(8,128)(2,1)S(1)}) custom-call(s32[2]{0:T(128)S(1)} %pad_add_fusion.info_ref.refs_0_, s32[3,8]{1,0:T(4,128)S(1)} %copy-done.3, f32[3,1024,512]{2,1,0:T(8,128)S(1)} %bitcast.4, bf16[512,512]{1,0:T(8,128)(2,1)S(1)} %shard_map.78.refs_3_.refs_4_.refs_2_.refs_1_, ...), custom_call_target="tpu_custom_call" | custom-call | flops 1024 | bytes 1024 | tf_op jit(solution)/shard_map/pallas_call | solution.py:89
  63.3 3.1 %collective-permute-done.13.refs_4_ = f32[512,256]{1,0:T(8,128)S(1)} collective-permute-done((f32[512,256]{1,0:T(8,128)S(1)}, f32[512,256]{1,0:T(8,128)S(1)}, u32[]{:S(2)}, u32[]{:S(2)}) %collective-permute-start.13) | collective-permute-done | bytes 524320 | tf_op jit(solution)/shard_map/ppermute | solution.py:65
  66.4 1.0 collective-permute-done.11.refs_1_.refs_7_.refs_6_
  68.1 2.7 %collective-permute-start.14 = (f32[256,256]{1,0:T(8,128)S(1)}, f32[256,256]{1,0:T(8,128)S(1)}, u32[]{:S(2)}, u32[]{:S(2)}) collective-permute-start(f32[256,256]{1,0:T(8,128)S(1)} %get-tuple-element.104), channel_id=1, source_target_pairs={{0,4},{1,5},{2,6},{3,7},{4,0},{5,1},{6,2},{7,3},{8,12},{9,13},{10,... | collective-permute-start | bytes 786440 | tf_op jit(solution)/shard_map/ppermute | solution.py:65
  70.8 1.3 collective-permute-start.17
  72.1 0.7 collective-permute-start.16
  72.8 2.5 %shard_map.90 = (f32[512,256]{1,0:T(8,128)S(1)}, f32[512,256]{1,0:T(8,128)S(1)}) custom-call(s32[2]{0:T(128)S(1)} %pad_add_fusion.info_ref.refs_0_, s32[3,8]{1,0:T(4,128)S(1)} %copy-done.3, bf16[1024,1024]{1,0:T(8,128)(2,1)S(1)} %get-tuple-element.89.refs_5_.refs_2_, bf16[1024,1024]{1,0:T(8,128)(2,1)S(1)} %get-tuple-element.95.refs_3_, ...), custom_call_target="tpu_custom_call" | custom-call | flops 1024 | bytes 1024 | tf_op jit(solution)/shard_map/pallas_call | solution.py:89
  75.3 1.0 shard_map.91.refs_3_.refs_13_
  76.3 5.6 %collective-permute-done.14.refs_2_ = f32[256,256]{1,0:T(8,128)S(1)} collective-permute-done((f32[256,256]{1,0:T(8,128)S(1)}, f32[256,256]{1,0:T(8,128)S(1)}, u32[]{:S(2)}, u32[]{:S(2)}) %collective-permute-start.14) | collective-permute-done | bytes 262176 | tf_op jit(solution)/shard_map/ppermute | solution.py:65
  82.6 1.4 collective-permute-done.15.refs_10_
  84.1 3.3 %shard_map.93 = (f32[128,512]{1,0:T(8,128)S(1)}, bf16[256,512]{1,0:T(8,128)(2,1)S(1)}, bf16[256,512]{1,0:T(8,128)(2,1)S(1)}, f32[3,128,256]{2,1,0:T(8,128)S(1)},...) custom-call(s32[2]{0:T(128)S(1)} %pad_add_fusion.info_ref.refs_0_, ...), custom_call_target="tpu_custom_call" | custom-call | flops 1024 | bytes 1024 | tf_op jit(solution)/shard_map/pallas_call | solution.py:89
  87.4 2.4 %shard_map.94 = (f32[512,256]{1,0:T(8,128)S(1)}, f32[512,256]{1,0:T(8,128)S(1)}) custom-call(s32[2]{0:T(128)S(1)} %pad_add_fusion.info_ref.refs_0_, s32[3,8]{1,0:T(4,128)S(1)} %copy-done.3, bf16[1024,1024]{1,0:T(8,128)(2,1)S(1)} %get-tuple-element.89.refs_5_.refs_2_, bf16[1024,1024]{1,0:T(8,128)(2,1)S(1)} %get-tuple-element.95.refs_3_, ...), custom_call_target="tpu_custom_call" | custom-call | flops 1024 | bytes 1024 | tf_op jit(solution)/shard_map/pallas_call | solution.py:89
  90.5 1.4 collective-permute-start.20
  91.9 1.4 collective-permute-start.21
  93.3 0.7 collective-permute-start.22
  93.9 3.4 %collective-permute-done.18.refs_2_ = f32[512,256]{1,0:T(8,128)S(1)} collective-permute-done((f32[512,256]{1,0:T(8,128)S(1)}, f32[512,256]{1,0:T(8,128)S(1)}, u32[]{:S(2)}, u32[]{:S(2)}) %collective-permute-start.18) | collective-permute-done | bytes 524320 | tf_op jit(solution)/shard_map/ppermute | solution.py:65
  97.9 1.4 collective-permute-start.19
  99.3 1.1 shard_map.96.refs_14_.refs_15_
  100.4 3.9 %shard_map.97 = (f32[2,128,256]{2,1,0:T(8,128)S(1)}, f32[2,128,256]{2,1,0:T(8,128)S(1)}, f32[2,128,256]{2,1,0:T(8,128)S(1)}, f32[2,128,256]{2,1,0:T(8,128)S(1)}, f32[2,128,512]{2,1,0:T(8,128)S(1)}) custom-call(s32[2]{0:T(128)S(1)} %pad_add_fusion.info_ref.refs_0_, bf16[512,512]{1,0:T(8,128)(2,1)S(1)} %shard_map.78.refs_3_.refs_4_.refs_2_.refs_1_, ...), custom_call_target="tpu_custom_call" | custom-call | flops 1024 | bytes 1024 | tf_op jit(solution)/shard_map/pallas_call | solution.py:89
  104.3 1.7 %collective-permute-start.26 = (f32[2,128,256]{2,1,0:T(8,128)S(1)}, f32[2,128,256]{2,1,0:T(8,128)S(1)}, u32[]{:S(2)}, u32[]{:S(2)}) collective-permute-start(f32[2,128,256]{2,1,0:T(8,128)S(1)} %get-tuple-element.131), channel_id=1, source_target_pairs={{0,8},{8,0},{16,24},{24,16},{1,9},{9,1},{17,25},{25,17},{2,10},{10... | collective-permute-start | bytes 786440 | tf_op jit(solution)/shard_map/ppermute | solution.py:65
  106.0 4.8 %collective-permute-done.21.refs_3_ = f32[3,128,256]{2,1,0:T(8,128)S(1)} collective-permute-done((f32[3,128,256]{2,1,0:T(8,128)S(1)}, f32[3,128,256]{2,1,0:T(8,128)S(1)}, u32[]{:S(2)}, u32[]{:S(2)}) %collective-permute-start.21) | collective-permute-done | bytes 393248 | tf_op jit(solution)/shard_map/ppermute | solution.py:65
  110.8 2.5 %collective-permute-start.27 = (f32[2,128,256]{2,1,0:T(8,128)S(1)}, f32[2,128,256]{2,1,0:T(8,128)S(1)}, u32[]{:S(2)}, u32[]{:S(2)}) collective-permute-start(f32[2,128,256]{2,1,0:T(8,128)S(1)} %get-tuple-element.132), channel_id=1, source_target_pairs={{0,16},{8,24},{16,0},{24,8},{1,17},{9,25},{17,1},{25,9},{2,18},{10... | collective-permute-start | bytes 786440 | tf_op jit(solution)/shard_map/ppermute | solution.py:65
  113.7 0.7 shard_map.98
  114.4 1.1 collective-permute-start.25
  115.5 2.3 %collective-permute-start.30 = (f32[256,256]{1,0:T(8,128)S(1)}, f32[256,256]{1,0:T(8,128)S(1)}, u32[]{:S(2)}, u32[]{:S(2)}) collective-permute-start(f32[256,256]{1,0:T(8,128)S(1)} %get-tuple-element.137), channel_id=1, source_target_pairs={{0,4},{1,5},{2,6},{3,7},{4,0},{5,1},{6,2},{7,3},{8,12},{9,13},{10,... | collective-permute-start | bytes 786440 | tf_op jit(solution)/shard_map/ppermute | solution.py:65
  118.3 4.9 %collective-permute-done.27.refs_5_ = f32[2,128,256]{2,1,0:T(8,128)S(1)} collective-permute-done((f32[2,128,256]{2,1,0:T(8,128)S(1)}, f32[2,128,256]{2,1,0:T(8,128)S(1)}, u32[]{:S(2)}, u32[]{:S(2)}) %collective-permute-start.27) | collective-permute-done | bytes 262176 | tf_op jit(solution)/shard_map/ppermute | solution.py:65
  123.2 1.6 %collective-permute-done.25.refs_2_ = f32[3,64,256]{2,1,0:T(8,128)S(1)} collective-permute-done((f32[3,64,256]{2,1,0:T(8,128)S(1)}, f32[3,64,256]{2,1,0:T(8,128)S(1)}, u32[]{:S(2)}, u32[]{:S(2)}) %collective-permute-start.25) | collective-permute-done | bytes 196640 | tf_op jit(solution)/shard_map/ppermute | solution.py:65
  125.5 1.5 collective-permute-start.29
  126.9 1.5 collective-permute-start.31
  128.5 2.9 %collective-permute-start.33 = (f32[2,32,256]{2,1,0:T(8,128)S(1)}, f32[2,32,256]{2,1,0:T(8,128)S(1)}, u32[]{:S(2)}, u32[]{:S(2)}) collective-permute-start(f32[2,32,256]{2,1,0:T(8,128)S(1)} %get-tuple-element.141), channel_id=1, source_target_pairs={{0,6},{1,7},{2,4},{3,5},{4,2},{5,3},{6,0},{7,1},{8,14},{9,15},{10,... | collective-permute-start | bytes 196616 | tf_op jit(solution)/shard_map/ppermute | solution.py:65
  131.3 7.1 %collective-permute-done.31.refs_6_ = f32[2,32,256]{2,1,0:T(8,128)S(1)} collective-permute-done((f32[2,32,256]{2,1,0:T(8,128)S(1)}, f32[2,32,256]{2,1,0:T(8,128)S(1)}, u32[]{:S(2)}, u32[]{:S(2)}) %collective-permute-start.31) | collective-permute-done | bytes 65568 | tf_op jit(solution)/shard_map/ppermute | solution.py:65
  139.6 0.9 collective-permute-done.36.refs_4_
  141.1 2.2 %collective-permute-start.39 = (f32[5,16,512]{2,1,0:T(8,128)S(1)}, f32[5,16,512]{2,1,0:T(8,128)S(1)}, u32[]{:S(2)}, u32[]{:S(2)}) collective-permute-start(f32[5,16,512]{2,1,0:T(8,128)S(1)} %shard_map.102.refs_8_.refs_0_), channel_id=1, source_target_pairs={{0,24},{8,16},{16,8},{24,0},{1,25},{9,17},{17,9},{25,1},{2,26},{10... | collective-permute-start | bytes 491528 | tf_op jit(solution)/shard_map/ppermute | solution.py:65
  143.3 0.9 collective-permute-start.38
  145.1 0.8 collective-permute-done.24.refs_5_
  146.2 1.5 %shard_map.103 = f32[3,128,512]{2,1,0:T(8,128)} custom-call(s32[2]{0:T(128)S(1)} %pad_add_fusion.info_ref.refs_0_, s32[3,8]{1,0:T(4,128)S(1)} %copy-done.3, f32[128,512]{1,0:T(8,128)S(1)} %get-tuple-element.109.refs_12_.refs_2_, f32[2,128,512]{2,1,0:T(8,128)S(1)} %get-tuple-element.120.refs_3_, f32[128,256]{1,0:T(8,128)S(1)} %get-tuple-element.128.refs_7_.refs_4_, ...), custom_call_target="tpu_custom_call" | custom-call | flops 1024 | bytes 1024 | tf_op jit(solution)/shard_map/pallas_call | solution.py:89
  147.7 1.4 collective-permute-done.39.refs_3_
  149.1 2.9 %collective-permute-done.38.refs_2_ = f32[5,16,512]{2,1,0:T(8,128)S(1)} collective-permute-done((f32[5,16,512]{2,1,0:T(8,128)S(1)}, f32[5,16,512]{2,1,0:T(8,128)S(1)}, u32[]{:S(2)}, u32[]{:S(2)}) %collective-permute-start.38) | collective-permute-done | bytes 163872 | tf_op jit(solution)/shard_map/ppermute | solution.py:65
  152.0 1.5 shard_map.104
  (60 shorter events, 11.3 us)
Async XLA Ops:
  0.6 24.6 %collective-permute-start.5 = (f32[1024,512]{1,0:T(8,128)}, f32[1024,512]{1,0:T(8,128)S(1)}, u32[]{:S(2)}, u32[]{:S(2)}) collective-permute-start(f32[1024,512]{1,0:T(8,128)} %refs_1_.12), channel_id=1, source_target_pairs={{0,1},{1,0},{2,3},{3,2},{4,5},{5,4},{6,7},{7,6},{8,9},{9,8},{10,11... | collective-permute-start | bytes 6291464 | tf_op jit(solution)/shard_map/ppermute | solution.py:65
  1.2 4.7 %copy-start.2 = (f32[2,64,512]{2,1,0:T(8,128)S(1)}, f32[2,64,512]{2,1,0:T(8,128)}, u32[]{:S(2)}) copy-start(f32[2,64,512]{2,1,0:T(8,128)} %param.7) | copy-start | bytes 786436
  1.2 9.7 %slice-start = ((s8[6291456]{0:T(1024)(128)(4,1)}), s8[4194304]{0:T(1024)(128)(4,1)S(1)}, s32[]{:S(2)}) async-start(s8[6291456]{0:T(1024)(128)(4,1)} %bitcast.3), calls=%async_computation | async-start | bytes 8388608
  3.3 15.1 %collective-permute-start.1 = (f32[512,256]{1,0:T(8,128)S(1)}, f32[512,256]{1,0:T(8,128)S(1)}, u32[]{:S(2)}, u32[]{:S(2)}) collective-permute-start(f32[512,256]{1,0:T(8,128)S(1)} %get-tuple-element.86.refs_8_), channel_id=1, source_target_pairs={{8,0},{24,8},{16,24},{0,16},{9,1},{25,9},{17,25},{1,17},{2,10},{18... | collective-permute-start | bytes 1572872 | tf_op jit(solution)/shard_map/ppermute | solution.py:486
  5.9 14.0 %collective-permute-start = (f32[512,256]{1,0:T(8,128)S(1)}, f32[512,256]{1,0:T(8,128)S(1)}, u32[]{:S(2)}, u32[]{:S(2)}) collective-permute-start(f32[512,256]{1,0:T(8,128)S(1)} %get-tuple-element.77.refs_2_.refs_4_), channel_id=1, source_target_pairs={{0,8},{8,24},{24,16},{16,0},{1,9},{9,25},{25,17},{17,1},{10,2},{2,... | collective-permute-start | bytes 1572872 | tf_op jit(solution)/shard_map/ppermute | solution.py:486
  5.9 5.0 %slice-start.1 = ((s8[6291456]{0:T(1024)(128)(4,1)}), s8[2097152]{0:T(1024)(128)(4,1)S(1)}, s32[]{:S(2)}) async-start(s8[6291456]{0:T(1024)(128)(4,1)} %bitcast.3), calls=%async_computation.1 | async-start | bytes 4194304
  5.9 5.0 %copy-start.3 = (s32[3,8]{1,0:T(4,128)S(1)}, s32[3,8]{1,0:T(4,128)}, u32[]{:S(2)}) copy-start(s32[3,8]{1,0:T(4,128)} %refs_1_.19) | copy-start | bytes 292
  5.9 8.5 %collective-permute-start.2 = (f32[1,2,64,512]{3,2,1,0:T(8,128)S(1)}, f32[1,2,64,512]{3,2,1,0:T(8,128)S(1)}, u32[]{:S(2)}, u32[]{:S(2)}) collective-permute-start(f32[1,2,64,512]{3,2,1,0:T(8,128)S(1)} %bitcast.5), channel_id=1, source_target_pairs={{0,2},{1,3},{2,0},{3,1},{4,6},{5,7},{6,4},{7,5},{8,10},{9,11},{10,... | collective-permute-start | bytes 786440 | tf_op jit(solution)/shard_map/ppermute | solution.py:65
  13.1 12.1 %copy-start.1 = (f32[1024,512]{1,0:T(8,128)S(1)}, f32[1024,512]{1,0:T(8,128)}, u32[]{:S(2)}) copy-start(f32[1024,512]{1,0:T(8,128)} %refs_1_.12) | copy-start | bytes 6291460
  20.6 13.3 %collective-permute-start.4 = (f32[512,256]{1,0:T(8,128)S(1)}, f32[512,256]{1,0:T(8,128)S(1)}, u32[]{:S(2)}, u32[]{:S(2)}) collective-permute-start(f32[512,256]{1,0:T(8,128)S(1)} %get-tuple-element.88.refs_8_), channel_id=1, source_target_pairs={{8,0},{24,8},{16,24},{0,16},{9,1},{25,9},{17,25},{1,17},{2,10},{18... | collective-permute-start | bytes 1572872 | tf_op jit(solution)/shard_map/ppermute | solution.py:486
  22.1 12.9 %collective-permute-start.3 = (f32[512,256]{1,0:T(8,128)S(1)}, f32[512,256]{1,0:T(8,128)S(1)}, u32[]{:S(2)}, u32[]{:S(2)}) collective-permute-start(f32[512,256]{1,0:T(8,128)S(1)} %get-tuple-element.87.refs_3_.refs_4_), channel_id=1, source_target_pairs={{0,8},{8,24},{24,16},{16,0},{1,9},{9,25},{25,17},{17,1},{10,2},{2,... | collective-permute-start | bytes 1572872 | tf_op jit(solution)/shard_map/ppermute | solution.py:486
  22.7 24.8 %collective-permute-start.8 = (f32[2,2,64,512]{3,2,1,0:T(8,128)S(1)}, f32[2,2,64,512]{3,2,1,0:T(8,128)S(1)}, u32[]{:S(2)}, u32[]{:S(2)}) collective-permute-start(f32[2,2,64,512]{3,2,1,0:T(8,128)S(1)} %get-tuple-element.92.refs_3_), channel_id=1, source_target_pairs={{0,4},{1,5},{2,6},{3,7},{4,0},{5,1},{6,2},{7,3},{8,12},{9,13},{10,... | collective-permute-start | bytes 1572872 | tf_op jit(solution)/shard_map/ppermute | solution.py:65
  35.7 12.1 %collective-permute-start.7 = (f32[512,256]{1,0:T(8,128)S(1)}, f32[512,256]{1,0:T(8,128)S(1)}, u32[]{:S(2)}, u32[]{:S(2)}) collective-permute-start(f32[512,256]{1,0:T(8,128)S(1)} %get-tuple-element.91.refs_8_), channel_id=1, source_target_pairs={{8,0},{24,8},{16,24},{0,16},{9,1},{25,9},{17,25},{1,17},{2,10},{18... | collective-permute-start | bytes 1572872 | tf_op jit(solution)/shard_map/ppermute | solution.py:486
  36.4 11.8 %collective-permute-start.6 = (f32[512,256]{1,0:T(8,128)S(1)}, f32[512,256]{1,0:T(8,128)S(1)}, u32[]{:S(2)}, u32[]{:S(2)}) collective-permute-start(f32[512,256]{1,0:T(8,128)S(1)} %get-tuple-element.90.refs_4_), channel_id=1, source_target_pairs={{0,8},{8,24},{24,16},{16,0},{1,9},{9,25},{25,17},{17,1},{10,2},{2,... | collective-permute-start | bytes 1572872 | tf_op jit(solution)/shard_map/ppermute | solution.py:486
  48.9 6.2 %collective-permute-start.9 = (f32[4,2,64,512]{3,2,1,0:T(8,128)S(1)}, f32[4,2,64,512]{3,2,1,0:T(8,128)S(1)}, u32[]{:S(2)}, u32[]{:S(2)}) collective-permute-start(f32[4,2,64,512]{3,2,1,0:T(8,128)S(1)} %get-tuple-element.94.refs_1_), channel_id=1, source_target_pairs={{0,1},{1,0},{2,3},{3,2},{4,5},{5,4},{6,7},{7,6},{8,9},{9,8},{10,11... | collective-permute-start | bytes 3145736 | tf_op jit(solution)/shard_map/ppermute | solution.py:65
  49.0 14.3 %collective-permute-start.12 = (f32[512,256]{1,0:T(8,128)S(1)}, f32[512,256]{1,0:T(8,128)S(1)}, u32[]{:S(2)}, u32[]{:S(2)}) collective-permute-start(f32[512,256]{1,0:T(8,128)S(1)} %get-tuple-element.100), channel_id=1, source_target_pairs={{8,0},{24,8},{16,24},{0,16},{9,1},{25,9},{17,25},{1,17},{2,10},{18... | collective-permute-start | bytes 1572872 | tf_op jit(solution)/shard_map/ppermute | solution.py:486
  49.8 5.2 %copy-start = (f32[3,64,512]{2,1,0:T(8,128)S(1)}, f32[3,64,512]{2,1,0:T(8,128)}, u32[]{:S(2)}) copy-start(f32[3,64,512]{2,1,0:T(8,128)} %diag_ref.1) | copy-start | bytes 1179652
  52.3 14.1 %collective-permute-start.13 = (f32[512,256]{1,0:T(8,128)S(1)}, f32[512,256]{1,0:T(8,128)S(1)}, u32[]{:S(2)}, u32[]{:S(2)}) collective-permute-start(f32[512,256]{1,0:T(8,128)S(1)} %get-tuple-element.101), channel_id=1, source_target_pairs={{0,2},{1,3},{2,0},{3,1},{4,6},{5,7},{6,4},{7,5},{8,10},{9,11},{10,... | collective-permute-start | bytes 1572872 | tf_op jit(solution)/shard_map/ppermute | solution.py:65
  53.7 13.7 %collective-permute-start.11 = (f32[512,256]{1,0:T(8,128)S(1)}, f32[512,256]{1,0:T(8,128)S(1)}, u32[]{:S(2)}, u32[]{:S(2)}) collective-permute-start(f32[512,256]{1,0:T(8,128)S(1)} %get-tuple-element.96.refs_12_), channel_id=1, source_target_pairs={{0,8},{8,24},{24,16},{16,0},{1,9},{9,25},{25,17},{17,1},{10,2},{2,... | collective-permute-start | bytes 1572872 | tf_op jit(solution)/shard_map/ppermute | solution.py:486
  55.0 1.4 collective-permute-start.10
  68.1 13.8 %collective-permute-start.14 = (f32[256,256]{1,0:T(8,128)S(1)}, f32[256,256]{1,0:T(8,128)S(1)}, u32[]{:S(2)}, u32[]{:S(2)}) collective-permute-start(f32[256,256]{1,0:T(8,128)S(1)} %get-tuple-element.104), channel_id=1, source_target_pairs={{0,4},{1,5},{2,6},{3,7},{4,0},{5,1},{6,2},{7,3},{8,12},{9,13},{10,... | collective-permute-start | bytes 786440 | tf_op jit(solution)/shard_map/ppermute | solution.py:65
  70.8 16.6 %collective-permute-start.17 = (f32[512,256]{1,0:T(8,128)S(1)}, f32[512,256]{1,0:T(8,128)S(1)}, u32[]{:S(2)}, u32[]{:S(2)}) collective-permute-start(f32[512,256]{1,0:T(8,128)S(1)} %get-tuple-element.116), channel_id=1, source_target_pairs={{8,0},{24,8},{16,24},{0,16},{9,1},{25,9},{17,25},{1,17},{2,10},{18... | collective-permute-start | bytes 1572872 | tf_op jit(solution)/shard_map/ppermute | solution.py:486
  72.1 15.3 %collective-permute-start.16 = (f32[512,256]{1,0:T(8,128)S(1)}, f32[512,256]{1,0:T(8,128)S(1)}, u32[]{:S(2)}, u32[]{:S(2)}) collective-permute-start(f32[512,256]{1,0:T(8,128)S(1)} %get-tuple-element.106.refs_12_), channel_id=1, source_target_pairs={{0,8},{8,24},{24,16},{16,0},{1,9},{9,25},{25,17},{17,1},{10,2},{2,... | collective-permute-start | bytes 1572872 | tf_op jit(solution)/shard_map/ppermute | solution.py:486
  82.5 1.6 %collective-permute-start.15 = (f32[256,256]{1,0:T(8,128)S(1)}, f32[256,256]{1,0:T(8,128)S(1)}, u32[]{:S(2)}, u32[]{:S(2)}) collective-permute-start(f32[256,256]{1,0:T(8,128)S(1)} %shard_map.92.refs_9_.refs_11_), channel_id=1, source_target_pairs={{0,1},{1,0},{2,3},{3,2},{4,5},{5,4},{6,7},{7,6},{8,9},{9,8},{10,11... | collective-permute-start | bytes 786440 | tf_op jit(solution)/shard_map/ppermute | solution.py:65
  82.6 14.8 %collective-permute-start.18 = (f32[512,256]{1,0:T(8,128)S(1)}, f32[512,256]{1,0:T(8,128)S(1)}, u32[]{:S(2)}, u32[]{:S(2)}) collective-permute-start(f32[512,256]{1,0:T(8,128)S(1)} %get-tuple-element.108.refs_3_), channel_id=1, source_target_pairs={{0,2},{1,3},{2,0},{3,1},{4,6},{5,7},{6,4},{7,5},{8,10},{9,11},{10,... | collective-permute-start | bytes 1572872 | tf_op jit(solution)/shard_map/ppermute | solution.py:65
  89.8 23.9 %collective-permute-start.23 = (f32[512,256]{1,0:T(8,128)S(1)}, f32[512,256]{1,0:T(8,128)S(1)}, u32[]{:S(2)}, u32[]{:S(2)}) collective-permute-start(f32[512,256]{1,0:T(8,128)S(1)} %get-tuple-element.118.refs_3_), channel_id=1, source_target_pairs={{0,2},{1,3},{2,0},{3,1},{4,6},{5,7},{6,4},{7,5},{8,10},{9,11},{10,... | collective-permute-start | bytes 1572872 | tf_op jit(solution)/shard_map/ppermute | solution.py:65
  90.5 13.8 %collective-permute-start.20 = (f32[3,128,256]{2,1,0:T(8,128)S(1)}, f32[3,128,256]{2,1,0:T(8,128)S(1)}, u32[]{:S(2)}, u32[]{:S(2)}) collective-permute-start(f32[3,128,256]{2,1,0:T(8,128)S(1)} %get-tuple-element.123), channel_id=1, source_target_pairs={{0,8},{8,0},{16,24},{24,16},{1,9},{9,1},{17,25},{25,17},{2,10},{10... | collective-permute-start | bytes 1179656 | tf_op jit(solution)/shard_map/ppermute | solution.py:65
  91.9 18.9 %collective-permute-start.21 = (f32[3,128,256]{2,1,0:T(8,128)S(1)}, f32[3,128,256]{2,1,0:T(8,128)S(1)}, u32[]{:S(2)}, u32[]{:S(2)}) collective-permute-start(f32[3,128,256]{2,1,0:T(8,128)S(1)} %get-tuple-element.124), channel_id=1, source_target_pairs={{0,16},{8,24},{16,0},{24,8},{1,17},{9,25},{17,1},{25,9},{2,18},{10... | collective-permute-start | bytes 1179656 | tf_op jit(solution)/shard_map/ppermute | solution.py:65
  93.3 20.0 %collective-permute-start.22 = (f32[3,128,256]{2,1,0:T(8,128)S(1)}, f32[3,128,256]{2,1,0:T(8,128)S(1)}, u32[]{:S(2)}, u32[]{:S(2)}) collective-permute-start(f32[3,128,256]{2,1,0:T(8,128)S(1)} %get-tuple-element.125), channel_id=1, source_target_pairs={{0,24},{8,16},{16,8},{24,0},{1,25},{9,17},{17,9},{25,1},{2,26},{10... | collective-permute-start | bytes 1179656 | tf_op jit(solution)/shard_map/ppermute | solution.py:65
  97.9 17.5 %collective-permute-start.19 = (f32[256,256]{1,0:T(8,128)S(1)}, f32[256,256]{1,0:T(8,128)S(1)}, u32[]{:S(2)}, u32[]{:S(2)}) collective-permute-start(f32[256,256]{1,0:T(8,128)S(1)} %get-tuple-element.121), channel_id=1, source_target_pairs={{0,4},{1,5},{2,6},{3,7},{4,0},{5,1},{6,2},{7,3},{8,12},{9,13},{10,... | collective-permute-start | bytes 786440 | tf_op jit(solution)/shard_map/ppermute | solution.py:65
  104.3 14.1 %collective-permute-start.26 = (f32[2,128,256]{2,1,0:T(8,128)S(1)}, f32[2,128,256]{2,1,0:T(8,128)S(1)}, u32[]{:S(2)}, u32[]{:S(2)}) collective-permute-start(f32[2,128,256]{2,1,0:T(8,128)S(1)} %get-tuple-element.131), channel_id=1, source_target_pairs={{0,8},{8,0},{16,24},{24,16},{1,9},{9,1},{17,25},{25,17},{2,10},{10... | collective-permute-start | bytes 786440 | tf_op jit(solution)/shard_map/ppermute | solution.py:65
  110.8 12.4 %collective-permute-start.27 = (f32[2,128,256]{2,1,0:T(8,128)S(1)}, f32[2,128,256]{2,1,0:T(8,128)S(1)}, u32[]{:S(2)}, u32[]{:S(2)}) collective-permute-start(f32[2,128,256]{2,1,0:T(8,128)S(1)} %get-tuple-element.132), channel_id=1, source_target_pairs={{0,16},{8,24},{16,0},{24,8},{1,17},{9,25},{17,1},{25,9},{2,18},{10... | collective-permute-start | bytes 786440 | tf_op jit(solution)/shard_map/ppermute | solution.py:65
  113.3 10.0 %collective-permute-start.28 = (f32[2,128,256]{2,1,0:T(8,128)S(1)}, f32[2,128,256]{2,1,0:T(8,128)S(1)}, u32[]{:S(2)}, u32[]{:S(2)}) collective-permute-start(f32[2,128,256]{2,1,0:T(8,128)S(1)} %get-tuple-element.133), channel_id=1, source_target_pairs={{0,24},{8,16},{16,8},{24,0},{1,25},{9,17},{17,9},{25,1},{2,26},{10... | collective-permute-start | bytes 786440 | tf_op jit(solution)/shard_map/ppermute | solution.py:65
  114.4 10.4 %collective-permute-start.25 = (f32[3,64,256]{2,1,0:T(8,128)S(1)}, f32[3,64,256]{2,1,0:T(8,128)S(1)}, u32[]{:S(2)}, u32[]{:S(2)}) collective-permute-start(f32[3,64,256]{2,1,0:T(8,128)S(1)} %get-tuple-element.130), channel_id=1, source_target_pairs={{0,2},{1,3},{2,0},{3,1},{4,6},{5,7},{6,4},{7,5},{8,10},{9,11},{10,... | collective-permute-start | bytes 589832 | tf_op jit(solution)/shard_map/ppermute | solution.py:65
  115.5 23.0 %collective-permute-start.30 = (f32[256,256]{1,0:T(8,128)S(1)}, f32[256,256]{1,0:T(8,128)S(1)}, u32[]{:S(2)}, u32[]{:S(2)}) collective-permute-start(f32[256,256]{1,0:T(8,128)S(1)} %get-tuple-element.137), channel_id=1, source_target_pairs={{0,4},{1,5},{2,6},{3,7},{4,0},{5,1},{6,2},{7,3},{8,12},{9,13},{10,... | collective-permute-start | bytes 786440 | tf_op jit(solution)/shard_map/ppermute | solution.py:65
  125.5 13.0 %collective-permute-start.29 = (f32[3,32,256]{2,1,0:T(8,128)S(1)}, f32[3,32,256]{2,1,0:T(8,128)S(1)}, u32[]{:S(2)}, u32[]{:S(2)}) collective-permute-start(f32[3,32,256]{2,1,0:T(8,128)S(1)} %get-tuple-element.135), channel_id=1, source_target_pairs={{0,4},{1,5},{2,6},{3,7},{4,0},{5,1},{6,2},{7,3},{8,12},{9,13},{10,... | collective-permute-start | bytes 294920 | tf_op jit(solution)/shard_map/ppermute | solution.py:65
  126.9 11.5 %collective-permute-start.31 = (f32[2,32,256]{2,1,0:T(8,128)S(1)}, f32[2,32,256]{2,1,0:T(8,128)S(1)}, u32[]{:S(2)}, u32[]{:S(2)}) collective-permute-start(f32[2,32,256]{2,1,0:T(8,128)S(1)} %get-tuple-element.139), channel_id=1, source_target_pairs={{0,4},{1,5},{2,6},{3,7},{4,0},{5,1},{6,2},{7,3},{8,12},{9,13},{10,... | collective-permute-start | bytes 196616 | tf_op jit(solution)/shard_map/ppermute | solution.py:65
  128.5 10.0 %collective-permute-start.32 = (f32[2,32,256]{2,1,0:T(8,128)S(1)}, f32[2,32,256]{2,1,0:T(8,128)S(1)}, u32[]{:S(2)}, u32[]{:S(2)}) collective-permute-start(f32[2,32,256]{2,1,0:T(8,128)S(1)} %get-tuple-element.140), channel_id=1, source_target_pairs={{0,2},{1,3},{2,0},{3,1},{4,6},{5,7},{6,4},{7,5},{8,10},{9,11},{10,... | collective-permute-start | bytes 196616 | tf_op jit(solution)/shard_map/ppermute | solution.py:65
  128.5 10.0 %collective-permute-start.33 = (f32[2,32,256]{2,1,0:T(8,128)S(1)}, f32[2,32,256]{2,1,0:T(8,128)S(1)}, u32[]{:S(2)}, u32[]{:S(2)}) collective-permute-start(f32[2,32,256]{2,1,0:T(8,128)S(1)} %get-tuple-element.141), channel_id=1, source_target_pairs={{0,6},{1,7},{2,4},{3,5},{4,2},{5,3},{6,0},{7,1},{8,14},{9,15},{10,... | collective-permute-start | bytes 196616 | tf_op jit(solution)/shard_map/ppermute | solution.py:65
  139.1 1.4 collective-permute-start.35
  139.1 1.4 collective-permute-start.36
  141.1 8.0 %collective-permute-start.39 = (f32[5,16,512]{2,1,0:T(8,128)S(1)}, f32[5,16,512]{2,1,0:T(8,128)S(1)}, u32[]{:S(2)}, u32[]{:S(2)}) collective-permute-start(f32[5,16,512]{2,1,0:T(8,128)S(1)} %shard_map.102.refs_8_.refs_0_), channel_id=1, source_target_pairs={{0,24},{8,16},{16,8},{24,0},{1,25},{9,17},{17,9},{25,1},{2,26},{10... | collective-permute-start | bytes 491528 | tf_op jit(solution)/shard_map/ppermute | solution.py:65
  143.3 8.7 %collective-permute-start.38 = (f32[5,16,512]{2,1,0:T(8,128)S(1)}, f32[5,16,512]{2,1,0:T(8,128)S(1)}, u32[]{:S(2)}, u32[]{:S(2)}) collective-permute-start(f32[5,16,512]{2,1,0:T(8,128)S(1)} %shard_map.102.refs_8_.refs_0_), channel_id=1, source_target_pairs={{0,16},{8,24},{16,0},{24,8},{1,17},{9,25},{17,1},{25,9},{2,18},{10... | collective-permute-start | bytes 491528 | tf_op jit(solution)/shard_map/ppermute | solution.py:65
  144.2 7.8 %collective-permute-start.37 = (f32[5,16,512]{2,1,0:T(8,128)S(1)}, f32[5,16,512]{2,1,0:T(8,128)S(1)}, u32[]{:S(2)}, u32[]{:S(2)}) collective-permute-start(f32[5,16,512]{2,1,0:T(8,128)S(1)} %shard_map.102.refs_8_.refs_0_), channel_id=1, source_target_pairs={{0,8},{8,0},{16,24},{24,16},{1,9},{9,1},{17,25},{25,17},{2,10},{10... | collective-permute-start | bytes 491528 | tf_op jit(solution)/shard_map/ppermute | solution.py:65
  144.6 1.3 collective-permute-start.24
  144.6 1.5 collective-permute-start.34

commit v17 on v15

--- a/solution.py
+++ b/solution.py
@@ -707,7 +707,7 @@
             except StopIteration:
                 pass
 
-    diags, uppers = heavy(
+    diags, uppers = call(
         functools.partial(finish_kernel, row_count),
         [shape(members, diag_width, width), shape(children, diag_width, width)],
         [info, diag_inverse, held["links"][4]] + held["totals"],

time: 154 us -> 153 us (level)
  no operation moved by 1% of the time
where the time goes in v17:
time: 153 us
  waiting for transfers between devices  60.5 us (40%)
  starting transfers between devices  46.9 us (31%)
  Pallas kernels  44.5 us (29%)
    ppermute x30, waiting for transfers between devices, swap(): lax.ppermute(value, axis, [(place, place ^ change) for place in range(siz...  44.9 us
    pallas_call x28, Pallas kernels, call(): pl.pallas_call(inner, out_shape=outs, in_specs=[pl.BlockSpec(memory_space...  44.5 us
    ppermute x30, starting transfers between devices, swap(): lax.ppermute(value, axis, [(place, place ^ change) for place in range(siz...  35.9 us
    ppermute x10, waiting for transfers between devices, ring_flow(): lax.ppermute(moving[way], AXES, rings[way])  15.6 us
    ppermute x10, starting transfers between devices, ring_flow(): lax.ppermute(moving[way], AXES, rings[way])  11 us
  transfers between devices with their start and end apart: 40, of which 24 were waited for; matrix products, arithmetic and copies ran while one was open for 0% of the time, Pallas kernels for 26%

profile of v17, /device:TPU:0, one launch (start us, length us, event | category | flops | bytes accessed | tf_op | source)
XLA Modules:
  0.0 152.9 jit_solution(1051073850572509253)
XLA Ops:
  1.2 2.0 %shard_map.76 = (f32[512,256]{1,0:T(8,128)S(1)}, f32[512,256]{1,0:T(8,128)S(1)}) custom-call(s32[2]{0:T(128)S(1)} %pad_add_fusion.info_ref.refs_0_, f32[3,1024,512]{2,1,0:T(8,128)} %refs_2_.7), custom_call_target="tpu_custom_call" | custom-call | flops 1024 | bytes 1024 | tf_op jit(solution)/shard_map/pallas_call | solution.py:89
  3.3 2.6 %collective-permute-start.1 = (f32[512,256]{1,0:T(8,128)S(1)}, f32[512,256]{1,0:T(8,128)S(1)}, u32[]{:S(2)}, u32[]{:S(2)}) collective-permute-start(f32[512,256]{1,0:T(8,128)S(1)} %get-tuple-element.86.refs_8_), channel_id=1, source_target_pairs={{8,0},{24,8},{16,24},{0,16},{9,1},{25,9},{17,25},{1,17},{2,10},{18... | collective-permute-start | bytes 1572872 | tf_op jit(solution)/shard_map/ppermute | solution.py:486
  5.9 2.0 %collective-permute-start.2 = (f32[1,2,64,512]{3,2,1,0:T(8,128)S(1)}, f32[1,2,64,512]{3,2,1,0:T(8,128)S(1)}, u32[]{:S(2)}, u32[]{:S(2)}) collective-permute-start(f32[1,2,64,512]{3,2,1,0:T(8,128)S(1)} %bitcast.5), channel_id=1, source_target_pairs={{0,2},{1,3},{2,0},{3,1},{4,6},{5,7},{6,4},{7,5},{8,10},{9,11},{10,... | collective-permute-start | bytes 786440 | tf_op jit(solution)/shard_map/ppermute | solution.py:65
  8.0 2.1 %shard_map.77 = (f32[512,256]{1,0:T(8,128)S(1)}, f32[512,256]{1,0:T(8,128)S(1)}, f32[512,256]{1,0:T(8,128)S(1)}, f32[512,256]{1,0:T(8,128)S(1)}) custom-call(s32[2]{0:T(128)S(1)} %pad_add_fusion.info_ref.refs_0_, f32[3,1024,512]{2,1,0:T(8,128)} %refs_2_.7, f32[512,256]{1,0:T(8,128)S(1)} %get-tuple-element.77.refs_2_.refs_4_), custom_call_target="tpu_custom_call" | custom-call | flops 1024 | bytes 1024 | tf_op jit(solution)/shard_map/pallas_call | solution.py:89
  10.1 0.8 shard_map.78.refs_3_.refs_4_.refs_2_.refs_1_
  10.9 2.2 %shard_map.79 = (bf16[3,256,512]{2,1,0:T(8,128)(2,1)S(1)}, bf16[3,256,512]{2,1,0:T(8,128)(2,1)S(1)}, bf16[3,512,256]{2,1,0:T(8,128)(2,1)S(1)}, bf16[3,512,256]{2,1,0:T(8,128)(2,1)S(1)}) custom-call(s32[2]{0:T(128)S(1)} %pad_add_fusion.info_ref.refs_0_, s32[3,8]{1,0:T(4,128)S(1)} %copy-done.3, f32[3,1024,512]{2,1,0:T(8,128)S(1)} %bitcast.4, ...), custom_call_target="tpu_custom_call" | custom-call | flops 1024 | bytes 1024 | tf_op jit(solution)/shard_map/pallas_call | solution.py:89
  13.2 1.2 collective-permute-done.2.refs_6_
  14.4 4.0 %collective-permute-done.1.refs_4_.refs_9_ = f32[512,256]{1,0:T(8,128)S(1)} collective-permute-done((f32[512,256]{1,0:T(8,128)S(1)}, f32[512,256]{1,0:T(8,128)S(1)}, u32[]{:S(2)}, u32[]{:S(2)}) %collective-permute-start.1) | collective-permute-done | bytes 524320 | tf_op jit(solution)/shard_map/ppermute | solution.py:486
  18.4 1.5 collective-permute-done.refs_3_.refs_5_
  19.9 0.7 shard_map.80
  20.6 1.5 %collective-permute-start.4 = (f32[512,256]{1,0:T(8,128)S(1)}, f32[512,256]{1,0:T(8,128)S(1)}, u32[]{:S(2)}, u32[]{:S(2)}) collective-permute-start(f32[512,256]{1,0:T(8,128)S(1)} %get-tuple-element.88.refs_8_), channel_id=1, source_target_pairs={{8,0},{24,8},{16,24},{0,16},{9,1},{25,9},{17,25},{1,17},{2,10},{18... | collective-permute-start | bytes 1572872 | tf_op jit(solution)/shard_map/ppermute | solution.py:486
  22.7 2.6 %collective-permute-start.8 = (f32[2,2,64,512]{3,2,1,0:T(8,128)S(1)}, f32[2,2,64,512]{3,2,1,0:T(8,128)S(1)}, u32[]{:S(2)}, u32[]{:S(2)}) collective-permute-start(f32[2,2,64,512]{3,2,1,0:T(8,128)S(1)} %get-tuple-element.92.refs_3_), channel_id=1, source_target_pairs={{0,4},{1,5},{2,6},{3,7},{4,0},{5,1},{6,2},{7,3},{8,12},{9,13},{10,... | collective-permute-start | bytes 1572872 | tf_op jit(solution)/shard_map/ppermute | solution.py:65
  25.2 1.7 %shard_map.81 = (bf16[1024,1024]{1,0:T(8,128)(2,1)S(1)}, bf16[1024,1024]{1,0:T(8,128)(2,1)S(1)}) custom-call(s32[2]{0:T(128)S(1)} %pad_add_fusion.info_ref.refs_0_, f32[1024,512]{1,0:T(8,128)S(1)} %copy-done.1, f32[1024,512]{1,0:T(8,128)S(1)} %collective-permute-done.5.refs_2_, f32[512,256]{1,0:T(8,128)S(1)} %get-tuple-element.87.refs_3_.refs_4_), custom_call_target="tpu_custom_call" | custom-call | flops 1024 | bytes 1024 | tf_op jit(solution)/shard_map/pallas_call | solution.py:89
  26.9 6.9 %collective-permute-done.4.refs_4_.refs_10_.refs_9_ = f32[512,256]{1,0:T(8,128)S(1)} collective-permute-done((f32[512,256]{1,0:T(8,128)S(1)}, f32[512,256]{1,0:T(8,128)S(1)}, u32[]{:S(2)}, u32[]{:S(2)}) %collective-permute-start.4) | collective-permute-done | bytes 524320 | tf_op jit(solution)/shard_map/ppermute | solution.py:486
  33.9 1.2 collective-permute-done.3.refs_3_.refs_6_.refs_5_
  36.4 1.4 collective-permute-start.6
  37.8 2.2 %shard_map.83 = (bf16[512,1024]{1,0:T(8,128)(2,1)S(1)}, bf16[512,1024]{1,0:T(8,128)(2,1)S(1)}) custom-call(s32[2]{0:T(128)S(1)} %pad_add_fusion.info_ref.refs_0_, s32[3,8]{1,0:T(4,128)S(1)} %copy-done.3, f32[3,1024,512]{2,1,0:T(8,128)S(1)} %bitcast.4, bf16[512,512]{1,0:T(8,128)(2,1)S(1)} %shard_map.78.refs_3_.refs_4_.refs_2_.refs_1_, ...), custom_call_target="tpu_custom_call" | custom-call | flops 1024 | bytes 1024 | tf_op jit(solution)/shard_map/pallas_call | solution.py:89
  40.0 7.4 %collective-permute-done.8.refs_4_ = f32[2,2,64,512]{3,2,1,0:T(8,128)S(1)} collective-permute-done((f32[2,2,64,512]{3,2,1,0:T(8,128)S(1)}, f32[2,2,64,512]{3,2,1,0:T(8,128)S(1)}, u32[]{:S(2)}, u32[]{:S(2)}) %collective-permute-start.8) | collective-permute-done | bytes 524320 | tf_op jit(solution)/shard_map/ppermute | solution.py:65
  48.2 0.7 shard_map.84
  49.0 0.8 collective-permute-start.12
  49.8 2.5 %shard_map.85 = (f32[512,256]{1,0:T(8,128)S(1)}, f32[512,256]{1,0:T(8,128)S(1)}) custom-call(s32[2]{0:T(128)S(1)} %pad_add_fusion.info_ref.refs_0_, s32[3,8]{1,0:T(4,128)S(1)} %copy-done.3, bf16[1024,1024]{1,0:T(8,128)(2,1)S(1)} %get-tuple-element.89.refs_5_.refs_2_, bf16[1024,1024]{1,0:T(8,128)(2,1)S(1)} %get-tuple-element.95.refs_3_, ...), custom_call_target="tpu_custom_call" | custom-call | flops 1024 | bytes 1024 | tf_op jit(solution)/shard_map/pallas_call | solution.py:89
  52.3 1.4 collective-permute-start.13
  53.7 1.3 collective-permute-start.11
  55.1 0.7 shard_map.86.refs_1_.refs_7_
  56.4 4.5 %shard_map.87 = (bf16[2,512,512]{2,1,0:T(8,128)(2,1)S(1)}, bf16[2,512,512]{2,1,0:T(8,128)(2,1)S(1)}, bf16[2,512,256]{2,1,0:T(8,128)(2,1)S(1)}, bf16[2,512,256]{2...) custom-call(s32[2]{0:T(128)S(1)} %pad_add_fusion.info_ref.refs_0_, ...), custom_call_target="tpu_custom_call" | custom-call | flops 1024 | bytes 1024 | tf_op jit(solution)/shard_map/pallas_call | solution.py:89
  61.0 2.2 %shard_map.88 = (bf16[512,1024]{1,0:T(8,128)(2,1)S(1)}, bf16[512,1024]{1,0:T(8,128)(2,1)S(1)}) custom-call(s32[2]{0:T(128)S(1)} %pad_add_fusion.info_ref.refs_0_, s32[3,8]{1,0:T(4,128)S(1)} %copy-done.3, f32[3,1024,512]{2,1,0:T(8,128)S(1)} %bitcast.4, bf16[512,512]{1,0:T(8,128)(2,1)S(1)} %shard_map.78.refs_3_.refs_4_.refs_2_.refs_1_, ...), custom_call_target="tpu_custom_call" | custom-call | flops 1024 | bytes 1024 | tf_op jit(solution)/shard_map/pallas_call | solution.py:89
  63.3 3.1 %collective-permute-done.13.refs_4_ = f32[512,256]{1,0:T(8,128)S(1)} collective-permute-done((f32[512,256]{1,0:T(8,128)S(1)}, f32[512,256]{1,0:T(8,128)S(1)}, u32[]{:S(2)}, u32[]{:S(2)}) %collective-permute-start.13) | collective-permute-done | bytes 524320 | tf_op jit(solution)/shard_map/ppermute | solution.py:65
  66.4 1.0 collective-permute-done.11.refs_1_.refs_7_.refs_6_
  67.4 0.7 shard_map.89
  68.1 2.7 %collective-permute-start.14 = (f32[256,256]{1,0:T(8,128)S(1)}, f32[256,256]{1,0:T(8,128)S(1)}, u32[]{:S(2)}, u32[]{:S(2)}) collective-permute-start(f32[256,256]{1,0:T(8,128)S(1)} %get-tuple-element.104), channel_id=1, source_target_pairs={{0,4},{1,5},{2,6},{3,7},{4,0},{5,1},{6,2},{7,3},{8,12},{9,13},{10,... | collective-permute-start | bytes 786440 | tf_op jit(solution)/shard_map/ppermute | solution.py:65
  70.8 1.3 collective-permute-start.17
  72.1 0.7 collective-permute-start.16
  72.8 2.5 %shard_map.90 = (f32[512,256]{1,0:T(8,128)S(1)}, f32[512,256]{1,0:T(8,128)S(1)}) custom-call(s32[2]{0:T(128)S(1)} %pad_add_fusion.info_ref.refs_0_, s32[3,8]{1,0:T(4,128)S(1)} %copy-done.3, bf16[1024,1024]{1,0:T(8,128)(2,1)S(1)} %get-tuple-element.89.refs_5_.refs_2_, bf16[1024,1024]{1,0:T(8,128)(2,1)S(1)} %get-tuple-element.95.refs_3_, ...), custom_call_target="tpu_custom_call" | custom-call | flops 1024 | bytes 1024 | tf_op jit(solution)/shard_map/pallas_call | solution.py:89
  75.8 1.0 shard_map.91.refs_3_.refs_13_
  76.9 5.1 %collective-permute-done.14.refs_2_ = f32[256,256]{1,0:T(8,128)S(1)} collective-permute-done((f32[256,256]{1,0:T(8,128)S(1)}, f32[256,256]{1,0:T(8,128)S(1)}, u32[]{:S(2)}, u32[]{:S(2)}) %collective-permute-start.14) | collective-permute-done | bytes 262176 | tf_op jit(solution)/shard_map/ppermute | solution.py:65
  82.7 1.5 collective-permute-done.15.refs_10_
  84.2 3.3 %shard_map.93 = (f32[128,512]{1,0:T(8,128)S(1)}, bf16[256,512]{1,0:T(8,128)(2,1)S(1)}, bf16[256,512]{1,0:T(8,128)(2,1)S(1)}, f32[3,128,256]{2,1,0:T(8,128)S(1)},...) custom-call(s32[2]{0:T(128)S(1)} %pad_add_fusion.info_ref.refs_0_, ...), custom_call_target="tpu_custom_call" | custom-call | flops 1024 | bytes 1024 | tf_op jit(solution)/shard_map/pallas_call | solution.py:89
  87.5 2.4 %shard_map.94 = (f32[512,256]{1,0:T(8,128)S(1)}, f32[512,256]{1,0:T(8,128)S(1)}) custom-call(s32[2]{0:T(128)S(1)} %pad_add_fusion.info_ref.refs_0_, s32[3,8]{1,0:T(4,128)S(1)} %copy-done.3, bf16[1024,1024]{1,0:T(8,128)(2,1)S(1)} %get-tuple-element.89.refs_5_.refs_2_, bf16[1024,1024]{1,0:T(8,128)(2,1)S(1)} %get-tuple-element.95.refs_3_, ...), custom_call_target="tpu_custom_call" | custom-call | flops 1024 | bytes 1024 | tf_op jit(solution)/shard_map/pallas_call | solution.py:89
  90.0 1.5 collective-permute-start.20
  91.5 1.4 collective-permute-start.21
  92.9 0.7 collective-permute-start.22
  94.2 3.2 %collective-permute-start.19 = (f32[256,256]{1,0:T(8,128)S(1)}, f32[256,256]{1,0:T(8,128)S(1)}, u32[]{:S(2)}, u32[]{:S(2)}) collective-permute-start(f32[256,256]{1,0:T(8,128)S(1)} %get-tuple-element.121), channel_id=1, source_target_pairs={{0,4},{1,5},{2,6},{3,7},{4,0},{5,1},{6,2},{7,3},{8,12},{9,13},{10,... | collective-permute-start | bytes 786440 | tf_op jit(solution)/shard_map/ppermute | solution.py:65
  97.4 1.0 shard_map.96.refs_14_.refs_15_
  98.5 3.9 %shard_map.97 = (f32[2,128,256]{2,1,0:T(8,128)S(1)}, f32[2,128,256]{2,1,0:T(8,128)S(1)}, f32[2,128,256]{2,1,0:T(8,128)S(1)}, f32[2,128,256]{2,1,0:T(8,128)S(1)}, f32[2,128,512]{2,1,0:T(8,128)S(1)}) custom-call(s32[2]{0:T(128)S(1)} %pad_add_fusion.info_ref.refs_0_, bf16[512,512]{1,0:T(8,128)(2,1)S(1)} %shard_map.78.refs_3_.refs_4_.refs_2_.refs_1_, ...), custom_call_target="tpu_custom_call" | custom-call | flops 1024 | bytes 1024 | tf_op jit(solution)/shard_map/pallas_call | solution.py:89
  102.3 5.1 %collective-permute-done.19.refs_2_ = f32[256,256]{1,0:T(8,128)S(1)} collective-permute-done((f32[256,256]{1,0:T(8,128)S(1)}, f32[256,256]{1,0:T(8,128)S(1)}, u32[]{:S(2)}, u32[]{:S(2)}) %collective-permute-start.19) | collective-permute-done | bytes 262176 | tf_op jit(solution)/shard_map/ppermute | solution.py:65
  107.4 1.4 collective-permute-start.26
  108.8 1.4 collective-permute-start.27
  110.8 1.5 collective-permute-start.28
  112.3 0.8 shard_map.98
  113.1 2.3 %collective-permute-start.25 = (f32[3,64,256]{2,1,0:T(8,128)S(1)}, f32[3,64,256]{2,1,0:T(8,128)S(1)}, u32[]{:S(2)}, u32[]{:S(2)}) collective-permute-start(f32[3,64,256]{2,1,0:T(8,128)S(1)} %get-tuple-element.130), channel_id=1, source_target_pairs={{0,2},{1,3},{2,0},{3,1},{4,6},{5,7},{6,4},{7,5},{8,10},{9,11},{10,... | collective-permute-start | bytes 589832 | tf_op jit(solution)/shard_map/ppermute | solution.py:65
  115.4 1.2 collective-permute-done.26.refs_4_
  116.6 5.5 %collective-permute-done.27.refs_5_ = f32[2,128,256]{2,1,0:T(8,128)S(1)} collective-permute-done((f32[2,128,256]{2,1,0:T(8,128)S(1)}, f32[2,128,256]{2,1,0:T(8,128)S(1)}, u32[]{:S(2)}, u32[]{:S(2)}) %collective-permute-start.27) | collective-permute-done | bytes 262176 | tf_op jit(solution)/shard_map/ppermute | solution.py:65
  122.7 3.4 %collective-permute-start.29 = (f32[3,32,256]{2,1,0:T(8,128)S(1)}, f32[3,32,256]{2,1,0:T(8,128)S(1)}, u32[]{:S(2)}, u32[]{:S(2)}) collective-permute-start(f32[3,32,256]{2,1,0:T(8,128)S(1)} %get-tuple-element.135), channel_id=1, source_target_pairs={{0,4},{1,5},{2,6},{3,7},{4,0},{5,1},{6,2},{7,3},{8,12},{9,13},{10,... | collective-permute-start | bytes 294920 | tf_op jit(solution)/shard_map/ppermute | solution.py:65
  126.2 3.4 %collective-permute-start.32 = (f32[2,32,256]{2,1,0:T(8,128)S(1)}, f32[2,32,256]{2,1,0:T(8,128)S(1)}, u32[]{:S(2)}, u32[]{:S(2)}) collective-permute-start(f32[2,32,256]{2,1,0:T(8,128)S(1)} %get-tuple-element.140), channel_id=1, source_target_pairs={{0,2},{1,3},{2,0},{3,1},{4,6},{5,7},{6,4},{7,5},{8,10},{9,11},{10,... | collective-permute-start | bytes 196616 | tf_op jit(solution)/shard_map/ppermute | solution.py:65
  129.6 0.9 collective-permute-start.33
  130.5 7.3 %collective-permute-done.31.refs_6_ = f32[2,32,256]{2,1,0:T(8,128)S(1)} collective-permute-done((f32[2,32,256]{2,1,0:T(8,128)S(1)}, f32[2,32,256]{2,1,0:T(8,128)S(1)}, u32[]{:S(2)}, u32[]{:S(2)}) %collective-permute-start.31) | collective-permute-done | bytes 65568 | tf_op jit(solution)/shard_map/ppermute | solution.py:65
  139.0 0.9 collective-permute-done.36.refs_4_
  140.4 2.3 %collective-permute-start.39 = (f32[5,16,512]{2,1,0:T(8,128)S(1)}, f32[5,16,512]{2,1,0:T(8,128)S(1)}, u32[]{:S(2)}, u32[]{:S(2)}) collective-permute-start(f32[5,16,512]{2,1,0:T(8,128)S(1)} %shard_map.101.refs_8_.refs_0_), channel_id=1, source_target_pairs={{0,24},{8,16},{16,8},{24,0},{1,25},{9,17},{17,9},{25,1},{2,26},{10... | collective-permute-start | bytes 491528 | tf_op jit(solution)/shard_map/ppermute | solution.py:65
  142.7 0.9 collective-permute-start.38
  144.5 0.8 collective-permute-done.24.refs_5_
  145.5 1.5 %shard_map.102 = f32[3,128,512]{2,1,0:T(8,128)} custom-call(s32[2]{0:T(128)S(1)} %pad_add_fusion.info_ref.refs_0_, s32[3,8]{1,0:T(4,128)S(1)} %copy-done.3, f32[128,512]{1,0:T(8,128)S(1)} %get-tuple-element.109.refs_12_.refs_2_, f32[2,128,512]{2,1,0:T(8,128)S(1)} %get-tuple-element.120.refs_3_, f32[128,256]{1,0:T(8,128)S(1)} %get-tuple-element.127.refs_7_.refs_4_, ...), custom_call_target="tpu_custom_call" | custom-call | flops 1024 | bytes 1024 | tf_op jit(solution)/shard_map/pallas_call | solution.py:89
  147.1 1.4 collective-permute-done.39.refs_3_
  148.5 2.9 %collective-permute-done.38.refs_2_ = f32[5,16,512]{2,1,0:T(8,128)S(1)} collective-permute-done((f32[5,16,512]{2,1,0:T(8,128)S(1)}, f32[5,16,512]{2,1,0:T(8,128)S(1)}, u32[]{:S(2)}, u32[]{:S(2)}) %collective-permute-start.38) | collective-permute-done | bytes 163872 | tf_op jit(solution)/shard_map/ppermute | solution.py:65
  151.4 1.5 shard_map.103
  (59 shorter events, 10.2 us)
Async XLA Ops:
  0.6 24.6 %collective-permute-start.5 = (f32[1024,512]{1,0:T(8,128)}, f32[1024,512]{1,0:T(8,128)S(1)}, u32[]{:S(2)}, u32[]{:S(2)}) collective-permute-start(f32[1024,512]{1,0:T(8,128)} %refs_1_.12), channel_id=1, source_target_pairs={{0,1},{1,0},{2,3},{3,2},{4,5},{5,4},{6,7},{7,6},{8,9},{9,8},{10,11... | collective-permute-start | bytes 6291464 | tf_op jit(solution)/shard_map/ppermute | solution.py:65
  1.2 4.7 %copy-start.2 = (f32[2,64,512]{2,1,0:T(8,128)S(1)}, f32[2,64,512]{2,1,0:T(8,128)}, u32[]{:S(2)}) copy-start(f32[2,64,512]{2,1,0:T(8,128)} %param.7) | copy-start | bytes 786436
  1.2 9.7 %slice-start = ((s8[6291456]{0:T(1024)(128)(4,1)}), s8[4194304]{0:T(1024)(128)(4,1)S(1)}, s32[]{:S(2)}) async-start(s8[6291456]{0:T(1024)(128)(4,1)} %bitcast.3), calls=%async_computation | async-start | bytes 8388608
  3.3 15.1 %collective-permute-start.1 = (f32[512,256]{1,0:T(8,128)S(1)}, f32[512,256]{1,0:T(8,128)S(1)}, u32[]{:S(2)}, u32[]{:S(2)}) collective-permute-start(f32[512,256]{1,0:T(8,128)S(1)} %get-tuple-element.86.refs_8_), channel_id=1, source_target_pairs={{8,0},{24,8},{16,24},{0,16},{9,1},{25,9},{17,25},{1,17},{2,10},{18... | collective-permute-start | bytes 1572872 | tf_op jit(solution)/shard_map/ppermute | solution.py:486
  5.9 14.0 %collective-permute-start = (f32[512,256]{1,0:T(8,128)S(1)}, f32[512,256]{1,0:T(8,128)S(1)}, u32[]{:S(2)}, u32[]{:S(2)}) collective-permute-start(f32[512,256]{1,0:T(8,128)S(1)} %get-tuple-element.77.refs_2_.refs_4_), channel_id=1, source_target_pairs={{0,8},{8,24},{24,16},{16,0},{1,9},{9,25},{25,17},{17,1},{10,2},{2,... | collective-permute-start | bytes 1572872 | tf_op jit(solution)/shard_map/ppermute | solution.py:486
  5.9 5.0 %slice-start.1 = ((s8[6291456]{0:T(1024)(128)(4,1)}), s8[2097152]{0:T(1024)(128)(4,1)S(1)}, s32[]{:S(2)}) async-start(s8[6291456]{0:T(1024)(128)(4,1)} %bitcast.3), calls=%async_computation.1 | async-start | bytes 4194304
  5.9 5.0 %copy-start.3 = (s32[3,8]{1,0:T(4,128)S(1)}, s32[3,8]{1,0:T(4,128)}, u32[]{:S(2)}) copy-start(s32[3,8]{1,0:T(4,128)} %refs_1_.19) | copy-start | bytes 292
  5.9 8.5 %collective-permute-start.2 = (f32[1,2,64,512]{3,2,1,0:T(8,128)S(1)}, f32[1,2,64,512]{3,2,1,0:T(8,128)S(1)}, u32[]{:S(2)}, u32[]{:S(2)}) collective-permute-start(f32[1,2,64,512]{3,2,1,0:T(8,128)S(1)} %bitcast.5), channel_id=1, source_target_pairs={{0,2},{1,3},{2,0},{3,1},{4,6},{5,7},{6,4},{7,5},{8,10},{9,11},{10,... | collective-permute-start | bytes 786440 | tf_op jit(solution)/shard_map/ppermute | solution.py:65
  13.1 12.1 %copy-start.1 = (f32[1024,512]{1,0:T(8,128)S(1)}, f32[1024,512]{1,0:T(8,128)}, u32[]{:S(2)}) copy-start(f32[1024,512]{1,0:T(8,128)} %refs_1_.12) | copy-start | bytes 6291460
  20.6 13.3 %collective-permute-start.4 = (f32[512,256]{1,0:T(8,128)S(1)}, f32[512,256]{1,0:T(8,128)S(1)}, u32[]{:S(2)}, u32[]{:S(2)}) collective-permute-start(f32[512,256]{1,0:T(8,128)S(1)} %get-tuple-element.88.refs_8_), channel_id=1, source_target_pairs={{8,0},{24,8},{16,24},{0,16},{9,1},{25,9},{17,25},{1,17},{2,10},{18... | collective-permute-start | bytes 1572872 | tf_op jit(solution)/shard_map/ppermute | solution.py:486
  22.1 12.9 %collective-permute-start.3 = (f32[512,256]{1,0:T(8,128)S(1)}, f32[512,256]{1,0:T(8,128)S(1)}, u32[]{:S(2)}, u32[]{:S(2)}) collective-permute-start(f32[512,256]{1,0:T(8,128)S(1)} %get-tuple-element.87.refs_3_.refs_4_), channel_id=1, source_target_pairs={{0,8},{8,24},{24,16},{16,0},{1,9},{9,25},{25,17},{17,1},{10,2},{2,... | collective-permute-start | bytes 1572872 | tf_op jit(solution)/shard_map/ppermute | solution.py:486
  22.7 24.8 %collective-permute-start.8 = (f32[2,2,64,512]{3,2,1,0:T(8,128)S(1)}, f32[2,2,64,512]{3,2,1,0:T(8,128)S(1)}, u32[]{:S(2)}, u32[]{:S(2)}) collective-permute-start(f32[2,2,64,512]{3,2,1,0:T(8,128)S(1)} %get-tuple-element.92.refs_3_), channel_id=1, source_target_pairs={{0,4},{1,5},{2,6},{3,7},{4,0},{5,1},{6,2},{7,3},{8,12},{9,13},{10,... | collective-permute-start | bytes 1572872 | tf_op jit(solution)/shard_map/ppermute | solution.py:65
  35.7 12.1 %collective-permute-start.7 = (f32[512,256]{1,0:T(8,128)S(1)}, f32[512,256]{1,0:T(8,128)S(1)}, u32[]{:S(2)}, u32[]{:S(2)}) collective-permute-start(f32[512,256]{1,0:T(8,128)S(1)} %get-tuple-element.91.refs_8_), channel_id=1, source_target_pairs={{8,0},{24,8},{16,24},{0,16},{9,1},{25,9},{17,25},{1,17},{2,10},{18... | collective-permute-start | bytes 1572872 | tf_op jit(solution)/shard_map/ppermute | solution.py:486
  36.4 11.8 %collective-permute-start.6 = (f32[512,256]{1,0:T(8,128)S(1)}, f32[512,256]{1,0:T(8,128)S(1)}, u32[]{:S(2)}, u32[]{:S(2)}) collective-permute-start(f32[512,256]{1,0:T(8,128)S(1)} %get-tuple-element.90.refs_4_), channel_id=1, source_target_pairs={{0,8},{8,24},{24,16},{16,0},{1,9},{9,25},{25,17},{17,1},{10,2},{2,... | collective-permute-start | bytes 1572872 | tf_op jit(solution)/shard_map/ppermute | solution.py:486
  48.9 6.2 %collective-permute-start.9 = (f32[4,2,64,512]{3,2,1,0:T(8,128)S(1)}, f32[4,2,64,512]{3,2,1,0:T(8,128)S(1)}, u32[]{:S(2)}, u32[]{:S(2)}) collective-permute-start(f32[4,2,64,512]{3,2,1,0:T(8,128)S(1)} %get-tuple-element.94.refs_1_), channel_id=1, source_target_pairs={{0,1},{1,0},{2,3},{3,2},{4,5},{5,4},{6,7},{7,6},{8,9},{9,8},{10,11... | collective-permute-start | bytes 3145736 | tf_op jit(solution)/shard_map/ppermute | solution.py:65
  49.0 14.3 %collective-permute-start.12 = (f32[512,256]{1,0:T(8,128)S(1)}, f32[512,256]{1,0:T(8,128)S(1)}, u32[]{:S(2)}, u32[]{:S(2)}) collective-permute-start(f32[512,256]{1,0:T(8,128)S(1)} %get-tuple-element.100), channel_id=1, source_target_pairs={{8,0},{24,8},{16,24},{0,16},{9,1},{25,9},{17,25},{1,17},{2,10},{18... | collective-permute-start | bytes 1572872 | tf_op jit(solution)/shard_map/ppermute | solution.py:486
  49.8 5.2 %copy-start = (f32[3,64,512]{2,1,0:T(8,128)S(1)}, f32[3,64,512]{2,1,0:T(8,128)}, u32[]{:S(2)}) copy-start(f32[3,64,512]{2,1,0:T(8,128)} %diag_ref.1) | copy-start | bytes 1179652
  52.3 14.1 %collective-permute-start.13 = (f32[512,256]{1,0:T(8,128)S(1)}, f32[512,256]{1,0:T(8,128)S(1)}, u32[]{:S(2)}, u32[]{:S(2)}) collective-permute-start(f32[512,256]{1,0:T(8,128)S(1)} %get-tuple-element.101), channel_id=1, source_target_pairs={{0,2},{1,3},{2,0},{3,1},{4,6},{5,7},{6,4},{7,5},{8,10},{9,11},{10,... | collective-permute-start | bytes 1572872 | tf_op jit(solution)/shard_map/ppermute | solution.py:65
  53.7 13.7 %collective-permute-start.11 = (f32[512,256]{1,0:T(8,128)S(1)}, f32[512,256]{1,0:T(8,128)S(1)}, u32[]{:S(2)}, u32[]{:S(2)}) collective-permute-start(f32[512,256]{1,0:T(8,128)S(1)} %get-tuple-element.96.refs_12_), channel_id=1, source_target_pairs={{0,8},{8,24},{24,16},{16,0},{1,9},{9,25},{25,17},{17,1},{10,2},{2,... | collective-permute-start | bytes 1572872 | tf_op jit(solution)/shard_map/ppermute | solution.py:486
  55.0 1.4 collective-permute-start.10
  68.1 13.9 %collective-permute-start.14 = (f32[256,256]{1,0:T(8,128)S(1)}, f32[256,256]{1,0:T(8,128)S(1)}, u32[]{:S(2)}, u32[]{:S(2)}) collective-permute-start(f32[256,256]{1,0:T(8,128)S(1)} %get-tuple-element.104), channel_id=1, source_target_pairs={{0,4},{1,5},{2,6},{3,7},{4,0},{5,1},{6,2},{7,3},{8,12},{9,13},{10,... | collective-permute-start | bytes 786440 | tf_op jit(solution)/shard_map/ppermute | solution.py:65
  70.8 16.7 %collective-permute-start.17 = (f32[512,256]{1,0:T(8,128)S(1)}, f32[512,256]{1,0:T(8,128)S(1)}, u32[]{:S(2)}, u32[]{:S(2)}) collective-permute-start(f32[512,256]{1,0:T(8,128)S(1)} %get-tuple-element.116), channel_id=1, source_target_pairs={{8,0},{24,8},{16,24},{0,16},{9,1},{25,9},{17,25},{1,17},{2,10},{18... | collective-permute-start | bytes 1572872 | tf_op jit(solution)/shard_map/ppermute | solution.py:486
  72.1 15.4 %collective-permute-start.16 = (f32[512,256]{1,0:T(8,128)S(1)}, f32[512,256]{1,0:T(8,128)S(1)}, u32[]{:S(2)}, u32[]{:S(2)}) collective-permute-start(f32[512,256]{1,0:T(8,128)S(1)} %get-tuple-element.106.refs_12_), channel_id=1, source_target_pairs={{0,8},{8,24},{24,16},{16,0},{1,9},{9,25},{25,17},{17,1},{10,2},{2,... | collective-permute-start | bytes 1572872 | tf_op jit(solution)/shard_map/ppermute | solution.py:486
  75.3 18.3 %collective-permute-start.18 = (f32[512,256]{1,0:T(8,128)S(1)}, f32[512,256]{1,0:T(8,128)S(1)}, u32[]{:S(2)}, u32[]{:S(2)}) collective-permute-start(f32[512,256]{1,0:T(8,128)S(1)} %get-tuple-element.108.refs_3_), channel_id=1, source_target_pairs={{0,2},{1,3},{2,0},{3,1},{4,6},{5,7},{6,4},{7,5},{8,10},{9,11},{10,... | collective-permute-start | bytes 1572872 | tf_op jit(solution)/shard_map/ppermute | solution.py:65
  82.6 1.6 %collective-permute-start.15 = (f32[256,256]{1,0:T(8,128)S(1)}, f32[256,256]{1,0:T(8,128)S(1)}, u32[]{:S(2)}, u32[]{:S(2)}) collective-permute-start(f32[256,256]{1,0:T(8,128)S(1)} %shard_map.92.refs_9_.refs_11_), channel_id=1, source_target_pairs={{0,1},{1,0},{2,3},{3,2},{4,5},{5,4},{6,7},{7,6},{8,9},{9,8},{10,11... | collective-permute-start | bytes 786440 | tf_op jit(solution)/shard_map/ppermute | solution.py:65
  89.9 22.4 %collective-permute-start.23 = (f32[512,256]{1,0:T(8,128)S(1)}, f32[512,256]{1,0:T(8,128)S(1)}, u32[]{:S(2)}, u32[]{:S(2)}) collective-permute-start(f32[512,256]{1,0:T(8,128)S(1)} %get-tuple-element.118.refs_3_), channel_id=1, source_target_pairs={{0,2},{1,3},{2,0},{3,1},{4,6},{5,7},{6,4},{7,5},{8,10},{9,11},{10,... | collective-permute-start | bytes 1572872 | tf_op jit(solution)/shard_map/ppermute | solution.py:65
  90.0 18.8 %collective-permute-start.20 = (f32[3,128,256]{2,1,0:T(8,128)S(1)}, f32[3,128,256]{2,1,0:T(8,128)S(1)}, u32[]{:S(2)}, u32[]{:S(2)}) collective-permute-start(f32[3,128,256]{2,1,0:T(8,128)S(1)} %get-tuple-element.123), channel_id=1, source_target_pairs={{0,8},{8,0},{16,24},{24,16},{1,9},{9,1},{17,25},{25,17},{2,10},{10... | collective-permute-start | bytes 1179656 | tf_op jit(solution)/shard_map/ppermute | solution.py:65
  91.5 19.3 %collective-permute-start.21 = (f32[3,128,256]{2,1,0:T(8,128)S(1)}, f32[3,128,256]{2,1,0:T(8,128)S(1)}, u32[]{:S(2)}, u32[]{:S(2)}) collective-permute-start(f32[3,128,256]{2,1,0:T(8,128)S(1)} %get-tuple-element.124), channel_id=1, source_target_pairs={{0,16},{8,24},{16,0},{24,8},{1,17},{9,25},{17,1},{25,9},{2,18},{10... | collective-permute-start | bytes 1179656 | tf_op jit(solution)/shard_map/ppermute | solution.py:65
  92.9 19.4 %collective-permute-start.22 = (f32[3,128,256]{2,1,0:T(8,128)S(1)}, f32[3,128,256]{2,1,0:T(8,128)S(1)}, u32[]{:S(2)}, u32[]{:S(2)}) collective-permute-start(f32[3,128,256]{2,1,0:T(8,128)S(1)} %get-tuple-element.125), channel_id=1, source_target_pairs={{0,24},{8,16},{16,8},{24,0},{1,25},{9,17},{17,9},{25,1},{2,26},{10... | collective-permute-start | bytes 1179656 | tf_op jit(solution)/shard_map/ppermute | solution.py:65
  94.2 13.2 %collective-permute-start.19 = (f32[256,256]{1,0:T(8,128)S(1)}, f32[256,256]{1,0:T(8,128)S(1)}, u32[]{:S(2)}, u32[]{:S(2)}) collective-permute-start(f32[256,256]{1,0:T(8,128)S(1)} %get-tuple-element.121), channel_id=1, source_target_pairs={{0,4},{1,5},{2,6},{3,7},{4,0},{5,1},{6,2},{7,3},{8,12},{9,13},{10,... | collective-permute-start | bytes 786440 | tf_op jit(solution)/shard_map/ppermute | solution.py:65
  107.4 9.2 %collective-permute-start.26 = (f32[2,128,256]{2,1,0:T(8,128)S(1)}, f32[2,128,256]{2,1,0:T(8,128)S(1)}, u32[]{:S(2)}, u32[]{:S(2)}) collective-permute-start(f32[2,128,256]{2,1,0:T(8,128)S(1)} %get-tuple-element.131), channel_id=1, source_target_pairs={{0,8},{8,0},{16,24},{24,16},{1,9},{9,1},{17,25},{25,17},{2,10},{10... | collective-permute-start | bytes 786440 | tf_op jit(solution)/shard_map/ppermute | solution.py:65
  108.8 13.2 %collective-permute-start.27 = (f32[2,128,256]{2,1,0:T(8,128)S(1)}, f32[2,128,256]{2,1,0:T(8,128)S(1)}, u32[]{:S(2)}, u32[]{:S(2)}) collective-permute-start(f32[2,128,256]{2,1,0:T(8,128)S(1)} %get-tuple-element.132), channel_id=1, source_target_pairs={{0,16},{8,24},{16,0},{24,8},{1,17},{9,25},{17,1},{25,9},{2,18},{10... | collective-permute-start | bytes 786440 | tf_op jit(solution)/shard_map/ppermute | solution.py:65
  110.8 11.2 %collective-permute-start.28 = (f32[2,128,256]{2,1,0:T(8,128)S(1)}, f32[2,128,256]{2,1,0:T(8,128)S(1)}, u32[]{:S(2)}, u32[]{:S(2)}) collective-permute-start(f32[2,128,256]{2,1,0:T(8,128)S(1)} %get-tuple-element.133), channel_id=1, source_target_pairs={{0,24},{8,16},{16,8},{24,0},{1,25},{9,17},{17,9},{25,1},{2,26},{10... | collective-permute-start | bytes 786440 | tf_op jit(solution)/shard_map/ppermute | solution.py:65
  113.1 9.0 %collective-permute-start.25 = (f32[3,64,256]{2,1,0:T(8,128)S(1)}, f32[3,64,256]{2,1,0:T(8,128)S(1)}, u32[]{:S(2)}, u32[]{:S(2)}) collective-permute-start(f32[3,64,256]{2,1,0:T(8,128)S(1)} %get-tuple-element.130), channel_id=1, source_target_pairs={{0,2},{1,3},{2,0},{3,1},{4,6},{5,7},{6,4},{7,5},{8,10},{9,11},{10,... | collective-permute-start | bytes 589832 | tf_op jit(solution)/shard_map/ppermute | solution.py:65
  115.4 22.4 %collective-permute-start.30 = (f32[256,256]{1,0:T(8,128)S(1)}, f32[256,256]{1,0:T(8,128)S(1)}, u32[]{:S(2)}, u32[]{:S(2)}) collective-permute-start(f32[256,256]{1,0:T(8,128)S(1)} %get-tuple-element.137), channel_id=1, source_target_pairs={{0,4},{1,5},{2,6},{3,7},{4,0},{5,1},{6,2},{7,3},{8,12},{9,13},{10,... | collective-permute-start | bytes 786440 | tf_op jit(solution)/shard_map/ppermute | solution.py:65
  122.7 15.1 %collective-permute-start.29 = (f32[3,32,256]{2,1,0:T(8,128)S(1)}, f32[3,32,256]{2,1,0:T(8,128)S(1)}, u32[]{:S(2)}, u32[]{:S(2)}) collective-permute-start(f32[3,32,256]{2,1,0:T(8,128)S(1)} %get-tuple-element.135), channel_id=1, source_target_pairs={{0,4},{1,5},{2,6},{3,7},{4,0},{5,1},{6,2},{7,3},{8,12},{9,13},{10,... | collective-permute-start | bytes 294920 | tf_op jit(solution)/shard_map/ppermute | solution.py:65
  126.1 11.7 %collective-permute-start.31 = (f32[2,32,256]{2,1,0:T(8,128)S(1)}, f32[2,32,256]{2,1,0:T(8,128)S(1)}, u32[]{:S(2)}, u32[]{:S(2)}) collective-permute-start(f32[2,32,256]{2,1,0:T(8,128)S(1)} %get-tuple-element.139), channel_id=1, source_target_pairs={{0,4},{1,5},{2,6},{3,7},{4,0},{5,1},{6,2},{7,3},{8,12},{9,13},{10,... | collective-permute-start | bytes 196616 | tf_op jit(solution)/shard_map/ppermute | solution.py:65
  126.2 11.6 %collective-permute-start.32 = (f32[2,32,256]{2,1,0:T(8,128)S(1)}, f32[2,32,256]{2,1,0:T(8,128)S(1)}, u32[]{:S(2)}, u32[]{:S(2)}) collective-permute-start(f32[2,32,256]{2,1,0:T(8,128)S(1)} %get-tuple-element.140), channel_id=1, source_target_pairs={{0,2},{1,3},{2,0},{3,1},{4,6},{5,7},{6,4},{7,5},{8,10},{9,11},{10,... | collective-permute-start | bytes 196616 | tf_op jit(solution)/shard_map/ppermute | solution.py:65
  129.6 8.2 %collective-permute-start.33 = (f32[2,32,256]{2,1,0:T(8,128)S(1)}, f32[2,32,256]{2,1,0:T(8,128)S(1)}, u32[]{:S(2)}, u32[]{:S(2)}) collective-permute-start(f32[2,32,256]{2,1,0:T(8,128)S(1)} %get-tuple-element.141), channel_id=1, source_target_pairs={{0,6},{1,7},{2,4},{3,5},{4,2},{5,3},{6,0},{7,1},{8,14},{9,15},{10,... | collective-permute-start | bytes 196616 | tf_op jit(solution)/shard_map/ppermute | solution.py:65
  138.4 1.4 collective-permute-start.35
  138.5 1.4 collective-permute-start.36
  140.4 8.0 %collective-permute-start.39 = (f32[5,16,512]{2,1,0:T(8,128)S(1)}, f32[5,16,512]{2,1,0:T(8,128)S(1)}, u32[]{:S(2)}, u32[]{:S(2)}) collective-permute-start(f32[5,16,512]{2,1,0:T(8,128)S(1)} %shard_map.101.refs_8_.refs_0_), channel_id=1, source_target_pairs={{0,24},{8,16},{16,8},{24,0},{1,25},{9,17},{17,9},{25,1},{2,26},{10... | collective-permute-start | bytes 491528 | tf_op jit(solution)/shard_map/ppermute | solution.py:65
  142.7 8.7 %collective-permute-start.38 = (f32[5,16,512]{2,1,0:T(8,128)S(1)}, f32[5,16,512]{2,1,0:T(8,128)S(1)}, u32[]{:S(2)}, u32[]{:S(2)}) collective-permute-start(f32[5,16,512]{2,1,0:T(8,128)S(1)} %shard_map.101.refs_8_.refs_0_), channel_id=1, source_target_pairs={{0,16},{8,24},{16,0},{24,8},{1,17},{9,25},{17,1},{25,9},{2,18},{10... | collective-permute-start | bytes 491528 | tf_op jit(solution)/shard_map/ppermute | solution.py:65
  143.6 7.8 %collective-permute-start.37 = (f32[5,16,512]{2,1,0:T(8,128)S(1)}, f32[5,16,512]{2,1,0:T(8,128)S(1)}, u32[]{:S(2)}, u32[]{:S(2)}) collective-permute-start(f32[5,16,512]{2,1,0:T(8,128)S(1)} %shard_map.101.refs_8_.refs_0_), channel_id=1, source_target_pairs={{0,8},{8,0},{16,24},{24,16},{1,9},{9,1},{17,25},{25,17},{2,10},{10... | collective-permute-start | bytes 491528 | tf_op jit(solution)/shard_map/ppermute | solution.py:65
  144.0 1.3 collective-permute-start.24
  144.0 1.5 %collective-permute-start.34 = (f32[128,256]{1,0:T(8,128)S(1)}, f32[128,256]{1,0:T(8,128)S(1)}, u32[]{:S(2)}, u32[]{:S(2)}) collective-permute-start(f32[128,256]{1,0:T(8,128)S(1)} %get-tuple-element.143), channel_id=1, source_target_pairs={{0,1},{1,0},{2,3},{3,2},{4,5},{5,4},{6,7},{7,6},{8,9},{9,8},{10,11... | collective-permute-start | bytes 393224 | tf_op jit(solution)/shard_map/ppermute | solution.py:65
